TPU v7x, 32 devices: a whole 2x2x4 slice. The times are simulated.
32 devices in a mesh: groups: 2 (over y), adapter: 4 (over z), tensor: 2 (over x), dp: 2 (over core).
Axes of the slice: x: 2, y: 2, z: 4, core: 2. Of those that a mesh axis runs over, the one named last changes fastest.
Arguments:
- tokens: bfloat16 [16384, 8192], P(('groups', 'adapter', 'dp'), 'tensor'), parts along dimension 0, may hold values from -6 to 6
- value_weight: bfloat16 [8192, 1024], P('tensor'), may hold values from -0.0625 to 0.0625
- adapter_down_weight: bfloat16 [16, 8192, 64], P(('groups', 'adapter'), 'tensor'), parts along dimension 0, may hold values from -0.0625 to 0.0625
- adapter_up_weight: bfloat16 [16, 64, 1024], P(('groups', 'adapter')), parts along dimension 0, may hold values from -0.75 to 0.75
- row_adapter_index: int32 [16384], P(('groups', 'adapter', 'dp')), parts along dimension 0, may hold values from 0 to 7, as said below
- adapter_slot_of: int32 [16], P('groups'), parts along dimension 0, may hold values from 0 to 7, as said below
Outputs:
- value: bfloat16 [16384, 1024], P(('groups', 'adapter', 'dp'), 'tensor'), parts along dimension 0
There are 2 independent parts, one for each index of `groups`. A program takes and returns all parts, laid end to end along the dimension named above; an argument that names none is the same for every part. Nothing has to cross between parts.
Inputs may be any that keep to these rules, and one draw needn't show every extreme that they name: `row_adapter_index`: all 128 rows of each aligned segment name one adapter. Call the owner of a row the index along the mesh axis `adapter` of the device that stores its slot, slot // 2. Among the 8 segments of one device's rows, at most 2 have one owner, and one owner receives exactly 2 segments from every device. `adapter_slot_of`: A permutation of the slots.
All inputs are finite; a program needn't handle non-finite values.
Results may differ from a plain program's by a relative error of at most 0.001.
Values may be sent and summed in bfloat16 or wider, within the bound.
No kernel may reach another device: no remote copies, remote signals or barrier semaphores. Data moves between devices by JAX's collectives and lax.ppermute only.
A program may use at most 128 MiB of HBM per device.

v0:
```python
import jax
import jax.numpy as jnp
from jax import lax
from jax.sharding import PartitionSpec as P

SEGMENT_ROWS = 128


adapter_scale = 0.5


def on_device(
    tokens, value_weight, adapter_down_weight, adapter_up_weight, row_adapter_index, adapter_slot_of
):
    input_rows, width = tokens.shape
    seg_dev = input_rows // SEGMENT_ROWS
    adapters_per_device = adapter_down_weight.shape[0]
    adapter_number = lax.axis_size("adapter")
    n_tensor = lax.axis_size("tensor")
    value_columns = value_weight.shape[1] // n_tensor
    column_offset = lax.axis_index("tensor") * value_columns
    base_output = jnp.dot(tokens, value_weight, preferred_element_type=jnp.float32)
    value_partial = lax.psum_scatter(base_output, "tensor", scatter_dimension=1, tiled=True)
    seg_ids = row_adapter_index.reshape(seg_dev, SEGMENT_ROWS)[:, 0]
    total = adapter_slot_of.shape[0]
    match = seg_ids[:, None] == jnp.arange(total, dtype=jnp.int32)[None, :]
    slot_indices = jnp.sum(jnp.where(match, adapter_slot_of[None, :], 0), axis=1)
    owners = slot_indices // adapters_per_device
    within = slot_indices % adapters_per_device
    segments = tokens.reshape(seg_dev, SEGMENT_ROWS, width)
    up_columns = lax.dynamic_slice_in_dim(adapter_up_weight, column_offset, value_columns, 2)
    slot_limit = max(2, seg_dev // 4)
    same = owners[:, None] == owners[None, :]
    earlier = jnp.arange(seg_dev)[None, :] < jnp.arange(seg_dev)[:, None]
    position = jnp.sum((same & earlier).astype(jnp.int32), axis=1)
    target_slot = owners * slot_limit + position
    place_mask = (
        target_slot[None, :] == jnp.arange(adapter_number * slot_limit, dtype=jnp.int32)[:, None]
    )
    placing = place_mask.astype(jnp.bfloat16)
    send_rows = jnp.einsum(
        "jk,ksd->jsd", placing, segments, preferred_element_type=jnp.float32
    ).astype(jnp.bfloat16)
    send_rows = send_rows.reshape(adapter_number, slot_limit, SEGMENT_ROWS, width)
    send_slots = jnp.max(jnp.where(place_mask, within[None, :], -1), axis=1).reshape(
        adapter_number, slot_limit
    )
    got_rows = lax.all_to_all(send_rows, "adapter", split_axis=0, concat_axis=0, tiled=True)
    got_slots = lax.all_to_all(send_slots, "adapter", split_axis=0, concat_axis=0, tiled=True)
    select_slot = (got_slots[..., None] == jnp.arange(adapters_per_device, dtype=jnp.int32)).astype(
        jnp.bfloat16
    )
    down_sel = jnp.einsum(
        "fqi,itw->fqtw", select_slot, adapter_down_weight, preferred_element_type=jnp.float32
    ).astype(jnp.bfloat16)
    shrink = jnp.einsum("ncsd,ncdr->ncsr", got_rows, down_sel, preferred_element_type=jnp.float32)
    shrink = lax.psum(shrink, "tensor")
    selected_up_weight = jnp.einsum(
        "oyp,put->oyut", select_slot, up_columns, preferred_element_type=jnp.float32
    )
    outcome = jnp.einsum(
        "ncsr,ncrv->ncsv", shrink, selected_up_weight, precision=lax.Precision.HIGHEST
    )
    gathered_output = lax.all_to_all(outcome, "adapter", split_axis=0, concat_axis=0, tiled=True)
    adapter_output = jnp.take(
        gathered_output.reshape(adapter_number * slot_limit, SEGMENT_ROWS, value_columns),
        target_slot,
        axis=0,
    )
    value_output_sum = value_partial + adapter_scale * adapter_output.reshape(
        input_rows, value_columns
    )
    return value_output_sum.astype(jnp.bfloat16)


def solution(mesh):
    return jax.shard_map(
        on_device,
        mesh=mesh,
        in_specs=(
            P(("groups", "adapter", "dp"), "tensor"),
            P("tensor", None),
            P(("groups", "adapter"), "tensor", None),
            P(("groups", "adapter"), None, None),
            P(("groups", "adapter", "dp")),
            P("groups"),
        ),
        out_specs=P(("groups", "adapter", "dp"), "tensor"),
        check_vma=False,
    )
```

profile of v0, /device:TPU:16, one launch (start us, length us, event | category | flops | bytes accessed | tf_op | source)
XLA Modules:
  0.0 328.5 jit_solution(10104891681277897655)
XLA Ops:
  6.5 0.0 copy-start
  6.5 0.8 slice_reduce_fusion
  7.4 0.8 select_reduce_fusion.1
  8.2 0.2 convert_reduce_fusion
  8.4 0.1 select_reduce_fusion
  8.5 0.7 all_to_all.13
  9.2 5.2 %all-to-all-start.1 = ((s32[4,1,2]{2,1,0:T(1,128)}), s32[4,1,2]{2,1,0:T(1,128)S(1)}, u32[]{:S(2)}, u32[]{:S(2)}) async-start(s32[4,1,2]{2,1,0:T(1,128)} %bitcast.5), calls=%async_computation.2 | async-start | bytes 4096 | tf_op jit(solution)/shard_map/all_to_all | solution.py:49
  14.4 16.1 %fusion.2 = bf16[8,128,4096]{2,0,1:T(8,128)(2,1)} fusion(bf16[8,128,4096]{2,1,0:T(8,128)(2,1)} %bitcast.52, s32[8]{0:T(128)S(1)} %get-tuple-element.6), kind=kOutput, calls=%fused_computation.3 | convolution fusion | flops 71303232 | bytes 16777248 | tf_op jit(solution)/shard_map/jk,ksd->jsd/dot_general | solution.py:41
  30.5 11.4 %copy.40 = bf16[8,128,4096]{2,1,0:T(8,128)(2,1)} copy(bf16[8,128,4096]{2,0,1:T(8,128)(2,1)} %fusion.2) | data formatting | bytes 16777216 | tf_op jit(solution)/shard_map/reshape | solution.py:44
  41.9 0.0 all-to-all-done.1
  41.9 0.0 copy-start.1
  41.9 5.8 %all-to-all-start = ((bf16[4,2,128,4096]{3,2,1,0:T(8,128)(2,1)}), bf16[4,2,128,4096]{3,2,1,0:T(8,128)(2,1)}, u32[]{:S(2)}, u32[]{:S(2)}) async-start(bf16[4,2,128,4096]{3,2,1,0:T(8,128)(2,1)} %bitcast.51), calls=%async_computation.1 | async-start | bytes 16777216 | tf_op jit(solution)/shard_map/all_to_all | solution.py:48
  47.7 0.0 all-reduce.2.cloned.1.call-start
  47.7 0.0 copy-done.1
  47.7 4.7 %convolution_convert_fusion = bf16[4,2,4096,64]{2,1,3,0:T(2,128)(2,1)} fusion(bf16[2,4096,64]{1,2,0:T(8,128)(2,1)S(1)} %copy-done.1, s32[4,2]{1,0:T(4,128)S(1)} %bitcast.55), kind=kOutput, calls=%fused_computation.4 | convolution fusion | flops 10485776 | bytes 5242912 | tf_op jit(solution)/shard_map/fqi,itw->fqtw/dot_general | solution.py:53
  52.4 175.0 %all-to-all-done = bf16[4,2,128,4096]{3,2,1,0:T(8,128)(2,1)} async-done(((bf16[4,2,128,4096]{3,2,1,0:T(8,128)(2,1)}), bf16[4,2,128,4096]{3,2,1,0:T(8,128)(2,1)}, u32[]{:S(2)}, u32[]{:S(2)}) %all-to-all-start) | async-done | bytes 8388640 | tf_op jit(solution)/shard_map/all_to_all | solution.py:48
  227.4 8.7 %fusion.5 = f32[4,2,128,64]{2,3,1,0:T(8,128)} fusion(bf16[4,2,128,4096]{3,2,1,0:T(8,128)(2,1)} %all-to-all-done, bf16[4,2,4096,64]{2,1,3,0:T(2,128)(2,1)} %convolution_convert_fusion), kind=kOutput, calls=%fused_computation.5 | convolution fusion | flops 536870912 | bytes 12845056 | tf_op jit(solution)/shard_map/ncsd,ncdr->ncsr/dot_general | solution.py:56
  236.1 0.0 all-reduce.2.cloned.1.call-update
  236.1 0.0 reduce-scatter.2.cloned.1.call-start
  236.2 15.2 %fusion.20 = f32[1024,1024]{1,0:T(8,128)} fusion(bf16[1024,4096]{1,0:T(8,128)(2,1)} %param.6, bf16[4096,1024]{1,0:T(8,128)(2,1)} %param.7), kind=kOutput, calls=%fused_computation.48 | convolution fusion | flops 8589934592 | bytes 20971520 | tf_op jit(solution)/shard_map/dot_general | solution.py:22
  251.4 0.0 reduce-scatter.2.cloned.1.call-update
  251.4 0.0 copy-done
  251.5 0.5 fusion.12
  252.0 9.5 %all-reduce.2.cloned.1.call-done = f32[4,2,128,64]{2,3,1,0:T(8,128)} async-done(((f32[4,2,128,64]{2,3,1,0:T(8,128)}), f32[4,2,128,64]{2,3,1,0:T(8,128)}) %all-reduce.2.cloned.1.call-update) | async-done | bytes 262160 | tf_op jit(solution)/shard_map/psum | solution.py:57
  261.4 4.2 %fusion.10 = f32[4,2,128,512]{3,2,1,0:T(8,128)} fusion(f32[4,2,128,64]{2,3,1,0:T(8,128)} %all-reduce.2.cloned.1.call-done, f32[4,2,64,512]{3,1,2,0:T(2,128)S(1)} %fusion.12), kind=kOutput, calls=%fused_computation.11 | convolution fusion | flops 402653184 | bytes 3407872 | tf_op jit(solution)/shard_map/ncsr,ncrv->ncsv/dot_general | solution.py:61
  265.6 5.1 %all-to-all-start.2 = ((f32[4,2,128,512]{3,2,1,0:T(8,128)}), f32[4,2,128,512]{3,2,1,0:T(8,128)S(1)}, u32[]{:S(2)}, u32[]{:S(2)}) async-start(f32[4,2,128,512]{3,2,1,0:T(8,128)} %fusion.10), calls=%async_computation.3 | async-start | bytes 4194304 | tf_op jit(solution)/shard_map/all_to_all | solution.py:64
  270.7 0.1 broadcast_bitcast_fusion
  270.8 44.4 %all-to-all-done.2 = f32[4,2,128,512]{3,2,1,0:T(8,128)S(1)} async-done(((f32[4,2,128,512]{3,2,1,0:T(8,128)}), f32[4,2,128,512]{3,2,1,0:T(8,128)S(1)}, u32[]{:S(2)}, u32[]{:S(2)}) %all-to-all-start.2) | async-done | bytes 2097184 | tf_op jit(solution)/shard_map/all_to_all | solution.py:64
  315.2 2.0 gather_fusion
  317.2 1.0 reduce-scatter.2.cloned.1.call-done
  318.2 3.5 %fusion.9 = bf16[1024,512]{1,0:T(8,128)(2,1)} fusion(f32[1024,512]{1,0:T(8,128)} %reduce-scatter.2.cloned.1.call-done, f32[8,128,512]{2,1,0:T(8,128)} %gather_fusion, pred[1024]{0:T(1024)(128)(4,1)S(1)} %broadcast_bitcast_fusion), kind=kLoop, calls=%fused_computation.10 | loop fusion | flops 2097152 | bytes 5243904 | tf_op jit(solution)/shard_map/convert_element_type | solution.py:73
  (5 shorter events, 0.1 us)
Async XLA Ops:
  6.5 244.9 %copy-start = (bf16[2,64,1024]{2,1,0:T(8,128)(2,1)S(1)}, bf16[2,64,1024]{2,1,0:T(8,128)(2,1)}, u32[]{:S(2)}) copy-start(bf16[2,64,1024]{2,1,0:T(8,128)(2,1)} %param.9) | copy-start | bytes 786436
  9.2 32.7 %all-to-all-start.1 = ((s32[4,1,2]{2,1,0:T(1,128)}), s32[4,1,2]{2,1,0:T(1,128)S(1)}, u32[]{:S(2)}, u32[]{:S(2)}) async-start(s32[4,1,2]{2,1,0:T(1,128)} %bitcast.5), calls=%async_computation.2 | async-start | bytes 4096 | tf_op jit(solution)/shard_map/all_to_all | solution.py:49
  41.9 5.8 %copy-start.1 = (bf16[2,4096,64]{1,2,0:T(8,128)(2,1)S(1)}, bf16[2,4096,64]{1,2,0:T(8,128)(2,1)}, u32[]{:S(2)}) copy-start(bf16[2,4096,64]{1,2,0:T(8,128)(2,1)} %param.8) | copy-start | bytes 3145732
  41.9 185.5 %all-to-all-start = ((bf16[4,2,128,4096]{3,2,1,0:T(8,128)(2,1)}), bf16[4,2,128,4096]{3,2,1,0:T(8,128)(2,1)}, u32[]{:S(2)}, u32[]{:S(2)}) async-start(bf16[4,2,128,4096]{3,2,1,0:T(8,128)(2,1)} %bitcast.51), calls=%async_computation.1 | async-start | bytes 16777216 | tf_op jit(solution)/shard_map/all_to_all | solution.py:48
  47.7 213.7 %all-reduce.2.cloned.1.call-start = ((), (), s32[]{:S(2)}) async-start(), calls=%async_computation.5 | async-start | bytes 524288 | tf_op jit(solution)/shard_map/psum | solution.py:57
  236.1 82.0 %reduce-scatter.2.cloned.1.call-start = ((), (), s32[]{:S(2)}) async-start(), calls=%async_computation.4 | async-start | bytes 6291456 | tf_op jit(solution)/shard_map/reduce_scatter | solution.py:23
  265.6 49.6 %all-to-all-start.2 = ((f32[4,2,128,512]{3,2,1,0:T(8,128)}), f32[4,2,128,512]{3,2,1,0:T(8,128)S(1)}, u32[]{:S(2)}, u32[]{:S(2)}) async-start(f32[4,2,128,512]{3,2,1,0:T(8,128)} %fusion.10), calls=%async_computation.3 | async-start | bytes 4194304 | tf_op jit(solution)/shard_map/all_to_all | solution.py:64
Sparse Core Ops, SparseCore 0:
  236.2 25.1 all-reduce.1
  263.8 54.3 reduce-scatter.1
where the time goes:
time: 332 us; the launch traced here: 329 us
  waiting for transfers between devices  230 us (69%)
  matrix products  49.3 us (15%)
  starting transfers between devices  16.2 us (5%)
  local copies, waits for them, and re-layouts  15 us (5%)
  between operations  13.5 us (4%)
  other arithmetic  4.7 us (1%)
    all_to_all x1, waiting for transfers between devices, on_device(): lax.all_to_all(send_rows, 'adapter', split_axis=0, concat_axis=0, tiled=T...  175 us
    all_to_all x1, waiting for transfers between devices, on_device(): lax.all_to_all(outcome, 'adapter', split_axis=0, concat_axis=0, tiled=True)  44.4 us
    dot_general x1, matrix products, on_device(): jnp.einsum('jk,ksd->jsd', placing, segments, preferred_element_type=jnp.f...  16.1 us
    dot_general x1, matrix products, on_device(): jnp.dot(tokens, value_weight, preferred_element_type=jnp.float32)  15.2 us
    reshape x1, local copies, waits for them, and re-layouts, on_device(): send_rows.reshape(adapter_number, slot_limit, SEGMENT_ROWS, width)  11.4 us
    psum x1, waiting for transfers between devices, on_device(): shrink = lax.psum(shrink, 'tensor')  9.46 us
    dot_general x1, matrix products, on_device(): jnp.einsum('ncsd,ncdr->ncsr', got_rows, down_sel, preferred_element_type=...  8.66 us
  transfers between devices with their start and end apart: 5, of which 4 were waited for; matrix products, arithmetic and copies ran while one was open for 16% of the time, Pallas kernels for 0%

commit v1 on v0

v1 whole, which is shorter than its diff:
```python
import jax
import jax.numpy as jnp
from jax import lax
from jax.sharding import PartitionSpec as P

SEGMENT_ROWS = 128
adapter_scale = 0.5


def on_device(
    tokens, value_weight, adapter_down_weight, adapter_up_weight, row_adapter_index, adapter_slot_of
):
    input_rows, width = tokens.shape
    seg_dev = input_rows // SEGMENT_ROWS
    per_device, _, rank = adapter_down_weight.shape
    n_adapter = lax.axis_size("adapter")
    n_tensor = lax.axis_size("tensor")
    n_dp = lax.axis_size("dp")
    me_t = lax.axis_index("tensor")
    me_dp = lax.axis_index("dp")
    columns = value_weight.shape[1] // n_tensor
    part = rank // n_dp

    down = jnp.swapaxes(adapter_down_weight, 1, 2)
    down_part = lax.dynamic_slice_in_dim(down, me_dp * part, part, 1)
    up_part = lax.dynamic_slice(
        adapter_up_weight, (0, me_dp * part, me_t * columns), (per_device, part, columns)
    )
    all_down = lax.all_gather(down_part, ("adapter", "dp"))
    all_up = lax.all_gather(up_part, ("adapter", "dp"))

    base = jnp.dot(tokens, value_weight, preferred_element_type=jnp.float32)
    value = lax.dynamic_slice_in_dim(base, me_t * columns, columns, 1)
    for step in range(1, n_tensor):
        target = (me_t + step) % n_tensor
        sent = lax.dynamic_slice_in_dim(base, target * columns, columns, 1)
        pairs = [(i, (i + step) % n_tensor) for i in range(n_tensor)]
        value = value + lax.ppermute(sent, "tensor", pairs)

    seg_ids = row_adapter_index.reshape(seg_dev, SEGMENT_ROWS)[:, 0]
    total = n_adapter * per_device
    match = seg_ids[:, None] == jnp.arange(total, dtype=jnp.int32)[None, :]
    slot = jnp.sum(jnp.where(match, adapter_slot_of[None, :], 0), axis=1)
    chosen = slot[:, None] == jnp.arange(total, dtype=jnp.int32)[None, :]
    chosen = chosen.reshape(seg_dev, 1, n_adapter, 1, per_device, 1)

    wide = lax.dot_general(
        tokens,
        all_down.reshape(n_adapter * n_dp * per_device * part, width),
        (((1,), (1,)), ((), ())),
        preferred_element_type=jnp.float32,
    ).reshape(seg_dev, SEGMENT_ROWS, n_adapter, n_dp, per_device, part)
    shrink = jnp.sum(jnp.where(chosen, wide, 0.0), axis=(2, 4)).reshape(input_rows, rank)
    mine = shrink
    for step in range(1, n_tensor):
        pairs = [(i, (i + step) % n_tensor) for i in range(n_tensor)]
        shrink = shrink + lax.ppermute(mine, "tensor", pairs)
    picked = jnp.sum(
        jnp.where(
            chosen.reshape(seg_dev, n_adapter, 1, per_device, 1, 1),
            all_up.reshape(1, n_adapter, n_dp, per_device, part, columns).astype(jnp.float32),
            0.0,
        ),
        axis=(1, 3),
    ).reshape(seg_dev, rank, columns)
    lora = jnp.einsum(
        "sru,suv->srv",
        shrink.reshape(seg_dev, SEGMENT_ROWS, rank),
        picked,
        precision=lax.Precision.HIGHEST,
    )
    return (value + adapter_scale * lora.reshape(input_rows, columns)).astype(jnp.bfloat16)


def solution(mesh):
    return jax.shard_map(
        on_device,
        mesh=mesh,
        in_specs=(
            P(("groups", "adapter", "dp"), "tensor"),
            P("tensor", None),
            P(("groups", "adapter"), "tensor", None),
            P(("groups", "adapter"), None, None),
            P(("groups", "adapter", "dp")),
            P("groups"),
        ),
        out_specs=P(("groups", "adapter", "dp"), "tensor"),
        check_vma=False,
    )
```

time: 332 us -> 92.7 us (0.28)
  the two profiles are of different devices: /device:TPU:16 before, /device:TPU:0 now
where the time goes in v1:
time: 92.7 us; the launch traced here: 92.5 us
  matrix products  22.7 us (24%)
  waiting for transfers between devices  22.3 us (24%)
  blocking collectives  17.5 us (19%)
  between operations  13.5 us (15%)
  local copies, waits for them, and re-layouts  7.05 us (8%)
  other arithmetic  5.02 us (5%)
  starting transfers between devices  4.5 us (5%)
    all_gather x1, blocking collectives, on_device(): all_up = lax.all_gather(up_part, ('adapter', 'dp'))  17.5 us
    all_gather x1, waiting for transfers between devices, on_device(): all_down = lax.all_gather(down_part, ('adapter', 'dp'))  16.4 us
    dot_general x1, matrix products, on_device(): base = jnp.dot(tokens, value_weight, preferred_element_type=jnp.float32)  12.6 us
    dot_general x1, matrix products, on_device(): lax.dot_general(tokens, all_down.reshape(n_adapter * n_dp * per_device *...  8.22 us
    ppermute x1, waiting for transfers between devices, on_device(): shrink = shrink + lax.ppermute(mine, 'tensor', pairs)  5.85 us
    unnamed x12, local copies, waits for them, and re-layouts  3.67 us
    convert_element_type x1, other arithmetic, on_device(): (value + adapter_scale * lora.reshape(input_rows, columns)).astype(jnp.bf...  3.32 us
    ppermute x1, starting transfers between devices, on_device(): value = value + lax.ppermute(sent, 'tensor', pairs)  2.94 us
  transfers between devices with their start and end apart: 3, of which 2 were waited for; matrix products, arithmetic and copies ran while one was open for 30% of the time, Pallas kernels for 0%

profile of v1, /device:TPU:0, one launch (start us, length us, event | category | flops | bytes accessed | tf_op | source)
XLA Modules:
  0.0 92.5 jit_solution(12713175369101173769)
XLA Ops:
  6.5 0.0 copy-start
  6.5 0.0 all-gather.4.cloned.1.call-start
  6.5 1.2 %copy-done = bf16[2,4096,64]{1,2,0:T(8,128)(2,1)S(1)} copy-done((bf16[2,4096,64]{1,2,0:T(8,128)(2,1)S(1)}, bf16[2,4096,64]{1,2,0:T(8,128)(2,1)}, u32[]{:S(2)}) %copy-start) | copy-done | bytes 1048600
  7.8 0.8 dynamic-slice_bitcast_fusion
  8.6 0.0 all-gather.4.cloned.1.call-update
  8.6 12.6 %fusion.3 = f32[1024,1024]{1,0:T(8,128)S(1)} fusion(bf16[1024,4096]{1,0:T(8,128)(2,1)} %param.6, bf16[4096,1024]{1,0:T(8,128)(2,1)} %param.7), kind=kOutput, calls=%fused_computation.19 | convolution fusion | flops 8589934592 | bytes 20971520 | tf_op jit(solution)/shard_map/dot_general | solution.py:32
  21.2 0.0 copy-start.1
  21.2 1.9 %copy-done.1 = f32[1024,1024]{1,0:T(8,128)} copy-done((f32[1024,1024]{1,0:T(8,128)}, f32[1024,1024]{1,0:T(8,128)S(1)}, u32[]{:S(2)}) %copy-start.1) | copy-done | bytes 4194328
  23.2 0.0 copy-start.3
  23.2 0.0 copy-start.4
  23.2 1.5 %constant_dynamic-slice_fusion.1 = f32[1024,512]{1,0:T(8,128)} fusion(f32[1024,1024]{1,0:T(8,128)S(1)} %fusion.3, s32[]{:T(128)S(6)} %select_n.32), kind=kLoop, calls=%fused_computation.17 | loop fusion | bytes 4194308 | tf_op jit(solution)/shard_map/dynamic_slice | solution.py:36
  24.6 2.9 %collective-permute-start = (f32[1024,512]{1,0:T(8,128)}, f32[1024,512]{1,0:T(8,128)}, u32[]{:S(2)}, u32[]{:S(2)}) collective-permute-start(f32[1024,512]{1,0:T(8,128)} %constant_dynamic-slice_fusion.1), channel_id=1, source_target_pairs={{0,2},{2,0},{1,3},{3,1},{4,6},{6,4},{5,7},{7,5},{8,10},{10,8},{9,1... | collective-permute-start | bytes 6291464 | tf_op jit(solution)/shard_map/ppermute | solution.py:38
  27.6 0.0 copy-done.3
  27.6 0.1 slice_reduce_fusion
  27.7 0.0 copy-done.4
  27.7 0.2 select_reduce_fusion.2
  27.9 0.1 broadcast_compare_fusion
  28.0 0.1 copy.14
  28.1 0.9 constant_dynamic-slice_fusion
  28.9 17.5 %all-gather.1 = bf16[16,32,512]{2,1,0:T(8,128)(2,1)S(1)} all-gather(bf16[2,32,512]{2,1,0:T(8,128)(2,1)S(1)} %constant_dynamic-slice_fusion), channel_id=3, replica_groups=mesh['groups'=2,'adapter'=4,'tensor'=2,'dp'=2] {'adapter','dp'}, dimensions={0}, use_global_device_ids=true | all-gather | bytes 589824 | tf_op jit(solution)/shard_map/all_gather | solution.py:30
  46.4 0.1 bitcast_convert_fusion
  46.6 16.4 %all-gather.4.cloned.1.call-done = bf16[16,32,4096]{2,1,0:T(8,128)(2,1)} async-done(((bf16[2,32,4096]{2,1,0:T(8,128)(2,1)}), bf16[16,32,4096]{2,1,0:T(8,128)(2,1)}) %all-gather.4.cloned.1.call-update) | async-done | bytes 4194320 | tf_op jit(solution)/shard_map/all_gather | solution.py:29
  63.0 8.2 %convolution_bitcast_fusion = f32[64,8,8,128]{3,1,2,0:T(8,128)S(1)} fusion(bf16[512,4096]{1,0:T(8,128)(2,1)} %bitcast.48, bf16[1024,4096]{1,0:T(8,128)(2,1)} %param.6), kind=kOutput, calls=%fused_computation.4 | convolution fusion | flops 4294967296 | bytes 14680064 | tf_op jit(solution)/shard_map/dot_general | solution.py:47
  71.2 0.5 copy.17
  71.7 0.0 copy-start.2
  71.7 0.2 select_reduce_fusion.1
  72.0 1.6 %collective-permute-start.1 = (f32[1024,64]{0,1:T(8,128)S(1)}, f32[1024,64]{0,1:T(8,128)S(1)}, u32[]{:S(2)}, u32[]{:S(2)}) collective-permute-start(f32[1024,64]{0,1:T(8,128)S(1)} %bitcast.46), channel_id=1, source_target_pairs={{0,2},{2,0},{1,3},{3,1},{4,6},{6,4},{5,7},{7,5},{8,10},{10,8},{9,1... | collective-permute-start | bytes 786440 | tf_op jit(solution)/shard_map/ppermute | solution.py:57
  73.5 1.1 %select_reduce_fusion = f32[8,2,32,512]{3,2,1,0:T(8,128)S(1)} fusion(f32[4,2,2,32,512]{4,3,2,1,0:T(8,128)S(1)} %bitcast_convert_fusion, pred[8,4,2]{2,1,0:T(4,128)(4,1)S(1)} %broadcast_compare_fusion), kind=kLoop, calls=%fused_computation | loop fusion | flops 3932160 | bytes 2097216 | tf_op jit(solution)/shard_map/reduce_sum | solution.py:58
  74.6 5.9 %collective-permute-done.1 = f32[1024,64]{0,1:T(8,128)S(1)} collective-permute-done((f32[1024,64]{0,1:T(8,128)S(1)}, f32[1024,64]{0,1:T(8,128)S(1)}, u32[]{:S(2)}, u32[]{:S(2)}) %collective-permute-start.1) | collective-permute-done | bytes 262176 | tf_op jit(solution)/shard_map/ppermute | solution.py:57
  80.5 1.8 %convolution_multiply_fusion = f32[8,128,512]{2,1,0:T(8,128)S(1)} fusion(f32[8,64,512]{2,1,0:T(8,128)S(1)} %bitcast.43, f32[1024,64]{0,1:T(8,128)S(1)} %collective-permute-done.1, f32[8,8,8,128]{3,2,1,0:T(8,128)S(1)} %bitcast.45), kind=kOutput, calls=%fused_computation.5 | convolution fusion | flops 403243008 | bytes 3670016 | tf_op jit(solution)/shard_map/sru,suv->srv/dot_general | solution.py:66
  82.3 0.0 collective-permute-done
  82.3 0.0 copy-done.2
  82.3 3.3 %fusion = bf16[1024,512]{1,0:T(8,128)(2,1)} fusion(f32[8,128,512]{2,1,0:T(8,128)S(1)} %convolution_multiply_fusion, f32[1024,512]{1,0:T(8,128)} %collective-permute-done, f32[1024,1024]{1,0:T(8,128)S(1)} %copy-done.2, s32[]{:T(128)S(6)} %select_n.30), kind=kLoop, calls=%fused_computation.2 | loop fusion | flops 1572864 | bytes 7340036 | tf_op jit(solution)/shard_map/convert_element_type | solution.py:72
  (2 shorter events, 0.1 us)
Async XLA Ops:
  6.5 1.2 %copy-start = (bf16[2,4096,64]{1,2,0:T(8,128)(2,1)S(1)}, bf16[2,4096,64]{1,2,0:T(8,128)(2,1)}, u32[]{:S(2)}) copy-start(bf16[2,4096,64]{1,2,0:T(8,128)(2,1)} %param.8) | copy-start | bytes 3145732
  6.5 56.4 %all-gather.4.cloned.1.call-start = ((), (), s32[]{:S(2)}) async-start(), calls=%async_computation | async-start | bytes 4718592 | tf_op jit(solution)/shard_map/all_gather | solution.py:29
  21.2 1.9 %copy-start.1 = (f32[1024,1024]{1,0:T(8,128)}, f32[1024,1024]{1,0:T(8,128)S(1)}, u32[]{:S(2)}) copy-start(f32[1024,1024]{1,0:T(8,128)S(1)} %fusion.3) | copy-start | bytes 12582916
  23.2 4.4 %copy-start.3 = (s32[1024]{0:T(1024)S(1)}, s32[1024]{0:T(1024)}, u32[]{:S(2)}) copy-start(s32[1024]{0:T(1024)} %param.10) | copy-start | bytes 12292
  23.2 4.5 %copy-start.4 = (s32[8]{0:T(128)S(1)}, s32[8]{0:T(128)}, u32[]{:S(2)}) copy-start(s32[8]{0:T(128)} %param.11) | copy-start | bytes 100
  24.6 57.7 %collective-permute-start = (f32[1024,512]{1,0:T(8,128)}, f32[1024,512]{1,0:T(8,128)}, u32[]{:S(2)}, u32[]{:S(2)}) collective-permute-start(f32[1024,512]{1,0:T(8,128)} %constant_dynamic-slice_fusion.1), channel_id=1, source_target_pairs={{0,2},{2,0},{1,3},{3,1},{4,6},{6,4},{5,7},{7,5},{8,10},{10,8},{9,1... | collective-permute-start | bytes 6291464 | tf_op jit(solution)/shard_map/ppermute | solution.py:38
  71.7 10.7 %copy-start.2 = (f32[1024,1024]{1,0:T(8,128)S(1)}, f32[1024,1024]{1,0:T(8,128)}, u32[]{:S(2)}) copy-start(f32[1024,1024]{1,0:T(8,128)} %copy-done.1) | copy-start | bytes 12582916
  72.0 8.5 %collective-permute-start.1 = (f32[1024,64]{0,1:T(8,128)S(1)}, f32[1024,64]{0,1:T(8,128)S(1)}, u32[]{:S(2)}, u32[]{:S(2)}) collective-permute-start(f32[1024,64]{0,1:T(8,128)S(1)} %bitcast.46), channel_id=1, source_target_pairs={{0,2},{2,0},{1,3},{3,1},{4,6},{6,4},{5,7},{7,5},{8,10},{10,8},{9,1... | collective-permute-start | bytes 786440 | tf_op jit(solution)/shard_map/ppermute | solution.py:57
Sparse Core Ops, SparseCore 0:
  9.0 53.9 all-gather.3

commit v2 on v1

v2 whole, which is shorter than its diff:
```python
import functools

import jax
import jax.numpy as jnp
from jax import lax
from jax.experimental import pallas as pl
from jax.experimental.pallas import tpu as pltpu
from jax.sharding import PartitionSpec as P

SEGMENT_ROWS = 128
adapter_scale = 0.5
VMEM_BYTES = 40 * 2**20
MOST = 2


def cost(flops, moved):
    return pl.CostEstimate(flops=int(flops), bytes_accessed=int(moved), transcendentals=0)


def params():
    return pltpu.CompilerParams(vmem_limit_bytes=VMEM_BYTES)


def segment_slot(ids, slots, s):
    return slots[ids[s * SEGMENT_ROWS]]


def find_segment(ids, slots, per_device, seg_dev, owner, rank):
    found, within, count = jnp.int32(-1), jnp.int32(0), jnp.int32(0)
    for s in range(seg_dev):
        slot = segment_slot(ids, slots, s)
        hit = lax.div(slot, jnp.int32(per_device)) == owner
        take = hit & (count == rank)
        found = jnp.where(take, s, found)
        within = jnp.where(take, lax.rem(slot, jnp.int32(per_device)), within)
        count = count + hit.astype(jnp.int32)
    return found, within


def base_kernel(column, x_ref, w_ref, o_ref):
    del column
    o_ref[...] = jnp.dot(x_ref[...], w_ref[...], preferred_element_type=jnp.float32)


def base_product(tokens, weight, column, columns):
    rows, width = tokens.shape
    block = min(256, rows)
    return pl.pallas_call(
        base_kernel,
        grid_spec=pltpu.PrefetchScalarGridSpec(
            num_scalar_prefetch=1,
            grid=(rows // block,),
            in_specs=[
                pl.BlockSpec((block, width), lambda i, c: (i, 0)),
                pl.BlockSpec((width, columns), lambda i, c: (0, c[0])),
            ],
            out_specs=pl.BlockSpec((block, columns), lambda i, c: (i, 0)),
        ),
        out_shape=jax.ShapeDtypeStruct((rows, columns), jnp.float32),
        compiler_params=params(),
        cost_estimate=cost(
            2 * rows * width * columns, 2 * rows * width + 2 * width * columns + 4 * rows * columns
        ),
    )(column.reshape(1), tokens, weight)


def shrink_kernel(n_bufs, per_device, rank, seg_dev, ids, slots, owners, *refs):
    x_refs, d_refs, o_ref = refs[:MOST], refs[MOST : MOST + n_bufs], refs[-1]
    width = x_refs[0].shape[1]
    step = pl.program_id(0)
    owner = owners[step]
    for buf in range(n_bufs):
        for j in range(MOST):
            seg, within = find_segment(ids, slots, per_device, seg_dev, owner, j)

            @pl.when((step == buf) & (seg >= 0))
            def _(buf=buf, j=j, within=within):
                down = d_refs[buf][pl.ds(pl.multiple_of(within * rank, rank), rank), :width]
                o_ref[0, :, j * rank : (j + 1) * rank] = lax.dot_general(
                    x_refs[j][...], down, (((1,), (1,)), ((), ())), preferred_element_type=jnp.float32
                )

            @pl.when((step == buf) & (seg < 0))
            def _(j=j):
                o_ref[0, :, j * rank : (j + 1) * rank] = jnp.zeros((SEGMENT_ROWS, rank), jnp.float32)


def shrink_product(tokens, ids, slots, owners, buffers, per_device, rank):
    rows, width = tokens.shape
    seg_dev = rows // SEGMENT_ROWS
    n_bufs = len(buffers)

    def segment_block(j):
        def index(i, ids, slots, owners):
            seg, _ = find_segment(ids, slots, per_device, seg_dev, owners[i], j)
            return jnp.maximum(seg, 0), 0

        return pl.BlockSpec((SEGMENT_ROWS, width), index)

    whole = [pl.BlockSpec(b.shape, lambda i, *_: (0, 0)) for b in buffers]
    return pl.pallas_call(
        functools.partial(shrink_kernel, n_bufs, per_device, rank, seg_dev),
        grid_spec=pltpu.PrefetchScalarGridSpec(
            num_scalar_prefetch=3,
            grid=(n_bufs,),
            in_specs=[segment_block(j) for j in range(MOST)] + whole,
            out_specs=pl.BlockSpec((1, SEGMENT_ROWS, MOST * rank), lambda i, *_: (i, 0, 0)),
        ),
        out_shape=jax.ShapeDtypeStruct((n_bufs, SEGMENT_ROWS, MOST * rank), jnp.float32),
        compiler_params=params(),
        cost_estimate=cost(
            n_bufs * MOST * 2 * SEGMENT_ROWS * width * 256,
            n_bufs * 2 * (MOST * SEGMENT_ROWS + per_device * rank) * width,
        ),
    )(ids, slots, owners, *([tokens] * MOST), *buffers)


def combine_kernel(n_bufs, n_base, n_shrink, per_device, rank, seg_dev, ids, slots, owners, *refs):
    base_refs, refs = refs[:n_base], refs[n_base:]
    up_refs, refs = refs[:n_bufs], refs[n_bufs:]
    shrink_refs, refs = refs[: n_bufs * n_shrink], refs[n_bufs * n_shrink :]
    o_ref, up, mid = refs
    s = pl.program_id(0)
    slot = segment_slot(ids, slots, s)
    owner = lax.div(slot, jnp.int32(per_device))
    within = lax.rem(slot, jnp.int32(per_device))
    j = jnp.int32(0)
    for other in range(seg_dev):
        same = lax.div(segment_slot(ids, slots, other), jnp.int32(per_device)) == owner
        j = j + ((other < s) & same).astype(jnp.int32)
    for b in range(n_bufs):

        @pl.when(owners[b] == owner)
        def _(b=b):
            up[...] = up_refs[b][pl.ds(pl.multiple_of(within * rank, rank), rank), :]
            total = shrink_refs[b * n_shrink][0]
            for r in shrink_refs[b * n_shrink + 1 : (b + 1) * n_shrink]:
                total = total + r[0]
            mid[...] = total

    total = jnp.where(j == 0, mid[:, :rank], mid[:, rank : 2 * rank])
    high = total.astype(jnp.bfloat16)
    left = total - high.astype(jnp.float32)
    middle = left.astype(jnp.bfloat16)
    low = (left - middle.astype(jnp.float32)).astype(jnp.bfloat16)
    lora = jnp.dot(low, up[...], preferred_element_type=jnp.float32)
    lora = lora + jnp.dot(middle, up[...], preferred_element_type=jnp.float32)
    lora = lora + jnp.dot(high, up[...], preferred_element_type=jnp.float32)
    value = base_refs[0][...]
    for r in base_refs[1:]:
        value = value + r[...]
    o_ref[...] = (value + adapter_scale * lora).astype(jnp.bfloat16)


def combine(ids, slots, owners, bases, buffers, shrinks, per_device, rank):
    rows, columns = bases[0].shape
    seg_dev = rows // SEGMENT_ROWS
    n_bufs, n_shrink = len(buffers), len(shrinks[0])
    last = buffers[0].shape[1] // columns - 1
    return pl.pallas_call(
        functools.partial(combine_kernel, n_bufs, len(bases), n_shrink, per_device, rank, seg_dev),
        grid_spec=pltpu.PrefetchScalarGridSpec(
            num_scalar_prefetch=3,
            grid=(seg_dev,),
            in_specs=[pl.BlockSpec((SEGMENT_ROWS, columns), lambda i, *_: (i, 0)) for _ in bases]
            + [pl.BlockSpec((b.shape[0], columns), lambda i, *_: (0, last)) for b in buffers]
            + [
                pl.BlockSpec((1, SEGMENT_ROWS, MOST * rank), lambda i, *_, place=place: (place, 0, 0))
                for group in shrinks
                for _, place in group
            ],
            out_specs=pl.BlockSpec((SEGMENT_ROWS, columns), lambda i, *_: (i, 0)),
            scratch_shapes=[
                pltpu.VMEM((rank, columns), jnp.bfloat16),
                pltpu.VMEM((SEGMENT_ROWS, MOST * rank), jnp.float32),
            ],
        ),
        out_shape=jax.ShapeDtypeStruct((rows, columns), jnp.bfloat16),
        compiler_params=params(),
        cost_estimate=cost(6 * rows * rank * columns, (4 * len(bases) + 2) * rows * columns),
    )(ids, slots, owners, *bases, *buffers, *[array for group in shrinks for array, _ in group])


def on_device(
    tokens, value_weight, adapter_down_weight, adapter_up_weight, row_adapter_index, adapter_slot_of
):
    width = tokens.shape[1]
    per_device, _, rank = adapter_down_weight.shape
    n_adapter = lax.axis_size("adapter")
    n_tensor = lax.axis_size("tensor")
    me_a = lax.axis_index("adapter")
    me_t = lax.axis_index("tensor")
    core = lax.axis_index("dp")
    columns = value_weight.shape[1] // n_tensor
    ids, slots = row_adapter_index, adapter_slot_of

    def swap_tensor(array, step):
        pairs = [(i, (i + step) % n_tensor) for i in range(n_tensor)]
        return lax.ppermute(array, "tensor", pairs)

    def along_line(array, stage):
        up = [(2 * i, 2 * (i + 1)) for i in range(stage - 1, n_adapter - 1)]
        down = [(2 * i + 1, 2 * (i - 1) + 1) for i in range(1, n_adapter - stage + 1)]
        return lax.ppermute(array, ("adapter", "dp"), up + down)

    def swap_cores(array):
        return lax.ppermute(array, "dp", [(0, 1), (1, 0)])

    down = jnp.swapaxes(adapter_down_weight, 1, 2).reshape(per_device * rank, width)
    up = lax.dynamic_slice_in_dim(adapter_up_weight, me_t * columns, columns, 2)
    message = jnp.concatenate([down, up.reshape(per_device * rank, columns)], axis=1)

    buffers, owners = [message], [me_a]
    held = message
    stages = []
    for stage in range(1, n_adapter):
        held = along_line(held, stage)
        stages.append((held, swap_cores(held)))
        toward = jnp.where(core == 0, -stage, stage)
        owners += [me_a + toward, me_a - toward]
        buffers += [held, stages[-1][1]]

    parts = [
        swap_tensor(base_product(tokens, value_weight, (me_t + step) % n_tensor, columns), step)
        for step in range(1, n_tensor)
    ]
    bases = [base_product(tokens, value_weight, me_t, columns)] + parts

    shrinks = []
    for stage in range(n_adapter):
        if stage == 0:
            mine = [message]
            whose = jnp.stack([me_a])
        else:
            mine = list(stages[stage - 1])
            whose = jnp.stack(owners[2 * stage - 1 : 2 * stage + 1])
        shrink = shrink_product(tokens, ids, slots, whose, mine, per_device, rank)
        copies = [shrink] + [swap_tensor(shrink, step) for step in range(1, n_tensor)]
        shrinks += [[(c, place) for c in copies] for place in range(len(mine))]

    return combine(ids, slots, jnp.stack(owners), bases, buffers, shrinks, per_device, rank)


def solution(mesh):
    return jax.shard_map(
        on_device,
        mesh=mesh,
        in_specs=(
            P(("groups", "adapter", "dp"), "tensor"),
            P("tensor", None),
            P(("groups", "adapter"), "tensor", None),
            P(("groups", "adapter"), None, None),
            P(("groups", "adapter", "dp")),
            P("groups"),
        ),
        out_specs=P(("groups", "adapter", "dp"), "tensor"),
        check_vma=False,
    )
```

time: 92.7 us -> 118 us (1.27)
  the two profiles are of different devices: /device:TPU:0 before, /device:TPU:10 now
where the time goes in v2:
time: 118 us
  waiting for transfers between devices  50.5 us (43%)
  Pallas kernels  38.1 us (32%)
  starting transfers between devices  14.9 us (13%)
  local copies, waits for them, and re-layouts  12.5 us (11%)
  other arithmetic  1.53 us (1%)
    ppermute x3, waiting for transfers between devices, along_line(): return lax.ppermute(array, ('adapter', 'dp'), up + down)  27.3 us
    ppermute x5, waiting for transfers between devices, swap_tensor(): return lax.ppermute(array, 'tensor', pairs)  23.2 us
    pallas_call x2, Pallas kernels, base_product(): pl.pallas_call(base_kernel, grid_spec=pltpu.PrefetchScalarGridSpec(num_sc...  15.3 us
    pallas_call x4, Pallas kernels, shrink_product(): pl.pallas_call(functools.partial(shrink_kernel, n_bufs, per_device, rank,...  14.9 us
    unnamed x20, local copies, waits for them, and re-layouts  12.4 us
    ppermute x3, starting transfers between devices, along_line(): return lax.ppermute(array, ('adapter', 'dp'), up + down)  9.68 us
    pallas_call x1, Pallas kernels, combine(): pl.pallas_call(functools.partial(combine_kernel, n_bufs, len(bases), n_sh...  7.85 us
    ppermute x5, starting transfers between devices, swap_tensor(): return lax.ppermute(array, 'tensor', pairs)  4.62 us
  transfers between devices with their start and end apart: 11, of which 6 were waited for; matrix products, arithmetic and copies ran while one was open for 0% of the time, Pallas kernels for 26%

profile of v2, /device:TPU:10, one launch (start us, length us, event | category | flops | bytes accessed | tf_op | source)
XLA Modules:
  0.0 117.5 jit_solution(5074801976237328691)
XLA Ops:
  0.0 0.0 copy-start
  0.0 0.9 copy-done
  1.0 1.3 %pad_maximum_fusion.refs_2_ = bf16[128,4608]{1,0:T(8,128)(2,1)S(1)} fusion(bf16[128,512]{1,0:T(8,128)(2,1)S(1)} %bitcast.16, bf16[128,4096]{1,0:T(8,128)(2,1)} %bitcast.15), kind=kLoop, calls=%fused_computation | loop fusion | flops 2359296 | bytes 2359296 | tf_op jit(solution)/shard_map/concatenate | solution.py:211
  2.3 3.5 %collective-permute-start.1 = (bf16[128,4608]{1,0:T(8,128)(2,1)S(1)}, bf16[128,4608]{1,0:T(8,128)(2,1)S(1)}, u32[]{:S(2)}, u32[]{:S(2)}) collective-permute-start(bf16[128,4608]{1,0:T(8,128)(2,1)S(1)} %pad_maximum_fusion.refs_2_), channel_id=1, source_target_pairs={{0,4},{4,8},{8,12},{5,1},{9,5},{13,9},{2,6},{6,10},{10,14},{7,3},{... | collective-permute-start | bytes 3538952 | tf_op jit(solution)/shard_map/ppermute | solution.py:204
  5.8 14.6 %collective-permute-done.1.refs_2_.refs_3_ = bf16[128,4608]{1,0:T(8,128)(2,1)S(1)} collective-permute-done((bf16[128,4608]{1,0:T(8,128)(2,1)S(1)}, bf16[128,4608]{1,0:T(8,128)(2,1)S(1)}, u32[]{:S(2)}, u32[]{:S(2)}) %collective-permute-start.1) | collective-permute-done | bytes 1179680 | tf_op jit(solution)/shard_map/ppermute | solution.py:204
  20.4 0.0 copy-start.4
  20.4 4.5 %collective-permute-start.3 = (bf16[128,4608]{1,0:T(8,128)(2,1)S(1)}, bf16[128,4608]{1,0:T(8,128)(2,1)}, u32[]{:S(2)}, u32[]{:S(2)}) collective-permute-start(bf16[128,4608]{1,0:T(8,128)(2,1)S(1)} %collective-permute-done.1.refs_2_.refs_3_), channel_id=1, source_target_pairs={{4,8},{8,12},{5,1},{9,5},{6,10},{10,14},{7,3},{11,7},{20,24},{24,2... | collective-permute-start | bytes 3538952 | tf_op jit(solution)/shard_map/ppermute | solution.py:204
  24.9 12.7 %collective-permute-done.3.refs_2_.refs_5_ = bf16[128,4608]{1,0:T(8,128)(2,1)} collective-permute-done((bf16[128,4608]{1,0:T(8,128)(2,1)S(1)}, bf16[128,4608]{1,0:T(8,128)(2,1)}, u32[]{:S(2)}, u32[]{:S(2)}) %collective-permute-start.3) | collective-permute-done | bytes 1179680 | tf_op jit(solution)/shard_map/ppermute | solution.py:204
  37.6 1.7 %collective-permute-start.5 = (bf16[128,4608]{1,0:T(8,128)(2,1)}, bf16[128,4608]{1,0:T(8,128)(2,1)}, u32[]{:S(2)}, u32[]{:S(2)}) collective-permute-start(bf16[128,4608]{1,0:T(8,128)(2,1)} %collective-permute-done.3.refs_2_.refs_5_), channel_id=1, source_target_pairs={{8,12},{5,1},{10,14},{7,3},{24,28},{21,17},{26,30},{23,19}} | collective-permute-start | bytes 3538952 | tf_op jit(solution)/shard_map/ppermute | solution.py:204
  39.2 0.0 copy-start.1
  39.2 3.4 %copy-done.1 = bf16[1024,4096]{1,0:T(8,128)(2,1)S(1)} copy-done((bf16[1024,4096]{1,0:T(8,128)(2,1)S(1)}, bf16[1024,4096]{1,0:T(8,128)(2,1)}, u32[]{:S(2)}) %copy-start.1) | copy-done | bytes 8388632
  42.6 0.0 copy-start.6
  42.6 0.0 copy-start.7
  42.6 8.0 %shard_map.65 = f32[1024,512]{1,0:T(8,128)} custom-call(s32[1]{0:T(128)} %bitcast.8.column, bf16[1024,4096]{1,0:T(8,128)(2,1)S(1)} %copy-done.1, bf16[4096,1024]{1,0:T(8,128)(2,1)} %w_ref.3), custom_call_target="tpu_custom_call" | custom-call | flops 4294967296 | bytes 14680064 | tf_op jit(solution)/shard_map/pallas_call | solution.py:48
  50.6 0.5 collective-permute-start
  51.2 0.0 collective-permute-start.2
  51.2 0.5 collective-permute-start.4
  51.7 0.0 collective-permute-done.5.refs_2_.refs_7_
  51.7 0.1 collective-permute-start.6
  51.8 0.0 copy-done.6
  51.8 0.0 copy-done.7
  51.8 0.0 copy-start.2
  51.8 3.4 %copy-done.2 = bf16[1024,4096]{1,0:T(8,128)(2,1)S(1)} copy-done((bf16[1024,4096]{1,0:T(8,128)(2,1)S(1)}, bf16[1024,4096]{1,0:T(8,128)(2,1)}, u32[]{:S(2)}) %copy-start.2) | copy-done | bytes 8388632
  55.1 2.3 %shard_map.66.refs_9_ = f32[1,128,128]{2,1,0:T(8,128)} custom-call(s32[1024]{0:T(1024)S(1)} %copy-done.6, s32[8]{0:T(128)S(1)} %copy-done.7, s32[1]{0:T(128)} %bitcast.owners, bf16[1024,4096]{1,0:T(8,128)(2,1)S(1)} %copy-done.2, bf16[1024,4096]{1,0:T(8,128)(2,1)S(1)} %copy-done.2, bf16[128,4608]{1,0:T(8,128)(2,1)S(1)} %pad_maximum_fusion.refs_2_), custom_call_target="tpu_custom_call" | custom-call | flops 536870912 | bytes 3145728 | tf_op jit(solution)/shard_map/pallas_call | solution.py:101
  57.4 1.4 %collective-permute-start.7 = (f32[1,128,128]{2,1,0:T(8,128)}, f32[1,128,128]{2,1,0:T(8,128)}, u32[]{:S(2)}, u32[]{:S(2)}) collective-permute-start(f32[1,128,128]{2,1,0:T(8,128)} %shard_map.66.refs_9_), channel_id=1, source_target_pairs={{0,2},{2,0},{1,3},{3,1},{4,6},{6,4},{5,7},{7,5},{8,10},{10,8},{9,1... | collective-permute-start | bytes 196616 | tf_op jit(solution)/shard_map/ppermute | solution.py:199
  58.9 0.1 pad_add_fusion.2.owners
  59.0 0.1 pad_add_fusion.1.owners
  59.0 0.1 pad_add_fusion.owners
  59.1 0.0 collective-permute-done.2.refs_3_.refs_4_
  59.1 0.0 copy-done.4
  59.1 0.0 copy-start.3
  59.1 3.4 %copy-done.3 = bf16[1024,4096]{1,0:T(8,128)(2,1)S(1)} copy-done((bf16[1024,4096]{1,0:T(8,128)(2,1)S(1)}, bf16[1024,4096]{1,0:T(8,128)(2,1)}, u32[]{:S(2)}) %copy-start.3) | copy-done | bytes 8388632
  62.5 4.8 %shard_map.67.refs_11_.refs_13_ = f32[2,128,128]{2,1,0:T(8,128)} custom-call(s32[1024]{0:T(1024)S(1)} %copy-done.6, s32[8]{0:T(128)S(1)} %copy-done.7, s32[2]{0:T(128)S(1)} %pad_add_fusion.owners, bf16[1024,4096]{1,0:T(8,128)(2,1)S(1)} %copy-done.3, bf16[1024,4096]{1,0:T(8,128)(2,1)S(1)} %copy-done.3, ...), custom_call_target="tpu_custom_call" | custom-call | flops 1073741824 | bytes 6291456 | tf_op jit(solution)/shard_map/pallas_call | solution.py:101
  67.3 0.6 collective-permute-start.8
  67.9 0.0 collective-permute-done.4.refs_3_.refs_6_
  67.9 0.0 slice-start
  67.9 4.5 %shard_map.68.refs_15_.refs_17_ = f32[2,128,128]{2,1,0:T(8,128)} custom-call(s32[1024]{0:T(1024)S(1)} %copy-done.6, s32[8]{0:T(128)S(1)} %copy-done.7, s32[2]{0:T(128)S(1)} %pad_add_fusion.1.owners, bf16[1024,4096]{1,0:T(8,128)(2,1)S(1)} %copy-done.3, bf16[1024,4096]{1,0:T(8,128)(2,1)S(1)} %copy-done.3, ...), custom_call_target="tpu_custom_call" | custom-call | flops 1073741824 | bytes 6291456 | tf_op jit(solution)/shard_map/pallas_call | solution.py:101
  72.4 0.0 slice-start.1
  72.4 1.4 %collective-permute-start.9 = (f32[2,128,128]{2,1,0:T(8,128)}, f32[2,128,128]{2,1,0:T(8,128)}, u32[]{:S(2)}, u32[]{:S(2)}) collective-permute-start(f32[2,128,128]{2,1,0:T(8,128)} %shard_map.68.refs_15_.refs_17_), channel_id=1, source_target_pairs={{0,2},{2,0},{1,3},{3,1},{4,6},{6,4},{5,7},{7,5},{8,10},{10,8},{9,1... | collective-permute-start | bytes 393224 | tf_op jit(solution)/shard_map/ppermute | solution.py:199
  73.8 0.0 collective-permute-done.6.refs_3_.refs_8_
  73.8 3.3 %shard_map.69.refs_19_.refs_21_ = f32[2,128,128]{2,1,0:T(8,128)} custom-call(s32[1024]{0:T(1024)S(1)} %copy-done.6, s32[8]{0:T(128)S(1)} %copy-done.7, s32[2]{0:T(128)S(1)} %pad_add_fusion.2.owners, bf16[1024,4096]{1,0:T(8,128)(2,1)S(1)} %copy-done.3, bf16[1024,4096]{1,0:T(8,128)(2,1)S(1)} %copy-done.3, ...), custom_call_target="tpu_custom_call" | custom-call | flops 1073741824 | bytes 6291456 | tf_op jit(solution)/shard_map/pallas_call | solution.py:101
  77.1 0.6 collective-permute-start.10
  77.8 0.0 slice-done
  77.8 0.0 slice-done.1
  77.8 7.3 %shard_map.64.refs_0_ = f32[1024,512]{1,0:T(8,128)S(1)} custom-call(s32[1]{0:T(128)} %bitcast.7.column, bf16[1024,4096]{1,0:T(8,128)(2,1)S(1)} %bitcast.14, bf16[4096,1024]{1,0:T(8,128)(2,1)} %w_ref.3), custom_call_target="tpu_custom_call" | custom-call | flops 4294967296 | bytes 14680064 | tf_op jit(solution)/shard_map/pallas_call | solution.py:48
  85.1 0.1 stack.47.owners
  85.2 15.7 %collective-permute-done.7.refs_10_ = f32[1,128,128]{2,1,0:T(8,128)} collective-permute-done((f32[1,128,128]{2,1,0:T(8,128)}, f32[1,128,128]{2,1,0:T(8,128)}, u32[]{:S(2)}, u32[]{:S(2)}) %collective-permute-start.7) | collective-permute-done | bytes 65568 | tf_op jit(solution)/shard_map/ppermute | solution.py:199
  100.8 0.0 collective-permute-done.refs_1_
  100.8 2.8 %collective-permute-done.8.refs_12_.refs_14_ = f32[2,128,128]{2,1,0:T(8,128)} collective-permute-done((f32[2,128,128]{2,1,0:T(8,128)}, f32[2,128,128]{2,1,0:T(8,128)}, u32[]{:S(2)}, u32[]{:S(2)}) %collective-permute-start.8) | collective-permute-done | bytes 131104 | tf_op jit(solution)/shard_map/ppermute | solution.py:199
  103.7 2.8 %collective-permute-done.9.refs_16_.refs_18_ = f32[2,128,128]{2,1,0:T(8,128)} collective-permute-done((f32[2,128,128]{2,1,0:T(8,128)}, f32[2,128,128]{2,1,0:T(8,128)}, u32[]{:S(2)}, u32[]{:S(2)}) %collective-permute-start.9) | collective-permute-done | bytes 131104 | tf_op jit(solution)/shard_map/ppermute | solution.py:199
  106.5 2.0 %collective-permute-done.10.refs_20_.refs_22_ = f32[2,128,128]{2,1,0:T(8,128)} collective-permute-done((f32[2,128,128]{2,1,0:T(8,128)}, f32[2,128,128]{2,1,0:T(8,128)}, u32[]{:S(2)}, u32[]{:S(2)}) %collective-permute-start.10) | collective-permute-done | bytes 131104 | tf_op jit(solution)/shard_map/ppermute | solution.py:199
  108.4 0.0 copy-start.5
  108.4 1.3 %copy-done.5 = bf16[128,4608]{1,0:T(8,128)(2,1)S(1)} copy-done((bf16[128,4608]{1,0:T(8,128)(2,1)S(1)}, bf16[128,4608]{1,0:T(8,128)(2,1)}, u32[]{:S(2)}) %copy-start.5) | copy-done | bytes 1179672
  109.7 7.9 %shard_map.70 = bf16[1024,512]{1,0:T(8,128)(2,1)} custom-call(s32[1024]{0:T(1024)S(1)} %copy-done.6, s32[8]{0:T(128)S(1)} %copy-done.7, s32[7]{0:T(128)S(1)} %stack.47.owners, f32[1024,512]{1,0:T(8,128)S(1)} %shard_map.64.refs_0_, f32[1024,512]{1,0:T(8,128)} %collective-permute-done.refs_1_, bf16[128,4608]{1,0:T(8,128)(2,1)S(1)} %pad_maximum_fusion.refs_2_, ...), custom_call_target="tpu_custom_call" | custom-call | flops 201326592 | bytes 5242880 | tf_op jit(solution)/shard_map/pallas_call | solution.py:160
  (2 shorter events, 0.0 us)
Async XLA Ops:
  0.0 1.0 copy-start
  2.3 18.1 %collective-permute-start.1 = (bf16[128,4608]{1,0:T(8,128)(2,1)S(1)}, bf16[128,4608]{1,0:T(8,128)(2,1)S(1)}, u32[]{:S(2)}, u32[]{:S(2)}) collective-permute-start(bf16[128,4608]{1,0:T(8,128)(2,1)S(1)} %pad_maximum_fusion.refs_2_), channel_id=1, source_target_pairs={{0,4},{4,8},{8,12},{5,1},{9,5},{13,9},{2,6},{6,10},{10,14},{7,3},{... | collective-permute-start | bytes 3538952 | tf_op jit(solution)/shard_map/ppermute | solution.py:204
  20.4 38.7 %copy-start.4 = (bf16[128,4608]{1,0:T(8,128)(2,1)}, bf16[128,4608]{1,0:T(8,128)(2,1)S(1)}, u32[]{:S(2)}) copy-start(bf16[128,4608]{1,0:T(8,128)(2,1)S(1)} %collective-permute-done.1.refs_2_.refs_3_) | copy-start | bytes 3538948
  20.4 17.2 %collective-permute-start.3 = (bf16[128,4608]{1,0:T(8,128)(2,1)S(1)}, bf16[128,4608]{1,0:T(8,128)(2,1)}, u32[]{:S(2)}, u32[]{:S(2)}) collective-permute-start(bf16[128,4608]{1,0:T(8,128)(2,1)S(1)} %collective-permute-done.1.refs_2_.refs_3_), channel_id=1, source_target_pairs={{4,8},{8,12},{5,1},{9,5},{6,10},{10,14},{7,3},{11,7},{20,24},{24,2... | collective-permute-start | bytes 3538952 | tf_op jit(solution)/shard_map/ppermute | solution.py:204
  37.6 14.1 %collective-permute-start.5 = (bf16[128,4608]{1,0:T(8,128)(2,1)}, bf16[128,4608]{1,0:T(8,128)(2,1)}, u32[]{:S(2)}, u32[]{:S(2)}) collective-permute-start(bf16[128,4608]{1,0:T(8,128)(2,1)} %collective-permute-done.3.refs_2_.refs_5_), channel_id=1, source_target_pairs={{8,12},{5,1},{10,14},{7,3},{24,28},{21,17},{26,30},{23,19}} | collective-permute-start | bytes 3538952 | tf_op jit(solution)/shard_map/ppermute | solution.py:204
  39.2 3.4 %copy-start.1 = (bf16[1024,4096]{1,0:T(8,128)(2,1)S(1)}, bf16[1024,4096]{1,0:T(8,128)(2,1)}, u32[]{:S(2)}) copy-start(bf16[1024,4096]{1,0:T(8,128)(2,1)} %refs_1_.7) | copy-start | bytes 25165828
  42.6 9.1 %copy-start.6 = (s32[1024]{0:T(1024)S(1)}, s32[1024]{0:T(1024)}, u32[]{:S(2)}) copy-start(s32[1024]{0:T(1024)} %ids.9) | copy-start | bytes 12292
  42.6 9.1 %copy-start.7 = (s32[8]{0:T(128)S(1)}, s32[8]{0:T(128)}, u32[]{:S(2)}) copy-start(s32[8]{0:T(128)} %slots.9) | copy-start | bytes 100
  50.6 50.2 %collective-permute-start = (f32[1024,512]{1,0:T(8,128)}, f32[1024,512]{1,0:T(8,128)}, u32[]{:S(2)}, u32[]{:S(2)}) collective-permute-start(f32[1024,512]{1,0:T(8,128)} %shard_map.65), channel_id=1, source_target_pairs={{0,2},{2,0},{1,3},{3,1},{4,6},{6,4},{5,7},{7,5},{8,10},{10,8},{9,1... | collective-permute-start | bytes 6291464 | tf_op jit(solution)/shard_map/ppermute | solution.py:199
  51.2 7.9 %collective-permute-start.2 = (bf16[128,4608]{1,0:T(8,128)(2,1)S(1)}, bf16[128,4608]{1,0:T(8,128)(2,1)}, u32[]{:S(2)}, u32[]{:S(2)}) collective-permute-start(bf16[128,4608]{1,0:T(8,128)(2,1)S(1)} %collective-permute-done.1.refs_2_.refs_3_), channel_id=1, source_target_pairs={{0,1},{1,0},{2,3},{3,2},{4,5},{5,4},{6,7},{7,6},{8,9},{9,8},{10,11... | collective-permute-start | bytes 3538952 | tf_op jit(solution)/shard_map/ppermute | solution.py:207
  51.2 16.7 %collective-permute-start.4 = (bf16[128,4608]{1,0:T(8,128)(2,1)}, bf16[128,4608]{1,0:T(8,128)(2,1)}, u32[]{:S(2)}, u32[]{:S(2)}) collective-permute-start(bf16[128,4608]{1,0:T(8,128)(2,1)} %collective-permute-done.3.refs_2_.refs_5_), channel_id=1, source_target_pairs={{0,1},{1,0},{2,3},{3,2},{4,5},{5,4},{6,7},{7,6},{8,9},{9,8},{10,11... | collective-permute-start | bytes 3538952 | tf_op jit(solution)/shard_map/ppermute | solution.py:207
  51.7 22.1 %collective-permute-start.6 = (bf16[128,4608]{1,0:T(8,128)(2,1)}, bf16[128,4608]{1,0:T(8,128)(2,1)}, u32[]{:S(2)}, u32[]{:S(2)}) collective-permute-start(bf16[128,4608]{1,0:T(8,128)(2,1)} %collective-permute-done.5.refs_2_.refs_7_), channel_id=1, source_target_pairs={{0,1},{1,0},{2,3},{3,2},{4,5},{5,4},{6,7},{7,6},{8,9},{9,8},{10,11... | collective-permute-start | bytes 3538952 | tf_op jit(solution)/shard_map/ppermute | solution.py:207
  51.8 3.4 %copy-start.2 = (bf16[1024,4096]{1,0:T(8,128)(2,1)S(1)}, bf16[1024,4096]{1,0:T(8,128)(2,1)}, u32[]{:S(2)}) copy-start(bf16[1024,4096]{1,0:T(8,128)(2,1)} %refs_1_.7) | copy-start | bytes 25165828
  57.4 43.4 %collective-permute-start.7 = (f32[1,128,128]{2,1,0:T(8,128)}, f32[1,128,128]{2,1,0:T(8,128)}, u32[]{:S(2)}, u32[]{:S(2)}) collective-permute-start(f32[1,128,128]{2,1,0:T(8,128)} %shard_map.66.refs_9_), channel_id=1, source_target_pairs={{0,2},{2,0},{1,3},{3,1},{4,6},{6,4},{5,7},{7,5},{8,10},{10,8},{9,1... | collective-permute-start | bytes 196616 | tf_op jit(solution)/shard_map/ppermute | solution.py:199
  59.1 3.4 %copy-start.3 = (bf16[1024,4096]{1,0:T(8,128)(2,1)S(1)}, bf16[1024,4096]{1,0:T(8,128)(2,1)}, u32[]{:S(2)}) copy-start(bf16[1024,4096]{1,0:T(8,128)(2,1)} %refs_1_.7) | copy-start | bytes 25165828
  67.3 36.4 %collective-permute-start.8 = (f32[2,128,128]{2,1,0:T(8,128)}, f32[2,128,128]{2,1,0:T(8,128)}, u32[]{:S(2)}, u32[]{:S(2)}) collective-permute-start(f32[2,128,128]{2,1,0:T(8,128)} %shard_map.67.refs_11_.refs_13_), channel_id=1, source_target_pairs={{0,2},{2,0},{1,3},{3,1},{4,6},{6,4},{5,7},{7,5},{8,10},{10,8},{9,1... | collective-permute-start | bytes 393224 | tf_op jit(solution)/shard_map/ppermute | solution.py:199
  67.9 9.9 %slice-start = ((s8[8388608]{0:T(1024)(128)(4,1)}), s8[4194304]{0:T(1024)(128)(4,1)S(1)}, s32[]{:S(2)}) async-start(s8[8388608]{0:T(1024)(128)(4,1)} %bitcast.13), calls=%async_computation | async-start | bytes 8388608
  72.4 5.4 %slice-start.1 = ((s8[8388608]{0:T(1024)(128)(4,1)}), s8[4194304]{0:T(1024)(128)(4,1)S(1)}, s32[]{:S(2)}) async-start(s8[8388608]{0:T(1024)(128)(4,1)} %bitcast.13), calls=%async_computation.1 | async-start | bytes 8388608
  72.4 34.1 %collective-permute-start.9 = (f32[2,128,128]{2,1,0:T(8,128)}, f32[2,128,128]{2,1,0:T(8,128)}, u32[]{:S(2)}, u32[]{:S(2)}) collective-permute-start(f32[2,128,128]{2,1,0:T(8,128)} %shard_map.68.refs_15_.refs_17_), channel_id=1, source_target_pairs={{0,2},{2,0},{1,3},{3,1},{4,6},{6,4},{5,7},{7,5},{8,10},{10,8},{9,1... | collective-permute-start | bytes 393224 | tf_op jit(solution)/shard_map/ppermute | solution.py:199
  77.1 31.3 %collective-permute-start.10 = (f32[2,128,128]{2,1,0:T(8,128)}, f32[2,128,128]{2,1,0:T(8,128)}, u32[]{:S(2)}, u32[]{:S(2)}) collective-permute-start(f32[2,128,128]{2,1,0:T(8,128)} %shard_map.69.refs_19_.refs_21_), channel_id=1, source_target_pairs={{0,2},{2,0},{1,3},{3,1},{4,6},{6,4},{5,7},{7,5},{8,10},{10,8},{9,1... | collective-permute-start | bytes 393224 | tf_op jit(solution)/shard_map/ppermute | solution.py:199
  108.4 1.3 %copy-start.5 = (bf16[128,4608]{1,0:T(8,128)(2,1)S(1)}, bf16[128,4608]{1,0:T(8,128)(2,1)}, u32[]{:S(2)}) copy-start(bf16[128,4608]{1,0:T(8,128)(2,1)} %copy-done.4) | copy-start | bytes 3538948

commit v3 on v1

v3 whole, which is shorter than its diff:
```python
import functools

import jax
import jax.numpy as jnp
from jax import lax
from jax.experimental import pallas as pl
from jax.experimental.pallas import tpu as pltpu
from jax.sharding import PartitionSpec as P

SEGMENT_ROWS = 128
adapter_scale = 0.5
VMEM_BYTES = 56 * 2**20
MOST = 2
CHUNKS = ((256, 3), (384, 0), (384, 1))
DEPTH = 1024
LIMIT = 2.0**23 - 1


def cost(flops, moved):
    return pl.CostEstimate(flops=int(flops), bytes_accessed=int(moved), transcendentals=0)


def params():
    return pltpu.CompilerParams(vmem_limit_bytes=VMEM_BYTES)


ANY = pl.BlockSpec(memory_space=pl.ANY)
SMEM = pl.BlockSpec(memory_space=pltpu.SMEM)


def segment_slot(ids, slots, s):
    return slots[ids[s * SEGMENT_ROWS]]


def find_segment(ids, slots, per_device, seg_dev, owner, number):
    found, within, count = jnp.int32(-1), jnp.int32(0), jnp.int32(0)
    for s in range(seg_dev):
        slot = segment_slot(ids, slots, s)
        hit = lax.div(slot, jnp.int32(per_device)) == owner
        take = hit & (count == number)
        found = jnp.where(take, s, found)
        within = jnp.where(take, lax.rem(slot, jnp.int32(per_device)), within)
        count = count + hit.astype(jnp.int32)
    return found, within


def arrival_order(me, n_adapter):
    order = [me] + [jnp.int32(-1)] * (n_adapter - 1)
    count = jnp.int32(1)
    for distance in range(1, n_adapter):
        for other in (me - distance, me + distance):
            valid = (other >= 0) & (other < n_adapter)
            order = [jnp.where(valid & (count == k), other, o) for k, o in enumerate(order)]
            count = count + valid.astype(jnp.int32)
    return order


def buffer_owners(me, core, stages):
    owners = {0: [me]}
    for stage in stages:
        if stage > 0:
            toward = jnp.where(core == 0, -stage, stage)
            owners[stage] = [me + toward, me - toward]
    return [o for stage in stages for o in owners[stage]]


def pack_kernel(place, down_ref, up_ref, o_ref, sems):
    width = down_ref.shape[1]
    columns = o_ref.shape[1] - width
    start = pl.multiple_of(place[0] * columns, columns)
    copies = [
        pltpu.make_async_copy(down_ref, o_ref.at[:, pl.ds(0, width)], sems.at[0]),
        pltpu.make_async_copy(
            up_ref.at[:, pl.ds(start, columns)], o_ref.at[:, pl.ds(width, columns)], sems.at[1]
        ),
    ]
    for copy in copies:
        copy.start()
    for copy in copies:
        copy.wait()


def pack_message(down, up, place, columns):
    rows, width = down.shape
    return pl.pallas_call(
        pack_kernel,
        in_specs=[SMEM, ANY, ANY],
        out_specs=ANY,
        out_shape=jax.ShapeDtypeStruct((rows, width + columns), jnp.bfloat16),
        scratch_shapes=[pltpu.SemaphoreType.DMA((2,))],
        compiler_params=params(),
        cost_estimate=cost(0, 4 * rows * (width + columns)),
    )(place.reshape(1), down, up)


def diagonal():
    shape = (SEGMENT_ROWS, SEGMENT_ROWS)
    return lax.broadcasted_iota(jnp.int32, shape, 0) == lax.broadcasted_iota(jnp.int32, shape, 1)


def coded_rows(rows):
    return rows * 3 // 4 + 8


def encode(values, o_ref):
    rows = values.shape[0]
    quarter = rows // 4
    largest = jnp.maximum(jnp.max(jnp.abs(values), axis=1, keepdims=True), 2.0**-100)
    power = jnp.floor(jnp.log2(largest))
    scaled = jnp.clip(jnp.round(values * jnp.exp2(22.0 - power)), -LIMIT, LIMIT)
    whole = scaled.astype(jnp.int32)
    q = [whole[i * quarter : (i + 1) * quarter] for i in range(4)]
    for i in range(3):
        o_ref[i * quarter : (i + 1) * quarter, :] = (q[i] & 0xFFFFFF) | ((q[3] >> (8 * i)) << 24)
    o_ref[3 * quarter :, :] = jnp.zeros((8, values.shape[1]), jnp.int32)
    for h in range(rows // SEGMENT_ROWS):
        column = power[h * SEGMENT_ROWS : (h + 1) * SEGMENT_ROWS]
        row = jnp.sum(jnp.where(diagonal(), column, 0.0), axis=0, keepdims=True)
        o_ref[3 * quarter + h : 3 * quarter + h + 1, :SEGMENT_ROWS] = row.astype(jnp.int32)


def decode(words, rows):
    quarter = rows // 4
    w = [words[i * quarter : (i + 1) * quarter] for i in range(3)]
    q = [(x << 8) >> 8 for x in w]
    q.append(((w[0] >> 24) & 0xFF) | (((w[1] >> 24) & 0xFF) << 8) | ((w[2] >> 24) << 16))
    powers = []
    for h in range(rows // SEGMENT_ROWS):
        row = words[3 * quarter + h : 3 * quarter + h + 1, :SEGMENT_ROWS].astype(jnp.float32)
        powers.append(jnp.sum(jnp.where(diagonal(), row, 0.0), axis=1, keepdims=True))
    scale = jnp.exp2(jnp.concatenate(powers, axis=0) - 22.0)
    return jnp.concatenate(q, axis=0).astype(jnp.float32) * scale


def base_kernel(coded, column, x_ref, w_ref, o_ref, total):
    del column
    step = pl.program_id(0)
    product = jnp.dot(x_ref[...], w_ref[...], preferred_element_type=jnp.float32)

    @pl.when(step == 0)
    def _():
        total[...] = product

    @pl.when(step > 0)
    def _():
        total[...] += product

    @pl.when(step == pl.num_programs(0) - 1)
    def _():
        if coded:
            encode(total[...], o_ref)
        else:
            o_ref[...] = total[...]


def base_product(tokens, weight, column, columns, rows, place, coded):
    width = tokens.shape[1]
    depth = min(DEPTH, width)
    out_rows = coded_rows(rows) if coded else rows
    return pl.pallas_call(
        functools.partial(base_kernel, coded),
        grid_spec=pltpu.PrefetchScalarGridSpec(
            num_scalar_prefetch=1,
            grid=(width // depth,),
            in_specs=[
                pl.BlockSpec((rows, depth), lambda i, c: (place, i)),
                pl.BlockSpec((depth, columns), lambda i, c: (i, c[0])),
            ],
            out_specs=pl.BlockSpec((out_rows, columns), lambda i, c: (0, 0)),
            scratch_shapes=[pltpu.VMEM((rows, columns), jnp.float32)],
        ),
        out_shape=jax.ShapeDtypeStruct((out_rows, columns), jnp.int32 if coded else jnp.float32),
        compiler_params=params(),
        cost_estimate=cost(
            2 * rows * width * columns, 2 * rows * width + 2 * width * columns + 4 * rows * columns
        ),
    )(column.reshape(1), tokens, weight)


def shrink_kernel(ks, stages, n_adapter, per_device, rank, ids, slots, here, x_ref, *refs):
    buffers, (o_ref, x, d, sems) = refs[:-4], refs[-4:]
    rows, width = x_ref.shape
    seg_dev = rows // SEGMENT_ROWS
    order = arrival_order(here[0], n_adapter)
    owners = buffer_owners(here[0], here[1], stages)
    work = []
    for i, k in enumerate(ks):
        for buffer, whose in zip(buffers, owners):
            down = pltpu.make_async_copy(buffer.at[:, pl.ds(0, width)], d.at[i], sems.at[i, MOST])
            pl.when(whose == order[k])(down.start)
        for j in range(MOST):
            seg, within = find_segment(ids, slots, per_device, seg_dev, order[k], j)
            start = pl.multiple_of(jnp.maximum(seg, 0) * SEGMENT_ROWS, SEGMENT_ROWS)
            load = pltpu.make_async_copy(
                x_ref.at[pl.ds(start, SEGMENT_ROWS), :], x.at[i, j], sems.at[i, j]
            )
            load.start()
            work.append((i, j, within, load, down))
    for i, j, within, load, down in work:
        if j == 0:
            down.wait()
        load.wait()
        factor = d[i, pl.ds(pl.multiple_of(within * rank, rank), rank), :]
        o_ref[i, :, j * rank : (j + 1) * rank] = lax.dot_general(
            x[i, j], factor, (((1,), (1,)), ((), ())), preferred_element_type=jnp.float32
        )


def shrink_product(ks, stages, n_adapter, tokens, ids, slots, here, buffers, per_device, rank):
    width = tokens.shape[1]
    n = len(ks)
    return pl.pallas_call(
        functools.partial(shrink_kernel, ks, stages, n_adapter, per_device, rank),
        in_specs=[SMEM, SMEM, SMEM, ANY] + [ANY] * len(buffers),
        out_specs=pl.BlockSpec(memory_space=pltpu.VMEM),
        out_shape=jax.ShapeDtypeStruct((n, SEGMENT_ROWS, MOST * rank), jnp.float32),
        scratch_shapes=[
            pltpu.VMEM((n, MOST, SEGMENT_ROWS, width), jnp.bfloat16),
            pltpu.VMEM((n, per_device * rank, width), jnp.bfloat16),
            pltpu.SemaphoreType.DMA((n, MOST + 1)),
        ],
        compiler_params=params(),
        cost_estimate=cost(
            n * MOST * 2 * SEGMENT_ROWS * width * 256,
            n * 2 * (MOST * SEGMENT_ROWS + per_device * rank) * width,
        ),
    )(ids, slots, here, tokens, *buffers)


def up_product(shrink, factor):
    high = shrink.astype(jnp.bfloat16)
    left = shrink - high.astype(jnp.float32)
    middle = left.astype(jnp.bfloat16)
    low = (left - middle.astype(jnp.float32)).astype(jnp.bfloat16)
    result = jnp.dot(low, factor, preferred_element_type=jnp.float32)
    result = result + jnp.dot(middle, factor, preferred_element_type=jnp.float32)
    return result + jnp.dot(high, factor, preferred_element_type=jnp.float32)


def fetch_up(buffers, owners, owner, target, sem):
    columns = target.shape[1]
    for buffer, whose in zip(buffers, owners):
        copy = pltpu.make_async_copy(
            buffer.at[:, pl.ds(buffer.shape[1] - columns, columns)], target, sem
        )
        pl.when(whose == owner)(copy.start)
    return copy


def early_kernel(n_adapter, n_tensor, n_calls, per_device, rank, ids, slots, here, *refs):
    n_chunks = len(CHUNKS)
    base_ref, coded_refs, refs = refs[0], refs[1 : 1 + n_chunks * (n_tensor - 1)], refs[1 + n_chunks * (n_tensor - 1) :]
    shrinks, refs = refs[: n_calls * n_tensor], refs[n_calls * n_tensor :]
    buffers, (o_ref, rest_ref, up, total, sems) = refs[:-5], refs[-5:]
    seg_dev = base_ref.shape[0] // SEGMENT_ROWS
    order = arrival_order(here[0], n_adapter)
    owners = buffer_owners(here[0], here[1], range(n_adapter - 1))
    waits = [
        fetch_up(buffers, owners, order[k], up.at[k], sems.at[k]) for k in range(n_adapter - 1)
    ]
    shares = []
    for call in range(n_calls):
        share = shrinks[call * n_tensor][...]
        for i in range(1, n_tensor):
            share = share + shrinks[call * n_tensor + i][...]
        shares += [share[i] for i in range(share.shape[0])]
    for chunk, (rows, place) in enumerate(CHUNKS):
        here_rows = pl.ds(place * rows, rows)
        value = base_ref[here_rows, :]
        for i in range(n_tensor - 1):
            value = value + decode(coded_refs[chunk * (n_tensor - 1) + i][...], rows)
        total[here_rows, :] = value
    for copy in waits:
        copy.wait()
    for k in range(n_adapter):
        for j in range(MOST):
            seg, within = find_segment(ids, slots, per_device, seg_dev, order[k], j)
            start = pl.multiple_of(jnp.maximum(seg, 0) * SEGMENT_ROWS, SEGMENT_ROWS)
            value = total[pl.ds(start, SEGMENT_ROWS), :]
            if k == n_adapter - 1:
                rest_ref[j] = value
                continue
            factor = up[k, pl.ds(pl.multiple_of(within * rank, rank), rank), :]
            lora = up_product(shares[k][:, j * rank : (j + 1) * rank], factor)

            @pl.when(seg >= 0)
            def _(start=start, value=value, lora=lora):
                o_ref[pl.ds(start, SEGMENT_ROWS), :] = (value + adapter_scale * lora).astype(
                    jnp.bfloat16
                )


def early(n_adapter, n_tensor, ids, slots, here, base, coded, shrinks, buffers, per_device, rank):
    rows, columns = base.shape
    vmem = pl.BlockSpec(memory_space=pltpu.VMEM)
    return pl.pallas_call(
        functools.partial(
            early_kernel, n_adapter, n_tensor, len(shrinks) // n_tensor, per_device, rank
        ),
        in_specs=[SMEM] * 3 + [vmem] * (1 + len(coded) + len(shrinks)) + [ANY] * len(buffers),
        out_specs=[vmem, vmem],
        out_shape=[
            jax.ShapeDtypeStruct((rows, columns), jnp.bfloat16),
            jax.ShapeDtypeStruct((MOST, SEGMENT_ROWS, columns), jnp.float32),
        ],
        scratch_shapes=[
            pltpu.VMEM((n_adapter - 1, per_device * rank, columns), jnp.bfloat16),
            pltpu.VMEM((rows, columns), jnp.float32),
            pltpu.SemaphoreType.DMA((n_adapter - 1,)),
        ],
        compiler_params=params(),
        cost_estimate=cost(6 * rows * rank * columns, (4 * n_tensor + 2) * rows * columns),
    )(ids, slots, here, base, *coded, *shrinks, *buffers)


def late_kernel(n_adapter, n_tensor, stages, per_device, rank, ids, slots, here, *refs):
    rest_ref, shrinks, refs = refs[0], refs[1 : 1 + n_tensor], refs[1 + n_tensor :]
    buffers, (_, o_ref, up, out, sems) = refs[:-5], refs[-5:]
    seg_dev = o_ref.shape[0] // SEGMENT_ROWS
    owner = arrival_order(here[0], n_adapter)[-1]
    owners = buffer_owners(here[0], here[1], stages)
    wait = fetch_up(buffers, owners, owner, up, sems.at[MOST])
    share = shrinks[0][0]
    for r in shrinks[1:]:
        share = share + r[0]
    wait.wait()
    stores = []
    for j in range(MOST):
        seg, within = find_segment(ids, slots, per_device, seg_dev, owner, j)
        start = pl.multiple_of(jnp.maximum(seg, 0) * SEGMENT_ROWS, SEGMENT_ROWS)
        factor = up[pl.ds(pl.multiple_of(within * rank, rank), rank), :]
        lora = up_product(share[:, j * rank : (j + 1) * rank], factor)
        out[j] = (rest_ref[j] + adapter_scale * lora).astype(jnp.bfloat16)
        store = pltpu.make_async_copy(out.at[j], o_ref.at[pl.ds(start, SEGMENT_ROWS), :], sems.at[j])
        pl.when(seg >= 0)(store.start)
        stores.append((seg, store))
    for seg, store in stores:
        pl.when(seg >= 0)(store.wait)


def late(n_adapter, n_tensor, stages, ids, slots, here, rest, shrinks, buffers, value, per_device, rank):
    rows, columns = value.shape
    vmem = pl.BlockSpec(memory_space=pltpu.VMEM)
    return pl.pallas_call(
        functools.partial(late_kernel, n_adapter, n_tensor, stages, per_device, rank),
        in_specs=[SMEM] * 3 + [vmem] * (1 + len(shrinks)) + [ANY] * (len(buffers) + 1),
        out_specs=ANY,
        out_shape=jax.ShapeDtypeStruct((rows, columns), jnp.bfloat16),
        scratch_shapes=[
            pltpu.VMEM((per_device * rank, columns), jnp.bfloat16),
            pltpu.VMEM((MOST, SEGMENT_ROWS, columns), jnp.bfloat16),
            pltpu.SemaphoreType.DMA((MOST + 1,)),
        ],
        input_output_aliases={4 + len(shrinks) + len(buffers): 0},
        compiler_params=params(),
        cost_estimate=cost(
            6 * MOST * SEGMENT_ROWS * rank * columns, 8 * MOST * SEGMENT_ROWS * columns
        ),
    )(ids, slots, here, rest, *shrinks, *buffers, value)


def after(array, *others):
    return lax.optimization_barrier((array, *others))[0]


def on_device(
    tokens, value_weight, adapter_down_weight, adapter_up_weight, row_adapter_index, adapter_slot_of
):
    rows, width = tokens.shape
    per_device, _, rank = adapter_down_weight.shape
    n_adapter = lax.axis_size("adapter")
    n_tensor = lax.axis_size("tensor")
    me_t = lax.axis_index("tensor")
    here = jnp.stack([lax.axis_index("adapter"), lax.axis_index("dp")])
    columns = value_weight.shape[1] // n_tensor
    ids, slots = row_adapter_index, adapter_slot_of

    def swap_tensor(array, step):
        pairs = [(i, (i + step) % n_tensor) for i in range(n_tensor)]
        return lax.ppermute(array, "tensor", pairs)

    def along_line(array, stage):
        up = [(2 * i, 2 * (i + 1)) for i in range(stage - 1, n_adapter - 1)]
        down = [(2 * i + 1, 2 * (i - 1) + 1) for i in range(1, n_adapter - stage + 1)]
        return lax.ppermute(array, ("adapter", "dp"), up + down)

    def swap_cores(array):
        return lax.ppermute(array, "dp", [(0, 1), (1, 0)])

    down = jnp.swapaxes(adapter_down_weight, 1, 2).reshape(per_device * rank, width)
    up = adapter_up_weight.reshape(per_device * rank, value_weight.shape[1])
    message = pack_message(down, up, me_t, columns)

    buffers, shrinks = [[message]], []

    def stage_buffers(stages):
        return [b for stage in stages for b in buffers[stage]]

    def shrink(ks, stages):
        mine = shrink_product(
            ks, stages, n_adapter, tokens, ids, slots, here, stage_buffers(stages), per_device, rank
        )
        shrinks.extend([mine] + [swap_tensor(mine, step) for step in range(1, n_tensor)])
        return shrinks[-n_tensor:]

    held = along_line(message, 1)
    parts = [
        [
            base_product(tokens, value_weight, (me_t + step) % n_tensor, columns, size, place, True)
            for step in range(1, n_tensor)
        ]
        for size, place in CHUNKS
    ]
    sent = [[swap_tensor(p, step + 1) for step, p in enumerate(parts[0])]]
    done = [p for group in parts for p in group] + sent[0]
    for stage in range(1, n_adapter):
        if stage < len(CHUNKS):
            sent.append([swap_tensor(after(p, held), step + 1) for step, p in enumerate(parts[stage])])
        if stage == n_adapter - 1:
            value, rest = early(
                n_adapter,
                n_tensor,
                ids,
                slots,
                here,
                base,
                [c for group in sent for c in group],
                shrinks,
                stage_buffers(range(n_adapter - 1)),
                per_device,
                rank,
            )
            done = [value]
        held = after(held, *done)
        done = sent[stage] if stage < len(CHUNKS) else []
        came = held
        if stage < n_adapter - 1:
            held = along_line(came, stage + 1)
        buffers.append([came, swap_cores(came)])
        if stage == 1:
            base = base_product(tokens, value_weight, me_t, columns, rows, 0, False)
            done = done + [base, shrink([0, 1], [0, 1])[0]]
        else:
            stages = list(range((stage + 1) // 2, stage + 1))
            done = done + [shrink([stage], stages)[0]]

    return late(
        n_adapter,
        n_tensor,
        stages,
        ids,
        slots,
        here,
        rest,
        shrinks[-n_tensor:],
        stage_buffers(stages),
        value,
        per_device,
        rank,
    )


def solution(mesh):
    return jax.shard_map(
        on_device,
        mesh=mesh,
        in_specs=(
            P(("groups", "adapter", "dp"), "tensor"),
            P("tensor", None),
            P(("groups", "adapter"), "tensor", None),
            P(("groups", "adapter"), None, None),
            P(("groups", "adapter", "dp")),
            P("groups"),
        ),
        out_specs=P(("groups", "adapter", "dp"), "tensor"),
        check_vma=False,
    )
```

time: 92.7 us -> 127 us (1.37)
  the two profiles are of different devices: /device:TPU:0 before, /device:TPU:16 now
where the time goes in v3:
time: 127 us; the launch traced here: 125 us
  Pallas kernels  87.9 us (69%)
  waiting for transfers between devices  15.9 us (13%)
  starting transfers between devices  14.7 us (12%)
  local copies, waits for them, and re-layouts  5.32 us (4%)
    pallas_call x1, Pallas kernels, pack_message(): pl.pallas_call(pack_kernel, in_specs=[SMEM, ANY, ANY], out_specs=ANY, out...  36.9 us
    pallas_call x4, Pallas kernels, base_product(): pl.pallas_call(functools.partial(base_kernel, coded), grid_spec=pltpu.Pre...  27.1 us
    pallas_call x3, Pallas kernels, shrink_product(): pl.pallas_call(functools.partial(shrink_kernel, ks, stages, n_adapter, pe...  14.6 us
    ppermute x6, waiting for transfers between devices, swap_tensor(): return lax.ppermute(array, 'tensor', pairs)  13.1 us
    ppermute x6, starting transfers between devices, swap_tensor(): return lax.ppermute(array, 'tensor', pairs)  7.35 us
    ppermute x3, starting transfers between devices, along_line(): return lax.ppermute(array, ('adapter', 'dp'), up + down)  6.75 us
    pallas_call x1, Pallas kernels, early(): pl.pallas_call(functools.partial(early_kernel, n_adapter, n_tensor, len(s...  6.25 us
    unnamed x26, local copies, waits for them, and re-layouts  5.32 us
  transfers between devices with their start and end apart: 12, of which 4 were waited for; matrix products, arithmetic and copies ran while one was open for 0% of the time, Pallas kernels for 35%

profile of v3, /device:TPU:16, one launch (start us, length us, event | category | flops | bytes accessed | tf_op | source)
XLA Modules:
  0.0 124.6 jit_solution(11221370164880872361)
XLA Ops:
  0.0 36.9 %shard_map.67.refs_0_.refs_8_ = bf16[128,4608]{1,0:T(8,128)(2,1)} custom-call(s32[1]{0:T(128)} %bitcast.2.column.place, bf16[128,4096]{1,0:T(8,128)(2,1)} %bitcast.8, bf16[128,1024]{1,0:T(8,128)(2,1)} %bitcast.9), custom_call_target="tpu_custom_call" | custom-call | bytes 2359296 | tf_op jit(solution)/shard_map/pallas_call | solution.py:85
  36.9 3.5 %collective-permute-start.1 = (bf16[128,4608]{1,0:T(8,128)(2,1)}, bf16[128,4608]{1,0:T(8,128)(2,1)S(1)}, u32[]{:S(2)}, u32[]{:S(2)}) collective-permute-start(bf16[128,4608]{1,0:T(8,128)(2,1)} %shard_map.67.refs_0_.refs_8_), channel_id=1, source_target_pairs={{0,4},{4,8},{8,12},{5,1},{9,5},{13,9},{2,6},{6,10},{10,14},{7,3},{... | collective-permute-start | bytes 3538952 | tf_op jit(solution)/shard_map/ppermute | solution.py:385
  40.4 5.4 %shard_map.65 = s32[200,512]{1,0:T(8,128)} custom-call(s32[1]{0:T(128)} %bitcast.3.column, bf16[1024,4096]{1,0:T(8,128)(2,1)} %x_ref.13, bf16[4096,1024]{1,0:T(8,128)(2,1)} %w_ref.7), custom_call_target="tpu_custom_call" | custom-call | flops 1073741824 | bytes 6815744 | tf_op jit(solution)/shard_map/pallas_call | solution.py:160
  45.7 1.5 %collective-permute-start = (s32[200,512]{1,0:T(8,128)}, s32[200,512]{1,0:T(8,128)S(1)}, u32[]{:S(2)}, u32[]{:S(2)}) collective-permute-start(s32[200,512]{1,0:T(8,128)} %shard_map.65), channel_id=1, source_target_pairs={{0,2},{2,0},{1,3},{3,1},{4,6},{6,4},{5,7},{7,5},{8,10},{10,8},{9,1... | collective-permute-start | bytes 1228808 | tf_op jit(solution)/shard_map/ppermute | solution.py:380
  47.2 6.1 %shard_map.66 = s32[296,512]{1,0:T(8,128)} custom-call(s32[1]{0:T(128)} %bitcast.3.column, bf16[1024,4096]{1,0:T(8,128)(2,1)} %x_ref.13, bf16[4096,1024]{1,0:T(8,128)(2,1)} %w_ref.7), custom_call_target="tpu_custom_call" | custom-call | flops 1610612736 | bytes 8126464 | tf_op jit(solution)/shard_map/pallas_call | solution.py:160
  53.3 6.1 %shard_map.68 = s32[296,512]{1,0:T(8,128)} custom-call(s32[1]{0:T(128)} %bitcast.3.column, bf16[1024,4096]{1,0:T(8,128)(2,1)} %x_ref.13, bf16[4096,1024]{1,0:T(8,128)(2,1)} %w_ref.7), custom_call_target="tpu_custom_call" | custom-call | flops 1610612736 | bytes 8126464 | tf_op jit(solution)/shard_map/pallas_call | solution.py:160
  59.4 0.0 collective-permute-done.refs_1_
  59.5 0.0 copy-start.9
  59.5 0.0 collective-permute-done.1.refs_1_.refs_0_.refs_9_
  59.5 0.7 copy-done.9
  60.2 0.0 copy-start.2
  60.2 0.0 collective-permute-start.5
  60.2 1.9 %collective-permute-start.3 = (bf16[128,4608]{1,0:T(8,128)(2,1)S(1)}, bf16[128,4608]{1,0:T(8,128)(2,1)S(1)}, u32[]{:S(2)}, u32[]{:S(2)}) collective-permute-start(bf16[128,4608]{1,0:T(8,128)(2,1)S(1)} %collective-permute-done.1.refs_1_.refs_0_.refs_9_), channel_id=1, source_target_pairs={{4,8},{8,12},{5,1},{9,5},{6,10},{10,14},{7,3},{11,7},{20,24},{24,2... | collective-permute-start | bytes 3538952 | tf_op jit(solution)/shard_map/ppermute | solution.py:385
  62.1 0.6 collective-permute-start.2
  62.7 0.6 pad_add_fusion.here
  63.2 9.6 %shard_map.64.refs_0_ = f32[1024,512]{1,0:T(8,128)} custom-call(s32[1]{0:T(128)} %bitcast.2.column.place, bf16[1024,4096]{1,0:T(8,128)(2,1)} %x_ref.13, bf16[4096,1024]{1,0:T(8,128)(2,1)} %w_ref.7), custom_call_target="tpu_custom_call" | custom-call | flops 4294967296 | bytes 14680064 | tf_op jit(solution)/shard_map/pallas_call | solution.py:160
  72.8 0.0 copy-done.2
  72.8 0.0 copy-start.8
  72.8 0.0 collective-permute-done.5.refs_2_.refs_1_.refs_10_
  72.8 0.0 copy-start.3
  72.8 1.0 copy-done.3
  73.8 5.9 %shard_map.69.refs_4_ = f32[2,128,128]{2,1,0:T(8,128)} custom-call(s32[1024]{0:T(1024)} %ids.9, s32[8]{0:T(128)} %slots.9, s32[2]{0:T(128)} %pad_add_fusion.here, bf16[1024,4096]{1,0:T(8,128)(2,1)} %x_ref.13, bf16[128,4608]{1,0:T(8,128)(2,1)} %shard_map.67.refs_0_.refs_8_, bf16[128,4608]{1,0:T(8,128)(2,1)} %copy-done.2, bf16[128,4608]{1,0:T(8,128)(2,1)} %copy-done.3), custom_call_target="tpu_custom_call" | custom-call | flops 1073741824 | bytes 6291456 | tf_op jit(solution)/shard_map/pallas_call | solution.py:212
  79.7 0.0 collective-permute-done.2.refs_2_
  79.7 0.0 copy-start.6
  79.7 0.0 collective-permute-done.3.refs_2_.refs_11_.refs_0_.refs_3_
  79.7 0.0 copy-start
  79.7 0.5 collective-permute-start.7
  80.3 1.4 %collective-permute-start.9 = (bf16[128,4608]{1,0:T(8,128)(2,1)S(1)}, bf16[128,4608]{1,0:T(8,128)(2,1)S(1)}, u32[]{:S(2)}, u32[]{:S(2)}) collective-permute-start(bf16[128,4608]{1,0:T(8,128)(2,1)S(1)} %collective-permute-done.3.refs_2_.refs_11_.refs_0_.refs_3_), channel_id=1, source_target_pairs={{8,12},{5,1},{10,14},{7,3},{24,28},{21,17},{26,30},{23,19}} | collective-permute-start | bytes 3538952 | tf_op jit(solution)/shard_map/ppermute | solution.py:385
  81.6 0.0 copy-done.8
  81.6 1.6 %collective-permute-start.4 = (s32[296,512]{1,0:T(8,128)S(1)}, s32[296,512]{1,0:T(8,128)S(1)}, u32[]{:S(2)}, u32[]{:S(2)}) collective-permute-start(s32[296,512]{1,0:T(8,128)S(1)} %copy-done.8), channel_id=1, source_target_pairs={{0,2},{2,0},{1,3},{3,1},{4,6},{6,4},{5,7},{7,5},{8,10},{10,8},{9,1... | collective-permute-start | bytes 1818632 | tf_op jit(solution)/shard_map/ppermute | solution.py:380
  83.2 0.5 collective-permute-start.6
  83.7 0.0 collective-permute-done.7.refs_3_.refs_12_.refs_1_.refs_4_
  83.7 0.0 copy-done
  83.7 0.0 copy-start.1
  83.7 1.1 copy-done.1
  84.8 4.4 %shard_map.70.refs_6_ = f32[1,128,128]{2,1,0:T(8,128)} custom-call(s32[1024]{0:T(1024)} %ids.9, s32[8]{0:T(128)} %slots.9, s32[2]{0:T(128)} %pad_add_fusion.here, bf16[1024,4096]{1,0:T(8,128)(2,1)} %x_ref.13, bf16[128,4608]{1,0:T(8,128)(2,1)} %copy-done.2, bf16[128,4608]{1,0:T(8,128)(2,1)} %copy-done.3, bf16[128,4608]{1,0:T(8,128)(2,1)} %copy-done, ...), custom_call_target="tpu_custom_call" | custom-call | flops 536870912 | bytes 3145728 | tf_op jit(solution)/shard_map/pallas_call | solution.py:212
  89.2 0.0 copy-done.6
  89.2 1.6 %collective-permute-start.8 = (f32[1,128,128]{2,1,0:T(8,128)}, f32[1,128,128]{2,1,0:T(8,128)S(1)}, u32[]{:S(2)}, u32[]{:S(2)}) collective-permute-start(f32[1,128,128]{2,1,0:T(8,128)} %shard_map.70.refs_6_), channel_id=1, source_target_pairs={{0,2},{2,0},{1,3},{3,1},{4,6},{6,4},{5,7},{7,5},{8,10},{10,8},{9,1... | collective-permute-start | bytes 196616 | tf_op jit(solution)/shard_map/ppermute | solution.py:380
  90.8 9.4 %collective-permute-done.6.refs_5_ = f32[2,128,128]{2,1,0:T(8,128)S(1)} collective-permute-done((f32[2,128,128]{2,1,0:T(8,128)}, f32[2,128,128]{2,1,0:T(8,128)S(1)}, u32[]{:S(2)}, u32[]{:S(2)}) %collective-permute-start.6) | collective-permute-done | bytes 131104 | tf_op jit(solution)/shard_map/ppermute | solution.py:380
  100.2 0.0 copy-start.10
  100.2 0.0 collective-permute-done.4.refs_3_
  100.2 0.0 copy-start.7
  100.2 0.7 collective-permute-done.8.refs_7_
  100.9 0.0 copy-done.10
  100.9 0.2 copy-done.7
  101.2 0.0 copy-start.11
  101.2 0.6 copy-done.11
  101.8 6.3 %shard_map.71 = (bf16[1024,512]{1,0:T(8,128)(2,1)}, f32[2,128,512]{2,1,0:T(8,128)}) custom-call(s32[1024]{0:T(1024)} %ids.9, s32[8]{0:T(128)} %slots.9, s32[2]{0:T(128)} %pad_add_fusion.here, f32[1024,512]{1,0:T(8,128)} %shard_map.64.refs_0_, s32[200,512]{1,0:T(8,128)} %copy-done.9, s32[296,512]{1,0:T(8,128)} %copy-done.6, s32[296,512]{1,0:T(8,128)} %copy-done.7, ...), custom_call_target="tpu_custom_call" | custom-call | flops 201326592 | bytes 5242880 | tf_op jit(solution)/shard_map/pallas_call | solution.py:296
  108.0 0.0 collective-permute-done.9.refs_2_.refs_5_
  108.1 0.0 copy-start.4
  108.1 0.1 collective-permute-start.10
  108.1 2.8 %collective-permute-done.10.refs_3_.refs_6_ = bf16[128,4608]{1,0:T(8,128)(2,1)S(1)} collective-permute-done((bf16[128,4608]{1,0:T(8,128)(2,1)S(1)}, bf16[128,4608]{1,0:T(8,128)(2,1)S(1)}, u32[]{:S(2)}, u32[]{:S(2)}) %collective-permute-start.10) | collective-permute-done | bytes 1179680 | tf_op jit(solution)/shard_map/ppermute | solution.py:388
  111.0 0.0 copy-done.4
  111.0 0.0 copy-start.5
  111.0 1.0 copy-done.5
  112.0 4.4 %shard_map.72.refs_1_ = f32[1,128,128]{2,1,0:T(8,128)} custom-call(s32[1024]{0:T(1024)} %ids.9, s32[8]{0:T(128)} %slots.9, s32[2]{0:T(128)} %pad_add_fusion.here, bf16[1024,4096]{1,0:T(8,128)(2,1)} %x_ref.13, bf16[128,4608]{1,0:T(8,128)(2,1)} %copy-done, bf16[128,4608]{1,0:T(8,128)(2,1)} %copy-done.1, bf16[128,4608]{1,0:T(8,128)(2,1)} %copy-done.4, ...), custom_call_target="tpu_custom_call" | custom-call | flops 536870912 | bytes 3145728 | tf_op jit(solution)/shard_map/pallas_call | solution.py:212
  116.4 1.6 %collective-permute-start.11 = (f32[1,128,128]{2,1,0:T(8,128)}, f32[1,128,128]{2,1,0:T(8,128)S(1)}, u32[]{:S(2)}, u32[]{:S(2)}) collective-permute-start(f32[1,128,128]{2,1,0:T(8,128)} %shard_map.72.refs_1_), channel_id=1, source_target_pairs={{0,2},{2,0},{1,3},{3,1},{4,6},{6,4},{5,7},{7,5},{8,10},{10,8},{9,1... | collective-permute-start | bytes 196616 | tf_op jit(solution)/shard_map/ppermute | solution.py:380
  117.9 3.0 %collective-permute-done.11.refs_2_ = f32[1,128,128]{2,1,0:T(8,128)S(1)} collective-permute-done((f32[1,128,128]{2,1,0:T(8,128)}, f32[1,128,128]{2,1,0:T(8,128)S(1)}, u32[]{:S(2)}, u32[]{:S(2)}) %collective-permute-start.11) | collective-permute-done | bytes 65568 | tf_op jit(solution)/shard_map/ppermute | solution.py:380
  120.9 0.0 copy-start.12
  120.9 0.6 copy-done.12
  121.5 3.1 %shard_map.73 = bf16[1024,512]{1,0:T(8,128)(2,1)} custom-call(s32[1024]{0:T(1024)} %ids.9, s32[8]{0:T(128)} %slots.9, s32[2]{0:T(128)} %pad_add_fusion.here, f32[2,128,512]{2,1,0:T(8,128)} %get-tuple-element.16.refs_0_, f32[1,128,128]{2,1,0:T(8,128)} %shard_map.72.refs_1_, f32[1,128,128]{2,1,0:T(8,128)} %copy-done.12, ...), custom_call_target="tpu_custom_call", output_to_operand_aliasing={{}: (10, {})} | custom-call | flops 50331648 | bytes 1048576 | tf_op jit(solution)/shard_map/pallas_call | solution.py:344
Async XLA Ops:
  36.9 22.6 %collective-permute-start.1 = (bf16[128,4608]{1,0:T(8,128)(2,1)}, bf16[128,4608]{1,0:T(8,128)(2,1)S(1)}, u32[]{:S(2)}, u32[]{:S(2)}) collective-permute-start(bf16[128,4608]{1,0:T(8,128)(2,1)} %shard_map.67.refs_0_.refs_8_), channel_id=1, source_target_pairs={{0,4},{4,8},{8,12},{5,1},{9,5},{13,9},{2,6},{6,10},{10,14},{7,3},{... | collective-permute-start | bytes 3538952 | tf_op jit(solution)/shard_map/ppermute | solution.py:385
  45.7 13.7 %collective-permute-start = (s32[200,512]{1,0:T(8,128)}, s32[200,512]{1,0:T(8,128)S(1)}, u32[]{:S(2)}, u32[]{:S(2)}) collective-permute-start(s32[200,512]{1,0:T(8,128)} %shard_map.65), channel_id=1, source_target_pairs={{0,2},{2,0},{1,3},{3,1},{4,6},{6,4},{5,7},{7,5},{8,10},{10,8},{9,1... | collective-permute-start | bytes 1228808 | tf_op jit(solution)/shard_map/ppermute | solution.py:380
  59.5 0.7 copy-start.9
  60.2 12.6 %copy-start.2 = (bf16[128,4608]{1,0:T(8,128)(2,1)}, bf16[128,4608]{1,0:T(8,128)(2,1)S(1)}, u32[]{:S(2)}) copy-start(bf16[128,4608]{1,0:T(8,128)(2,1)S(1)} %collective-permute-done.1.refs_1_.refs_0_.refs_9_) | copy-start | bytes 3538948
  60.2 12.6 %collective-permute-start.5 = (bf16[128,4608]{1,0:T(8,128)(2,1)S(1)}, bf16[128,4608]{1,0:T(8,128)(2,1)S(1)}, u32[]{:S(2)}, u32[]{:S(2)}) collective-permute-start(bf16[128,4608]{1,0:T(8,128)(2,1)S(1)} %collective-permute-done.1.refs_1_.refs_0_.refs_9_), channel_id=1, source_target_pairs={{0,1},{1,0},{2,3},{3,2},{4,5},{5,4},{6,7},{7,6},{8,9},{9,8},{10,11... | collective-permute-start | bytes 3538952 | tf_op jit(solution)/shard_map/ppermute | solution.py:388
  60.2 19.5 %collective-permute-start.3 = (bf16[128,4608]{1,0:T(8,128)(2,1)S(1)}, bf16[128,4608]{1,0:T(8,128)(2,1)S(1)}, u32[]{:S(2)}, u32[]{:S(2)}) collective-permute-start(bf16[128,4608]{1,0:T(8,128)(2,1)S(1)} %collective-permute-done.1.refs_1_.refs_0_.refs_9_), channel_id=1, source_target_pairs={{4,8},{8,12},{5,1},{9,5},{6,10},{10,14},{7,3},{11,7},{20,24},{24,2... | collective-permute-start | bytes 3538952 | tf_op jit(solution)/shard_map/ppermute | solution.py:385
  62.1 17.6 %collective-permute-start.2 = (s32[296,512]{1,0:T(8,128)}, s32[296,512]{1,0:T(8,128)S(1)}, u32[]{:S(2)}, u32[]{:S(2)}) collective-permute-start(s32[296,512]{1,0:T(8,128)} %shard_map.66), channel_id=1, source_target_pairs={{0,2},{2,0},{1,3},{3,1},{4,6},{6,4},{5,7},{7,5},{8,10},{10,8},{9,1... | collective-permute-start | bytes 1818632 | tf_op jit(solution)/shard_map/ppermute | solution.py:380
  72.8 8.8 %copy-start.8 = (s32[296,512]{1,0:T(8,128)S(1)}, s32[296,512]{1,0:T(8,128)}, u32[]{:S(2)}) copy-start(s32[296,512]{1,0:T(8,128)} %shard_map.68) | copy-start | bytes 1818628
  72.8 1.0 copy-start.3
  79.7 9.5 %copy-start.6 = (s32[296,512]{1,0:T(8,128)}, s32[296,512]{1,0:T(8,128)S(1)}, u32[]{:S(2)}) copy-start(s32[296,512]{1,0:T(8,128)S(1)} %collective-permute-done.2.refs_2_) | copy-start | bytes 1818628
  79.7 4.0 %copy-start = (bf16[128,4608]{1,0:T(8,128)(2,1)}, bf16[128,4608]{1,0:T(8,128)(2,1)S(1)}, u32[]{:S(2)}) copy-start(bf16[128,4608]{1,0:T(8,128)(2,1)S(1)} %collective-permute-done.3.refs_2_.refs_11_.refs_0_.refs_3_) | copy-start | bytes 3538948
  79.7 4.0 %collective-permute-start.7 = (bf16[128,4608]{1,0:T(8,128)(2,1)S(1)}, bf16[128,4608]{1,0:T(8,128)(2,1)S(1)}, u32[]{:S(2)}, u32[]{:S(2)}) collective-permute-start(bf16[128,4608]{1,0:T(8,128)(2,1)S(1)} %collective-permute-done.3.refs_2_.refs_11_.refs_0_.refs_3_), channel_id=1, source_target_pairs={{0,1},{1,0},{2,3},{3,2},{4,5},{5,4},{6,7},{7,6},{8,9},{9,8},{10,11... | collective-permute-start | bytes 3538952 | tf_op jit(solution)/shard_map/ppermute | solution.py:388
  80.3 27.8 %collective-permute-start.9 = (bf16[128,4608]{1,0:T(8,128)(2,1)S(1)}, bf16[128,4608]{1,0:T(8,128)(2,1)S(1)}, u32[]{:S(2)}, u32[]{:S(2)}) collective-permute-start(bf16[128,4608]{1,0:T(8,128)(2,1)S(1)} %collective-permute-done.3.refs_2_.refs_11_.refs_0_.refs_3_), channel_id=1, source_target_pairs={{8,12},{5,1},{10,14},{7,3},{24,28},{21,17},{26,30},{23,19}} | collective-permute-start | bytes 3538952 | tf_op jit(solution)/shard_map/ppermute | solution.py:385
  81.6 18.6 %collective-permute-start.4 = (s32[296,512]{1,0:T(8,128)S(1)}, s32[296,512]{1,0:T(8,128)S(1)}, u32[]{:S(2)}, u32[]{:S(2)}) collective-permute-start(s32[296,512]{1,0:T(8,128)S(1)} %copy-done.8), channel_id=1, source_target_pairs={{0,2},{2,0},{1,3},{3,1},{4,6},{6,4},{5,7},{7,5},{8,10},{10,8},{9,1... | collective-permute-start | bytes 1818632 | tf_op jit(solution)/shard_map/ppermute | solution.py:380
  83.2 17.0 %collective-permute-start.6 = (f32[2,128,128]{2,1,0:T(8,128)}, f32[2,128,128]{2,1,0:T(8,128)S(1)}, u32[]{:S(2)}, u32[]{:S(2)}) collective-permute-start(f32[2,128,128]{2,1,0:T(8,128)} %shard_map.69.refs_4_), channel_id=1, source_target_pairs={{0,2},{2,0},{1,3},{3,1},{4,6},{6,4},{5,7},{7,5},{8,10},{10,8},{9,1... | collective-permute-start | bytes 393224 | tf_op jit(solution)/shard_map/ppermute | solution.py:380
  83.7 1.1 copy-start.1
  89.2 11.7 %collective-permute-start.8 = (f32[1,128,128]{2,1,0:T(8,128)}, f32[1,128,128]{2,1,0:T(8,128)S(1)}, u32[]{:S(2)}, u32[]{:S(2)}) collective-permute-start(f32[1,128,128]{2,1,0:T(8,128)} %shard_map.70.refs_6_), channel_id=1, source_target_pairs={{0,2},{2,0},{1,3},{3,1},{4,6},{6,4},{5,7},{7,5},{8,10},{10,8},{9,1... | collective-permute-start | bytes 196616 | tf_op jit(solution)/shard_map/ppermute | solution.py:380
  100.2 0.7 copy-start.10
  100.2 0.9 copy-start.7
  101.2 0.6 copy-start.11
  108.1 2.9 %copy-start.4 = (bf16[128,4608]{1,0:T(8,128)(2,1)}, bf16[128,4608]{1,0:T(8,128)(2,1)S(1)}, u32[]{:S(2)}) copy-start(bf16[128,4608]{1,0:T(8,128)(2,1)S(1)} %collective-permute-done.9.refs_2_.refs_5_) | copy-start | bytes 3538948
  108.1 2.9 %collective-permute-start.10 = (bf16[128,4608]{1,0:T(8,128)(2,1)S(1)}, bf16[128,4608]{1,0:T(8,128)(2,1)S(1)}, u32[]{:S(2)}, u32[]{:S(2)}) collective-permute-start(bf16[128,4608]{1,0:T(8,128)(2,1)S(1)} %collective-permute-done.9.refs_2_.refs_5_), channel_id=1, source_target_pairs={{0,1},{1,0},{2,3},{3,2},{4,5},{5,4},{6,7},{7,6},{8,9},{9,8},{10,11... | collective-permute-start | bytes 3538952 | tf_op jit(solution)/shard_map/ppermute | solution.py:388
  111.0 1.0 copy-start.5
  116.4 4.5 %collective-permute-start.11 = (f32[1,128,128]{2,1,0:T(8,128)}, f32[1,128,128]{2,1,0:T(8,128)S(1)}, u32[]{:S(2)}, u32[]{:S(2)}) collective-permute-start(f32[1,128,128]{2,1,0:T(8,128)} %shard_map.72.refs_1_), channel_id=1, source_target_pairs={{0,2},{2,0},{1,3},{3,1},{4,6},{6,4},{5,7},{7,5},{8,10},{10,8},{9,1... | collective-permute-start | bytes 196616 | tf_op jit(solution)/shard_map/ppermute | solution.py:380
  120.9 0.6 copy-start.12

commit v4 on v3

v4 whole, which is shorter than its diff:
```python
import functools

import jax
import jax.numpy as jnp
from jax import lax
from jax.experimental import pallas as pl
from jax.experimental.pallas import tpu as pltpu
from jax.sharding import PartitionSpec as P

SEGMENT_ROWS = 128
adapter_scale = 0.5
MOST = 2
BLOCK = 256
PIECES = 4
CHUNKS = ((6, 2), (0, 3), (3, 3))
ENTRIES = 8
MIDDLE = 1.5 * 2.0**23


def cost(flops, moved):
    return pl.CostEstimate(flops=int(flops), bytes_accessed=int(moved), transcendentals=0)


def params(mib):
    return pltpu.CompilerParams(vmem_limit_bytes=mib * 2**20)


ANY = pl.BlockSpec(memory_space=pl.ANY)
HBM = pl.BlockSpec(memory_space=pltpu.HBM)
SMEM = pl.BlockSpec(memory_space=pltpu.SMEM)
VMEM = pl.BlockSpec(memory_space=pltpu.VMEM)


def arrival_order(me, n_adapter):
    order = [me] + [jnp.int32(-1)] * (n_adapter - 1)
    count = jnp.int32(1)
    for distance in range(1, n_adapter):
        for other in (me - distance, me + distance):
            valid = (other >= 0) & (other < n_adapter)
            order = [jnp.where(valid & (count == k), other, o) for k, o in enumerate(order)]
            count = count + valid.astype(jnp.int32)
    return order


def buffer_owners(here, stages):
    owners = []
    for stage in stages:
        toward = jnp.where(here[1] == 0, -stage, stage)
        owners += [here[0] + toward, here[0] - toward] if stage > 0 else [here[0]]
    return owners


def segment_of(table, k, j):
    seg = table[k * ENTRIES + 1 + 2 * j]
    start = pl.multiple_of(jnp.maximum(seg, 0) * SEGMENT_ROWS, SEGMENT_ROWS)
    return start, seg >= 0, table[k * ENTRIES + 2 + 2 * j]


def open_kernel(n_adapter, per_device, here, ids, slots, down_ref, up_ref, o_ref, table, sems):
    width = down_ref.shape[1]
    columns = o_ref.shape[1] - width
    start = pl.multiple_of(here[2] * columns, columns)
    copies = [
        pltpu.make_async_copy(down_ref, o_ref.at[:, pl.ds(0, width)], sems.at[0]),
        pltpu.make_async_copy(
            up_ref.at[:, pl.ds(start, columns)], o_ref.at[:, pl.ds(width, columns)], sems.at[1]
        ),
    ]
    for copy in copies:
        copy.start()
    seg_dev = ids.shape[0] // SEGMENT_ROWS
    used = [slots[ids[s * SEGMENT_ROWS]] for s in range(seg_dev)]
    for k, owner in enumerate(arrival_order(here[0], n_adapter)):
        table[k * ENTRIES] = owner
        found, place = [jnp.int32(-1)] * MOST, [jnp.int32(0)] * MOST
        count = jnp.int32(0)
        for s, slot in enumerate(used):
            within = slot - owner * per_device
            hit = (within >= 0) & (within < per_device)
            for j in range(MOST):
                take = hit & (count == j)
                found[j] = jnp.where(take, s, found[j])
                place[j] = jnp.where(take, within, place[j])
            count = count + hit.astype(jnp.int32)
        for j in range(MOST):
            table[k * ENTRIES + 1 + 2 * j] = found[j]
            table[k * ENTRIES + 2 + 2 * j] = place[j]
    for copy in copies:
        copy.wait()


def open_call(here, ids, slots, down, up, n_adapter, per_device, columns):
    rows, width = down.shape
    return pl.pallas_call(
        functools.partial(open_kernel, n_adapter, per_device),
        in_specs=[SMEM, SMEM, SMEM, HBM, HBM],
        out_specs=[VMEM, SMEM],
        out_shape=[
            jax.ShapeDtypeStruct((rows, width + columns), jnp.bfloat16),
            jax.ShapeDtypeStruct((n_adapter * ENTRIES,), jnp.int32),
        ],
        scratch_shapes=[pltpu.SemaphoreType.DMA((2,))],
        compiler_params=params(8),
        cost_estimate=cost(0, 4 * rows * (width + columns)),
    )(here, ids, slots, down, up)


def diagonal():
    shape = (SEGMENT_ROWS, SEGMENT_ROWS)
    return lax.broadcasted_iota(jnp.int32, shape, 0) == lax.broadcasted_iota(jnp.int32, shape, 1)


WORDS = SEGMENT_ROWS * 3 // 4
QUARTER = SEGMENT_ROWS // 4


def coded_rows(segments):
    return segments * WORDS + 8


def encode(values, o_ref, unit, units):
    largest = jnp.maximum(jnp.max(jnp.abs(values), axis=1, keepdims=True), 2.0**-100)
    power = jnp.floor(jnp.log2(largest))
    whole = (values * jnp.exp2(21.0 - power) + MIDDLE).astype(jnp.int32) - int(MIDDLE)
    q = [whole[i * QUARTER : (i + 1) * QUARTER] for i in range(4)]
    for i in range(3):
        o_ref[unit * WORDS + i * QUARTER : unit * WORDS + (i + 1) * QUARTER, :] = (
            q[i] & 0xFFFFFF
        ) | ((q[3] >> (8 * i)) << 24)
    row = jnp.sum(jnp.where(diagonal(), power, 0.0), axis=0, keepdims=True)
    o_ref[units * WORDS + unit : units * WORDS + unit + 1, :SEGMENT_ROWS] = row.astype(jnp.int32)


def decode(ref, unit, units):
    w = [ref[unit * WORDS + i * QUARTER : unit * WORDS + (i + 1) * QUARTER, :] for i in range(3)]
    q = [(x << 8) >> 8 for x in w]
    q.append(((w[0] >> 24) & 0xFF) | (((w[1] >> 24) & 0xFF) << 8) | ((w[2] >> 24) << 16))
    row = ref[units * WORDS + unit : units * WORDS + unit + 1, :SEGMENT_ROWS].astype(jnp.float32)
    power = jnp.sum(jnp.where(diagonal(), row, 0.0), axis=1, keepdims=True)
    return jnp.concatenate(q, axis=0).astype(jnp.float32) * jnp.exp2(power - 21.0)


def base_kernel(first, sizes, coded, column, x_ref, w_ref, *refs):
    outs, (x, w, sems) = refs[: len(sizes)], refs[len(sizes) :]
    width, columns = w.shape
    rows = sum(sizes) * SEGMENT_ROWS
    start = pl.multiple_of(column[0] * columns, columns)
    depth = width // PIECES
    blocks = [(r, min(BLOCK, rows - r)) for r in range(0, rows, BLOCK)]

    def x_copy(at, size, features, sem):
        return pltpu.make_async_copy(
            x_ref.at[pl.ds(first * SEGMENT_ROWS + at, size), features],
            x.at[pl.ds(at, size), features],
            sem,
        )

    pieces = []
    for p in range(PIECES):
        features = pl.ds(p * depth, depth)
        pieces.append(
            (
                pltpu.make_async_copy(
                    w_ref.at[features, pl.ds(start, columns)], w.at[features, :], sems.at[0, p]
                ),
                x_copy(0, blocks[0][1], features, sems.at[1, p]),
            )
        )
    later = [x_copy(at, size, slice(None), sems.at[2, i]) for i, (at, size) in enumerate(blocks[1:])]
    for copy in [c for pair in pieces for c in pair] + later:
        copy.start()
    owner = [(out, unit) for out, size in enumerate(sizes) for unit in range(size)]
    if coded:
        for out, size in zip(outs, sizes):
            out[size * WORDS :, :] = jnp.zeros((8, columns), jnp.int32)
    for i, (at, size) in enumerate(blocks):
        if i == 0:
            product = None
            for p, pair in enumerate(pieces):
                for copy in pair:
                    copy.wait()
                term = jnp.dot(
                    x[at : at + size, p * depth : (p + 1) * depth],
                    w[p * depth : (p + 1) * depth, :],
                    preferred_element_type=jnp.float32,
                )
                product = term if product is None else product + term
        else:
            later[i - 1].wait()
            product = jnp.dot(x[at : at + size, :], w[...], preferred_element_type=jnp.float32)
        if not coded:
            outs[0][at : at + size, :] = product
            continue
        for r in range(0, size, SEGMENT_ROWS):
            out, unit = owner[(at + r) // SEGMENT_ROWS]
            encode(product[r : r + SEGMENT_ROWS], outs[out], unit, sizes[out])


def base_product(tokens, weight, column, columns, first, sizes, coded):
    width = tokens.shape[1]
    rows = sum(sizes) * SEGMENT_ROWS
    kind = jnp.int32 if coded else jnp.float32
    shapes = [coded_rows(n) if coded else n * SEGMENT_ROWS for n in sizes]
    return pl.pallas_call(
        functools.partial(base_kernel, first, sizes, coded),
        in_specs=[SMEM, HBM, HBM],
        out_specs=[VMEM] * len(sizes),
        out_shape=[jax.ShapeDtypeStruct((n, columns), kind) for n in shapes],
        scratch_shapes=[
            pltpu.VMEM((rows, width), jnp.bfloat16),
            pltpu.VMEM((width, columns), jnp.bfloat16),
            pltpu.SemaphoreType.DMA((3, max(PIECES, rows // BLOCK))),
        ],
        compiler_params=params(24),
        cost_estimate=cost(
            2 * rows * width * columns, 2 * rows * width + 2 * width * columns + 4 * rows * columns
        ),
    )(column.reshape(1), tokens, weight)


def shrink_kernel(ks, stages, rank, table, here, x_ref, *refs):
    buffers, (o_ref, x, d, sems) = refs[:-4], refs[-4:]
    width = x_ref.shape[1]
    owners = buffer_owners(here, stages)
    work = []
    for i, k in enumerate(ks):
        for buffer, whose in zip(buffers, owners):
            down = pltpu.make_async_copy(buffer.at[:, pl.ds(0, width)], d.at[i], sems.at[i, MOST])
            pl.when(whose == table[k * ENTRIES])(down.start)
        for j in range(MOST):
            start, _, within = segment_of(table, k, j)
            load = pltpu.make_async_copy(
                x_ref.at[pl.ds(start, SEGMENT_ROWS), :], x.at[i, j], sems.at[i, j]
            )
            load.start()
            work.append((i, j, within, load, down))
    for i, j, within, load, down in work:
        if j == 0:
            down.wait()
        load.wait()
        factor = d[i, pl.ds(pl.multiple_of(within * rank, rank), rank), :]
        o_ref[i, :, j * rank : (j + 1) * rank] = lax.dot_general(
            x[i, j], factor, (((1,), (1,)), ((), ())), preferred_element_type=jnp.float32
        )


def shrink_product(ks, stages, table, here, tokens, buffers, per_device, rank):
    width = tokens.shape[1]
    n = len(ks)
    return pl.pallas_call(
        functools.partial(shrink_kernel, ks, stages, rank),
        in_specs=[SMEM, SMEM, HBM] + [ANY] * len(buffers),
        out_specs=VMEM,
        out_shape=jax.ShapeDtypeStruct((n, SEGMENT_ROWS, MOST * rank), jnp.float32),
        scratch_shapes=[
            pltpu.VMEM((n, MOST, SEGMENT_ROWS, width), jnp.bfloat16),
            pltpu.VMEM((n, per_device * rank, width), jnp.bfloat16),
            pltpu.SemaphoreType.DMA((n, MOST + 1)),
        ],
        compiler_params=params(16),
        cost_estimate=cost(
            n * MOST * 2 * SEGMENT_ROWS * width * 256,
            n * 2 * (MOST * SEGMENT_ROWS + per_device * rank) * width,
        ),
    )(table, here, tokens, *buffers)


def up_product(shrink, factor):
    high = shrink.astype(jnp.bfloat16)
    left = shrink - high.astype(jnp.float32)
    middle = left.astype(jnp.bfloat16)
    low = (left - middle.astype(jnp.float32)).astype(jnp.bfloat16)
    result = jnp.dot(low, factor, preferred_element_type=jnp.float32)
    result = result + jnp.dot(middle, factor, preferred_element_type=jnp.float32)
    return result + jnp.dot(high, factor, preferred_element_type=jnp.float32)


def fetch_up(buffers, owners, owner, target, sem):
    columns = target.shape[1]
    for buffer, whose in zip(buffers, owners):
        copy = pltpu.make_async_copy(
            buffer.at[:, pl.ds(buffer.shape[1] - columns, columns)], target, sem
        )
        pl.when(whose == owner)(copy.start)
    return copy


def early_kernel(n_adapter, n_tensor, n_calls, rank, table, here, *refs):
    n_coded = len(CHUNKS) * (n_tensor - 1)
    base_ref, coded_refs, refs = refs[0], refs[1 : 1 + n_coded], refs[1 + n_coded :]
    shrinks, refs = refs[: n_calls * n_tensor], refs[n_calls * n_tensor :]
    buffers, (o_ref, rest_ref, up, total, sems) = refs[:-5], refs[-5:]
    owners = buffer_owners(here, range(n_adapter - 1))
    waits = [
        fetch_up(buffers, owners, table[k * ENTRIES], up.at[k], sems.at[k])
        for k in range(n_adapter - 1)
    ]
    shares = []
    for call in range(n_calls):
        share = shrinks[call * n_tensor][...]
        for i in range(1, n_tensor):
            share = share + shrinks[call * n_tensor + i][...]
        shares += [share[i] for i in range(share.shape[0])]
    for chunk, (first, number) in enumerate(CHUNKS):
        for unit in range(number):
            here_rows = pl.ds((first + unit) * SEGMENT_ROWS, SEGMENT_ROWS)
            value = base_ref[here_rows, :]
            for i in range(n_tensor - 1):
                value = value + decode(coded_refs[chunk * (n_tensor - 1) + i], unit, number)
            total[here_rows, :] = value
    for copy in waits:
        copy.wait()
    for k in range(n_adapter):
        for j in range(MOST):
            start, used, within = segment_of(table, k, j)
            value = total[pl.ds(start, SEGMENT_ROWS), :]
            if k == n_adapter - 1:
                rest_ref[j] = value
                continue
            factor = up[k, pl.ds(pl.multiple_of(within * rank, rank), rank), :]
            lora = up_product(shares[k][:, j * rank : (j + 1) * rank], factor)

            @pl.when(used)
            def _(start=start, value=value, lora=lora):
                o_ref[pl.ds(start, SEGMENT_ROWS), :] = (value + adapter_scale * lora).astype(
                    jnp.bfloat16
                )


def early(n_adapter, n_tensor, table, here, base, coded, shrinks, buffers, per_device, rank):
    rows, columns = base.shape
    return pl.pallas_call(
        functools.partial(early_kernel, n_adapter, n_tensor, len(shrinks) // n_tensor, rank),
        in_specs=[SMEM] * 2 + [VMEM] * (1 + len(coded) + len(shrinks)) + [ANY] * len(buffers),
        out_specs=[VMEM, VMEM],
        out_shape=[
            jax.ShapeDtypeStruct((rows, columns), jnp.bfloat16),
            jax.ShapeDtypeStruct((MOST, SEGMENT_ROWS, columns), jnp.float32),
        ],
        scratch_shapes=[
            pltpu.VMEM((n_adapter - 1, per_device * rank, columns), jnp.bfloat16),
            pltpu.VMEM((rows, columns), jnp.float32),
            pltpu.SemaphoreType.DMA((n_adapter - 1,)),
        ],
        compiler_params=params(16),
        cost_estimate=cost(6 * rows * rank * columns, (4 * n_tensor + 2) * rows * columns),
    )(table, here, base, *coded, *shrinks, *buffers)


def late_kernel(k, n_tensor, stages, rank, table, here, *refs):
    rest_ref, shrinks, refs = refs[0], refs[1 : 1 + n_tensor], refs[1 + n_tensor :]
    buffers, (_, o_ref, up, out, sems) = refs[:-5], refs[-5:]
    owners = buffer_owners(here, stages)
    wait = fetch_up(buffers, owners, table[k * ENTRIES], up, sems.at[MOST])
    share = shrinks[0][0]
    for r in shrinks[1:]:
        share = share + r[0]
    wait.wait()
    stores = []
    for j in range(MOST):
        start, used, within = segment_of(table, k, j)
        factor = up[pl.ds(pl.multiple_of(within * rank, rank), rank), :]
        lora = up_product(share[:, j * rank : (j + 1) * rank], factor)
        out[j] = (rest_ref[j] + adapter_scale * lora).astype(jnp.bfloat16)
        store = pltpu.make_async_copy(out.at[j], o_ref.at[pl.ds(start, SEGMENT_ROWS), :], sems.at[j])
        pl.when(used)(store.start)
        stores.append((used, store))
    for used, store in stores:
        pl.when(used)(store.wait)


def late(k, n_tensor, stages, table, here, rest, shrinks, buffers, value, per_device, rank):
    rows, columns = value.shape
    return pl.pallas_call(
        functools.partial(late_kernel, k, n_tensor, stages, rank),
        in_specs=[SMEM] * 2 + [VMEM] * (1 + len(shrinks)) + [ANY] * (len(buffers) + 1),
        out_specs=ANY,
        out_shape=jax.ShapeDtypeStruct((rows, columns), jnp.bfloat16),
        scratch_shapes=[
            pltpu.VMEM((per_device * rank, columns), jnp.bfloat16),
            pltpu.VMEM((MOST, SEGMENT_ROWS, columns), jnp.bfloat16),
            pltpu.SemaphoreType.DMA((MOST + 1,)),
        ],
        input_output_aliases={3 + len(shrinks) + len(buffers): 0},
        compiler_params=params(8),
        cost_estimate=cost(
            6 * MOST * SEGMENT_ROWS * rank * columns, 8 * MOST * SEGMENT_ROWS * columns
        ),
    )(table, here, rest, *shrinks, *buffers, value)


def after(array, *others):
    return lax.optimization_barrier((array, *others))[0]


def on_device(
    tokens, value_weight, adapter_down_weight, adapter_up_weight, row_adapter_index, adapter_slot_of
):
    rows, width = tokens.shape
    per_device, _, rank = adapter_down_weight.shape
    n_adapter = lax.axis_size("adapter")
    n_tensor = lax.axis_size("tensor")
    me_t = lax.axis_index("tensor")
    here = jnp.stack([lax.axis_index("adapter"), lax.axis_index("dp"), me_t])
    columns = value_weight.shape[1] // n_tensor

    def swap_tensor(array, step):
        pairs = [(i, (i + step) % n_tensor) for i in range(n_tensor)]
        return lax.ppermute(array, "tensor", pairs)

    def along_line(array, stage):
        up = [(2 * i, 2 * (i + 1)) for i in range(stage - 1, n_adapter - 1)]
        down = [(2 * i + 1, 2 * (i - 1) + 1) for i in range(1, n_adapter - stage + 1)]
        return lax.ppermute(array, ("adapter", "dp"), up + down)

    def swap_cores(array):
        return lax.ppermute(array, "dp", [(0, 1), (1, 0)])

    down = jnp.swapaxes(adapter_down_weight, 1, 2).reshape(per_device * rank, width)
    up = adapter_up_weight.reshape(per_device * rank, value_weight.shape[1])
    tokens, value_weight, down, up = (
        pltpu.with_memory_space_constraint(a, pltpu.HBM) for a in (tokens, value_weight, down, up)
    )
    message, table = open_call(
        here, row_adapter_index, adapter_slot_of, down, up, n_adapter, per_device, columns
    )

    buffers, shrinks = [[message]], []

    def stage_buffers(stages):
        return [b for stage in stages for b in buffers[stage]]

    def shrink(ks, stages):
        mine = shrink_product(
            ks, stages, table, here, tokens, stage_buffers(stages), per_device, rank
        )
        shrinks.extend([mine] + [swap_tensor(mine, step) for step in range(1, n_tensor)])
        return mine

    def base_for(step, chunks):
        return base_product(
            tokens,
            value_weight,
            (me_t + step) % n_tensor,
            columns,
            chunks[0][0],
            [number for _, number in chunks],
            step > 0,
        )

    held = along_line(message, 1)
    others = range(1, n_tensor)
    parts = [[base_for(step, CHUNKS[:1])[0] for step in others]]
    sent = [[swap_tensor(p, step) for step, p in zip(others, parts[0])]]
    rest_parts = [base_for(step, CHUNKS[1:]) for step in others]
    parts += [[p[i] for p in rest_parts] for i in range(len(CHUNKS) - 1)]
    done = [p for group in parts for p in group] + sent[0]
    for stage in range(1, n_adapter):
        if stage < len(CHUNKS):
            sent.append([swap_tensor(after(p, held), step) for step, p in zip(others, parts[stage])])
        came = after(held, *done)
        done = sent[stage] if stage < len(CHUNKS) else []
        if stage < n_adapter - 1:
            held = along_line(came, stage + 1)
        buffers.append([came, swap_cores(came)])
        if stage == 1:
            base = base_for(0, ((0, rows // SEGMENT_ROWS),))[0]
            done = done + [base, shrink([0, 1], [0, 1])]
            continue
        stages = list(range((stage + 1) // 2, stage + 1))
        done = [shrink([stage], stages)] + (done if stage < n_adapter - 2 else [])

    value, remaining = early(
        n_adapter,
        n_tensor,
        table,
        here,
        base,
        [c for group in sent for c in group],
        shrinks[:-n_tensor],
        stage_buffers(range(n_adapter - 1)),
        per_device,
        rank,
    )
    return late(
        n_adapter - 1,
        n_tensor,
        stages,
        table,
        here,
        remaining,
        shrinks[-n_tensor:],
        stage_buffers(stages),
        value,
        per_device,
        rank,
    )


def solution(mesh):
    return jax.shard_map(
        on_device,
        mesh=mesh,
        in_specs=(
            P(("groups", "adapter", "dp"), "tensor"),
            P("tensor", None),
            P(("groups", "adapter"), "tensor", None),
            P(("groups", "adapter"), None, None),
            P(("groups", "adapter", "dp")),
            P("groups"),
        ),
        out_specs=P(("groups", "adapter", "dp"), "tensor"),
        check_vma=False,
    )
```

time: 127 us -> 85.5 us (0.67)
  Pallas kernels: 87.9 us -> 37.4 us
  waiting for transfers between devices: 15.9 us -> 26 us
  starting transfers between devices: 14.7 us -> 17.5 us
  local copies, waits for them, and re-layouts: 5.32 us -> 2.96 us
    pallas_call x9 -> x8, Pallas kernels: 81.7 us -> 32.8 us  [the longest x3 17.4 us: base_product(): pl.pallas_call(functools.partial(base_kernel, first, sizes, coded), in_sp...]
    ppermute x3, waiting for transfers between devices: 0.01 us -> 10.7 us  [along_line(): return lax.ppermute(array, ('adapter', 'dp'), up + down)]
    ppermute x3, starting transfers between devices: 6.75 us -> 9.97 us  [along_line(): return lax.ppermute(array, ('adapter', 'dp'), up + down)]
    ppermute x3, waiting for transfers between devices: 2.84 us -> 0.01 us  [swap_cores(): return lax.ppermute(array, 'dp', [(0, 1), (1, 0)])]
    unnamed x26 -> x16, local copies, waits for them, and re-layouts: 5.32 us -> 2.96 us
    ppermute x6, waiting for transfers between devices: 13.1 us -> 15.3 us  [swap_tensor(): return lax.ppermute(array, 'tensor', pairs)]
    pallas_call x1, Pallas kernels: 6.25 us -> 4.52 us  [early(): pl.pallas_call(functools.partial(early_kernel, n_adapter, n_tensor, len(s...]
  transfers between devices with their start and end apart: 12 -> 12, of which waited for: 4 -> 6; matrix products, arithmetic and copies ran while one was open for 0% -> 0% of each run, Pallas kernels for 35% -> 40%
where the time goes in v4:
time: 85.5 us; the launch traced here: 84.1 us
  Pallas kernels  37.4 us (44%)
  waiting for transfers between devices  26 us (30%)
  starting transfers between devices  17.5 us (20%)
  local copies, waits for them, and re-layouts  2.96 us (3%)
    pallas_call x3, Pallas kernels, base_product(): pl.pallas_call(functools.partial(base_kernel, first, sizes, coded), in_sp...  17.4 us
    ppermute x6, waiting for transfers between devices, swap_tensor(): return lax.ppermute(array, 'tensor', pairs)  15.3 us
    pallas_call x3, Pallas kernels, shrink_product(): pl.pallas_call(functools.partial(shrink_kernel, ks, stages, rank), in_spe...  11.4 us
    ppermute x3, waiting for transfers between devices, along_line(): return lax.ppermute(array, ('adapter', 'dp'), up + down)  10.7 us
    ppermute x3, starting transfers between devices, along_line(): return lax.ppermute(array, ('adapter', 'dp'), up + down)  9.97 us
    ppermute x6, starting transfers between devices, swap_tensor(): return lax.ppermute(array, 'tensor', pairs)  7.56 us
    pallas_call x1, Pallas kernels, early(): pl.pallas_call(functools.partial(early_kernel, n_adapter, n_tensor, len(s...  4.52 us
    unnamed x16, local copies, waits for them, and re-layouts  2.96 us
  transfers between devices with their start and end apart: 12, of which 6 were waited for; matrix products, arithmetic and copies ran while one was open for 0% of the time, Pallas kernels for 40%

profile of v4, /device:TPU:16, one launch (start us, length us, event | category | flops | bytes accessed | tf_op | source)
XLA Modules:
  0.0 84.1 jit_solution(18012794185699974422)
XLA Ops:
  0.0 0.1 pad_add_fusion.here
  0.1 0.0 copy-start.4
  0.1 0.7 copy-done.4
  0.8 0.0 copy-start.5
  0.8 0.7 copy-done.5
  1.4 2.4 %shard_map.64 = (bf16[128,4608]{1,0:T(8,128)(2,1)S(1)}, s32[32]{0:T(128)S(1)}) custom-call(s32[3]{0:T(128)S(1)} %pad_add_fusion.here, s32[1024]{0:T(1024)S(1)} %copy-done.4, s32[8]{0:T(128)S(1)} %copy-done.5, bf16[128,4096]{1,0:T(8,128)(2,1)} %bitcast.9, bf16[128,1024]{1,0:T(8,128)(2,1)} %bitcast.10), custom_call_target="tpu_custom_call" | custom-call | bytes 2359296 | tf_op jit(solution)/shard_map/pallas_call | solution.py:94
  3.9 0.0 copy-start
  3.9 3.5 %collective-permute-start.1 = (bf16[128,4608]{1,0:T(8,128)(2,1)S(1)}, bf16[128,4608]{1,0:T(8,128)(2,1)S(1)}, u32[]{:S(2)}, u32[]{:S(2)}) collective-permute-start(bf16[128,4608]{1,0:T(8,128)(2,1)S(1)} %get-tuple-element.18.refs_0_.refs_8_), channel_id=1, source_target_pairs={{0,4},{4,8},{8,12},{5,1},{9,5},{13,9},{2,6},{6,10},{10,14},{7,3},{... | collective-permute-start | bytes 3538952 | tf_op jit(solution)/shard_map/ppermute | solution.py:414
  7.4 3.5 %shard_map.66 = s32[200,512]{1,0:T(8,128)S(1)} custom-call(s32[1]{0:T(128)} %bitcast.7.column, bf16[1024,4096]{1,0:T(8,128)(2,1)} %x_ref.11, bf16[4096,1024]{1,0:T(8,128)(2,1)} %w_ref.5), custom_call_target="tpu_custom_call" | custom-call | flops 1073741824 | bytes 6815744 | tf_op jit(solution)/shard_map/pallas_call | solution.py:204
  10.9 0.0 copy-done
  10.9 1.6 %collective-permute-start = (s32[200,512]{1,0:T(8,128)S(1)}, s32[200,512]{1,0:T(8,128)S(1)}, u32[]{:S(2)}, u32[]{:S(2)}) collective-permute-start(s32[200,512]{1,0:T(8,128)S(1)} %shard_map.66), channel_id=1, source_target_pairs={{0,2},{2,0},{1,3},{3,1},{4,6},{6,4},{5,7},{7,5},{8,10},{10,8},{9,1... | collective-permute-start | bytes 1228808 | tf_op jit(solution)/shard_map/ppermute | solution.py:409
  12.5 6.5 %shard_map.67 = (s32[296,512]{1,0:T(8,128)}, s32[296,512]{1,0:T(8,128)S(1)}) custom-call(s32[1]{0:T(128)} %bitcast.7.column, bf16[1024,4096]{1,0:T(8,128)(2,1)} %x_ref.11, bf16[4096,1024]{1,0:T(8,128)(2,1)} %w_ref.5), custom_call_target="tpu_custom_call" | custom-call | flops 3221225472 | bytes 12058624 | tf_op jit(solution)/shard_map/pallas_call | solution.py:204
  19.0 0.0 copy-start.6
  19.0 0.8 copy-done.6
  19.8 0.9 %collective-permute-done.refs_1_ = s32[200,512]{1,0:T(8,128)S(1)} collective-permute-done((s32[200,512]{1,0:T(8,128)S(1)}, s32[200,512]{1,0:T(8,128)S(1)}, u32[]{:S(2)}, u32[]{:S(2)}) %collective-permute-start) | collective-permute-done | bytes 409632 | tf_op jit(solution)/shard_map/ppermute | solution.py:409
  20.8 0.0 copy-start.2
  20.8 0.8 copy-done.2
  21.5 0.4 collective-permute-done.1.refs_1_.refs_0_.refs_9_
  22.0 0.0 collective-permute-start.5
  22.0 3.5 %collective-permute-start.3 = (bf16[128,4608]{1,0:T(8,128)(2,1)S(1)}, bf16[128,4608]{1,0:T(8,128)(2,1)S(1)}, u32[]{:S(2)}, u32[]{:S(2)}) collective-permute-start(bf16[128,4608]{1,0:T(8,128)(2,1)S(1)} %collective-permute-done.1.refs_1_.refs_0_.refs_9_), channel_id=1, source_target_pairs={{4,8},{8,12},{5,1},{9,5},{6,10},{10,14},{7,3},{11,7},{20,24},{24,2... | collective-permute-start | bytes 3538952 | tf_op jit(solution)/shard_map/ppermute | solution.py:414
  25.5 1.6 %collective-permute-start.2 = (s32[296,512]{1,0:T(8,128)}, s32[296,512]{1,0:T(8,128)}, u32[]{:S(2)}, u32[]{:S(2)}) collective-permute-start(s32[296,512]{1,0:T(8,128)} %get-tuple-element.19), channel_id=1, source_target_pairs={{0,2},{2,0},{1,3},{3,1},{4,6},{6,4},{5,7},{7,5},{8,10},{10,8},{9,1... | collective-permute-start | bytes 1818632 | tf_op jit(solution)/shard_map/ppermute | solution.py:409
  27.0 0.0 copy-start.1
  27.0 7.4 %shard_map.65.refs_0_ = f32[1024,512]{1,0:T(8,128)S(1)} custom-call(s32[1]{0:T(128)} %bitcast.6.column, bf16[1024,4096]{1,0:T(8,128)(2,1)} %x_ref.11, bf16[4096,1024]{1,0:T(8,128)(2,1)} %w_ref.5), custom_call_target="tpu_custom_call" | custom-call | flops 4294967296 | bytes 14680064 | tf_op jit(solution)/shard_map/pallas_call | solution.py:204
  34.4 0.0 collective-permute-done.5.refs_2_.refs_1_.refs_10_
  34.5 0.0 copy-done.1
  34.5 4.7 %shard_map.68.refs_4_ = f32[2,128,128]{2,1,0:T(8,128)S(1)} custom-call(s32[32]{0:T(128)S(1)} %get-tuple-element.16.table, s32[3]{0:T(128)S(1)} %pad_add_fusion.here, bf16[1024,4096]{1,0:T(8,128)(2,1)} %x_ref.11, bf16[128,4608]{1,0:T(8,128)(2,1)S(1)} %copy-done.1, bf16[128,4608]{1,0:T(8,128)(2,1)S(1)} %collective-permute-done.1.refs_1_.refs_0_.refs_9_, ...), custom_call_target="tpu_custom_call" | custom-call | flops 1073741824 | bytes 6291456 | tf_op jit(solution)/shard_map/pallas_call | solution.py:250
  39.2 0.0 copy-start.7
  39.2 1.4 %collective-permute-done.2.refs_2_ = s32[296,512]{1,0:T(8,128)} collective-permute-done((s32[296,512]{1,0:T(8,128)}, s32[296,512]{1,0:T(8,128)}, u32[]{:S(2)}, u32[]{:S(2)}) %collective-permute-start.2) | collective-permute-done | bytes 606240 | tf_op jit(solution)/shard_map/ppermute | solution.py:409
  40.6 0.0 collective-permute-done.3.refs_2_.refs_11_.refs_0_.refs_3_
  40.6 0.0 collective-permute-start.7
  40.6 3.0 %collective-permute-start.9 = (bf16[128,4608]{1,0:T(8,128)(2,1)S(1)}, bf16[128,4608]{1,0:T(8,128)(2,1)S(1)}, u32[]{:S(2)}, u32[]{:S(2)}) collective-permute-start(bf16[128,4608]{1,0:T(8,128)(2,1)S(1)} %collective-permute-done.3.refs_2_.refs_11_.refs_0_.refs_3_), channel_id=1, source_target_pairs={{8,12},{5,1},{10,14},{7,3},{24,28},{21,17},{26,30},{23,19}} | collective-permute-start | bytes 3538952 | tf_op jit(solution)/shard_map/ppermute | solution.py:414
  43.6 0.0 collective-permute-done.7.refs_3_.refs_12_.refs_1_.refs_4_
  43.6 3.3 %shard_map.69.refs_6_ = f32[1,128,128]{2,1,0:T(8,128)S(1)} custom-call(s32[32]{0:T(128)S(1)} %get-tuple-element.16.table, s32[3]{0:T(128)S(1)} %pad_add_fusion.here, bf16[1024,4096]{1,0:T(8,128)(2,1)} %x_ref.11, bf16[128,4608]{1,0:T(8,128)(2,1)S(1)} %collective-permute-done.1.refs_1_.refs_0_.refs_9_, ...), custom_call_target="tpu_custom_call" | custom-call | flops 536870912 | bytes 3145728 | tf_op jit(solution)/shard_map/pallas_call | solution.py:250
  47.0 0.0 copy-start.3
  47.0 10.3 %collective-permute-done.9.refs_2_.refs_5_ = bf16[128,4608]{1,0:T(8,128)(2,1)S(1)} collective-permute-done((bf16[128,4608]{1,0:T(8,128)(2,1)S(1)}, bf16[128,4608]{1,0:T(8,128)(2,1)S(1)}, u32[]{:S(2)}, u32[]{:S(2)}) %collective-permute-start.9) | collective-permute-done | bytes 1179680 | tf_op jit(solution)/shard_map/ppermute | solution.py:414
  57.3 0.0 collective-permute-start.10
  57.3 0.0 copy-done.7
  57.3 1.5 %collective-permute-start.4 = (s32[296,512]{1,0:T(8,128)S(1)}, s32[296,512]{1,0:T(8,128)S(1)}, u32[]{:S(2)}, u32[]{:S(2)}) collective-permute-start(s32[296,512]{1,0:T(8,128)S(1)} %copy-done.7), channel_id=1, source_target_pairs={{0,2},{2,0},{1,3},{3,1},{4,6},{6,4},{5,7},{7,5},{8,10},{10,8},{9,1... | collective-permute-start | bytes 1818632 | tf_op jit(solution)/shard_map/ppermute | solution.py:409
  58.8 0.5 collective-permute-start.6
  59.3 1.5 %collective-permute-start.8 = (f32[1,128,128]{2,1,0:T(8,128)S(1)}, f32[1,128,128]{2,1,0:T(8,128)S(1)}, u32[]{:S(2)}, u32[]{:S(2)}) collective-permute-start(f32[1,128,128]{2,1,0:T(8,128)S(1)} %shard_map.69.refs_6_), channel_id=1, source_target_pairs={{0,2},{2,0},{1,3},{3,1},{4,6},{6,4},{5,7},{7,5},{8,10},{10,8},{9,1... | collective-permute-start | bytes 196616 | tf_op jit(solution)/shard_map/ppermute | solution.py:409
  60.8 0.0 collective-permute-done.10.refs_3_.refs_6_
  60.8 3.3 %shard_map.71.refs_1_ = f32[1,128,128]{2,1,0:T(8,128)S(1)} custom-call(s32[32]{0:T(128)S(1)} %get-tuple-element.16.table, s32[3]{0:T(128)S(1)} %pad_add_fusion.here, bf16[1024,4096]{1,0:T(8,128)(2,1)} %x_ref.11, bf16[128,4608]{1,0:T(8,128)(2,1)S(1)} %collective-permute-done.3.refs_2_.refs_11_.refs_0_.refs_3_, ...), custom_call_target="tpu_custom_call" | custom-call | flops 536870912 | bytes 3145728 | tf_op jit(solution)/shard_map/pallas_call | solution.py:250
  64.1 0.9 %collective-permute-start.11 = (f32[1,128,128]{2,1,0:T(8,128)S(1)}, f32[1,128,128]{2,1,0:T(8,128)S(1)}, u32[]{:S(2)}, u32[]{:S(2)}) collective-permute-start(f32[1,128,128]{2,1,0:T(8,128)S(1)} %shard_map.71.refs_1_), channel_id=1, source_target_pairs={{0,2},{2,0},{1,3},{3,1},{4,6},{6,4},{5,7},{7,5},{8,10},{10,8},{9,1... | collective-permute-start | bytes 196616 | tf_op jit(solution)/shard_map/ppermute | solution.py:409
  65.0 11.6 %collective-permute-done.6.refs_5_ = f32[2,128,128]{2,1,0:T(8,128)S(1)} collective-permute-done((f32[2,128,128]{2,1,0:T(8,128)S(1)}, f32[2,128,128]{2,1,0:T(8,128)S(1)}, u32[]{:S(2)}, u32[]{:S(2)}) %collective-permute-start.6) | collective-permute-done | bytes 131104 | tf_op jit(solution)/shard_map/ppermute | solution.py:409
  76.5 0.0 collective-permute-done.4.refs_3_
  76.5 1.4 %collective-permute-done.8.refs_7_ = f32[1,128,128]{2,1,0:T(8,128)S(1)} collective-permute-done((f32[1,128,128]{2,1,0:T(8,128)S(1)}, f32[1,128,128]{2,1,0:T(8,128)S(1)}, u32[]{:S(2)}, u32[]{:S(2)}) %collective-permute-start.8) | collective-permute-done | bytes 65568 | tf_op jit(solution)/shard_map/ppermute | solution.py:409
  78.0 0.0 copy-done.3
  78.0 4.5 %shard_map.70 = (bf16[1024,512]{1,0:T(8,128)(2,1)}, f32[2,128,512]{2,1,0:T(8,128)S(1)}) custom-call(s32[32]{0:T(128)S(1)} %get-tuple-element.16.table, s32[3]{0:T(128)S(1)} %pad_add_fusion.here, f32[1024,512]{1,0:T(8,128)S(1)} %shard_map.65.refs_0_, s32[200,512]{1,0:T(8,128)S(1)} %copy-done.3, s32[296,512]{1,0:T(8,128)} %collective-permute-done.2.refs_2_, ...), custom_call_target="tpu_custom_call" | custom-call | flops 201326592 | bytes 5242880 | tf_op jit(solution)/shard_map/pallas_call | solution.py:332
  82.5 0.0 collective-permute-done.11.refs_2_
  82.5 1.6 %shard_map.72 = bf16[1024,512]{1,0:T(8,128)(2,1)} custom-call(s32[32]{0:T(128)S(1)} %get-tuple-element.16.table, s32[3]{0:T(128)S(1)} %pad_add_fusion.here, f32[2,128,512]{2,1,0:T(8,128)S(1)} %get-tuple-element.24.refs_0_, f32[1,128,128]{2,1,0:T(8,128)S(1)} %shard_map.71.refs_1_, ...), custom_call_target="tpu_custom_call", output_to_operand_aliasing={{}: (9, {})} | custom-call | flops 50331648 | bytes 1048576 | tf_op jit(solution)/shard_map/pallas_call | solution.py:374
Async XLA Ops:
  0.1 0.7 copy-start.4
  0.8 0.7 copy-start.5
  3.9 7.0 %copy-start = (bf16[128,4608]{1,0:T(8,128)(2,1)}, bf16[128,4608]{1,0:T(8,128)(2,1)S(1)}, u32[]{:S(2)}) copy-start(bf16[128,4608]{1,0:T(8,128)(2,1)S(1)} %get-tuple-element.18.refs_0_.refs_8_) | copy-start | bytes 3538948
  3.9 18.1 %collective-permute-start.1 = (bf16[128,4608]{1,0:T(8,128)(2,1)S(1)}, bf16[128,4608]{1,0:T(8,128)(2,1)S(1)}, u32[]{:S(2)}, u32[]{:S(2)}) collective-permute-start(bf16[128,4608]{1,0:T(8,128)(2,1)S(1)} %get-tuple-element.18.refs_0_.refs_8_), channel_id=1, source_target_pairs={{0,4},{4,8},{8,12},{5,1},{9,5},{13,9},{2,6},{6,10},{10,14},{7,3},{... | collective-permute-start | bytes 3538952 | tf_op jit(solution)/shard_map/ppermute | solution.py:414
  10.9 9.9 %collective-permute-start = (s32[200,512]{1,0:T(8,128)S(1)}, s32[200,512]{1,0:T(8,128)S(1)}, u32[]{:S(2)}, u32[]{:S(2)}) collective-permute-start(s32[200,512]{1,0:T(8,128)S(1)} %shard_map.66), channel_id=1, source_target_pairs={{0,2},{2,0},{1,3},{3,1},{4,6},{6,4},{5,7},{7,5},{8,10},{10,8},{9,1... | collective-permute-start | bytes 1228808 | tf_op jit(solution)/shard_map/ppermute | solution.py:409
  19.0 0.8 copy-start.6
  20.8 0.8 copy-start.2
  22.0 12.5 %collective-permute-start.5 = (bf16[128,4608]{1,0:T(8,128)(2,1)S(1)}, bf16[128,4608]{1,0:T(8,128)(2,1)S(1)}, u32[]{:S(2)}, u32[]{:S(2)}) collective-permute-start(bf16[128,4608]{1,0:T(8,128)(2,1)S(1)} %collective-permute-done.1.refs_1_.refs_0_.refs_9_), channel_id=1, source_target_pairs={{0,1},{1,0},{2,3},{3,2},{4,5},{5,4},{6,7},{7,6},{8,9},{9,8},{10,11... | collective-permute-start | bytes 3538952 | tf_op jit(solution)/shard_map/ppermute | solution.py:417
  22.0 18.6 %collective-permute-start.3 = (bf16[128,4608]{1,0:T(8,128)(2,1)S(1)}, bf16[128,4608]{1,0:T(8,128)(2,1)S(1)}, u32[]{:S(2)}, u32[]{:S(2)}) collective-permute-start(bf16[128,4608]{1,0:T(8,128)(2,1)S(1)} %collective-permute-done.1.refs_1_.refs_0_.refs_9_), channel_id=1, source_target_pairs={{4,8},{8,12},{5,1},{9,5},{6,10},{10,14},{7,3},{11,7},{20,24},{24,2... | collective-permute-start | bytes 3538952 | tf_op jit(solution)/shard_map/ppermute | solution.py:414
  25.5 15.1 %collective-permute-start.2 = (s32[296,512]{1,0:T(8,128)}, s32[296,512]{1,0:T(8,128)}, u32[]{:S(2)}, u32[]{:S(2)}) collective-permute-start(s32[296,512]{1,0:T(8,128)} %get-tuple-element.19), channel_id=1, source_target_pairs={{0,2},{2,0},{1,3},{3,1},{4,6},{6,4},{5,7},{7,5},{8,10},{10,8},{9,1... | collective-permute-start | bytes 1818632 | tf_op jit(solution)/shard_map/ppermute | solution.py:409
  27.0 7.4 %copy-start.1 = (bf16[128,4608]{1,0:T(8,128)(2,1)S(1)}, bf16[128,4608]{1,0:T(8,128)(2,1)}, u32[]{:S(2)}) copy-start(bf16[128,4608]{1,0:T(8,128)(2,1)} %copy-done) | copy-start | bytes 3538948
  39.2 18.0 %copy-start.7 = (s32[296,512]{1,0:T(8,128)S(1)}, s32[296,512]{1,0:T(8,128)}, u32[]{:S(2)}) copy-start(s32[296,512]{1,0:T(8,128)} %copy-done.6) | copy-start | bytes 1818628
  40.6 3.0 %collective-permute-start.7 = (bf16[128,4608]{1,0:T(8,128)(2,1)S(1)}, bf16[128,4608]{1,0:T(8,128)(2,1)S(1)}, u32[]{:S(2)}, u32[]{:S(2)}) collective-permute-start(bf16[128,4608]{1,0:T(8,128)(2,1)S(1)} %collective-permute-done.3.refs_2_.refs_11_.refs_0_.refs_3_), channel_id=1, source_target_pairs={{0,1},{1,0},{2,3},{3,2},{4,5},{5,4},{6,7},{7,6},{8,9},{9,8},{10,11... | collective-permute-start | bytes 3538952 | tf_op jit(solution)/shard_map/ppermute | solution.py:417
  40.6 16.6 %collective-permute-start.9 = (bf16[128,4608]{1,0:T(8,128)(2,1)S(1)}, bf16[128,4608]{1,0:T(8,128)(2,1)S(1)}, u32[]{:S(2)}, u32[]{:S(2)}) collective-permute-start(bf16[128,4608]{1,0:T(8,128)(2,1)S(1)} %collective-permute-done.3.refs_2_.refs_11_.refs_0_.refs_3_), channel_id=1, source_target_pairs={{8,12},{5,1},{10,14},{7,3},{24,28},{21,17},{26,30},{23,19}} | collective-permute-start | bytes 3538952 | tf_op jit(solution)/shard_map/ppermute | solution.py:414
  47.0 31.0 %copy-start.3 = (s32[200,512]{1,0:T(8,128)S(1)}, s32[200,512]{1,0:T(8,128)}, u32[]{:S(2)}) copy-start(s32[200,512]{1,0:T(8,128)} %copy-done.2) | copy-start | bytes 1228804
  57.3 3.5 %collective-permute-start.10 = (bf16[128,4608]{1,0:T(8,128)(2,1)S(1)}, bf16[128,4608]{1,0:T(8,128)(2,1)S(1)}, u32[]{:S(2)}, u32[]{:S(2)}) collective-permute-start(bf16[128,4608]{1,0:T(8,128)(2,1)S(1)} %collective-permute-done.9.refs_2_.refs_5_), channel_id=1, source_target_pairs={{0,1},{1,0},{2,3},{3,2},{4,5},{5,4},{6,7},{7,6},{8,9},{9,8},{10,11... | collective-permute-start | bytes 3538952 | tf_op jit(solution)/shard_map/ppermute | solution.py:417
  57.3 19.3 %collective-permute-start.4 = (s32[296,512]{1,0:T(8,128)S(1)}, s32[296,512]{1,0:T(8,128)S(1)}, u32[]{:S(2)}, u32[]{:S(2)}) collective-permute-start(s32[296,512]{1,0:T(8,128)S(1)} %copy-done.7), channel_id=1, source_target_pairs={{0,2},{2,0},{1,3},{3,1},{4,6},{6,4},{5,7},{7,5},{8,10},{10,8},{9,1... | collective-permute-start | bytes 1818632 | tf_op jit(solution)/shard_map/ppermute | solution.py:409
  58.8 17.8 %collective-permute-start.6 = (f32[2,128,128]{2,1,0:T(8,128)S(1)}, f32[2,128,128]{2,1,0:T(8,128)S(1)}, u32[]{:S(2)}, u32[]{:S(2)}) collective-permute-start(f32[2,128,128]{2,1,0:T(8,128)S(1)} %shard_map.68.refs_4_), channel_id=1, source_target_pairs={{0,2},{2,0},{1,3},{3,1},{4,6},{6,4},{5,7},{7,5},{8,10},{10,8},{9,1... | collective-permute-start | bytes 393224 | tf_op jit(solution)/shard_map/ppermute | solution.py:409
  59.3 18.7 %collective-permute-start.8 = (f32[1,128,128]{2,1,0:T(8,128)S(1)}, f32[1,128,128]{2,1,0:T(8,128)S(1)}, u32[]{:S(2)}, u32[]{:S(2)}) collective-permute-start(f32[1,128,128]{2,1,0:T(8,128)S(1)} %shard_map.69.refs_6_), channel_id=1, source_target_pairs={{0,2},{2,0},{1,3},{3,1},{4,6},{6,4},{5,7},{7,5},{8,10},{10,8},{9,1... | collective-permute-start | bytes 196616 | tf_op jit(solution)/shard_map/ppermute | solution.py:409
  64.1 18.4 %collective-permute-start.11 = (f32[1,128,128]{2,1,0:T(8,128)S(1)}, f32[1,128,128]{2,1,0:T(8,128)S(1)}, u32[]{:S(2)}, u32[]{:S(2)}) collective-permute-start(f32[1,128,128]{2,1,0:T(8,128)S(1)} %shard_map.71.refs_1_), channel_id=1, source_target_pairs={{0,2},{2,0},{1,3},{3,1},{4,6},{6,4},{5,7},{7,5},{8,10},{10,8},{9,1... | collective-permute-start | bytes 196616 | tf_op jit(solution)/shard_map/ppermute | solution.py:409

commit v5 on v4

v5 whole, which is shorter than its diff:
```python
import functools

import jax
import jax.numpy as jnp
from jax import lax
from jax.experimental import pallas as pl
from jax.experimental.pallas import tpu as pltpu
from jax.sharding import PartitionSpec as P

SEGMENT_ROWS = 128
adapter_scale = 0.5
MOST = 2
BLOCK = 256
PIECES = 4
CHUNKS = ((6, 2), (0, 3), (3, 3))
ENTRIES = 8
MIDDLE = 1.5 * 2.0**23


def cost(flops, moved):
    return pl.CostEstimate(flops=int(flops), bytes_accessed=int(moved), transcendentals=0)


def params(mib):
    return pltpu.CompilerParams(vmem_limit_bytes=mib * 2**20)


ANY = pl.BlockSpec(memory_space=pl.ANY)
HBM = pl.BlockSpec(memory_space=pltpu.HBM)
SMEM = pl.BlockSpec(memory_space=pltpu.SMEM)
VMEM = pl.BlockSpec(memory_space=pltpu.VMEM)


def arrival_order(me, n_adapter):
    order = [me] + [jnp.int32(-1)] * (n_adapter - 1)
    count = jnp.int32(1)
    for distance in range(1, n_adapter):
        for other in (me - distance, me + distance):
            valid = (other >= 0) & (other < n_adapter)
            order = [jnp.where(valid & (count == k), other, o) for k, o in enumerate(order)]
            count = count + valid.astype(jnp.int32)
    return order


def buffer_owners(here, stages):
    owners = []
    for stage in stages:
        toward = jnp.where(here[1] == 0, -stage, stage)
        owners += [here[0] + toward, here[0] - toward] if stage > 0 else [here[0]]
    return owners


def segment_of(table, k, j):
    seg = table[k * ENTRIES + 1 + 2 * j]
    start = pl.multiple_of(jnp.maximum(seg, 0) * SEGMENT_ROWS, SEGMENT_ROWS)
    return start, seg >= 0, table[k * ENTRIES + 2 + 2 * j]


def message_kernel(here, down_ref, up_ref, o_ref, sems):
    width = down_ref.shape[1]
    columns = o_ref.shape[1] - width
    start = pl.multiple_of(here[2] * columns, columns)
    copies = [
        pltpu.make_async_copy(down_ref, o_ref.at[:, pl.ds(0, width)], sems.at[0]),
        pltpu.make_async_copy(
            up_ref.at[:, pl.ds(start, columns)], o_ref.at[:, pl.ds(width, columns)], sems.at[1]
        ),
    ]
    for copy in copies:
        copy.start()
    for copy in copies:
        copy.wait()


def message_call(here, down, up, columns):
    rows, width = down.shape
    return pl.pallas_call(
        message_kernel,
        in_specs=[SMEM, HBM, HBM],
        out_specs=VMEM,
        out_shape=jax.ShapeDtypeStruct((rows, width + columns), jnp.bfloat16),
        scratch_shapes=[pltpu.SemaphoreType.DMA((2,))],
        compiler_params=params(8),
        cost_estimate=cost(0, 4 * rows * (width + columns)),
    )(here, down, up)


def table_kernel(n_adapter, per_device, here, ids, slots, table):
    seg_dev = ids.shape[0] // SEGMENT_ROWS
    used = [slots[ids[s * SEGMENT_ROWS]] for s in range(seg_dev)]
    for k, owner in enumerate(arrival_order(here[0], n_adapter)):
        table[k * ENTRIES] = owner
        found, place = [jnp.int32(-1)] * MOST, [jnp.int32(0)] * MOST
        count = jnp.int32(0)
        for s, slot in enumerate(used):
            within = slot - owner * per_device
            hit = (within >= 0) & (within < per_device)
            for j in range(MOST):
                take = hit & (count == j)
                found[j] = jnp.where(take, s, found[j])
                place[j] = jnp.where(take, within, place[j])
            count = count + hit.astype(jnp.int32)
        for j in range(MOST):
            table[k * ENTRIES + 1 + 2 * j] = found[j]
            table[k * ENTRIES + 2 + 2 * j] = place[j]


def table_call(here, ids, slots, n_adapter, per_device):
    return pl.pallas_call(
        functools.partial(table_kernel, n_adapter, per_device),
        in_specs=[SMEM, SMEM, SMEM],
        out_specs=SMEM,
        out_shape=jax.ShapeDtypeStruct((n_adapter * ENTRIES,), jnp.int32),
        cost_estimate=cost(0, 4 * ids.shape[0]),
    )(here, ids, slots)


def diagonal():
    shape = (SEGMENT_ROWS, SEGMENT_ROWS)
    return lax.broadcasted_iota(jnp.int32, shape, 0) == lax.broadcasted_iota(jnp.int32, shape, 1)


WORDS = SEGMENT_ROWS * 3 // 4
QUARTER = SEGMENT_ROWS // 4


def coded_rows(segments):
    return segments * WORDS + 8


def encode(values, o_ref, unit, units):
    largest = jnp.maximum(jnp.max(jnp.abs(values), axis=1, keepdims=True), 2.0**-100)
    power = jnp.floor(jnp.log2(largest))
    whole = (values * jnp.exp2(21.0 - power) + MIDDLE).astype(jnp.int32) - int(MIDDLE)
    q = [whole[i * QUARTER : (i + 1) * QUARTER] for i in range(4)]
    for i in range(3):
        o_ref[unit * WORDS + i * QUARTER : unit * WORDS + (i + 1) * QUARTER, :] = (
            q[i] & 0xFFFFFF
        ) | ((q[3] >> (8 * i)) << 24)
    row = jnp.sum(jnp.where(diagonal(), power, 0.0), axis=0, keepdims=True)
    o_ref[units * WORDS + unit : units * WORDS + unit + 1, :SEGMENT_ROWS] = row.astype(jnp.int32)


def decode(ref, unit, units):
    w = [ref[unit * WORDS + i * QUARTER : unit * WORDS + (i + 1) * QUARTER, :] for i in range(3)]
    q = [(x << 8) >> 8 for x in w]
    q.append(((w[0] >> 24) & 0xFF) | (((w[1] >> 24) & 0xFF) << 8) | ((w[2] >> 24) << 16))
    row = ref[units * WORDS + unit : units * WORDS + unit + 1, :SEGMENT_ROWS].astype(jnp.float32)
    power = jnp.sum(jnp.where(diagonal(), row, 0.0), axis=1, keepdims=True)
    return jnp.concatenate(q, axis=0).astype(jnp.float32) * jnp.exp2(power - 21.0)


def load_base(first, segments, column, x_ref, w_ref, x, w, sems):
    width, columns = w.shape
    rows = segments * SEGMENT_ROWS
    start = pl.multiple_of(column * columns, columns)
    depth = width // PIECES
    blocks = [(r, min(BLOCK, rows - r)) for r in range(0, rows, BLOCK)]

    def x_copy(at, size, features, sem):
        return pltpu.make_async_copy(
            x_ref.at[pl.ds(first * SEGMENT_ROWS + at, size), features],
            x.at[pl.ds(at, size), features],
            sem,
        )

    work = []
    for i, (at, size) in enumerate(blocks):
        terms = []
        if i == 0:
            for p in range(PIECES):
                features = pl.ds(p * depth, depth)
                copies = (
                    pltpu.make_async_copy(
                        w_ref.at[features, pl.ds(start, columns)], w.at[features, :], sems.at[0, p]
                    ),
                    x_copy(0, size, features, sems.at[1, p]),
                )
                terms.append((copies, slice(p * depth, (p + 1) * depth)))
        else:
            terms.append(((x_copy(at, size, slice(None), sems.at[2, i]),), slice(None)))
        work.append((at, size, terms))
    for _, _, terms in work:
        for copies, _ in terms:
            for copy in copies:
                copy.start()
    return work


def block_product(x, w, at, size, terms):
    total = None
    for copies, features in terms:
        for copy in copies:
            copy.wait()
        term = jnp.dot(
            x[at : at + size, features], w[features, :], preferred_element_type=jnp.float32
        )
        total = term if total is None else total + term
    return total


def base_scratch(segments, width, columns):
    rows = segments * SEGMENT_ROWS
    return [
        pltpu.VMEM((rows, width), jnp.bfloat16),
        pltpu.VMEM((width, columns), jnp.bfloat16),
        pltpu.SemaphoreType.DMA((3, max(PIECES, rows // BLOCK + 1))),
    ]


def sent_kernel(first, sizes, column, x_ref, w_ref, *refs):
    outs, (x, w, sems) = refs[: len(sizes)], refs[len(sizes) :]
    work = load_base(first, sum(sizes), column[0], x_ref, w_ref, x, w, sems)
    unit_of = [(out, unit) for out, size in enumerate(sizes) for unit in range(size)]
    for out, size in zip(outs, sizes):
        out[size * WORDS :, :] = jnp.zeros((8, w.shape[1]), jnp.int32)
    for at, size, terms in work:
        product = block_product(x, w, at, size, terms)
        for r in range(0, size, SEGMENT_ROWS):
            out, unit = unit_of[(at + r) // SEGMENT_ROWS]
            encode(product[r : r + SEGMENT_ROWS], outs[out], unit, sizes[out])


def sent_call(tokens, weight, column, columns, first, sizes):
    width = tokens.shape[1]
    rows = sum(sizes) * SEGMENT_ROWS
    return pl.pallas_call(
        functools.partial(sent_kernel, first, sizes),
        in_specs=[SMEM, HBM, HBM],
        out_specs=[VMEM] * len(sizes),
        out_shape=[jax.ShapeDtypeStruct((coded_rows(n), columns), jnp.int32) for n in sizes],
        scratch_shapes=base_scratch(sum(sizes), width, columns),
        compiler_params=params(24),
        cost_estimate=cost(
            2 * rows * width * columns, 2 * rows * width + 2 * width * columns + 4 * rows * columns
        ),
    )(column.reshape(1), tokens, weight)


def shrink_into(o_ref, i, table, k, rows_of, buffers, owners, rank):
    for buffer, whose in zip(buffers, owners):

        @pl.when(whose == table[k * ENTRIES])
        def _(buffer=buffer):
            for j in range(MOST):
                _, _, within = segment_of(table, k, j)
                rows = rows_of(j)
                width = rows.shape[1]
                factor = buffer[pl.ds(pl.multiple_of(within * rank, rank), rank), :width]
                o_ref[i, :, j * rank : (j + 1) * rank] = lax.dot_general(
                    rows, factor, (((1,), (1,)), ((), ())), preferred_element_type=jnp.float32
                )


def stages_of(k):
    return range((k + 1) // 2, k + 1)


def own_kernel(n_adapter, rank, table, here, x_ref, w_ref, *refs):
    buffers, (o_ref, s_ref, kept_ref, x, w, sems, kept_sems) = refs[:3], refs[3:]
    work = load_base(0, x.shape[0] // SEGMENT_ROWS, here[2], x_ref, w_ref, x, w, sems)
    keeps = []
    for at, size, terms in work:
        o_ref[at : at + size, :] = block_product(x, w, at, size, terms)
    for k in range(2, n_adapter):
        for j in range(MOST):
            start, _, _ = segment_of(table, k, j)
            keeps.append(
                pltpu.make_async_copy(
                    x.at[pl.ds(start, SEGMENT_ROWS), :], kept_ref.at[k - 2, j], kept_sems.at[k - 2, j]
                )
            )
            keeps[-1].start()
    for k in range(2):

        def rows_of(j, k=k):
            start, _, _ = segment_of(table, k, j)
            return x[pl.ds(start, SEGMENT_ROWS), :]

        here_buffers = buffers[:1] if k == 0 else buffers[1:]
        shrink_into(s_ref, k, table, k, rows_of, here_buffers, buffer_owners(here, stages_of(k)), rank)
    for copy in keeps:
        copy.wait()


def own_call(table, here, tokens, weight, buffers, columns, n_adapter, rank):
    rows, width = tokens.shape
    segments = rows // SEGMENT_ROWS
    return pl.pallas_call(
        functools.partial(own_kernel, n_adapter, rank),
        in_specs=[SMEM, SMEM, HBM, HBM] + [VMEM] * len(buffers),
        out_specs=[VMEM] * 3,
        out_shape=[
            jax.ShapeDtypeStruct((rows, columns), jnp.float32),
            jax.ShapeDtypeStruct((2, SEGMENT_ROWS, MOST * rank), jnp.float32),
            jax.ShapeDtypeStruct((n_adapter - 2, MOST, SEGMENT_ROWS, width), jnp.bfloat16),
        ],
        scratch_shapes=base_scratch(segments, width, columns)
        + [pltpu.SemaphoreType.DMA((n_adapter - 2, MOST))],
        compiler_params=params(32),
        cost_estimate=cost(
            2 * rows * width * columns, 2 * rows * width + 2 * width * columns + 4 * rows * columns
        ),
    )(table, here, tokens, weight, *buffers)


def shrink_kernel(k, rank, table, here, kept_ref, *refs):
    buffers, o_ref = refs[:-1], refs[-1]
    shrink_into(
        o_ref, 0, table, k, lambda j: kept_ref[k - 2, j], buffers, buffer_owners(here, stages_of(k)), rank
    )


def shrink_call(k, table, here, kept, buffers, rank):
    width = kept.shape[3]
    return pl.pallas_call(
        functools.partial(shrink_kernel, k, rank),
        in_specs=[SMEM, SMEM, VMEM] + [VMEM] * len(buffers),
        out_specs=VMEM,
        out_shape=jax.ShapeDtypeStruct((1, SEGMENT_ROWS, MOST * rank), jnp.float32),
        compiler_params=params(16),
        cost_estimate=cost(MOST * 2 * SEGMENT_ROWS * width * 256, 4 * SEGMENT_ROWS * width),
    )(table, here, kept, *buffers)


def fetch_up(up, at, table, k, j, buffers, owners, rank):
    columns = up.shape[2]
    _, _, within = segment_of(table, k, j)
    for buffer, whose in zip(buffers, owners):

        @pl.when(whose == table[k * ENTRIES])
        def _(buffer=buffer):
            first = buffer.shape[1] - columns
            factor = buffer[pl.ds(pl.multiple_of(within * rank, rank), rank), first:]
            up[at, :rank, :] = factor
            up[at, rank:, :] = factor


def up_product(share, j, factor, rank):
    lane = lax.broadcasted_iota(jnp.int32, share.shape, 1)
    other = pltpu.roll(share, rank, 1)
    both = jnp.where((lane < rank) == (j == 0), share, other)
    high = both.astype(jnp.bfloat16).astype(jnp.float32)
    terms = jnp.where(lane < rank, high, both - high).astype(jnp.bfloat16)
    return jnp.dot(terms, factor, preferred_element_type=jnp.float32)


def early_kernel(n_adapter, n_tensor, rank, table, here, *refs):
    n_coded, n_calls = len(CHUNKS) * (n_tensor - 1), n_adapter - 2
    base_ref, coded_refs, refs = refs[0], refs[1 : 1 + n_coded], refs[1 + n_coded :]
    shrinks, refs = refs[: n_calls * n_tensor], refs[n_calls * n_tensor :]
    buffers, (o_ref, rest_ref, up, total) = refs[:-4], refs[-4:]
    for k in range(n_adapter - 1):
        at = 0 if k == 0 else 2 * stages_of(k)[0] - 1
        to = 2 * k + 1
        owners = buffer_owners(here, stages_of(k))
        for j in range(MOST):
            fetch_up(up, k * MOST + j, table, k, j, buffers[at:to], owners, rank)
    shares = []
    for call in range(n_calls):
        share = shrinks[call * n_tensor][...]
        for i in range(1, n_tensor):
            share = share + shrinks[call * n_tensor + i][...]
        shares += [share[i] for i in range(share.shape[0])]
    for chunk, (first, number) in enumerate(CHUNKS):
        for unit in range(number):
            here_rows = pl.ds((first + unit) * SEGMENT_ROWS, SEGMENT_ROWS)
            value = base_ref[here_rows, :]
            for i in range(n_tensor - 1):
                value = value + decode(coded_refs[chunk * (n_tensor - 1) + i], unit, number)
            total[here_rows, :] = value
    for k in range(n_adapter):
        for j in range(MOST):
            start, used, _ = segment_of(table, k, j)
            value = total[pl.ds(start, SEGMENT_ROWS), :]
            if k == n_adapter - 1:
                rest_ref[j] = value
                continue
            lora = up_product(shares[k], j, up[k * MOST + j], rank)

            @pl.when(used)
            def _(start=start, value=value, lora=lora):
                o_ref[pl.ds(start, SEGMENT_ROWS), :] = (value + adapter_scale * lora).astype(
                    jnp.bfloat16
                )


def early(n_adapter, n_tensor, table, here, base, coded, shrinks, buffers, rank):
    rows, columns = base.shape
    return pl.pallas_call(
        functools.partial(early_kernel, n_adapter, n_tensor, rank),
        in_specs=[SMEM] * 2 + [VMEM] * (1 + len(coded) + len(shrinks) + len(buffers)),
        out_specs=[VMEM, VMEM],
        out_shape=[
            jax.ShapeDtypeStruct((rows, columns), jnp.bfloat16),
            jax.ShapeDtypeStruct((MOST, SEGMENT_ROWS, columns), jnp.float32),
        ],
        scratch_shapes=[
            pltpu.VMEM(((n_adapter - 1) * MOST, 2 * rank, columns), jnp.bfloat16),
            pltpu.VMEM((rows, columns), jnp.float32),
        ],
        compiler_params=params(16),
        cost_estimate=cost(6 * rows * rank * columns, (4 * n_tensor + 2) * rows * columns),
    )(table, here, base, *coded, *shrinks, *buffers)


def late_kernel(k, n_tensor, rank, table, here, *refs):
    rest_ref, shrinks, refs = refs[0], refs[1 : 1 + n_tensor], refs[1 + n_tensor :]
    buffers, (_, o_ref, up, out, sems) = refs[:-5], refs[-5:]
    owners = buffer_owners(here, stages_of(k))
    share = shrinks[0][0]
    for r in shrinks[1:]:
        share = share + r[0]
    stores = []
    for j in range(MOST):
        fetch_up(up, j, table, k, j, buffers, owners, rank)
        start, used, _ = segment_of(table, k, j)
        lora = up_product(share, j, up[j], rank)
        out[j] = (rest_ref[j] + adapter_scale * lora).astype(jnp.bfloat16)
        store = pltpu.make_async_copy(out.at[j], o_ref.at[pl.ds(start, SEGMENT_ROWS), :], sems.at[j])
        pl.when(used)(store.start)
        stores.append((used, store))
    for used, store in stores:
        pl.when(used)(store.wait)


def late(k, n_tensor, table, here, rest, shrinks, buffers, value, rank):
    rows, columns = value.shape
    return pl.pallas_call(
        functools.partial(late_kernel, k, n_tensor, rank),
        in_specs=[SMEM] * 2 + [VMEM] * (1 + len(shrinks) + len(buffers)) + [ANY],
        out_specs=ANY,
        out_shape=jax.ShapeDtypeStruct((rows, columns), jnp.bfloat16),
        scratch_shapes=[
            pltpu.VMEM((MOST, 2 * rank, columns), jnp.bfloat16),
            pltpu.VMEM((MOST, SEGMENT_ROWS, columns), jnp.bfloat16),
            pltpu.SemaphoreType.DMA((MOST,)),
        ],
        input_output_aliases={3 + len(shrinks) + len(buffers): 0},
        compiler_params=params(8),
        cost_estimate=cost(
            6 * MOST * SEGMENT_ROWS * rank * columns, 8 * MOST * SEGMENT_ROWS * columns
        ),
    )(table, here, rest, *shrinks, *buffers, value)


def after(array, *others):
    return lax.optimization_barrier((array, *others))[0]


def on_device(
    tokens, value_weight, adapter_down_weight, adapter_up_weight, row_adapter_index, adapter_slot_of
):
    rows, width = tokens.shape
    per_device, _, rank = adapter_down_weight.shape
    n_adapter = lax.axis_size("adapter")
    n_tensor = lax.axis_size("tensor")
    me_t = lax.axis_index("tensor")
    here = jnp.stack([lax.axis_index("adapter"), lax.axis_index("dp"), me_t])
    columns = value_weight.shape[1] // n_tensor

    def swap_tensor(array, step):
        pairs = [(i, (i + step) % n_tensor) for i in range(n_tensor)]
        return lax.ppermute(array, "tensor", pairs)

    def along_line(array, stage):
        up = [(2 * i, 2 * (i + 1)) for i in range(stage - 1, n_adapter - 1)]
        down = [(2 * i + 1, 2 * (i - 1) + 1) for i in range(1, n_adapter - stage + 1)]
        return lax.ppermute(array, ("adapter", "dp"), up + down)

    def swap_cores(array):
        return lax.ppermute(array, "dp", [(0, 1), (1, 0)])

    down = jnp.swapaxes(adapter_down_weight, 1, 2).reshape(per_device * rank, width)
    up = adapter_up_weight.reshape(per_device * rank, value_weight.shape[1])
    tokens, value_weight, down, up = (
        pltpu.with_memory_space_constraint(a, pltpu.HBM) for a in (tokens, value_weight, down, up)
    )
    message = message_call(here, down, up, columns)
    table = table_call(here, row_adapter_index, adapter_slot_of, n_adapter, per_device)

    buffers, shrinks = [[message]], []

    def buffers_of(stages):
        return [b for stage in stages for b in buffers[stage]]

    def add_shrink(mine):
        shrinks.extend([mine] + [swap_tensor(mine, step) for step in range(1, n_tensor)])

    held = along_line(message, 1)
    others = range(1, n_tensor)

    def sent_for(step, chunks):
        sizes = [number for _, number in chunks]
        target = (me_t + step) % n_tensor
        return sent_call(tokens, value_weight, target, columns, chunks[0][0], sizes)

    parts = [[sent_for(step, CHUNKS[:1])[0] for step in others]]
    sent = [[swap_tensor(p, step) for step, p in zip(others, parts[0])]]
    rest_parts = [sent_for(step, CHUNKS[1:]) for step in others]
    parts += [[p[i] for p in rest_parts] for i in range(len(CHUNKS) - 1)]
    done = [table] + [p for group in parts for p in group] + sent[0]
    for stage in range(1, n_adapter):
        if stage < len(CHUNKS):
            sent.append([swap_tensor(after(p, held), step) for step, p in zip(others, parts[stage])])
        came = after(held, *done)
        done = sent[stage] if stage < len(CHUNKS) else []
        if stage < n_adapter - 1:
            held = along_line(came, stage + 1)
        buffers.append([came, swap_cores(came)])
        if stage == 1:
            base, mine, kept = own_call(
                table, here, tokens, value_weight, buffers_of(range(2)), columns, n_adapter, rank
            )
        else:
            mine = shrink_call(stage, table, here, kept, buffers_of(stages_of(stage)), rank)
        add_shrink(mine)
        done = done + [mine]

    value, remaining = early(
        n_adapter,
        n_tensor,
        table,
        here,
        base,
        [c for group in sent for c in group],
        shrinks[:-n_tensor],
        buffers_of(range(n_adapter - 1)),
        rank,
    )
    last = n_adapter - 1
    return late(
        last,
        n_tensor,
        table,
        here,
        remaining,
        shrinks[-n_tensor:],
        buffers_of(stages_of(last)),
        value,
        rank,
    )


def solution(mesh):
    return jax.shard_map(
        on_device,
        mesh=mesh,
        in_specs=(
            P(("groups", "adapter", "dp"), "tensor"),
            P("tensor", None),
            P(("groups", "adapter"), "tensor", None),
            P(("groups", "adapter"), None, None),
            P(("groups", "adapter", "dp")),
            P("groups"),
        ),
        out_specs=P(("groups", "adapter", "dp"), "tensor"),
        check_vma=False,
    )
```

time: 85.5 us -> 69 us (0.81)
  waiting for transfers between devices: 26 us -> 18.1 us
  Pallas kernels: 37.4 us -> 30.9 us
  local copies, waits for them, and re-layouts: 2.96 us -> 0.01 us
  starting transfers between devices: 17.5 us -> 18.6 us
    ppermute x3, waiting for transfers between devices: 10.7 us -> 1.29 us  [along_line(): return lax.ppermute(array, ('adapter', 'dp'), up + down)]
    pallas_call x9, Pallas kernels: 37.4 us -> 30.9 us  [the longest x2 9.97 us: sent_call(): pl.pallas_call(functools.partial(sent_kernel, first, sizes), in_specs=[SM...]
    unnamed x16 -> x6, local copies, waits for them, and re-layouts: 2.96 us -> 0.01 us
  transfers between devices with their start and end apart: 12 -> 12, of which waited for: 6 -> 8; matrix products, arithmetic and copies ran while one was open for 0% -> 0% of each run, Pallas kernels for 40% -> 40%
where the time goes in v5:
time: 69 us; the launch traced here: 67.9 us
  Pallas kernels  30.9 us (45%)
  starting transfers between devices  18.6 us (27%)
  waiting for transfers between devices  18.1 us (26%)
    ppermute x6, waiting for transfers between devices, swap_tensor(): return lax.ppermute(array, 'tensor', pairs)  15.9 us
    ppermute x3, starting transfers between devices, along_line(): return lax.ppermute(array, ('adapter', 'dp'), up + down)  10.3 us
    pallas_call x2, Pallas kernels, sent_call(): pl.pallas_call(functools.partial(sent_kernel, first, sizes), in_specs=[SM...  9.97 us
    pallas_call x1, Pallas kernels, own_call(): pl.pallas_call(functools.partial(own_kernel, n_adapter, rank), in_specs=[...  9.78 us
    ppermute x6, starting transfers between devices, swap_tensor(): return lax.ppermute(array, 'tensor', pairs)  8.31 us
    pallas_call x1, Pallas kernels, early(): pl.pallas_call(functools.partial(early_kernel, n_adapter, n_tensor, rank)...  3.4 us
    pallas_call x2, Pallas kernels, shrink_call(): pl.pallas_call(functools.partial(shrink_kernel, k, rank), in_specs=[SMEM,...  2.83 us
    pallas_call x1, Pallas kernels, message_call(): pl.pallas_call(message_kernel, in_specs=[SMEM, HBM, HBM], out_specs=VMEM,...  1.79 us
  transfers between devices with their start and end apart: 12, of which 8 were waited for; matrix products, arithmetic and copies ran while one was open for 0% of the time, Pallas kernels for 40%

profile of v5, /device:TPU:16, one launch (start us, length us, event | category | flops | bytes accessed | tf_op | source)
XLA Modules:
  0.0 67.9 jit_solution(4023986433102721526)
XLA Ops:
  0.0 0.1 pad_add_fusion.here
  0.1 0.0 copy-start
  0.1 1.8 %shard_map.65.refs_0_.refs_8_ = bf16[128,4608]{1,0:T(8,128)(2,1)S(1)} custom-call(s32[3]{0:T(128)S(1)} %pad_add_fusion.here, bf16[128,4096]{1,0:T(8,128)(2,1)} %bitcast.8, bf16[128,1024]{1,0:T(8,128)(2,1)} %bitcast.9), custom_call_target="tpu_custom_call" | custom-call | bytes 2359296 | tf_op jit(solution)/shard_map/pallas_call | solution.py:77
  1.9 0.0 copy-done
  1.9 3.5 %collective-permute-start = (bf16[128,4608]{1,0:T(8,128)(2,1)S(1)}, bf16[128,4608]{1,0:T(8,128)(2,1)S(1)}, u32[]{:S(2)}, u32[]{:S(2)}) collective-permute-start(bf16[128,4608]{1,0:T(8,128)(2,1)S(1)} %shard_map.65.refs_0_.refs_8_), channel_id=1, source_target_pairs={{0,4},{4,8},{8,12},{5,1},{9,5},{13,9},{2,6},{6,10},{10,14},{7,3},{... | collective-permute-start | bytes 3538952 | tf_op jit(solution)/shard_map/ppermute | solution.py:469
  5.4 3.5 %shard_map.66 = s32[200,512]{1,0:T(8,128)S(1)} custom-call(s32[1]{0:T(128)} %bitcast.6.column, bf16[1024,4096]{1,0:T(8,128)(2,1)} %x_ref.5, bf16[4096,1024]{1,0:T(8,128)(2,1)} %w_ref.5), custom_call_target="tpu_custom_call" | custom-call | flops 1073741824 | bytes 6815744 | tf_op jit(solution)/shard_map/pallas_call | solution.py:227
  8.9 1.6 %collective-permute-start.1 = (s32[200,512]{1,0:T(8,128)S(1)}, s32[200,512]{1,0:T(8,128)S(1)}, u32[]{:S(2)}, u32[]{:S(2)}) collective-permute-start(s32[200,512]{1,0:T(8,128)S(1)} %shard_map.66), channel_id=1, source_target_pairs={{0,2},{2,0},{1,3},{3,1},{4,6},{6,4},{5,7},{7,5},{8,10},{10,8},{9,1... | collective-permute-start | bytes 1228808 | tf_op jit(solution)/shard_map/ppermute | solution.py:464
  10.5 1.4 %shard_map.64.table = s32[32]{0:T(128)} custom-call(s32[3]{0:T(128)} %copy-done, s32[1024]{0:T(1024)} %ids.1, s32[8]{0:T(128)} %slots.1), custom_call_target="tpu_custom_call" | custom-call | bytes 4096 | tf_op jit(solution)/shard_map/pallas_call | solution.py:109
  11.9 0.0 copy-start.1
  12.0 0.0 copy-start.2
  12.0 6.5 %shard_map.67 = (s32[296,512]{1,0:T(8,128)S(1)}, s32[296,512]{1,0:T(8,128)S(1)}) custom-call(s32[1]{0:T(128)} %bitcast.6.column, bf16[1024,4096]{1,0:T(8,128)(2,1)} %x_ref.5, bf16[4096,1024]{1,0:T(8,128)(2,1)} %w_ref.5), custom_call_target="tpu_custom_call" | custom-call | flops 3221225472 | bytes 12058624 | tf_op jit(solution)/shard_map/pallas_call | solution.py:227
  18.4 0.3 collective-permute-done.1.refs_1_
  18.8 1.2 %collective-permute-done.refs_1_.refs_0_.refs_9_ = bf16[128,4608]{1,0:T(8,128)(2,1)S(1)} collective-permute-done((bf16[128,4608]{1,0:T(8,128)(2,1)S(1)}, bf16[128,4608]{1,0:T(8,128)(2,1)S(1)}, u32[]{:S(2)}, u32[]{:S(2)}) %collective-permute-start) | collective-permute-done | bytes 1179680 | tf_op jit(solution)/shard_map/ppermute | solution.py:469
  20.0 0.0 collective-permute-start.2
  20.0 3.5 %collective-permute-start.4 = (bf16[128,4608]{1,0:T(8,128)(2,1)S(1)}, bf16[128,4608]{1,0:T(8,128)(2,1)S(1)}, u32[]{:S(2)}, u32[]{:S(2)}) collective-permute-start(bf16[128,4608]{1,0:T(8,128)(2,1)S(1)} %collective-permute-done.refs_1_.refs_0_.refs_9_), channel_id=1, source_target_pairs={{4,8},{8,12},{5,1},{9,5},{6,10},{10,14},{7,3},{11,7},{20,24},{24,2... | collective-permute-start | bytes 3538952 | tf_op jit(solution)/shard_map/ppermute | solution.py:469
  23.5 1.6 %collective-permute-start.3 = (s32[296,512]{1,0:T(8,128)S(1)}, s32[296,512]{1,0:T(8,128)S(1)}, u32[]{:S(2)}, u32[]{:S(2)}) collective-permute-start(s32[296,512]{1,0:T(8,128)S(1)} %get-tuple-element.21), channel_id=1, source_target_pairs={{0,2},{2,0},{1,3},{3,1},{4,6},{6,4},{5,7},{7,5},{8,10},{10,8},{9,1... | collective-permute-start | bytes 1818632 | tf_op jit(solution)/shard_map/ppermute | solution.py:464
  25.0 0.0 collective-permute-done.2.refs_2_.refs_1_.refs_10_
  25.0 0.0 copy-done.1
  25.0 0.0 copy-done.2
  25.0 9.8 %shard_map.68 = (f32[1024,512]{1,0:T(8,128)S(1)}, f32[2,128,128]{2,1,0:T(8,128)S(1)}, bf16[2,2,128,4096]{3,2,1,0:T(8,128)(2,1)S(1)}) custom-call(s32[32]{0:T(128)S(1)} %copy-done.2, s32[3]{0:T(128)S(1)} %copy-done.1, bf16[1024,4096]{1,0:T(8,128)(2,1)} %x_ref.5, bf16[4096,1024]{1,0:T(8,128)(2,1)} %w_ref.5, bf16[128,4608]{1,0:T(8,128)(2,1)S(1)} %shard_map.65.refs_0_.refs_8_, ...), custom_call_target="tpu_custom_call" | custom-call | flops 4294967296 | bytes 14680064 | tf_op jit(solution)/shard_map/pallas_call | solution.py:289
  34.8 3.5 %collective-permute-done.3.refs_2_ = s32[296,512]{1,0:T(8,128)S(1)} collective-permute-done((s32[296,512]{1,0:T(8,128)S(1)}, s32[296,512]{1,0:T(8,128)S(1)}, u32[]{:S(2)}, u32[]{:S(2)}) %collective-permute-start.3) | collective-permute-done | bytes 606240 | tf_op jit(solution)/shard_map/ppermute | solution.py:464
  38.3 0.0 collective-permute-done.4.refs_2_.refs_11_.refs_0_.refs_3_
  38.3 0.0 collective-permute-start.7
  38.3 3.3 %collective-permute-start.9 = (bf16[128,4608]{1,0:T(8,128)(2,1)S(1)}, bf16[128,4608]{1,0:T(8,128)(2,1)S(1)}, u32[]{:S(2)}, u32[]{:S(2)}) collective-permute-start(bf16[128,4608]{1,0:T(8,128)(2,1)S(1)} %collective-permute-done.4.refs_2_.refs_11_.refs_0_.refs_3_), channel_id=1, source_target_pairs={{8,12},{5,1},{10,14},{7,3},{24,28},{21,17},{26,30},{23,19}} | collective-permute-start | bytes 3538952 | tf_op jit(solution)/shard_map/ppermute | solution.py:469
  41.6 1.6 %collective-permute-start.5 = (s32[296,512]{1,0:T(8,128)S(1)}, s32[296,512]{1,0:T(8,128)S(1)}, u32[]{:S(2)}, u32[]{:S(2)}) collective-permute-start(s32[296,512]{1,0:T(8,128)S(1)} %get-tuple-element.22), channel_id=1, source_target_pairs={{0,2},{2,0},{1,3},{3,1},{4,6},{6,4},{5,7},{7,5},{8,10},{10,8},{9,1... | collective-permute-start | bytes 1818632 | tf_op jit(solution)/shard_map/ppermute | solution.py:464
  43.2 0.0 collective-permute-done.7.refs_3_.refs_12_.refs_1_.refs_4_
  43.2 1.3 %shard_map.69.refs_6_ = f32[1,128,128]{2,1,0:T(8,128)S(1)} custom-call(s32[32]{0:T(128)S(1)} %copy-done.2, s32[3]{0:T(128)S(1)} %copy-done.1, bf16[2,2,128,4096]{3,2,1,0:T(8,128)(2,1)S(1)} %get-tuple-element.24.kept_ref, bf16[128,4608]{1,0:T(8,128)(2,1)S(1)} %collective-permute-done.refs_1_.refs_0_.refs_9_, ...), custom_call_target="tpu_custom_call" | custom-call | flops 536870912 | bytes 2097152 | tf_op jit(solution)/shard_map/pallas_call | solution.py:316
  44.5 10.7 %collective-permute-done.5.refs_3_ = s32[296,512]{1,0:T(8,128)S(1)} collective-permute-done((s32[296,512]{1,0:T(8,128)S(1)}, s32[296,512]{1,0:T(8,128)S(1)}, u32[]{:S(2)}, u32[]{:S(2)}) %collective-permute-start.5) | collective-permute-done | bytes 606240 | tf_op jit(solution)/shard_map/ppermute | solution.py:464
  55.2 0.1 collective-permute-done.9.refs_2_.refs_5_
  55.3 0.0 collective-permute-start.10
  55.3 1.5 %collective-permute-start.6 = (f32[2,128,128]{2,1,0:T(8,128)S(1)}, f32[2,128,128]{2,1,0:T(8,128)S(1)}, u32[]{:S(2)}, u32[]{:S(2)}) collective-permute-start(f32[2,128,128]{2,1,0:T(8,128)S(1)} %get-tuple-element.23.refs_4_), channel_id=1, source_target_pairs={{0,2},{2,0},{1,3},{3,1},{4,6},{6,4},{5,7},{7,5},{8,10},{10,8},{9,1... | collective-permute-start | bytes 393224 | tf_op jit(solution)/shard_map/ppermute | solution.py:464
  56.7 0.5 collective-permute-start.8
  57.3 0.8 %collective-permute-done.10.refs_3_.refs_6_ = bf16[128,4608]{1,0:T(8,128)(2,1)S(1)} collective-permute-done((bf16[128,4608]{1,0:T(8,128)(2,1)S(1)}, bf16[128,4608]{1,0:T(8,128)(2,1)S(1)}, u32[]{:S(2)}, u32[]{:S(2)}) %collective-permute-start.10) | collective-permute-done | bytes 1179680 | tf_op jit(solution)/shard_map/ppermute | solution.py:472
  58.1 1.5 %shard_map.71.refs_1_ = f32[1,128,128]{2,1,0:T(8,128)S(1)} custom-call(s32[32]{0:T(128)S(1)} %copy-done.2, s32[3]{0:T(128)S(1)} %copy-done.1, bf16[2,2,128,4096]{3,2,1,0:T(8,128)(2,1)S(1)} %get-tuple-element.24.kept_ref, bf16[128,4608]{1,0:T(8,128)(2,1)S(1)} %collective-permute-done.4.refs_2_.refs_11_.refs_0_.refs_3_, ...), custom_call_target="tpu_custom_call" | custom-call | flops 536870912 | bytes 2097152 | tf_op jit(solution)/shard_map/pallas_call | solution.py:316
  59.6 1.6 %collective-permute-start.11 = (f32[1,128,128]{2,1,0:T(8,128)S(1)}, f32[1,128,128]{2,1,0:T(8,128)S(1)}, u32[]{:S(2)}, u32[]{:S(2)}) collective-permute-start(f32[1,128,128]{2,1,0:T(8,128)S(1)} %shard_map.71.refs_1_), channel_id=1, source_target_pairs={{0,2},{2,0},{1,3},{3,1},{4,6},{6,4},{5,7},{7,5},{8,10},{10,8},{9,1... | collective-permute-start | bytes 196616 | tf_op jit(solution)/shard_map/ppermute | solution.py:464
  61.2 0.4 collective-permute-done.6.refs_5_
  61.6 1.1 %collective-permute-done.8.refs_7_ = f32[1,128,128]{2,1,0:T(8,128)S(1)} collective-permute-done((f32[1,128,128]{2,1,0:T(8,128)S(1)}, f32[1,128,128]{2,1,0:T(8,128)S(1)}, u32[]{:S(2)}, u32[]{:S(2)}) %collective-permute-start.8) | collective-permute-done | bytes 65568 | tf_op jit(solution)/shard_map/ppermute | solution.py:464
  62.7 3.4 %shard_map.70 = (bf16[1024,512]{1,0:T(8,128)(2,1)}, f32[2,128,512]{2,1,0:T(8,128)S(1)}) custom-call(s32[32]{0:T(128)S(1)} %copy-done.2, s32[3]{0:T(128)S(1)} %copy-done.1, f32[1024,512]{1,0:T(8,128)S(1)} %get-tuple-element.20.refs_0_, s32[200,512]{1,0:T(8,128)S(1)} %collective-permute-done.1.refs_1_, s32[296,512]{1,0:T(8,128)S(1)} %collective-permute-done.3.refs_2_, ...), custom_call_target="tpu_custom_call" | custom-call | flops 201326592 | bytes 5242880 | tf_op jit(solution)/shard_map/pallas_call | solution.py:390
  66.1 0.0 collective-permute-done.11.refs_2_
  66.1 1.7 %shard_map.72 = bf16[1024,512]{1,0:T(8,128)(2,1)} custom-call(s32[32]{0:T(128)S(1)} %copy-done.2, s32[3]{0:T(128)S(1)} %copy-done.1, f32[2,128,512]{2,1,0:T(8,128)S(1)} %get-tuple-element.26.refs_0_, f32[1,128,128]{2,1,0:T(8,128)S(1)} %shard_map.71.refs_1_, f32[1,128,128]{2,1,0:T(8,128)S(1)} %collective-permute-done.11.refs_2_, ...), custom_call_target="tpu_custom_call", output_to_operand_aliasing={{}: (9, {})} | custom-call | flops 50331648 | bytes 1048576 | tf_op jit(solution)/shard_map/pallas_call | solution.py:429
Async XLA Ops:
  0.1 1.8 %copy-start = (s32[3]{0:T(128)}, s32[3]{0:T(128)S(1)}, u32[]{:S(2)}) copy-start(s32[3]{0:T(128)S(1)} %pad_add_fusion.here) | copy-start | bytes 40
  1.9 18.1 %collective-permute-start = (bf16[128,4608]{1,0:T(8,128)(2,1)S(1)}, bf16[128,4608]{1,0:T(8,128)(2,1)S(1)}, u32[]{:S(2)}, u32[]{:S(2)}) collective-permute-start(bf16[128,4608]{1,0:T(8,128)(2,1)S(1)} %shard_map.65.refs_0_.refs_8_), channel_id=1, source_target_pairs={{0,4},{4,8},{8,12},{5,1},{9,5},{13,9},{2,6},{6,10},{10,14},{7,3},{... | collective-permute-start | bytes 3538952 | tf_op jit(solution)/shard_map/ppermute | solution.py:469
  8.9 9.9 %collective-permute-start.1 = (s32[200,512]{1,0:T(8,128)S(1)}, s32[200,512]{1,0:T(8,128)S(1)}, u32[]{:S(2)}, u32[]{:S(2)}) collective-permute-start(s32[200,512]{1,0:T(8,128)S(1)} %shard_map.66), channel_id=1, source_target_pairs={{0,2},{2,0},{1,3},{3,1},{4,6},{6,4},{5,7},{7,5},{8,10},{10,8},{9,1... | collective-permute-start | bytes 1228808 | tf_op jit(solution)/shard_map/ppermute | solution.py:464
  11.9 13.1 %copy-start.1 = (s32[3]{0:T(128)S(1)}, s32[3]{0:T(128)}, u32[]{:S(2)}) copy-start(s32[3]{0:T(128)} %copy-done) | copy-start | bytes 40
  12.0 13.1 %copy-start.2 = (s32[32]{0:T(128)S(1)}, s32[32]{0:T(128)}, u32[]{:S(2)}) copy-start(s32[32]{0:T(128)} %shard_map.64.table) | copy-start | bytes 388
  20.0 5.0 %collective-permute-start.2 = (bf16[128,4608]{1,0:T(8,128)(2,1)S(1)}, bf16[128,4608]{1,0:T(8,128)(2,1)S(1)}, u32[]{:S(2)}, u32[]{:S(2)}) collective-permute-start(bf16[128,4608]{1,0:T(8,128)(2,1)S(1)} %collective-permute-done.refs_1_.refs_0_.refs_9_), channel_id=1, source_target_pairs={{0,1},{1,0},{2,3},{3,2},{4,5},{5,4},{6,7},{7,6},{8,9},{9,8},{10,11... | collective-permute-start | bytes 3538952 | tf_op jit(solution)/shard_map/ppermute | solution.py:472
  20.0 18.3 %collective-permute-start.4 = (bf16[128,4608]{1,0:T(8,128)(2,1)S(1)}, bf16[128,4608]{1,0:T(8,128)(2,1)S(1)}, u32[]{:S(2)}, u32[]{:S(2)}) collective-permute-start(bf16[128,4608]{1,0:T(8,128)(2,1)S(1)} %collective-permute-done.refs_1_.refs_0_.refs_9_), channel_id=1, source_target_pairs={{4,8},{8,12},{5,1},{9,5},{6,10},{10,14},{7,3},{11,7},{20,24},{24,2... | collective-permute-start | bytes 3538952 | tf_op jit(solution)/shard_map/ppermute | solution.py:469
  23.5 14.8 %collective-permute-start.3 = (s32[296,512]{1,0:T(8,128)S(1)}, s32[296,512]{1,0:T(8,128)S(1)}, u32[]{:S(2)}, u32[]{:S(2)}) collective-permute-start(s32[296,512]{1,0:T(8,128)S(1)} %get-tuple-element.21), channel_id=1, source_target_pairs={{0,2},{2,0},{1,3},{3,1},{4,6},{6,4},{5,7},{7,5},{8,10},{10,8},{9,1... | collective-permute-start | bytes 1818632 | tf_op jit(solution)/shard_map/ppermute | solution.py:464
  38.3 4.9 %collective-permute-start.7 = (bf16[128,4608]{1,0:T(8,128)(2,1)S(1)}, bf16[128,4608]{1,0:T(8,128)(2,1)S(1)}, u32[]{:S(2)}, u32[]{:S(2)}) collective-permute-start(bf16[128,4608]{1,0:T(8,128)(2,1)S(1)} %collective-permute-done.4.refs_2_.refs_11_.refs_0_.refs_3_), channel_id=1, source_target_pairs={{0,1},{1,0},{2,3},{3,2},{4,5},{5,4},{6,7},{7,6},{8,9},{9,8},{10,11... | collective-permute-start | bytes 3538952 | tf_op jit(solution)/shard_map/ppermute | solution.py:472
  38.3 17.0 %collective-permute-start.9 = (bf16[128,4608]{1,0:T(8,128)(2,1)S(1)}, bf16[128,4608]{1,0:T(8,128)(2,1)S(1)}, u32[]{:S(2)}, u32[]{:S(2)}) collective-permute-start(bf16[128,4608]{1,0:T(8,128)(2,1)S(1)} %collective-permute-done.4.refs_2_.refs_11_.refs_0_.refs_3_), channel_id=1, source_target_pairs={{8,12},{5,1},{10,14},{7,3},{24,28},{21,17},{26,30},{23,19}} | collective-permute-start | bytes 3538952 | tf_op jit(solution)/shard_map/ppermute | solution.py:469
  41.6 13.6 %collective-permute-start.5 = (s32[296,512]{1,0:T(8,128)S(1)}, s32[296,512]{1,0:T(8,128)S(1)}, u32[]{:S(2)}, u32[]{:S(2)}) collective-permute-start(s32[296,512]{1,0:T(8,128)S(1)} %get-tuple-element.22), channel_id=1, source_target_pairs={{0,2},{2,0},{1,3},{3,1},{4,6},{6,4},{5,7},{7,5},{8,10},{10,8},{9,1... | collective-permute-start | bytes 1818632 | tf_op jit(solution)/shard_map/ppermute | solution.py:464
  55.3 2.8 %collective-permute-start.10 = (bf16[128,4608]{1,0:T(8,128)(2,1)S(1)}, bf16[128,4608]{1,0:T(8,128)(2,1)S(1)}, u32[]{:S(2)}, u32[]{:S(2)}) collective-permute-start(bf16[128,4608]{1,0:T(8,128)(2,1)S(1)} %collective-permute-done.9.refs_2_.refs_5_), channel_id=1, source_target_pairs={{0,1},{1,0},{2,3},{3,2},{4,5},{5,4},{6,7},{7,6},{8,9},{9,8},{10,11... | collective-permute-start | bytes 3538952 | tf_op jit(solution)/shard_map/ppermute | solution.py:472
  55.3 6.3 %collective-permute-start.6 = (f32[2,128,128]{2,1,0:T(8,128)S(1)}, f32[2,128,128]{2,1,0:T(8,128)S(1)}, u32[]{:S(2)}, u32[]{:S(2)}) collective-permute-start(f32[2,128,128]{2,1,0:T(8,128)S(1)} %get-tuple-element.23.refs_4_), channel_id=1, source_target_pairs={{0,2},{2,0},{1,3},{3,1},{4,6},{6,4},{5,7},{7,5},{8,10},{10,8},{9,1... | collective-permute-start | bytes 393224 | tf_op jit(solution)/shard_map/ppermute | solution.py:464
  56.7 5.9 %collective-permute-start.8 = (f32[1,128,128]{2,1,0:T(8,128)S(1)}, f32[1,128,128]{2,1,0:T(8,128)S(1)}, u32[]{:S(2)}, u32[]{:S(2)}) collective-permute-start(f32[1,128,128]{2,1,0:T(8,128)S(1)} %shard_map.69.refs_6_), channel_id=1, source_target_pairs={{0,2},{2,0},{1,3},{3,1},{4,6},{6,4},{5,7},{7,5},{8,10},{10,8},{9,1... | collective-permute-start | bytes 196616 | tf_op jit(solution)/shard_map/ppermute | solution.py:464
  59.6 6.5 %collective-permute-start.11 = (f32[1,128,128]{2,1,0:T(8,128)S(1)}, f32[1,128,128]{2,1,0:T(8,128)S(1)}, u32[]{:S(2)}, u32[]{:S(2)}) collective-permute-start(f32[1,128,128]{2,1,0:T(8,128)S(1)} %shard_map.71.refs_1_), channel_id=1, source_target_pairs={{0,2},{2,0},{1,3},{3,1},{4,6},{6,4},{5,7},{7,5},{8,10},{10,8},{9,1... | collective-permute-start | bytes 196616 | tf_op jit(solution)/shard_map/ppermute | solution.py:464

commit v6 on v5

--- a/solution.py
+++ b/solution.py
@@ -12,7 +12,7 @@
 MOST = 2
 BLOCK = 256
 PIECES = 4
-CHUNKS = ((6, 2), (0, 3), (3, 3))
+CHUNKS = ((6, 2), (0, 4), (4, 2))
 ENTRIES = 8
 MIDDLE = 1.5 * 2.0**23
 
@@ -120,8 +120,8 @@
     return lax.broadcasted_iota(jnp.int32, shape, 0) == lax.broadcasted_iota(jnp.int32, shape, 1)
 
 
-WORDS = SEGMENT_ROWS * 3 // 4
-QUARTER = SEGMENT_ROWS // 4
+GROUP = SEGMENT_ROWS // 8
+WORDS = 5 * GROUP
 
 
 def coded_rows(segments):
@@ -131,23 +131,33 @@
 def encode(values, o_ref, unit, units):
     largest = jnp.maximum(jnp.max(jnp.abs(values), axis=1, keepdims=True), 2.0**-100)
     power = jnp.floor(jnp.log2(largest))
-    whole = (values * jnp.exp2(21.0 - power) + MIDDLE).astype(jnp.int32) - int(MIDDLE)
-    q = [whole[i * QUARTER : (i + 1) * QUARTER] for i in range(4)]
-    for i in range(3):
-        o_ref[unit * WORDS + i * QUARTER : unit * WORDS + (i + 1) * QUARTER, :] = (
-            q[i] & 0xFFFFFF
-        ) | ((q[3] >> (8 * i)) << 24)
+    whole = (values * jnp.exp2(18.0 - power) + MIDDLE).astype(jnp.int32) - int(MIDDLE)
+    whole = jnp.minimum(whole, 2**19 - 1)
+    v = [whole[i * GROUP : (i + 1) * GROUP] for i in range(8)]
+    over = [
+        v[5] & 0xFFF,
+        ((v[5] >> 12) & 0xFF) | ((v[6] & 0xF) << 8),
+        (v[6] >> 4) & 0xFFF,
+        ((v[6] >> 16) & 0xF) | ((v[7] & 0xFF) << 4),
+        v[7] >> 8,
+    ]
+    for i in range(5):
+        o_ref[unit * WORDS + i * GROUP : unit * WORDS + (i + 1) * GROUP, :] = (v[i] & 0xFFFFF) | (
+            over[i] << 20
+        )
     row = jnp.sum(jnp.where(diagonal(), power, 0.0), axis=0, keepdims=True)
     o_ref[units * WORDS + unit : units * WORDS + unit + 1, :SEGMENT_ROWS] = row.astype(jnp.int32)
 
 
 def decode(ref, unit, units):
-    w = [ref[unit * WORDS + i * QUARTER : unit * WORDS + (i + 1) * QUARTER, :] for i in range(3)]
-    q = [(x << 8) >> 8 for x in w]
-    q.append(((w[0] >> 24) & 0xFF) | (((w[1] >> 24) & 0xFF) << 8) | ((w[2] >> 24) << 16))
+    w = [ref[unit * WORDS + i * GROUP : unit * WORDS + (i + 1) * GROUP, :] for i in range(5)]
+    v = [(x << 12) >> 12 for x in w]
+    v.append(((w[0] >> 20) & 0xFFF) | (((w[1] << 4) >> 24) << 12))
+    v.append(((w[1] >> 28) & 0xF) | (((w[2] >> 20) & 0xFFF) << 4) | (((w[3] << 8) >> 28) << 16))
+    v.append(((w[3] >> 24) & 0xFF) | ((w[4] >> 20) << 8))
     row = ref[units * WORDS + unit : units * WORDS + unit + 1, :SEGMENT_ROWS].astype(jnp.float32)
     power = jnp.sum(jnp.where(diagonal(), row, 0.0), axis=1, keepdims=True)
-    return jnp.concatenate(q, axis=0).astype(jnp.float32) * jnp.exp2(power - 21.0)
+    return jnp.concatenate(v, axis=0).astype(jnp.float32) * jnp.exp2(power - 18.0)
 
 
 def load_base(first, segments, column, x_ref, w_ref, x, w, sems):
@@ -256,71 +266,72 @@
     return range((k + 1) // 2, k + 1)
 
 
-def own_kernel(n_adapter, rank, table, here, x_ref, w_ref, *refs):
-    buffers, (o_ref, s_ref, kept_ref, x, w, sems, kept_sems) = refs[:3], refs[3:]
+def own_kernel(n_adapter, rank, table, here, x_ref, w_ref, message, *refs):
+    o_ref, s_ref, kept_ref, x, w, sems, kept_sems = refs
     work = load_base(0, x.shape[0] // SEGMENT_ROWS, here[2], x_ref, w_ref, x, w, sems)
     keeps = []
     for at, size, terms in work:
         o_ref[at : at + size, :] = block_product(x, w, at, size, terms)
-    for k in range(2, n_adapter):
+    for k in range(1, n_adapter):
         for j in range(MOST):
             start, _, _ = segment_of(table, k, j)
             keeps.append(
                 pltpu.make_async_copy(
-                    x.at[pl.ds(start, SEGMENT_ROWS), :], kept_ref.at[k - 2, j], kept_sems.at[k - 2, j]
+                    x.at[pl.ds(start, SEGMENT_ROWS), :], kept_ref.at[k - 1, j], kept_sems.at[k - 1, j]
                 )
             )
             keeps[-1].start()
-    for k in range(2):
-
-        def rows_of(j, k=k):
-            start, _, _ = segment_of(table, k, j)
-            return x[pl.ds(start, SEGMENT_ROWS), :]
-
-        here_buffers = buffers[:1] if k == 0 else buffers[1:]
-        shrink_into(s_ref, k, table, k, rows_of, here_buffers, buffer_owners(here, stages_of(k)), rank)
+
+    def rows_of(j):
+        start, _, _ = segment_of(table, 0, j)
+        return x[pl.ds(start, SEGMENT_ROWS), :]
+
+    shrink_into(s_ref, 0, table, 0, rows_of, [message], [here[0]], rank)
     for copy in keeps:
         copy.wait()
 
 
-def own_call(table, here, tokens, weight, buffers, columns, n_adapter, rank):
+def own_call(table, here, tokens, weight, message, columns, n_adapter, rank):
     rows, width = tokens.shape
     segments = rows // SEGMENT_ROWS
     return pl.pallas_call(
         functools.partial(own_kernel, n_adapter, rank),
-        in_specs=[SMEM, SMEM, HBM, HBM] + [VMEM] * len(buffers),
+        in_specs=[SMEM, SMEM, HBM, HBM, VMEM],
         out_specs=[VMEM] * 3,
         out_shape=[
             jax.ShapeDtypeStruct((rows, columns), jnp.float32),
-            jax.ShapeDtypeStruct((2, SEGMENT_ROWS, MOST * rank), jnp.float32),
-            jax.ShapeDtypeStruct((n_adapter - 2, MOST, SEGMENT_ROWS, width), jnp.bfloat16),
+            jax.ShapeDtypeStruct((1, SEGMENT_ROWS, MOST * rank), jnp.float32),
+            jax.ShapeDtypeStruct((n_adapter - 1, MOST, SEGMENT_ROWS, width), jnp.bfloat16),
         ],
         scratch_shapes=base_scratch(segments, width, columns)
-        + [pltpu.SemaphoreType.DMA((n_adapter - 2, MOST))],
+        + [pltpu.SemaphoreType.DMA((n_adapter - 1, MOST))],
         compiler_params=params(32),
         cost_estimate=cost(
             2 * rows * width * columns, 2 * rows * width + 2 * width * columns + 4 * rows * columns
         ),
-    )(table, here, tokens, weight, *buffers)
-
-
-def shrink_kernel(k, rank, table, here, kept_ref, *refs):
-    buffers, o_ref = refs[:-1], refs[-1]
-    shrink_into(
-        o_ref, 0, table, k, lambda j: kept_ref[k - 2, j], buffers, buffer_owners(here, stages_of(k)), rank
-    )
-
-
-def shrink_call(k, table, here, kept, buffers, rank):
+    )(table, here, tokens, weight, message)
+
+
+def shrink_kernel(k, rank, n_before, table, here, kept_ref, *refs):
+    buffers, o_ref = refs[n_before:-1], refs[-1]
+    for r in refs[:n_before]:
+        o_ref[:1] = r[...]
+    rows_of = lambda j: kept_ref[k - 1, j]
+    owners = buffer_owners(here, stages_of(k))
+    shrink_into(o_ref, n_before, table, k, rows_of, buffers, owners, rank)
+
+
+def shrink_call(k, table, here, kept, before, buffers, rank):
     width = kept.shape[3]
-    return pl.pallas_call(
-        functools.partial(shrink_kernel, k, rank),
-        in_specs=[SMEM, SMEM, VMEM] + [VMEM] * len(buffers),
+    n = 1 + len(before)
+    return pl.pallas_call(
+        functools.partial(shrink_kernel, k, rank, len(before)),
+        in_specs=[SMEM, SMEM, VMEM] + [VMEM] * (n - 1 + len(buffers)),
         out_specs=VMEM,
-        out_shape=jax.ShapeDtypeStruct((1, SEGMENT_ROWS, MOST * rank), jnp.float32),
+        out_shape=jax.ShapeDtypeStruct((n, SEGMENT_ROWS, MOST * rank), jnp.float32),
         compiler_params=params(16),
         cost_estimate=cost(MOST * 2 * SEGMENT_ROWS * width * 256, 4 * SEGMENT_ROWS * width),
-    )(table, here, kept, *buffers)
+    )(table, here, kept, *before, *buffers)
 
 
 def fetch_up(up, at, table, k, j, buffers, owners, rank):
@@ -346,9 +357,9 @@
 
 
 def early_kernel(n_adapter, n_tensor, rank, table, here, *refs):
-    n_coded, n_calls = len(CHUNKS) * (n_tensor - 1), n_adapter - 2
+    n_coded, n_buffers = len(CHUNKS) * (n_tensor - 1), 2 * n_adapter - 3
     base_ref, coded_refs, refs = refs[0], refs[1 : 1 + n_coded], refs[1 + n_coded :]
-    shrinks, refs = refs[: n_calls * n_tensor], refs[n_calls * n_tensor :]
+    shrinks, refs = refs[: -4 - n_buffers], refs[-4 - n_buffers :]
     buffers, (o_ref, rest_ref, up, total) = refs[:-4], refs[-4:]
     for k in range(n_adapter - 1):
         at = 0 if k == 0 else 2 * stages_of(k)[0] - 1
@@ -357,7 +368,7 @@
         for j in range(MOST):
             fetch_up(up, k * MOST + j, table, k, j, buffers[at:to], owners, rank)
     shares = []
-    for call in range(n_calls):
+    for call in range(len(shrinks) // n_tensor):
         share = shrinks[call * n_tensor][...]
         for i in range(1, n_tensor):
             share = share + shrinks[call * n_tensor + i][...]
@@ -496,27 +507,35 @@
         return sent_call(tokens, value_weight, target, columns, chunks[0][0], sizes)
 
     parts = [[sent_for(step, CHUNKS[:1])[0] for step in others]]
-    sent = [[swap_tensor(p, step) for step, p in zip(others, parts[0])]]
     rest_parts = [sent_for(step, CHUNKS[1:]) for step in others]
     parts += [[p[i] for p in rest_parts] for i in range(len(CHUNKS) - 1)]
+    sent = [[swap_tensor(p, step) for step, p in zip(others, parts[0])]]
+    last = n_adapter - 1
     done = [table] + [p for group in parts for p in group] + sent[0]
-    for stage in range(1, n_adapter):
+    before = None
+    for stage in range(1, last):
+        came = after(held, *done)
+        held = along_line(came, stage + 1)
         if stage < len(CHUNKS):
-            sent.append([swap_tensor(after(p, held), step) for step, p in zip(others, parts[stage])])
-        came = after(held, *done)
-        done = sent[stage] if stage < len(CHUNKS) else []
-        if stage < n_adapter - 1:
-            held = along_line(came, stage + 1)
+            sent.append([swap_tensor(after(p, came), step) for step, p in zip(others, parts[stage])])
+        if stage == 1:
+            base, before, kept = own_call(
+                after(table, came), here, tokens, value_weight, message, columns, n_adapter, rank
+            )
+            add_shrink(before)
+            done = sent[1] + [before]
+        else:
+            before = shrink_call(
+                stage - 1, table, here, after(kept, came), [], buffers_of(stages_of(stage - 1)), rank
+            )
+            if stage < last - 1:
+                add_shrink(before)
+            done = []
         buffers.append([came, swap_cores(came)])
-        if stage == 1:
-            base, mine, kept = own_call(
-                table, here, tokens, value_weight, buffers_of(range(2)), columns, n_adapter, rank
-            )
-        else:
-            mine = shrink_call(stage, table, here, kept, buffers_of(stages_of(stage)), rank)
-        add_shrink(mine)
-        done = done + [mine]
-
+    merged = shrink_call(
+        last - 1, table, here, kept, [before], buffers_of(stages_of(last - 1)), rank
+    )
+    add_shrink(merged)
     value, remaining = early(
         n_adapter,
         n_tensor,
@@ -524,11 +543,13 @@
         here,
         base,
         [c for group in sent for c in group],
-        shrinks[:-n_tensor],
-        buffers_of(range(n_adapter - 1)),
+        shrinks,
+        buffers_of(range(last)),
         rank,
     )
-    last = n_adapter - 1
+    came = after(held, value)
+    buffers.append([came, swap_cores(came)])
+    add_shrink(shrink_call(last, table, here, kept, [], buffers_of(stages_of(last)), rank))
     return late(
         last,
         n_tensor,

time: 69 us -> 68.2 us (0.988)
  waiting for transfers between devices: 18.1 us -> 16.5 us
  Pallas kernels: 30.9 us -> 31.8 us
    ppermute x6, waiting for transfers between devices: 15.9 us -> 12.2 us  [swap_tensor(): return lax.ppermute(array, 'tensor', pairs)]
    ppermute x3, waiting for transfers between devices: 0.82 us -> 2.85 us  [swap_cores(): return lax.ppermute(array, 'dp', [(0, 1), (1, 0)])]
    pallas_call x2 -> x3, Pallas kernels: 2.83 us -> 4.14 us  [shrink_call(): pl.pallas_call(functools.partial(shrink_kernel, k, rank, len(before)), in...]
  transfers between devices with their start and end apart: 12 -> 12, of which waited for: 8 -> 5; matrix products, arithmetic and copies ran while one was open for 0% -> 0% of each run, Pallas kernels for 40% -> 40%
where the time goes in v6:
time: 68.2 us; the launch traced here: 67.4 us
  Pallas kernels  31.8 us (47%)
  starting transfers between devices  18.8 us (28%)
  waiting for transfers between devices  16.5 us (24%)
    ppermute x6, waiting for transfers between devices, swap_tensor(): return lax.ppermute(array, 'tensor', pairs)  12.2 us
    ppermute x3, starting transfers between devices, along_line(): return lax.ppermute(array, ('adapter', 'dp'), up + down)  10.4 us
    pallas_call x2, Pallas kernels, sent_call(): pl.pallas_call(functools.partial(sent_kernel, first, sizes), in_specs=[SM...  10.1 us
    pallas_call x1, Pallas kernels, own_call(): pl.pallas_call(functools.partial(own_kernel, n_adapter, rank), in_specs=[...  9.2 us
    ppermute x6, starting transfers between devices, swap_tensor(): return lax.ppermute(array, 'tensor', pairs)  8.37 us
    pallas_call x3, Pallas kernels, shrink_call(): pl.pallas_call(functools.partial(shrink_kernel, k, rank, len(before)), in...  4.14 us
    pallas_call x1, Pallas kernels, early(): pl.pallas_call(functools.partial(early_kernel, n_adapter, n_tensor, rank)...  3.41 us
    ppermute x3, waiting for transfers between devices, swap_cores(): return lax.ppermute(array, 'dp', [(0, 1), (1, 0)])  2.85 us
  transfers between devices with their start and end apart: 12, of which 5 were waited for; matrix products, arithmetic and copies ran while one was open for 0% of the time, Pallas kernels for 40%

profile of v6, /device:TPU:16, one launch (start us, length us, event | category | flops | bytes accessed | tf_op | source)
XLA Modules:
  0.0 67.4 jit_solution(10148805397793984247)
XLA Ops:
  0.0 0.1 pad_add_fusion.here
  0.1 0.0 copy-start
  0.1 1.8 %shard_map.65.message.refs_8_ = bf16[128,4608]{1,0:T(8,128)(2,1)S(1)} custom-call(s32[3]{0:T(128)S(1)} %pad_add_fusion.here, bf16[128,4096]{1,0:T(8,128)(2,1)} %bitcast.8, bf16[128,1024]{1,0:T(8,128)(2,1)} %bitcast.9), custom_call_target="tpu_custom_call" | custom-call | bytes 2359296 | tf_op jit(solution)/shard_map/pallas_call | solution.py:77
  1.9 0.0 copy-done
  1.9 3.5 %collective-permute-start = (bf16[128,4608]{1,0:T(8,128)(2,1)S(1)}, bf16[128,4608]{1,0:T(8,128)(2,1)S(1)}, u32[]{:S(2)}, u32[]{:S(2)}) collective-permute-start(bf16[128,4608]{1,0:T(8,128)(2,1)S(1)} %shard_map.65.message.refs_8_), channel_id=1, source_target_pairs={{0,4},{4,8},{8,12},{5,1},{9,5},{13,9},{2,6},{6,10},{10,14},{7,3},{... | collective-permute-start | bytes 3538952 | tf_op jit(solution)/shard_map/ppermute | solution.py:480
  5.4 3.6 %shard_map.66 = s32[168,512]{1,0:T(8,128)S(1)} custom-call(s32[1]{0:T(128)} %bitcast.6.column, bf16[1024,4096]{1,0:T(8,128)(2,1)} %x_ref.5, bf16[4096,1024]{1,0:T(8,128)(2,1)} %w_ref.5), custom_call_target="tpu_custom_call" | custom-call | flops 1073741824 | bytes 6815744 | tf_op jit(solution)/shard_map/pallas_call | solution.py:237
  9.0 1.6 %collective-permute-start.1 = (s32[168,512]{1,0:T(8,128)S(1)}, s32[168,512]{1,0:T(8,128)S(1)}, u32[]{:S(2)}, u32[]{:S(2)}) collective-permute-start(s32[168,512]{1,0:T(8,128)S(1)} %shard_map.66), channel_id=1, source_target_pairs={{0,2},{2,0},{1,3},{3,1},{4,6},{6,4},{5,7},{7,5},{8,10},{10,8},{9,1... | collective-permute-start | bytes 1032200 | tf_op jit(solution)/shard_map/ppermute | solution.py:475
  10.6 1.4 %shard_map.64.table = s32[32]{0:T(128)} custom-call(s32[3]{0:T(128)} %copy-done, s32[1024]{0:T(1024)} %ids.1, s32[8]{0:T(128)} %slots.1), custom_call_target="tpu_custom_call" | custom-call | bytes 4096 | tf_op jit(solution)/shard_map/pallas_call | solution.py:109
  12.0 0.0 copy-start.1
  12.0 0.0 copy-start.2
  12.0 6.6 %shard_map.67 = (s32[328,512]{1,0:T(8,128)S(1)}, s32[168,512]{1,0:T(8,128)S(1)}) custom-call(s32[1]{0:T(128)} %bitcast.6.column, bf16[1024,4096]{1,0:T(8,128)(2,1)} %x_ref.5, bf16[4096,1024]{1,0:T(8,128)(2,1)} %w_ref.5), custom_call_target="tpu_custom_call" | custom-call | flops 3221225472 | bytes 12058624 | tf_op jit(solution)/shard_map/pallas_call | solution.py:237
  18.6 0.0 collective-permute-done.1.refs_1_
  18.6 1.4 %collective-permute-done.refs_0_.refs_1_.refs_9_ = bf16[128,4608]{1,0:T(8,128)(2,1)S(1)} collective-permute-done((bf16[128,4608]{1,0:T(8,128)(2,1)S(1)}, bf16[128,4608]{1,0:T(8,128)(2,1)S(1)}, u32[]{:S(2)}, u32[]{:S(2)}) %collective-permute-start) | collective-permute-done | bytes 1179680 | tf_op jit(solution)/shard_map/ppermute | solution.py:480
  20.0 3.5 %collective-permute-start.3 = (bf16[128,4608]{1,0:T(8,128)(2,1)S(1)}, bf16[128,4608]{1,0:T(8,128)(2,1)S(1)}, u32[]{:S(2)}, u32[]{:S(2)}) collective-permute-start(bf16[128,4608]{1,0:T(8,128)(2,1)S(1)} %collective-permute-done.refs_0_.refs_1_.refs_9_), channel_id=1, source_target_pairs={{4,8},{8,12},{5,1},{9,5},{6,10},{10,14},{7,3},{11,7},{20,24},{24,2... | collective-permute-start | bytes 3538952 | tf_op jit(solution)/shard_map/ppermute | solution.py:480
  23.5 1.6 %collective-permute-start.2 = (s32[328,512]{1,0:T(8,128)S(1)}, s32[328,512]{1,0:T(8,128)S(1)}, u32[]{:S(2)}, u32[]{:S(2)}) collective-permute-start(s32[328,512]{1,0:T(8,128)S(1)} %get-tuple-element.24), channel_id=1, source_target_pairs={{0,2},{2,0},{1,3},{3,1},{4,6},{6,4},{5,7},{7,5},{8,10},{10,8},{9,1... | collective-permute-start | bytes 2015240 | tf_op jit(solution)/shard_map/ppermute | solution.py:475
  25.0 0.0 collective-permute-start.6
  25.0 0.0 copy-done.1
  25.0 0.0 copy-done.2
  25.0 9.2 %shard_map.68 = (f32[1024,512]{1,0:T(8,128)S(1)}, f32[1,128,128]{2,1,0:T(8,128)S(1)}, bf16[3,2,128,4096]{3,2,1,0:T(8,128)(2,1)S(1)}) custom-call(s32[32]{0:T(128)S(1)} %copy-done.2, s32[3]{0:T(128)S(1)} %copy-done.1, bf16[1024,4096]{1,0:T(8,128)(2,1)} %x_ref.5, bf16[4096,1024]{1,0:T(8,128)(2,1)} %w_ref.5, bf16[128,4608]{1,0:T(8,128)(2,1)S(1)} %shard_map.65.message.refs_8_), custom_call_target="tpu_custom_call" | custom-call | flops 4294967296 | bytes 14680064 | tf_op jit(solution)/shard_map/pallas_call | solution.py:297
  34.2 3.9 %collective-permute-done.2.refs_2_ = s32[328,512]{1,0:T(8,128)S(1)} collective-permute-done((s32[328,512]{1,0:T(8,128)S(1)}, s32[328,512]{1,0:T(8,128)S(1)}, u32[]{:S(2)}, u32[]{:S(2)}) %collective-permute-start.2) | collective-permute-done | bytes 671776 | tf_op jit(solution)/shard_map/ppermute | solution.py:475
  38.2 0.0 collective-permute-done.3.refs_3_.refs_11_.refs_0_
  38.2 0.0 collective-permute-start.7
  38.2 3.4 %collective-permute-start.9 = (bf16[128,4608]{1,0:T(8,128)(2,1)S(1)}, bf16[128,4608]{1,0:T(8,128)(2,1)S(1)}, u32[]{:S(2)}, u32[]{:S(2)}) collective-permute-start(bf16[128,4608]{1,0:T(8,128)(2,1)S(1)} %collective-permute-done.3.refs_3_.refs_11_.refs_0_), channel_id=1, source_target_pairs={{8,12},{5,1},{10,14},{7,3},{24,28},{21,17},{26,30},{23,19}} | collective-permute-start | bytes 3538952 | tf_op jit(solution)/shard_map/ppermute | solution.py:480
  41.6 1.6 %collective-permute-start.4 = (s32[168,512]{1,0:T(8,128)S(1)}, s32[168,512]{1,0:T(8,128)S(1)}, u32[]{:S(2)}, u32[]{:S(2)}) collective-permute-start(s32[168,512]{1,0:T(8,128)S(1)} %get-tuple-element.27), channel_id=1, source_target_pairs={{0,2},{2,0},{1,3},{3,1},{4,6},{6,4},{5,7},{7,5},{8,10},{10,8},{9,1... | collective-permute-start | bytes 1032200 | tf_op jit(solution)/shard_map/ppermute | solution.py:475
  43.2 0.0 collective-permute-done.6.refs_1_.refs_2_.refs_10_
  43.2 1.3 %shard_map.69.refs_0_ = f32[1,128,128]{2,1,0:T(8,128)S(1)} custom-call(s32[32]{0:T(128)S(1)} %copy-done.2, s32[3]{0:T(128)S(1)} %copy-done.1, bf16[3,2,128,4096]{3,2,1,0:T(8,128)(2,1)S(1)} %get-tuple-element.29.kept_ref, bf16[128,4608]{1,0:T(8,128)(2,1)S(1)} %collective-permute-done.refs_0_.refs_1_.refs_9_, ...), custom_call_target="tpu_custom_call" | custom-call | flops 536870912 | bytes 2097152 | tf_op jit(solution)/shard_map/pallas_call | solution.py:327
  44.5 0.0 collective-permute-done.7.refs_4_.refs_12_.refs_1_
  44.5 1.5 %shard_map.70.refs_6_ = f32[2,128,128]{2,1,0:T(8,128)S(1)} custom-call(s32[32]{0:T(128)S(1)} %copy-done.2, s32[3]{0:T(128)S(1)} %copy-done.1, bf16[3,2,128,4096]{3,2,1,0:T(8,128)(2,1)S(1)} %get-tuple-element.29.kept_ref, f32[1,128,128]{2,1,0:T(8,128)S(1)} %shard_map.69.refs_0_, bf16[128,4608]{1,0:T(8,128)(2,1)S(1)} %collective-permute-done.refs_0_.refs_1_.refs_9_, ...), custom_call_target="tpu_custom_call" | custom-call | flops 536870912 | bytes 2097152 | tf_op jit(solution)/shard_map/pallas_call | solution.py:327
  46.0 0.6 collective-permute-start.8
  46.6 1.5 %collective-permute-start.5 = (f32[1,128,128]{2,1,0:T(8,128)S(1)}, f32[1,128,128]{2,1,0:T(8,128)S(1)}, u32[]{:S(2)}, u32[]{:S(2)}) collective-permute-start(f32[1,128,128]{2,1,0:T(8,128)S(1)} %get-tuple-element.25.refs_4_), channel_id=1, source_target_pairs={{0,2},{2,0},{1,3},{3,1},{4,6},{6,4},{5,7},{7,5},{8,10},{10,8},{9,1... | collective-permute-start | bytes 196616 | tf_op jit(solution)/shard_map/ppermute | solution.py:475
  48.1 5.5 %collective-permute-done.5.refs_5_ = f32[1,128,128]{2,1,0:T(8,128)S(1)} collective-permute-done((f32[1,128,128]{2,1,0:T(8,128)S(1)}, f32[1,128,128]{2,1,0:T(8,128)S(1)}, u32[]{:S(2)}, u32[]{:S(2)}) %collective-permute-start.5) | collective-permute-done | bytes 65568 | tf_op jit(solution)/shard_map/ppermute | solution.py:475
  53.7 0.0 collective-permute-done.4.refs_3_
  53.7 0.0 collective-permute-done.8.refs_7_
  53.7 3.4 %shard_map.71 = (bf16[1024,512]{1,0:T(8,128)(2,1)}, f32[2,128,512]{2,1,0:T(8,128)S(1)}) custom-call(s32[32]{0:T(128)S(1)} %copy-done.2, s32[3]{0:T(128)S(1)} %copy-done.1, f32[1024,512]{1,0:T(8,128)S(1)} %get-tuple-element.23.refs_0_, s32[168,512]{1,0:T(8,128)S(1)} %collective-permute-done.1.refs_1_, s32[328,512]{1,0:T(8,128)S(1)} %collective-permute-done.2.refs_2_, ...), custom_call_target="tpu_custom_call" | custom-call | flops 201326592 | bytes 5242880 | tf_op jit(solution)/shard_map/pallas_call | solution.py:401
  57.1 0.0 collective-permute-done.9.refs_2_.refs_5_
  57.1 0.0 collective-permute-start.10
  57.1 2.8 %collective-permute-done.10.refs_3_.refs_6_ = bf16[128,4608]{1,0:T(8,128)(2,1)S(1)} collective-permute-done((bf16[128,4608]{1,0:T(8,128)(2,1)S(1)}, bf16[128,4608]{1,0:T(8,128)(2,1)S(1)}, u32[]{:S(2)}, u32[]{:S(2)}) %collective-permute-start.10) | collective-permute-done | bytes 1179680 | tf_op jit(solution)/shard_map/ppermute | solution.py:483
  59.9 1.3 %shard_map.72.refs_1_ = f32[1,128,128]{2,1,0:T(8,128)S(1)} custom-call(s32[32]{0:T(128)S(1)} %copy-done.2, s32[3]{0:T(128)S(1)} %copy-done.1, bf16[3,2,128,4096]{3,2,1,0:T(8,128)(2,1)S(1)} %get-tuple-element.29.kept_ref, bf16[128,4608]{1,0:T(8,128)(2,1)S(1)} %collective-permute-done.3.refs_3_.refs_11_.refs_0_, ...), custom_call_target="tpu_custom_call" | custom-call | flops 536870912 | bytes 2097152 | tf_op jit(solution)/shard_map/pallas_call | solution.py:327
  61.2 1.6 %collective-permute-start.11 = (f32[1,128,128]{2,1,0:T(8,128)S(1)}, f32[1,128,128]{2,1,0:T(8,128)S(1)}, u32[]{:S(2)}, u32[]{:S(2)}) collective-permute-start(f32[1,128,128]{2,1,0:T(8,128)S(1)} %shard_map.72.refs_1_), channel_id=1, source_target_pairs={{0,2},{2,0},{1,3},{3,1},{4,6},{6,4},{5,7},{7,5},{8,10},{10,8},{9,1... | collective-permute-start | bytes 196616 | tf_op jit(solution)/shard_map/ppermute | solution.py:475
  62.8 2.8 %collective-permute-done.11.refs_2_ = f32[1,128,128]{2,1,0:T(8,128)S(1)} collective-permute-done((f32[1,128,128]{2,1,0:T(8,128)S(1)}, f32[1,128,128]{2,1,0:T(8,128)S(1)}, u32[]{:S(2)}, u32[]{:S(2)}) %collective-permute-start.11) | collective-permute-done | bytes 65568 | tf_op jit(solution)/shard_map/ppermute | solution.py:475
  65.6 1.7 %shard_map.73 = bf16[1024,512]{1,0:T(8,128)(2,1)} custom-call(s32[32]{0:T(128)S(1)} %copy-done.2, s32[3]{0:T(128)S(1)} %copy-done.1, f32[2,128,512]{2,1,0:T(8,128)S(1)} %get-tuple-element.30.refs_0_, f32[1,128,128]{2,1,0:T(8,128)S(1)} %shard_map.72.refs_1_, f32[1,128,128]{2,1,0:T(8,128)S(1)} %collective-permute-done.11.refs_2_, ...), custom_call_target="tpu_custom_call", output_to_operand_aliasing={{}: (9, {})} | custom-call | flops 50331648 | bytes 1048576 | tf_op jit(solution)/shard_map/pallas_call | solution.py:440
Async XLA Ops:
  0.1 1.8 %copy-start = (s32[3]{0:T(128)}, s32[3]{0:T(128)S(1)}, u32[]{:S(2)}) copy-start(s32[3]{0:T(128)S(1)} %pad_add_fusion.here) | copy-start | bytes 40
  1.9 18.1 %collective-permute-start = (bf16[128,4608]{1,0:T(8,128)(2,1)S(1)}, bf16[128,4608]{1,0:T(8,128)(2,1)S(1)}, u32[]{:S(2)}, u32[]{:S(2)}) collective-permute-start(bf16[128,4608]{1,0:T(8,128)(2,1)S(1)} %shard_map.65.message.refs_8_), channel_id=1, source_target_pairs={{0,4},{4,8},{8,12},{5,1},{9,5},{13,9},{2,6},{6,10},{10,14},{7,3},{... | collective-permute-start | bytes 3538952 | tf_op jit(solution)/shard_map/ppermute | solution.py:480
  9.0 9.7 %collective-permute-start.1 = (s32[168,512]{1,0:T(8,128)S(1)}, s32[168,512]{1,0:T(8,128)S(1)}, u32[]{:S(2)}, u32[]{:S(2)}) collective-permute-start(s32[168,512]{1,0:T(8,128)S(1)} %shard_map.66), channel_id=1, source_target_pairs={{0,2},{2,0},{1,3},{3,1},{4,6},{6,4},{5,7},{7,5},{8,10},{10,8},{9,1... | collective-permute-start | bytes 1032200 | tf_op jit(solution)/shard_map/ppermute | solution.py:475
  12.0 13.0 %copy-start.1 = (s32[3]{0:T(128)S(1)}, s32[3]{0:T(128)}, u32[]{:S(2)}) copy-start(s32[3]{0:T(128)} %copy-done) | copy-start | bytes 40
  12.0 13.0 %copy-start.2 = (s32[32]{0:T(128)S(1)}, s32[32]{0:T(128)}, u32[]{:S(2)}) copy-start(s32[32]{0:T(128)} %shard_map.64.table) | copy-start | bytes 388
  20.0 18.2 %collective-permute-start.3 = (bf16[128,4608]{1,0:T(8,128)(2,1)S(1)}, bf16[128,4608]{1,0:T(8,128)(2,1)S(1)}, u32[]{:S(2)}, u32[]{:S(2)}) collective-permute-start(bf16[128,4608]{1,0:T(8,128)(2,1)S(1)} %collective-permute-done.refs_0_.refs_1_.refs_9_), channel_id=1, source_target_pairs={{4,8},{8,12},{5,1},{9,5},{6,10},{10,14},{7,3},{11,7},{20,24},{24,2... | collective-permute-start | bytes 3538952 | tf_op jit(solution)/shard_map/ppermute | solution.py:480
  23.5 14.7 %collective-permute-start.2 = (s32[328,512]{1,0:T(8,128)S(1)}, s32[328,512]{1,0:T(8,128)S(1)}, u32[]{:S(2)}, u32[]{:S(2)}) collective-permute-start(s32[328,512]{1,0:T(8,128)S(1)} %get-tuple-element.24), channel_id=1, source_target_pairs={{0,2},{2,0},{1,3},{3,1},{4,6},{6,4},{5,7},{7,5},{8,10},{10,8},{9,1... | collective-permute-start | bytes 2015240 | tf_op jit(solution)/shard_map/ppermute | solution.py:475
  25.0 18.2 %collective-permute-start.6 = (bf16[128,4608]{1,0:T(8,128)(2,1)S(1)}, bf16[128,4608]{1,0:T(8,128)(2,1)S(1)}, u32[]{:S(2)}, u32[]{:S(2)}) collective-permute-start(bf16[128,4608]{1,0:T(8,128)(2,1)S(1)} %collective-permute-done.refs_0_.refs_1_.refs_9_), channel_id=1, source_target_pairs={{0,1},{1,0},{2,3},{3,2},{4,5},{5,4},{6,7},{7,6},{8,9},{9,8},{10,11... | collective-permute-start | bytes 3538952 | tf_op jit(solution)/shard_map/ppermute | solution.py:483
  38.2 6.3 %collective-permute-start.7 = (bf16[128,4608]{1,0:T(8,128)(2,1)S(1)}, bf16[128,4608]{1,0:T(8,128)(2,1)S(1)}, u32[]{:S(2)}, u32[]{:S(2)}) collective-permute-start(bf16[128,4608]{1,0:T(8,128)(2,1)S(1)} %collective-permute-done.3.refs_3_.refs_11_.refs_0_), channel_id=1, source_target_pairs={{0,1},{1,0},{2,3},{3,2},{4,5},{5,4},{6,7},{7,6},{8,9},{9,8},{10,11... | collective-permute-start | bytes 3538952 | tf_op jit(solution)/shard_map/ppermute | solution.py:483
  38.2 18.9 %collective-permute-start.9 = (bf16[128,4608]{1,0:T(8,128)(2,1)S(1)}, bf16[128,4608]{1,0:T(8,128)(2,1)S(1)}, u32[]{:S(2)}, u32[]{:S(2)}) collective-permute-start(bf16[128,4608]{1,0:T(8,128)(2,1)S(1)} %collective-permute-done.3.refs_3_.refs_11_.refs_0_), channel_id=1, source_target_pairs={{8,12},{5,1},{10,14},{7,3},{24,28},{21,17},{26,30},{23,19}} | collective-permute-start | bytes 3538952 | tf_op jit(solution)/shard_map/ppermute | solution.py:480
  41.6 12.0 %collective-permute-start.4 = (s32[168,512]{1,0:T(8,128)S(1)}, s32[168,512]{1,0:T(8,128)S(1)}, u32[]{:S(2)}, u32[]{:S(2)}) collective-permute-start(s32[168,512]{1,0:T(8,128)S(1)} %get-tuple-element.27), channel_id=1, source_target_pairs={{0,2},{2,0},{1,3},{3,1},{4,6},{6,4},{5,7},{7,5},{8,10},{10,8},{9,1... | collective-permute-start | bytes 1032200 | tf_op jit(solution)/shard_map/ppermute | solution.py:475
  46.0 7.6 %collective-permute-start.8 = (f32[2,128,128]{2,1,0:T(8,128)S(1)}, f32[2,128,128]{2,1,0:T(8,128)S(1)}, u32[]{:S(2)}, u32[]{:S(2)}) collective-permute-start(f32[2,128,128]{2,1,0:T(8,128)S(1)} %shard_map.70.refs_6_), channel_id=1, source_target_pairs={{0,2},{2,0},{1,3},{3,1},{4,6},{6,4},{5,7},{7,5},{8,10},{10,8},{9,1... | collective-permute-start | bytes 393224 | tf_op jit(solution)/shard_map/ppermute | solution.py:475
  46.6 7.0 %collective-permute-start.5 = (f32[1,128,128]{2,1,0:T(8,128)S(1)}, f32[1,128,128]{2,1,0:T(8,128)S(1)}, u32[]{:S(2)}, u32[]{:S(2)}) collective-permute-start(f32[1,128,128]{2,1,0:T(8,128)S(1)} %get-tuple-element.25.refs_4_), channel_id=1, source_target_pairs={{0,2},{2,0},{1,3},{3,1},{4,6},{6,4},{5,7},{7,5},{8,10},{10,8},{9,1... | collective-permute-start | bytes 196616 | tf_op jit(solution)/shard_map/ppermute | solution.py:475
  57.1 2.8 %collective-permute-start.10 = (bf16[128,4608]{1,0:T(8,128)(2,1)S(1)}, bf16[128,4608]{1,0:T(8,128)(2,1)S(1)}, u32[]{:S(2)}, u32[]{:S(2)}) collective-permute-start(bf16[128,4608]{1,0:T(8,128)(2,1)S(1)} %collective-permute-done.9.refs_2_.refs_5_), channel_id=1, source_target_pairs={{0,1},{1,0},{2,3},{3,2},{4,5},{5,4},{6,7},{7,6},{8,9},{9,8},{10,11... | collective-permute-start | bytes 3538952 | tf_op jit(solution)/shard_map/ppermute | solution.py:483
  61.2 4.3 %collective-permute-start.11 = (f32[1,128,128]{2,1,0:T(8,128)S(1)}, f32[1,128,128]{2,1,0:T(8,128)S(1)}, u32[]{:S(2)}, u32[]{:S(2)}) collective-permute-start(f32[1,128,128]{2,1,0:T(8,128)S(1)} %shard_map.72.refs_1_), channel_id=1, source_target_pairs={{0,2},{2,0},{1,3},{3,1},{4,6},{6,4},{5,7},{7,5},{8,10},{10,8},{9,1... | collective-permute-start | bytes 196616 | tf_op jit(solution)/shard_map/ppermute | solution.py:475

commit v7 on v6

--- a/solution.py
+++ b/solution.py
@@ -60,12 +60,20 @@
     width = down_ref.shape[1]
     columns = o_ref.shape[1] - width
     start = pl.multiple_of(here[2] * columns, columns)
+    rows = down_ref.shape[0] // PIECES
     copies = [
-        pltpu.make_async_copy(down_ref, o_ref.at[:, pl.ds(0, width)], sems.at[0]),
         pltpu.make_async_copy(
-            up_ref.at[:, pl.ds(start, columns)], o_ref.at[:, pl.ds(width, columns)], sems.at[1]
-        ),
+            down_ref.at[pl.ds(p * rows, rows), :],
+            o_ref.at[pl.ds(p * rows, rows), pl.ds(0, width)],
+            sems.at[p],
+        )
+        for p in range(PIECES)
     ]
+    copies.append(
+        pltpu.make_async_copy(
+            up_ref.at[:, pl.ds(start, columns)], o_ref.at[:, pl.ds(width, columns)], sems.at[PIECES]
+        )
+    )
     for copy in copies:
         copy.start()
     for copy in copies:
@@ -79,7 +87,7 @@
         in_specs=[SMEM, HBM, HBM],
         out_specs=VMEM,
         out_shape=jax.ShapeDtypeStruct((rows, width + columns), jnp.bfloat16),
-        scratch_shapes=[pltpu.SemaphoreType.DMA((2,))],
+        scratch_shapes=[pltpu.SemaphoreType.DMA((PIECES + 1,))],
         compiler_params=params(8),
         cost_estimate=cost(0, 4 * rows * (width + columns)),
     )(here, down, up)
@@ -158,6 +166,16 @@
     row = ref[units * WORDS + unit : units * WORDS + unit + 1, :SEGMENT_ROWS].astype(jnp.float32)
     power = jnp.sum(jnp.where(diagonal(), row, 0.0), axis=1, keepdims=True)
     return jnp.concatenate(v, axis=0).astype(jnp.float32) * jnp.exp2(power - 18.0)
+
+
+def add_decoded(sums, chunk, refs):
+    first, number = CHUNKS[chunk]
+    for unit in range(number):
+        rows = pl.ds((first + unit) * SEGMENT_ROWS, SEGMENT_ROWS)
+        value = sums[rows, :]
+        for ref in refs:
+            value = value + decode(ref, unit, number)
+        sums[rows, :] = value
 
 
 def load_base(first, segments, column, x_ref, w_ref, x, w, sems):
@@ -247,6 +265,23 @@
     )(column.reshape(1), tokens, weight)
 
 
+def add_kernel(chunk, base_ref, *refs):
+    coded_refs, o_ref = refs[:-1], refs[-1]
+    o_ref[...] = base_ref[...]
+    add_decoded(o_ref, chunk, coded_refs)
+
+
+def add_call(chunk, base, coded):
+    return pl.pallas_call(
+        functools.partial(add_kernel, chunk),
+        in_specs=[VMEM] * (1 + len(coded)),
+        out_specs=VMEM,
+        out_shape=jax.ShapeDtypeStruct(base.shape, base.dtype),
+        compiler_params=params(8),
+        cost_estimate=cost(0, 4 * base.size),
+    )(base, *coded)
+
+
 def shrink_into(o_ref, i, table, k, rows_of, buffers, owners, rank):
     for buffer, whose in zip(buffers, owners):
 
@@ -267,11 +302,12 @@
 
 
 def own_kernel(n_adapter, rank, table, here, x_ref, w_ref, message, *refs):
-    o_ref, s_ref, kept_ref, x, w, sems, kept_sems = refs
+    coded_refs, (o_ref, s_ref, kept_ref, x, w, sems, kept_sems) = refs[:-7], refs[-7:]
     work = load_base(0, x.shape[0] // SEGMENT_ROWS, here[2], x_ref, w_ref, x, w, sems)
     keeps = []
     for at, size, terms in work:
         o_ref[at : at + size, :] = block_product(x, w, at, size, terms)
+    add_decoded(o_ref, 0, coded_refs)
     for k in range(1, n_adapter):
         for j in range(MOST):
             start, _, _ = segment_of(table, k, j)
@@ -291,12 +327,12 @@
         copy.wait()
 
 
-def own_call(table, here, tokens, weight, message, columns, n_adapter, rank):
+def own_call(table, here, tokens, weight, message, coded, columns, n_adapter, rank):
     rows, width = tokens.shape
     segments = rows // SEGMENT_ROWS
     return pl.pallas_call(
         functools.partial(own_kernel, n_adapter, rank),
-        in_specs=[SMEM, SMEM, HBM, HBM, VMEM],
+        in_specs=[SMEM, SMEM, HBM, HBM] + [VMEM] * (1 + len(coded)),
         out_specs=[VMEM] * 3,
         out_shape=[
             jax.ShapeDtypeStruct((rows, columns), jnp.float32),
@@ -309,7 +345,7 @@
         cost_estimate=cost(
             2 * rows * width * columns, 2 * rows * width + 2 * width * columns + 4 * rows * columns
         ),
-    )(table, here, tokens, weight, message)
+    )(table, here, tokens, weight, message, *coded)
 
 
 def shrink_kernel(k, rank, n_before, table, here, kept_ref, *refs):
@@ -357,7 +393,7 @@
 
 
 def early_kernel(n_adapter, n_tensor, rank, table, here, *refs):
-    n_coded, n_buffers = len(CHUNKS) * (n_tensor - 1), 2 * n_adapter - 3
+    n_coded, n_buffers = n_tensor - 1, 2 * n_adapter - 3
     base_ref, coded_refs, refs = refs[0], refs[1 : 1 + n_coded], refs[1 + n_coded :]
     shrinks, refs = refs[: -4 - n_buffers], refs[-4 - n_buffers :]
     buffers, (o_ref, rest_ref, up, total) = refs[:-4], refs[-4:]
@@ -373,13 +409,8 @@
         for i in range(1, n_tensor):
             share = share + shrinks[call * n_tensor + i][...]
         shares += [share[i] for i in range(share.shape[0])]
-    for chunk, (first, number) in enumerate(CHUNKS):
-        for unit in range(number):
-            here_rows = pl.ds((first + unit) * SEGMENT_ROWS, SEGMENT_ROWS)
-            value = base_ref[here_rows, :]
-            for i in range(n_tensor - 1):
-                value = value + decode(coded_refs[chunk * (n_tensor - 1) + i], unit, number)
-            total[here_rows, :] = value
+    total[...] = base_ref[...]
+    add_decoded(total, len(CHUNKS) - 1, coded_refs)
     for k in range(n_adapter):
         for j in range(MOST):
             start, used, _ = segment_of(table, k, j)
@@ -520,11 +551,13 @@
             sent.append([swap_tensor(after(p, came), step) for step, p in zip(others, parts[stage])])
         if stage == 1:
             base, before, kept = own_call(
-                after(table, came), here, tokens, value_weight, message, columns, n_adapter, rank
+                after(table, came), here, tokens, value_weight, message, sent[0], columns, n_adapter, rank
             )
             add_shrink(before)
-            done = sent[1] + [before]
+            done = sent[1] + shrinks
         else:
+            if stage == 2:
+                base = add_call(1, after(base, came), sent[1])
             before = shrink_call(
                 stage - 1, table, here, after(kept, came), [], buffers_of(stages_of(stage - 1)), rank
             )
@@ -542,7 +575,7 @@
         table,
         here,
         base,
-        [c for group in sent for c in group],
+        sent[2],
         shrinks,
         buffers_of(range(last)),
         rank,

time: 68.2 us -> 67.9 us (level)
  starting transfers between devices: 18.8 us -> 16.5 us
  waiting for transfers between devices: 16.5 us -> 18.4 us
    ppermute x6, waiting for transfers between devices: 12.2 us -> 14.2 us  [swap_tensor(): return lax.ppermute(array, 'tensor', pairs)]
    ppermute x3, starting transfers between devices: 10.4 us -> 8.99 us  [along_line(): return lax.ppermute(array, ('adapter', 'dp'), up + down)]
    ppermute x6, starting transfers between devices: 8.37 us -> 7.48 us  [swap_tensor(): return lax.ppermute(array, 'tensor', pairs)]
  transfers between devices with their start and end apart: 12 -> 12, of which waited for: 5 -> 6; matrix products, arithmetic and copies ran while one was open for 0% -> 0% of each run, Pallas kernels for 40% -> 40%
where the time goes in v7:
time: 67.9 us; the launch traced here: 67.2 us
  Pallas kernels  31.8 us (47%)
  waiting for transfers between devices  18.4 us (27%)
  starting transfers between devices  16.5 us (24%)
    ppermute x6, waiting for transfers between devices, swap_tensor(): return lax.ppermute(array, 'tensor', pairs)  14.2 us
    pallas_call x2, Pallas kernels, sent_call(): pl.pallas_call(functools.partial(sent_kernel, first, sizes), in_specs=[SM...  10.1 us
    pallas_call x1, Pallas kernels, own_call(): pl.pallas_call(functools.partial(own_kernel, n_adapter, rank), in_specs=[...  9.2 us
    ppermute x3, starting transfers between devices, along_line(): return lax.ppermute(array, ('adapter', 'dp'), up + down)  8.99 us
    ppermute x6, starting transfers between devices, swap_tensor(): return lax.ppermute(array, 'tensor', pairs)  7.48 us
    pallas_call x3, Pallas kernels, shrink_call(): pl.pallas_call(functools.partial(shrink_kernel, k, rank, len(before)), in...  4.14 us
    pallas_call x1, Pallas kernels, early(): pl.pallas_call(functools.partial(early_kernel, n_adapter, n_tensor, rank)...  3.12 us
    ppermute x3, waiting for transfers between devices, swap_cores(): return lax.ppermute(array, 'dp', [(0, 1), (1, 0)])  2.85 us
  transfers between devices with their start and end apart: 12, of which 6 were waited for; matrix products, arithmetic and copies ran while one was open for 0% of the time, Pallas kernels for 40%

profile of v7, /device:TPU:16, one launch (start us, length us, event | category | flops | bytes accessed | tf_op | source)
XLA Modules:
  0.0 67.2 jit_solution(14843033213007865638)
XLA Ops:
  0.0 0.1 pad_add_fusion.here
  0.1 0.0 copy-start
  0.1 1.8 %shard_map.65.message.refs_6_ = bf16[128,4608]{1,0:T(8,128)(2,1)S(1)} custom-call(s32[3]{0:T(128)S(1)} %pad_add_fusion.here, bf16[128,4096]{1,0:T(8,128)(2,1)} %bitcast.8, bf16[128,1024]{1,0:T(8,128)(2,1)} %bitcast.9), custom_call_target="tpu_custom_call" | custom-call | bytes 2359296 | tf_op jit(solution)/shard_map/pallas_call | solution.py:85
  1.9 0.0 copy-done
  1.9 3.5 %collective-permute-start = (bf16[128,4608]{1,0:T(8,128)(2,1)S(1)}, bf16[128,4608]{1,0:T(8,128)(2,1)S(1)}, u32[]{:S(2)}, u32[]{:S(2)}) collective-permute-start(bf16[128,4608]{1,0:T(8,128)(2,1)S(1)} %shard_map.65.message.refs_6_), channel_id=1, source_target_pairs={{0,4},{4,8},{8,12},{5,1},{9,5},{13,9},{2,6},{6,10},{10,14},{7,3},{... | collective-permute-start | bytes 3538952 | tf_op jit(solution)/shard_map/ppermute | solution.py:511
  5.4 3.6 %shard_map.66 = s32[168,512]{1,0:T(8,128)S(1)} custom-call(s32[1]{0:T(128)} %bitcast.6.column, bf16[1024,4096]{1,0:T(8,128)(2,1)} %x_ref.5, bf16[4096,1024]{1,0:T(8,128)(2,1)} %w_ref.5), custom_call_target="tpu_custom_call" | custom-call | flops 1073741824 | bytes 6815744 | tf_op jit(solution)/shard_map/pallas_call | solution.py:255
  9.0 1.6 %collective-permute-start.1 = (s32[168,512]{1,0:T(8,128)S(1)}, s32[168,512]{1,0:T(8,128)S(1)}, u32[]{:S(2)}, u32[]{:S(2)}) collective-permute-start(s32[168,512]{1,0:T(8,128)S(1)} %shard_map.66), channel_id=1, source_target_pairs={{0,2},{2,0},{1,3},{3,1},{4,6},{6,4},{5,7},{7,5},{8,10},{10,8},{9,1... | collective-permute-start | bytes 1032200 | tf_op jit(solution)/shard_map/ppermute | solution.py:506
  10.6 1.4 %shard_map.64.table = s32[32]{0:T(128)} custom-call(s32[3]{0:T(128)} %copy-done, s32[1024]{0:T(1024)} %ids.1, s32[8]{0:T(128)} %slots.1), custom_call_target="tpu_custom_call" | custom-call | bytes 4096 | tf_op jit(solution)/shard_map/pallas_call | solution.py:117
  12.0 0.0 copy-start.1
  12.0 0.0 copy-start.2
  12.0 6.6 %shard_map.67 = (s32[328,512]{1,0:T(8,128)S(1)}, s32[168,512]{1,0:T(8,128)S(1)}) custom-call(s32[1]{0:T(128)} %bitcast.6.column, bf16[1024,4096]{1,0:T(8,128)(2,1)} %x_ref.5, bf16[4096,1024]{1,0:T(8,128)(2,1)} %w_ref.5), custom_call_target="tpu_custom_call" | custom-call | flops 3221225472 | bytes 12058624 | tf_op jit(solution)/shard_map/pallas_call | solution.py:255
  18.6 0.0 collective-permute-done.1.refs_0_
  18.6 1.4 %collective-permute-done.refs_0_.refs_1_.refs_7_ = bf16[128,4608]{1,0:T(8,128)(2,1)S(1)} collective-permute-done((bf16[128,4608]{1,0:T(8,128)(2,1)S(1)}, bf16[128,4608]{1,0:T(8,128)(2,1)S(1)}, u32[]{:S(2)}, u32[]{:S(2)}) %collective-permute-start) | collective-permute-done | bytes 1179680 | tf_op jit(solution)/shard_map/ppermute | solution.py:511
  20.0 3.5 %collective-permute-start.2 = (bf16[128,4608]{1,0:T(8,128)(2,1)S(1)}, bf16[128,4608]{1,0:T(8,128)(2,1)S(1)}, u32[]{:S(2)}, u32[]{:S(2)}) collective-permute-start(bf16[128,4608]{1,0:T(8,128)(2,1)S(1)} %collective-permute-done.refs_0_.refs_1_.refs_7_), channel_id=1, source_target_pairs={{4,8},{8,12},{5,1},{9,5},{6,10},{10,14},{7,3},{11,7},{20,24},{24,2... | collective-permute-start | bytes 3538952 | tf_op jit(solution)/shard_map/ppermute | solution.py:511
  23.5 1.6 %collective-permute-start.3 = (s32[328,512]{1,0:T(8,128)S(1)}, s32[328,512]{1,0:T(8,128)S(1)}, u32[]{:S(2)}, u32[]{:S(2)}) collective-permute-start(s32[328,512]{1,0:T(8,128)S(1)} %get-tuple-element.25), channel_id=1, source_target_pairs={{0,2},{2,0},{1,3},{3,1},{4,6},{6,4},{5,7},{7,5},{8,10},{10,8},{9,1... | collective-permute-start | bytes 2015240 | tf_op jit(solution)/shard_map/ppermute | solution.py:506
  25.0 0.0 copy-done.1
  25.0 0.0 copy-done.2
  25.0 9.2 %shard_map.68 = (f32[1024,512]{1,0:T(8,128)S(1)}, f32[1,128,128]{2,1,0:T(8,128)S(1)}, bf16[3,2,128,4096]{3,2,1,0:T(8,128)(2,1)S(1)}) custom-call(s32[32]{0:T(128)S(1)} %copy-done.2, s32[3]{0:T(128)S(1)} %copy-done.1, bf16[1024,4096]{1,0:T(8,128)(2,1)} %x_ref.5, bf16[4096,1024]{1,0:T(8,128)(2,1)} %w_ref.5, bf16[128,4608]{1,0:T(8,128)(2,1)S(1)} %shard_map.65.message.refs_6_, ...), custom_call_target="tpu_custom_call" | custom-call | flops 4294967296 | bytes 14680064 | tf_op jit(solution)/shard_map/pallas_call | solution.py:333
  34.2 0.6 collective-permute-start.4
  34.8 0.0 collective-permute-start.6
  34.8 4.7 %collective-permute-done.4.refs_3_ = f32[1,128,128]{2,1,0:T(8,128)S(1)} collective-permute-done((f32[1,128,128]{2,1,0:T(8,128)S(1)}, f32[1,128,128]{2,1,0:T(8,128)S(1)}, u32[]{:S(2)}, u32[]{:S(2)}) %collective-permute-start.4) | collective-permute-done | bytes 65568 | tf_op jit(solution)/shard_map/ppermute | solution.py:506
  39.6 0.0 collective-permute-done.3.refs_0_
  39.6 0.0 collective-permute-done.2.refs_3_.refs_9_.refs_0_
  39.6 0.0 collective-permute-start.7
  39.6 2.0 %collective-permute-start.9 = (bf16[128,4608]{1,0:T(8,128)(2,1)S(1)}, bf16[128,4608]{1,0:T(8,128)(2,1)S(1)}, u32[]{:S(2)}, u32[]{:S(2)}) collective-permute-start(bf16[128,4608]{1,0:T(8,128)(2,1)S(1)} %collective-permute-done.2.refs_3_.refs_9_.refs_0_), channel_id=1, source_target_pairs={{8,12},{5,1},{10,14},{7,3},{24,28},{21,17},{26,30},{23,19}} | collective-permute-start | bytes 3538952 | tf_op jit(solution)/shard_map/ppermute | solution.py:511
  41.6 1.6 %collective-permute-start.5 = (s32[168,512]{1,0:T(8,128)S(1)}, s32[168,512]{1,0:T(8,128)S(1)}, u32[]{:S(2)}, u32[]{:S(2)}) collective-permute-start(s32[168,512]{1,0:T(8,128)S(1)} %get-tuple-element.29), channel_id=1, source_target_pairs={{0,2},{2,0},{1,3},{3,1},{4,6},{6,4},{5,7},{7,5},{8,10},{10,8},{9,1... | collective-permute-start | bytes 1032200 | tf_op jit(solution)/shard_map/ppermute | solution.py:506
  43.2 0.0 collective-permute-done.6.refs_1_.refs_2_.refs_8_
  43.2 1.3 %shard_map.70.refs_0_ = f32[1,128,128]{2,1,0:T(8,128)S(1)} custom-call(s32[32]{0:T(128)S(1)} %copy-done.2, s32[3]{0:T(128)S(1)} %copy-done.1, bf16[3,2,128,4096]{3,2,1,0:T(8,128)(2,1)S(1)} %get-tuple-element.31.kept_ref, bf16[128,4608]{1,0:T(8,128)(2,1)S(1)} %collective-permute-done.refs_0_.refs_1_.refs_7_, ...), custom_call_target="tpu_custom_call" | custom-call | flops 536870912 | bytes 2097152 | tf_op jit(solution)/shard_map/pallas_call | solution.py:363
  44.5 0.0 collective-permute-done.7.refs_4_.refs_10_.refs_1_
  44.5 1.5 %shard_map.71.refs_4_ = f32[2,128,128]{2,1,0:T(8,128)S(1)} custom-call(s32[32]{0:T(128)S(1)} %copy-done.2, s32[3]{0:T(128)S(1)} %copy-done.1, bf16[3,2,128,4096]{3,2,1,0:T(8,128)(2,1)S(1)} %get-tuple-element.31.kept_ref, f32[1,128,128]{2,1,0:T(8,128)S(1)} %shard_map.70.refs_0_, bf16[128,4608]{1,0:T(8,128)(2,1)S(1)} %collective-permute-done.refs_0_.refs_1_.refs_7_, ...), custom_call_target="tpu_custom_call" | custom-call | flops 536870912 | bytes 2097152 | tf_op jit(solution)/shard_map/pallas_call | solution.py:363
  46.0 0.6 collective-permute-start.8
  46.6 0.3 shard_map.69.refs_0_
  47.0 5.3 %collective-permute-done.5.refs_1_ = s32[168,512]{1,0:T(8,128)S(1)} collective-permute-done((s32[168,512]{1,0:T(8,128)S(1)}, s32[168,512]{1,0:T(8,128)S(1)}, u32[]{:S(2)}, u32[]{:S(2)}) %collective-permute-start.5) | collective-permute-done | bytes 344096 | tf_op jit(solution)/shard_map/ppermute | solution.py:506
  52.3 1.4 %collective-permute-done.8.refs_5_ = f32[2,128,128]{2,1,0:T(8,128)S(1)} collective-permute-done((f32[2,128,128]{2,1,0:T(8,128)S(1)}, f32[2,128,128]{2,1,0:T(8,128)S(1)}, u32[]{:S(2)}, u32[]{:S(2)}) %collective-permute-start.8) | collective-permute-done | bytes 131104 | tf_op jit(solution)/shard_map/ppermute | solution.py:506
  53.7 3.1 %shard_map.72 = (bf16[1024,512]{1,0:T(8,128)(2,1)}, f32[2,128,512]{2,1,0:T(8,128)S(1)}) custom-call(s32[32]{0:T(128)S(1)} %copy-done.2, s32[3]{0:T(128)S(1)} %copy-done.1, f32[1024,512]{1,0:T(8,128)S(1)} %shard_map.69.refs_0_, s32[168,512]{1,0:T(8,128)S(1)} %collective-permute-done.5.refs_1_, f32[1,128,128]{2,1,0:T(8,128)S(1)} %get-tuple-element.26.refs_2_, ...), custom_call_target="tpu_custom_call" | custom-call | flops 201326592 | bytes 5242880 | tf_op jit(solution)/shard_map/pallas_call | solution.py:432
  56.8 0.0 collective-permute-done.9.refs_2_.refs_5_
  56.8 0.0 collective-permute-start.10
  56.8 2.8 %collective-permute-done.10.refs_3_.refs_6_ = bf16[128,4608]{1,0:T(8,128)(2,1)S(1)} collective-permute-done((bf16[128,4608]{1,0:T(8,128)(2,1)S(1)}, bf16[128,4608]{1,0:T(8,128)(2,1)S(1)}, u32[]{:S(2)}, u32[]{:S(2)}) %collective-permute-start.10) | collective-permute-done | bytes 1179680 | tf_op jit(solution)/shard_map/ppermute | solution.py:514
  59.6 1.3 %shard_map.73.refs_1_ = f32[1,128,128]{2,1,0:T(8,128)S(1)} custom-call(s32[32]{0:T(128)S(1)} %copy-done.2, s32[3]{0:T(128)S(1)} %copy-done.1, bf16[3,2,128,4096]{3,2,1,0:T(8,128)(2,1)S(1)} %get-tuple-element.31.kept_ref, bf16[128,4608]{1,0:T(8,128)(2,1)S(1)} %collective-permute-done.2.refs_3_.refs_9_.refs_0_, ...), custom_call_target="tpu_custom_call" | custom-call | flops 536870912 | bytes 2097152 | tf_op jit(solution)/shard_map/pallas_call | solution.py:363
  61.0 1.6 %collective-permute-start.11 = (f32[1,128,128]{2,1,0:T(8,128)S(1)}, f32[1,128,128]{2,1,0:T(8,128)S(1)}, u32[]{:S(2)}, u32[]{:S(2)}) collective-permute-start(f32[1,128,128]{2,1,0:T(8,128)S(1)} %shard_map.73.refs_1_), channel_id=1, source_target_pairs={{0,2},{2,0},{1,3},{3,1},{4,6},{6,4},{5,7},{7,5},{8,10},{10,8},{9,1... | collective-permute-start | bytes 196616 | tf_op jit(solution)/shard_map/ppermute | solution.py:506
  62.5 2.8 %collective-permute-done.11.refs_2_ = f32[1,128,128]{2,1,0:T(8,128)S(1)} collective-permute-done((f32[1,128,128]{2,1,0:T(8,128)S(1)}, f32[1,128,128]{2,1,0:T(8,128)S(1)}, u32[]{:S(2)}, u32[]{:S(2)}) %collective-permute-start.11) | collective-permute-done | bytes 65568 | tf_op jit(solution)/shard_map/ppermute | solution.py:506
  65.3 1.7 %shard_map.74 = bf16[1024,512]{1,0:T(8,128)(2,1)} custom-call(s32[32]{0:T(128)S(1)} %copy-done.2, s32[3]{0:T(128)S(1)} %copy-done.1, f32[2,128,512]{2,1,0:T(8,128)S(1)} %get-tuple-element.32.refs_0_, f32[1,128,128]{2,1,0:T(8,128)S(1)} %shard_map.73.refs_1_, f32[1,128,128]{2,1,0:T(8,128)S(1)} %collective-permute-done.11.refs_2_, ...), custom_call_target="tpu_custom_call", output_to_operand_aliasing={{}: (9, {})} | custom-call | flops 50331648 | bytes 1048576 | tf_op jit(solution)/shard_map/pallas_call | solution.py:471
Async XLA Ops:
  0.1 1.8 %copy-start = (s32[3]{0:T(128)}, s32[3]{0:T(128)S(1)}, u32[]{:S(2)}) copy-start(s32[3]{0:T(128)S(1)} %pad_add_fusion.here) | copy-start | bytes 40
  1.9 18.1 %collective-permute-start = (bf16[128,4608]{1,0:T(8,128)(2,1)S(1)}, bf16[128,4608]{1,0:T(8,128)(2,1)S(1)}, u32[]{:S(2)}, u32[]{:S(2)}) collective-permute-start(bf16[128,4608]{1,0:T(8,128)(2,1)S(1)} %shard_map.65.message.refs_6_), channel_id=1, source_target_pairs={{0,4},{4,8},{8,12},{5,1},{9,5},{13,9},{2,6},{6,10},{10,14},{7,3},{... | collective-permute-start | bytes 3538952 | tf_op jit(solution)/shard_map/ppermute | solution.py:511
  9.0 9.7 %collective-permute-start.1 = (s32[168,512]{1,0:T(8,128)S(1)}, s32[168,512]{1,0:T(8,128)S(1)}, u32[]{:S(2)}, u32[]{:S(2)}) collective-permute-start(s32[168,512]{1,0:T(8,128)S(1)} %shard_map.66), channel_id=1, source_target_pairs={{0,2},{2,0},{1,3},{3,1},{4,6},{6,4},{5,7},{7,5},{8,10},{10,8},{9,1... | collective-permute-start | bytes 1032200 | tf_op jit(solution)/shard_map/ppermute | solution.py:506
  12.0 13.0 %copy-start.1 = (s32[3]{0:T(128)S(1)}, s32[3]{0:T(128)}, u32[]{:S(2)}) copy-start(s32[3]{0:T(128)} %copy-done) | copy-start | bytes 40
  12.0 13.0 %copy-start.2 = (s32[32]{0:T(128)S(1)}, s32[32]{0:T(128)}, u32[]{:S(2)}) copy-start(s32[32]{0:T(128)} %shard_map.64.table) | copy-start | bytes 388
  20.0 19.6 %collective-permute-start.2 = (bf16[128,4608]{1,0:T(8,128)(2,1)S(1)}, bf16[128,4608]{1,0:T(8,128)(2,1)S(1)}, u32[]{:S(2)}, u32[]{:S(2)}) collective-permute-start(bf16[128,4608]{1,0:T(8,128)(2,1)S(1)} %collective-permute-done.refs_0_.refs_1_.refs_7_), channel_id=1, source_target_pairs={{4,8},{8,12},{5,1},{9,5},{6,10},{10,14},{7,3},{11,7},{20,24},{24,2... | collective-permute-start | bytes 3538952 | tf_op jit(solution)/shard_map/ppermute | solution.py:511
  23.5 16.1 %collective-permute-start.3 = (s32[328,512]{1,0:T(8,128)S(1)}, s32[328,512]{1,0:T(8,128)S(1)}, u32[]{:S(2)}, u32[]{:S(2)}) collective-permute-start(s32[328,512]{1,0:T(8,128)S(1)} %get-tuple-element.25), channel_id=1, source_target_pairs={{0,2},{2,0},{1,3},{3,1},{4,6},{6,4},{5,7},{7,5},{8,10},{10,8},{9,1... | collective-permute-start | bytes 2015240 | tf_op jit(solution)/shard_map/ppermute | solution.py:506
  34.2 5.3 %collective-permute-start.4 = (f32[1,128,128]{2,1,0:T(8,128)S(1)}, f32[1,128,128]{2,1,0:T(8,128)S(1)}, u32[]{:S(2)}, u32[]{:S(2)}) collective-permute-start(f32[1,128,128]{2,1,0:T(8,128)S(1)} %get-tuple-element.26.refs_2_), channel_id=1, source_target_pairs={{0,2},{2,0},{1,3},{3,1},{4,6},{6,4},{5,7},{7,5},{8,10},{10,8},{9,1... | collective-permute-start | bytes 196616 | tf_op jit(solution)/shard_map/ppermute | solution.py:506
  34.8 8.4 %collective-permute-start.6 = (bf16[128,4608]{1,0:T(8,128)(2,1)S(1)}, bf16[128,4608]{1,0:T(8,128)(2,1)S(1)}, u32[]{:S(2)}, u32[]{:S(2)}) collective-permute-start(bf16[128,4608]{1,0:T(8,128)(2,1)S(1)} %collective-permute-done.refs_0_.refs_1_.refs_7_), channel_id=1, source_target_pairs={{0,1},{1,0},{2,3},{3,2},{4,5},{5,4},{6,7},{7,6},{8,9},{9,8},{10,11... | collective-permute-start | bytes 3538952 | tf_op jit(solution)/shard_map/ppermute | solution.py:514
  39.6 4.9 %collective-permute-start.7 = (bf16[128,4608]{1,0:T(8,128)(2,1)S(1)}, bf16[128,4608]{1,0:T(8,128)(2,1)S(1)}, u32[]{:S(2)}, u32[]{:S(2)}) collective-permute-start(bf16[128,4608]{1,0:T(8,128)(2,1)S(1)} %collective-permute-done.2.refs_3_.refs_9_.refs_0_), channel_id=1, source_target_pairs={{0,1},{1,0},{2,3},{3,2},{4,5},{5,4},{6,7},{7,6},{8,9},{9,8},{10,11... | collective-permute-start | bytes 3538952 | tf_op jit(solution)/shard_map/ppermute | solution.py:514
  39.6 17.2 %collective-permute-start.9 = (bf16[128,4608]{1,0:T(8,128)(2,1)S(1)}, bf16[128,4608]{1,0:T(8,128)(2,1)S(1)}, u32[]{:S(2)}, u32[]{:S(2)}) collective-permute-start(bf16[128,4608]{1,0:T(8,128)(2,1)S(1)} %collective-permute-done.2.refs_3_.refs_9_.refs_0_), channel_id=1, source_target_pairs={{8,12},{5,1},{10,14},{7,3},{24,28},{21,17},{26,30},{23,19}} | collective-permute-start | bytes 3538952 | tf_op jit(solution)/shard_map/ppermute | solution.py:511
  41.6 10.6 %collective-permute-start.5 = (s32[168,512]{1,0:T(8,128)S(1)}, s32[168,512]{1,0:T(8,128)S(1)}, u32[]{:S(2)}, u32[]{:S(2)}) collective-permute-start(s32[168,512]{1,0:T(8,128)S(1)} %get-tuple-element.29), channel_id=1, source_target_pairs={{0,2},{2,0},{1,3},{3,1},{4,6},{6,4},{5,7},{7,5},{8,10},{10,8},{9,1... | collective-permute-start | bytes 1032200 | tf_op jit(solution)/shard_map/ppermute | solution.py:506
  46.0 7.6 %collective-permute-start.8 = (f32[2,128,128]{2,1,0:T(8,128)S(1)}, f32[2,128,128]{2,1,0:T(8,128)S(1)}, u32[]{:S(2)}, u32[]{:S(2)}) collective-permute-start(f32[2,128,128]{2,1,0:T(8,128)S(1)} %shard_map.71.refs_4_), channel_id=1, source_target_pairs={{0,2},{2,0},{1,3},{3,1},{4,6},{6,4},{5,7},{7,5},{8,10},{10,8},{9,1... | collective-permute-start | bytes 393224 | tf_op jit(solution)/shard_map/ppermute | solution.py:506
  56.8 2.8 %collective-permute-start.10 = (bf16[128,4608]{1,0:T(8,128)(2,1)S(1)}, bf16[128,4608]{1,0:T(8,128)(2,1)S(1)}, u32[]{:S(2)}, u32[]{:S(2)}) collective-permute-start(bf16[128,4608]{1,0:T(8,128)(2,1)S(1)} %collective-permute-done.9.refs_2_.refs_5_), channel_id=1, source_target_pairs={{0,1},{1,0},{2,3},{3,2},{4,5},{5,4},{6,7},{7,6},{8,9},{9,8},{10,11... | collective-permute-start | bytes 3538952 | tf_op jit(solution)/shard_map/ppermute | solution.py:514
  61.0 4.3 %collective-permute-start.11 = (f32[1,128,128]{2,1,0:T(8,128)S(1)}, f32[1,128,128]{2,1,0:T(8,128)S(1)}, u32[]{:S(2)}, u32[]{:S(2)}) collective-permute-start(f32[1,128,128]{2,1,0:T(8,128)S(1)} %shard_map.73.refs_1_), channel_id=1, source_target_pairs={{0,2},{2,0},{1,3},{3,1},{4,6},{6,4},{5,7},{7,5},{8,10},{10,8},{9,1... | collective-permute-start | bytes 196616 | tf_op jit(solution)/shard_map/ppermute | solution.py:506

commit v8 on v7

--- a/solution.py
+++ b/solution.py
@@ -42,12 +42,13 @@
     return order
 
 
-def buffer_owners(here, stages):
-    owners = []
+def buffer_tags(here, stages, per_device):
+    tags = []
     for stage in stages:
-        toward = jnp.where(here[1] == 0, -stage, stage)
-        owners += [here[0] + toward, here[0] - toward] if stage > 0 else [here[0]]
-    return owners
+        for i in range(per_device):
+            toward = jnp.where(here[1] == i % 2, -stage, stage)
+            tags += [(here[0] + toward, i), (here[0] - toward, i)] if stage > 0 else [(here[0], i)]
+    return tags
 
 
 def segment_of(table, k, j):
@@ -56,38 +57,36 @@
     return start, seg >= 0, table[k * ENTRIES + 2 + 2 * j]
 
 
-def message_kernel(here, down_ref, up_ref, o_ref, sems):
+def message_kernel(here, down_ref, up_ref, *refs):
+    outs, sems = refs[:-1], refs[-1]
+    rank = outs[0].shape[0]
     width = down_ref.shape[1]
-    columns = o_ref.shape[1] - width
+    columns = outs[0].shape[1] - width
     start = pl.multiple_of(here[2] * columns, columns)
-    rows = down_ref.shape[0] // PIECES
-    copies = [
-        pltpu.make_async_copy(
-            down_ref.at[pl.ds(p * rows, rows), :],
-            o_ref.at[pl.ds(p * rows, rows), pl.ds(0, width)],
-            sems.at[p],
-        )
-        for p in range(PIECES)
-    ]
-    copies.append(
-        pltpu.make_async_copy(
-            up_ref.at[:, pl.ds(start, columns)], o_ref.at[:, pl.ds(width, columns)], sems.at[PIECES]
-        )
-    )
+    copies = []
+    for i, out in enumerate(outs):
+        rows = pl.ds(i * rank, rank)
+        copies += [
+            pltpu.make_async_copy(down_ref.at[rows, :], out.at[:, pl.ds(0, width)], sems.at[0, i]),
+            pltpu.make_async_copy(
+                up_ref.at[rows, pl.ds(start, columns)], out.at[:, pl.ds(width, columns)], sems.at[1, i]
+            ),
+        ]
     for copy in copies:
         copy.start()
     for copy in copies:
         copy.wait()
 
 
-def message_call(here, down, up, columns):
+def message_call(here, down, up, columns, per_device):
     rows, width = down.shape
+    shape = jax.ShapeDtypeStruct((rows // per_device, width + columns), jnp.bfloat16)
     return pl.pallas_call(
         message_kernel,
         in_specs=[SMEM, HBM, HBM],
-        out_specs=VMEM,
-        out_shape=jax.ShapeDtypeStruct((rows, width + columns), jnp.bfloat16),
-        scratch_shapes=[pltpu.SemaphoreType.DMA((PIECES + 1,))],
+        out_specs=[VMEM] * per_device,
+        out_shape=[shape] * per_device,
+        scratch_shapes=[pltpu.SemaphoreType.DMA((2, per_device))],
         compiler_params=params(8),
         cost_estimate=cost(0, 4 * rows * (width + columns)),
     )(here, down, up)
@@ -282,103 +281,85 @@
     )(base, *coded)
 
 
-def shrink_into(o_ref, i, table, k, rows_of, buffers, owners, rank):
-    for buffer, whose in zip(buffers, owners):
-
-        @pl.when(whose == table[k * ENTRIES])
-        def _(buffer=buffer):
-            for j in range(MOST):
-                _, _, within = segment_of(table, k, j)
-                rows = rows_of(j)
-                width = rows.shape[1]
-                factor = buffer[pl.ds(pl.multiple_of(within * rank, rank), rank), :width]
-                o_ref[i, :, j * rank : (j + 1) * rank] = lax.dot_general(
-                    rows, factor, (((1,), (1,)), ((), ())), preferred_element_type=jnp.float32
-                )
-
-
-def stages_of(k):
-    return range((k + 1) // 2, k + 1)
-
-
-def own_kernel(n_adapter, rank, table, here, x_ref, w_ref, message, *refs):
-    coded_refs, (o_ref, s_ref, kept_ref, x, w, sems, kept_sems) = refs[:-7], refs[-7:]
-    work = load_base(0, x.shape[0] // SEGMENT_ROWS, here[2], x_ref, w_ref, x, w, sems)
-    keeps = []
+def own_kernel(column, x_ref, w_ref, *refs):
+    coded_refs, (o_ref, x, w, sems) = refs[:-4], refs[-4:]
+    work = load_base(0, x.shape[0] // SEGMENT_ROWS, column[0], x_ref, w_ref, x, w, sems)
     for at, size, terms in work:
         o_ref[at : at + size, :] = block_product(x, w, at, size, terms)
     add_decoded(o_ref, 0, coded_refs)
-    for k in range(1, n_adapter):
-        for j in range(MOST):
-            start, _, _ = segment_of(table, k, j)
-            keeps.append(
-                pltpu.make_async_copy(
-                    x.at[pl.ds(start, SEGMENT_ROWS), :], kept_ref.at[k - 1, j], kept_sems.at[k - 1, j]
-                )
-            )
-            keeps[-1].start()
-
-    def rows_of(j):
-        start, _, _ = segment_of(table, 0, j)
-        return x[pl.ds(start, SEGMENT_ROWS), :]
-
-    shrink_into(s_ref, 0, table, 0, rows_of, [message], [here[0]], rank)
-    for copy in keeps:
-        copy.wait()
-
-
-def own_call(table, here, tokens, weight, message, coded, columns, n_adapter, rank):
+
+
+def own_call(tokens, weight, column, coded, columns):
     rows, width = tokens.shape
-    segments = rows // SEGMENT_ROWS
-    return pl.pallas_call(
-        functools.partial(own_kernel, n_adapter, rank),
-        in_specs=[SMEM, SMEM, HBM, HBM] + [VMEM] * (1 + len(coded)),
-        out_specs=[VMEM] * 3,
+    x, *scratch = base_scratch(rows // SEGMENT_ROWS, width, columns)
+    return pl.pallas_call(
+        own_kernel,
+        in_specs=[SMEM, HBM, HBM] + [VMEM] * len(coded),
+        out_specs=[VMEM, VMEM],
         out_shape=[
             jax.ShapeDtypeStruct((rows, columns), jnp.float32),
-            jax.ShapeDtypeStruct((1, SEGMENT_ROWS, MOST * rank), jnp.float32),
-            jax.ShapeDtypeStruct((n_adapter - 1, MOST, SEGMENT_ROWS, width), jnp.bfloat16),
+            jax.ShapeDtypeStruct(x.shape, x.dtype),
         ],
-        scratch_shapes=base_scratch(segments, width, columns)
-        + [pltpu.SemaphoreType.DMA((n_adapter - 1, MOST))],
-        compiler_params=params(32),
+        scratch_shapes=scratch,
+        compiler_params=params(24),
         cost_estimate=cost(
             2 * rows * width * columns, 2 * rows * width + 2 * width * columns + 4 * rows * columns
         ),
-    )(table, here, tokens, weight, message, *coded)
-
-
-def shrink_kernel(k, rank, n_before, table, here, kept_ref, *refs):
+    )(column.reshape(1), tokens, weight, *coded)
+
+
+def stages_of(k):
+    return range((k + 1) // 2, k + 1)
+
+
+def stages_of_all(ks):
+    return range(stages_of(ks[0])[0], ks[-1] + 1)
+
+
+def shrink_kernel(ks, stages, per_device, rank, n_before, table, here, x, *refs):
     buffers, o_ref = refs[n_before:-1], refs[-1]
+    width = x.shape[1]
     for r in refs[:n_before]:
-        o_ref[:1] = r[...]
-    rows_of = lambda j: kept_ref[k - 1, j]
-    owners = buffer_owners(here, stages_of(k))
-    shrink_into(o_ref, n_before, table, k, rows_of, buffers, owners, rank)
-
-
-def shrink_call(k, table, here, kept, before, buffers, rank):
-    width = kept.shape[3]
-    n = 1 + len(before)
-    return pl.pallas_call(
-        functools.partial(shrink_kernel, k, rank, len(before)),
-        in_specs=[SMEM, SMEM, VMEM] + [VMEM] * (n - 1 + len(buffers)),
+        o_ref[: r.shape[0]] = r[...]
+    tags = buffer_tags(here, stages, per_device)
+    for at, k in enumerate(ks, o_ref.shape[0] - len(ks)):
+        for j in range(MOST):
+            start, _, within = segment_of(table, k, j)
+            for buffer, (whose, i) in zip(buffers, tags):
+
+                @pl.when((whose == table[k * ENTRIES]) & (within == i))
+                def _(at=at, j=j, start=start, buffer=buffer):
+                    o_ref[at, :, j * rank : (j + 1) * rank] = lax.dot_general(
+                        x[pl.ds(start, SEGMENT_ROWS), :],
+                        buffer[:, :width],
+                        (((1,), (1,)), ((), ())),
+                        preferred_element_type=jnp.float32,
+                    )
+
+
+def shrink_call(ks, table, here, x, before, buffers, per_device, rank):
+    n = len(ks) + sum(b.shape[0] for b in before)
+    return pl.pallas_call(
+        functools.partial(shrink_kernel, ks, stages_of_all(ks), per_device, rank, len(before)),
+        in_specs=[SMEM, SMEM, VMEM] + [VMEM] * (len(before) + len(buffers)),
         out_specs=VMEM,
         out_shape=jax.ShapeDtypeStruct((n, SEGMENT_ROWS, MOST * rank), jnp.float32),
         compiler_params=params(16),
-        cost_estimate=cost(MOST * 2 * SEGMENT_ROWS * width * 256, 4 * SEGMENT_ROWS * width),
-    )(table, here, kept, *before, *buffers)
-
-
-def fetch_up(up, at, table, k, j, buffers, owners, rank):
+        cost_estimate=cost(
+            len(ks) * MOST * 2 * SEGMENT_ROWS * x.shape[1] * 256,
+            len(ks) * 4 * SEGMENT_ROWS * x.shape[1],
+        ),
+    )(table, here, x, *before, *buffers)
+
+
+def fetch_up(up, at, table, k, j, buffers, tags, rank):
     columns = up.shape[2]
     _, _, within = segment_of(table, k, j)
-    for buffer, whose in zip(buffers, owners):
-
-        @pl.when(whose == table[k * ENTRIES])
+    for buffer, (whose, i) in zip(buffers, tags):
+
+        @pl.when((whose == table[k * ENTRIES]) & (within == i))
         def _(buffer=buffer):
-            first = buffer.shape[1] - columns
-            factor = buffer[pl.ds(pl.multiple_of(within * rank, rank), rank), first:]
+            factor = buffer[:, buffer.shape[1] - columns :]
             up[at, :rank, :] = factor
             up[at, rank:, :] = factor
 
@@ -392,31 +373,37 @@
     return jnp.dot(terms, factor, preferred_element_type=jnp.float32)
 
 
-def early_kernel(n_adapter, n_tensor, rank, table, here, *refs):
-    n_coded, n_buffers = n_tensor - 1, 2 * n_adapter - 3
-    base_ref, coded_refs, refs = refs[0], refs[1 : 1 + n_coded], refs[1 + n_coded :]
-    shrinks, refs = refs[: -4 - n_buffers], refs[-4 - n_buffers :]
+LATE = 2
+
+
+def total_shrinks(shrinks, n_tensor):
+    shares = []
+    for call in range(0, len(shrinks), n_tensor):
+        share = shrinks[call][...]
+        for r in shrinks[call + 1 : call + n_tensor]:
+            share = share + r[...]
+        shares += [share[i] for i in range(share.shape[0])]
+    return shares
+
+
+def early_kernel(n_adapter, n_tensor, per_device, rank, n_shrinks, table, here, *refs):
+    base_ref, coded_refs, refs = refs[0], refs[1:n_tensor], refs[n_tensor:]
+    shrinks, refs = refs[:n_shrinks], refs[n_shrinks:]
     buffers, (o_ref, rest_ref, up, total) = refs[:-4], refs[-4:]
-    for k in range(n_adapter - 1):
-        at = 0 if k == 0 else 2 * stages_of(k)[0] - 1
-        to = 2 * k + 1
-        owners = buffer_owners(here, stages_of(k))
+    first = n_adapter - LATE
+    tags = buffer_tags(here, range(first), per_device)
+    for k in range(first):
         for j in range(MOST):
-            fetch_up(up, k * MOST + j, table, k, j, buffers[at:to], owners, rank)
-    shares = []
-    for call in range(len(shrinks) // n_tensor):
-        share = shrinks[call * n_tensor][...]
-        for i in range(1, n_tensor):
-            share = share + shrinks[call * n_tensor + i][...]
-        shares += [share[i] for i in range(share.shape[0])]
+            fetch_up(up, k * MOST + j, table, k, j, buffers, tags, rank)
+    shares = total_shrinks(shrinks, n_tensor)
     total[...] = base_ref[...]
     add_decoded(total, len(CHUNKS) - 1, coded_refs)
     for k in range(n_adapter):
         for j in range(MOST):
             start, used, _ = segment_of(table, k, j)
             value = total[pl.ds(start, SEGMENT_ROWS), :]
-            if k == n_adapter - 1:
-                rest_ref[j] = value
+            if k >= first:
+                rest_ref[k - first, j] = value
                 continue
             lora = up_product(shares[k], j, up[k * MOST + j], rank)
 
@@ -427,18 +414,18 @@
                 )
 
 
-def early(n_adapter, n_tensor, table, here, base, coded, shrinks, buffers, rank):
+def early(n_adapter, n_tensor, table, here, base, coded, shrinks, buffers, per_device, rank):
     rows, columns = base.shape
     return pl.pallas_call(
-        functools.partial(early_kernel, n_adapter, n_tensor, rank),
+        functools.partial(early_kernel, n_adapter, n_tensor, per_device, rank, len(shrinks)),
         in_specs=[SMEM] * 2 + [VMEM] * (1 + len(coded) + len(shrinks) + len(buffers)),
         out_specs=[VMEM, VMEM],
         out_shape=[
             jax.ShapeDtypeStruct((rows, columns), jnp.bfloat16),
-            jax.ShapeDtypeStruct((MOST, SEGMENT_ROWS, columns), jnp.float32),
+            jax.ShapeDtypeStruct((LATE, MOST, SEGMENT_ROWS, columns), jnp.float32),
         ],
         scratch_shapes=[
-            pltpu.VMEM(((n_adapter - 1) * MOST, 2 * rank, columns), jnp.bfloat16),
+            pltpu.VMEM(((n_adapter - LATE) * MOST, 2 * rank, columns), jnp.bfloat16),
             pltpu.VMEM((rows, columns), jnp.float32),
         ],
         compiler_params=params(16),
@@ -446,42 +433,44 @@
     )(table, here, base, *coded, *shrinks, *buffers)
 
 
-def late_kernel(k, n_tensor, rank, table, here, *refs):
+def late_kernel(ks, n_tensor, per_device, rank, table, here, *refs):
     rest_ref, shrinks, refs = refs[0], refs[1 : 1 + n_tensor], refs[1 + n_tensor :]
     buffers, (_, o_ref, up, out, sems) = refs[:-5], refs[-5:]
-    owners = buffer_owners(here, stages_of(k))
-    share = shrinks[0][0]
-    for r in shrinks[1:]:
-        share = share + r[0]
+    tags = buffer_tags(here, stages_of_all(ks), per_device)
+    shares = total_shrinks(shrinks, n_tensor)
     stores = []
-    for j in range(MOST):
-        fetch_up(up, j, table, k, j, buffers, owners, rank)
-        start, used, _ = segment_of(table, k, j)
-        lora = up_product(share, j, up[j], rank)
-        out[j] = (rest_ref[j] + adapter_scale * lora).astype(jnp.bfloat16)
-        store = pltpu.make_async_copy(out.at[j], o_ref.at[pl.ds(start, SEGMENT_ROWS), :], sems.at[j])
-        pl.when(used)(store.start)
-        stores.append((used, store))
+    for i, k in enumerate(ks):
+        for j in range(MOST):
+            fetch_up(up, i * MOST + j, table, k, j, buffers, tags, rank)
+            start, used, _ = segment_of(table, k, j)
+            lora = up_product(shares[i], j, up[i * MOST + j], rank)
+            out[i, j] = (rest_ref[i, j] + adapter_scale * lora).astype(jnp.bfloat16)
+            store = pltpu.make_async_copy(
+                out.at[i, j], o_ref.at[pl.ds(start, SEGMENT_ROWS), :], sems.at[i, j]
+            )
+            pl.when(used)(store.start)
+            stores.append((used, store))
     for used, store in stores:
         pl.when(used)(store.wait)
 
 
-def late(k, n_tensor, table, here, rest, shrinks, buffers, value, rank):
+def late(ks, n_tensor, table, here, rest, shrinks, buffers, value, per_device, rank):
     rows, columns = value.shape
     return pl.pallas_call(
-        functools.partial(late_kernel, k, n_tensor, rank),
+        functools.partial(late_kernel, ks, n_tensor, per_device, rank),
         in_specs=[SMEM] * 2 + [VMEM] * (1 + len(shrinks) + len(buffers)) + [ANY],
         out_specs=ANY,
         out_shape=jax.ShapeDtypeStruct((rows, columns), jnp.bfloat16),
         scratch_shapes=[
-            pltpu.VMEM((MOST, 2 * rank, columns), jnp.bfloat16),
-            pltpu.VMEM((MOST, SEGMENT_ROWS, columns), jnp.bfloat16),
-            pltpu.SemaphoreType.DMA((MOST,)),
+            pltpu.VMEM((LATE * MOST, 2 * rank, columns), jnp.bfloat16),
+            pltpu.VMEM((LATE, MOST, SEGMENT_ROWS, columns), jnp.bfloat16),
+            pltpu.SemaphoreType.DMA((LATE, MOST)),
         ],
         input_output_aliases={3 + len(shrinks) + len(buffers): 0},
         compiler_params=params(8),
         cost_estimate=cost(
-            6 * MOST * SEGMENT_ROWS * rank * columns, 8 * MOST * SEGMENT_ROWS * columns
+            6 * LATE * MOST * SEGMENT_ROWS * rank * columns,
+            8 * LATE * MOST * SEGMENT_ROWS * columns,
         ),
     )(table, here, rest, *shrinks, *buffers, value)
 
@@ -505,31 +494,36 @@
         pairs = [(i, (i + step) % n_tensor) for i in range(n_tensor)]
         return lax.ppermute(array, "tensor", pairs)
 
-    def along_line(array, stage):
-        up = [(2 * i, 2 * (i + 1)) for i in range(stage - 1, n_adapter - 1)]
-        down = [(2 * i + 1, 2 * (i - 1) + 1) for i in range(1, n_adapter - stage + 1)]
-        return lax.ppermute(array, ("adapter", "dp"), up + down)
-
-    def swap_cores(array):
-        return lax.ppermute(array, "dp", [(0, 1), (1, 0)])
+    def along_line(arrays, stage):
+        moved = []
+        for i, array in enumerate(arrays):
+            up, down = i % 2, 1 - i % 2
+            pairs = [(2 * z + up, 2 * (z + 1) + up) for z in range(stage - 1, n_adapter - 1)]
+            pairs += [(2 * z + down, 2 * (z - 1) + down) for z in range(1, n_adapter - stage + 1)]
+            moved.append(lax.ppermute(array, ("adapter", "dp"), pairs))
+        return moved
+
+    def swap_cores(arrays):
+        return [lax.ppermute(a, "dp", [(0, 1), (1, 0)]) for a in arrays]
 
     down = jnp.swapaxes(adapter_down_weight, 1, 2).reshape(per_device * rank, width)
     up = adapter_up_weight.reshape(per_device * rank, value_weight.shape[1])
     tokens, value_weight, down, up = (
         pltpu.with_memory_space_constraint(a, pltpu.HBM) for a in (tokens, value_weight, down, up)
     )
-    message = message_call(here, down, up, columns)
-    table = table_call(here, row_adapter_index, adapter_slot_of, n_adapter, per_device)
-
-    buffers, shrinks = [[message]], []
+    messages = message_call(here, down, up, columns, per_device)
+    buffers = [[[m] for m in messages]]
 
     def buffers_of(stages):
-        return [b for stage in stages for b in buffers[stage]]
-
-    def add_shrink(mine):
-        shrinks.extend([mine] + [swap_tensor(mine, step) for step in range(1, n_tensor)])
-
-    held = along_line(message, 1)
+        return [b for stage in stages for pair in buffers[stage] for b in pair]
+
+    def swapped(mine):
+        return [mine] + [swap_tensor(mine, step) for step in range(1, n_tensor)]
+
+    def shrink(ks, x, before=()):
+        mine = buffers_of(stages_of_all(ks))
+        return shrink_call(ks, table, here, x, list(before), mine, per_device, rank)
+
     others = range(1, n_tensor)
 
     def sent_for(step, chunks):
@@ -537,61 +531,58 @@
         target = (me_t + step) % n_tensor
         return sent_call(tokens, value_weight, target, columns, chunks[0][0], sizes)
 
+    held = along_line(messages, 1)
     parts = [[sent_for(step, CHUNKS[:1])[0] for step in others]]
     rest_parts = [sent_for(step, CHUNKS[1:]) for step in others]
     parts += [[p[i] for p in rest_parts] for i in range(len(CHUNKS) - 1)]
     sent = [[swap_tensor(p, step) for step, p in zip(others, parts[0])]]
-    last = n_adapter - 1
-    done = [table] + [p for group in parts for p in group] + sent[0]
-    before = None
-    for stage in range(1, last):
-        came = after(held, *done)
-        held = along_line(came, stage + 1)
+    done = [p for group in parts for p in group] + sent[0]
+    shrinks = []
+    for stage in range(1, n_adapter):
+        if stage == n_adapter - 1:
+            value, remaining = early(
+                n_adapter,
+                n_tensor,
+                table,
+                here,
+                base,
+                sent[2],
+                shrinks,
+                buffers_of(range(n_adapter - LATE)),
+                per_device,
+                rank,
+            )
+            done = [value]
+        came = list(lax.optimization_barrier((*held, *done)))[:per_device]
+        if stage < n_adapter - 1:
+            held = along_line(came, stage + 1)
+        buffers.append([list(pair) for pair in zip(came, swap_cores(came))])
         if stage < len(CHUNKS):
-            sent.append([swap_tensor(after(p, came), step) for step, p in zip(others, parts[stage])])
+            sent.append([swap_tensor(after(p, *came), step) for step, p in zip(others, parts[stage])])
         if stage == 1:
-            base, before, kept = own_call(
-                after(table, came), here, tokens, value_weight, message, sent[0], columns, n_adapter, rank
-            )
-            add_shrink(before)
-            done = sent[1] + shrinks
-        else:
+            base, x = own_call(tokens, value_weight, after(me_t, *came), sent[0], columns)
+            done = sent[1] + [base]
+        elif stage < n_adapter - 1:
+            done = []
             if stage == 2:
-                base = add_call(1, after(base, came), sent[1])
-            before = shrink_call(
-                stage - 1, table, here, after(kept, came), [], buffers_of(stages_of(stage - 1)), rank
-            )
-            if stage < last - 1:
-                add_shrink(before)
-            done = []
-        buffers.append([came, swap_cores(came)])
-    merged = shrink_call(
-        last - 1, table, here, kept, [before], buffers_of(stages_of(last - 1)), rank
-    )
-    add_shrink(merged)
-    value, remaining = early(
-        n_adapter,
-        n_tensor,
-        table,
-        here,
-        base,
-        sent[2],
-        shrinks,
-        buffers_of(range(last)),
-        rank,
-    )
-    came = after(held, value)
-    buffers.append([came, swap_cores(came)])
-    add_shrink(shrink_call(last, table, here, kept, [], buffers_of(stages_of(last)), rank))
+                table = table_call(
+                    after(here, *came), row_adapter_index, adapter_slot_of, n_adapter, per_device
+                )
+                base = add_call(1, after(base, *came), sent[1])
+            shrinks += swapped(shrink([0, 1] if stage == 2 else [stage - 1], x))
+    last = [n_adapter - 2, n_adapter - 1]
+    mine = shrink(last[:1], after(x, *came))
+    mine = shrink(last[1:], x, [mine])
     return late(
         last,
         n_tensor,
         table,
         here,
         remaining,
-        shrinks[-n_tensor:],
-        buffers_of(stages_of(last)),
+        swapped(mine),
+        buffers_of(stages_of_all(last)),
         value,
+        per_device,
         rank,
     )
 

time: 67.9 us -> 80.6 us (1.19)
  local copies, waits for them, and re-layouts: 0.01 us -> 11.7 us
  waiting for transfers between devices: 18.4 us -> 10.1 us
  starting transfers between devices: 16.5 us -> 23 us
  Pallas kernels: 31.8 us -> 34.8 us
    unnamed x6 -> x28, local copies, waits for them, and re-layouts: 0.01 us -> 11.7 us
    ppermute x6 -> x12, starting transfers between devices: 9 us -> 16.7 us  [the longest x6 15.5 us: along_line(): moved.append(lax.ppermute(array, ('adapter', 'dp'), pairs))]
    ppermute x6 -> x5, waiting for transfers between devices: 14.2 us -> 9.07 us  [swap_tensor(): return lax.ppermute(array, 'tensor', pairs)]
    ppermute x6 -> x12, waiting for transfers between devices: 4.21 us -> 1.04 us  [the longest x6 1.02 us: swap_cores(): return [lax.ppermute(a, 'dp', [(0, 1), (1, 0)]) for a in arrays]]
    pallas_call x7, Pallas kernels: 20 us -> 22.2 us  [the longest x1 7.49 us: own_call(): pl.pallas_call(own_kernel, in_specs=[SMEM, HBM, HBM] + [VMEM] * len(coded...]
    ppermute x6 -> x5, starting transfers between devices: 7.48 us -> 6.31 us  [swap_tensor(): return lax.ppermute(array, 'tensor', pairs)]
  transfers between devices with their start and end apart: 12 -> 17, of which waited for: 6 -> 5; matrix products, arithmetic and copies ran while one was open for 0% -> 0% of each run, Pallas kernels for 40% -> 34%
where the time goes in v8:
time: 80.6 us; the launch traced here: 80.1 us
  Pallas kernels  34.8 us (43%)
  starting transfers between devices  23 us (29%)
  local copies, waits for them, and re-layouts  11.7 us (15%)
  waiting for transfers between devices  10.1 us (13%)
    ppermute x6, starting transfers between devices, along_line(): moved.append(lax.ppermute(array, ('adapter', 'dp'), pairs))  15.5 us
    unnamed x28, local copies, waits for them, and re-layouts  11.7 us
    pallas_call x2, Pallas kernels, sent_call(): pl.pallas_call(functools.partial(sent_kernel, first, sizes), in_specs=[SM...  10.9 us
    ppermute x5, waiting for transfers between devices, swap_tensor(): return lax.ppermute(array, 'tensor', pairs)  9.07 us
    pallas_call x1, Pallas kernels, own_call(): pl.pallas_call(own_kernel, in_specs=[SMEM, HBM, HBM] + [VMEM] * len(coded...  7.49 us
    pallas_call x3, Pallas kernels, shrink_call(): pl.pallas_call(functools.partial(shrink_kernel, ks, stages_of_all(ks), pe...  6.56 us
    ppermute x5, starting transfers between devices, swap_tensor(): return lax.ppermute(array, 'tensor', pairs)  6.31 us
    pallas_call x1, Pallas kernels, late(): pl.pallas_call(functools.partial(late_kernel, ks, n_tensor, per_device, r...  3.17 us
  transfers between devices with their start and end apart: 17, of which 5 were waited for; matrix products, arithmetic and copies ran while one was open for 0% of the time, Pallas kernels for 34%

profile of v8, /device:TPU:16, one launch (start us, length us, event | category | flops | bytes accessed | tf_op | source)
XLA Modules:
  0.0 80.1 jit_solution(7140454240455258110)
XLA Ops:
  0.0 0.1 pad_add_fusion.here
  0.1 1.8 %shard_map.64 = (bf16[64,4608]{1,0:T(8,128)(2,1)S(1)}, bf16[64,4608]{1,0:T(8,128)(2,1)S(1)}) custom-call(s32[3]{0:T(128)S(1)} %pad_add_fusion.here, bf16[128,4096]{1,0:T(8,128)(2,1)} %bitcast.9, bf16[128,1024]{1,0:T(8,128)(2,1)} %bitcast.10), custom_call_target="tpu_custom_call" | custom-call | bytes 2359296 | tf_op jit(solution)/shard_map/pallas_call | solution.py:84
  1.9 0.0 copy-start.3
  1.9 0.0 copy-start.5
  1.9 3.5 %collective-permute-start = (bf16[64,4608]{1,0:T(8,128)(2,1)S(1)}, bf16[64,4608]{1,0:T(8,128)(2,1)S(1)}, u32[]{:S(2)}, u32[]{:S(2)}) collective-permute-start(bf16[64,4608]{1,0:T(8,128)(2,1)S(1)} %get-tuple-element.25.refs_0_.refs_4_), channel_id=1, source_target_pairs={{0,4},{4,8},{8,12},{5,1},{9,5},{13,9},{2,6},{6,10},{10,14},{7,3},{... | collective-permute-start | bytes 1769480 | tf_op jit(solution)/shard_map/ppermute | solution.py:503
  5.4 2.4 %collective-permute-start.1 = (bf16[64,4608]{1,0:T(8,128)(2,1)S(1)}, bf16[64,4608]{1,0:T(8,128)(2,1)S(1)}, u32[]{:S(2)}, u32[]{:S(2)}) collective-permute-start(bf16[64,4608]{1,0:T(8,128)(2,1)S(1)} %get-tuple-element.26.refs_1_.refs_5_), channel_id=1, source_target_pairs={{1,5},{5,9},{9,13},{4,0},{8,4},{12,8},{3,7},{7,11},{11,15},{6,2},{... | collective-permute-start | bytes 1769480 | tf_op jit(solution)/shard_map/ppermute | solution.py:503
  7.8 3.6 %shard_map.65 = s32[168,512]{1,0:T(8,128)S(1)} custom-call(s32[1]{0:T(128)} %bitcast.6.column, bf16[1024,4096]{1,0:T(8,128)(2,1)} %x_ref.5, bf16[4096,1024]{1,0:T(8,128)(2,1)} %w_ref.5), custom_call_target="tpu_custom_call" | custom-call | flops 1073741824 | bytes 6815744 | tf_op jit(solution)/shard_map/pallas_call | solution.py:254
  11.3 0.0 copy-done.11
  11.4 0.0 copy-done.3
  11.4 0.0 copy-done.5
  11.4 1.6 %collective-permute-start.2 = (s32[168,512]{1,0:T(8,128)S(1)}, s32[168,512]{1,0:T(8,128)S(1)}, u32[]{:S(2)}, u32[]{:S(2)}) collective-permute-start(s32[168,512]{1,0:T(8,128)S(1)} %shard_map.65), channel_id=1, source_target_pairs={{0,2},{2,0},{1,3},{3,1},{4,6},{6,4},{5,7},{7,5},{8,10},{10,8},{9,1... | collective-permute-start | bytes 1032200 | tf_op jit(solution)/shard_map/ppermute | solution.py:495
  12.9 7.3 %shard_map.66 = (s32[328,512]{1,0:T(8,128)S(1)}, s32[168,512]{1,0:T(8,128)}) custom-call(s32[1]{0:T(128)} %bitcast.6.column, bf16[1024,4096]{1,0:T(8,128)(2,1)} %x_ref.5, bf16[4096,1024]{1,0:T(8,128)(2,1)} %w_ref.5), custom_call_target="tpu_custom_call" | custom-call | flops 3221225472 | bytes 12058624 | tf_op jit(solution)/shard_map/pallas_call | solution.py:254
  20.3 0.4 collective-permute-done.2.refs_0_
  20.7 0.0 collective-permute-done.refs_2_.refs_6_.refs_0_.refs_3_
  20.7 0.0 collective-permute-done.1.refs_4_.refs_8_.refs_2_.refs_5_
  20.7 1.5 %collective-permute-start.5 = (s32[328,512]{1,0:T(8,128)S(1)}, s32[328,512]{1,0:T(8,128)S(1)}, u32[]{:S(2)}, u32[]{:S(2)}) collective-permute-start(s32[328,512]{1,0:T(8,128)S(1)} %get-tuple-element.31), channel_id=1, source_target_pairs={{0,2},{2,0},{1,3},{3,1},{4,6},{6,4},{5,7},{7,5},{8,10},{10,8},{9,1... | collective-permute-start | bytes 2015240 | tf_op jit(solution)/shard_map/ppermute | solution.py:495
  22.2 2.2 %collective-permute-start.3 = (bf16[64,4608]{1,0:T(8,128)(2,1)S(1)}, bf16[64,4608]{1,0:T(8,128)(2,1)S(1)}, u32[]{:S(2)}, u32[]{:S(2)}) collective-permute-start(bf16[64,4608]{1,0:T(8,128)(2,1)S(1)} %collective-permute-done.refs_2_.refs_6_.refs_0_.refs_3_), channel_id=1, source_target_pairs={{4,8},{8,12},{5,1},{9,5},{6,10},{10,14},{7,3},{11,7},{20,24},{24,2... | collective-permute-start | bytes 1769480 | tf_op jit(solution)/shard_map/ppermute | solution.py:503
  24.4 3.7 %collective-permute-start.4 = (bf16[64,4608]{1,0:T(8,128)(2,1)S(1)}, bf16[64,4608]{1,0:T(8,128)(2,1)S(1)}, u32[]{:S(2)}, u32[]{:S(2)}) collective-permute-start(bf16[64,4608]{1,0:T(8,128)(2,1)S(1)} %collective-permute-done.1.refs_4_.refs_8_.refs_2_.refs_5_), channel_id=1, source_target_pairs={{5,9},{9,13},{4,0},{8,4},{7,11},{11,15},{6,2},{10,6},{21,25},{25,2... | collective-permute-start | bytes 1769480 | tf_op jit(solution)/shard_map/ppermute | solution.py:503
  28.1 0.1 collective-permute-start.7
  28.2 0.5 collective-permute-start.8
  28.7 7.5 %shard_map.67 = (f32[1024,512]{1,0:T(8,128)S(1)}, bf16[1024,4096]{1,0:T(8,128)(2,1)S(1)}) custom-call(s32[1]{0:T(128)} %bitcast.7.column, bf16[1024,4096]{1,0:T(8,128)(2,1)} %x_ref.5, bf16[4096,1024]{1,0:T(8,128)(2,1)} %w_ref.5, s32[168,512]{1,0:T(8,128)S(1)} %collective-permute-done.2.refs_0_), custom_call_target="tpu_custom_call" | custom-call | flops 4294967296 | bytes 14680064 | tf_op jit(solution)/shard_map/pallas_call | solution.py:295
  36.2 0.0 copy-start
  36.2 3.3 %copy-done = bf16[1024,4096]{1,0:T(8,128)(2,1)} copy-done((bf16[1024,4096]{1,0:T(8,128)(2,1)}, bf16[1024,4096]{1,0:T(8,128)(2,1)S(1)}, u32[]{:S(2)}) %copy-start) | copy-done | bytes 8388632
  39.5 1.4 %copy-done.7 = f32[1024,512]{1,0:T(8,128)} copy-done((f32[1024,512]{1,0:T(8,128)}, f32[1024,512]{1,0:T(8,128)S(1)}, u32[]{:S(2)}) %copy-start.7) | copy-done | bytes 2097176
  40.8 0.0 collective-permute-done.3.refs_4_.refs_1_.refs_7_
  40.8 0.0 collective-permute-done.4.refs_6_.refs_3_.refs_9_
  40.8 0.0 collective-permute-done.5.refs_0_
  40.9 0.0 copy-start.9
  40.9 0.8 %copy-done.9 = s32[328,512]{1,0:T(8,128)} copy-done((s32[328,512]{1,0:T(8,128)}, s32[328,512]{1,0:T(8,128)S(1)}, u32[]{:S(2)}) %copy-start.9) | copy-done | bytes 671768
  41.7 2.2 %collective-permute-start.10 = (bf16[64,4608]{1,0:T(8,128)(2,1)S(1)}, bf16[64,4608]{1,0:T(8,128)(2,1)}, u32[]{:S(2)}, u32[]{:S(2)}) collective-permute-start(bf16[64,4608]{1,0:T(8,128)(2,1)S(1)} %collective-permute-done.3.refs_4_.refs_1_.refs_7_), channel_id=1, source_target_pairs={{8,12},{5,1},{10,14},{7,3},{24,28},{21,17},{26,30},{23,19}} | collective-permute-start | bytes 1769480 | tf_op jit(solution)/shard_map/ppermute | solution.py:503
  43.9 1.5 %collective-permute-start.11 = (bf16[64,4608]{1,0:T(8,128)(2,1)S(1)}, bf16[64,4608]{1,0:T(8,128)(2,1)}, u32[]{:S(2)}, u32[]{:S(2)}) collective-permute-start(bf16[64,4608]{1,0:T(8,128)(2,1)S(1)} %collective-permute-done.4.refs_6_.refs_3_.refs_9_), channel_id=1, source_target_pairs={{9,13},{4,0},{11,15},{6,2},{25,29},{20,16},{27,31},{22,18}} | collective-permute-start | bytes 1769480 | tf_op jit(solution)/shard_map/ppermute | solution.py:503
  45.4 1.0 %collective-permute-start.6 = (s32[168,512]{1,0:T(8,128)}, s32[168,512]{1,0:T(8,128)}, u32[]{:S(2)}, u32[]{:S(2)}) collective-permute-start(s32[168,512]{1,0:T(8,128)} %get-tuple-element.38), channel_id=1, source_target_pairs={{0,2},{2,0},{1,3},{3,1},{4,6},{6,4},{5,7},{7,5},{8,10},{10,8},{9,1... | collective-permute-start | bytes 1032200 | tf_op jit(solution)/shard_map/ppermute | solution.py:495
  46.5 1.4 %shard_map.68.table = s32[32]{0:T(128)} custom-call(s32[3]{0:T(128)} %copy-done.11, s32[1024]{0:T(1024)} %ids.1, s32[8]{0:T(128)} %slots.1), custom_call_target="tpu_custom_call" | custom-call | bytes 4096 | tf_op jit(solution)/shard_map/pallas_call | solution.py:116
  47.9 0.0 collective-permute-done.7.refs_3_.refs_7_.refs_1_.refs_4_
  47.9 0.0 collective-permute-done.8.refs_5_.refs_9_.refs_3_.refs_6_
  47.9 0.0 copy-done.12
  47.9 0.0 copy-start.1
  47.9 3.4 %copy-done.1 = bf16[1024,4096]{1,0:T(8,128)(2,1)S(1)} copy-done((bf16[1024,4096]{1,0:T(8,128)(2,1)S(1)}, bf16[1024,4096]{1,0:T(8,128)(2,1)}, u32[]{:S(2)}) %copy-start.1) | copy-done | bytes 8388632
  51.3 1.1 %copy-done.4 = bf16[64,4608]{1,0:T(8,128)(2,1)S(1)} copy-done((bf16[64,4608]{1,0:T(8,128)(2,1)S(1)}, bf16[64,4608]{1,0:T(8,128)(2,1)}, u32[]{:S(2)}) %copy-start.4) | copy-done | bytes 589848
  52.4 1.1 %copy-done.6 = bf16[64,4608]{1,0:T(8,128)(2,1)S(1)} copy-done((bf16[64,4608]{1,0:T(8,128)(2,1)S(1)}, bf16[64,4608]{1,0:T(8,128)(2,1)}, u32[]{:S(2)}) %copy-start.6) | copy-done | bytes 589848
  53.4 0.7 copy-done.13
  54.1 2.7 %shard_map.70.refs_2_ = f32[2,128,128]{2,1,0:T(8,128)S(1)} custom-call(s32[32]{0:T(128)S(1)} %copy-done.13, s32[3]{0:T(128)S(1)} %copy-done.12, bf16[1024,4096]{1,0:T(8,128)(2,1)S(1)} %copy-done.1, bf16[64,4608]{1,0:T(8,128)(2,1)S(1)} %copy-done.4, bf16[64,4608]{1,0:T(8,128)(2,1)S(1)} %copy-done.6, ...), custom_call_target="tpu_custom_call" | custom-call | flops 1073741824 | bytes 4194304 | tf_op jit(solution)/shard_map/pallas_call | solution.py:342
  56.8 0.0 copy-start.2
  56.8 1.1 %collective-permute-start.9 = (f32[2,128,128]{2,1,0:T(8,128)S(1)}, f32[2,128,128]{2,1,0:T(8,128)S(1)}, u32[]{:S(2)}, u32[]{:S(2)}) collective-permute-start(f32[2,128,128]{2,1,0:T(8,128)S(1)} %shard_map.70.refs_2_), channel_id=1, source_target_pairs={{0,2},{2,0},{1,3},{3,1},{4,6},{6,4},{5,7},{7,5},{8,10},{10,8},{9,1... | collective-permute-start | bytes 393224 | tf_op jit(solution)/shard_map/ppermute | solution.py:495
  57.9 0.0 collective-permute-start.12
  57.9 4.0 %collective-permute-done.9.refs_3_ = f32[2,128,128]{2,1,0:T(8,128)S(1)} collective-permute-done((f32[2,128,128]{2,1,0:T(8,128)S(1)}, f32[2,128,128]{2,1,0:T(8,128)S(1)}, u32[]{:S(2)}, u32[]{:S(2)}) %collective-permute-start.9) | collective-permute-done | bytes 131104 | tf_op jit(solution)/shard_map/ppermute | solution.py:495
  61.9 0.0 collective-permute-start.13
  61.9 0.0 copy-done.8
  61.9 0.3 shard_map.69.refs_0_
  62.2 0.0 collective-permute-done.6.refs_1_
  62.2 3.2 %shard_map.71 = (bf16[1024,512]{1,0:T(8,128)(2,1)}, f32[2,2,128,512]{3,2,1,0:T(8,128)S(1)}) custom-call(s32[32]{0:T(128)S(1)} %copy-done.13, s32[3]{0:T(128)S(1)} %copy-done.12, f32[1024,512]{1,0:T(8,128)S(1)} %shard_map.69.refs_0_, s32[168,512]{1,0:T(8,128)} %collective-permute-done.6.refs_1_, f32[2,128,128]{2,1,0:T(8,128)S(1)} %shard_map.70.refs_2_, ...), custom_call_target="tpu_custom_call" | custom-call | flops 201326592 | bytes 5242880 | tf_op jit(solution)/shard_map/pallas_call | solution.py:419
  65.4 0.0 collective-permute-done.10.refs_5_.refs_11_
  65.4 0.0 collective-permute-done.11.refs_7_.refs_13_
  65.4 0.6 collective-permute-start.14
  65.9 0.1 collective-permute-start.15
  66.0 0.0 collective-permute-done.12.refs_5_.refs_2_.refs_8_
  66.0 0.0 collective-permute-done.13.refs_7_.refs_4_.refs_10_
  66.0 1.6 %shard_map.72.refs_0_ = f32[1,128,128]{2,1,0:T(8,128)S(1)} custom-call(s32[32]{0:T(128)S(1)} %copy-done.13, s32[3]{0:T(128)S(1)} %copy-done.12, bf16[1024,4096]{1,0:T(8,128)(2,1)S(1)} %copy-done.2, bf16[64,4608]{1,0:T(8,128)(2,1)S(1)} %collective-permute-done.refs_2_.refs_6_.refs_0_.refs_3_, ...), custom_call_target="tpu_custom_call" | custom-call | flops 536870912 | bytes 2097152 | tf_op jit(solution)/shard_map/pallas_call | solution.py:342
  67.6 0.2 collective-permute-done.14.refs_6_.refs_12_
  67.8 0.8 %collective-permute-done.15.refs_8_.refs_14_ = bf16[64,4608]{1,0:T(8,128)(2,1)S(1)} collective-permute-done((bf16[64,4608]{1,0:T(8,128)(2,1)}, bf16[64,4608]{1,0:T(8,128)(2,1)S(1)}, u32[]{:S(2)}, u32[]{:S(2)}) %collective-permute-start.15) | collective-permute-done | bytes 589856 | tf_op jit(solution)/shard_map/ppermute | solution.py:507
  68.6 2.3 %shard_map.73.refs_1_ = f32[2,128,128]{2,1,0:T(8,128)S(1)} custom-call(s32[32]{0:T(128)S(1)} %copy-done.13, s32[3]{0:T(128)S(1)} %copy-done.12, bf16[1024,4096]{1,0:T(8,128)(2,1)S(1)} %copy-done.2, f32[1,128,128]{2,1,0:T(8,128)S(1)} %shard_map.72.refs_0_, bf16[64,4608]{1,0:T(8,128)(2,1)S(1)} %collective-permute-done.3.refs_4_.refs_1_.refs_7_, ...), custom_call_target="tpu_custom_call" | custom-call | flops 536870912 | bytes 2097152 | tf_op jit(solution)/shard_map/pallas_call | solution.py:342
  70.9 1.2 %collective-permute-start.16 = (f32[2,128,128]{2,1,0:T(8,128)S(1)}, f32[2,128,128]{2,1,0:T(8,128)S(1)}, u32[]{:S(2)}, u32[]{:S(2)}) collective-permute-start(f32[2,128,128]{2,1,0:T(8,128)S(1)} %shard_map.73.refs_1_), channel_id=1, source_target_pairs={{0,2},{2,0},{1,3},{3,1},{4,6},{6,4},{5,7},{7,5},{8,10},{10,8},{9,1... | collective-permute-start | bytes 393224 | tf_op jit(solution)/shard_map/ppermute | solution.py:495
  72.1 4.7 %collective-permute-done.16.refs_2_ = f32[2,128,128]{2,1,0:T(8,128)S(1)} collective-permute-done((f32[2,128,128]{2,1,0:T(8,128)S(1)}, f32[2,128,128]{2,1,0:T(8,128)S(1)}, u32[]{:S(2)}, u32[]{:S(2)}) %collective-permute-start.16) | collective-permute-done | bytes 131104 | tf_op jit(solution)/shard_map/ppermute | solution.py:495
  76.8 3.2 %shard_map.74 = bf16[1024,512]{1,0:T(8,128)(2,1)} custom-call(s32[32]{0:T(128)S(1)} %copy-done.13, s32[3]{0:T(128)S(1)} %copy-done.12, f32[2,2,128,512]{3,2,1,0:T(8,128)S(1)} %get-tuple-element.40.refs_0_, f32[2,128,128]{2,1,0:T(8,128)S(1)} %shard_map.73.refs_1_, ...), custom_call_target="tpu_custom_call", output_to_operand_aliasing={{}: (17, {})} | custom-call | flops 100663296 | bytes 2097152 | tf_op jit(solution)/shard_map/pallas_call | solution.py:459
  (10 shorter events, 0.0 us)
Async XLA Ops:
  0.1 11.3 %copy-start.11 = (s32[3]{0:T(128)}, s32[3]{0:T(128)S(1)}, u32[]{:S(2)}) copy-start(s32[3]{0:T(128)S(1)} %pad_add_fusion.here) | copy-start | bytes 40
  1.9 9.5 %copy-start.3 = (bf16[64,4608]{1,0:T(8,128)(2,1)}, bf16[64,4608]{1,0:T(8,128)(2,1)S(1)}, u32[]{:S(2)}) copy-start(bf16[64,4608]{1,0:T(8,128)(2,1)S(1)} %get-tuple-element.25.refs_0_.refs_4_) | copy-start | bytes 1769476
  1.9 9.5 %copy-start.5 = (bf16[64,4608]{1,0:T(8,128)(2,1)}, bf16[64,4608]{1,0:T(8,128)(2,1)S(1)}, u32[]{:S(2)}) copy-start(bf16[64,4608]{1,0:T(8,128)(2,1)S(1)} %get-tuple-element.26.refs_1_.refs_5_) | copy-start | bytes 1769476
  1.9 18.8 %collective-permute-start = (bf16[64,4608]{1,0:T(8,128)(2,1)S(1)}, bf16[64,4608]{1,0:T(8,128)(2,1)S(1)}, u32[]{:S(2)}, u32[]{:S(2)}) collective-permute-start(bf16[64,4608]{1,0:T(8,128)(2,1)S(1)} %get-tuple-element.25.refs_0_.refs_4_), channel_id=1, source_target_pairs={{0,4},{4,8},{8,12},{5,1},{9,5},{13,9},{2,6},{6,10},{10,14},{7,3},{... | collective-permute-start | bytes 1769480 | tf_op jit(solution)/shard_map/ppermute | solution.py:503
  5.4 15.3 %collective-permute-start.1 = (bf16[64,4608]{1,0:T(8,128)(2,1)S(1)}, bf16[64,4608]{1,0:T(8,128)(2,1)S(1)}, u32[]{:S(2)}, u32[]{:S(2)}) collective-permute-start(bf16[64,4608]{1,0:T(8,128)(2,1)S(1)} %get-tuple-element.26.refs_1_.refs_5_), channel_id=1, source_target_pairs={{1,5},{5,9},{9,13},{4,0},{8,4},{12,8},{3,7},{7,11},{11,15},{6,2},{... | collective-permute-start | bytes 1769480 | tf_op jit(solution)/shard_map/ppermute | solution.py:503
  11.4 9.3 %collective-permute-start.2 = (s32[168,512]{1,0:T(8,128)S(1)}, s32[168,512]{1,0:T(8,128)S(1)}, u32[]{:S(2)}, u32[]{:S(2)}) collective-permute-start(s32[168,512]{1,0:T(8,128)S(1)} %shard_map.65), channel_id=1, source_target_pairs={{0,2},{2,0},{1,3},{3,1},{4,6},{6,4},{5,7},{7,5},{8,10},{10,8},{9,1... | collective-permute-start | bytes 1032200 | tf_op jit(solution)/shard_map/ppermute | solution.py:495
  20.7 20.1 %collective-permute-start.5 = (s32[328,512]{1,0:T(8,128)S(1)}, s32[328,512]{1,0:T(8,128)S(1)}, u32[]{:S(2)}, u32[]{:S(2)}) collective-permute-start(s32[328,512]{1,0:T(8,128)S(1)} %get-tuple-element.31), channel_id=1, source_target_pairs={{0,2},{2,0},{1,3},{3,1},{4,6},{6,4},{5,7},{7,5},{8,10},{10,8},{9,1... | collective-permute-start | bytes 2015240 | tf_op jit(solution)/shard_map/ppermute | solution.py:495
  22.2 18.6 %collective-permute-start.3 = (bf16[64,4608]{1,0:T(8,128)(2,1)S(1)}, bf16[64,4608]{1,0:T(8,128)(2,1)S(1)}, u32[]{:S(2)}, u32[]{:S(2)}) collective-permute-start(bf16[64,4608]{1,0:T(8,128)(2,1)S(1)} %collective-permute-done.refs_2_.refs_6_.refs_0_.refs_3_), channel_id=1, source_target_pairs={{4,8},{8,12},{5,1},{9,5},{6,10},{10,14},{7,3},{11,7},{20,24},{24,2... | collective-permute-start | bytes 1769480 | tf_op jit(solution)/shard_map/ppermute | solution.py:503
  24.4 16.4 %collective-permute-start.4 = (bf16[64,4608]{1,0:T(8,128)(2,1)S(1)}, bf16[64,4608]{1,0:T(8,128)(2,1)S(1)}, u32[]{:S(2)}, u32[]{:S(2)}) collective-permute-start(bf16[64,4608]{1,0:T(8,128)(2,1)S(1)} %collective-permute-done.1.refs_4_.refs_8_.refs_2_.refs_5_), channel_id=1, source_target_pairs={{5,9},{9,13},{4,0},{8,4},{7,11},{11,15},{6,2},{10,6},{21,25},{25,2... | collective-permute-start | bytes 1769480 | tf_op jit(solution)/shard_map/ppermute | solution.py:503
  28.1 19.8 %collective-permute-start.7 = (bf16[64,4608]{1,0:T(8,128)(2,1)S(1)}, bf16[64,4608]{1,0:T(8,128)(2,1)S(1)}, u32[]{:S(2)}, u32[]{:S(2)}) collective-permute-start(bf16[64,4608]{1,0:T(8,128)(2,1)S(1)} %collective-permute-done.refs_2_.refs_6_.refs_0_.refs_3_), channel_id=1, source_target_pairs={{0,1},{1,0},{2,3},{3,2},{4,5},{5,4},{6,7},{7,6},{8,9},{9,8},{10,11... | collective-permute-start | bytes 1769480 | tf_op jit(solution)/shard_map/ppermute | solution.py:507
  28.2 19.7 %collective-permute-start.8 = (bf16[64,4608]{1,0:T(8,128)(2,1)S(1)}, bf16[64,4608]{1,0:T(8,128)(2,1)S(1)}, u32[]{:S(2)}, u32[]{:S(2)}) collective-permute-start(bf16[64,4608]{1,0:T(8,128)(2,1)S(1)} %collective-permute-done.1.refs_4_.refs_8_.refs_2_.refs_5_), channel_id=1, source_target_pairs={{0,1},{1,0},{2,3},{3,2},{4,5},{5,4},{6,7},{7,6},{8,9},{9,8},{10,11... | collective-permute-start | bytes 1769480 | tf_op jit(solution)/shard_map/ppermute | solution.py:507
  28.7 19.2 %copy-start.12 = (s32[3]{0:T(128)S(1)}, s32[3]{0:T(128)}, u32[]{:S(2)}) copy-start(s32[3]{0:T(128)} %copy-done.11) | copy-start | bytes 40
  36.2 3.3 %copy-start = (bf16[1024,4096]{1,0:T(8,128)(2,1)}, bf16[1024,4096]{1,0:T(8,128)(2,1)S(1)}, u32[]{:S(2)}) copy-start(bf16[1024,4096]{1,0:T(8,128)(2,1)S(1)} %get-tuple-element.44.x) | copy-start | bytes 25165828
  39.5 1.4 %copy-start.7 = (f32[1024,512]{1,0:T(8,128)}, f32[1024,512]{1,0:T(8,128)S(1)}, u32[]{:S(2)}) copy-start(f32[1024,512]{1,0:T(8,128)S(1)} %get-tuple-element.37.base_ref) | copy-start | bytes 6291460
  40.9 0.8 %copy-start.9 = (s32[328,512]{1,0:T(8,128)}, s32[328,512]{1,0:T(8,128)S(1)}, u32[]{:S(2)}) copy-start(s32[328,512]{1,0:T(8,128)S(1)} %collective-permute-done.5.refs_0_) | copy-start | bytes 2015236
  41.7 23.7 %collective-permute-start.10 = (bf16[64,4608]{1,0:T(8,128)(2,1)S(1)}, bf16[64,4608]{1,0:T(8,128)(2,1)}, u32[]{:S(2)}, u32[]{:S(2)}) collective-permute-start(bf16[64,4608]{1,0:T(8,128)(2,1)S(1)} %collective-permute-done.3.refs_4_.refs_1_.refs_7_), channel_id=1, source_target_pairs={{8,12},{5,1},{10,14},{7,3},{24,28},{21,17},{26,30},{23,19}} | collective-permute-start | bytes 1769480 | tf_op jit(solution)/shard_map/ppermute | solution.py:503
  43.9 21.4 %collective-permute-start.11 = (bf16[64,4608]{1,0:T(8,128)(2,1)S(1)}, bf16[64,4608]{1,0:T(8,128)(2,1)}, u32[]{:S(2)}, u32[]{:S(2)}) collective-permute-start(bf16[64,4608]{1,0:T(8,128)(2,1)S(1)} %collective-permute-done.4.refs_6_.refs_3_.refs_9_), channel_id=1, source_target_pairs={{9,13},{4,0},{11,15},{6,2},{25,29},{20,16},{27,31},{22,18}} | collective-permute-start | bytes 1769480 | tf_op jit(solution)/shard_map/ppermute | solution.py:503
  45.4 16.8 %collective-permute-start.6 = (s32[168,512]{1,0:T(8,128)}, s32[168,512]{1,0:T(8,128)}, u32[]{:S(2)}, u32[]{:S(2)}) collective-permute-start(s32[168,512]{1,0:T(8,128)} %get-tuple-element.38), channel_id=1, source_target_pairs={{0,2},{2,0},{1,3},{3,1},{4,6},{6,4},{5,7},{7,5},{8,10},{10,8},{9,1... | collective-permute-start | bytes 1032200 | tf_op jit(solution)/shard_map/ppermute | solution.py:495
  47.9 3.4 %copy-start.1 = (bf16[1024,4096]{1,0:T(8,128)(2,1)S(1)}, bf16[1024,4096]{1,0:T(8,128)(2,1)}, u32[]{:S(2)}) copy-start(bf16[1024,4096]{1,0:T(8,128)(2,1)} %copy-done) | copy-start | bytes 25165828
  51.3 1.1 %copy-start.4 = (bf16[64,4608]{1,0:T(8,128)(2,1)S(1)}, bf16[64,4608]{1,0:T(8,128)(2,1)}, u32[]{:S(2)}) copy-start(bf16[64,4608]{1,0:T(8,128)(2,1)} %copy-done.3) | copy-start | bytes 1769476
  52.4 1.1 %copy-start.6 = (bf16[64,4608]{1,0:T(8,128)(2,1)S(1)}, bf16[64,4608]{1,0:T(8,128)(2,1)}, u32[]{:S(2)}) copy-start(bf16[64,4608]{1,0:T(8,128)(2,1)} %copy-done.5) | copy-start | bytes 1769476
  53.4 0.7 copy-start.13
  54.1 7.8 %copy-start.8 = (f32[1024,512]{1,0:T(8,128)S(1)}, f32[1024,512]{1,0:T(8,128)}, u32[]{:S(2)}) copy-start(f32[1024,512]{1,0:T(8,128)} %copy-done.7) | copy-start | bytes 6291460
  54.1 7.8 %copy-start.10 = (s32[328,512]{1,0:T(8,128)S(1)}, s32[328,512]{1,0:T(8,128)}, u32[]{:S(2)}) copy-start(s32[328,512]{1,0:T(8,128)} %copy-done.9) | copy-start | bytes 2015236
  56.8 9.2 %copy-start.2 = (bf16[1024,4096]{1,0:T(8,128)(2,1)S(1)}, bf16[1024,4096]{1,0:T(8,128)(2,1)}, u32[]{:S(2)}) copy-start(bf16[1024,4096]{1,0:T(8,128)(2,1)} %copy-done) | copy-start | bytes 25165828
  56.8 5.0 %collective-permute-start.9 = (f32[2,128,128]{2,1,0:T(8,128)S(1)}, f32[2,128,128]{2,1,0:T(8,128)S(1)}, u32[]{:S(2)}, u32[]{:S(2)}) collective-permute-start(f32[2,128,128]{2,1,0:T(8,128)S(1)} %shard_map.70.refs_2_), channel_id=1, source_target_pairs={{0,2},{2,0},{1,3},{3,1},{4,6},{6,4},{5,7},{7,5},{8,10},{10,8},{9,1... | collective-permute-start | bytes 393224 | tf_op jit(solution)/shard_map/ppermute | solution.py:495
  57.9 8.1 %collective-permute-start.12 = (bf16[64,4608]{1,0:T(8,128)(2,1)S(1)}, bf16[64,4608]{1,0:T(8,128)(2,1)S(1)}, u32[]{:S(2)}, u32[]{:S(2)}) collective-permute-start(bf16[64,4608]{1,0:T(8,128)(2,1)S(1)} %collective-permute-done.3.refs_4_.refs_1_.refs_7_), channel_id=1, source_target_pairs={{0,1},{1,0},{2,3},{3,2},{4,5},{5,4},{6,7},{7,6},{8,9},{9,8},{10,11... | collective-permute-start | bytes 1769480 | tf_op jit(solution)/shard_map/ppermute | solution.py:507
  61.9 4.2 %collective-permute-start.13 = (bf16[64,4608]{1,0:T(8,128)(2,1)S(1)}, bf16[64,4608]{1,0:T(8,128)(2,1)S(1)}, u32[]{:S(2)}, u32[]{:S(2)}) collective-permute-start(bf16[64,4608]{1,0:T(8,128)(2,1)S(1)} %collective-permute-done.4.refs_6_.refs_3_.refs_9_), channel_id=1, source_target_pairs={{0,1},{1,0},{2,3},{3,2},{4,5},{5,4},{6,7},{7,6},{8,9},{9,8},{10,11... | collective-permute-start | bytes 1769480 | tf_op jit(solution)/shard_map/ppermute | solution.py:507
  65.4 2.4 %collective-permute-start.14 = (bf16[64,4608]{1,0:T(8,128)(2,1)}, bf16[64,4608]{1,0:T(8,128)(2,1)S(1)}, u32[]{:S(2)}, u32[]{:S(2)}) collective-permute-start(bf16[64,4608]{1,0:T(8,128)(2,1)} %collective-permute-done.10.refs_5_.refs_11_), channel_id=1, source_target_pairs={{0,1},{1,0},{2,3},{3,2},{4,5},{5,4},{6,7},{7,6},{8,9},{9,8},{10,11... | collective-permute-start | bytes 1769480 | tf_op jit(solution)/shard_map/ppermute | solution.py:507
  65.9 2.7 %collective-permute-start.15 = (bf16[64,4608]{1,0:T(8,128)(2,1)}, bf16[64,4608]{1,0:T(8,128)(2,1)S(1)}, u32[]{:S(2)}, u32[]{:S(2)}) collective-permute-start(bf16[64,4608]{1,0:T(8,128)(2,1)} %collective-permute-done.11.refs_7_.refs_13_), channel_id=1, source_target_pairs={{0,1},{1,0},{2,3},{3,2},{4,5},{5,4},{6,7},{7,6},{8,9},{9,8},{10,11... | collective-permute-start | bytes 1769480 | tf_op jit(solution)/shard_map/ppermute | solution.py:507
  70.9 5.8 %collective-permute-start.16 = (f32[2,128,128]{2,1,0:T(8,128)S(1)}, f32[2,128,128]{2,1,0:T(8,128)S(1)}, u32[]{:S(2)}, u32[]{:S(2)}) collective-permute-start(f32[2,128,128]{2,1,0:T(8,128)S(1)} %shard_map.73.refs_1_), channel_id=1, source_target_pairs={{0,2},{2,0},{1,3},{3,1},{4,6},{6,4},{5,7},{7,5},{8,10},{10,8},{9,1... | collective-permute-start | bytes 393224 | tf_op jit(solution)/shard_map/ppermute | solution.py:495

commit v9 on v7

--- a/solution.py
+++ b/solution.py
@@ -12,7 +12,7 @@
 MOST = 2
 BLOCK = 256
 PIECES = 4
-CHUNKS = ((6, 2), (0, 4), (4, 2))
+CHUNKS = ((6, 2), (0, 3), (3, 3))
 ENTRIES = 8
 MIDDLE = 1.5 * 2.0**23
 
@@ -554,7 +554,7 @@
                 after(table, came), here, tokens, value_weight, message, sent[0], columns, n_adapter, rank
             )
             add_shrink(before)
-            done = sent[1] + shrinks
+            done = sent[1] + [base]
         else:
             if stage == 2:
                 base = add_call(1, after(base, came), sent[1])
@@ -580,9 +580,9 @@
         buffers_of(range(last)),
         rank,
     )
-    came = after(held, value)
+    came = after(held, *shrinks, *sent[2])
     buffers.append([came, swap_cores(came)])
-    add_shrink(shrink_call(last, table, here, kept, [], buffers_of(stages_of(last)), rank))
+    add_shrink(shrink_call(last, table, here, after(kept, value), [], buffers_of(stages_of(last)), rank))
     return late(
         last,
         n_tensor,

time: 67.9 us -> 68.6 us (1.010)
  starting transfers between devices: 16.5 us -> 19 us
  waiting for transfers between devices: 18.4 us -> 17.2 us
    ppermute x3, waiting for transfers between devices: 1.36 us -> 4.77 us  [along_line(): return lax.ppermute(array, ('adapter', 'dp'), up + down)]
    ppermute x3, waiting for transfers between devices: 2.85 us -> 0.01 us  [swap_cores(): return lax.ppermute(array, 'dp', [(0, 1), (1, 0)])]
    ppermute x6, waiting for transfers between devices: 14.2 us -> 12.4 us  [swap_tensor(): return lax.ppermute(array, 'tensor', pairs)]
    ppermute x3, starting transfers between devices: 8.99 us -> 10.5 us  [along_line(): return lax.ppermute(array, ('adapter', 'dp'), up + down)]
    ppermute x6, starting transfers between devices: 7.48 us -> 8.37 us  [swap_tensor(): return lax.ppermute(array, 'tensor', pairs)]
  transfers between devices with their start and end apart: 12 -> 12, of which waited for: 6 -> 5; matrix products, arithmetic and copies ran while one was open for 0% -> 0% of each run, Pallas kernels for 40% -> 39%
where the time goes in v9:
time: 68.6 us; the launch traced here: 68.4 us
  Pallas kernels  31.8 us (46%)
  starting transfers between devices  19 us (28%)
  waiting for transfers between devices  17.2 us (25%)
    ppermute x6, waiting for transfers between devices, swap_tensor(): return lax.ppermute(array, 'tensor', pairs)  12.4 us
    ppermute x3, starting transfers between devices, along_line(): return lax.ppermute(array, ('adapter', 'dp'), up + down)  10.5 us
    pallas_call x2, Pallas kernels, sent_call(): pl.pallas_call(functools.partial(sent_kernel, first, sizes), in_specs=[SM...  10.1 us
    pallas_call x1, Pallas kernels, own_call(): pl.pallas_call(functools.partial(own_kernel, n_adapter, rank), in_specs=[...  9.2 us
    ppermute x6, starting transfers between devices, swap_tensor(): return lax.ppermute(array, 'tensor', pairs)  8.37 us
    ppermute x3, waiting for transfers between devices, along_line(): return lax.ppermute(array, ('adapter', 'dp'), up + down)  4.77 us
    pallas_call x3, Pallas kernels, shrink_call(): pl.pallas_call(functools.partial(shrink_kernel, k, rank, len(before)), in...  4.14 us
    pallas_call x1, Pallas kernels, early(): pl.pallas_call(functools.partial(early_kernel, n_adapter, n_tensor, rank)...  3.15 us
  transfers between devices with their start and end apart: 12, of which 5 were waited for; matrix products, arithmetic and copies ran while one was open for 0% of the time, Pallas kernels for 39%

profile of v9, /device:TPU:16, one launch (start us, length us, event | category | flops | bytes accessed | tf_op | source)
XLA Modules:
  0.0 68.4 jit_solution(7586783327514356363)
XLA Ops:
  0.0 0.1 pad_add_fusion.here
  0.1 0.0 copy-start
  0.1 1.8 %shard_map.65.message.refs_6_ = bf16[128,4608]{1,0:T(8,128)(2,1)S(1)} custom-call(s32[3]{0:T(128)S(1)} %pad_add_fusion.here, bf16[128,4096]{1,0:T(8,128)(2,1)} %bitcast.8, bf16[128,1024]{1,0:T(8,128)(2,1)} %bitcast.9), custom_call_target="tpu_custom_call" | custom-call | bytes 2359296 | tf_op jit(solution)/shard_map/pallas_call | solution.py:85
  1.9 0.0 copy-done
  1.9 3.5 %collective-permute-start = (bf16[128,4608]{1,0:T(8,128)(2,1)S(1)}, bf16[128,4608]{1,0:T(8,128)(2,1)S(1)}, u32[]{:S(2)}, u32[]{:S(2)}) collective-permute-start(bf16[128,4608]{1,0:T(8,128)(2,1)S(1)} %shard_map.65.message.refs_6_), channel_id=1, source_target_pairs={{0,4},{4,8},{8,12},{5,1},{9,5},{13,9},{2,6},{6,10},{10,14},{7,3},{... | collective-permute-start | bytes 3538952 | tf_op jit(solution)/shard_map/ppermute | solution.py:511
  5.4 3.6 %shard_map.66 = s32[168,512]{1,0:T(8,128)S(1)} custom-call(s32[1]{0:T(128)} %bitcast.6.column, bf16[1024,4096]{1,0:T(8,128)(2,1)} %x_ref.5, bf16[4096,1024]{1,0:T(8,128)(2,1)} %w_ref.5), custom_call_target="tpu_custom_call" | custom-call | flops 1073741824 | bytes 6815744 | tf_op jit(solution)/shard_map/pallas_call | solution.py:255
  9.0 1.6 %collective-permute-start.1 = (s32[168,512]{1,0:T(8,128)S(1)}, s32[168,512]{1,0:T(8,128)S(1)}, u32[]{:S(2)}, u32[]{:S(2)}) collective-permute-start(s32[168,512]{1,0:T(8,128)S(1)} %shard_map.66), channel_id=1, source_target_pairs={{0,2},{2,0},{1,3},{3,1},{4,6},{6,4},{5,7},{7,5},{8,10},{10,8},{9,1... | collective-permute-start | bytes 1032200 | tf_op jit(solution)/shard_map/ppermute | solution.py:506
  10.6 1.4 %shard_map.64.table = s32[32]{0:T(128)} custom-call(s32[3]{0:T(128)} %copy-done, s32[1024]{0:T(1024)} %ids.1, s32[8]{0:T(128)} %slots.1), custom_call_target="tpu_custom_call" | custom-call | bytes 4096 | tf_op jit(solution)/shard_map/pallas_call | solution.py:117
  12.0 0.0 copy-start.1
  12.0 0.0 copy-start.2
  12.0 6.6 %shard_map.67 = (s32[248,512]{1,0:T(8,128)S(1)}, s32[248,512]{1,0:T(8,128)S(1)}) custom-call(s32[1]{0:T(128)} %bitcast.6.column, bf16[1024,4096]{1,0:T(8,128)(2,1)} %x_ref.5, bf16[4096,1024]{1,0:T(8,128)(2,1)} %w_ref.5), custom_call_target="tpu_custom_call" | custom-call | flops 3221225472 | bytes 12058624 | tf_op jit(solution)/shard_map/pallas_call | solution.py:255
  18.6 0.0 collective-permute-done.1.refs_0_
  18.6 1.4 %collective-permute-done.refs_0_.refs_1_.refs_7_ = bf16[128,4608]{1,0:T(8,128)(2,1)S(1)} collective-permute-done((bf16[128,4608]{1,0:T(8,128)(2,1)S(1)}, bf16[128,4608]{1,0:T(8,128)(2,1)S(1)}, u32[]{:S(2)}, u32[]{:S(2)}) %collective-permute-start) | collective-permute-done | bytes 1179680 | tf_op jit(solution)/shard_map/ppermute | solution.py:511
  20.0 3.5 %collective-permute-start.2 = (bf16[128,4608]{1,0:T(8,128)(2,1)S(1)}, bf16[128,4608]{1,0:T(8,128)(2,1)S(1)}, u32[]{:S(2)}, u32[]{:S(2)}) collective-permute-start(bf16[128,4608]{1,0:T(8,128)(2,1)S(1)} %collective-permute-done.refs_0_.refs_1_.refs_7_), channel_id=1, source_target_pairs={{4,8},{8,12},{5,1},{9,5},{6,10},{10,14},{7,3},{11,7},{20,24},{24,2... | collective-permute-start | bytes 3538952 | tf_op jit(solution)/shard_map/ppermute | solution.py:511
  23.5 1.6 %collective-permute-start.3 = (s32[248,512]{1,0:T(8,128)S(1)}, s32[248,512]{1,0:T(8,128)S(1)}, u32[]{:S(2)}, u32[]{:S(2)}) collective-permute-start(s32[248,512]{1,0:T(8,128)S(1)} %get-tuple-element.26), channel_id=1, source_target_pairs={{0,2},{2,0},{1,3},{3,1},{4,6},{6,4},{5,7},{7,5},{8,10},{10,8},{9,1... | collective-permute-start | bytes 1523720 | tf_op jit(solution)/shard_map/ppermute | solution.py:506
  25.0 0.0 collective-permute-start.6
  25.0 0.0 copy-done.1
  25.0 0.0 copy-done.2
  25.0 9.2 %shard_map.68 = (f32[1024,512]{1,0:T(8,128)S(1)}, f32[1,128,128]{2,1,0:T(8,128)S(1)}, bf16[3,2,128,4096]{3,2,1,0:T(8,128)(2,1)S(1)}) custom-call(s32[32]{0:T(128)S(1)} %copy-done.2, s32[3]{0:T(128)S(1)} %copy-done.1, bf16[1024,4096]{1,0:T(8,128)(2,1)} %x_ref.5, bf16[4096,1024]{1,0:T(8,128)(2,1)} %w_ref.5, bf16[128,4608]{1,0:T(8,128)(2,1)S(1)} %shard_map.65.message.refs_6_, ...), custom_call_target="tpu_custom_call" | custom-call | flops 4294967296 | bytes 14680064 | tf_op jit(solution)/shard_map/pallas_call | solution.py:333
  34.3 0.4 collective-permute-done.3.refs_0_
  34.7 3.4 %collective-permute-done.2.refs_3_.refs_9_.refs_0_ = bf16[128,4608]{1,0:T(8,128)(2,1)S(1)} collective-permute-done((bf16[128,4608]{1,0:T(8,128)(2,1)S(1)}, bf16[128,4608]{1,0:T(8,128)(2,1)S(1)}, u32[]{:S(2)}, u32[]{:S(2)}) %collective-permute-start.2) | collective-permute-done | bytes 1179680 | tf_op jit(solution)/shard_map/ppermute | solution.py:511
  38.1 0.0 collective-permute-start.7
  38.1 3.5 %collective-permute-start.9 = (bf16[128,4608]{1,0:T(8,128)(2,1)S(1)}, bf16[128,4608]{1,0:T(8,128)(2,1)S(1)}, u32[]{:S(2)}, u32[]{:S(2)}) collective-permute-start(bf16[128,4608]{1,0:T(8,128)(2,1)S(1)} %collective-permute-done.2.refs_3_.refs_9_.refs_0_), channel_id=1, source_target_pairs={{8,12},{5,1},{10,14},{7,3},{24,28},{21,17},{26,30},{23,19}} | collective-permute-start | bytes 3538952 | tf_op jit(solution)/shard_map/ppermute | solution.py:511
  41.6 1.6 %collective-permute-start.4 = (s32[248,512]{1,0:T(8,128)S(1)}, s32[248,512]{1,0:T(8,128)S(1)}, u32[]{:S(2)}, u32[]{:S(2)}) collective-permute-start(s32[248,512]{1,0:T(8,128)S(1)} %get-tuple-element.29), channel_id=1, source_target_pairs={{0,2},{2,0},{1,3},{3,1},{4,6},{6,4},{5,7},{7,5},{8,10},{10,8},{9,1... | collective-permute-start | bytes 1523720 | tf_op jit(solution)/shard_map/ppermute | solution.py:506
  43.2 0.0 collective-permute-done.6.refs_1_.refs_2_.refs_8_
  43.2 1.3 %shard_map.70.refs_0_ = f32[1,128,128]{2,1,0:T(8,128)S(1)} custom-call(s32[32]{0:T(128)S(1)} %copy-done.2, s32[3]{0:T(128)S(1)} %copy-done.1, bf16[3,2,128,4096]{3,2,1,0:T(8,128)(2,1)S(1)} %get-tuple-element.35.kept_ref, bf16[128,4608]{1,0:T(8,128)(2,1)S(1)} %collective-permute-done.refs_0_.refs_1_.refs_7_, ...), custom_call_target="tpu_custom_call" | custom-call | flops 536870912 | bytes 2097152 | tf_op jit(solution)/shard_map/pallas_call | solution.py:363
  44.5 0.0 collective-permute-done.7.refs_4_.refs_10_.refs_1_
  44.5 1.5 %shard_map.71.refs_4_ = f32[2,128,128]{2,1,0:T(8,128)S(1)} custom-call(s32[32]{0:T(128)S(1)} %copy-done.2, s32[3]{0:T(128)S(1)} %copy-done.1, bf16[3,2,128,4096]{3,2,1,0:T(8,128)(2,1)S(1)} %get-tuple-element.35.kept_ref, f32[1,128,128]{2,1,0:T(8,128)S(1)} %shard_map.70.refs_0_, bf16[128,4608]{1,0:T(8,128)(2,1)S(1)} %collective-permute-done.refs_0_.refs_1_.refs_7_, ...), custom_call_target="tpu_custom_call" | custom-call | flops 536870912 | bytes 2097152 | tf_op jit(solution)/shard_map/pallas_call | solution.py:363
  46.0 0.6 collective-permute-start.8
  46.6 1.5 %collective-permute-start.5 = (f32[1,128,128]{2,1,0:T(8,128)S(1)}, f32[1,128,128]{2,1,0:T(8,128)S(1)}, u32[]{:S(2)}, u32[]{:S(2)}) collective-permute-start(f32[1,128,128]{2,1,0:T(8,128)S(1)} %get-tuple-element.30.refs_2_), channel_id=1, source_target_pairs={{0,2},{2,0},{1,3},{3,1},{4,6},{6,4},{5,7},{7,5},{8,10},{10,8},{9,1... | collective-permute-start | bytes 196616 | tf_op jit(solution)/shard_map/ppermute | solution.py:506
  48.1 9.0 %collective-permute-done.5.refs_3_ = f32[1,128,128]{2,1,0:T(8,128)S(1)} collective-permute-done((f32[1,128,128]{2,1,0:T(8,128)S(1)}, f32[1,128,128]{2,1,0:T(8,128)S(1)}, u32[]{:S(2)}, u32[]{:S(2)}) %collective-permute-start.5) | collective-permute-done | bytes 65568 | tf_op jit(solution)/shard_map/ppermute | solution.py:506
  57.1 0.0 collective-permute-done.4.refs_1_
  57.1 0.0 collective-permute-done.9.refs_2_.refs_5_
  57.1 0.0 collective-permute-done.8.refs_5_
  57.1 0.1 collective-permute-start.10
  57.2 0.3 shard_map.69.refs_0_
  57.5 3.1 %shard_map.72 = (bf16[1024,512]{1,0:T(8,128)(2,1)}, f32[2,128,512]{2,1,0:T(8,128)S(1)}) custom-call(s32[32]{0:T(128)S(1)} %copy-done.2, s32[3]{0:T(128)S(1)} %copy-done.1, f32[1024,512]{1,0:T(8,128)S(1)} %shard_map.69.refs_0_, s32[248,512]{1,0:T(8,128)S(1)} %collective-permute-done.4.refs_1_, f32[1,128,128]{2,1,0:T(8,128)S(1)} %get-tuple-element.30.refs_2_, ...), custom_call_target="tpu_custom_call" | custom-call | flops 201326592 | bytes 5242880 | tf_op jit(solution)/shard_map/pallas_call | solution.py:432
  60.6 0.0 collective-permute-done.10.refs_3_.refs_6_
  60.6 1.3 %shard_map.73.refs_1_ = f32[1,128,128]{2,1,0:T(8,128)S(1)} custom-call(s32[32]{0:T(128)S(1)} %copy-done.2, s32[3]{0:T(128)S(1)} %copy-done.1, bf16[3,2,128,4096]{3,2,1,0:T(8,128)(2,1)S(1)} %get-tuple-element.35.kept_ref, bf16[128,4608]{1,0:T(8,128)(2,1)S(1)} %collective-permute-done.2.refs_3_.refs_9_.refs_0_, ...), custom_call_target="tpu_custom_call" | custom-call | flops 536870912 | bytes 2097152 | tf_op jit(solution)/shard_map/pallas_call | solution.py:363
  61.9 1.6 %collective-permute-start.11 = (f32[1,128,128]{2,1,0:T(8,128)S(1)}, f32[1,128,128]{2,1,0:T(8,128)S(1)}, u32[]{:S(2)}, u32[]{:S(2)}) collective-permute-start(f32[1,128,128]{2,1,0:T(8,128)S(1)} %shard_map.73.refs_1_), channel_id=1, source_target_pairs={{0,2},{2,0},{1,3},{3,1},{4,6},{6,4},{5,7},{7,5},{8,10},{10,8},{9,1... | collective-permute-start | bytes 196616 | tf_op jit(solution)/shard_map/ppermute | solution.py:506
  63.5 3.0 %collective-permute-done.11.refs_2_ = f32[1,128,128]{2,1,0:T(8,128)S(1)} collective-permute-done((f32[1,128,128]{2,1,0:T(8,128)S(1)}, f32[1,128,128]{2,1,0:T(8,128)S(1)}, u32[]{:S(2)}, u32[]{:S(2)}) %collective-permute-start.11) | collective-permute-done | bytes 65568 | tf_op jit(solution)/shard_map/ppermute | solution.py:506
  66.5 1.7 %shard_map.74 = bf16[1024,512]{1,0:T(8,128)(2,1)} custom-call(s32[32]{0:T(128)S(1)} %copy-done.2, s32[3]{0:T(128)S(1)} %copy-done.1, f32[2,128,512]{2,1,0:T(8,128)S(1)} %get-tuple-element.33.refs_0_, f32[1,128,128]{2,1,0:T(8,128)S(1)} %shard_map.73.refs_1_, f32[1,128,128]{2,1,0:T(8,128)S(1)} %collective-permute-done.11.refs_2_, ...), custom_call_target="tpu_custom_call", output_to_operand_aliasing={{}: (9, {})} | custom-call | flops 50331648 | bytes 1048576 | tf_op jit(solution)/shard_map/pallas_call | solution.py:471
Async XLA Ops:
  0.1 1.8 %copy-start = (s32[3]{0:T(128)}, s32[3]{0:T(128)S(1)}, u32[]{:S(2)}) copy-start(s32[3]{0:T(128)S(1)} %pad_add_fusion.here) | copy-start | bytes 40
  1.9 18.1 %collective-permute-start = (bf16[128,4608]{1,0:T(8,128)(2,1)S(1)}, bf16[128,4608]{1,0:T(8,128)(2,1)S(1)}, u32[]{:S(2)}, u32[]{:S(2)}) collective-permute-start(bf16[128,4608]{1,0:T(8,128)(2,1)S(1)} %shard_map.65.message.refs_6_), channel_id=1, source_target_pairs={{0,4},{4,8},{8,12},{5,1},{9,5},{13,9},{2,6},{6,10},{10,14},{7,3},{... | collective-permute-start | bytes 3538952 | tf_op jit(solution)/shard_map/ppermute | solution.py:511
  9.0 9.7 %collective-permute-start.1 = (s32[168,512]{1,0:T(8,128)S(1)}, s32[168,512]{1,0:T(8,128)S(1)}, u32[]{:S(2)}, u32[]{:S(2)}) collective-permute-start(s32[168,512]{1,0:T(8,128)S(1)} %shard_map.66), channel_id=1, source_target_pairs={{0,2},{2,0},{1,3},{3,1},{4,6},{6,4},{5,7},{7,5},{8,10},{10,8},{9,1... | collective-permute-start | bytes 1032200 | tf_op jit(solution)/shard_map/ppermute | solution.py:506
  12.0 13.0 %copy-start.1 = (s32[3]{0:T(128)S(1)}, s32[3]{0:T(128)}, u32[]{:S(2)}) copy-start(s32[3]{0:T(128)} %copy-done) | copy-start | bytes 40
  12.0 13.0 %copy-start.2 = (s32[32]{0:T(128)S(1)}, s32[32]{0:T(128)}, u32[]{:S(2)}) copy-start(s32[32]{0:T(128)} %shard_map.64.table) | copy-start | bytes 388
  20.0 18.1 %collective-permute-start.2 = (bf16[128,4608]{1,0:T(8,128)(2,1)S(1)}, bf16[128,4608]{1,0:T(8,128)(2,1)S(1)}, u32[]{:S(2)}, u32[]{:S(2)}) collective-permute-start(bf16[128,4608]{1,0:T(8,128)(2,1)S(1)} %collective-permute-done.refs_0_.refs_1_.refs_7_), channel_id=1, source_target_pairs={{4,8},{8,12},{5,1},{9,5},{6,10},{10,14},{7,3},{11,7},{20,24},{24,2... | collective-permute-start | bytes 3538952 | tf_op jit(solution)/shard_map/ppermute | solution.py:511
  23.5 11.2 %collective-permute-start.3 = (s32[248,512]{1,0:T(8,128)S(1)}, s32[248,512]{1,0:T(8,128)S(1)}, u32[]{:S(2)}, u32[]{:S(2)}) collective-permute-start(s32[248,512]{1,0:T(8,128)S(1)} %get-tuple-element.26), channel_id=1, source_target_pairs={{0,2},{2,0},{1,3},{3,1},{4,6},{6,4},{5,7},{7,5},{8,10},{10,8},{9,1... | collective-permute-start | bytes 1523720 | tf_op jit(solution)/shard_map/ppermute | solution.py:506
  25.0 18.2 %collective-permute-start.6 = (bf16[128,4608]{1,0:T(8,128)(2,1)S(1)}, bf16[128,4608]{1,0:T(8,128)(2,1)S(1)}, u32[]{:S(2)}, u32[]{:S(2)}) collective-permute-start(bf16[128,4608]{1,0:T(8,128)(2,1)S(1)} %collective-permute-done.refs_0_.refs_1_.refs_7_), channel_id=1, source_target_pairs={{0,1},{1,0},{2,3},{3,2},{4,5},{5,4},{6,7},{7,6},{8,9},{9,8},{10,11... | collective-permute-start | bytes 3538952 | tf_op jit(solution)/shard_map/ppermute | solution.py:514
  38.1 6.4 %collective-permute-start.7 = (bf16[128,4608]{1,0:T(8,128)(2,1)S(1)}, bf16[128,4608]{1,0:T(8,128)(2,1)S(1)}, u32[]{:S(2)}, u32[]{:S(2)}) collective-permute-start(bf16[128,4608]{1,0:T(8,128)(2,1)S(1)} %collective-permute-done.2.refs_3_.refs_9_.refs_0_), channel_id=1, source_target_pairs={{0,1},{1,0},{2,3},{3,2},{4,5},{5,4},{6,7},{7,6},{8,9},{9,8},{10,11... | collective-permute-start | bytes 3538952 | tf_op jit(solution)/shard_map/ppermute | solution.py:514
  38.1 19.0 %collective-permute-start.9 = (bf16[128,4608]{1,0:T(8,128)(2,1)S(1)}, bf16[128,4608]{1,0:T(8,128)(2,1)S(1)}, u32[]{:S(2)}, u32[]{:S(2)}) collective-permute-start(bf16[128,4608]{1,0:T(8,128)(2,1)S(1)} %collective-permute-done.2.refs_3_.refs_9_.refs_0_), channel_id=1, source_target_pairs={{8,12},{5,1},{10,14},{7,3},{24,28},{21,17},{26,30},{23,19}} | collective-permute-start | bytes 3538952 | tf_op jit(solution)/shard_map/ppermute | solution.py:511
  41.6 15.4 %collective-permute-start.4 = (s32[248,512]{1,0:T(8,128)S(1)}, s32[248,512]{1,0:T(8,128)S(1)}, u32[]{:S(2)}, u32[]{:S(2)}) collective-permute-start(s32[248,512]{1,0:T(8,128)S(1)} %get-tuple-element.29), channel_id=1, source_target_pairs={{0,2},{2,0},{1,3},{3,1},{4,6},{6,4},{5,7},{7,5},{8,10},{10,8},{9,1... | collective-permute-start | bytes 1523720 | tf_op jit(solution)/shard_map/ppermute | solution.py:506
  46.0 11.1 %collective-permute-start.8 = (f32[2,128,128]{2,1,0:T(8,128)S(1)}, f32[2,128,128]{2,1,0:T(8,128)S(1)}, u32[]{:S(2)}, u32[]{:S(2)}) collective-permute-start(f32[2,128,128]{2,1,0:T(8,128)S(1)} %shard_map.71.refs_4_), channel_id=1, source_target_pairs={{0,2},{2,0},{1,3},{3,1},{4,6},{6,4},{5,7},{7,5},{8,10},{10,8},{9,1... | collective-permute-start | bytes 393224 | tf_op jit(solution)/shard_map/ppermute | solution.py:506
  46.6 10.4 %collective-permute-start.5 = (f32[1,128,128]{2,1,0:T(8,128)S(1)}, f32[1,128,128]{2,1,0:T(8,128)S(1)}, u32[]{:S(2)}, u32[]{:S(2)}) collective-permute-start(f32[1,128,128]{2,1,0:T(8,128)S(1)} %get-tuple-element.30.refs_2_), channel_id=1, source_target_pairs={{0,2},{2,0},{1,3},{3,1},{4,6},{6,4},{5,7},{7,5},{8,10},{10,8},{9,1... | collective-permute-start | bytes 196616 | tf_op jit(solution)/shard_map/ppermute | solution.py:506
  57.1 3.5 %collective-permute-start.10 = (bf16[128,4608]{1,0:T(8,128)(2,1)S(1)}, bf16[128,4608]{1,0:T(8,128)(2,1)S(1)}, u32[]{:S(2)}, u32[]{:S(2)}) collective-permute-start(bf16[128,4608]{1,0:T(8,128)(2,1)S(1)} %collective-permute-done.9.refs_2_.refs_5_), channel_id=1, source_target_pairs={{0,1},{1,0},{2,3},{3,2},{4,5},{5,4},{6,7},{7,6},{8,9},{9,8},{10,11... | collective-permute-start | bytes 3538952 | tf_op jit(solution)/shard_map/ppermute | solution.py:514
  61.9 4.6 %collective-permute-start.11 = (f32[1,128,128]{2,1,0:T(8,128)S(1)}, f32[1,128,128]{2,1,0:T(8,128)S(1)}, u32[]{:S(2)}, u32[]{:S(2)}) collective-permute-start(f32[1,128,128]{2,1,0:T(8,128)S(1)} %shard_map.73.refs_1_), channel_id=1, source_target_pairs={{0,2},{2,0},{1,3},{3,1},{4,6},{6,4},{5,7},{7,5},{8,10},{10,8},{9,1... | collective-permute-start | bytes 196616 | tf_op jit(solution)/shard_map/ppermute | solution.py:506

commit v10 on v9

--- a/solution.py
+++ b/solution.py
@@ -12,7 +12,7 @@
 MOST = 2
 BLOCK = 256
 PIECES = 4
-CHUNKS = ((6, 2), (0, 3), (3, 3))
+CHUNKS = ((6, 2), (0, 6))
 ENTRIES = 8
 MIDDLE = 1.5 * 2.0**23
 
@@ -42,12 +42,13 @@
     return order
 
 
-def buffer_owners(here, stages):
-    owners = []
+def buffer_tags(here, stages, per_device):
+    tags = []
     for stage in stages:
-        toward = jnp.where(here[1] == 0, -stage, stage)
-        owners += [here[0] + toward, here[0] - toward] if stage > 0 else [here[0]]
-    return owners
+        for i in range(per_device):
+            toward = jnp.where(here[1] == 0, -stage, stage)
+            tags += [(here[0] + toward, i), (here[0] - toward, i)] if stage > 0 else [(here[0], i)]
+    return tags
 
 
 def segment_of(table, k, j):
@@ -56,38 +57,36 @@
     return start, seg >= 0, table[k * ENTRIES + 2 + 2 * j]
 
 
-def message_kernel(here, down_ref, up_ref, o_ref, sems):
+def message_kernel(here, down_ref, up_ref, *refs):
+    outs, sems = refs[:-1], refs[-1]
+    rank = outs[0].shape[0]
     width = down_ref.shape[1]
-    columns = o_ref.shape[1] - width
+    columns = outs[0].shape[1] - width
     start = pl.multiple_of(here[2] * columns, columns)
-    rows = down_ref.shape[0] // PIECES
-    copies = [
-        pltpu.make_async_copy(
-            down_ref.at[pl.ds(p * rows, rows), :],
-            o_ref.at[pl.ds(p * rows, rows), pl.ds(0, width)],
-            sems.at[p],
-        )
-        for p in range(PIECES)
-    ]
-    copies.append(
-        pltpu.make_async_copy(
-            up_ref.at[:, pl.ds(start, columns)], o_ref.at[:, pl.ds(width, columns)], sems.at[PIECES]
-        )
-    )
+    copies = []
+    for i, out in enumerate(outs):
+        rows = pl.ds(i * rank, rank)
+        copies += [
+            pltpu.make_async_copy(down_ref.at[rows, :], out.at[:, pl.ds(0, width)], sems.at[0, i]),
+            pltpu.make_async_copy(
+                up_ref.at[rows, pl.ds(start, columns)], out.at[:, pl.ds(width, columns)], sems.at[1, i]
+            ),
+        ]
     for copy in copies:
         copy.start()
     for copy in copies:
         copy.wait()
 
 
-def message_call(here, down, up, columns):
+def message_call(here, down, up, columns, per_device):
     rows, width = down.shape
+    shape = jax.ShapeDtypeStruct((rows // per_device, width + columns), jnp.bfloat16)
     return pl.pallas_call(
         message_kernel,
         in_specs=[SMEM, HBM, HBM],
-        out_specs=VMEM,
-        out_shape=jax.ShapeDtypeStruct((rows, width + columns), jnp.bfloat16),
-        scratch_shapes=[pltpu.SemaphoreType.DMA((PIECES + 1,))],
+        out_specs=[VMEM] * per_device,
+        out_shape=[shape] * per_device,
+        scratch_shapes=[pltpu.SemaphoreType.DMA((2, per_device))],
         compiler_params=params(8),
         cost_estimate=cost(0, 4 * rows * (width + columns)),
     )(here, down, up)
@@ -278,22 +277,23 @@
         out_specs=VMEM,
         out_shape=jax.ShapeDtypeStruct(base.shape, base.dtype),
         compiler_params=params(8),
-        cost_estimate=cost(0, 4 * base.size),
+        cost_estimate=cost(20000 * base.size, 12 * base.size),
     )(base, *coded)
 
 
-def shrink_into(o_ref, i, table, k, rows_of, buffers, owners, rank):
-    for buffer, whose in zip(buffers, owners):
-
-        @pl.when(whose == table[k * ENTRIES])
-        def _(buffer=buffer):
-            for j in range(MOST):
-                _, _, within = segment_of(table, k, j)
+def shrink_into(o_ref, at, table, k, rows_of, buffers, tags, rank):
+    for j in range(MOST):
+        _, _, within = segment_of(table, k, j)
+        for buffer, (whose, i) in zip(buffers, tags):
+
+            @pl.when((whose == table[k * ENTRIES]) & (within == i))
+            def _(j=j, buffer=buffer):
                 rows = rows_of(j)
-                width = rows.shape[1]
-                factor = buffer[pl.ds(pl.multiple_of(within * rank, rank), rank), :width]
-                o_ref[i, :, j * rank : (j + 1) * rank] = lax.dot_general(
-                    rows, factor, (((1,), (1,)), ((), ())), preferred_element_type=jnp.float32
+                o_ref[at, :, j * rank : (j + 1) * rank] = lax.dot_general(
+                    rows,
+                    buffer[:, : rows.shape[1]],
+                    (((1,), (1,)), ((), ())),
+                    preferred_element_type=jnp.float32,
                 )
 
 
@@ -301,7 +301,8 @@
     return range((k + 1) // 2, k + 1)
 
 
-def own_kernel(n_adapter, rank, table, here, x_ref, w_ref, message, *refs):
+def own_kernel(n_adapter, per_device, rank, table, here, x_ref, w_ref, *refs):
+    messages, refs = refs[:per_device], refs[per_device:]
     coded_refs, (o_ref, s_ref, kept_ref, x, w, sems, kept_sems) = refs[:-7], refs[-7:]
     work = load_base(0, x.shape[0] // SEGMENT_ROWS, here[2], x_ref, w_ref, x, w, sems)
     keeps = []
@@ -322,17 +323,18 @@
         start, _, _ = segment_of(table, 0, j)
         return x[pl.ds(start, SEGMENT_ROWS), :]
 
-    shrink_into(s_ref, 0, table, 0, rows_of, [message], [here[0]], rank)
+    shrink_into(s_ref, 0, table, 0, rows_of, messages, buffer_tags(here, [0], per_device), rank)
     for copy in keeps:
         copy.wait()
 
 
-def own_call(table, here, tokens, weight, message, coded, columns, n_adapter, rank):
+def own_call(table, here, tokens, weight, messages, coded, columns, n_adapter):
     rows, width = tokens.shape
     segments = rows // SEGMENT_ROWS
-    return pl.pallas_call(
-        functools.partial(own_kernel, n_adapter, rank),
-        in_specs=[SMEM, SMEM, HBM, HBM] + [VMEM] * (1 + len(coded)),
+    per_device, rank = len(messages), messages[0].shape[0]
+    return pl.pallas_call(
+        functools.partial(own_kernel, n_adapter, per_device, rank),
+        in_specs=[SMEM, SMEM, HBM, HBM] + [VMEM] * (per_device + len(coded)),
         out_specs=[VMEM] * 3,
         out_shape=[
             jax.ShapeDtypeStruct((rows, columns), jnp.float32),
@@ -345,40 +347,38 @@
         cost_estimate=cost(
             2 * rows * width * columns, 2 * rows * width + 2 * width * columns + 4 * rows * columns
         ),
-    )(table, here, tokens, weight, message, *coded)
-
-
-def shrink_kernel(k, rank, n_before, table, here, kept_ref, *refs):
-    buffers, o_ref = refs[n_before:-1], refs[-1]
-    for r in refs[:n_before]:
-        o_ref[:1] = r[...]
-    rows_of = lambda j: kept_ref[k - 1, j]
-    owners = buffer_owners(here, stages_of(k))
-    shrink_into(o_ref, n_before, table, k, rows_of, buffers, owners, rank)
-
-
-def shrink_call(k, table, here, kept, before, buffers, rank):
+    )(table, here, tokens, weight, *messages, *coded)
+
+
+def shrink_kernel(k, per_device, rank, at, table, here, kept_ref, *refs):
+    buffers, o_ref = refs[1 if at else 0 : -1], refs[-1]
+    if at:
+        o_ref[:at] = refs[0][...]
+    tags = buffer_tags(here, stages_of(k), per_device)
+    shrink_into(o_ref, at, table, k, lambda j: kept_ref[k - 1, j], buffers, tags, rank)
+
+
+def shrink_call(k, table, here, kept, before, buffers, per_device, rank):
     width = kept.shape[3]
-    n = 1 + len(before)
-    return pl.pallas_call(
-        functools.partial(shrink_kernel, k, rank, len(before)),
-        in_specs=[SMEM, SMEM, VMEM] + [VMEM] * (n - 1 + len(buffers)),
+    at = sum(b.shape[0] for b in before)
+    return pl.pallas_call(
+        functools.partial(shrink_kernel, k, per_device, rank, at),
+        in_specs=[SMEM, SMEM, VMEM] + [VMEM] * (len(before) + len(buffers)),
         out_specs=VMEM,
-        out_shape=jax.ShapeDtypeStruct((n, SEGMENT_ROWS, MOST * rank), jnp.float32),
+        out_shape=jax.ShapeDtypeStruct((at + 1, SEGMENT_ROWS, MOST * rank), jnp.float32),
         compiler_params=params(16),
         cost_estimate=cost(MOST * 2 * SEGMENT_ROWS * width * 256, 4 * SEGMENT_ROWS * width),
     )(table, here, kept, *before, *buffers)
 
 
-def fetch_up(up, at, table, k, j, buffers, owners, rank):
+def fetch_up(up, at, table, k, j, buffers, tags, rank):
     columns = up.shape[2]
     _, _, within = segment_of(table, k, j)
-    for buffer, whose in zip(buffers, owners):
-
-        @pl.when(whose == table[k * ENTRIES])
+    for buffer, (whose, i) in zip(buffers, tags):
+
+        @pl.when((whose == table[k * ENTRIES]) & (within == i))
         def _(buffer=buffer):
-            first = buffer.shape[1] - columns
-            factor = buffer[pl.ds(pl.multiple_of(within * rank, rank), rank), first:]
+            factor = buffer[:, buffer.shape[1] - columns :]
             up[at, :rank, :] = factor
             up[at, rank:, :] = factor
 
@@ -392,29 +392,26 @@
     return jnp.dot(terms, factor, preferred_element_type=jnp.float32)
 
 
-def early_kernel(n_adapter, n_tensor, rank, table, here, *refs):
-    n_coded, n_buffers = n_tensor - 1, 2 * n_adapter - 3
-    base_ref, coded_refs, refs = refs[0], refs[1 : 1 + n_coded], refs[1 + n_coded :]
-    shrinks, refs = refs[: -4 - n_buffers], refs[-4 - n_buffers :]
-    buffers, (o_ref, rest_ref, up, total) = refs[:-4], refs[-4:]
+def early_kernel(n_adapter, n_tensor, per_device, rank, n_shrinks, table, here, *refs):
+    base_ref, refs = refs[0], refs[1:]
+    shrinks, refs = refs[:n_shrinks], refs[n_shrinks:]
+    buffers, (o_ref, rest_ref, up) = refs[:-3], refs[-3:]
+    tags = buffer_tags(here, range(n_adapter - 1), per_device)
     for k in range(n_adapter - 1):
-        at = 0 if k == 0 else 2 * stages_of(k)[0] - 1
-        to = 2 * k + 1
-        owners = buffer_owners(here, stages_of(k))
+        at = per_device * (0 if k == 0 else 2 * stages_of(k)[0] - 1)
+        to = per_device * (2 * k + 1)
         for j in range(MOST):
-            fetch_up(up, k * MOST + j, table, k, j, buffers[at:to], owners, rank)
+            fetch_up(up, k * MOST + j, table, k, j, buffers[at:to], tags[at:to], rank)
     shares = []
-    for call in range(len(shrinks) // n_tensor):
-        share = shrinks[call * n_tensor][...]
-        for i in range(1, n_tensor):
-            share = share + shrinks[call * n_tensor + i][...]
+    for call in range(0, n_shrinks, n_tensor):
+        share = shrinks[call][...]
+        for r in shrinks[call + 1 : call + n_tensor]:
+            share = share + r[...]
         shares += [share[i] for i in range(share.shape[0])]
-    total[...] = base_ref[...]
-    add_decoded(total, len(CHUNKS) - 1, coded_refs)
     for k in range(n_adapter):
         for j in range(MOST):
             start, used, _ = segment_of(table, k, j)
-            value = total[pl.ds(start, SEGMENT_ROWS), :]
+            value = base_ref[pl.ds(start, SEGMENT_ROWS), :]
             if k == n_adapter - 1:
                 rest_ref[j] = value
                 continue
@@ -427,11 +424,11 @@
                 )
 
 
-def early(n_adapter, n_tensor, table, here, base, coded, shrinks, buffers, rank):
+def early(n_adapter, n_tensor, table, here, base, shrinks, buffers, per_device, rank):
     rows, columns = base.shape
     return pl.pallas_call(
-        functools.partial(early_kernel, n_adapter, n_tensor, rank),
-        in_specs=[SMEM] * 2 + [VMEM] * (1 + len(coded) + len(shrinks) + len(buffers)),
+        functools.partial(early_kernel, n_adapter, n_tensor, per_device, rank, len(shrinks)),
+        in_specs=[SMEM] * 2 + [VMEM] * (1 + len(shrinks) + len(buffers)),
         out_specs=[VMEM, VMEM],
         out_shape=[
             jax.ShapeDtypeStruct((rows, columns), jnp.bfloat16),
@@ -439,23 +436,22 @@
         ],
         scratch_shapes=[
             pltpu.VMEM(((n_adapter - 1) * MOST, 2 * rank, columns), jnp.bfloat16),
-            pltpu.VMEM((rows, columns), jnp.float32),
         ],
         compiler_params=params(16),
         cost_estimate=cost(6 * rows * rank * columns, (4 * n_tensor + 2) * rows * columns),
-    )(table, here, base, *coded, *shrinks, *buffers)
-
-
-def late_kernel(k, n_tensor, rank, table, here, *refs):
+    )(table, here, base, *shrinks, *buffers)
+
+
+def late_kernel(k, n_tensor, per_device, rank, table, here, *refs):
     rest_ref, shrinks, refs = refs[0], refs[1 : 1 + n_tensor], refs[1 + n_tensor :]
     buffers, (_, o_ref, up, out, sems) = refs[:-5], refs[-5:]
-    owners = buffer_owners(here, stages_of(k))
+    tags = buffer_tags(here, stages_of(k), per_device)
     share = shrinks[0][0]
     for r in shrinks[1:]:
         share = share + r[0]
     stores = []
     for j in range(MOST):
-        fetch_up(up, j, table, k, j, buffers, owners, rank)
+        fetch_up(up, j, table, k, j, buffers, tags, rank)
         start, used, _ = segment_of(table, k, j)
         lora = up_product(share, j, up[j], rank)
         out[j] = (rest_ref[j] + adapter_scale * lora).astype(jnp.bfloat16)
@@ -466,10 +462,10 @@
         pl.when(used)(store.wait)
 
 
-def late(k, n_tensor, table, here, rest, shrinks, buffers, value, rank):
+def late(k, n_tensor, table, here, rest, shrinks, buffers, value, per_device, rank):
     rows, columns = value.shape
     return pl.pallas_call(
-        functools.partial(late_kernel, k, n_tensor, rank),
+        functools.partial(late_kernel, k, n_tensor, per_device, rank),
         in_specs=[SMEM] * 2 + [VMEM] * (1 + len(shrinks) + len(buffers)) + [ANY],
         out_specs=ANY,
         out_shape=jax.ShapeDtypeStruct((rows, columns), jnp.bfloat16),
@@ -506,8 +502,8 @@
         return lax.ppermute(array, "tensor", pairs)
 
     def along_line(array, stage):
-        up = [(2 * i, 2 * (i + 1)) for i in range(stage - 1, n_adapter - 1)]
-        down = [(2 * i + 1, 2 * (i - 1) + 1) for i in range(1, n_adapter - stage + 1)]
+        up = [(2 * z, 2 * (z + 1)) for z in range(stage - 1, n_adapter - 1)]
+        down = [(2 * z + 1, 2 * (z - 1) + 1) for z in range(1, n_adapter - stage + 1)]
         return lax.ppermute(array, ("adapter", "dp"), up + down)
 
     def swap_cores(array):
@@ -518,56 +514,63 @@
     tokens, value_weight, down, up = (
         pltpu.with_memory_space_constraint(a, pltpu.HBM) for a in (tokens, value_weight, down, up)
     )
-    message = message_call(here, down, up, columns)
+    messages = message_call(here, down, up, columns, per_device)
     table = table_call(here, row_adapter_index, adapter_slot_of, n_adapter, per_device)
-
-    buffers, shrinks = [[message]], []
+    buffers, shrinks = [[[m] for m in messages]], []
 
     def buffers_of(stages):
-        return [b for stage in stages for b in buffers[stage]]
+        return [b for stage in stages for pair in buffers[stage] for b in pair]
 
     def add_shrink(mine):
         shrinks.extend([mine] + [swap_tensor(mine, step) for step in range(1, n_tensor)])
 
-    held = along_line(message, 1)
+    def shrink(k, kept, before=()):
+        mine = buffers_of(stages_of(k))
+        return shrink_call(k, table, here, kept, list(before), mine, per_device, rank)
+
     others = range(1, n_tensor)
 
-    def sent_for(step, chunks):
+    def sent_for(step, chunks, *ahead):
         sizes = [number for _, number in chunks]
-        target = (me_t + step) % n_tensor
+        target = after((me_t + step) % n_tensor, *ahead)
         return sent_call(tokens, value_weight, target, columns, chunks[0][0], sizes)
 
-    parts = [[sent_for(step, CHUNKS[:1])[0] for step in others]]
-    rest_parts = [sent_for(step, CHUNKS[1:]) for step in others]
-    parts += [[p[i] for p in rest_parts] for i in range(len(CHUNKS) - 1)]
-    sent = [[swap_tensor(p, step) for step, p in zip(others, parts[0])]]
+    def send(parts, *ahead):
+        return [swap_tensor(after(p, *ahead), step) for step, p in zip(others, parts)]
+
     last = n_adapter - 1
-    done = [table] + [p for group in parts for p in group] + sent[0]
-    before = None
+    held = [along_line(m, 1) for m in messages]
+    part_a = [sent_for(step, CHUNKS[:1])[0] for step in others]
+    sent = [send(part_a)]
+    part_b = [sent_for(step, CHUNKS[1:], held[0], *part_a)[0] for step in others]
+    sent.append(send(part_b))
     for stage in range(1, last):
-        came = after(held, *done)
-        held = along_line(came, stage + 1)
-        if stage < len(CHUNKS):
-            sent.append([swap_tensor(after(p, came), step) for step, p in zip(others, parts[stage])])
+        came = held
+        if stage == 1:
+            came = [after(held[0], *part_a)] + [after(h, *part_b, *sent[0]) for h in held[1:]]
+        if stage == 2:
+            came = held[:1] + [after(h, base) for h in held[1:]]
+        held = [along_line(c, stage + 1) for c in came]
+        swapped = [swap_cores(after(c, base) if stage == 2 else c) for c in came]
+        buffers.append([list(pair) for pair in zip(came, swapped)])
         if stage == 1:
             base, before, kept = own_call(
-                after(table, came), here, tokens, value_weight, message, sent[0], columns, n_adapter, rank
+                after(table, held[0]),
+                here,
+                tokens,
+                value_weight,
+                messages,
+                sent[0],
+                columns,
+                n_adapter,
             )
-            add_shrink(before)
-            done = sent[1] + [base]
         else:
+            ready = kept
             if stage == 2:
-                base = add_call(1, after(base, came), sent[1])
-            before = shrink_call(
-                stage - 1, table, here, after(kept, came), [], buffers_of(stages_of(stage - 1)), rank
-            )
-            if stage < last - 1:
-                add_shrink(before)
-            done = []
-        buffers.append([came, swap_cores(came)])
-    merged = shrink_call(
-        last - 1, table, here, kept, [before], buffers_of(stages_of(last - 1)), rank
-    )
+                base = add_call(1, after(base, held[0], *came), sent[1])
+                ready = after(kept, base, *held[1:])
+            before = shrink(stage - 1, ready, [before])
+    merged = shrink(last - 1, kept, [before])
     add_shrink(merged)
     value, remaining = early(
         n_adapter,
@@ -575,14 +578,13 @@
         table,
         here,
         base,
-        sent[2],
         shrinks,
         buffers_of(range(last)),
+        per_device,
         rank,
     )
-    came = after(held, *shrinks, *sent[2])
-    buffers.append([came, swap_cores(came)])
-    add_shrink(shrink_call(last, table, here, after(kept, value), [], buffers_of(stages_of(last)), rank))
+    buffers.append([[h, swap_cores(h)] for h in held])
+    add_shrink(shrink(last, kept))
     return late(
         last,
         n_tensor,
@@ -592,6 +594,7 @@
         shrinks[-n_tensor:],
         buffers_of(stages_of(last)),
         value,
+        per_device,
         rank,
     )
 

time: 68.6 us -> 74.6 us (1.087)
  the two profiles are of different devices: /device:TPU:16 before, /device:TPU:0 now
where the time goes in v10:
time: 74.6 us; the launch traced here: 74.3 us
  Pallas kernels  35.1 us (47%)
  starting transfers between devices  25.6 us (34%)
  waiting for transfers between devices  10.9 us (15%)
  local copies, waits for them, and re-layouts  2.29 us (3%)
    ppermute x6, starting transfers between devices, along_line(): return lax.ppermute(array, ('adapter', 'dp'), up + down)  11.2 us
    pallas_call x2, Pallas kernels, sent_call(): pl.pallas_call(functools.partial(sent_kernel, first, sizes), in_specs=[SM...  11.1 us
    ppermute x4, waiting for transfers between devices, swap_tensor(): return lax.ppermute(array, 'tensor', pairs)  10.6 us
    pallas_call x1, Pallas kernels, own_call(): pl.pallas_call(functools.partial(own_kernel, n_adapter, per_device, rank)...  9.35 us
    ppermute x6, starting transfers between devices, swap_cores(): return lax.ppermute(array, 'dp', [(0, 1), (1, 0)])  8.92 us
    ppermute x4, starting transfers between devices, swap_tensor(): return lax.ppermute(array, 'tensor', pairs)  5.43 us
    pallas_call x3, Pallas kernels, shrink_call(): pl.pallas_call(functools.partial(shrink_kernel, k, per_device, rank, at),...  4.81 us
    pallas_call x1, Pallas kernels, early(): pl.pallas_call(functools.partial(early_kernel, n_adapter, n_tensor, per_d...  3.16 us
  transfers between devices with their start and end apart: 16, of which 4 were waited for; matrix products, arithmetic and copies ran while one was open for 0% of the time, Pallas kernels for 42%

profile of v10, /device:TPU:0, one launch (start us, length us, event | category | flops | bytes accessed | tf_op | source)
XLA Modules:
  0.0 74.3 jit_solution(7571826743878969381)
XLA Ops:
  0.0 0.1 pad_add_fusion.here
  0.1 0.0 copy-start.2
  0.1 1.8 %shard_map.65 = (bf16[64,4608]{1,0:T(8,128)(2,1)S(1)}, bf16[64,4608]{1,0:T(8,128)(2,1)S(1)}) custom-call(s32[3]{0:T(128)S(1)} %pad_add_fusion.here, bf16[128,4096]{1,0:T(8,128)(2,1)} %bitcast.9, bf16[128,1024]{1,0:T(8,128)(2,1)} %bitcast.10), custom_call_target="tpu_custom_call" | custom-call | bytes 2359296 | tf_op jit(solution)/shard_map/pallas_call | solution.py:84
  1.9 5.0 %collective-permute-start = (bf16[64,4608]{1,0:T(8,128)(2,1)S(1)}, bf16[64,4608]{1,0:T(8,128)(2,1)S(1)}, u32[]{:S(2)}, u32[]{:S(2)}) collective-permute-start(bf16[64,4608]{1,0:T(8,128)(2,1)S(1)} %get-tuple-element.21.refs_0_.refs_3_), channel_id=1, source_target_pairs={{0,4},{4,8},{8,12},{5,1},{9,5},{13,9},{2,6},{6,10},{10,14},{7,3},{... | collective-permute-start | bytes 1769480 | tf_op jit(solution)/shard_map/ppermute | solution.py:507
  6.9 3.5 %collective-permute-start.4 = (bf16[64,4608]{1,0:T(8,128)(2,1)S(1)}, bf16[64,4608]{1,0:T(8,128)(2,1)S(1)}, u32[]{:S(2)}, u32[]{:S(2)}) collective-permute-start(bf16[64,4608]{1,0:T(8,128)(2,1)S(1)} %get-tuple-element.24.refs_1_.refs_4_), channel_id=1, source_target_pairs={{0,4},{4,8},{8,12},{5,1},{9,5},{13,9},{2,6},{6,10},{10,14},{7,3},{... | collective-permute-start | bytes 1769480 | tf_op jit(solution)/shard_map/ppermute | solution.py:507
  10.4 3.6 %shard_map.66 = s32[168,512]{1,0:T(8,128)S(1)} custom-call(s32[1]{0:T(128)} %bitcast.6.column, bf16[1024,4096]{1,0:T(8,128)(2,1)} %x_ref.5, bf16[4096,1024]{1,0:T(8,128)(2,1)} %w_ref.5), custom_call_target="tpu_custom_call" | custom-call | flops 1073741824 | bytes 6815744 | tf_op jit(solution)/shard_map/pallas_call | solution.py:254
  13.9 0.0 copy-done.2
  13.9 0.3 collective-permute-done.refs_1_.refs_5_
  14.2 0.7 collective-permute-start.1
  14.9 1.6 %collective-permute-start.2 = (s32[168,512]{1,0:T(8,128)S(1)}, s32[168,512]{1,0:T(8,128)S(1)}, u32[]{:S(2)}, u32[]{:S(2)}) collective-permute-start(s32[168,512]{1,0:T(8,128)S(1)} %shard_map.66), channel_id=1, source_target_pairs={{0,2},{2,0},{1,3},{3,1},{4,6},{6,4},{5,7},{7,5},{8,10},{10,8},{9,1... | collective-permute-start | bytes 1032200 | tf_op jit(solution)/shard_map/ppermute | solution.py:502
  16.5 0.0 copy-start.3
  16.5 7.5 %shard_map.68 = s32[488,512]{1,0:T(8,128)} custom-call(s32[1]{0:T(128)} %bitcast.7.column, bf16[1024,4096]{1,0:T(8,128)(2,1)} %x_ref.5, bf16[4096,1024]{1,0:T(8,128)(2,1)} %w_ref.5), custom_call_target="tpu_custom_call" | custom-call | flops 3221225472 | bytes 12058624 | tf_op jit(solution)/shard_map/pallas_call | solution.py:254
  24.0 1.0 %collective-permute-done.2.refs_2_ = s32[168,512]{1,0:T(8,128)S(1)} collective-permute-done((s32[168,512]{1,0:T(8,128)S(1)}, s32[168,512]{1,0:T(8,128)S(1)}, u32[]{:S(2)}, u32[]{:S(2)}) %collective-permute-start.2) | collective-permute-done | bytes 344096 | tf_op jit(solution)/shard_map/ppermute | solution.py:502
  25.0 0.0 copy-start
  25.0 0.7 copy-done
  25.7 0.0 collective-permute-done.4.refs_3_.refs_7_
  25.7 0.7 collective-permute-start.5
  26.4 1.7 %collective-permute-start.6 = (s32[488,512]{1,0:T(8,128)}, s32[488,512]{1,0:T(8,128)}, u32[]{:S(2)}, u32[]{:S(2)}) collective-permute-start(s32[488,512]{1,0:T(8,128)} %shard_map.68), channel_id=1, source_target_pairs={{0,2},{2,0},{1,3},{3,1},{4,6},{6,4},{5,7},{7,5},{8,10},{10,8},{9,1... | collective-permute-start | bytes 2998280 | tf_op jit(solution)/shard_map/ppermute | solution.py:502
  28.1 1.4 %shard_map.64.table = s32[32]{0:T(128)} custom-call(s32[3]{0:T(128)} %copy-done.2, s32[1024]{0:T(1024)} %ids.1, s32[8]{0:T(128)} %slots.1), custom_call_target="tpu_custom_call" | custom-call | bytes 4096 | tf_op jit(solution)/shard_map/pallas_call | solution.py:116
  29.5 0.1 collective-permute-start.8
  29.6 0.0 collective-permute-done.1.refs_5_.refs_9_.refs_0_.refs_3_
  29.6 0.7 collective-permute-start.3
  30.3 0.0 copy-done.3
  30.3 0.0 copy-start.1
  30.4 1.0 %copy-done.1 = s32[168,512]{1,0:T(8,128)S(1)} copy-done((s32[168,512]{1,0:T(8,128)S(1)}, s32[168,512]{1,0:T(8,128)}, u32[]{:S(2)}) %copy-start.1) | copy-done | bytes 344088
  31.3 0.0 copy-start.4
  31.3 0.6 copy-done.4
  31.9 9.4 %shard_map.67 = (f32[1024,512]{1,0:T(8,128)S(1)}, f32[1,128,128]{2,1,0:T(8,128)S(1)}, bf16[3,2,128,4096]{3,2,1,0:T(8,128)(2,1)S(1)}) custom-call(s32[32]{0:T(128)S(1)} %copy-done.4, s32[3]{0:T(128)S(1)} %copy-done.3, bf16[1024,4096]{1,0:T(8,128)(2,1)} %x_ref.5, bf16[4096,1024]{1,0:T(8,128)(2,1)} %w_ref.5, ...), custom_call_target="tpu_custom_call" | custom-call | flops 4294967296 | bytes 14680064 | tf_op jit(solution)/shard_map/pallas_call | solution.py:335
  41.3 0.0 collective-permute-done.5.refs_7_.refs_11_.refs_2_.refs_5_
  41.3 0.7 collective-permute-start.7
  42.0 1.7 %collective-permute-start.9 = (bf16[64,4608]{1,0:T(8,128)(2,1)S(1)}, bf16[64,4608]{1,0:T(8,128)(2,1)S(1)}, u32[]{:S(2)}, u32[]{:S(2)}) collective-permute-start(bf16[64,4608]{1,0:T(8,128)(2,1)S(1)} %collective-permute-done.4.refs_3_.refs_7_), channel_id=1, source_target_pairs={{0,1},{1,0},{2,3},{3,2},{4,5},{5,4},{6,7},{7,6},{8,9},{9,8},{10,11... | collective-permute-start | bytes 1769480 | tf_op jit(solution)/shard_map/ppermute | solution.py:510
  43.7 0.0 collective-permute-done.3.refs_4_.refs_7_
  43.7 1.1 %collective-permute-start.10 = (bf16[64,4608]{1,0:T(8,128)(2,1)S(1)}, bf16[64,4608]{1,0:T(8,128)(2,1)S(1)}, u32[]{:S(2)}, u32[]{:S(2)}) collective-permute-start(bf16[64,4608]{1,0:T(8,128)(2,1)S(1)} %collective-permute-done.1.refs_5_.refs_9_.refs_0_.refs_3_), channel_id=1, source_target_pairs={{0,1},{1,0},{2,3},{3,2},{4,5},{5,4},{6,7},{7,6},{8,9},{9,8},{10,11... | collective-permute-start | bytes 1769480 | tf_op jit(solution)/shard_map/ppermute | solution.py:510
  44.8 0.0 collective-permute-done.8.refs_2_.refs_6_
  44.8 0.0 collective-permute-start.11
  44.8 5.8 %collective-permute-done.6.refs_0_ = s32[488,512]{1,0:T(8,128)} collective-permute-done((s32[488,512]{1,0:T(8,128)}, s32[488,512]{1,0:T(8,128)}, u32[]{:S(2)}, u32[]{:S(2)}) %collective-permute-start.6) | collective-permute-done | bytes 999456 | tf_op jit(solution)/shard_map/ppermute | solution.py:502
  50.6 0.0 collective-permute-start.13
  50.7 0.0 collective-permute-done.7.refs_6_.refs_9_
  50.7 6.0 %collective-permute-start.14 = (bf16[64,4608]{1,0:T(8,128)(2,1)S(1)}, bf16[64,4608]{1,0:T(8,128)(2,1)S(1)}, u32[]{:S(2)}, u32[]{:S(2)}) collective-permute-start(bf16[64,4608]{1,0:T(8,128)(2,1)S(1)} %collective-permute-done.7.refs_6_.refs_9_), channel_id=1, source_target_pairs={{0,1},{1,0},{2,3},{3,2},{4,5},{5,4},{6,7},{7,6},{8,9},{9,8},{10,11... | collective-permute-start | bytes 1769480 | tf_op jit(solution)/shard_map/ppermute | solution.py:510
  56.7 1.7 %shard_map.69.refs_0_ = f32[1024,512]{1,0:T(8,128)S(1)} custom-call(f32[1024,512]{1,0:T(8,128)S(1)} %get-tuple-element.29.base_ref, s32[488,512]{1,0:T(8,128)} %collective-permute-done.6.refs_0_), custom_call_target="tpu_custom_call" | custom-call | flops 10485760000 | bytes 6291456 | tf_op jit(solution)/shard_map/pallas_call | solution.py:274
  58.3 0.0 collective-permute-done.9.refs_4_.refs_8_
  58.3 1.7 %shard_map.70.refs_0_ = f32[2,128,128]{2,1,0:T(8,128)S(1)} custom-call(s32[32]{0:T(128)S(1)} %copy-done.4, s32[3]{0:T(128)S(1)} %copy-done.3, bf16[3,2,128,4096]{3,2,1,0:T(8,128)(2,1)S(1)} %get-tuple-element.31.kept_ref, f32[1,128,128]{2,1,0:T(8,128)S(1)} %get-tuple-element.32.refs_0_, bf16[64,4608]{1,0:T(8,128)(2,1)S(1)} %collective-permute-done.refs_1_.refs_5_, ...), custom_call_target="tpu_custom_call" | custom-call | flops 536870912 | bytes 2097152 | tf_op jit(solution)/shard_map/pallas_call | solution.py:364
  60.0 0.0 collective-permute-done.10.refs_6_.refs_10_.refs_1_.refs_4_
  60.0 0.0 collective-permute-done.11.refs_8_.refs_12_.refs_3_.refs_6_
  60.1 1.6 %shard_map.71.refs_1_ = f32[3,128,128]{2,1,0:T(8,128)S(1)} custom-call(s32[32]{0:T(128)S(1)} %copy-done.4, s32[3]{0:T(128)S(1)} %copy-done.3, bf16[3,2,128,4096]{3,2,1,0:T(8,128)(2,1)S(1)} %get-tuple-element.31.kept_ref, f32[2,128,128]{2,1,0:T(8,128)S(1)} %shard_map.70.refs_0_, bf16[64,4608]{1,0:T(8,128)(2,1)S(1)} %collective-permute-done.refs_1_.refs_5_, ...), custom_call_target="tpu_custom_call" | custom-call | flops 536870912 | bytes 2097152 | tf_op jit(solution)/shard_map/pallas_call | solution.py:364
  61.6 1.5 %collective-permute-start.12 = (f32[3,128,128]{2,1,0:T(8,128)S(1)}, f32[3,128,128]{2,1,0:T(8,128)S(1)}, u32[]{:S(2)}, u32[]{:S(2)}) collective-permute-start(f32[3,128,128]{2,1,0:T(8,128)S(1)} %shard_map.71.refs_1_), channel_id=1, source_target_pairs={{0,2},{2,0},{1,3},{3,1},{4,6},{6,4},{5,7},{7,5},{8,10},{10,8},{9,1... | collective-permute-start | bytes 589832 | tf_op jit(solution)/shard_map/ppermute | solution.py:502
  63.2 0.0 collective-permute-done.13.refs_5_.refs_8_
  63.2 0.0 collective-permute-done.14.refs_7_.refs_10_
  63.2 1.6 %shard_map.73.refs_1_ = f32[1,128,128]{2,1,0:T(8,128)S(1)} custom-call(s32[32]{0:T(128)S(1)} %copy-done.4, s32[3]{0:T(128)S(1)} %copy-done.3, bf16[3,2,128,4096]{3,2,1,0:T(8,128)(2,1)S(1)} %get-tuple-element.31.kept_ref, bf16[64,4608]{1,0:T(8,128)(2,1)S(1)} %collective-permute-done.1.refs_5_.refs_9_.refs_0_.refs_3_, ...), custom_call_target="tpu_custom_call" | custom-call | flops 536870912 | bytes 2097152 | tf_op jit(solution)/shard_map/pallas_call | solution.py:364
  64.7 0.6 collective-permute-start.15
  65.4 3.8 %collective-permute-done.12.refs_2_ = f32[3,128,128]{2,1,0:T(8,128)S(1)} collective-permute-done((f32[3,128,128]{2,1,0:T(8,128)S(1)}, f32[3,128,128]{2,1,0:T(8,128)S(1)}, u32[]{:S(2)}, u32[]{:S(2)}) %collective-permute-start.12) | collective-permute-done | bytes 196640 | tf_op jit(solution)/shard_map/ppermute | solution.py:502
  69.2 3.2 %shard_map.72 = (bf16[1024,512]{1,0:T(8,128)(2,1)}, f32[2,128,512]{2,1,0:T(8,128)S(1)}) custom-call(s32[32]{0:T(128)S(1)} %copy-done.4, s32[3]{0:T(128)S(1)} %copy-done.3, f32[1024,512]{1,0:T(8,128)S(1)} %shard_map.69.refs_0_, f32[3,128,128]{2,1,0:T(8,128)S(1)} %shard_map.71.refs_1_, f32[3,128,128]{2,1,0:T(8,128)S(1)} %collective-permute-done.12.refs_2_, ...), custom_call_target="tpu_custom_call" | custom-call | flops 201326592 | bytes 5242880 | tf_op jit(solution)/shard_map/pallas_call | solution.py:429
  72.4 0.0 collective-permute-done.15.refs_2_
  72.4 1.8 %shard_map.74 = bf16[1024,512]{1,0:T(8,128)(2,1)} custom-call(s32[32]{0:T(128)S(1)} %copy-done.4, s32[3]{0:T(128)S(1)} %copy-done.3, f32[2,128,512]{2,1,0:T(8,128)S(1)} %get-tuple-element.35.refs_0_, f32[1,128,128]{2,1,0:T(8,128)S(1)} %shard_map.73.refs_1_, f32[1,128,128]{2,1,0:T(8,128)S(1)} %collective-permute-done.15.refs_2_, ...), custom_call_target="tpu_custom_call", output_to_operand_aliasing={{}: (13, {})} | custom-call | flops 50331648 | bytes 1048576 | tf_op jit(solution)/shard_map/pallas_call | solution.py:467
Async XLA Ops:
  0.1 13.9 %copy-start.2 = (s32[3]{0:T(128)}, s32[3]{0:T(128)S(1)}, u32[]{:S(2)}) copy-start(s32[3]{0:T(128)S(1)} %pad_add_fusion.here) | copy-start | bytes 40
  1.9 12.3 %collective-permute-start = (bf16[64,4608]{1,0:T(8,128)(2,1)S(1)}, bf16[64,4608]{1,0:T(8,128)(2,1)S(1)}, u32[]{:S(2)}, u32[]{:S(2)}) collective-permute-start(bf16[64,4608]{1,0:T(8,128)(2,1)S(1)} %get-tuple-element.21.refs_0_.refs_3_), channel_id=1, source_target_pairs={{0,4},{4,8},{8,12},{5,1},{9,5},{13,9},{2,6},{6,10},{10,14},{7,3},{... | collective-permute-start | bytes 1769480 | tf_op jit(solution)/shard_map/ppermute | solution.py:507
  6.9 18.8 %collective-permute-start.4 = (bf16[64,4608]{1,0:T(8,128)(2,1)S(1)}, bf16[64,4608]{1,0:T(8,128)(2,1)S(1)}, u32[]{:S(2)}, u32[]{:S(2)}) collective-permute-start(bf16[64,4608]{1,0:T(8,128)(2,1)S(1)} %get-tuple-element.24.refs_1_.refs_4_), channel_id=1, source_target_pairs={{0,4},{4,8},{8,12},{5,1},{9,5},{13,9},{2,6},{6,10},{10,14},{7,3},{... | collective-permute-start | bytes 1769480 | tf_op jit(solution)/shard_map/ppermute | solution.py:507
  14.2 15.4 %collective-permute-start.1 = (bf16[64,4608]{1,0:T(8,128)(2,1)S(1)}, bf16[64,4608]{1,0:T(8,128)(2,1)S(1)}, u32[]{:S(2)}, u32[]{:S(2)}) collective-permute-start(bf16[64,4608]{1,0:T(8,128)(2,1)S(1)} %collective-permute-done.refs_1_.refs_5_), channel_id=1, source_target_pairs={{4,8},{8,12},{5,1},{9,5},{6,10},{10,14},{7,3},{11,7},{20,24},{24,2... | collective-permute-start | bytes 1769480 | tf_op jit(solution)/shard_map/ppermute | solution.py:507
  14.9 10.1 %collective-permute-start.2 = (s32[168,512]{1,0:T(8,128)S(1)}, s32[168,512]{1,0:T(8,128)S(1)}, u32[]{:S(2)}, u32[]{:S(2)}) collective-permute-start(s32[168,512]{1,0:T(8,128)S(1)} %shard_map.66), channel_id=1, source_target_pairs={{0,2},{2,0},{1,3},{3,1},{4,6},{6,4},{5,7},{7,5},{8,10},{10,8},{9,1... | collective-permute-start | bytes 1032200 | tf_op jit(solution)/shard_map/ppermute | solution.py:502
  16.5 13.9 %copy-start.3 = (s32[3]{0:T(128)S(1)}, s32[3]{0:T(128)}, u32[]{:S(2)}) copy-start(s32[3]{0:T(128)} %copy-done.2) | copy-start | bytes 40
  25.0 0.7 copy-start
  25.7 15.6 %collective-permute-start.5 = (bf16[64,4608]{1,0:T(8,128)(2,1)S(1)}, bf16[64,4608]{1,0:T(8,128)(2,1)S(1)}, u32[]{:S(2)}, u32[]{:S(2)}) collective-permute-start(bf16[64,4608]{1,0:T(8,128)(2,1)S(1)} %collective-permute-done.4.refs_3_.refs_7_), channel_id=1, source_target_pairs={{4,8},{8,12},{5,1},{9,5},{6,10},{10,14},{7,3},{11,7},{20,24},{24,2... | collective-permute-start | bytes 1769480 | tf_op jit(solution)/shard_map/ppermute | solution.py:507
  26.4 24.3 %collective-permute-start.6 = (s32[488,512]{1,0:T(8,128)}, s32[488,512]{1,0:T(8,128)}, u32[]{:S(2)}, u32[]{:S(2)}) collective-permute-start(s32[488,512]{1,0:T(8,128)} %shard_map.68), channel_id=1, source_target_pairs={{0,2},{2,0},{1,3},{3,1},{4,6},{6,4},{5,7},{7,5},{8,10},{10,8},{9,1... | collective-permute-start | bytes 2998280 | tf_op jit(solution)/shard_map/ppermute | solution.py:502
  29.5 15.3 %collective-permute-start.8 = (bf16[64,4608]{1,0:T(8,128)(2,1)S(1)}, bf16[64,4608]{1,0:T(8,128)(2,1)S(1)}, u32[]{:S(2)}, u32[]{:S(2)}) collective-permute-start(bf16[64,4608]{1,0:T(8,128)(2,1)S(1)} %collective-permute-done.refs_1_.refs_5_), channel_id=1, source_target_pairs={{0,1},{1,0},{2,3},{3,2},{4,5},{5,4},{6,7},{7,6},{8,9},{9,8},{10,11... | collective-permute-start | bytes 1769480 | tf_op jit(solution)/shard_map/ppermute | solution.py:510
  29.6 14.1 %collective-permute-start.3 = (bf16[64,4608]{1,0:T(8,128)(2,1)S(1)}, bf16[64,4608]{1,0:T(8,128)(2,1)S(1)}, u32[]{:S(2)}, u32[]{:S(2)}) collective-permute-start(bf16[64,4608]{1,0:T(8,128)(2,1)S(1)} %collective-permute-done.1.refs_5_.refs_9_.refs_0_.refs_3_), channel_id=1, source_target_pairs={{8,12},{5,1},{10,14},{7,3},{24,28},{21,17},{26,30},{23,19}} | collective-permute-start | bytes 1769480 | tf_op jit(solution)/shard_map/ppermute | solution.py:507
  30.3 1.0 %copy-start.1 = (s32[168,512]{1,0:T(8,128)S(1)}, s32[168,512]{1,0:T(8,128)}, u32[]{:S(2)}) copy-start(s32[168,512]{1,0:T(8,128)} %copy-done) | copy-start | bytes 1032196
  31.3 0.6 copy-start.4
  41.3 9.4 %collective-permute-start.7 = (bf16[64,4608]{1,0:T(8,128)(2,1)S(1)}, bf16[64,4608]{1,0:T(8,128)(2,1)S(1)}, u32[]{:S(2)}, u32[]{:S(2)}) collective-permute-start(bf16[64,4608]{1,0:T(8,128)(2,1)S(1)} %collective-permute-done.5.refs_7_.refs_11_.refs_2_.refs_5_), channel_id=1, source_target_pairs={{8,12},{5,1},{10,14},{7,3},{24,28},{21,17},{26,30},{23,19}} | collective-permute-start | bytes 1769480 | tf_op jit(solution)/shard_map/ppermute | solution.py:507
  42.0 16.4 %collective-permute-start.9 = (bf16[64,4608]{1,0:T(8,128)(2,1)S(1)}, bf16[64,4608]{1,0:T(8,128)(2,1)S(1)}, u32[]{:S(2)}, u32[]{:S(2)}) collective-permute-start(bf16[64,4608]{1,0:T(8,128)(2,1)S(1)} %collective-permute-done.4.refs_3_.refs_7_), channel_id=1, source_target_pairs={{0,1},{1,0},{2,3},{3,2},{4,5},{5,4},{6,7},{7,6},{8,9},{9,8},{10,11... | collective-permute-start | bytes 1769480 | tf_op jit(solution)/shard_map/ppermute | solution.py:510
  43.7 16.3 %collective-permute-start.10 = (bf16[64,4608]{1,0:T(8,128)(2,1)S(1)}, bf16[64,4608]{1,0:T(8,128)(2,1)S(1)}, u32[]{:S(2)}, u32[]{:S(2)}) collective-permute-start(bf16[64,4608]{1,0:T(8,128)(2,1)S(1)} %collective-permute-done.1.refs_5_.refs_9_.refs_0_.refs_3_), channel_id=1, source_target_pairs={{0,1},{1,0},{2,3},{3,2},{4,5},{5,4},{6,7},{7,6},{8,9},{9,8},{10,11... | collective-permute-start | bytes 1769480 | tf_op jit(solution)/shard_map/ppermute | solution.py:510
  44.8 15.2 %collective-permute-start.11 = (bf16[64,4608]{1,0:T(8,128)(2,1)S(1)}, bf16[64,4608]{1,0:T(8,128)(2,1)S(1)}, u32[]{:S(2)}, u32[]{:S(2)}) collective-permute-start(bf16[64,4608]{1,0:T(8,128)(2,1)S(1)} %collective-permute-done.5.refs_7_.refs_11_.refs_2_.refs_5_), channel_id=1, source_target_pairs={{0,1},{1,0},{2,3},{3,2},{4,5},{5,4},{6,7},{7,6},{8,9},{9,8},{10,11... | collective-permute-start | bytes 1769480 | tf_op jit(solution)/shard_map/ppermute | solution.py:510
  50.6 12.5 %collective-permute-start.13 = (bf16[64,4608]{1,0:T(8,128)(2,1)S(1)}, bf16[64,4608]{1,0:T(8,128)(2,1)S(1)}, u32[]{:S(2)}, u32[]{:S(2)}) collective-permute-start(bf16[64,4608]{1,0:T(8,128)(2,1)S(1)} %collective-permute-done.3.refs_4_.refs_7_), channel_id=1, source_target_pairs={{0,1},{1,0},{2,3},{3,2},{4,5},{5,4},{6,7},{7,6},{8,9},{9,8},{10,11... | collective-permute-start | bytes 1769480 | tf_op jit(solution)/shard_map/ppermute | solution.py:510
  50.7 12.5 %collective-permute-start.14 = (bf16[64,4608]{1,0:T(8,128)(2,1)S(1)}, bf16[64,4608]{1,0:T(8,128)(2,1)S(1)}, u32[]{:S(2)}, u32[]{:S(2)}) collective-permute-start(bf16[64,4608]{1,0:T(8,128)(2,1)S(1)} %collective-permute-done.7.refs_6_.refs_9_), channel_id=1, source_target_pairs={{0,1},{1,0},{2,3},{3,2},{4,5},{5,4},{6,7},{7,6},{8,9},{9,8},{10,11... | collective-permute-start | bytes 1769480 | tf_op jit(solution)/shard_map/ppermute | solution.py:510
  61.6 7.6 %collective-permute-start.12 = (f32[3,128,128]{2,1,0:T(8,128)S(1)}, f32[3,128,128]{2,1,0:T(8,128)S(1)}, u32[]{:S(2)}, u32[]{:S(2)}) collective-permute-start(f32[3,128,128]{2,1,0:T(8,128)S(1)} %shard_map.71.refs_1_), channel_id=1, source_target_pairs={{0,2},{2,0},{1,3},{3,1},{4,6},{6,4},{5,7},{7,5},{8,10},{10,8},{9,1... | collective-permute-start | bytes 589832 | tf_op jit(solution)/shard_map/ppermute | solution.py:502
  64.7 7.6 %collective-permute-start.15 = (f32[1,128,128]{2,1,0:T(8,128)S(1)}, f32[1,128,128]{2,1,0:T(8,128)S(1)}, u32[]{:S(2)}, u32[]{:S(2)}) collective-permute-start(f32[1,128,128]{2,1,0:T(8,128)S(1)} %shard_map.73.refs_1_), channel_id=1, source_target_pairs={{0,2},{2,0},{1,3},{3,1},{4,6},{6,4},{5,7},{7,5},{8,10},{10,8},{9,1... | collective-permute-start | bytes 196616 | tf_op jit(solution)/shard_map/ppermute | solution.py:502

commit v11 on v7

--- a/solution.py
+++ b/solution.py
@@ -56,10 +56,10 @@
     return start, seg >= 0, table[k * ENTRIES + 2 + 2 * j]
 
 
-def message_kernel(here, down_ref, up_ref, o_ref, sems):
+def message_kernel(down_ref, up_ref, o_ref, sems):
     width = down_ref.shape[1]
     columns = o_ref.shape[1] - width
-    start = pl.multiple_of(here[2] * columns, columns)
+    start = pl.multiple_of(lax.axis_index("tensor") * columns, columns)
     rows = down_ref.shape[0] // PIECES
     copies = [
         pltpu.make_async_copy(
@@ -80,17 +80,17 @@
         copy.wait()
 
 
-def message_call(here, down, up, columns):
+def message_call(down, up, columns):
     rows, width = down.shape
     return pl.pallas_call(
         message_kernel,
-        in_specs=[SMEM, HBM, HBM],
+        in_specs=[HBM, HBM],
         out_specs=VMEM,
         out_shape=jax.ShapeDtypeStruct((rows, width + columns), jnp.bfloat16),
         scratch_shapes=[pltpu.SemaphoreType.DMA((PIECES + 1,))],
         compiler_params=params(8),
         cost_estimate=cost(0, 4 * rows * (width + columns)),
-    )(here, down, up)
+    )(down, up)
 
 
 def table_kernel(n_adapter, per_device, here, ids, slots, table):
@@ -236,9 +236,10 @@
     ]
 
 
-def sent_kernel(first, sizes, column, x_ref, w_ref, *refs):
+def sent_kernel(first, sizes, step, n_tensor, x_ref, w_ref, *refs):
     outs, (x, w, sems) = refs[: len(sizes)], refs[len(sizes) :]
-    work = load_base(first, sum(sizes), column[0], x_ref, w_ref, x, w, sems)
+    column = lax.rem(lax.axis_index("tensor") + step, n_tensor)
+    work = load_base(first, sum(sizes), column, x_ref, w_ref, x, w, sems)
     unit_of = [(out, unit) for out, size in enumerate(sizes) for unit in range(size)]
     for out, size in zip(outs, sizes):
         out[size * WORDS :, :] = jnp.zeros((8, w.shape[1]), jnp.int32)
@@ -249,12 +250,12 @@
             encode(product[r : r + SEGMENT_ROWS], outs[out], unit, sizes[out])
 
 
-def sent_call(tokens, weight, column, columns, first, sizes):
+def sent_call(tokens, weight, step, n_tensor, columns, first, sizes):
     width = tokens.shape[1]
     rows = sum(sizes) * SEGMENT_ROWS
     return pl.pallas_call(
-        functools.partial(sent_kernel, first, sizes),
-        in_specs=[SMEM, HBM, HBM],
+        functools.partial(sent_kernel, first, sizes, step, n_tensor),
+        in_specs=[HBM, HBM],
         out_specs=[VMEM] * len(sizes),
         out_shape=[jax.ShapeDtypeStruct((coded_rows(n), columns), jnp.int32) for n in sizes],
         scratch_shapes=base_scratch(sum(sizes), width, columns),
@@ -262,7 +263,7 @@
         cost_estimate=cost(
             2 * rows * width * columns, 2 * rows * width + 2 * width * columns + 4 * rows * columns
         ),
-    )(column.reshape(1), tokens, weight)
+    )(tokens, weight)
 
 
 def add_kernel(chunk, base_ref, *refs):
@@ -348,23 +349,22 @@
     )(table, here, tokens, weight, message, *coded)
 
 
-def shrink_kernel(k, rank, n_before, table, here, kept_ref, *refs):
-    buffers, o_ref = refs[n_before:-1], refs[-1]
-    for r in refs[:n_before]:
-        o_ref[:1] = r[...]
-    rows_of = lambda j: kept_ref[k - 1, j]
+def shrink_kernel(k, rank, at, table, here, kept_ref, *refs):
+    buffers, o_ref = refs[1 if at else 0 : -1], refs[-1]
+    if at:
+        o_ref[:at] = refs[0][...]
     owners = buffer_owners(here, stages_of(k))
-    shrink_into(o_ref, n_before, table, k, rows_of, buffers, owners, rank)
+    shrink_into(o_ref, at, table, k, lambda j: kept_ref[k - 1, j], buffers, owners, rank)
 
 
 def shrink_call(k, table, here, kept, before, buffers, rank):
     width = kept.shape[3]
-    n = 1 + len(before)
-    return pl.pallas_call(
-        functools.partial(shrink_kernel, k, rank, len(before)),
-        in_specs=[SMEM, SMEM, VMEM] + [VMEM] * (n - 1 + len(buffers)),
+    at = sum(b.shape[0] for b in before)
+    return pl.pallas_call(
+        functools.partial(shrink_kernel, k, rank, at),
+        in_specs=[SMEM, SMEM, VMEM] + [VMEM] * (len(before) + len(buffers)),
         out_specs=VMEM,
-        out_shape=jax.ShapeDtypeStruct((n, SEGMENT_ROWS, MOST * rank), jnp.float32),
+        out_shape=jax.ShapeDtypeStruct((at + 1, SEGMENT_ROWS, MOST * rank), jnp.float32),
         compiler_params=params(16),
         cost_estimate=cost(MOST * 2 * SEGMENT_ROWS * width * 256, 4 * SEGMENT_ROWS * width),
     )(table, here, kept, *before, *buffers)
@@ -392,12 +392,16 @@
     return jnp.dot(terms, factor, preferred_element_type=jnp.float32)
 
 
+LATE = 2
+
+
 def early_kernel(n_adapter, n_tensor, rank, table, here, *refs):
-    n_coded, n_buffers = n_tensor - 1, 2 * n_adapter - 3
-    base_ref, coded_refs, refs = refs[0], refs[1 : 1 + n_coded], refs[1 + n_coded :]
+    first = n_adapter - LATE
+    n_buffers = 2 * first - 1
+    base_ref, coded_refs, refs = refs[0], refs[1:n_tensor], refs[n_tensor:]
     shrinks, refs = refs[: -4 - n_buffers], refs[-4 - n_buffers :]
     buffers, (o_ref, rest_ref, up, total) = refs[:-4], refs[-4:]
-    for k in range(n_adapter - 1):
+    for k in range(first):
         at = 0 if k == 0 else 2 * stages_of(k)[0] - 1
         to = 2 * k + 1
         owners = buffer_owners(here, stages_of(k))
@@ -415,8 +419,8 @@
         for j in range(MOST):
             start, used, _ = segment_of(table, k, j)
             value = total[pl.ds(start, SEGMENT_ROWS), :]
-            if k == n_adapter - 1:
-                rest_ref[j] = value
+            if k >= first:
+                rest_ref[k - first, j] = value
                 continue
             lora = up_product(shares[k], j, up[k * MOST + j], rank)
 
@@ -435,10 +439,10 @@
         out_specs=[VMEM, VMEM],
         out_shape=[
             jax.ShapeDtypeStruct((rows, columns), jnp.bfloat16),
-            jax.ShapeDtypeStruct((MOST, SEGMENT_ROWS, columns), jnp.float32),
+            jax.ShapeDtypeStruct((LATE, MOST, SEGMENT_ROWS, columns), jnp.float32),
         ],
         scratch_shapes=[
-            pltpu.VMEM(((n_adapter - 1) * MOST, 2 * rank, columns), jnp.bfloat16),
+            pltpu.VMEM(((n_adapter - LATE) * MOST, 2 * rank, columns), jnp.bfloat16),
             pltpu.VMEM((rows, columns), jnp.float32),
         ],
         compiler_params=params(16),
@@ -446,7 +450,7 @@
     )(table, here, base, *coded, *shrinks, *buffers)
 
 
-def late_kernel(k, n_tensor, rank, table, here, *refs):
+def late_kernel(k, number, n_tensor, rank, table, here, *refs):
     rest_ref, shrinks, refs = refs[0], refs[1 : 1 + n_tensor], refs[1 + n_tensor :]
     buffers, (_, o_ref, up, out, sems) = refs[:-5], refs[-5:]
     owners = buffer_owners(here, stages_of(k))
@@ -458,7 +462,7 @@
         fetch_up(up, j, table, k, j, buffers, owners, rank)
         start, used, _ = segment_of(table, k, j)
         lora = up_product(share, j, up[j], rank)
-        out[j] = (rest_ref[j] + adapter_scale * lora).astype(jnp.bfloat16)
+        out[j] = (rest_ref[number, j] + adapter_scale * lora).astype(jnp.bfloat16)
         store = pltpu.make_async_copy(out.at[j], o_ref.at[pl.ds(start, SEGMENT_ROWS), :], sems.at[j])
         pl.when(used)(store.start)
         stores.append((used, store))
@@ -466,10 +470,10 @@
         pl.when(used)(store.wait)
 
 
-def late(k, n_tensor, table, here, rest, shrinks, buffers, value, rank):
+def late(k, number, n_tensor, table, here, rest, shrinks, buffers, value, rank):
     rows, columns = value.shape
     return pl.pallas_call(
-        functools.partial(late_kernel, k, n_tensor, rank),
+        functools.partial(late_kernel, k, number, n_tensor, rank),
         in_specs=[SMEM] * 2 + [VMEM] * (1 + len(shrinks) + len(buffers)) + [ANY],
         out_specs=ANY,
         out_shape=jax.ShapeDtypeStruct((rows, columns), jnp.bfloat16),
@@ -518,7 +522,7 @@
     tokens, value_weight, down, up = (
         pltpu.with_memory_space_constraint(a, pltpu.HBM) for a in (tokens, value_weight, down, up)
     )
-    message = message_call(here, down, up, columns)
+    message = message_call(down, up, columns)
     table = table_call(here, row_adapter_index, adapter_slot_of, n_adapter, per_device)
 
     buffers, shrinks = [[message]], []
@@ -526,6 +530,9 @@
     def buffers_of(stages):
         return [b for stage in stages for b in buffers[stage]]
 
+    def shrink(k, kept, before):
+        return shrink_call(k, table, here, kept, before, buffers_of(stages_of(k)), rank)
+
     def add_shrink(mine):
         shrinks.extend([mine] + [swap_tensor(mine, step) for step in range(1, n_tensor)])
 
@@ -534,8 +541,7 @@
 
     def sent_for(step, chunks):
         sizes = [number for _, number in chunks]
-        target = (me_t + step) % n_tensor
-        return sent_call(tokens, value_weight, target, columns, chunks[0][0], sizes)
+        return sent_call(tokens, value_weight, step, n_tensor, columns, chunks[0][0], sizes)
 
     parts = [[sent_for(step, CHUNKS[:1])[0] for step in others]]
     rest_parts = [sent_for(step, CHUNKS[1:]) for step in others]
@@ -543,32 +549,23 @@
     sent = [[swap_tensor(p, step) for step, p in zip(others, parts[0])]]
     last = n_adapter - 1
     done = [table] + [p for group in parts for p in group] + sent[0]
-    before = None
     for stage in range(1, last):
         came = after(held, *done)
         held = along_line(came, stage + 1)
+        buffers.append([came, swap_cores(came)])
         if stage < len(CHUNKS):
             sent.append([swap_tensor(after(p, came), step) for step, p in zip(others, parts[stage])])
         if stage == 1:
             base, before, kept = own_call(
                 after(table, came), here, tokens, value_weight, message, sent[0], columns, n_adapter, rank
             )
-            add_shrink(before)
-            done = sent[1] + shrinks
+            done = sent[1] + [base]
         else:
             if stage == 2:
                 base = add_call(1, after(base, came), sent[1])
-            before = shrink_call(
-                stage - 1, table, here, after(kept, came), [], buffers_of(stages_of(stage - 1)), rank
-            )
-            if stage < last - 1:
-                add_shrink(before)
+            before = shrink(stage - 1, after(kept, came), [before])
             done = []
-        buffers.append([came, swap_cores(came)])
-    merged = shrink_call(
-        last - 1, table, here, kept, [before], buffers_of(stages_of(last - 1)), rank
-    )
-    add_shrink(merged)
+    add_shrink(before)
     value, remaining = early(
         n_adapter,
         n_tensor,
@@ -577,23 +574,30 @@
         base,
         sent[2],
         shrinks,
-        buffers_of(range(last)),
+        buffers_of(range(last - 1)),
         rank,
     )
     came = after(held, value)
     buffers.append([came, swap_cores(came)])
-    add_shrink(shrink_call(last, table, here, kept, [], buffers_of(stages_of(last)), rank))
-    return late(
-        last,
-        n_tensor,
-        table,
-        here,
-        remaining,
-        shrinks[-n_tensor:],
-        buffers_of(stages_of(last)),
-        value,
-        rank,
-    )
+    ready = after(kept, came)
+    for k in (last - 1, last):
+        mine = shrink(k, ready, [])
+        add_shrink(mine)
+        ready = after(kept, mine)
+    for number, k in enumerate((last - 1, last)):
+        value = late(
+            k,
+            number,
+            n_tensor,
+            table,
+            here,
+            remaining,
+            shrinks[(number - LATE) * n_tensor :][:n_tensor],
+            buffers_of(stages_of(k)),
+            value,
+            rank,
+        )
+    return value
 
 
 def solution(mesh):

time: 67.9 us -> 66.4 us (0.978)
  waiting for transfers between devices: 18.4 us -> 13.2 us
  starting transfers between devices: 16.5 us -> 18.6 us
  Pallas kernels: 31.8 us -> 32.5 us
    ppermute x6, waiting for transfers between devices: 14.2 us -> 10.1 us  [swap_tensor(): return lax.ppermute(array, 'tensor', pairs)]
    ppermute x3, waiting for transfers between devices: 2.85 us -> 0.01 us  [swap_cores(): return lax.ppermute(array, 'dp', [(0, 1), (1, 0)])]
    ppermute x3, waiting for transfers between devices: 1.36 us -> 3.01 us  [along_line(): return lax.ppermute(array, ('adapter', 'dp'), up + down)]
    ppermute x3, starting transfers between devices: 8.99 us -> 10.4 us  [along_line(): return lax.ppermute(array, ('adapter', 'dp'), up + down)]
    pallas_call x7 -> x8, Pallas kernels: 17.8 us -> 19 us  [the longest x2 10.2 us: sent_call(): pl.pallas_call(functools.partial(sent_kernel, first, sizes, step, n_tenso...]
    ppermute x6, starting transfers between devices: 7.48 us -> 8.21 us  [swap_tensor(): return lax.ppermute(array, 'tensor', pairs)]
  transfers between devices with their start and end apart: 12 -> 12, of which waited for: 6 -> 6; matrix products, arithmetic and copies ran while one was open for 0% -> 1% of each run, Pallas kernels for 40% -> 45%
where the time goes in v11:
time: 66.4 us; the launch traced here: 65.2 us
  Pallas kernels  32.5 us (49%)
  starting transfers between devices  18.6 us (28%)
  waiting for transfers between devices  13.2 us (20%)
    ppermute x3, starting transfers between devices, along_line(): return lax.ppermute(array, ('adapter', 'dp'), up + down)  10.4 us
    pallas_call x2, Pallas kernels, sent_call(): pl.pallas_call(functools.partial(sent_kernel, first, sizes, step, n_tenso...  10.2 us
    ppermute x6, waiting for transfers between devices, swap_tensor(): return lax.ppermute(array, 'tensor', pairs)  10.1 us
    pallas_call x1, Pallas kernels, own_call(): pl.pallas_call(functools.partial(own_kernel, n_adapter, rank), in_specs=[...  9.2 us
    ppermute x6, starting transfers between devices, swap_tensor(): return lax.ppermute(array, 'tensor', pairs)  8.21 us
    pallas_call x3, Pallas kernels, shrink_call(): pl.pallas_call(functools.partial(shrink_kernel, k, rank, at), in_specs=[S...  4.14 us
    pallas_call x2, Pallas kernels, late(): pl.pallas_call(functools.partial(late_kernel, k, number, n_tensor, rank),...  3.4 us
    ppermute x3, waiting for transfers between devices, along_line(): return lax.ppermute(array, ('adapter', 'dp'), up + down)  3.01 us
  transfers between devices with their start and end apart: 12, of which 6 were waited for; matrix products, arithmetic and copies ran while one was open for 1% of the time, Pallas kernels for 45%

profile of v11, /device:TPU:16, one launch (start us, length us, event | category | flops | bytes accessed | tf_op | source)
XLA Modules:
  0.0 65.2 jit_solution(7690602611715627837)
XLA Ops:
  0.0 1.3 %shard_map.65.message.refs_4_ = bf16[128,4608]{1,0:T(8,128)(2,1)S(1)} custom-call(bf16[128,4096]{1,0:T(8,128)(2,1)} %bitcast.7, bf16[128,1024]{1,0:T(8,128)(2,1)} %bitcast.8), custom_call_target="tpu_custom_call" | custom-call | bytes 2359296 | tf_op jit(solution)/shard_map/pallas_call | solution.py:85
  1.3 3.5 %collective-permute-start = (bf16[128,4608]{1,0:T(8,128)(2,1)S(1)}, bf16[128,4608]{1,0:T(8,128)(2,1)S(1)}, u32[]{:S(2)}, u32[]{:S(2)}) collective-permute-start(bf16[128,4608]{1,0:T(8,128)(2,1)S(1)} %shard_map.65.message.refs_4_), channel_id=1, source_target_pairs={{0,4},{4,8},{8,12},{5,1},{9,5},{13,9},{2,6},{6,10},{10,14},{7,3},{... | collective-permute-start | bytes 3538952 | tf_op jit(solution)/shard_map/ppermute | solution.py:515
  4.8 3.6 %shard_map.66 = s32[168,512]{1,0:T(8,128)S(1)} custom-call(bf16[1024,4096]{1,0:T(8,128)(2,1)} %x_ref.5, bf16[4096,1024]{1,0:T(8,128)(2,1)} %w_ref.5), custom_call_target="tpu_custom_call" | custom-call | flops 1073741824 | bytes 6815744 | tf_op jit(solution)/shard_map/pallas_call | solution.py:256
  8.3 1.6 %collective-permute-start.1 = (s32[168,512]{1,0:T(8,128)S(1)}, s32[168,512]{1,0:T(8,128)S(1)}, u32[]{:S(2)}, u32[]{:S(2)}) collective-permute-start(s32[168,512]{1,0:T(8,128)S(1)} %shard_map.66), channel_id=1, source_target_pairs={{0,2},{2,0},{1,3},{3,1},{4,6},{6,4},{5,7},{7,5},{8,10},{10,8},{9,1... | collective-permute-start | bytes 1032200 | tf_op jit(solution)/shard_map/ppermute | solution.py:510
  10.0 0.7 %pad_add_fusion.here = s32[3]{0:T(128)} fusion(s32[1]{0:T(128)} %bitcast.2, s32[1]{0:T(128)} %bitcast.1, s32[1]{0:T(128)} %bitcast), kind=kLoop, calls=%fused_computation | loop fusion | flops 6 | bytes 24 | tf_op jit(solution)/shard_map/stack | solution.py:505
  10.6 1.4 %shard_map.64.table = s32[32]{0:T(128)} custom-call(s32[3]{0:T(128)} %pad_add_fusion.here, s32[1024]{0:T(1024)} %ids.1, s32[8]{0:T(128)} %slots.1), custom_call_target="tpu_custom_call" | custom-call | bytes 4096 | tf_op jit(solution)/shard_map/pallas_call | solution.py:117
  12.1 0.0 copy-start
  12.1 0.0 copy-start.1
  12.1 6.6 %shard_map.67 = (s32[328,512]{1,0:T(8,128)S(1)}, s32[168,512]{1,0:T(8,128)S(1)}) custom-call(bf16[1024,4096]{1,0:T(8,128)(2,1)} %x_ref.5, bf16[4096,1024]{1,0:T(8,128)(2,1)} %w_ref.5), custom_call_target="tpu_custom_call" | custom-call | flops 3221225472 | bytes 12058624 | tf_op jit(solution)/shard_map/pallas_call | solution.py:256
  18.7 0.0 collective-permute-done.1.refs_0_
  18.7 0.7 %collective-permute-done.refs_1_.refs_5_.refs_0_.refs_3_ = bf16[128,4608]{1,0:T(8,128)(2,1)S(1)} collective-permute-done((bf16[128,4608]{1,0:T(8,128)(2,1)S(1)}, bf16[128,4608]{1,0:T(8,128)(2,1)S(1)}, u32[]{:S(2)}, u32[]{:S(2)}) %collective-permute-start) | collective-permute-done | bytes 1179680 | tf_op jit(solution)/shard_map/ppermute | solution.py:515
  19.4 3.5 %collective-permute-start.2 = (bf16[128,4608]{1,0:T(8,128)(2,1)S(1)}, bf16[128,4608]{1,0:T(8,128)(2,1)S(1)}, u32[]{:S(2)}, u32[]{:S(2)}) collective-permute-start(bf16[128,4608]{1,0:T(8,128)(2,1)S(1)} %collective-permute-done.refs_1_.refs_5_.refs_0_.refs_3_), channel_id=1, source_target_pairs={{4,8},{8,12},{5,1},{9,5},{6,10},{10,14},{7,3},{11,7},{20,24},{24,2... | collective-permute-start | bytes 3538952 | tf_op jit(solution)/shard_map/ppermute | solution.py:515
  22.8 1.6 %collective-permute-start.3 = (s32[328,512]{1,0:T(8,128)S(1)}, s32[328,512]{1,0:T(8,128)S(1)}, u32[]{:S(2)}, u32[]{:S(2)}) collective-permute-start(s32[328,512]{1,0:T(8,128)S(1)} %get-tuple-element.27), channel_id=1, source_target_pairs={{0,2},{2,0},{1,3},{3,1},{4,6},{6,4},{5,7},{7,5},{8,10},{10,8},{9,1... | collective-permute-start | bytes 2015240 | tf_op jit(solution)/shard_map/ppermute | solution.py:510
  24.4 0.0 collective-permute-start.5
  24.4 0.0 copy-done
  24.4 0.0 copy-done.1
  24.4 9.2 %shard_map.68 = (f32[1024,512]{1,0:T(8,128)S(1)}, f32[1,128,128]{2,1,0:T(8,128)S(1)}, bf16[3,2,128,4096]{3,2,1,0:T(8,128)(2,1)S(1)}) custom-call(s32[32]{0:T(128)S(1)} %copy-done.1, s32[3]{0:T(128)S(1)} %copy-done, bf16[1024,4096]{1,0:T(8,128)(2,1)} %x_ref.5, bf16[4096,1024]{1,0:T(8,128)(2,1)} %w_ref.5, bf16[128,4608]{1,0:T(8,128)(2,1)S(1)} %shard_map.65.message.refs_4_, ...), custom_call_target="tpu_custom_call" | custom-call | flops 4294967296 | bytes 14680064 | tf_op jit(solution)/shard_map/pallas_call | solution.py:334
  33.6 3.9 %collective-permute-done.3.refs_0_ = s32[328,512]{1,0:T(8,128)S(1)} collective-permute-done((s32[328,512]{1,0:T(8,128)S(1)}, s32[328,512]{1,0:T(8,128)S(1)}, u32[]{:S(2)}, u32[]{:S(2)}) %collective-permute-start.3) | collective-permute-done | bytes 671776 | tf_op jit(solution)/shard_map/ppermute | solution.py:510
  37.5 0.0 collective-permute-done.2.refs_2_.refs_0_.refs_5_.refs_3_
  37.5 3.4 %collective-permute-start.7 = (bf16[128,4608]{1,0:T(8,128)(2,1)S(1)}, bf16[128,4608]{1,0:T(8,128)(2,1)S(1)}, u32[]{:S(2)}, u32[]{:S(2)}) collective-permute-start(bf16[128,4608]{1,0:T(8,128)(2,1)S(1)} %collective-permute-done.2.refs_2_.refs_0_.refs_5_.refs_3_), channel_id=1, source_target_pairs={{8,12},{5,1},{10,14},{7,3},{24,28},{21,17},{26,30},{23,19}} | collective-permute-start | bytes 3538952 | tf_op jit(solution)/shard_map/ppermute | solution.py:515
  41.0 1.6 %collective-permute-start.4 = (s32[168,512]{1,0:T(8,128)S(1)}, s32[168,512]{1,0:T(8,128)S(1)}, u32[]{:S(2)}, u32[]{:S(2)}) collective-permute-start(s32[168,512]{1,0:T(8,128)S(1)} %get-tuple-element.30), channel_id=1, source_target_pairs={{0,2},{2,0},{1,3},{3,1},{4,6},{6,4},{5,7},{7,5},{8,10},{10,8},{9,1... | collective-permute-start | bytes 1032200 | tf_op jit(solution)/shard_map/ppermute | solution.py:510
  42.6 0.0 collective-permute-done.5.refs_2_.refs_6_.refs_1_.refs_4_
  42.6 1.3 %shard_map.70.refs_2_ = f32[2,128,128]{2,1,0:T(8,128)S(1)} custom-call(s32[32]{0:T(128)S(1)} %copy-done.1, s32[3]{0:T(128)S(1)} %copy-done, bf16[3,2,128,4096]{3,2,1,0:T(8,128)(2,1)S(1)} %get-tuple-element.38.kept_ref, f32[1,128,128]{2,1,0:T(8,128)S(1)} %get-tuple-element.33.refs_0_, ...), custom_call_target="tpu_custom_call" | custom-call | flops 536870912 | bytes 2097152 | tf_op jit(solution)/shard_map/pallas_call | solution.py:363
  43.9 0.6 collective-permute-start.6
  44.5 0.0 collective-permute-start.8
  44.5 0.3 shard_map.69.refs_0_
  44.8 4.9 %collective-permute-done.6.refs_3_ = f32[2,128,128]{2,1,0:T(8,128)S(1)} collective-permute-done((f32[2,128,128]{2,1,0:T(8,128)S(1)}, f32[2,128,128]{2,1,0:T(8,128)S(1)}, u32[]{:S(2)}, u32[]{:S(2)}) %collective-permute-start.6) | collective-permute-done | bytes 131104 | tf_op jit(solution)/shard_map/ppermute | solution.py:510
  49.7 0.0 collective-permute-done.4.refs_1_
  49.7 2.6 %shard_map.71 = (bf16[1024,512]{1,0:T(8,128)(2,1)}, f32[2,2,128,512]{3,2,1,0:T(8,128)S(1)}) custom-call(s32[32]{0:T(128)S(1)} %copy-done.1, s32[3]{0:T(128)S(1)} %copy-done, f32[1024,512]{1,0:T(8,128)S(1)} %shard_map.69.refs_0_, s32[168,512]{1,0:T(8,128)S(1)} %collective-permute-done.4.refs_1_, f32[2,128,128]{2,1,0:T(8,128)S(1)} %shard_map.70.refs_2_, ...), custom_call_target="tpu_custom_call" | custom-call | flops 201326592 | bytes 5242880 | tf_op jit(solution)/shard_map/pallas_call | solution.py:436
  52.3 2.3 %collective-permute-done.7.refs_2_.refs_5_ = bf16[128,4608]{1,0:T(8,128)(2,1)S(1)} collective-permute-done((bf16[128,4608]{1,0:T(8,128)(2,1)S(1)}, bf16[128,4608]{1,0:T(8,128)(2,1)S(1)}, u32[]{:S(2)}, u32[]{:S(2)}) %collective-permute-start.7) | collective-permute-done | bytes 1179680 | tf_op jit(solution)/shard_map/ppermute | solution.py:515
  54.6 0.0 collective-permute-start.9
  54.6 0.0 collective-permute-done.8.refs_3_.refs_1_.refs_6_.refs_4_
  54.6 1.5 %shard_map.72.refs_1_ = f32[1,128,128]{2,1,0:T(8,128)S(1)} custom-call(s32[32]{0:T(128)S(1)} %copy-done.1, s32[3]{0:T(128)S(1)} %copy-done, bf16[3,2,128,4096]{3,2,1,0:T(8,128)(2,1)S(1)} %get-tuple-element.38.kept_ref, bf16[128,4608]{1,0:T(8,128)(2,1)S(1)} %collective-permute-done.refs_1_.refs_5_.refs_0_.refs_3_, ...), custom_call_target="tpu_custom_call" | custom-call | flops 536870912 | bytes 2097152 | tf_op jit(solution)/shard_map/pallas_call | solution.py:363
  56.2 1.6 %collective-permute-start.11 = (f32[1,128,128]{2,1,0:T(8,128)S(1)}, f32[1,128,128]{2,1,0:T(8,128)S(1)}, u32[]{:S(2)}, u32[]{:S(2)}) collective-permute-start(f32[1,128,128]{2,1,0:T(8,128)S(1)} %shard_map.72.refs_1_), channel_id=1, source_target_pairs={{0,2},{2,0},{1,3},{3,1},{4,6},{6,4},{5,7},{7,5},{8,10},{10,8},{9,1... | collective-permute-start | bytes 196616 | tf_op jit(solution)/shard_map/ppermute | solution.py:510
  57.7 0.0 collective-permute-done.9.refs_3_.refs_6_
  57.7 1.3 %shard_map.73.refs_1_ = f32[1,128,128]{2,1,0:T(8,128)S(1)} custom-call(s32[32]{0:T(128)S(1)} %copy-done.1, s32[3]{0:T(128)S(1)} %copy-done, bf16[3,2,128,4096]{3,2,1,0:T(8,128)(2,1)S(1)} %get-tuple-element.38.kept_ref, bf16[128,4608]{1,0:T(8,128)(2,1)S(1)} %collective-permute-done.2.refs_2_.refs_0_.refs_5_.refs_3_, ...), custom_call_target="tpu_custom_call" | custom-call | flops 536870912 | bytes 2097152 | tf_op jit(solution)/shard_map/pallas_call | solution.py:363
  59.0 1.3 %collective-permute-start.10 = (f32[1,128,128]{2,1,0:T(8,128)S(1)}, f32[1,128,128]{2,1,0:T(8,128)S(1)}, u32[]{:S(2)}, u32[]{:S(2)}) collective-permute-start(f32[1,128,128]{2,1,0:T(8,128)S(1)} %shard_map.73.refs_1_), channel_id=1, source_target_pairs={{0,2},{2,0},{1,3},{3,1},{4,6},{6,4},{5,7},{7,5},{8,10},{10,8},{9,1... | collective-permute-start | bytes 196616 | tf_op jit(solution)/shard_map/ppermute | solution.py:510
  60.4 0.4 collective-permute-done.11.refs_2_
  60.7 1.7 %shard_map.74.refs_7_ = bf16[1024,512]{1,0:T(8,128)(2,1)} custom-call(s32[32]{0:T(128)S(1)} %copy-done.1, s32[3]{0:T(128)S(1)} %copy-done, f32[2,2,128,512]{3,2,1,0:T(8,128)S(1)} %get-tuple-element.34.refs_0_, f32[1,128,128]{2,1,0:T(8,128)S(1)} %shard_map.72.refs_1_, ...), custom_call_target="tpu_custom_call", output_to_operand_aliasing={{}: (9, {})} | custom-call | flops 50331648 | bytes 1048576 | tf_op jit(solution)/shard_map/pallas_call | solution.py:475
  62.4 0.9 %collective-permute-done.10.refs_2_ = f32[1,128,128]{2,1,0:T(8,128)S(1)} collective-permute-done((f32[1,128,128]{2,1,0:T(8,128)S(1)}, f32[1,128,128]{2,1,0:T(8,128)S(1)}, u32[]{:S(2)}, u32[]{:S(2)}) %collective-permute-start.10) | collective-permute-done | bytes 65568 | tf_op jit(solution)/shard_map/ppermute | solution.py:510
  63.4 1.7 %shard_map.75 = bf16[1024,512]{1,0:T(8,128)(2,1)} custom-call(s32[32]{0:T(128)S(1)} %copy-done.1, s32[3]{0:T(128)S(1)} %copy-done, f32[2,2,128,512]{3,2,1,0:T(8,128)S(1)} %get-tuple-element.34.refs_0_, f32[1,128,128]{2,1,0:T(8,128)S(1)} %shard_map.73.refs_1_, f32[1,128,128]{2,1,0:T(8,128)S(1)} %collective-permute-done.10.refs_2_, ...), custom_call_target="tpu_custom_call", output_to_operand_aliasing={{}: (9, {})} | custom-call | flops 50331648 | bytes 1048576 | tf_op jit(solution)/shard_map/pallas_call | solution.py:475
Async XLA Ops:
  1.3 18.1 %collective-permute-start = (bf16[128,4608]{1,0:T(8,128)(2,1)S(1)}, bf16[128,4608]{1,0:T(8,128)(2,1)S(1)}, u32[]{:S(2)}, u32[]{:S(2)}) collective-permute-start(bf16[128,4608]{1,0:T(8,128)(2,1)S(1)} %shard_map.65.message.refs_4_), channel_id=1, source_target_pairs={{0,4},{4,8},{8,12},{5,1},{9,5},{13,9},{2,6},{6,10},{10,14},{7,3},{... | collective-permute-start | bytes 3538952 | tf_op jit(solution)/shard_map/ppermute | solution.py:515
  8.3 10.3 %collective-permute-start.1 = (s32[168,512]{1,0:T(8,128)S(1)}, s32[168,512]{1,0:T(8,128)S(1)}, u32[]{:S(2)}, u32[]{:S(2)}) collective-permute-start(s32[168,512]{1,0:T(8,128)S(1)} %shard_map.66), channel_id=1, source_target_pairs={{0,2},{2,0},{1,3},{3,1},{4,6},{6,4},{5,7},{7,5},{8,10},{10,8},{9,1... | collective-permute-start | bytes 1032200 | tf_op jit(solution)/shard_map/ppermute | solution.py:510
  12.1 12.4 %copy-start = (s32[3]{0:T(128)S(1)}, s32[3]{0:T(128)}, u32[]{:S(2)}) copy-start(s32[3]{0:T(128)} %pad_add_fusion.here) | copy-start | bytes 40
  12.1 12.3 %copy-start.1 = (s32[32]{0:T(128)S(1)}, s32[32]{0:T(128)}, u32[]{:S(2)}) copy-start(s32[32]{0:T(128)} %shard_map.64.table) | copy-start | bytes 388
  19.4 18.2 %collective-permute-start.2 = (bf16[128,4608]{1,0:T(8,128)(2,1)S(1)}, bf16[128,4608]{1,0:T(8,128)(2,1)S(1)}, u32[]{:S(2)}, u32[]{:S(2)}) collective-permute-start(bf16[128,4608]{1,0:T(8,128)(2,1)S(1)} %collective-permute-done.refs_1_.refs_5_.refs_0_.refs_3_), channel_id=1, source_target_pairs={{4,8},{8,12},{5,1},{9,5},{6,10},{10,14},{7,3},{11,7},{20,24},{24,2... | collective-permute-start | bytes 3538952 | tf_op jit(solution)/shard_map/ppermute | solution.py:515
  22.8 14.7 %collective-permute-start.3 = (s32[328,512]{1,0:T(8,128)S(1)}, s32[328,512]{1,0:T(8,128)S(1)}, u32[]{:S(2)}, u32[]{:S(2)}) collective-permute-start(s32[328,512]{1,0:T(8,128)S(1)} %get-tuple-element.27), channel_id=1, source_target_pairs={{0,2},{2,0},{1,3},{3,1},{4,6},{6,4},{5,7},{7,5},{8,10},{10,8},{9,1... | collective-permute-start | bytes 2015240 | tf_op jit(solution)/shard_map/ppermute | solution.py:510
  24.4 18.2 %collective-permute-start.5 = (bf16[128,4608]{1,0:T(8,128)(2,1)S(1)}, bf16[128,4608]{1,0:T(8,128)(2,1)S(1)}, u32[]{:S(2)}, u32[]{:S(2)}) collective-permute-start(bf16[128,4608]{1,0:T(8,128)(2,1)S(1)} %collective-permute-done.refs_1_.refs_5_.refs_0_.refs_3_), channel_id=1, source_target_pairs={{0,1},{1,0},{2,3},{3,2},{4,5},{5,4},{6,7},{7,6},{8,9},{9,8},{10,11... | collective-permute-start | bytes 3538952 | tf_op jit(solution)/shard_map/ppermute | solution.py:518
  37.5 17.1 %collective-permute-start.7 = (bf16[128,4608]{1,0:T(8,128)(2,1)S(1)}, bf16[128,4608]{1,0:T(8,128)(2,1)S(1)}, u32[]{:S(2)}, u32[]{:S(2)}) collective-permute-start(bf16[128,4608]{1,0:T(8,128)(2,1)S(1)} %collective-permute-done.2.refs_2_.refs_0_.refs_5_.refs_3_), channel_id=1, source_target_pairs={{8,12},{5,1},{10,14},{7,3},{24,28},{21,17},{26,30},{23,19}} | collective-permute-start | bytes 3538952 | tf_op jit(solution)/shard_map/ppermute | solution.py:515
  41.0 8.7 %collective-permute-start.4 = (s32[168,512]{1,0:T(8,128)S(1)}, s32[168,512]{1,0:T(8,128)S(1)}, u32[]{:S(2)}, u32[]{:S(2)}) collective-permute-start(s32[168,512]{1,0:T(8,128)S(1)} %get-tuple-element.30), channel_id=1, source_target_pairs={{0,2},{2,0},{1,3},{3,1},{4,6},{6,4},{5,7},{7,5},{8,10},{10,8},{9,1... | collective-permute-start | bytes 1032200 | tf_op jit(solution)/shard_map/ppermute | solution.py:510
  43.9 5.8 %collective-permute-start.6 = (f32[2,128,128]{2,1,0:T(8,128)S(1)}, f32[2,128,128]{2,1,0:T(8,128)S(1)}, u32[]{:S(2)}, u32[]{:S(2)}) collective-permute-start(f32[2,128,128]{2,1,0:T(8,128)S(1)} %shard_map.70.refs_2_), channel_id=1, source_target_pairs={{0,2},{2,0},{1,3},{3,1},{4,6},{6,4},{5,7},{7,5},{8,10},{10,8},{9,1... | collective-permute-start | bytes 393224 | tf_op jit(solution)/shard_map/ppermute | solution.py:510
  44.5 10.2 %collective-permute-start.8 = (bf16[128,4608]{1,0:T(8,128)(2,1)S(1)}, bf16[128,4608]{1,0:T(8,128)(2,1)S(1)}, u32[]{:S(2)}, u32[]{:S(2)}) collective-permute-start(bf16[128,4608]{1,0:T(8,128)(2,1)S(1)} %collective-permute-done.2.refs_2_.refs_0_.refs_5_.refs_3_), channel_id=1, source_target_pairs={{0,1},{1,0},{2,3},{3,2},{4,5},{5,4},{6,7},{7,6},{8,9},{9,8},{10,11... | collective-permute-start | bytes 3538952 | tf_op jit(solution)/shard_map/ppermute | solution.py:518
  54.6 3.1 %collective-permute-start.9 = (bf16[128,4608]{1,0:T(8,128)(2,1)S(1)}, bf16[128,4608]{1,0:T(8,128)(2,1)S(1)}, u32[]{:S(2)}, u32[]{:S(2)}) collective-permute-start(bf16[128,4608]{1,0:T(8,128)(2,1)S(1)} %collective-permute-done.7.refs_2_.refs_5_), channel_id=1, source_target_pairs={{0,1},{1,0},{2,3},{3,2},{4,5},{5,4},{6,7},{7,6},{8,9},{9,8},{10,11... | collective-permute-start | bytes 3538952 | tf_op jit(solution)/shard_map/ppermute | solution.py:518
  56.2 4.6 %collective-permute-start.11 = (f32[1,128,128]{2,1,0:T(8,128)S(1)}, f32[1,128,128]{2,1,0:T(8,128)S(1)}, u32[]{:S(2)}, u32[]{:S(2)}) collective-permute-start(f32[1,128,128]{2,1,0:T(8,128)S(1)} %shard_map.72.refs_1_), channel_id=1, source_target_pairs={{0,2},{2,0},{1,3},{3,1},{4,6},{6,4},{5,7},{7,5},{8,10},{10,8},{9,1... | collective-permute-start | bytes 196616 | tf_op jit(solution)/shard_map/ppermute | solution.py:510
  59.0 4.3 %collective-permute-start.10 = (f32[1,128,128]{2,1,0:T(8,128)S(1)}, f32[1,128,128]{2,1,0:T(8,128)S(1)}, u32[]{:S(2)}, u32[]{:S(2)}) collective-permute-start(f32[1,128,128]{2,1,0:T(8,128)S(1)} %shard_map.73.refs_1_), channel_id=1, source_target_pairs={{0,2},{2,0},{1,3},{3,1},{4,6},{6,4},{5,7},{7,5},{8,10},{10,8},{9,1... | collective-permute-start | bytes 196616 | tf_op jit(solution)/shard_map/ppermute | solution.py:510

commit v12 on v11

--- a/solution.py
+++ b/solution.py
@@ -42,12 +42,19 @@
     return order
 
 
-def buffer_owners(here, stages):
-    owners = []
+def views_of(refs, stages, layout, rank):
+    me, core = lax.axis_index("adapter"), lax.axis_index("dp")
+    refs, views = list(refs), []
     for stage in stages:
-        toward = jnp.where(here[1] == 0, -stage, stage)
-        owners += [here[0] + toward, here[0] - toward] if stage > 0 else [here[0]]
-    return owners
+        came, swapped = layout[stage]
+        toward = jnp.where(core == 0, -stage, stage)
+        for i in range(came):
+            views.append((refs.pop(0), 0, me + toward if stage > 0 else me, i))
+        for i in range(swapped):
+            ref = refs.pop(0)
+            for part in range(came // swapped):
+                views.append((ref, part * rank, me - toward, i + part))
+    return views
 
 
 def segment_of(table, k, j):
@@ -56,47 +63,45 @@
     return start, seg >= 0, table[k * ENTRIES + 2 + 2 * j]
 
 
-def message_kernel(down_ref, up_ref, o_ref, sems):
+def message_kernel(down_ref, up_ref, *refs):
+    outs, sems = refs[:-1], refs[-1]
+    rank = outs[0].shape[0]
     width = down_ref.shape[1]
-    columns = o_ref.shape[1] - width
+    columns = outs[0].shape[1] - width
     start = pl.multiple_of(lax.axis_index("tensor") * columns, columns)
-    rows = down_ref.shape[0] // PIECES
-    copies = [
-        pltpu.make_async_copy(
-            down_ref.at[pl.ds(p * rows, rows), :],
-            o_ref.at[pl.ds(p * rows, rows), pl.ds(0, width)],
-            sems.at[p],
-        )
-        for p in range(PIECES)
-    ]
-    copies.append(
-        pltpu.make_async_copy(
-            up_ref.at[:, pl.ds(start, columns)], o_ref.at[:, pl.ds(width, columns)], sems.at[PIECES]
-        )
-    )
+    copies = []
+    for i, out in enumerate(outs):
+        rows = pl.ds(i * rank, rank)
+        copies += [
+            pltpu.make_async_copy(down_ref.at[rows, :], out.at[:, pl.ds(0, width)], sems.at[0, i]),
+            pltpu.make_async_copy(
+                up_ref.at[rows, pl.ds(start, columns)], out.at[:, pl.ds(width, columns)], sems.at[1, i]
+            ),
+        ]
     for copy in copies:
         copy.start()
     for copy in copies:
         copy.wait()
 
 
-def message_call(down, up, columns):
+def message_call(down, up, columns, per_device):
     rows, width = down.shape
+    shape = jax.ShapeDtypeStruct((rows // per_device, width + columns), jnp.bfloat16)
     return pl.pallas_call(
         message_kernel,
         in_specs=[HBM, HBM],
-        out_specs=VMEM,
-        out_shape=jax.ShapeDtypeStruct((rows, width + columns), jnp.bfloat16),
-        scratch_shapes=[pltpu.SemaphoreType.DMA((PIECES + 1,))],
+        out_specs=[VMEM] * per_device,
+        out_shape=[shape] * per_device,
+        scratch_shapes=[pltpu.SemaphoreType.DMA((2, per_device))],
         compiler_params=params(8),
         cost_estimate=cost(0, 4 * rows * (width + columns)),
     )(down, up)
 
 
-def table_kernel(n_adapter, per_device, here, ids, slots, table):
+def table_kernel(n_adapter, per_device, ids, slots, table):
     seg_dev = ids.shape[0] // SEGMENT_ROWS
     used = [slots[ids[s * SEGMENT_ROWS]] for s in range(seg_dev)]
-    for k, owner in enumerate(arrival_order(here[0], n_adapter)):
+    for k, owner in enumerate(arrival_order(lax.axis_index("adapter"), n_adapter)):
         table[k * ENTRIES] = owner
         found, place = [jnp.int32(-1)] * MOST, [jnp.int32(0)] * MOST
         count = jnp.int32(0)
@@ -113,14 +118,14 @@
             table[k * ENTRIES + 2 + 2 * j] = place[j]
 
 
-def table_call(here, ids, slots, n_adapter, per_device):
+def table_call(ids, slots, n_adapter, per_device):
     return pl.pallas_call(
         functools.partial(table_kernel, n_adapter, per_device),
-        in_specs=[SMEM, SMEM, SMEM],
+        in_specs=[SMEM, SMEM],
         out_specs=SMEM,
         out_shape=jax.ShapeDtypeStruct((n_adapter * ENTRIES,), jnp.int32),
         cost_estimate=cost(0, 4 * ids.shape[0]),
-    )(here, ids, slots)
+    )(ids, slots)
 
 
 def diagonal():
@@ -259,7 +264,7 @@
         out_specs=[VMEM] * len(sizes),
         out_shape=[jax.ShapeDtypeStruct((coded_rows(n), columns), jnp.int32) for n in sizes],
         scratch_shapes=base_scratch(sum(sizes), width, columns),
-        compiler_params=params(24),
+        compiler_params=params(16),
         cost_estimate=cost(
             2 * rows * width * columns, 2 * rows * width + 2 * width * columns + 4 * rows * columns
         ),
@@ -279,32 +284,44 @@
         out_specs=VMEM,
         out_shape=jax.ShapeDtypeStruct(base.shape, base.dtype),
         compiler_params=params(8),
-        cost_estimate=cost(0, 4 * base.size),
+        cost_estimate=cost(20 * base.size, 12 * base.size),
     )(base, *coded)
 
 
-def shrink_into(o_ref, i, table, k, rows_of, buffers, owners, rank):
-    for buffer, whose in zip(buffers, owners):
-
-        @pl.when(whose == table[k * ENTRIES])
-        def _(buffer=buffer):
-            for j in range(MOST):
-                _, _, within = segment_of(table, k, j)
+def shrink_into(o_ref, at, table, k, rows_of, views, rank):
+    for j in range(MOST):
+        _, _, within = segment_of(table, k, j)
+        for ref, first, whose, i in views:
+
+            @pl.when((whose == table[k * ENTRIES]) & (within == i))
+            def _(j=j, ref=ref, first=first):
                 rows = rows_of(j)
-                width = rows.shape[1]
-                factor = buffer[pl.ds(pl.multiple_of(within * rank, rank), rank), :width]
-                o_ref[i, :, j * rank : (j + 1) * rank] = lax.dot_general(
-                    rows, factor, (((1,), (1,)), ((), ())), preferred_element_type=jnp.float32
+                o_ref[at, :, j * rank : (j + 1) * rank] = lax.dot_general(
+                    rows,
+                    ref[first : first + rank, : rows.shape[1]],
+                    (((1,), (1,)), ((), ())),
+                    preferred_element_type=jnp.float32,
                 )
+
+
+def join_copies(halves, whole, sems):
+    copies, rank = [], halves[0].shape[0]
+    for i, half in enumerate(halves):
+        copies.append(
+            pltpu.make_async_copy(half, whole.at[pl.ds(i * rank, rank), :], sems.at[i])
+        )
+        copies[-1].start()
+    return copies
 
 
 def stages_of(k):
     return range((k + 1) // 2, k + 1)
 
 
-def own_kernel(n_adapter, rank, table, here, x_ref, w_ref, message, *refs):
+def own_kernel(n_adapter, per_device, rank, table, x_ref, w_ref, *refs):
+    messages, refs = refs[:per_device], refs[per_device:]
     coded_refs, (o_ref, s_ref, kept_ref, x, w, sems, kept_sems) = refs[:-7], refs[-7:]
-    work = load_base(0, x.shape[0] // SEGMENT_ROWS, here[2], x_ref, w_ref, x, w, sems)
+    work = load_base(0, x.shape[0] // SEGMENT_ROWS, lax.axis_index("tensor"), x_ref, w_ref, x, w, sems)
     keeps = []
     for at, size, terms in work:
         o_ref[at : at + size, :] = block_product(x, w, at, size, terms)
@@ -323,62 +340,74 @@
         start, _, _ = segment_of(table, 0, j)
         return x[pl.ds(start, SEGMENT_ROWS), :]
 
-    shrink_into(s_ref, 0, table, 0, rows_of, [message], [here[0]], rank)
+    views = views_of(messages, [0], [(per_device, 0)], rank)
+    shrink_into(s_ref, 0, table, 0, rows_of, views, rank)
     for copy in keeps:
         copy.wait()
 
 
-def own_call(table, here, tokens, weight, message, coded, columns, n_adapter, rank):
+def own_call(table, tokens, weight, messages, coded, columns, n_adapter):
     rows, width = tokens.shape
-    segments = rows // SEGMENT_ROWS
-    return pl.pallas_call(
-        functools.partial(own_kernel, n_adapter, rank),
-        in_specs=[SMEM, SMEM, HBM, HBM] + [VMEM] * (1 + len(coded)),
+    per_device, rank = len(messages), messages[0].shape[0]
+    return pl.pallas_call(
+        functools.partial(own_kernel, n_adapter, per_device, rank),
+        in_specs=[SMEM, HBM, HBM] + [VMEM] * (per_device + len(coded)),
         out_specs=[VMEM] * 3,
         out_shape=[
             jax.ShapeDtypeStruct((rows, columns), jnp.float32),
             jax.ShapeDtypeStruct((1, SEGMENT_ROWS, MOST * rank), jnp.float32),
             jax.ShapeDtypeStruct((n_adapter - 1, MOST, SEGMENT_ROWS, width), jnp.bfloat16),
         ],
-        scratch_shapes=base_scratch(segments, width, columns)
+        scratch_shapes=base_scratch(rows // SEGMENT_ROWS, width, columns)
         + [pltpu.SemaphoreType.DMA((n_adapter - 1, MOST))],
-        compiler_params=params(32),
+        compiler_params=params(20),
         cost_estimate=cost(
             2 * rows * width * columns, 2 * rows * width + 2 * width * columns + 4 * rows * columns
         ),
-    )(table, here, tokens, weight, message, *coded)
-
-
-def shrink_kernel(k, rank, at, table, here, kept_ref, *refs):
-    buffers, o_ref = refs[1 if at else 0 : -1], refs[-1]
-    if at:
-        o_ref[:at] = refs[0][...]
-    owners = buffer_owners(here, stages_of(k))
-    shrink_into(o_ref, at, table, k, lambda j: kept_ref[k - 1, j], buffers, owners, rank)
-
-
-def shrink_call(k, table, here, kept, before, buffers, rank):
+    )(table, tokens, weight, *messages, *coded)
+
+
+def shrink_kernel(k, rank, at, layout, n_halves, table, kept_ref, *refs):
+    before, refs = refs[: 1 if at else 0], refs[1 if at else 0 :]
+    halves, refs = refs[:n_halves], refs[n_halves:]
+    joins = []
+    if n_halves:
+        refs, whole_ref, sems = refs[:-2], refs[-2], refs[-1]
+        joins = join_copies(halves, whole_ref, sems)
+    buffers, o_ref = refs[:-1], refs[-1]
+    for r in before:
+        o_ref[:at] = r[...]
+    views = views_of(buffers, stages_of(k), layout, rank)
+    shrink_into(o_ref, at, table, k, lambda j: kept_ref[k - 1, j], views, rank)
+    for copy in joins:
+        copy.wait()
+
+
+def shrink_call(k, table, kept, before, halves, buffers, layout, rank):
     width = kept.shape[3]
     at = sum(b.shape[0] for b in before)
-    return pl.pallas_call(
-        functools.partial(shrink_kernel, k, rank, at),
-        in_specs=[SMEM, SMEM, VMEM] + [VMEM] * (len(before) + len(buffers)),
-        out_specs=VMEM,
-        out_shape=jax.ShapeDtypeStruct((at + 1, SEGMENT_ROWS, MOST * rank), jnp.float32),
-        compiler_params=params(16),
+    shapes = [jax.ShapeDtypeStruct((at + 1, SEGMENT_ROWS, MOST * rank), jnp.float32)]
+    if halves:
+        shapes.append(jax.ShapeDtypeStruct((len(halves) * rank, halves[0].shape[1]), jnp.bfloat16))
+    return pl.pallas_call(
+        functools.partial(shrink_kernel, k, rank, at, layout, len(halves)),
+        in_specs=[SMEM] + [VMEM] * (1 + len(before) + len(halves) + len(buffers)),
+        out_specs=[VMEM] * len(shapes),
+        out_shape=shapes,
+        scratch_shapes=[pltpu.SemaphoreType.DMA((len(halves),))] if halves else [],
+        compiler_params=params(4),
         cost_estimate=cost(MOST * 2 * SEGMENT_ROWS * width * 256, 4 * SEGMENT_ROWS * width),
-    )(table, here, kept, *before, *buffers)
-
-
-def fetch_up(up, at, table, k, j, buffers, owners, rank):
+    )(table, kept, *before, *halves, *buffers)
+
+
+def fetch_up(up, at, table, k, j, views, rank):
     columns = up.shape[2]
     _, _, within = segment_of(table, k, j)
-    for buffer, whose in zip(buffers, owners):
-
-        @pl.when(whose == table[k * ENTRIES])
-        def _(buffer=buffer):
-            first = buffer.shape[1] - columns
-            factor = buffer[pl.ds(pl.multiple_of(within * rank, rank), rank), first:]
+    for ref, first, whose, i in views:
+
+        @pl.when((whose == table[k * ENTRIES]) & (within == i))
+        def _(ref=ref, first=first):
+            factor = ref[first : first + rank, ref.shape[1] - columns :]
             up[at, :rank, :] = factor
             up[at, rank:, :] = factor
 
@@ -395,18 +424,15 @@
 LATE = 2
 
 
-def early_kernel(n_adapter, n_tensor, rank, table, here, *refs):
+def early_kernel(n_adapter, n_tensor, rank, layout, n_buffers, table, *refs):
     first = n_adapter - LATE
-    n_buffers = 2 * first - 1
     base_ref, coded_refs, refs = refs[0], refs[1:n_tensor], refs[n_tensor:]
     shrinks, refs = refs[: -4 - n_buffers], refs[-4 - n_buffers :]
     buffers, (o_ref, rest_ref, up, total) = refs[:-4], refs[-4:]
+    views = views_of(buffers, range(first), layout, rank)
     for k in range(first):
-        at = 0 if k == 0 else 2 * stages_of(k)[0] - 1
-        to = 2 * k + 1
-        owners = buffer_owners(here, stages_of(k))
         for j in range(MOST):
-            fetch_up(up, k * MOST + j, table, k, j, buffers[at:to], owners, rank)
+            fetch_up(up, k * MOST + j, table, k, j, views, rank)
     shares = []
     for call in range(len(shrinks) // n_tensor):
         share = shrinks[call * n_tensor][...]
@@ -431,11 +457,11 @@
                 )
 
 
-def early(n_adapter, n_tensor, table, here, base, coded, shrinks, buffers, rank):
+def early(n_adapter, n_tensor, table, base, coded, shrinks, buffers, layout, rank):
     rows, columns = base.shape
     return pl.pallas_call(
-        functools.partial(early_kernel, n_adapter, n_tensor, rank),
-        in_specs=[SMEM] * 2 + [VMEM] * (1 + len(coded) + len(shrinks) + len(buffers)),
+        functools.partial(early_kernel, n_adapter, n_tensor, rank, layout, len(buffers)),
+        in_specs=[SMEM] + [VMEM] * (1 + len(coded) + len(shrinks) + len(buffers)),
         out_specs=[VMEM, VMEM],
         out_shape=[
             jax.ShapeDtypeStruct((rows, columns), jnp.bfloat16),
@@ -447,19 +473,19 @@
         ],
         compiler_params=params(16),
         cost_estimate=cost(6 * rows * rank * columns, (4 * n_tensor + 2) * rows * columns),
-    )(table, here, base, *coded, *shrinks, *buffers)
-
-
-def late_kernel(k, number, n_tensor, rank, table, here, *refs):
+    )(table, base, *coded, *shrinks, *buffers)
+
+
+def late_kernel(k, number, n_tensor, rank, layout, table, *refs):
     rest_ref, shrinks, refs = refs[0], refs[1 : 1 + n_tensor], refs[1 + n_tensor :]
     buffers, (_, o_ref, up, out, sems) = refs[:-5], refs[-5:]
-    owners = buffer_owners(here, stages_of(k))
+    views = views_of(buffers, stages_of(k), layout, rank)
     share = shrinks[0][0]
     for r in shrinks[1:]:
         share = share + r[0]
     stores = []
     for j in range(MOST):
-        fetch_up(up, j, table, k, j, buffers, owners, rank)
+        fetch_up(up, j, table, k, j, views, rank)
         start, used, _ = segment_of(table, k, j)
         lora = up_product(share, j, up[j], rank)
         out[j] = (rest_ref[number, j] + adapter_scale * lora).astype(jnp.bfloat16)
@@ -470,11 +496,11 @@
         pl.when(used)(store.wait)
 
 
-def late(k, number, n_tensor, table, here, rest, shrinks, buffers, value, rank):
+def late(k, number, n_tensor, table, rest, shrinks, buffers, value, layout, rank):
     rows, columns = value.shape
     return pl.pallas_call(
-        functools.partial(late_kernel, k, number, n_tensor, rank),
-        in_specs=[SMEM] * 2 + [VMEM] * (1 + len(shrinks) + len(buffers)) + [ANY],
+        functools.partial(late_kernel, k, number, n_tensor, rank, layout),
+        in_specs=[SMEM] + [VMEM] * (1 + len(shrinks) + len(buffers)) + [ANY],
         out_specs=ANY,
         out_shape=jax.ShapeDtypeStruct((rows, columns), jnp.bfloat16),
         scratch_shapes=[
@@ -482,12 +508,12 @@
             pltpu.VMEM((MOST, SEGMENT_ROWS, columns), jnp.bfloat16),
             pltpu.SemaphoreType.DMA((MOST,)),
         ],
-        input_output_aliases={3 + len(shrinks) + len(buffers): 0},
+        input_output_aliases={2 + len(shrinks) + len(buffers): 0},
         compiler_params=params(8),
         cost_estimate=cost(
             6 * MOST * SEGMENT_ROWS * rank * columns, 8 * MOST * SEGMENT_ROWS * columns
         ),
-    )(table, here, rest, *shrinks, *buffers, value)
+    )(table, rest, *shrinks, *buffers, value)
 
 
 def after(array, *others):
@@ -501,8 +527,6 @@
     per_device, _, rank = adapter_down_weight.shape
     n_adapter = lax.axis_size("adapter")
     n_tensor = lax.axis_size("tensor")
-    me_t = lax.axis_index("tensor")
-    here = jnp.stack([lax.axis_index("adapter"), lax.axis_index("dp"), me_t])
     columns = value_weight.shape[1] // n_tensor
 
     def swap_tensor(array, step):
@@ -522,66 +546,81 @@
     tokens, value_weight, down, up = (
         pltpu.with_memory_space_constraint(a, pltpu.HBM) for a in (tokens, value_weight, down, up)
     )
-    message = message_call(down, up, columns)
-    table = table_call(here, row_adapter_index, adapter_slot_of, n_adapter, per_device)
-
-    buffers, shrinks = [[message]], []
+    messages = message_call(down, up, columns, per_device)
+    table = table_call(row_adapter_index, adapter_slot_of, n_adapter, per_device)
+    last = n_adapter - 1
+    buffers, shrinks = [list(messages)], []
+    layout = [(per_device, 0)] + [(per_device, per_device)] * last
 
     def buffers_of(stages):
         return [b for stage in stages for b in buffers[stage]]
 
-    def shrink(k, kept, before):
-        return shrink_call(k, table, here, kept, before, buffers_of(stages_of(k)), rank)
+    def shrink(k, kept, before=(), halves=()):
+        mine = buffers_of(stages_of(k))
+        return shrink_call(k, table, kept, list(before), list(halves), mine, layout, rank)
 
     def add_shrink(mine):
         shrinks.extend([mine] + [swap_tensor(mine, step) for step in range(1, n_tensor)])
 
-    held = along_line(message, 1)
     others = range(1, n_tensor)
 
-    def sent_for(step, chunks):
+    def sent_for(step, chunks, rows):
         sizes = [number for _, number in chunks]
-        return sent_call(tokens, value_weight, step, n_tensor, columns, chunks[0][0], sizes)
-
-    parts = [[sent_for(step, CHUNKS[:1])[0] for step in others]]
-    rest_parts = [sent_for(step, CHUNKS[1:]) for step in others]
-    parts += [[p[i] for p in rest_parts] for i in range(len(CHUNKS) - 1)]
-    sent = [[swap_tensor(p, step) for step, p in zip(others, parts[0])]]
-    last = n_adapter - 1
-    done = [table] + [p for group in parts for p in group] + sent[0]
+        return sent_call(rows, value_weight, step, n_tensor, columns, chunks[0][0], sizes)
+
+    def send(parts, *ahead):
+        return [swap_tensor(after(p, *ahead), step) for step, p in zip(others, parts)]
+
+    held = [along_line(m, 1) for m in messages]
+    part_a = [sent_for(step, CHUNKS[:1], tokens)[0] for step in others]
+    sent = [send(part_a)]
+    first = after(held[0], table, *part_a)
+    rest_parts = [sent_for(step, CHUNKS[1:], after(tokens, first)) for step in others]
+    parts = [[p[i] for p in rest_parts] for i in range(len(CHUNKS) - 1)]
+    part_b = [p for group in parts for p in group]
+    held1 = held
     for stage in range(1, last):
-        came = after(held, *done)
-        held = along_line(came, stage + 1)
-        buffers.append([came, swap_cores(came)])
-        if stage < len(CHUNKS):
-            sent.append([swap_tensor(after(p, came), step) for step, p in zip(others, parts[stage])])
+        came = held
+        if stage == 1:
+            came = [first] + [after(h, *part_b, *sent[0]) for h in held[1:]]
+            sent.append(send(parts[0], *came))
+        if stage == 2:
+            came = held[:1] + [after(h, base) for h in held[1:]]
+            sent.append(send(parts[1], base, *sent[1]))
+        held = [along_line(c, stage + 1) for c in came]
         if stage == 1:
             base, before, kept = own_call(
-                after(table, came), here, tokens, value_weight, message, sent[0], columns, n_adapter, rank
+                after(table, held[0]),
+                tokens,
+                value_weight,
+                messages,
+                sent[0],
+                columns,
+                n_adapter,
             )
-            done = sent[1] + [base]
         else:
+            ready = kept
             if stage == 2:
-                base = add_call(1, after(base, came), sent[1])
-            before = shrink(stage - 1, after(kept, came), [before])
-            done = []
+                base = add_call(1, after(base, held[0], *came), sent[1])
+                ready = after(kept, base)
+            before = shrink(stage - 1, ready, [before])[0]
+        buffers.append([*came, *[swap_cores(h) for h in (held1 if stage == 1 else came)]])
     add_shrink(before)
     value, remaining = early(
         n_adapter,
         n_tensor,
         table,
-        here,
         base,
         sent[2],
         shrinks,
         buffers_of(range(last - 1)),
+        layout,
         rank,
     )
-    came = after(held, value)
-    buffers.append([came, swap_cores(came)])
-    ready = after(kept, came)
+    buffers.append([*held, *[swap_cores(after(h, before, *sent[2])) for h in held]])
+    ready = after(kept, *held)
     for k in (last - 1, last):
-        mine = shrink(k, ready, [])
+        mine = shrink(k, ready)[0]
         add_shrink(mine)
         ready = after(kept, mine)
     for number, k in enumerate((last - 1, last)):
@@ -590,11 +629,11 @@
             number,
             n_tensor,
             table,
-            here,
             remaining,
             shrinks[(number - LATE) * n_tensor :][:n_tensor],
             buffers_of(stages_of(k)),
             value,
+            layout,
             rank,
         )
     return value

time: 66.4 us -> 65.1 us (0.980)
  the two profiles are of different devices: /device:TPU:16 before, /device:TPU:8 now
where the time goes in v12:
time: 65.1 us; the launch traced here: 64.8 us
  Pallas kernels  33.6 us (52%)
  starting transfers between devices  23.5 us (36%)
  waiting for transfers between devices  7.3 us (11%)
    ppermute x6, starting transfers between devices, along_line(): return lax.ppermute(array, ('adapter', 'dp'), up + down)  15.1 us
    pallas_call x2, Pallas kernels, sent_call(): pl.pallas_call(functools.partial(sent_kernel, first, sizes, step, n_tenso...  10.2 us
    pallas_call x1, Pallas kernels, own_call(): pl.pallas_call(functools.partial(own_kernel, n_adapter, per_device, rank)...  9.37 us
    ppermute x6, waiting for transfers between devices, swap_tensor(): return lax.ppermute(array, 'tensor', pairs)  7.27 us
    ppermute x6, starting transfers between devices, swap_tensor(): return lax.ppermute(array, 'tensor', pairs)  6.34 us
    pallas_call x3, Pallas kernels, shrink_call(): pl.pallas_call(functools.partial(shrink_kernel, k, rank, at, layout, len(...  4.82 us
    pallas_call x2, Pallas kernels, late(): pl.pallas_call(functools.partial(late_kernel, k, number, n_tensor, rank,...  3.53 us
    pallas_call x1, Pallas kernels, early(): pl.pallas_call(functools.partial(early_kernel, n_adapter, n_tensor, rank,...  2.72 us
  transfers between devices with their start and end apart: 18, of which 3 were waited for; matrix products, arithmetic and copies ran while one was open for 0% of the time, Pallas kernels for 47%

profile of v12, /device:TPU:8, one launch (start us, length us, event | category | flops | bytes accessed | tf_op | source)
XLA Modules:
  0.0 64.8 jit_solution(7437703267583904050)
XLA Ops:
  0.0 1.3 %shard_map.65 = (bf16[64,4608]{1,0:T(8,128)(2,1)S(1)}, bf16[64,4608]{1,0:T(8,128)(2,1)S(1)}) custom-call(bf16[128,4096]{1,0:T(8,128)(2,1)} %bitcast.4, bf16[128,1024]{1,0:T(8,128)(2,1)} %bitcast.5), custom_call_target="tpu_custom_call" | custom-call | bytes 2359296 | tf_op jit(solution)/shard_map/pallas_call | solution.py:90
  1.3 3.5 %collective-permute-start = (bf16[64,4608]{1,0:T(8,128)(2,1)S(1)}, bf16[64,4608]{1,0:T(8,128)(2,1)S(1)}, u32[]{:S(2)}, u32[]{:S(2)}) collective-permute-start(bf16[64,4608]{1,0:T(8,128)(2,1)S(1)} %get-tuple-element.27.refs_0_.refs_4_), channel_id=1, source_target_pairs={{0,4},{4,8},{8,12},{5,1},{9,5},{13,9},{2,6},{6,10},{10,14},{7,3},{... | collective-permute-start | bytes 1769480 | tf_op jit(solution)/shard_map/ppermute | solution.py:539
  4.8 3.5 %collective-permute-start.4 = (bf16[64,4608]{1,0:T(8,128)(2,1)S(1)}, bf16[64,4608]{1,0:T(8,128)(2,1)S(1)}, u32[]{:S(2)}, u32[]{:S(2)}) collective-permute-start(bf16[64,4608]{1,0:T(8,128)(2,1)S(1)} %get-tuple-element.30.refs_1_.refs_5_), channel_id=1, source_target_pairs={{0,4},{4,8},{8,12},{5,1},{9,5},{13,9},{2,6},{6,10},{10,14},{7,3},{... | collective-permute-start | bytes 1769480 | tf_op jit(solution)/shard_map/ppermute | solution.py:539
  8.2 1.4 %shard_map.64.table = s32[32]{0:T(128)} custom-call(s32[1024]{0:T(1024)} %ids.1, s32[8]{0:T(128)} %slots.1), custom_call_target="tpu_custom_call" | custom-call | bytes 4096 | tf_op jit(solution)/shard_map/pallas_call | solution.py:122
  9.7 3.6 %shard_map.66 = s32[168,512]{1,0:T(8,128)S(1)} custom-call(bf16[1024,4096]{1,0:T(8,128)(2,1)} %x_ref.4, bf16[4096,1024]{1,0:T(8,128)(2,1)} %w_ref.5), custom_call_target="tpu_custom_call" | custom-call | flops 1073741824 | bytes 6815744 | tf_op jit(solution)/shard_map/pallas_call | solution.py:261
  13.3 0.0 copy-start
  13.3 0.0 collective-permute-done.refs_1_.refs_6_.refs_0_.refs_3_
  13.3 3.3 %collective-permute-start.1 = (bf16[64,4608]{1,0:T(8,128)(2,1)S(1)}, bf16[64,4608]{1,0:T(8,128)(2,1)S(1)}, u32[]{:S(2)}, u32[]{:S(2)}) collective-permute-start(bf16[64,4608]{1,0:T(8,128)(2,1)S(1)} %collective-permute-done.refs_1_.refs_6_.refs_0_.refs_3_), channel_id=1, source_target_pairs={{4,8},{8,12},{5,1},{9,5},{6,10},{10,14},{7,3},{11,7},{20,24},{24,2... | collective-permute-start | bytes 1769480 | tf_op jit(solution)/shard_map/ppermute | solution.py:539
  16.6 1.6 %collective-permute-start.2 = (s32[168,512]{1,0:T(8,128)S(1)}, s32[168,512]{1,0:T(8,128)S(1)}, u32[]{:S(2)}, u32[]{:S(2)}) collective-permute-start(s32[168,512]{1,0:T(8,128)S(1)} %shard_map.66), channel_id=1, source_target_pairs={{0,2},{2,0},{1,3},{3,1},{4,6},{6,4},{5,7},{7,5},{8,10},{10,8},{9,1... | collective-permute-start | bytes 1032200 | tf_op jit(solution)/shard_map/ppermute | solution.py:534
  18.1 6.6 %shard_map.68 = (s32[328,512]{1,0:T(8,128)S(1)}, s32[168,512]{1,0:T(8,128)S(1)}) custom-call(bf16[1024,4096]{1,0:T(8,128)(2,1)} %x_ref.4, bf16[4096,1024]{1,0:T(8,128)(2,1)} %w_ref.5), custom_call_target="tpu_custom_call" | custom-call | flops 3221225472 | bytes 12058624 | tf_op jit(solution)/shard_map/pallas_call | solution.py:261
  24.7 0.0 collective-permute-done.2.refs_2_
  24.7 0.0 collective-permute-done.4.refs_2_.refs_7_.refs_1_.refs_4_
  24.7 3.5 %collective-permute-start.5 = (bf16[64,4608]{1,0:T(8,128)(2,1)S(1)}, bf16[64,4608]{1,0:T(8,128)(2,1)S(1)}, u32[]{:S(2)}, u32[]{:S(2)}) collective-permute-start(bf16[64,4608]{1,0:T(8,128)(2,1)S(1)} %collective-permute-done.4.refs_2_.refs_7_.refs_1_.refs_4_), channel_id=1, source_target_pairs={{4,8},{8,12},{5,1},{9,5},{6,10},{10,14},{7,3},{11,7},{20,24},{24,2... | collective-permute-start | bytes 1769480 | tf_op jit(solution)/shard_map/ppermute | solution.py:539
  28.2 1.0 %collective-permute-start.6 = (s32[328,512]{1,0:T(8,128)S(1)}, s32[328,512]{1,0:T(8,128)S(1)}, u32[]{:S(2)}, u32[]{:S(2)}) collective-permute-start(s32[328,512]{1,0:T(8,128)S(1)} %get-tuple-element.38), channel_id=1, source_target_pairs={{0,2},{2,0},{1,3},{3,1},{4,6},{6,4},{5,7},{7,5},{8,10},{10,8},{9,1... | collective-permute-start | bytes 2015240 | tf_op jit(solution)/shard_map/ppermute | solution.py:534
  29.2 0.0 collective-permute-start.8
  29.2 0.5 collective-permute-start.9
  29.7 0.0 collective-permute-done.1.refs_4_.refs_0_.refs_7_.refs_3_
  29.7 0.7 %collective-permute-start.3 = (bf16[64,4608]{1,0:T(8,128)(2,1)S(1)}, bf16[64,4608]{1,0:T(8,128)(2,1)S(1)}, u32[]{:S(2)}, u32[]{:S(2)}) collective-permute-start(bf16[64,4608]{1,0:T(8,128)(2,1)S(1)} %collective-permute-done.1.refs_4_.refs_0_.refs_7_.refs_3_), channel_id=1, source_target_pairs={{8,12},{5,1},{10,14},{7,3},{24,28},{21,17},{26,30},{23,19}} | collective-permute-start | bytes 1769480 | tf_op jit(solution)/shard_map/ppermute | solution.py:539
  30.4 0.0 copy-done
  30.5 9.4 %shard_map.67 = (f32[1024,512]{1,0:T(8,128)S(1)}, f32[1,128,128]{2,1,0:T(8,128)S(1)}, bf16[3,2,128,4096]{3,2,1,0:T(8,128)(2,1)S(1)}) custom-call(s32[32]{0:T(128)S(1)} %copy-done, bf16[1024,4096]{1,0:T(8,128)(2,1)} %x_ref.4, bf16[4096,1024]{1,0:T(8,128)(2,1)} %w_ref.5, bf16[64,4608]{1,0:T(8,128)(2,1)S(1)} %get-tuple-element.27.refs_0_.refs_4_, ...), custom_call_target="tpu_custom_call" | custom-call | flops 4294967296 | bytes 14680064 | tf_op jit(solution)/shard_map/pallas_call | solution.py:352
  39.8 0.0 collective-permute-done.5.refs_5_.refs_1_.refs_8_.refs_4_
  39.8 0.7 %collective-permute-start.11 = (bf16[64,4608]{1,0:T(8,128)(2,1)S(1)}, bf16[64,4608]{1,0:T(8,128)(2,1)S(1)}, u32[]{:S(2)}, u32[]{:S(2)}) collective-permute-start(bf16[64,4608]{1,0:T(8,128)(2,1)S(1)} %collective-permute-done.5.refs_5_.refs_1_.refs_8_.refs_4_), channel_id=1, source_target_pairs={{8,12},{5,1},{10,14},{7,3},{24,28},{21,17},{26,30},{23,19}} | collective-permute-start | bytes 1769480 | tf_op jit(solution)/shard_map/ppermute | solution.py:539
  40.6 0.3 collective-permute-done.6.refs_0_
  40.8 0.9 %collective-permute-start.7 = (s32[168,512]{1,0:T(8,128)S(1)}, s32[168,512]{1,0:T(8,128)S(1)}, u32[]{:S(2)}, u32[]{:S(2)}) collective-permute-start(s32[168,512]{1,0:T(8,128)S(1)} %get-tuple-element.39), channel_id=1, source_target_pairs={{0,2},{2,0},{1,3},{3,1},{4,6},{6,4},{5,7},{7,5},{8,10},{10,8},{9,1... | collective-permute-start | bytes 1032200 | tf_op jit(solution)/shard_map/ppermute | solution.py:534
  41.7 0.0 collective-permute-done.3.refs_4_.refs_7_
  41.7 1.0 %collective-permute-start.13 = (bf16[64,4608]{1,0:T(8,128)(2,1)S(1)}, bf16[64,4608]{1,0:T(8,128)(2,1)S(1)}, u32[]{:S(2)}, u32[]{:S(2)}) collective-permute-start(bf16[64,4608]{1,0:T(8,128)(2,1)S(1)} %collective-permute-done.5.refs_5_.refs_1_.refs_8_.refs_4_), channel_id=1, source_target_pairs={{0,1},{1,0},{2,3},{3,2},{4,5},{5,4},{6,7},{7,6},{8,9},{9,8},{10,11... | collective-permute-start | bytes 1769480 | tf_op jit(solution)/shard_map/ppermute | solution.py:542
  42.7 0.3 shard_map.69.refs_0_
  43.0 0.0 collective-permute-done.8.refs_3_.refs_8_.refs_2_.refs_5_
  43.0 0.1 collective-permute-start.12
  43.1 0.0 collective-permute-done.9.refs_4_.refs_9_.refs_3_.refs_6_
  43.1 1.7 %shard_map.70.refs_2_ = f32[2,128,128]{2,1,0:T(8,128)S(1)} custom-call(s32[32]{0:T(128)S(1)} %copy-done, bf16[3,2,128,4096]{3,2,1,0:T(8,128)(2,1)S(1)} %get-tuple-element.45.kept_ref, f32[1,128,128]{2,1,0:T(8,128)S(1)} %get-tuple-element.42.refs_0_, bf16[64,4608]{1,0:T(8,128)(2,1)S(1)} %collective-permute-done.refs_1_.refs_6_.refs_0_.refs_3_, ...), custom_call_target="tpu_custom_call" | custom-call | flops 536870912 | bytes 2097152 | tf_op jit(solution)/shard_map/pallas_call | solution.py:392
  44.8 6.8 %collective-permute-done.7.refs_1_ = s32[168,512]{1,0:T(8,128)S(1)} collective-permute-done((s32[168,512]{1,0:T(8,128)S(1)}, s32[168,512]{1,0:T(8,128)S(1)}, u32[]{:S(2)}, u32[]{:S(2)}) %collective-permute-start.7) | collective-permute-done | bytes 344096 | tf_op jit(solution)/shard_map/ppermute | solution.py:534
  51.6 0.1 collective-permute-start.14
  51.8 0.0 collective-permute-done.11.refs_5_.refs_8_
  51.8 0.4 collective-permute-start.15
  52.2 0.7 %collective-permute-start.10 = (f32[2,128,128]{2,1,0:T(8,128)S(1)}, f32[2,128,128]{2,1,0:T(8,128)S(1)}, u32[]{:S(2)}, u32[]{:S(2)}) collective-permute-start(f32[2,128,128]{2,1,0:T(8,128)S(1)} %shard_map.70.refs_2_), channel_id=1, source_target_pairs={{0,2},{2,0},{1,3},{3,1},{4,6},{6,4},{5,7},{7,5},{8,10},{10,8},{9,1... | collective-permute-start | bytes 393224 | tf_op jit(solution)/shard_map/ppermute | solution.py:534
  52.9 0.0 collective-permute-done.12.refs_6_.refs_2_.refs_9_.refs_5_
  52.9 0.0 collective-permute-done.13.refs_7_.refs_3_.refs_10_.refs_6_
  52.9 1.6 %shard_map.72.refs_1_ = f32[1,128,128]{2,1,0:T(8,128)S(1)} custom-call(s32[32]{0:T(128)S(1)} %copy-done, bf16[3,2,128,4096]{3,2,1,0:T(8,128)(2,1)S(1)} %get-tuple-element.45.kept_ref, bf16[64,4608]{1,0:T(8,128)(2,1)S(1)} %collective-permute-done.refs_1_.refs_6_.refs_0_.refs_3_, bf16[64,4608]{1,0:T(8,128)(2,1)S(1)} %collective-permute-done.4.refs_2_.refs_7_.refs_1_.refs_4_, ...), custom_call_target="tpu_custom_call" | custom-call | flops 536870912 | bytes 2097152 | tf_op jit(solution)/shard_map/pallas_call | solution.py:392
  54.4 1.4 %collective-permute-start.17 = (f32[1,128,128]{2,1,0:T(8,128)S(1)}, f32[1,128,128]{2,1,0:T(8,128)S(1)}, u32[]{:S(2)}, u32[]{:S(2)}) collective-permute-start(f32[1,128,128]{2,1,0:T(8,128)S(1)} %shard_map.72.refs_1_), channel_id=1, source_target_pairs={{0,2},{2,0},{1,3},{3,1},{4,6},{6,4},{5,7},{7,5},{8,10},{10,8},{9,1... | collective-permute-start | bytes 196616 | tf_op jit(solution)/shard_map/ppermute | solution.py:534
  55.8 0.0 collective-permute-done.14.refs_6_.refs_9_
  55.8 0.0 collective-permute-done.15.refs_7_.refs_10_
  55.8 1.6 %shard_map.73.refs_1_ = f32[1,128,128]{2,1,0:T(8,128)S(1)} custom-call(s32[32]{0:T(128)S(1)} %copy-done, bf16[3,2,128,4096]{3,2,1,0:T(8,128)(2,1)S(1)} %get-tuple-element.45.kept_ref, bf16[64,4608]{1,0:T(8,128)(2,1)S(1)} %collective-permute-done.1.refs_4_.refs_0_.refs_7_.refs_3_, bf16[64,4608]{1,0:T(8,128)(2,1)S(1)} %collective-permute-done.5.refs_5_.refs_1_.refs_8_.refs_4_, ...), custom_call_target="tpu_custom_call" | custom-call | flops 536870912 | bytes 2097152 | tf_op jit(solution)/shard_map/pallas_call | solution.py:392
  57.4 0.8 %collective-permute-start.16 = (f32[1,128,128]{2,1,0:T(8,128)S(1)}, f32[1,128,128]{2,1,0:T(8,128)S(1)}, u32[]{:S(2)}, u32[]{:S(2)}) collective-permute-start(f32[1,128,128]{2,1,0:T(8,128)S(1)} %shard_map.73.refs_1_), channel_id=1, source_target_pairs={{0,2},{2,0},{1,3},{3,1},{4,6},{6,4},{5,7},{7,5},{8,10},{10,8},{9,1... | collective-permute-start | bytes 196616 | tf_op jit(solution)/shard_map/ppermute | solution.py:534
  58.2 0.2 collective-permute-done.10.refs_3_
  58.4 2.7 %shard_map.71 = (bf16[1024,512]{1,0:T(8,128)(2,1)}, f32[2,2,128,512]{3,2,1,0:T(8,128)S(1)}) custom-call(s32[32]{0:T(128)S(1)} %copy-done, f32[1024,512]{1,0:T(8,128)S(1)} %shard_map.69.refs_0_, s32[168,512]{1,0:T(8,128)S(1)} %collective-permute-done.7.refs_1_, f32[2,128,128]{2,1,0:T(8,128)S(1)} %shard_map.70.refs_2_, ...), custom_call_target="tpu_custom_call" | custom-call | flops 201326592 | bytes 5242880 | tf_op jit(solution)/shard_map/pallas_call | solution.py:462
  61.1 0.0 collective-permute-done.17.refs_2_
  61.1 1.8 %shard_map.74.refs_11_ = bf16[1024,512]{1,0:T(8,128)(2,1)} custom-call(s32[32]{0:T(128)S(1)} %copy-done, f32[2,2,128,512]{3,2,1,0:T(8,128)S(1)} %get-tuple-element.43.refs_0_, f32[1,128,128]{2,1,0:T(8,128)S(1)} %shard_map.72.refs_1_, f32[1,128,128]{2,1,0:T(8,128)S(1)} %collective-permute-done.17.refs_2_, ...), custom_call_target="tpu_custom_call", output_to_operand_aliasing={{}: (12, {})} | custom-call | flops 50331648 | bytes 1048576 | tf_op jit(solution)/shard_map/pallas_call | solution.py:501
  62.8 0.0 collective-permute-done.16.refs_2_
  62.9 1.8 %shard_map.75 = bf16[1024,512]{1,0:T(8,128)(2,1)} custom-call(s32[32]{0:T(128)S(1)} %copy-done, f32[2,2,128,512]{3,2,1,0:T(8,128)S(1)} %get-tuple-element.43.refs_0_, f32[1,128,128]{2,1,0:T(8,128)S(1)} %shard_map.73.refs_1_, f32[1,128,128]{2,1,0:T(8,128)S(1)} %collective-permute-done.16.refs_2_, ...), custom_call_target="tpu_custom_call", output_to_operand_aliasing={{}: (12, {})} | custom-call | flops 50331648 | bytes 1048576 | tf_op jit(solution)/shard_map/pallas_call | solution.py:501
Async XLA Ops:
  1.3 12.0 %collective-permute-start = (bf16[64,4608]{1,0:T(8,128)(2,1)S(1)}, bf16[64,4608]{1,0:T(8,128)(2,1)S(1)}, u32[]{:S(2)}, u32[]{:S(2)}) collective-permute-start(bf16[64,4608]{1,0:T(8,128)(2,1)S(1)} %get-tuple-element.27.refs_0_.refs_4_), channel_id=1, source_target_pairs={{0,4},{4,8},{8,12},{5,1},{9,5},{13,9},{2,6},{6,10},{10,14},{7,3},{... | collective-permute-start | bytes 1769480 | tf_op jit(solution)/shard_map/ppermute | solution.py:539
  4.8 20.0 %collective-permute-start.4 = (bf16[64,4608]{1,0:T(8,128)(2,1)S(1)}, bf16[64,4608]{1,0:T(8,128)(2,1)S(1)}, u32[]{:S(2)}, u32[]{:S(2)}) collective-permute-start(bf16[64,4608]{1,0:T(8,128)(2,1)S(1)} %get-tuple-element.30.refs_1_.refs_5_), channel_id=1, source_target_pairs={{0,4},{4,8},{8,12},{5,1},{9,5},{13,9},{2,6},{6,10},{10,14},{7,3},{... | collective-permute-start | bytes 1769480 | tf_op jit(solution)/shard_map/ppermute | solution.py:539
  13.3 17.2 %copy-start = (s32[32]{0:T(128)S(1)}, s32[32]{0:T(128)}, u32[]{:S(2)}) copy-start(s32[32]{0:T(128)} %shard_map.64.table) | copy-start | bytes 388
  13.3 16.5 %collective-permute-start.1 = (bf16[64,4608]{1,0:T(8,128)(2,1)S(1)}, bf16[64,4608]{1,0:T(8,128)(2,1)S(1)}, u32[]{:S(2)}, u32[]{:S(2)}) collective-permute-start(bf16[64,4608]{1,0:T(8,128)(2,1)S(1)} %collective-permute-done.refs_1_.refs_6_.refs_0_.refs_3_), channel_id=1, source_target_pairs={{4,8},{8,12},{5,1},{9,5},{6,10},{10,14},{7,3},{11,7},{20,24},{24,2... | collective-permute-start | bytes 1769480 | tf_op jit(solution)/shard_map/ppermute | solution.py:539
  16.6 8.1 %collective-permute-start.2 = (s32[168,512]{1,0:T(8,128)S(1)}, s32[168,512]{1,0:T(8,128)S(1)}, u32[]{:S(2)}, u32[]{:S(2)}) collective-permute-start(s32[168,512]{1,0:T(8,128)S(1)} %shard_map.66), channel_id=1, source_target_pairs={{0,2},{2,0},{1,3},{3,1},{4,6},{6,4},{5,7},{7,5},{8,10},{10,8},{9,1... | collective-permute-start | bytes 1032200 | tf_op jit(solution)/shard_map/ppermute | solution.py:534
  24.7 15.1 %collective-permute-start.5 = (bf16[64,4608]{1,0:T(8,128)(2,1)S(1)}, bf16[64,4608]{1,0:T(8,128)(2,1)S(1)}, u32[]{:S(2)}, u32[]{:S(2)}) collective-permute-start(bf16[64,4608]{1,0:T(8,128)(2,1)S(1)} %collective-permute-done.4.refs_2_.refs_7_.refs_1_.refs_4_), channel_id=1, source_target_pairs={{4,8},{8,12},{5,1},{9,5},{6,10},{10,14},{7,3},{11,7},{20,24},{24,2... | collective-permute-start | bytes 1769480 | tf_op jit(solution)/shard_map/ppermute | solution.py:539
  28.2 12.6 %collective-permute-start.6 = (s32[328,512]{1,0:T(8,128)S(1)}, s32[328,512]{1,0:T(8,128)S(1)}, u32[]{:S(2)}, u32[]{:S(2)}) collective-permute-start(s32[328,512]{1,0:T(8,128)S(1)} %get-tuple-element.38), channel_id=1, source_target_pairs={{0,2},{2,0},{1,3},{3,1},{4,6},{6,4},{5,7},{7,5},{8,10},{10,8},{9,1... | collective-permute-start | bytes 2015240 | tf_op jit(solution)/shard_map/ppermute | solution.py:534
  29.2 13.8 %collective-permute-start.8 = (bf16[64,4608]{1,0:T(8,128)(2,1)S(1)}, bf16[64,4608]{1,0:T(8,128)(2,1)S(1)}, u32[]{:S(2)}, u32[]{:S(2)}) collective-permute-start(bf16[64,4608]{1,0:T(8,128)(2,1)S(1)} %collective-permute-done.refs_1_.refs_6_.refs_0_.refs_3_), channel_id=1, source_target_pairs={{0,1},{1,0},{2,3},{3,2},{4,5},{5,4},{6,7},{7,6},{8,9},{9,8},{10,11... | collective-permute-start | bytes 1769480 | tf_op jit(solution)/shard_map/ppermute | solution.py:542
  29.2 13.9 %collective-permute-start.9 = (bf16[64,4608]{1,0:T(8,128)(2,1)S(1)}, bf16[64,4608]{1,0:T(8,128)(2,1)S(1)}, u32[]{:S(2)}, u32[]{:S(2)}) collective-permute-start(bf16[64,4608]{1,0:T(8,128)(2,1)S(1)} %collective-permute-done.4.refs_2_.refs_7_.refs_1_.refs_4_), channel_id=1, source_target_pairs={{0,1},{1,0},{2,3},{3,2},{4,5},{5,4},{6,7},{7,6},{8,9},{9,8},{10,11... | collective-permute-start | bytes 1769480 | tf_op jit(solution)/shard_map/ppermute | solution.py:542
  29.7 12.0 %collective-permute-start.3 = (bf16[64,4608]{1,0:T(8,128)(2,1)S(1)}, bf16[64,4608]{1,0:T(8,128)(2,1)S(1)}, u32[]{:S(2)}, u32[]{:S(2)}) collective-permute-start(bf16[64,4608]{1,0:T(8,128)(2,1)S(1)} %collective-permute-done.1.refs_4_.refs_0_.refs_7_.refs_3_), channel_id=1, source_target_pairs={{8,12},{5,1},{10,14},{7,3},{24,28},{21,17},{26,30},{23,19}} | collective-permute-start | bytes 1769480 | tf_op jit(solution)/shard_map/ppermute | solution.py:539
  39.8 11.9 %collective-permute-start.11 = (bf16[64,4608]{1,0:T(8,128)(2,1)S(1)}, bf16[64,4608]{1,0:T(8,128)(2,1)S(1)}, u32[]{:S(2)}, u32[]{:S(2)}) collective-permute-start(bf16[64,4608]{1,0:T(8,128)(2,1)S(1)} %collective-permute-done.5.refs_5_.refs_1_.refs_8_.refs_4_), channel_id=1, source_target_pairs={{8,12},{5,1},{10,14},{7,3},{24,28},{21,17},{26,30},{23,19}} | collective-permute-start | bytes 1769480 | tf_op jit(solution)/shard_map/ppermute | solution.py:539
  40.8 10.8 %collective-permute-start.7 = (s32[168,512]{1,0:T(8,128)S(1)}, s32[168,512]{1,0:T(8,128)S(1)}, u32[]{:S(2)}, u32[]{:S(2)}) collective-permute-start(s32[168,512]{1,0:T(8,128)S(1)} %get-tuple-element.39), channel_id=1, source_target_pairs={{0,2},{2,0},{1,3},{3,1},{4,6},{6,4},{5,7},{7,5},{8,10},{10,8},{9,1... | collective-permute-start | bytes 1032200 | tf_op jit(solution)/shard_map/ppermute | solution.py:534
  41.7 11.2 %collective-permute-start.13 = (bf16[64,4608]{1,0:T(8,128)(2,1)S(1)}, bf16[64,4608]{1,0:T(8,128)(2,1)S(1)}, u32[]{:S(2)}, u32[]{:S(2)}) collective-permute-start(bf16[64,4608]{1,0:T(8,128)(2,1)S(1)} %collective-permute-done.5.refs_5_.refs_1_.refs_8_.refs_4_), channel_id=1, source_target_pairs={{0,1},{1,0},{2,3},{3,2},{4,5},{5,4},{6,7},{7,6},{8,9},{9,8},{10,11... | collective-permute-start | bytes 1769480 | tf_op jit(solution)/shard_map/ppermute | solution.py:542
  43.0 9.9 %collective-permute-start.12 = (bf16[64,4608]{1,0:T(8,128)(2,1)S(1)}, bf16[64,4608]{1,0:T(8,128)(2,1)S(1)}, u32[]{:S(2)}, u32[]{:S(2)}) collective-permute-start(bf16[64,4608]{1,0:T(8,128)(2,1)S(1)} %collective-permute-done.1.refs_4_.refs_0_.refs_7_.refs_3_), channel_id=1, source_target_pairs={{0,1},{1,0},{2,3},{3,2},{4,5},{5,4},{6,7},{7,6},{8,9},{9,8},{10,11... | collective-permute-start | bytes 1769480 | tf_op jit(solution)/shard_map/ppermute | solution.py:542
  51.6 4.2 %collective-permute-start.14 = (bf16[64,4608]{1,0:T(8,128)(2,1)S(1)}, bf16[64,4608]{1,0:T(8,128)(2,1)S(1)}, u32[]{:S(2)}, u32[]{:S(2)}) collective-permute-start(bf16[64,4608]{1,0:T(8,128)(2,1)S(1)} %collective-permute-done.3.refs_4_.refs_7_), channel_id=1, source_target_pairs={{0,1},{1,0},{2,3},{3,2},{4,5},{5,4},{6,7},{7,6},{8,9},{9,8},{10,11... | collective-permute-start | bytes 1769480 | tf_op jit(solution)/shard_map/ppermute | solution.py:542
  51.8 4.1 %collective-permute-start.15 = (bf16[64,4608]{1,0:T(8,128)(2,1)S(1)}, bf16[64,4608]{1,0:T(8,128)(2,1)S(1)}, u32[]{:S(2)}, u32[]{:S(2)}) collective-permute-start(bf16[64,4608]{1,0:T(8,128)(2,1)S(1)} %collective-permute-done.11.refs_5_.refs_8_), channel_id=1, source_target_pairs={{0,1},{1,0},{2,3},{3,2},{4,5},{5,4},{6,7},{7,6},{8,9},{9,8},{10,11... | collective-permute-start | bytes 1769480 | tf_op jit(solution)/shard_map/ppermute | solution.py:542
  52.2 6.2 %collective-permute-start.10 = (f32[2,128,128]{2,1,0:T(8,128)S(1)}, f32[2,128,128]{2,1,0:T(8,128)S(1)}, u32[]{:S(2)}, u32[]{:S(2)}) collective-permute-start(f32[2,128,128]{2,1,0:T(8,128)S(1)} %shard_map.70.refs_2_), channel_id=1, source_target_pairs={{0,2},{2,0},{1,3},{3,1},{4,6},{6,4},{5,7},{7,5},{8,10},{10,8},{9,1... | collective-permute-start | bytes 393224 | tf_op jit(solution)/shard_map/ppermute | solution.py:534
  54.4 6.6 %collective-permute-start.17 = (f32[1,128,128]{2,1,0:T(8,128)S(1)}, f32[1,128,128]{2,1,0:T(8,128)S(1)}, u32[]{:S(2)}, u32[]{:S(2)}) collective-permute-start(f32[1,128,128]{2,1,0:T(8,128)S(1)} %shard_map.72.refs_1_), channel_id=1, source_target_pairs={{0,2},{2,0},{1,3},{3,1},{4,6},{6,4},{5,7},{7,5},{8,10},{10,8},{9,1... | collective-permute-start | bytes 196616 | tf_op jit(solution)/shard_map/ppermute | solution.py:534
  57.4 5.5 %collective-permute-start.16 = (f32[1,128,128]{2,1,0:T(8,128)S(1)}, f32[1,128,128]{2,1,0:T(8,128)S(1)}, u32[]{:S(2)}, u32[]{:S(2)}) collective-permute-start(f32[1,128,128]{2,1,0:T(8,128)S(1)} %shard_map.73.refs_1_), channel_id=1, source_target_pairs={{0,2},{2,0},{1,3},{3,1},{4,6},{6,4},{5,7},{7,5},{8,10},{10,8},{9,1... | collective-permute-start | bytes 196616 | tf_op jit(solution)/shard_map/ppermute | solution.py:534

commit v13 on v12

--- a/solution.py
+++ b/solution.py
@@ -12,7 +12,7 @@
 MOST = 2
 BLOCK = 256
 PIECES = 4
-CHUNKS = ((6, 2), (0, 4), (4, 2))
+CHUNKS = ((5, 3), (0, 5))
 ENTRIES = 8
 MIDDLE = 1.5 * 2.0**23
 
@@ -173,10 +173,13 @@
     return jnp.concatenate(v, axis=0).astype(jnp.float32) * jnp.exp2(power - 18.0)
 
 
-def add_decoded(sums, chunk, refs):
+def add_decoded(sums, chunk, refs, above):
     first, number = CHUNKS[chunk]
     for unit in range(number):
-        rows = pl.ds((first + unit) * SEGMENT_ROWS, SEGMENT_ROWS)
+        at = first + unit - above
+        if at < 0 or at >= sums.shape[0] // SEGMENT_ROWS:
+            continue
+        rows = pl.ds(at * SEGMENT_ROWS, SEGMENT_ROWS)
         value = sums[rows, :]
         for ref in refs:
             value = value + decode(ref, unit, number)
@@ -271,21 +274,21 @@
     )(tokens, weight)
 
 
-def add_kernel(chunk, base_ref, *refs):
+def add_kernel(chunk, above, sums_ref, *refs):
     coded_refs, o_ref = refs[:-1], refs[-1]
-    o_ref[...] = base_ref[...]
-    add_decoded(o_ref, chunk, coded_refs)
-
-
-def add_call(chunk, base, coded):
-    return pl.pallas_call(
-        functools.partial(add_kernel, chunk),
+    o_ref[...] = sums_ref[...]
+    add_decoded(o_ref, chunk, coded_refs, above)
+
+
+def add_call(chunk, above, sums, coded):
+    return pl.pallas_call(
+        functools.partial(add_kernel, chunk, above),
         in_specs=[VMEM] * (1 + len(coded)),
         out_specs=VMEM,
-        out_shape=jax.ShapeDtypeStruct(base.shape, base.dtype),
+        out_shape=jax.ShapeDtypeStruct(sums.shape, sums.dtype),
         compiler_params=params(8),
-        cost_estimate=cost(20 * base.size, 12 * base.size),
-    )(base, *coded)
+        cost_estimate=cost(40000 * sums.size, 12 * sums.size),
+    )(sums, *coded)
 
 
 def shrink_into(o_ref, at, table, k, rows_of, views, rank):
@@ -318,53 +321,92 @@
     return range((k + 1) // 2, k + 1)
 
 
-def own_kernel(n_adapter, per_device, rank, table, x_ref, w_ref, *refs):
-    messages, refs = refs[:per_device], refs[per_device:]
-    coded_refs, (o_ref, s_ref, kept_ref, x, w, sems, kept_sems) = refs[:-7], refs[-7:]
+def upper_kernel(n_adapter, table, x_ref, w_ref, o_ref, kept_ref, x, w, sems, kept_sems):
     work = load_base(0, x.shape[0] // SEGMENT_ROWS, lax.axis_index("tensor"), x_ref, w_ref, x, w, sems)
     keeps = []
-    for at, size, terms in work:
-        o_ref[at : at + size, :] = block_product(x, w, at, size, terms)
-    add_decoded(o_ref, 0, coded_refs)
     for k in range(1, n_adapter):
         for j in range(MOST):
             start, _, _ = segment_of(table, k, j)
             keeps.append(
                 pltpu.make_async_copy(
-                    x.at[pl.ds(start, SEGMENT_ROWS), :], kept_ref.at[k - 1, j], kept_sems.at[k - 1, j]
+                    x_ref.at[pl.ds(start, SEGMENT_ROWS), :],
+                    kept_ref.at[k - 1, j],
+                    kept_sems.at[k - 1, j],
                 )
             )
             keeps[-1].start()
-
-    def rows_of(j):
-        start, _, _ = segment_of(table, 0, j)
-        return x[pl.ds(start, SEGMENT_ROWS), :]
-
-    views = views_of(messages, [0], [(per_device, 0)], rank)
-    shrink_into(s_ref, 0, table, 0, rows_of, views, rank)
+    for at, size, terms in work:
+        o_ref[at : at + size, :] = block_product(x, w, at, size, terms)
     for copy in keeps:
         copy.wait()
 
 
-def own_call(table, tokens, weight, messages, coded, columns, n_adapter):
+def upper_call(table, tokens, weight, columns, n_adapter):
     rows, width = tokens.shape
-    per_device, rank = len(messages), messages[0].shape[0]
-    return pl.pallas_call(
-        functools.partial(own_kernel, n_adapter, per_device, rank),
-        in_specs=[SMEM, HBM, HBM] + [VMEM] * (per_device + len(coded)),
+    half = rows // 2
+    return pl.pallas_call(
+        functools.partial(upper_kernel, n_adapter),
+        in_specs=[SMEM, HBM, HBM],
+        out_specs=[VMEM] * 2,
+        out_shape=[
+            jax.ShapeDtypeStruct((half, columns), jnp.float32),
+            jax.ShapeDtypeStruct((n_adapter - 1, MOST, SEGMENT_ROWS, width), jnp.bfloat16),
+        ],
+        scratch_shapes=base_scratch(half // SEGMENT_ROWS, width, columns)
+        + [pltpu.SemaphoreType.DMA((n_adapter - 1, MOST))],
+        compiler_params=params(12),
+        cost_estimate=cost(2 * half * width * columns, 2 * rows * width + 2 * width * columns),
+    )(table, tokens, weight)
+
+
+def lower_kernel(per_device, rank, table, x_ref, w_ref, *refs):
+    messages, halves, refs = refs[:per_device], refs[per_device : 2 * per_device], refs[2 * per_device :]
+    coded_refs, (o_ref, s_ref, whole_ref, x, w, sems, mine, mine_sems, join_sems) = refs[:-9], refs[-9:]
+    above = x.shape[0] // SEGMENT_ROWS
+    work = load_base(above, above, lax.axis_index("tensor"), x_ref, w_ref, x, w, sems)
+    joins = join_copies(halves, whole_ref, join_sems)
+    loads = []
+    for j in range(MOST):
+        start, _, _ = segment_of(table, 0, j)
+        loads.append(
+            pltpu.make_async_copy(
+                x_ref.at[pl.ds(start, SEGMENT_ROWS), :], mine.at[j], mine_sems.at[j]
+            )
+        )
+        loads[-1].start()
+    for at, size, terms in work:
+        o_ref[at : at + size, :] = block_product(x, w, at, size, terms)
+    add_decoded(o_ref, 0, coded_refs, above)
+    for copy in loads:
+        copy.wait()
+    views = views_of(messages, [0], [(per_device, 0)], rank)
+    shrink_into(s_ref, 0, table, 0, lambda j: mine[j], views, rank)
+    for copy in joins:
+        copy.wait()
+
+
+def lower_call(table, tokens, weight, messages, halves, coded, columns):
+    rows, width = tokens.shape
+    half = rows // 2
+    per_device, (rank, long) = len(messages), messages[0].shape
+    return pl.pallas_call(
+        functools.partial(lower_kernel, per_device, rank),
+        in_specs=[SMEM, HBM, HBM] + [VMEM] * (2 * per_device + len(coded)),
         out_specs=[VMEM] * 3,
         out_shape=[
-            jax.ShapeDtypeStruct((rows, columns), jnp.float32),
+            jax.ShapeDtypeStruct((half, columns), jnp.float32),
             jax.ShapeDtypeStruct((1, SEGMENT_ROWS, MOST * rank), jnp.float32),
-            jax.ShapeDtypeStruct((n_adapter - 1, MOST, SEGMENT_ROWS, width), jnp.bfloat16),
+            jax.ShapeDtypeStruct((per_device * rank, long), jnp.bfloat16),
         ],
-        scratch_shapes=base_scratch(rows // SEGMENT_ROWS, width, columns)
-        + [pltpu.SemaphoreType.DMA((n_adapter - 1, MOST))],
-        compiler_params=params(20),
-        cost_estimate=cost(
-            2 * rows * width * columns, 2 * rows * width + 2 * width * columns + 4 * rows * columns
-        ),
-    )(table, tokens, weight, *messages, *coded)
+        scratch_shapes=base_scratch(half // SEGMENT_ROWS, width, columns)
+        + [
+            pltpu.VMEM((MOST, SEGMENT_ROWS, width), jnp.bfloat16),
+            pltpu.SemaphoreType.DMA((MOST,)),
+            pltpu.SemaphoreType.DMA((per_device,)),
+        ],
+        compiler_params=params(14),
+        cost_estimate=cost(0 * half * width * columns, 4 * rows * columns),
+    )(table, tokens, weight, *messages, *halves, *coded)
 
 
 def shrink_kernel(k, rank, at, layout, n_halves, table, kept_ref, *refs):
@@ -426,9 +468,12 @@
 
 def early_kernel(n_adapter, n_tensor, rank, layout, n_buffers, table, *refs):
     first = n_adapter - LATE
-    base_ref, coded_refs, refs = refs[0], refs[1:n_tensor], refs[n_tensor:]
+    upper_ref, lower_ref, refs = refs[0], refs[1], refs[2:]
     shrinks, refs = refs[: -4 - n_buffers], refs[-4 - n_buffers :]
-    buffers, (o_ref, rest_ref, up, total) = refs[:-4], refs[-4:]
+    buffers, (o_ref, rest_ref, up, base_ref) = refs[:-4], refs[-4:]
+    rows = upper_ref.shape[0]
+    base_ref[:rows, :] = upper_ref[...]
+    base_ref[rows:, :] = lower_ref[...]
     views = views_of(buffers, range(first), layout, rank)
     for k in range(first):
         for j in range(MOST):
@@ -439,12 +484,10 @@
         for i in range(1, n_tensor):
             share = share + shrinks[call * n_tensor + i][...]
         shares += [share[i] for i in range(share.shape[0])]
-    total[...] = base_ref[...]
-    add_decoded(total, len(CHUNKS) - 1, coded_refs)
     for k in range(n_adapter):
         for j in range(MOST):
             start, used, _ = segment_of(table, k, j)
-            value = total[pl.ds(start, SEGMENT_ROWS), :]
+            value = base_ref[pl.ds(start, SEGMENT_ROWS), :]
             if k >= first:
                 rest_ref[k - first, j] = value
                 continue
@@ -457,11 +500,11 @@
                 )
 
 
-def early(n_adapter, n_tensor, table, base, coded, shrinks, buffers, layout, rank):
-    rows, columns = base.shape
+def early(n_adapter, n_tensor, table, upper, lower, shrinks, buffers, layout, rank):
+    rows, columns = upper.shape[0] + lower.shape[0], upper.shape[1]
     return pl.pallas_call(
         functools.partial(early_kernel, n_adapter, n_tensor, rank, layout, len(buffers)),
-        in_specs=[SMEM] + [VMEM] * (1 + len(coded) + len(shrinks) + len(buffers)),
+        in_specs=[SMEM] + [VMEM] * (2 + len(shrinks) + len(buffers)),
         out_specs=[VMEM, VMEM],
         out_shape=[
             jax.ShapeDtypeStruct((rows, columns), jnp.bfloat16),
@@ -473,45 +516,53 @@
         ],
         compiler_params=params(16),
         cost_estimate=cost(6 * rows * rank * columns, (4 * n_tensor + 2) * rows * columns),
-    )(table, base, *coded, *shrinks, *buffers)
-
-
-def late_kernel(k, number, n_tensor, rank, layout, table, *refs):
-    rest_ref, shrinks, refs = refs[0], refs[1 : 1 + n_tensor], refs[1 + n_tensor :]
+    )(table, upper, lower, *shrinks, *buffers)
+
+
+def late_kernel(ks, n_tensor, rank, layout, table, *refs):
+    rest_ref, shrinks, refs = refs[0], refs[1 : 1 + len(ks) * n_tensor], refs[1 + len(ks) * n_tensor :]
     buffers, (_, o_ref, up, out, sems) = refs[:-5], refs[-5:]
-    views = views_of(buffers, stages_of(k), layout, rank)
-    share = shrinks[0][0]
-    for r in shrinks[1:]:
-        share = share + r[0]
+    views = views_of(buffers, stages_of_all(ks), layout, rank)
     stores = []
-    for j in range(MOST):
-        fetch_up(up, j, table, k, j, views, rank)
-        start, used, _ = segment_of(table, k, j)
-        lora = up_product(share, j, up[j], rank)
-        out[j] = (rest_ref[number, j] + adapter_scale * lora).astype(jnp.bfloat16)
-        store = pltpu.make_async_copy(out.at[j], o_ref.at[pl.ds(start, SEGMENT_ROWS), :], sems.at[j])
-        pl.when(used)(store.start)
-        stores.append((used, store))
+    for i, k in enumerate(ks):
+        share = shrinks[i * n_tensor][0]
+        for r in shrinks[i * n_tensor + 1 : (i + 1) * n_tensor]:
+            share = share + r[0]
+        for j in range(MOST):
+            fetch_up(up, i * MOST + j, table, k, j, views, rank)
+            start, used, _ = segment_of(table, k, j)
+            lora = up_product(share, j, up[i * MOST + j], rank)
+            out[i, j] = (rest_ref[i, j] + adapter_scale * lora).astype(jnp.bfloat16)
+            store = pltpu.make_async_copy(
+                out.at[i, j], o_ref.at[pl.ds(start, SEGMENT_ROWS), :], sems.at[i, j]
+            )
+            pl.when(used)(store.start)
+            stores.append((used, store))
     for used, store in stores:
         pl.when(used)(store.wait)
 
 
-def late(k, number, n_tensor, table, rest, shrinks, buffers, value, layout, rank):
+def stages_of_all(ks):
+    return range(stages_of(ks[0])[0], ks[-1] + 1)
+
+
+def late(ks, n_tensor, table, rest, shrinks, buffers, value, layout, rank):
     rows, columns = value.shape
     return pl.pallas_call(
-        functools.partial(late_kernel, k, number, n_tensor, rank, layout),
+        functools.partial(late_kernel, ks, n_tensor, rank, layout),
         in_specs=[SMEM] + [VMEM] * (1 + len(shrinks) + len(buffers)) + [ANY],
         out_specs=ANY,
         out_shape=jax.ShapeDtypeStruct((rows, columns), jnp.bfloat16),
         scratch_shapes=[
-            pltpu.VMEM((MOST, 2 * rank, columns), jnp.bfloat16),
-            pltpu.VMEM((MOST, SEGMENT_ROWS, columns), jnp.bfloat16),
-            pltpu.SemaphoreType.DMA((MOST,)),
+            pltpu.VMEM((LATE * MOST, 2 * rank, columns), jnp.bfloat16),
+            pltpu.VMEM((LATE, MOST, SEGMENT_ROWS, columns), jnp.bfloat16),
+            pltpu.SemaphoreType.DMA((LATE, MOST)),
         ],
         input_output_aliases={2 + len(shrinks) + len(buffers): 0},
         compiler_params=params(8),
         cost_estimate=cost(
-            6 * MOST * SEGMENT_ROWS * rank * columns, 8 * MOST * SEGMENT_ROWS * columns
+            6 * LATE * MOST * SEGMENT_ROWS * rank * columns,
+            8 * LATE * MOST * SEGMENT_ROWS * columns,
         ),
     )(table, rest, *shrinks, *buffers, value)
 
@@ -550,7 +601,7 @@
     table = table_call(row_adapter_index, adapter_slot_of, n_adapter, per_device)
     last = n_adapter - 1
     buffers, shrinks = [list(messages)], []
-    layout = [(per_device, 0)] + [(per_device, per_device)] * last
+    layout = [(per_device, 0), (per_device, 1)] + [(per_device, per_device)] * (last - 1)
 
     def buffers_of(stages):
         return [b for stage in stages for b in buffers[stage]]
@@ -578,65 +629,63 @@
     rest_parts = [sent_for(step, CHUNKS[1:], after(tokens, first)) for step in others]
     parts = [[p[i] for p in rest_parts] for i in range(len(CHUNKS) - 1)]
     part_b = [p for group in parts for p in group]
-    held1 = held
     for stage in range(1, last):
         came = held
         if stage == 1:
-            came = [first] + [after(h, *part_b, *sent[0]) for h in held[1:]]
-            sent.append(send(parts[0], *came))
+            came = [first] + [after(h, *part_b) for h in held[1:]]
+            sent.append(send(parts[0], *came, *sent[0]))
         if stage == 2:
-            came = held[:1] + [after(h, base) for h in held[1:]]
-            sent.append(send(parts[1], base, *sent[1]))
+            came = held[:1] + [after(h, upper) for h in held[1:]]
         held = [along_line(c, stage + 1) for c in came]
         if stage == 1:
-            base, before, kept = own_call(
-                after(table, held[0]),
-                tokens,
-                value_weight,
-                messages,
-                sent[0],
-                columns,
-                n_adapter,
+            upper, kept = upper_call(
+                after(table, held[0], *came), tokens, value_weight, columns, n_adapter
             )
+        elif stage == 2:
+            lower, before, joined = lower_call(
+                after(table, *came), tokens, value_weight, messages, buffers[1], sent[0], columns
+            )
+            buffers[1] += [swap_cores(joined)]
+            free = lower
+            above = rows // SEGMENT_ROWS // 2
+            upper = add_call(1, 0, after(upper, held[0]), sent[1])
+            lower = add_call(1, above, after(lower, upper, *held[1:]), sent[1])
+            before = shrink(1, after(kept, lower), [before])[0]
         else:
-            ready = kept
-            if stage == 2:
-                base = add_call(1, after(base, held[0], *came), sent[1])
-                ready = after(kept, base)
-            before = shrink(stage - 1, ready, [before])[0]
-        buffers.append([*came, *[swap_cores(h) for h in (held1 if stage == 1 else came)]])
+            before = shrink(stage - 1, kept, [before])[0]
+        ahead = [free] if stage == 2 else []
+        swapped = [swap_cores(after(c, *ahead)) for c in came] if stage > 1 else []
+        buffers.append([*came, *swapped])
     add_shrink(before)
     value, remaining = early(
         n_adapter,
         n_tensor,
         table,
-        base,
-        sent[2],
+        upper,
+        lower,
         shrinks,
         buffers_of(range(last - 1)),
         layout,
         rank,
     )
-    buffers.append([*held, *[swap_cores(after(h, before, *sent[2])) for h in held]])
+    buffers.append([*held, *[swap_cores(h) for h in held]])
     ready = after(kept, *held)
     for k in (last - 1, last):
         mine = shrink(k, ready)[0]
         add_shrink(mine)
         ready = after(kept, mine)
-    for number, k in enumerate((last - 1, last)):
-        value = late(
-            k,
-            number,
-            n_tensor,
-            table,
-            remaining,
-            shrinks[(number - LATE) * n_tensor :][:n_tensor],
-            buffers_of(stages_of(k)),
-            value,
-            layout,
-            rank,
-        )
-    return value
+    ks = (last - 1, last)
+    return late(
+        ks,
+        n_tensor,
+        table,
+        remaining,
+        shrinks[-LATE * n_tensor :],
+        buffers_of(stages_of_all(ks)),
+        value,
+        layout,
+        rank,
+    )
 
 
 def solution(mesh):

time: 65.1 us -> 63.3 us (0.972)
  the two profiles are of different devices: /device:TPU:8 before, /device:TPU:16 now
where the time goes in v13:
time: 63.3 us; the launch traced here: 62.5 us
  Pallas kernels  37.3 us (59%)
  starting transfers between devices  21.9 us (35%)
  waiting for transfers between devices  3.03 us (5%)
    ppermute x6, starting transfers between devices, along_line(): return lax.ppermute(array, ('adapter', 'dp'), up + down)  14.7 us
    pallas_call x2, Pallas kernels, sent_call(): pl.pallas_call(functools.partial(sent_kernel, first, sizes, step, n_tenso...  10.5 us
    pallas_call x1, Pallas kernels, upper_call(): pl.pallas_call(functools.partial(upper_kernel, n_adapter), in_specs=[SMEM...  7.31 us
    pallas_call x1, Pallas kernels, lower_call(): pl.pallas_call(functools.partial(lower_kernel, per_device, rank), in_spec...  6.38 us
    ppermute x5, starting transfers between devices, swap_tensor(): return lax.ppermute(array, 'tensor', pairs)  6.02 us
    pallas_call x3, Pallas kernels, shrink_call(): pl.pallas_call(functools.partial(shrink_kernel, k, rank, at, layout, len(...  4.82 us
    pallas_call x1, Pallas kernels, early(): pl.pallas_call(functools.partial(early_kernel, n_adapter, n_tensor, rank,...  2.76 us
    pallas_call x1, Pallas kernels, late(): pl.pallas_call(functools.partial(late_kernel, ks, n_tensor, rank, layout)...  2.46 us
  transfers between devices with their start and end apart: 16, of which 6 were waited for; matrix products, arithmetic and copies ran while one was open for 0% of the time, Pallas kernels for 54%

profile of v13, /device:TPU:16, one launch (start us, length us, event | category | flops | bytes accessed | tf_op | source)
XLA Modules:
  0.0 62.5 jit_solution(169862511792336965)
XLA Ops:
  0.0 1.3 %shard_map.65 = (bf16[64,4608]{1,0:T(8,128)(2,1)S(1)}, bf16[64,4608]{1,0:T(8,128)(2,1)S(1)}) custom-call(bf16[128,4096]{1,0:T(8,128)(2,1)} %bitcast.4, bf16[128,1024]{1,0:T(8,128)(2,1)} %bitcast.5), custom_call_target="tpu_custom_call" | custom-call | bytes 2359296 | tf_op jit(solution)/shard_map/pallas_call | solution.py:90
  1.3 3.5 %collective-permute-start = (bf16[64,4608]{1,0:T(8,128)(2,1)S(1)}, bf16[64,4608]{1,0:T(8,128)(2,1)S(1)}, u32[]{:S(2)}, u32[]{:S(2)}) collective-permute-start(bf16[64,4608]{1,0:T(8,128)(2,1)S(1)} %get-tuple-element.28.refs_0_.refs_4_), channel_id=1, source_target_pairs={{0,4},{4,8},{8,12},{5,1},{9,5},{13,9},{2,6},{6,10},{10,14},{7,3},{... | collective-permute-start | bytes 1769480 | tf_op jit(solution)/shard_map/ppermute | solution.py:590
  4.8 1.9 %collective-permute-start.2 = (bf16[64,4608]{1,0:T(8,128)(2,1)S(1)}, bf16[64,4608]{1,0:T(8,128)(2,1)S(1)}, u32[]{:S(2)}, u32[]{:S(2)}) collective-permute-start(bf16[64,4608]{1,0:T(8,128)(2,1)S(1)} %get-tuple-element.30.refs_1_.refs_5_), channel_id=1, source_target_pairs={{0,4},{4,8},{8,12},{5,1},{9,5},{13,9},{2,6},{6,10},{10,14},{7,3},{... | collective-permute-start | bytes 1769480 | tf_op jit(solution)/shard_map/ppermute | solution.py:590
  6.7 4.5 %shard_map.66 = s32[248,512]{1,0:T(8,128)S(1)} custom-call(bf16[1024,4096]{1,0:T(8,128)(2,1)} %x_ref.6, bf16[4096,1024]{1,0:T(8,128)(2,1)} %w_ref.7), custom_call_target="tpu_custom_call" | custom-call | flops 1610612736 | bytes 8126464 | tf_op jit(solution)/shard_map/pallas_call | solution.py:264
  11.2 1.6 %collective-permute-start.4 = (s32[248,512]{1,0:T(8,128)S(1)}, s32[248,512]{1,0:T(8,128)S(1)}, u32[]{:S(2)}, u32[]{:S(2)}) collective-permute-start(s32[248,512]{1,0:T(8,128)S(1)} %shard_map.66), channel_id=1, source_target_pairs={{0,2},{2,0},{1,3},{3,1},{4,6},{6,4},{5,7},{7,5},{8,10},{10,8},{9,1... | collective-permute-start | bytes 1523720 | tf_op jit(solution)/shard_map/ppermute | solution.py:585
  12.8 1.4 %shard_map.64.table = s32[32]{0:T(128)} custom-call(s32[1024]{0:T(1024)} %ids.1, s32[8]{0:T(128)} %slots.1), custom_call_target="tpu_custom_call" | custom-call | bytes 4096 | tf_op jit(solution)/shard_map/pallas_call | solution.py:122
  14.2 0.0 copy-start
  14.2 0.0 collective-permute-done.refs_2_.refs_1_.refs_6_.refs_0_.refs_5_
  14.2 2.3 %collective-permute-start.1 = (bf16[64,4608]{1,0:T(8,128)(2,1)S(1)}, bf16[64,4608]{1,0:T(8,128)(2,1)S(1)}, u32[]{:S(2)}, u32[]{:S(2)}) collective-permute-start(bf16[64,4608]{1,0:T(8,128)(2,1)S(1)} %collective-permute-done.refs_2_.refs_1_.refs_6_.refs_0_.refs_5_), channel_id=1, source_target_pairs={{4,8},{8,12},{5,1},{9,5},{6,10},{10,14},{7,3},{11,7},{20,24},{24,2... | collective-permute-start | bytes 1769480 | tf_op jit(solution)/shard_map/ppermute | solution.py:590
  16.5 6.0 %shard_map.67 = s32[408,512]{1,0:T(8,128)S(1)} custom-call(bf16[1024,4096]{1,0:T(8,128)(2,1)} %x_ref.6, bf16[4096,1024]{1,0:T(8,128)(2,1)} %w_ref.7), custom_call_target="tpu_custom_call" | custom-call | flops 2684354560 | bytes 10747904 | tf_op jit(solution)/shard_map/pallas_call | solution.py:264
  22.5 0.0 collective-permute-done.2.refs_3_.refs_2_.refs_7_.refs_1_.refs_6_
  22.5 0.6 collective-permute-done.4.refs_4_
  23.1 1.7 %collective-permute-start.5 = (s32[408,512]{1,0:T(8,128)S(1)}, s32[408,512]{1,0:T(8,128)S(1)}, u32[]{:S(2)}, u32[]{:S(2)}) collective-permute-start(s32[408,512]{1,0:T(8,128)S(1)} %shard_map.67), channel_id=1, source_target_pairs={{0,2},{2,0},{1,3},{3,1},{4,6},{6,4},{5,7},{7,5},{8,10},{10,8},{9,1... | collective-permute-start | bytes 2506760 | tf_op jit(solution)/shard_map/ppermute | solution.py:585
  24.8 2.6 %collective-permute-start.6 = (bf16[64,4608]{1,0:T(8,128)(2,1)S(1)}, bf16[64,4608]{1,0:T(8,128)(2,1)S(1)}, u32[]{:S(2)}, u32[]{:S(2)}) collective-permute-start(bf16[64,4608]{1,0:T(8,128)(2,1)S(1)} %collective-permute-done.2.refs_3_.refs_2_.refs_7_.refs_1_.refs_6_), channel_id=1, source_target_pairs={{4,8},{8,12},{5,1},{9,5},{6,10},{10,14},{7,3},{11,7},{20,24},{24,2... | collective-permute-start | bytes 1769480 | tf_op jit(solution)/shard_map/ppermute | solution.py:590
  27.5 0.0 collective-permute-done.1.refs_3_.refs_0_.refs_8_
  27.5 1.7 %collective-permute-start.3 = (bf16[64,4608]{1,0:T(8,128)(2,1)S(1)}, bf16[64,4608]{1,0:T(8,128)(2,1)S(1)}, u32[]{:S(2)}, u32[]{:S(2)}) collective-permute-start(bf16[64,4608]{1,0:T(8,128)(2,1)S(1)} %collective-permute-done.1.refs_3_.refs_0_.refs_8_), channel_id=1, source_target_pairs={{8,12},{5,1},{10,14},{7,3},{24,28},{21,17},{26,30},{23,19}} | collective-permute-start | bytes 1769480 | tf_op jit(solution)/shard_map/ppermute | solution.py:590
  29.2 0.0 copy-done
  29.2 7.3 %shard_map.68 = (f32[512,512]{1,0:T(8,128)S(1)}, bf16[3,2,128,4096]{3,2,1,0:T(8,128)(2,1)S(1)}) custom-call(s32[32]{0:T(128)S(1)} %copy-done, bf16[1024,4096]{1,0:T(8,128)(2,1)} %x_ref.6, bf16[4096,1024]{1,0:T(8,128)(2,1)} %w_ref.7), custom_call_target="tpu_custom_call" | custom-call | flops 2147483648 | bytes 12582912 | tf_op jit(solution)/shard_map/pallas_call | solution.py:347
  36.5 0.1 collective-permute-done.6.refs_4_.refs_1_.refs_9_
  36.6 2.7 %collective-permute-start.7 = (bf16[64,4608]{1,0:T(8,128)(2,1)S(1)}, bf16[64,4608]{1,0:T(8,128)(2,1)S(1)}, u32[]{:S(2)}, u32[]{:S(2)}) collective-permute-start(bf16[64,4608]{1,0:T(8,128)(2,1)S(1)} %collective-permute-done.6.refs_4_.refs_1_.refs_9_), channel_id=1, source_target_pairs={{8,12},{5,1},{10,14},{7,3},{24,28},{21,17},{26,30},{23,19}} | collective-permute-start | bytes 1769480 | tf_op jit(solution)/shard_map/ppermute | solution.py:590
  39.3 6.4 %shard_map.70 = (f32[512,512]{1,0:T(8,128)S(1)}, f32[1,128,128]{2,1,0:T(8,128)S(1)}, bf16[128,4608]{1,0:T(8,128)(2,1)S(1)}) custom-call(s32[32]{0:T(128)S(1)} %copy-done, bf16[1024,4096]{1,0:T(8,128)(2,1)} %x_ref.6, bf16[4096,1024]{1,0:T(8,128)(2,1)} %w_ref.7, bf16[64,4608]{1,0:T(8,128)(2,1)S(1)} %get-tuple-element.28.refs_0_.refs_4_, ...), custom_call_target="tpu_custom_call" | custom-call | bytes 2097152 | tf_op jit(solution)/shard_map/pallas_call | solution.py:392
  45.7 0.1 collective-permute-start.8
  45.8 0.5 collective-permute-start.10
  46.2 0.0 collective-permute-done.3.refs_4_.refs_12_
  46.3 0.1 collective-permute-start.11
  46.3 0.0 collective-permute-done.5.refs_0_
  46.3 0.3 shard_map.69.refs_0_
  46.6 0.9 %collective-permute-done.7.refs_5_.refs_13_ = bf16[64,4608]{1,0:T(8,128)(2,1)S(1)} collective-permute-done((bf16[64,4608]{1,0:T(8,128)(2,1)S(1)}, bf16[64,4608]{1,0:T(8,128)(2,1)S(1)}, u32[]{:S(2)}, u32[]{:S(2)}) %collective-permute-start.7) | collective-permute-done | bytes 589856 | tf_op jit(solution)/shard_map/ppermute | solution.py:590
  47.5 0.0 collective-permute-start.13
  47.5 0.5 collective-permute-start.14
  48.0 0.1 shard_map.71.refs_1_
  48.1 0.4 collective-permute-done.8.refs_3_.refs_8_.refs_2_.refs_7_
  48.6 1.7 %shard_map.72.refs_2_ = f32[2,128,128]{2,1,0:T(8,128)S(1)} custom-call(s32[32]{0:T(128)S(1)} %copy-done, bf16[3,2,128,4096]{3,2,1,0:T(8,128)(2,1)S(1)} %get-tuple-element.49.kept_ref, f32[1,128,128]{2,1,0:T(8,128)S(1)} %get-tuple-element.43.refs_0_, bf16[64,4608]{1,0:T(8,128)(2,1)S(1)} %collective-permute-done.refs_2_.refs_1_.refs_6_.refs_0_.refs_5_, ...), custom_call_target="tpu_custom_call" | custom-call | flops 536870912 | bytes 2097152 | tf_op jit(solution)/shard_map/pallas_call | solution.py:434
  50.3 0.5 collective-permute-start.9
  50.8 0.0 collective-permute-done.10.refs_5_.refs_2_.refs_10_
  50.8 0.0 collective-permute-done.11.refs_6_.refs_3_.refs_11_
  50.8 1.6 %shard_map.74.refs_1_ = f32[1,128,128]{2,1,0:T(8,128)S(1)} custom-call(s32[32]{0:T(128)S(1)} %copy-done, bf16[3,2,128,4096]{3,2,1,0:T(8,128)(2,1)S(1)} %get-tuple-element.49.kept_ref, bf16[64,4608]{1,0:T(8,128)(2,1)S(1)} %collective-permute-done.refs_2_.refs_1_.refs_6_.refs_0_.refs_5_, ...), custom_call_target="tpu_custom_call" | custom-call | flops 536870912 | bytes 2097152 | tf_op jit(solution)/shard_map/pallas_call | solution.py:434
  52.4 1.6 %collective-permute-start.12 = (f32[1,128,128]{2,1,0:T(8,128)S(1)}, f32[1,128,128]{2,1,0:T(8,128)S(1)}, u32[]{:S(2)}, u32[]{:S(2)}) collective-permute-start(f32[1,128,128]{2,1,0:T(8,128)S(1)} %shard_map.74.refs_1_), channel_id=1, source_target_pairs={{0,2},{2,0},{1,3},{3,1},{4,6},{6,4},{5,7},{7,5},{8,10},{10,8},{9,1... | collective-permute-start | bytes 196616 | tf_op jit(solution)/shard_map/ppermute | solution.py:585
  54.0 0.0 collective-permute-done.13.refs_6_.refs_14_
  54.0 0.0 collective-permute-done.14.refs_7_.refs_15_
  54.0 1.6 %shard_map.75.refs_3_ = f32[1,128,128]{2,1,0:T(8,128)S(1)} custom-call(s32[32]{0:T(128)S(1)} %copy-done, bf16[3,2,128,4096]{3,2,1,0:T(8,128)(2,1)S(1)} %get-tuple-element.49.kept_ref, bf16[64,4608]{1,0:T(8,128)(2,1)S(1)} %collective-permute-done.1.refs_3_.refs_0_.refs_8_, bf16[64,4608]{1,0:T(8,128)(2,1)S(1)} %collective-permute-done.6.refs_4_.refs_1_.refs_9_, ...), custom_call_target="tpu_custom_call" | custom-call | flops 536870912 | bytes 2097152 | tf_op jit(solution)/shard_map/pallas_call | solution.py:434
  55.6 0.5 collective-permute-start.15
  56.1 0.4 collective-permute-done.9.refs_3_
  56.6 2.8 %shard_map.73 = (bf16[1024,512]{1,0:T(8,128)(2,1)}, f32[2,2,128,512]{3,2,1,0:T(8,128)S(1)}) custom-call(s32[32]{0:T(128)S(1)} %copy-done, f32[512,512]{1,0:T(8,128)S(1)} %shard_map.69.refs_0_, f32[512,512]{1,0:T(8,128)S(1)} %shard_map.71.refs_1_, f32[2,128,128]{2,1,0:T(8,128)S(1)} %shard_map.72.refs_2_, f32[2,128,128]{2,1,0:T(8,128)S(1)} %collective-permute-done.9.refs_3_, ...), custom_call_target="tpu_custom_call" | custom-call | flops 201326592 | bytes 5242880 | tf_op jit(solution)/shard_map/pallas_call | solution.py:505
  59.3 0.0 collective-permute-done.12.refs_2_
  59.3 0.6 collective-permute-done.15.refs_4_
  59.9 2.5 %shard_map.76 = bf16[1024,512]{1,0:T(8,128)(2,1)} custom-call(s32[32]{0:T(128)S(1)} %copy-done, f32[2,2,128,512]{3,2,1,0:T(8,128)S(1)} %get-tuple-element.45.refs_0_, f32[1,128,128]{2,1,0:T(8,128)S(1)} %shard_map.74.refs_1_, f32[1,128,128]{2,1,0:T(8,128)S(1)} %collective-permute-done.12.refs_2_, ...), custom_call_target="tpu_custom_call", output_to_operand_aliasing={{}: (17, {})} | custom-call | flops 100663296 | bytes 2097152 | tf_op jit(solution)/shard_map/pallas_call | solution.py:551
Async XLA Ops:
  1.3 12.9 %collective-permute-start = (bf16[64,4608]{1,0:T(8,128)(2,1)S(1)}, bf16[64,4608]{1,0:T(8,128)(2,1)S(1)}, u32[]{:S(2)}, u32[]{:S(2)}) collective-permute-start(bf16[64,4608]{1,0:T(8,128)(2,1)S(1)} %get-tuple-element.28.refs_0_.refs_4_), channel_id=1, source_target_pairs={{0,4},{4,8},{8,12},{5,1},{9,5},{13,9},{2,6},{6,10},{10,14},{7,3},{... | collective-permute-start | bytes 1769480 | tf_op jit(solution)/shard_map/ppermute | solution.py:590
  4.8 17.8 %collective-permute-start.2 = (bf16[64,4608]{1,0:T(8,128)(2,1)S(1)}, bf16[64,4608]{1,0:T(8,128)(2,1)S(1)}, u32[]{:S(2)}, u32[]{:S(2)}) collective-permute-start(bf16[64,4608]{1,0:T(8,128)(2,1)S(1)} %get-tuple-element.30.refs_1_.refs_5_), channel_id=1, source_target_pairs={{0,4},{4,8},{8,12},{5,1},{9,5},{13,9},{2,6},{6,10},{10,14},{7,3},{... | collective-permute-start | bytes 1769480 | tf_op jit(solution)/shard_map/ppermute | solution.py:590
  11.2 12.0 %collective-permute-start.4 = (s32[248,512]{1,0:T(8,128)S(1)}, s32[248,512]{1,0:T(8,128)S(1)}, u32[]{:S(2)}, u32[]{:S(2)}) collective-permute-start(s32[248,512]{1,0:T(8,128)S(1)} %shard_map.66), channel_id=1, source_target_pairs={{0,2},{2,0},{1,3},{3,1},{4,6},{6,4},{5,7},{7,5},{8,10},{10,8},{9,1... | collective-permute-start | bytes 1523720 | tf_op jit(solution)/shard_map/ppermute | solution.py:585
  14.2 15.0 %copy-start = (s32[32]{0:T(128)S(1)}, s32[32]{0:T(128)}, u32[]{:S(2)}) copy-start(s32[32]{0:T(128)} %shard_map.64.table) | copy-start | bytes 388
  14.2 13.3 %collective-permute-start.1 = (bf16[64,4608]{1,0:T(8,128)(2,1)S(1)}, bf16[64,4608]{1,0:T(8,128)(2,1)S(1)}, u32[]{:S(2)}, u32[]{:S(2)}) collective-permute-start(bf16[64,4608]{1,0:T(8,128)(2,1)S(1)} %collective-permute-done.refs_2_.refs_1_.refs_6_.refs_0_.refs_5_), channel_id=1, source_target_pairs={{4,8},{8,12},{5,1},{9,5},{6,10},{10,14},{7,3},{11,7},{20,24},{24,2... | collective-permute-start | bytes 1769480 | tf_op jit(solution)/shard_map/ppermute | solution.py:590
  23.1 23.2 %collective-permute-start.5 = (s32[408,512]{1,0:T(8,128)S(1)}, s32[408,512]{1,0:T(8,128)S(1)}, u32[]{:S(2)}, u32[]{:S(2)}) collective-permute-start(s32[408,512]{1,0:T(8,128)S(1)} %shard_map.67), channel_id=1, source_target_pairs={{0,2},{2,0},{1,3},{3,1},{4,6},{6,4},{5,7},{7,5},{8,10},{10,8},{9,1... | collective-permute-start | bytes 2506760 | tf_op jit(solution)/shard_map/ppermute | solution.py:585
  24.8 11.8 %collective-permute-start.6 = (bf16[64,4608]{1,0:T(8,128)(2,1)S(1)}, bf16[64,4608]{1,0:T(8,128)(2,1)S(1)}, u32[]{:S(2)}, u32[]{:S(2)}) collective-permute-start(bf16[64,4608]{1,0:T(8,128)(2,1)S(1)} %collective-permute-done.2.refs_3_.refs_2_.refs_7_.refs_1_.refs_6_), channel_id=1, source_target_pairs={{4,8},{8,12},{5,1},{9,5},{6,10},{10,14},{7,3},{11,7},{20,24},{24,2... | collective-permute-start | bytes 1769480 | tf_op jit(solution)/shard_map/ppermute | solution.py:590
  27.5 18.8 %collective-permute-start.3 = (bf16[64,4608]{1,0:T(8,128)(2,1)S(1)}, bf16[64,4608]{1,0:T(8,128)(2,1)S(1)}, u32[]{:S(2)}, u32[]{:S(2)}) collective-permute-start(bf16[64,4608]{1,0:T(8,128)(2,1)S(1)} %collective-permute-done.1.refs_3_.refs_0_.refs_8_), channel_id=1, source_target_pairs={{8,12},{5,1},{10,14},{7,3},{24,28},{21,17},{26,30},{23,19}} | collective-permute-start | bytes 1769480 | tf_op jit(solution)/shard_map/ppermute | solution.py:590
  36.6 10.9 %collective-permute-start.7 = (bf16[64,4608]{1,0:T(8,128)(2,1)S(1)}, bf16[64,4608]{1,0:T(8,128)(2,1)S(1)}, u32[]{:S(2)}, u32[]{:S(2)}) collective-permute-start(bf16[64,4608]{1,0:T(8,128)(2,1)S(1)} %collective-permute-done.6.refs_4_.refs_1_.refs_9_), channel_id=1, source_target_pairs={{8,12},{5,1},{10,14},{7,3},{24,28},{21,17},{26,30},{23,19}} | collective-permute-start | bytes 1769480 | tf_op jit(solution)/shard_map/ppermute | solution.py:590
  45.7 2.9 %collective-permute-start.8 = (bf16[128,4608]{1,0:T(8,128)(2,1)S(1)}, bf16[128,4608]{1,0:T(8,128)(2,1)S(1)}, u32[]{:S(2)}, u32[]{:S(2)}) collective-permute-start(bf16[128,4608]{1,0:T(8,128)(2,1)S(1)} %get-tuple-element.44), channel_id=1, source_target_pairs={{0,1},{1,0},{2,3},{3,2},{4,5},{5,4},{6,7},{7,6},{8,9},{9,8},{10,11... | collective-permute-start | bytes 3538952 | tf_op jit(solution)/shard_map/ppermute | solution.py:593
  45.8 5.1 %collective-permute-start.10 = (bf16[64,4608]{1,0:T(8,128)(2,1)S(1)}, bf16[64,4608]{1,0:T(8,128)(2,1)S(1)}, u32[]{:S(2)}, u32[]{:S(2)}) collective-permute-start(bf16[64,4608]{1,0:T(8,128)(2,1)S(1)} %collective-permute-done.1.refs_3_.refs_0_.refs_8_), channel_id=1, source_target_pairs={{0,1},{1,0},{2,3},{3,2},{4,5},{5,4},{6,7},{7,6},{8,9},{9,8},{10,11... | collective-permute-start | bytes 1769480 | tf_op jit(solution)/shard_map/ppermute | solution.py:593
  46.3 4.6 %collective-permute-start.11 = (bf16[64,4608]{1,0:T(8,128)(2,1)S(1)}, bf16[64,4608]{1,0:T(8,128)(2,1)S(1)}, u32[]{:S(2)}, u32[]{:S(2)}) collective-permute-start(bf16[64,4608]{1,0:T(8,128)(2,1)S(1)} %collective-permute-done.6.refs_4_.refs_1_.refs_9_), channel_id=1, source_target_pairs={{0,1},{1,0},{2,3},{3,2},{4,5},{5,4},{6,7},{7,6},{8,9},{9,8},{10,11... | collective-permute-start | bytes 1769480 | tf_op jit(solution)/shard_map/ppermute | solution.py:593
  47.5 6.5 %collective-permute-start.13 = (bf16[64,4608]{1,0:T(8,128)(2,1)S(1)}, bf16[64,4608]{1,0:T(8,128)(2,1)S(1)}, u32[]{:S(2)}, u32[]{:S(2)}) collective-permute-start(bf16[64,4608]{1,0:T(8,128)(2,1)S(1)} %collective-permute-done.3.refs_4_.refs_12_), channel_id=1, source_target_pairs={{0,1},{1,0},{2,3},{3,2},{4,5},{5,4},{6,7},{7,6},{8,9},{9,8},{10,11... | collective-permute-start | bytes 1769480 | tf_op jit(solution)/shard_map/ppermute | solution.py:593
  47.5 6.5 %collective-permute-start.14 = (bf16[64,4608]{1,0:T(8,128)(2,1)S(1)}, bf16[64,4608]{1,0:T(8,128)(2,1)S(1)}, u32[]{:S(2)}, u32[]{:S(2)}) collective-permute-start(bf16[64,4608]{1,0:T(8,128)(2,1)S(1)} %collective-permute-done.7.refs_5_.refs_13_), channel_id=1, source_target_pairs={{0,1},{1,0},{2,3},{3,2},{4,5},{5,4},{6,7},{7,6},{8,9},{9,8},{10,11... | collective-permute-start | bytes 1769480 | tf_op jit(solution)/shard_map/ppermute | solution.py:593
  50.3 6.3 %collective-permute-start.9 = (f32[2,128,128]{2,1,0:T(8,128)S(1)}, f32[2,128,128]{2,1,0:T(8,128)S(1)}, u32[]{:S(2)}, u32[]{:S(2)}) collective-permute-start(f32[2,128,128]{2,1,0:T(8,128)S(1)} %shard_map.72.refs_2_), channel_id=1, source_target_pairs={{0,2},{2,0},{1,3},{3,1},{4,6},{6,4},{5,7},{7,5},{8,10},{10,8},{9,1... | collective-permute-start | bytes 393224 | tf_op jit(solution)/shard_map/ppermute | solution.py:585
  52.4 6.9 %collective-permute-start.12 = (f32[1,128,128]{2,1,0:T(8,128)S(1)}, f32[1,128,128]{2,1,0:T(8,128)S(1)}, u32[]{:S(2)}, u32[]{:S(2)}) collective-permute-start(f32[1,128,128]{2,1,0:T(8,128)S(1)} %shard_map.74.refs_1_), channel_id=1, source_target_pairs={{0,2},{2,0},{1,3},{3,1},{4,6},{6,4},{5,7},{7,5},{8,10},{10,8},{9,1... | collective-permute-start | bytes 196616 | tf_op jit(solution)/shard_map/ppermute | solution.py:585
  55.6 4.3 %collective-permute-start.15 = (f32[1,128,128]{2,1,0:T(8,128)S(1)}, f32[1,128,128]{2,1,0:T(8,128)S(1)}, u32[]{:S(2)}, u32[]{:S(2)}) collective-permute-start(f32[1,128,128]{2,1,0:T(8,128)S(1)} %shard_map.75.refs_3_), channel_id=1, source_target_pairs={{0,2},{2,0},{1,3},{3,1},{4,6},{6,4},{5,7},{7,5},{8,10},{10,8},{9,1... | collective-permute-start | bytes 196616 | tf_op jit(solution)/shard_map/ppermute | solution.py:585

commit v14 on v13

--- a/solution.py
+++ b/solution.py
@@ -12,7 +12,8 @@
 MOST = 2
 BLOCK = 256
 PIECES = 4
-CHUNKS = ((5, 3), (0, 5))
+CHUNKS = ((6, 2), (0, 6))
+UPPER = 3
 ENTRIES = 8
 MIDDLE = 1.5 * 2.0**23
 
@@ -49,11 +50,11 @@
         came, swapped = layout[stage]
         toward = jnp.where(core == 0, -stage, stage)
         for i in range(came):
-            views.append((refs.pop(0), 0, me + toward if stage > 0 else me, i))
+            views.append((stage, refs.pop(0), 0, me + toward if stage > 0 else me, i))
         for i in range(swapped):
             ref = refs.pop(0)
             for part in range(came // swapped):
-                views.append((ref, part * rank, me - toward, i + part))
+                views.append((stage, ref, part * rank, me - toward, i + part))
     return views
 
 
@@ -294,7 +295,9 @@
 def shrink_into(o_ref, at, table, k, rows_of, views, rank):
     for j in range(MOST):
         _, _, within = segment_of(table, k, j)
-        for ref, first, whose, i in views:
+        for stage, ref, first, whose, i in views:
+            if stage not in stages_of(k):
+                continue
 
             @pl.when((whose == table[k * ENTRIES]) & (within == i))
             def _(j=j, ref=ref, first=first):
@@ -319,6 +322,10 @@
 
 def stages_of(k):
     return range((k + 1) // 2, k + 1)
+
+
+def stages_of_all(ks):
+    return range(stages_of(ks[0])[0], ks[-1] + 1)
 
 
 def upper_kernel(n_adapter, table, x_ref, w_ref, o_ref, kept_ref, x, w, sems, kept_sems):
@@ -343,7 +350,7 @@
 
 def upper_call(table, tokens, weight, columns, n_adapter):
     rows, width = tokens.shape
-    half = rows // 2
+    half = UPPER * SEGMENT_ROWS
     return pl.pallas_call(
         functools.partial(upper_kernel, n_adapter),
         in_specs=[SMEM, HBM, HBM],
@@ -362,8 +369,7 @@
 def lower_kernel(per_device, rank, table, x_ref, w_ref, *refs):
     messages, halves, refs = refs[:per_device], refs[per_device : 2 * per_device], refs[2 * per_device :]
     coded_refs, (o_ref, s_ref, whole_ref, x, w, sems, mine, mine_sems, join_sems) = refs[:-9], refs[-9:]
-    above = x.shape[0] // SEGMENT_ROWS
-    work = load_base(above, above, lax.axis_index("tensor"), x_ref, w_ref, x, w, sems)
+    work = load_base(UPPER, x.shape[0] // SEGMENT_ROWS, lax.axis_index("tensor"), x_ref, w_ref, x, w, sems)
     joins = join_copies(halves, whole_ref, join_sems)
     loads = []
     for j in range(MOST):
@@ -376,7 +382,7 @@
         loads[-1].start()
     for at, size, terms in work:
         o_ref[at : at + size, :] = block_product(x, w, at, size, terms)
-    add_decoded(o_ref, 0, coded_refs, above)
+    add_decoded(o_ref, 0, coded_refs, UPPER)
     for copy in loads:
         copy.wait()
     views = views_of(messages, [0], [(per_device, 0)], rank)
@@ -387,7 +393,7 @@
 
 def lower_call(table, tokens, weight, messages, halves, coded, columns):
     rows, width = tokens.shape
-    half = rows // 2
+    half = rows - UPPER * SEGMENT_ROWS
     per_device, (rank, long) = len(messages), messages[0].shape
     return pl.pallas_call(
         functools.partial(lower_kernel, per_device, rank),
@@ -409,43 +415,36 @@
     )(table, tokens, weight, *messages, *halves, *coded)
 
 
-def shrink_kernel(k, rank, at, layout, n_halves, table, kept_ref, *refs):
-    before, refs = refs[: 1 if at else 0], refs[1 if at else 0 :]
-    halves, refs = refs[:n_halves], refs[n_halves:]
-    joins = []
-    if n_halves:
-        refs, whole_ref, sems = refs[:-2], refs[-2], refs[-1]
-        joins = join_copies(halves, whole_ref, sems)
-    buffers, o_ref = refs[:-1], refs[-1]
-    for r in before:
-        o_ref[:at] = r[...]
-    views = views_of(buffers, stages_of(k), layout, rank)
-    shrink_into(o_ref, at, table, k, lambda j: kept_ref[k - 1, j], views, rank)
-    for copy in joins:
-        copy.wait()
-
-
-def shrink_call(k, table, kept, before, halves, buffers, layout, rank):
+def shrink_kernel(ks, rank, at, layout, table, kept_ref, *refs):
+    buffers, o_ref = refs[1 if at else 0 : -1], refs[-1]
+    if at:
+        o_ref[:at] = refs[0][...]
+    views = views_of(buffers, stages_of_all(ks), layout, rank)
+    for i, k in enumerate(ks):
+        shrink_into(o_ref, at + i, table, k, lambda j, k=k: kept_ref[k - 1, j], views, rank)
+
+
+def shrink_call(ks, table, kept, before, buffers, layout, rank):
     width = kept.shape[3]
     at = sum(b.shape[0] for b in before)
-    shapes = [jax.ShapeDtypeStruct((at + 1, SEGMENT_ROWS, MOST * rank), jnp.float32)]
-    if halves:
-        shapes.append(jax.ShapeDtypeStruct((len(halves) * rank, halves[0].shape[1]), jnp.bfloat16))
-    return pl.pallas_call(
-        functools.partial(shrink_kernel, k, rank, at, layout, len(halves)),
-        in_specs=[SMEM] + [VMEM] * (1 + len(before) + len(halves) + len(buffers)),
-        out_specs=[VMEM] * len(shapes),
-        out_shape=shapes,
-        scratch_shapes=[pltpu.SemaphoreType.DMA((len(halves),))] if halves else [],
+    return pl.pallas_call(
+        functools.partial(shrink_kernel, ks, rank, at, layout),
+        in_specs=[SMEM] + [VMEM] * (1 + len(before) + len(buffers)),
+        out_specs=VMEM,
+        out_shape=jax.ShapeDtypeStruct((at + len(ks), SEGMENT_ROWS, MOST * rank), jnp.float32),
         compiler_params=params(4),
-        cost_estimate=cost(MOST * 2 * SEGMENT_ROWS * width * 256, 4 * SEGMENT_ROWS * width),
-    )(table, kept, *before, *halves, *buffers)
+        cost_estimate=cost(
+            len(ks) * MOST * 2 * SEGMENT_ROWS * width * 256, len(ks) * 4 * SEGMENT_ROWS * width
+        ),
+    )(table, kept, *before, *buffers)
 
 
 def fetch_up(up, at, table, k, j, views, rank):
     columns = up.shape[2]
     _, _, within = segment_of(table, k, j)
-    for ref, first, whose, i in views:
+    for stage, ref, first, whose, i in views:
+        if stage not in stages_of(k):
+            continue
 
         @pl.when((whose == table[k * ENTRIES]) & (within == i))
         def _(ref=ref, first=first):
@@ -470,10 +469,7 @@
     first = n_adapter - LATE
     upper_ref, lower_ref, refs = refs[0], refs[1], refs[2:]
     shrinks, refs = refs[: -4 - n_buffers], refs[-4 - n_buffers :]
-    buffers, (o_ref, rest_ref, up, base_ref) = refs[:-4], refs[-4:]
-    rows = upper_ref.shape[0]
-    base_ref[:rows, :] = upper_ref[...]
-    base_ref[rows:, :] = lower_ref[...]
+    buffers, (o_ref, rest_ref, up, sums) = refs[:-4], refs[-4:]
     views = views_of(buffers, range(first), layout, rank)
     for k in range(first):
         for j in range(MOST):
@@ -487,7 +483,19 @@
     for k in range(n_adapter):
         for j in range(MOST):
             start, used, _ = segment_of(table, k, j)
-            value = base_ref[pl.ds(start, SEGMENT_ROWS), :]
+            upper_rows = upper_ref.shape[0]
+
+            @pl.when(start < upper_rows)
+            def _(start=start):
+                at = pl.multiple_of(jnp.minimum(start, upper_rows - SEGMENT_ROWS), SEGMENT_ROWS)
+                sums[...] = upper_ref[pl.ds(at, SEGMENT_ROWS), :]
+
+            @pl.when(start >= upper_rows)
+            def _(start=start):
+                at = pl.multiple_of(jnp.maximum(start - upper_rows, 0), SEGMENT_ROWS)
+                sums[...] = lower_ref[pl.ds(at, SEGMENT_ROWS), :]
+
+            value = sums[...]
             if k >= first:
                 rest_ref[k - first, j] = value
                 continue
@@ -512,7 +520,7 @@
         ],
         scratch_shapes=[
             pltpu.VMEM(((n_adapter - LATE) * MOST, 2 * rank, columns), jnp.bfloat16),
-            pltpu.VMEM((rows, columns), jnp.float32),
+            pltpu.VMEM((SEGMENT_ROWS, columns), jnp.float32),
         ],
         compiler_params=params(16),
         cost_estimate=cost(6 * rows * rank * columns, (4 * n_tensor + 2) * rows * columns),
@@ -520,14 +528,14 @@
 
 
 def late_kernel(ks, n_tensor, rank, layout, table, *refs):
-    rest_ref, shrinks, refs = refs[0], refs[1 : 1 + len(ks) * n_tensor], refs[1 + len(ks) * n_tensor :]
+    rest_ref, shrinks, refs = refs[0], refs[1 : 1 + n_tensor], refs[1 + n_tensor :]
     buffers, (_, o_ref, up, out, sems) = refs[:-5], refs[-5:]
     views = views_of(buffers, stages_of_all(ks), layout, rank)
     stores = []
     for i, k in enumerate(ks):
-        share = shrinks[i * n_tensor][0]
-        for r in shrinks[i * n_tensor + 1 : (i + 1) * n_tensor]:
-            share = share + r[0]
+        share = shrinks[0][i]
+        for r in shrinks[1:]:
+            share = share + r[i]
         for j in range(MOST):
             fetch_up(up, i * MOST + j, table, k, j, views, rank)
             start, used, _ = segment_of(table, k, j)
@@ -540,10 +548,6 @@
             stores.append((used, store))
     for used, store in stores:
         pl.when(used)(store.wait)
-
-
-def stages_of_all(ks):
-    return range(stages_of(ks[0])[0], ks[-1] + 1)
 
 
 def late(ks, n_tensor, table, rest, shrinks, buffers, value, layout, rank):
@@ -606,9 +610,9 @@
     def buffers_of(stages):
         return [b for stage in stages for b in buffers[stage]]
 
-    def shrink(k, kept, before=(), halves=()):
-        mine = buffers_of(stages_of(k))
-        return shrink_call(k, table, kept, list(before), list(halves), mine, layout, rank)
+    def shrink(ks, kept, before=()):
+        mine = buffers_of(stages_of_all(ks))
+        return shrink_call(ks, table, kept, list(before), mine, layout, rank)
 
     def add_shrink(mine):
         shrinks.extend([mine] + [swap_tensor(mine, step) for step in range(1, n_tensor)])
@@ -647,12 +651,11 @@
             )
             buffers[1] += [swap_cores(joined)]
             free = lower
-            above = rows // SEGMENT_ROWS // 2
             upper = add_call(1, 0, after(upper, held[0]), sent[1])
-            lower = add_call(1, above, after(lower, upper, *held[1:]), sent[1])
-            before = shrink(1, after(kept, lower), [before])[0]
+            lower = add_call(1, UPPER, after(lower, upper, *held[1:]), sent[1])
+            before = shrink([1], after(kept, lower), [before])
         else:
-            before = shrink(stage - 1, kept, [before])[0]
+            before = shrink([stage - 1], kept, [before])
         ahead = [free] if stage == 2 else []
         swapped = [swap_cores(after(c, *ahead)) for c in came] if stage > 1 else []
         buffers.append([*came, *swapped])
@@ -669,18 +672,14 @@
         rank,
     )
     buffers.append([*held, *[swap_cores(h) for h in held]])
-    ready = after(kept, *held)
-    for k in (last - 1, last):
-        mine = shrink(k, ready)[0]
-        add_shrink(mine)
-        ready = after(kept, mine)
     ks = (last - 1, last)
+    add_shrink(shrink(ks, after(kept, *held)))
     return late(
         ks,
         n_tensor,
         table,
         remaining,
-        shrinks[-LATE * n_tensor :],
+        shrinks[-n_tensor:],
         buffers_of(stages_of_all(ks)),
         value,
         layout,

time: 63.3 us -> 63.2 us (level)
  waiting for transfers between devices: 3.03 us -> 4.91 us
  Pallas kernels: 37.3 us -> 36.2 us
    ppermute x5, waiting for transfers between devices: 0.45 us -> 2.87 us  [swap_cores(): return lax.ppermute(array, 'dp', [(0, 1), (1, 0)])]
    pallas_call x1, Pallas kernels: 7.31 us -> 6.19 us  [upper_call(): pl.pallas_call(functools.partial(upper_kernel, n_adapter), in_specs=[SMEM...]
    pallas_call x1, Pallas kernels: 6.38 us -> 7.27 us  [lower_call(): pl.pallas_call(functools.partial(lower_kernel, per_device, rank), in_spec...]
    ppermute x5 -> x4, waiting for transfers between devices: 1.61 us -> 0.91 us  [swap_tensor(): return lax.ppermute(array, 'tensor', pairs)]
    ppermute x5 -> x4, starting transfers between devices: 6.02 us -> 5.34 us  [swap_tensor(): return lax.ppermute(array, 'tensor', pairs)]
    pallas_call x3 -> x2, Pallas kernels: 4.82 us -> 4.27 us  [shrink_call(): pl.pallas_call(functools.partial(shrink_kernel, ks, rank, at, layout), in...]
  transfers between devices with their start and end apart: 16 -> 15, of which waited for: 6 -> 4; matrix products, arithmetic and copies ran while one was open for 0% -> 0% of each run, Pallas kernels for 54% -> 52%
where the time goes in v14:
time: 63.2 us; the launch traced here: 63 us
  Pallas kernels  36.2 us (57%)
  starting transfers between devices  21.5 us (34%)
  waiting for transfers between devices  4.91 us (8%)
    ppermute x6, starting transfers between devices, along_line(): return lax.ppermute(array, ('adapter', 'dp'), up + down)  15 us
    pallas_call x2, Pallas kernels, sent_call(): pl.pallas_call(functools.partial(sent_kernel, first, sizes, step, n_tenso...  10.2 us
    pallas_call x1, Pallas kernels, lower_call(): pl.pallas_call(functools.partial(lower_kernel, per_device, rank), in_spec...  7.27 us
    pallas_call x1, Pallas kernels, upper_call(): pl.pallas_call(functools.partial(upper_kernel, n_adapter), in_specs=[SMEM...  6.19 us
    ppermute x4, starting transfers between devices, swap_tensor(): return lax.ppermute(array, 'tensor', pairs)  5.34 us
    pallas_call x2, Pallas kernels, shrink_call(): pl.pallas_call(functools.partial(shrink_kernel, ks, rank, at, layout), in...  4.27 us
    ppermute x5, waiting for transfers between devices, swap_cores(): return lax.ppermute(array, 'dp', [(0, 1), (1, 0)])  2.87 us
    pallas_call x1, Pallas kernels, early(): pl.pallas_call(functools.partial(early_kernel, n_adapter, n_tensor, rank,...  2.81 us
  transfers between devices with their start and end apart: 15, of which 4 were waited for; matrix products, arithmetic and copies ran while one was open for 0% of the time, Pallas kernels for 52%

profile of v14, /device:TPU:16, one launch (start us, length us, event | category | flops | bytes accessed | tf_op | source)
XLA Modules:
  0.0 63.0 jit_solution(17978581524751040227)
XLA Ops:
  0.0 1.3 %shard_map.65 = (bf16[64,4608]{1,0:T(8,128)(2,1)S(1)}, bf16[64,4608]{1,0:T(8,128)(2,1)S(1)}) custom-call(bf16[128,4096]{1,0:T(8,128)(2,1)} %bitcast.4, bf16[128,1024]{1,0:T(8,128)(2,1)} %bitcast.5), custom_call_target="tpu_custom_call" | custom-call | bytes 2359296 | tf_op jit(solution)/shard_map/pallas_call | solution.py:91
  1.3 3.5 %collective-permute-start = (bf16[64,4608]{1,0:T(8,128)(2,1)S(1)}, bf16[64,4608]{1,0:T(8,128)(2,1)S(1)}, u32[]{:S(2)}, u32[]{:S(2)}) collective-permute-start(bf16[64,4608]{1,0:T(8,128)(2,1)S(1)} %get-tuple-element.27.refs_0_.refs_4_), channel_id=1, source_target_pairs={{0,4},{4,8},{8,12},{5,1},{9,5},{13,9},{2,6},{6,10},{10,14},{7,3},{... | collective-permute-start | bytes 1769480 | tf_op jit(solution)/shard_map/ppermute | solution.py:594
  4.8 1.9 %collective-permute-start.2 = (bf16[64,4608]{1,0:T(8,128)(2,1)S(1)}, bf16[64,4608]{1,0:T(8,128)(2,1)S(1)}, u32[]{:S(2)}, u32[]{:S(2)}) collective-permute-start(bf16[64,4608]{1,0:T(8,128)(2,1)S(1)} %get-tuple-element.29.refs_1_.refs_5_), channel_id=1, source_target_pairs={{0,4},{4,8},{8,12},{5,1},{9,5},{13,9},{2,6},{6,10},{10,14},{7,3},{... | collective-permute-start | bytes 1769480 | tf_op jit(solution)/shard_map/ppermute | solution.py:594
  6.7 3.6 %shard_map.66 = s32[168,512]{1,0:T(8,128)S(1)} custom-call(bf16[1024,4096]{1,0:T(8,128)(2,1)} %x_ref.6, bf16[4096,1024]{1,0:T(8,128)(2,1)} %w_ref.7), custom_call_target="tpu_custom_call" | custom-call | flops 1073741824 | bytes 6815744 | tf_op jit(solution)/shard_map/pallas_call | solution.py:265
  10.3 1.6 %collective-permute-start.4 = (s32[168,512]{1,0:T(8,128)S(1)}, s32[168,512]{1,0:T(8,128)S(1)}, u32[]{:S(2)}, u32[]{:S(2)}) collective-permute-start(s32[168,512]{1,0:T(8,128)S(1)} %shard_map.66), channel_id=1, source_target_pairs={{0,2},{2,0},{1,3},{3,1},{4,6},{6,4},{5,7},{7,5},{8,10},{10,8},{9,1... | collective-permute-start | bytes 1032200 | tf_op jit(solution)/shard_map/ppermute | solution.py:589
  11.9 1.4 %shard_map.64.table = s32[32]{0:T(128)} custom-call(s32[1024]{0:T(1024)} %ids.1, s32[8]{0:T(128)} %slots.1), custom_call_target="tpu_custom_call" | custom-call | bytes 4096 | tf_op jit(solution)/shard_map/pallas_call | solution.py:123
  13.3 0.0 copy-start
  13.3 0.0 collective-permute-done.refs_2_.refs_1_.refs_6_.refs_0_.refs_3_
  13.3 3.2 %collective-permute-start.1 = (bf16[64,4608]{1,0:T(8,128)(2,1)S(1)}, bf16[64,4608]{1,0:T(8,128)(2,1)S(1)}, u32[]{:S(2)}, u32[]{:S(2)}) collective-permute-start(bf16[64,4608]{1,0:T(8,128)(2,1)S(1)} %collective-permute-done.refs_2_.refs_1_.refs_6_.refs_0_.refs_3_), channel_id=1, source_target_pairs={{4,8},{8,12},{5,1},{9,5},{6,10},{10,14},{7,3},{11,7},{20,24},{24,2... | collective-permute-start | bytes 1769480 | tf_op jit(solution)/shard_map/ppermute | solution.py:594
  16.5 6.6 %shard_map.67 = s32[488,512]{1,0:T(8,128)S(1)} custom-call(bf16[1024,4096]{1,0:T(8,128)(2,1)} %x_ref.6, bf16[4096,1024]{1,0:T(8,128)(2,1)} %w_ref.7), custom_call_target="tpu_custom_call" | custom-call | flops 3221225472 | bytes 12058624 | tf_op jit(solution)/shard_map/pallas_call | solution.py:265
  23.1 0.0 collective-permute-done.2.refs_3_.refs_2_.refs_7_.refs_1_.refs_4_
  23.1 0.0 collective-permute-done.4.refs_4_
  23.1 1.6 %collective-permute-start.5 = (s32[488,512]{1,0:T(8,128)S(1)}, s32[488,512]{1,0:T(8,128)S(1)}, u32[]{:S(2)}, u32[]{:S(2)}) collective-permute-start(s32[488,512]{1,0:T(8,128)S(1)} %shard_map.67), channel_id=1, source_target_pairs={{0,2},{2,0},{1,3},{3,1},{4,6},{6,4},{5,7},{7,5},{8,10},{10,8},{9,1... | collective-permute-start | bytes 2998280 | tf_op jit(solution)/shard_map/ppermute | solution.py:589
  24.7 1.9 %collective-permute-start.6 = (bf16[64,4608]{1,0:T(8,128)(2,1)S(1)}, bf16[64,4608]{1,0:T(8,128)(2,1)S(1)}, u32[]{:S(2)}, u32[]{:S(2)}) collective-permute-start(bf16[64,4608]{1,0:T(8,128)(2,1)S(1)} %collective-permute-done.2.refs_3_.refs_2_.refs_7_.refs_1_.refs_4_), channel_id=1, source_target_pairs={{4,8},{8,12},{5,1},{9,5},{6,10},{10,14},{7,3},{11,7},{20,24},{24,2... | collective-permute-start | bytes 1769480 | tf_op jit(solution)/shard_map/ppermute | solution.py:594
  26.6 0.0 collective-permute-done.1.refs_3_.refs_6_
  26.6 2.5 %collective-permute-start.3 = (bf16[64,4608]{1,0:T(8,128)(2,1)S(1)}, bf16[64,4608]{1,0:T(8,128)(2,1)S(1)}, u32[]{:S(2)}, u32[]{:S(2)}) collective-permute-start(bf16[64,4608]{1,0:T(8,128)(2,1)S(1)} %collective-permute-done.1.refs_3_.refs_6_), channel_id=1, source_target_pairs={{8,12},{5,1},{10,14},{7,3},{24,28},{21,17},{26,30},{23,19}} | collective-permute-start | bytes 1769480 | tf_op jit(solution)/shard_map/ppermute | solution.py:594
  29.2 0.0 copy-done
  29.2 6.2 %shard_map.68 = (f32[384,512]{1,0:T(8,128)S(1)}, bf16[3,2,128,4096]{3,2,1,0:T(8,128)(2,1)S(1)}) custom-call(s32[32]{0:T(128)S(1)} %copy-done, bf16[1024,4096]{1,0:T(8,128)(2,1)} %x_ref.6, bf16[4096,1024]{1,0:T(8,128)(2,1)} %w_ref.7), custom_call_target="tpu_custom_call" | custom-call | flops 1610612736 | bytes 12582912 | tf_op jit(solution)/shard_map/pallas_call | solution.py:354
  35.4 1.1 %collective-permute-done.6.refs_4_.refs_7_ = bf16[64,4608]{1,0:T(8,128)(2,1)S(1)} collective-permute-done((bf16[64,4608]{1,0:T(8,128)(2,1)S(1)}, bf16[64,4608]{1,0:T(8,128)(2,1)S(1)}, u32[]{:S(2)}, u32[]{:S(2)}) %collective-permute-start.6) | collective-permute-done | bytes 589856 | tf_op jit(solution)/shard_map/ppermute | solution.py:594
  36.5 1.9 %collective-permute-start.7 = (bf16[64,4608]{1,0:T(8,128)(2,1)S(1)}, bf16[64,4608]{1,0:T(8,128)(2,1)S(1)}, u32[]{:S(2)}, u32[]{:S(2)}) collective-permute-start(bf16[64,4608]{1,0:T(8,128)(2,1)S(1)} %collective-permute-done.6.refs_4_.refs_7_), channel_id=1, source_target_pairs={{8,12},{5,1},{10,14},{7,3},{24,28},{21,17},{26,30},{23,19}} | collective-permute-start | bytes 1769480 | tf_op jit(solution)/shard_map/ppermute | solution.py:594
  38.4 7.3 %shard_map.70 = (f32[640,512]{1,0:T(8,128)S(1)}, f32[1,128,128]{2,1,0:T(8,128)S(1)}, bf16[128,4608]{1,0:T(8,128)(2,1)S(1)}) custom-call(s32[32]{0:T(128)S(1)} %copy-done, bf16[1024,4096]{1,0:T(8,128)(2,1)} %x_ref.6, bf16[4096,1024]{1,0:T(8,128)(2,1)} %w_ref.7, bf16[64,4608]{1,0:T(8,128)(2,1)S(1)} %get-tuple-element.27.refs_0_.refs_4_, ...), custom_call_target="tpu_custom_call" | custom-call | bytes 2097152 | tf_op jit(solution)/shard_map/pallas_call | solution.py:398
  45.7 0.1 collective-permute-start.10
  45.8 0.5 collective-permute-start.11
  46.3 0.0 collective-permute-done.3.refs_7_.refs_10_
  46.3 0.1 collective-permute-start.8
  46.4 0.0 collective-permute-done.5.refs_0_
  46.4 0.2 shard_map.69.refs_0_
  46.6 0.0 collective-permute-done.7.refs_8_.refs_11_
  46.6 0.5 collective-permute-start.12
  47.1 0.1 collective-permute-start.13
  47.2 0.3 shard_map.71.refs_1_
  47.4 2.9 %collective-permute-done.8.refs_3_.refs_8_.refs_2_.refs_5_ = bf16[128,4608]{1,0:T(8,128)(2,1)S(1)} collective-permute-done((bf16[128,4608]{1,0:T(8,128)(2,1)S(1)}, bf16[128,4608]{1,0:T(8,128)(2,1)S(1)}, u32[]{:S(2)}, u32[]{:S(2)}) %collective-permute-start.8) | collective-permute-done | bytes 1179680 | tf_op jit(solution)/shard_map/ppermute | solution.py:597
  50.3 1.7 %shard_map.72.refs_2_ = f32[2,128,128]{2,1,0:T(8,128)S(1)} custom-call(s32[32]{0:T(128)S(1)} %copy-done, bf16[3,2,128,4096]{3,2,1,0:T(8,128)(2,1)S(1)} %get-tuple-element.45.kept_ref, f32[1,128,128]{2,1,0:T(8,128)S(1)} %get-tuple-element.42.refs_0_, bf16[64,4608]{1,0:T(8,128)(2,1)S(1)} %collective-permute-done.refs_2_.refs_1_.refs_6_.refs_0_.refs_3_, ...), custom_call_target="tpu_custom_call" | custom-call | flops 536870912 | bytes 2097152 | tf_op jit(solution)/shard_map/pallas_call | solution.py:430
  52.0 0.6 collective-permute-start.9
  52.6 0.0 collective-permute-done.10.refs_5_.refs_8_
  52.6 0.0 collective-permute-done.11.refs_6_.refs_9_
  52.6 0.0 collective-permute-done.12.refs_9_.refs_12_
  52.6 0.0 collective-permute-done.13.refs_10_.refs_13_
  52.6 2.6 %shard_map.74.refs_1_ = f32[2,128,128]{2,1,0:T(8,128)S(1)} custom-call(s32[32]{0:T(128)S(1)} %copy-done, bf16[3,2,128,4096]{3,2,1,0:T(8,128)(2,1)S(1)} %get-tuple-element.45.kept_ref, bf16[64,4608]{1,0:T(8,128)(2,1)S(1)} %collective-permute-done.refs_2_.refs_1_.refs_6_.refs_0_.refs_3_, ...), custom_call_target="tpu_custom_call" | custom-call | flops 1073741824 | bytes 4194304 | tf_op jit(solution)/shard_map/pallas_call | solution.py:430
  55.2 1.6 %collective-permute-start.14 = (f32[2,128,128]{2,1,0:T(8,128)S(1)}, f32[2,128,128]{2,1,0:T(8,128)S(1)}, u32[]{:S(2)}, u32[]{:S(2)}) collective-permute-start(f32[2,128,128]{2,1,0:T(8,128)S(1)} %shard_map.74.refs_1_), channel_id=1, source_target_pairs={{0,2},{2,0},{1,3},{3,1},{4,6},{6,4},{5,7},{7,5},{8,10},{10,8},{9,1... | collective-permute-start | bytes 393224 | tf_op jit(solution)/shard_map/ppermute | solution.py:589
  56.8 0.8 %collective-permute-done.9.refs_3_ = f32[2,128,128]{2,1,0:T(8,128)S(1)} collective-permute-done((f32[2,128,128]{2,1,0:T(8,128)S(1)}, f32[2,128,128]{2,1,0:T(8,128)S(1)}, u32[]{:S(2)}, u32[]{:S(2)}) %collective-permute-start.9) | collective-permute-done | bytes 131104 | tf_op jit(solution)/shard_map/ppermute | solution.py:589
  57.6 2.8 %shard_map.73 = (bf16[1024,512]{1,0:T(8,128)(2,1)}, f32[2,2,128,512]{3,2,1,0:T(8,128)S(1)}) custom-call(s32[32]{0:T(128)S(1)} %copy-done, f32[384,512]{1,0:T(8,128)S(1)} %shard_map.69.refs_0_, f32[640,512]{1,0:T(8,128)S(1)} %shard_map.71.refs_1_, f32[2,128,128]{2,1,0:T(8,128)S(1)} %shard_map.72.refs_2_, f32[2,128,128]{2,1,0:T(8,128)S(1)} %collective-permute-done.9.refs_3_, ...), custom_call_target="tpu_custom_call" | custom-call | flops 201326592 | bytes 5242880 | tf_op jit(solution)/shard_map/pallas_call | solution.py:513
  60.4 0.1 collective-permute-done.14.refs_2_
  60.5 2.3 %shard_map.75 = bf16[1024,512]{1,0:T(8,128)(2,1)} custom-call(s32[32]{0:T(128)S(1)} %copy-done, f32[2,2,128,512]{3,2,1,0:T(8,128)S(1)} %get-tuple-element.44.refs_0_, f32[2,128,128]{2,1,0:T(8,128)S(1)} %shard_map.74.refs_1_, f32[2,128,128]{2,1,0:T(8,128)S(1)} %collective-permute-done.14.refs_2_, ...), custom_call_target="tpu_custom_call", output_to_operand_aliasing={{}: (15, {})} | custom-call | flops 100663296 | bytes 2097152 | tf_op jit(solution)/shard_map/pallas_call | solution.py:555
Async XLA Ops:
  1.3 12.1 %collective-permute-start = (bf16[64,4608]{1,0:T(8,128)(2,1)S(1)}, bf16[64,4608]{1,0:T(8,128)(2,1)S(1)}, u32[]{:S(2)}, u32[]{:S(2)}) collective-permute-start(bf16[64,4608]{1,0:T(8,128)(2,1)S(1)} %get-tuple-element.27.refs_0_.refs_4_), channel_id=1, source_target_pairs={{0,4},{4,8},{8,12},{5,1},{9,5},{13,9},{2,6},{6,10},{10,14},{7,3},{... | collective-permute-start | bytes 1769480 | tf_op jit(solution)/shard_map/ppermute | solution.py:594
  4.8 18.4 %collective-permute-start.2 = (bf16[64,4608]{1,0:T(8,128)(2,1)S(1)}, bf16[64,4608]{1,0:T(8,128)(2,1)S(1)}, u32[]{:S(2)}, u32[]{:S(2)}) collective-permute-start(bf16[64,4608]{1,0:T(8,128)(2,1)S(1)} %get-tuple-element.29.refs_1_.refs_5_), channel_id=1, source_target_pairs={{0,4},{4,8},{8,12},{5,1},{9,5},{13,9},{2,6},{6,10},{10,14},{7,3},{... | collective-permute-start | bytes 1769480 | tf_op jit(solution)/shard_map/ppermute | solution.py:594
  10.3 12.9 %collective-permute-start.4 = (s32[168,512]{1,0:T(8,128)S(1)}, s32[168,512]{1,0:T(8,128)S(1)}, u32[]{:S(2)}, u32[]{:S(2)}) collective-permute-start(s32[168,512]{1,0:T(8,128)S(1)} %shard_map.66), channel_id=1, source_target_pairs={{0,2},{2,0},{1,3},{3,1},{4,6},{6,4},{5,7},{7,5},{8,10},{10,8},{9,1... | collective-permute-start | bytes 1032200 | tf_op jit(solution)/shard_map/ppermute | solution.py:589
  13.3 15.9 %copy-start = (s32[32]{0:T(128)S(1)}, s32[32]{0:T(128)}, u32[]{:S(2)}) copy-start(s32[32]{0:T(128)} %shard_map.64.table) | copy-start | bytes 388
  13.3 13.3 %collective-permute-start.1 = (bf16[64,4608]{1,0:T(8,128)(2,1)S(1)}, bf16[64,4608]{1,0:T(8,128)(2,1)S(1)}, u32[]{:S(2)}, u32[]{:S(2)}) collective-permute-start(bf16[64,4608]{1,0:T(8,128)(2,1)S(1)} %collective-permute-done.refs_2_.refs_1_.refs_6_.refs_0_.refs_3_), channel_id=1, source_target_pairs={{4,8},{8,12},{5,1},{9,5},{6,10},{10,14},{7,3},{11,7},{20,24},{24,2... | collective-permute-start | bytes 1769480 | tf_op jit(solution)/shard_map/ppermute | solution.py:594
  23.1 23.2 %collective-permute-start.5 = (s32[488,512]{1,0:T(8,128)S(1)}, s32[488,512]{1,0:T(8,128)S(1)}, u32[]{:S(2)}, u32[]{:S(2)}) collective-permute-start(s32[488,512]{1,0:T(8,128)S(1)} %shard_map.67), channel_id=1, source_target_pairs={{0,2},{2,0},{1,3},{3,1},{4,6},{6,4},{5,7},{7,5},{8,10},{10,8},{9,1... | collective-permute-start | bytes 2998280 | tf_op jit(solution)/shard_map/ppermute | solution.py:589
  24.7 11.8 %collective-permute-start.6 = (bf16[64,4608]{1,0:T(8,128)(2,1)S(1)}, bf16[64,4608]{1,0:T(8,128)(2,1)S(1)}, u32[]{:S(2)}, u32[]{:S(2)}) collective-permute-start(bf16[64,4608]{1,0:T(8,128)(2,1)S(1)} %collective-permute-done.2.refs_3_.refs_2_.refs_7_.refs_1_.refs_4_), channel_id=1, source_target_pairs={{4,8},{8,12},{5,1},{9,5},{6,10},{10,14},{7,3},{11,7},{20,24},{24,2... | collective-permute-start | bytes 1769480 | tf_op jit(solution)/shard_map/ppermute | solution.py:594
  26.6 19.6 %collective-permute-start.3 = (bf16[64,4608]{1,0:T(8,128)(2,1)S(1)}, bf16[64,4608]{1,0:T(8,128)(2,1)S(1)}, u32[]{:S(2)}, u32[]{:S(2)}) collective-permute-start(bf16[64,4608]{1,0:T(8,128)(2,1)S(1)} %collective-permute-done.1.refs_3_.refs_6_), channel_id=1, source_target_pairs={{8,12},{5,1},{10,14},{7,3},{24,28},{21,17},{26,30},{23,19}} | collective-permute-start | bytes 1769480 | tf_op jit(solution)/shard_map/ppermute | solution.py:594
  36.5 10.2 %collective-permute-start.7 = (bf16[64,4608]{1,0:T(8,128)(2,1)S(1)}, bf16[64,4608]{1,0:T(8,128)(2,1)S(1)}, u32[]{:S(2)}, u32[]{:S(2)}) collective-permute-start(bf16[64,4608]{1,0:T(8,128)(2,1)S(1)} %collective-permute-done.6.refs_4_.refs_7_), channel_id=1, source_target_pairs={{8,12},{5,1},{10,14},{7,3},{24,28},{21,17},{26,30},{23,19}} | collective-permute-start | bytes 1769480 | tf_op jit(solution)/shard_map/ppermute | solution.py:594
  45.7 6.9 %collective-permute-start.10 = (bf16[64,4608]{1,0:T(8,128)(2,1)S(1)}, bf16[64,4608]{1,0:T(8,128)(2,1)S(1)}, u32[]{:S(2)}, u32[]{:S(2)}) collective-permute-start(bf16[64,4608]{1,0:T(8,128)(2,1)S(1)} %collective-permute-done.1.refs_3_.refs_6_), channel_id=1, source_target_pairs={{0,1},{1,0},{2,3},{3,2},{4,5},{5,4},{6,7},{7,6},{8,9},{9,8},{10,11... | collective-permute-start | bytes 1769480 | tf_op jit(solution)/shard_map/ppermute | solution.py:597
  45.8 6.8 %collective-permute-start.11 = (bf16[64,4608]{1,0:T(8,128)(2,1)S(1)}, bf16[64,4608]{1,0:T(8,128)(2,1)S(1)}, u32[]{:S(2)}, u32[]{:S(2)}) collective-permute-start(bf16[64,4608]{1,0:T(8,128)(2,1)S(1)} %collective-permute-done.6.refs_4_.refs_7_), channel_id=1, source_target_pairs={{0,1},{1,0},{2,3},{3,2},{4,5},{5,4},{6,7},{7,6},{8,9},{9,8},{10,11... | collective-permute-start | bytes 1769480 | tf_op jit(solution)/shard_map/ppermute | solution.py:597
  46.3 4.0 %collective-permute-start.8 = (bf16[128,4608]{1,0:T(8,128)(2,1)S(1)}, bf16[128,4608]{1,0:T(8,128)(2,1)S(1)}, u32[]{:S(2)}, u32[]{:S(2)}) collective-permute-start(bf16[128,4608]{1,0:T(8,128)(2,1)S(1)} %get-tuple-element.43), channel_id=1, source_target_pairs={{0,1},{1,0},{2,3},{3,2},{4,5},{5,4},{6,7},{7,6},{8,9},{9,8},{10,11... | collective-permute-start | bytes 3538952 | tf_op jit(solution)/shard_map/ppermute | solution.py:597
  46.6 5.9 %collective-permute-start.12 = (bf16[64,4608]{1,0:T(8,128)(2,1)S(1)}, bf16[64,4608]{1,0:T(8,128)(2,1)S(1)}, u32[]{:S(2)}, u32[]{:S(2)}) collective-permute-start(bf16[64,4608]{1,0:T(8,128)(2,1)S(1)} %collective-permute-done.3.refs_7_.refs_10_), channel_id=1, source_target_pairs={{0,1},{1,0},{2,3},{3,2},{4,5},{5,4},{6,7},{7,6},{8,9},{9,8},{10,11... | collective-permute-start | bytes 1769480 | tf_op jit(solution)/shard_map/ppermute | solution.py:597
  47.1 5.5 %collective-permute-start.13 = (bf16[64,4608]{1,0:T(8,128)(2,1)S(1)}, bf16[64,4608]{1,0:T(8,128)(2,1)S(1)}, u32[]{:S(2)}, u32[]{:S(2)}) collective-permute-start(bf16[64,4608]{1,0:T(8,128)(2,1)S(1)} %collective-permute-done.7.refs_8_.refs_11_), channel_id=1, source_target_pairs={{0,1},{1,0},{2,3},{3,2},{4,5},{5,4},{6,7},{7,6},{8,9},{9,8},{10,11... | collective-permute-start | bytes 1769480 | tf_op jit(solution)/shard_map/ppermute | solution.py:597
  52.0 5.6 %collective-permute-start.9 = (f32[2,128,128]{2,1,0:T(8,128)S(1)}, f32[2,128,128]{2,1,0:T(8,128)S(1)}, u32[]{:S(2)}, u32[]{:S(2)}) collective-permute-start(f32[2,128,128]{2,1,0:T(8,128)S(1)} %shard_map.72.refs_2_), channel_id=1, source_target_pairs={{0,2},{2,0},{1,3},{3,1},{4,6},{6,4},{5,7},{7,5},{8,10},{10,8},{9,1... | collective-permute-start | bytes 393224 | tf_op jit(solution)/shard_map/ppermute | solution.py:589
  55.2 5.3 %collective-permute-start.14 = (f32[2,128,128]{2,1,0:T(8,128)S(1)}, f32[2,128,128]{2,1,0:T(8,128)S(1)}, u32[]{:S(2)}, u32[]{:S(2)}) collective-permute-start(f32[2,128,128]{2,1,0:T(8,128)S(1)} %shard_map.74.refs_1_), channel_id=1, source_target_pairs={{0,2},{2,0},{1,3},{3,1},{4,6},{6,4},{5,7},{7,5},{8,10},{10,8},{9,1... | collective-permute-start | bytes 393224 | tf_op jit(solution)/shard_map/ppermute | solution.py:589

commit v15 on v14

--- a/solution.py
+++ b/solution.py
@@ -310,11 +310,23 @@
                 )
 
 
-def join_copies(halves, whole, sems):
-    copies, rank = [], halves[0].shape[0]
-    for i, half in enumerate(halves):
+SPLIT = 2
+
+
+def split_copies(halves, quarters, sems):
+    copies, rows = [], quarters[0].shape[0]
+    for i, quarter in enumerate(quarters):
+        part = halves[i // SPLIT].at[pl.ds(i % SPLIT * rows, rows), :]
+        copies.append(pltpu.make_async_copy(part, quarter, sems.at[i]))
+        copies[-1].start()
+    return copies
+
+
+def join_copies(quarters, whole, sems):
+    copies, rows = [], quarters[0].shape[0]
+    for i, quarter in enumerate(quarters):
         copies.append(
-            pltpu.make_async_copy(half, whole.at[pl.ds(i * rank, rank), :], sems.at[i])
+            pltpu.make_async_copy(quarter, whole.at[pl.ds(i * rows, rows), :], sems.at[i])
         )
         copies[-1].start()
     return copies
@@ -368,9 +380,10 @@
 
 def lower_kernel(per_device, rank, table, x_ref, w_ref, *refs):
     messages, halves, refs = refs[:per_device], refs[per_device : 2 * per_device], refs[2 * per_device :]
-    coded_refs, (o_ref, s_ref, whole_ref, x, w, sems, mine, mine_sems, join_sems) = refs[:-9], refs[-9:]
+    coded_refs, (o_ref, s_ref, *refs) = refs[: -8 - SPLIT * per_device], refs[-8 - SPLIT * per_device :]
+    quarters, (x, w, sems, mine, mine_sems, join_sems) = refs[:-6], refs[-6:]
     work = load_base(UPPER, x.shape[0] // SEGMENT_ROWS, lax.axis_index("tensor"), x_ref, w_ref, x, w, sems)
-    joins = join_copies(halves, whole_ref, join_sems)
+    joins = split_copies(halves, quarters, join_sems)
     loads = []
     for j in range(MOST):
         start, _, _ = segment_of(table, 0, j)
@@ -398,45 +411,60 @@
     return pl.pallas_call(
         functools.partial(lower_kernel, per_device, rank),
         in_specs=[SMEM, HBM, HBM] + [VMEM] * (2 * per_device + len(coded)),
-        out_specs=[VMEM] * 3,
+        out_specs=[VMEM] * (2 + SPLIT * per_device),
         out_shape=[
             jax.ShapeDtypeStruct((half, columns), jnp.float32),
             jax.ShapeDtypeStruct((1, SEGMENT_ROWS, MOST * rank), jnp.float32),
-            jax.ShapeDtypeStruct((per_device * rank, long), jnp.bfloat16),
-        ],
+        ]
+        + [jax.ShapeDtypeStruct((rank // SPLIT, long), jnp.bfloat16)] * (SPLIT * per_device),
         scratch_shapes=base_scratch(half // SEGMENT_ROWS, width, columns)
         + [
             pltpu.VMEM((MOST, SEGMENT_ROWS, width), jnp.bfloat16),
             pltpu.SemaphoreType.DMA((MOST,)),
-            pltpu.SemaphoreType.DMA((per_device,)),
+            pltpu.SemaphoreType.DMA((SPLIT * per_device,)),
         ],
         compiler_params=params(14),
         cost_estimate=cost(0 * half * width * columns, 4 * rows * columns),
     )(table, tokens, weight, *messages, *halves, *coded)
 
 
-def shrink_kernel(ks, rank, at, layout, table, kept_ref, *refs):
-    buffers, o_ref = refs[1 if at else 0 : -1], refs[-1]
-    if at:
-        o_ref[:at] = refs[0][...]
+def shrink_kernel(ks, rank, at, layout, n_quarters, table, kept_ref, *refs):
+    before, refs = refs[: 1 if at else 0], refs[1 if at else 0 :]
+    quarters, refs = refs[:n_quarters], refs[n_quarters:]
+    if n_quarters:
+        buffers, (o_ref, whole_ref, sems) = refs[:-3], refs[-3:]
+        joins = join_copies(quarters, whole_ref, sems)
+        buffers = [*buffers, whole_ref]
+    else:
+        buffers, o_ref, joins = refs[:-1], refs[-1], []
+    for r in before:
+        o_ref[:at] = r[...]
+    for copy in joins:
+        copy.wait()
     views = views_of(buffers, stages_of_all(ks), layout, rank)
     for i, k in enumerate(ks):
         shrink_into(o_ref, at + i, table, k, lambda j, k=k: kept_ref[k - 1, j], views, rank)
 
 
-def shrink_call(ks, table, kept, before, buffers, layout, rank):
+def shrink_call(ks, table, kept, before, quarters, buffers, layout, rank):
     width = kept.shape[3]
     at = sum(b.shape[0] for b in before)
-    return pl.pallas_call(
-        functools.partial(shrink_kernel, ks, rank, at, layout),
-        in_specs=[SMEM] + [VMEM] * (1 + len(before) + len(buffers)),
-        out_specs=VMEM,
-        out_shape=jax.ShapeDtypeStruct((at + len(ks), SEGMENT_ROWS, MOST * rank), jnp.float32),
+    n = len(quarters)
+    shapes = [jax.ShapeDtypeStruct((at + len(ks), SEGMENT_ROWS, MOST * rank), jnp.float32)]
+    if n:
+        rows, long = quarters[0].shape
+        shapes.append(jax.ShapeDtypeStruct((n * rows, long), jnp.bfloat16))
+    return pl.pallas_call(
+        functools.partial(shrink_kernel, ks, rank, at, layout, n),
+        in_specs=[SMEM] + [VMEM] * (1 + len(before) + n + len(buffers)),
+        out_specs=[VMEM] * len(shapes),
+        out_shape=shapes,
+        scratch_shapes=[pltpu.SemaphoreType.DMA((n,))] if n else [],
         compiler_params=params(4),
         cost_estimate=cost(
             len(ks) * MOST * 2 * SEGMENT_ROWS * width * 256, len(ks) * 4 * SEGMENT_ROWS * width
         ),
-    )(table, kept, *before, *buffers)
+    )(table, kept, *before, *quarters, *buffers)
 
 
 def fetch_up(up, at, table, k, j, views, rank):
@@ -610,9 +638,9 @@
     def buffers_of(stages):
         return [b for stage in stages for b in buffers[stage]]
 
-    def shrink(ks, kept, before=()):
+    def shrink(ks, kept, before=(), quarters=()):
         mine = buffers_of(stages_of_all(ks))
-        return shrink_call(ks, table, kept, list(before), mine, layout, rank)
+        return shrink_call(ks, table, kept, list(before), list(quarters), mine, layout, rank)
 
     def add_shrink(mine):
         shrinks.extend([mine] + [swap_tensor(mine, step) for step in range(1, n_tensor)])
@@ -646,16 +674,17 @@
                 after(table, held[0], *came), tokens, value_weight, columns, n_adapter
             )
         elif stage == 2:
-            lower, before, joined = lower_call(
+            lower, before, *quarters = lower_call(
                 after(table, *came), tokens, value_weight, messages, buffers[1], sent[0], columns
             )
-            buffers[1] += [swap_cores(joined)]
+            quarters = [swap_cores(q) for q in quarters]
             free = lower
             upper = add_call(1, 0, after(upper, held[0]), sent[1])
-            lower = add_call(1, UPPER, after(lower, upper, *held[1:]), sent[1])
-            before = shrink([1], after(kept, lower), [before])
+            lower = add_call(1, UPPER, after(lower, upper), sent[1])
+            before, joined = shrink([1], after(kept, lower), [before], quarters)
+            buffers[1].append(joined)
         else:
-            before = shrink([stage - 1], kept, [before])
+            before = shrink([stage - 1], kept, [before])[0]
         ahead = [free] if stage == 2 else []
         swapped = [swap_cores(after(c, *ahead)) for c in came] if stage > 1 else []
         buffers.append([*came, *swapped])
@@ -671,9 +700,9 @@
         layout,
         rank,
     )
-    buffers.append([*held, *[swap_cores(h) for h in held]])
+    buffers.append([*held, *[swap_cores(after(h, before)) for h in held]])
     ks = (last - 1, last)
-    add_shrink(shrink(ks, after(kept, *held)))
+    add_shrink(shrink(ks, after(kept, *held))[0])
     return late(
         ks,
         n_tensor,

time: 63.2 us -> 64.5 us (1.021)
  waiting for transfers between devices: 4.91 us -> 6.02 us
    ppermute x4, waiting for transfers between devices: 0.91 us -> 2.21 us  [swap_tensor(): return lax.ppermute(array, 'tensor', pairs)]
    ppermute x4, starting transfers between devices: 5.34 us -> 4.31 us  [swap_tensor(): return lax.ppermute(array, 'tensor', pairs)]
    ppermute x5 -> x8, starting transfers between devices: 1.19 us -> 1.93 us  [swap_cores(): return lax.ppermute(array, 'dp', [(0, 1), (1, 0)])]
    ppermute x5 -> x8, waiting for transfers between devices: 2.87 us -> 2.88 us  [swap_cores(): return lax.ppermute(array, 'dp', [(0, 1), (1, 0)])]
  transfers between devices with their start and end apart: 15 -> 18, of which waited for: 4 -> 8; matrix products, arithmetic and copies ran while one was open for 0% -> 0% of each run, Pallas kernels for 52% -> 51%
where the time goes in v15:
time: 64.5 us; the launch traced here: 64.1 us
  Pallas kernels  36.5 us (57%)
  starting transfers between devices  21.2 us (33%)
  waiting for transfers between devices  6.02 us (9%)
    ppermute x6, starting transfers between devices, along_line(): return lax.ppermute(array, ('adapter', 'dp'), up + down)  15 us
    pallas_call x2, Pallas kernels, sent_call(): pl.pallas_call(functools.partial(sent_kernel, first, sizes, step, n_tenso...  10.2 us
    pallas_call x1, Pallas kernels, lower_call(): pl.pallas_call(functools.partial(lower_kernel, per_device, rank), in_spec...  7.12 us
    pallas_call x1, Pallas kernels, upper_call(): pl.pallas_call(functools.partial(upper_kernel, n_adapter), in_specs=[SMEM...  6.36 us
    pallas_call x2, Pallas kernels, shrink_call(): pl.pallas_call(functools.partial(shrink_kernel, ks, rank, at, layout, n),...  4.55 us
    ppermute x4, starting transfers between devices, swap_tensor(): return lax.ppermute(array, 'tensor', pairs)  4.31 us
    ppermute x8, waiting for transfers between devices, swap_cores(): return lax.ppermute(array, 'dp', [(0, 1), (1, 0)])  2.88 us
    pallas_call x1, Pallas kernels, early(): pl.pallas_call(functools.partial(early_kernel, n_adapter, n_tensor, rank,...  2.81 us
  transfers between devices with their start and end apart: 18, of which 8 were waited for; matrix products, arithmetic and copies ran while one was open for 0% of the time, Pallas kernels for 51%

profile of v15, /device:TPU:16, one launch (start us, length us, event | category | flops | bytes accessed | tf_op | source)
XLA Modules:
  0.0 64.1 jit_solution(12019597158425626305)
XLA Ops:
  0.0 1.3 %shard_map.65 = (bf16[64,4608]{1,0:T(8,128)(2,1)S(1)}, bf16[64,4608]{1,0:T(8,128)(2,1)S(1)}) custom-call(bf16[128,4096]{1,0:T(8,128)(2,1)} %bitcast.4, bf16[128,1024]{1,0:T(8,128)(2,1)} %bitcast.5), custom_call_target="tpu_custom_call" | custom-call | bytes 2359296 | tf_op jit(solution)/shard_map/pallas_call | solution.py:91
  1.3 3.5 %collective-permute-start = (bf16[64,4608]{1,0:T(8,128)(2,1)S(1)}, bf16[64,4608]{1,0:T(8,128)(2,1)S(1)}, u32[]{:S(2)}, u32[]{:S(2)}) collective-permute-start(bf16[64,4608]{1,0:T(8,128)(2,1)S(1)} %get-tuple-element.34.refs_0_.refs_4_), channel_id=1, source_target_pairs={{0,4},{4,8},{8,12},{5,1},{9,5},{13,9},{2,6},{6,10},{10,14},{7,3},{... | collective-permute-start | bytes 1769480 | tf_op jit(solution)/shard_map/ppermute | solution.py:622
  4.8 1.9 %collective-permute-start.2 = (bf16[64,4608]{1,0:T(8,128)(2,1)S(1)}, bf16[64,4608]{1,0:T(8,128)(2,1)S(1)}, u32[]{:S(2)}, u32[]{:S(2)}) collective-permute-start(bf16[64,4608]{1,0:T(8,128)(2,1)S(1)} %get-tuple-element.36.refs_1_.refs_5_), channel_id=1, source_target_pairs={{0,4},{4,8},{8,12},{5,1},{9,5},{13,9},{2,6},{6,10},{10,14},{7,3},{... | collective-permute-start | bytes 1769480 | tf_op jit(solution)/shard_map/ppermute | solution.py:622
  6.7 3.6 %shard_map.66 = s32[168,512]{1,0:T(8,128)S(1)} custom-call(bf16[1024,4096]{1,0:T(8,128)(2,1)} %x_ref.6, bf16[4096,1024]{1,0:T(8,128)(2,1)} %w_ref.7), custom_call_target="tpu_custom_call" | custom-call | flops 1073741824 | bytes 6815744 | tf_op jit(solution)/shard_map/pallas_call | solution.py:265
  10.3 1.6 %collective-permute-start.4 = (s32[168,512]{1,0:T(8,128)S(1)}, s32[168,512]{1,0:T(8,128)S(1)}, u32[]{:S(2)}, u32[]{:S(2)}) collective-permute-start(s32[168,512]{1,0:T(8,128)S(1)} %shard_map.66), channel_id=1, source_target_pairs={{0,2},{2,0},{1,3},{3,1},{4,6},{6,4},{5,7},{7,5},{8,10},{10,8},{9,1... | collective-permute-start | bytes 1032200 | tf_op jit(solution)/shard_map/ppermute | solution.py:617
  11.9 1.4 %shard_map.64.table = s32[32]{0:T(128)} custom-call(s32[1024]{0:T(1024)} %ids.1, s32[8]{0:T(128)} %slots.1), custom_call_target="tpu_custom_call" | custom-call | bytes 4096 | tf_op jit(solution)/shard_map/pallas_call | solution.py:123
  13.3 0.0 copy-start
  13.3 0.0 collective-permute-done.refs_2_.refs_5_.refs_6_.refs_0_.refs_3_
  13.3 3.2 %collective-permute-start.1 = (bf16[64,4608]{1,0:T(8,128)(2,1)S(1)}, bf16[64,4608]{1,0:T(8,128)(2,1)S(1)}, u32[]{:S(2)}, u32[]{:S(2)}) collective-permute-start(bf16[64,4608]{1,0:T(8,128)(2,1)S(1)} %collective-permute-done.refs_2_.refs_5_.refs_6_.refs_0_.refs_3_), channel_id=1, source_target_pairs={{4,8},{8,12},{5,1},{9,5},{6,10},{10,14},{7,3},{11,7},{20,24},{24,2... | collective-permute-start | bytes 1769480 | tf_op jit(solution)/shard_map/ppermute | solution.py:622
  16.5 6.6 %shard_map.67 = s32[488,512]{1,0:T(8,128)S(1)} custom-call(bf16[1024,4096]{1,0:T(8,128)(2,1)} %x_ref.6, bf16[4096,1024]{1,0:T(8,128)(2,1)} %w_ref.7), custom_call_target="tpu_custom_call" | custom-call | flops 3221225472 | bytes 12058624 | tf_op jit(solution)/shard_map/pallas_call | solution.py:265
  23.1 0.0 collective-permute-done.2.refs_3_.refs_6_.refs_7_.refs_1_.refs_4_
  23.1 0.0 collective-permute-done.4.refs_4_
  23.1 1.6 %collective-permute-start.5 = (s32[488,512]{1,0:T(8,128)S(1)}, s32[488,512]{1,0:T(8,128)S(1)}, u32[]{:S(2)}, u32[]{:S(2)}) collective-permute-start(s32[488,512]{1,0:T(8,128)S(1)} %shard_map.67), channel_id=1, source_target_pairs={{0,2},{2,0},{1,3},{3,1},{4,6},{6,4},{5,7},{7,5},{8,10},{10,8},{9,1... | collective-permute-start | bytes 2998280 | tf_op jit(solution)/shard_map/ppermute | solution.py:617
  24.7 1.9 %collective-permute-start.6 = (bf16[64,4608]{1,0:T(8,128)(2,1)S(1)}, bf16[64,4608]{1,0:T(8,128)(2,1)S(1)}, u32[]{:S(2)}, u32[]{:S(2)}) collective-permute-start(bf16[64,4608]{1,0:T(8,128)(2,1)S(1)} %collective-permute-done.2.refs_3_.refs_6_.refs_7_.refs_1_.refs_4_), channel_id=1, source_target_pairs={{4,8},{8,12},{5,1},{9,5},{6,10},{10,14},{7,3},{11,7},{20,24},{24,2... | collective-permute-start | bytes 1769480 | tf_op jit(solution)/shard_map/ppermute | solution.py:622
  26.6 0.0 collective-permute-done.1.refs_3_.refs_6_
  26.6 2.5 %collective-permute-start.3 = (bf16[64,4608]{1,0:T(8,128)(2,1)S(1)}, bf16[64,4608]{1,0:T(8,128)(2,1)S(1)}, u32[]{:S(2)}, u32[]{:S(2)}) collective-permute-start(bf16[64,4608]{1,0:T(8,128)(2,1)S(1)} %collective-permute-done.1.refs_3_.refs_6_), channel_id=1, source_target_pairs={{8,12},{5,1},{10,14},{7,3},{24,28},{21,17},{26,30},{23,19}} | collective-permute-start | bytes 1769480 | tf_op jit(solution)/shard_map/ppermute | solution.py:622
  29.2 0.0 copy-done
  29.2 6.4 %shard_map.68 = (f32[384,512]{1,0:T(8,128)S(1)}, bf16[3,2,128,4096]{3,2,1,0:T(8,128)(2,1)S(1)}) custom-call(s32[32]{0:T(128)S(1)} %copy-done, bf16[1024,4096]{1,0:T(8,128)(2,1)} %x_ref.6, bf16[4096,1024]{1,0:T(8,128)(2,1)} %w_ref.7), custom_call_target="tpu_custom_call" | custom-call | flops 1610612736 | bytes 12582912 | tf_op jit(solution)/shard_map/pallas_call | solution.py:366
  35.6 0.9 %collective-permute-done.6.refs_4_.refs_7_ = bf16[64,4608]{1,0:T(8,128)(2,1)S(1)} collective-permute-done((bf16[64,4608]{1,0:T(8,128)(2,1)S(1)}, bf16[64,4608]{1,0:T(8,128)(2,1)S(1)}, u32[]{:S(2)}, u32[]{:S(2)}) %collective-permute-start.6) | collective-permute-done | bytes 589856 | tf_op jit(solution)/shard_map/ppermute | solution.py:622
  36.5 1.9 %collective-permute-start.12 = (bf16[64,4608]{1,0:T(8,128)(2,1)S(1)}, bf16[64,4608]{1,0:T(8,128)(2,1)S(1)}, u32[]{:S(2)}, u32[]{:S(2)}) collective-permute-start(bf16[64,4608]{1,0:T(8,128)(2,1)S(1)} %collective-permute-done.6.refs_4_.refs_7_), channel_id=1, source_target_pairs={{8,12},{5,1},{10,14},{7,3},{24,28},{21,17},{26,30},{23,19}} | collective-permute-start | bytes 1769480 | tf_op jit(solution)/shard_map/ppermute | solution.py:622
  38.4 7.1 %shard_map.70 = (f32[640,512]{1,0:T(8,128)S(1)}, f32[1,128,128]{2,1,0:T(8,128)S(1)}, bf16[32,4608]{1,0:T(8,128)(2,1)S(1)}, bf16[32,4608]{1,0:T(8,128)(2,1)S(1)},...) custom-call(s32[32]{0:T(128)S(1)} %copy-done, bf16[1024,4096]{1,0:T(8,128)(2,1)} %x_ref.6, ...), custom_call_target="tpu_custom_call" | custom-call | bytes 2097152 | tf_op jit(solution)/shard_map/pallas_call | solution.py:411
  45.6 0.1 collective-permute-start.7
  45.6 0.5 collective-permute-start.8
  46.1 0.0 collective-permute-done.3.refs_7_.refs_10_
  46.1 0.1 collective-permute-start.9
  46.2 0.0 collective-permute-done.5.refs_0_
  46.2 0.4 collective-permute-start.10
  46.6 0.2 shard_map.69.refs_0_
  46.9 0.2 shard_map.71.refs_1_
  47.1 0.1 collective-permute-done.7.refs_1_
  47.2 0.1 collective-permute-start.13
  47.3 0.3 collective-permute-done.8.refs_2_
  47.6 0.1 collective-permute-start.14
  47.8 0.3 collective-permute-done.9.refs_3_
  48.0 0.4 collective-permute-done.10.refs_4_
  48.5 2.0 %shard_map.72 = (f32[2,128,128]{2,1,0:T(8,128)S(1)}, bf16[128,4608]{1,0:T(8,128)(2,1)S(1)}) custom-call(s32[32]{0:T(128)S(1)} %copy-done, bf16[3,2,128,4096]{3,2,1,0:T(8,128)(2,1)S(1)} %get-tuple-element.57.kept_ref, f32[1,128,128]{2,1,0:T(8,128)S(1)} %get-tuple-element.49.refs_0_, bf16[32,4608]{1,0:T(8,128)(2,1)S(1)} %collective-permute-done.7.refs_1_, ...), custom_call_target="tpu_custom_call" | custom-call | flops 536870912 | bytes 2097152 | tf_op jit(solution)/shard_map/pallas_call | solution.py:457
  50.4 0.0 collective-permute-done.12.refs_8_.refs_11_
  50.5 0.2 collective-permute-start.15
  50.6 0.4 collective-permute-start.16
  51.0 0.5 collective-permute-start.11
  51.6 0.0 collective-permute-done.13.refs_5_.refs_8_
  51.6 0.0 collective-permute-done.14.refs_6_.refs_9_
  51.6 1.0 %collective-permute-done.15.refs_9_.refs_12_ = bf16[64,4608]{1,0:T(8,128)(2,1)S(1)} collective-permute-done((bf16[64,4608]{1,0:T(8,128)(2,1)S(1)}, bf16[64,4608]{1,0:T(8,128)(2,1)S(1)}, u32[]{:S(2)}, u32[]{:S(2)}) %collective-permute-start.15) | collective-permute-done | bytes 589856 | tf_op jit(solution)/shard_map/ppermute | solution.py:625
  52.5 0.8 %collective-permute-done.16.refs_10_.refs_13_ = bf16[64,4608]{1,0:T(8,128)(2,1)S(1)} collective-permute-done((bf16[64,4608]{1,0:T(8,128)(2,1)S(1)}, bf16[64,4608]{1,0:T(8,128)(2,1)S(1)}, u32[]{:S(2)}, u32[]{:S(2)}) %collective-permute-start.16) | collective-permute-done | bytes 589856 | tf_op jit(solution)/shard_map/ppermute | solution.py:625
  53.4 2.6 %shard_map.74.refs_1_ = f32[2,128,128]{2,1,0:T(8,128)S(1)} custom-call(s32[32]{0:T(128)S(1)} %copy-done, bf16[3,2,128,4096]{3,2,1,0:T(8,128)(2,1)S(1)} %get-tuple-element.57.kept_ref, bf16[64,4608]{1,0:T(8,128)(2,1)S(1)} %collective-permute-done.refs_2_.refs_5_.refs_6_.refs_0_.refs_3_, ...), custom_call_target="tpu_custom_call" | custom-call | flops 1073741824 | bytes 4194304 | tf_op jit(solution)/shard_map/pallas_call | solution.py:457
  56.0 0.6 collective-permute-start.17
  56.6 0.0 collective-permute-done.11.refs_3_
  56.6 2.8 %shard_map.73 = (bf16[1024,512]{1,0:T(8,128)(2,1)}, f32[2,2,128,512]{3,2,1,0:T(8,128)S(1)}) custom-call(s32[32]{0:T(128)S(1)} %copy-done, f32[384,512]{1,0:T(8,128)S(1)} %shard_map.69.refs_0_, f32[640,512]{1,0:T(8,128)S(1)} %shard_map.71.refs_1_, f32[2,128,128]{2,1,0:T(8,128)S(1)} %get-tuple-element.54.refs_2_, ...), custom_call_target="tpu_custom_call" | custom-call | flops 201326592 | bytes 5242880 | tf_op jit(solution)/shard_map/pallas_call | solution.py:541
  59.4 2.2 %collective-permute-done.17.refs_2_ = f32[2,128,128]{2,1,0:T(8,128)S(1)} collective-permute-done((f32[2,128,128]{2,1,0:T(8,128)S(1)}, f32[2,128,128]{2,1,0:T(8,128)S(1)}, u32[]{:S(2)}, u32[]{:S(2)}) %collective-permute-start.17) | collective-permute-done | bytes 131104 | tf_op jit(solution)/shard_map/ppermute | solution.py:617
  61.6 2.3 %shard_map.75 = bf16[1024,512]{1,0:T(8,128)(2,1)} custom-call(s32[32]{0:T(128)S(1)} %copy-done, f32[2,2,128,512]{3,2,1,0:T(8,128)S(1)} %get-tuple-element.56.refs_0_, f32[2,128,128]{2,1,0:T(8,128)S(1)} %shard_map.74.refs_1_, f32[2,128,128]{2,1,0:T(8,128)S(1)} %collective-permute-done.17.refs_2_, ...), custom_call_target="tpu_custom_call", output_to_operand_aliasing={{}: (15, {})} | custom-call | flops 100663296 | bytes 2097152 | tf_op jit(solution)/shard_map/pallas_call | solution.py:583
Async XLA Ops:
  1.3 12.1 %collective-permute-start = (bf16[64,4608]{1,0:T(8,128)(2,1)S(1)}, bf16[64,4608]{1,0:T(8,128)(2,1)S(1)}, u32[]{:S(2)}, u32[]{:S(2)}) collective-permute-start(bf16[64,4608]{1,0:T(8,128)(2,1)S(1)} %get-tuple-element.34.refs_0_.refs_4_), channel_id=1, source_target_pairs={{0,4},{4,8},{8,12},{5,1},{9,5},{13,9},{2,6},{6,10},{10,14},{7,3},{... | collective-permute-start | bytes 1769480 | tf_op jit(solution)/shard_map/ppermute | solution.py:622
  4.8 18.4 %collective-permute-start.2 = (bf16[64,4608]{1,0:T(8,128)(2,1)S(1)}, bf16[64,4608]{1,0:T(8,128)(2,1)S(1)}, u32[]{:S(2)}, u32[]{:S(2)}) collective-permute-start(bf16[64,4608]{1,0:T(8,128)(2,1)S(1)} %get-tuple-element.36.refs_1_.refs_5_), channel_id=1, source_target_pairs={{0,4},{4,8},{8,12},{5,1},{9,5},{13,9},{2,6},{6,10},{10,14},{7,3},{... | collective-permute-start | bytes 1769480 | tf_op jit(solution)/shard_map/ppermute | solution.py:622
  10.3 12.9 %collective-permute-start.4 = (s32[168,512]{1,0:T(8,128)S(1)}, s32[168,512]{1,0:T(8,128)S(1)}, u32[]{:S(2)}, u32[]{:S(2)}) collective-permute-start(s32[168,512]{1,0:T(8,128)S(1)} %shard_map.66), channel_id=1, source_target_pairs={{0,2},{2,0},{1,3},{3,1},{4,6},{6,4},{5,7},{7,5},{8,10},{10,8},{9,1... | collective-permute-start | bytes 1032200 | tf_op jit(solution)/shard_map/ppermute | solution.py:617
  13.3 15.9 %copy-start = (s32[32]{0:T(128)S(1)}, s32[32]{0:T(128)}, u32[]{:S(2)}) copy-start(s32[32]{0:T(128)} %shard_map.64.table) | copy-start | bytes 388
  13.3 13.3 %collective-permute-start.1 = (bf16[64,4608]{1,0:T(8,128)(2,1)S(1)}, bf16[64,4608]{1,0:T(8,128)(2,1)S(1)}, u32[]{:S(2)}, u32[]{:S(2)}) collective-permute-start(bf16[64,4608]{1,0:T(8,128)(2,1)S(1)} %collective-permute-done.refs_2_.refs_5_.refs_6_.refs_0_.refs_3_), channel_id=1, source_target_pairs={{4,8},{8,12},{5,1},{9,5},{6,10},{10,14},{7,3},{11,7},{20,24},{24,2... | collective-permute-start | bytes 1769480 | tf_op jit(solution)/shard_map/ppermute | solution.py:622
  23.1 23.1 %collective-permute-start.5 = (s32[488,512]{1,0:T(8,128)S(1)}, s32[488,512]{1,0:T(8,128)S(1)}, u32[]{:S(2)}, u32[]{:S(2)}) collective-permute-start(s32[488,512]{1,0:T(8,128)S(1)} %shard_map.67), channel_id=1, source_target_pairs={{0,2},{2,0},{1,3},{3,1},{4,6},{6,4},{5,7},{7,5},{8,10},{10,8},{9,1... | collective-permute-start | bytes 2998280 | tf_op jit(solution)/shard_map/ppermute | solution.py:617
  24.7 11.8 %collective-permute-start.6 = (bf16[64,4608]{1,0:T(8,128)(2,1)S(1)}, bf16[64,4608]{1,0:T(8,128)(2,1)S(1)}, u32[]{:S(2)}, u32[]{:S(2)}) collective-permute-start(bf16[64,4608]{1,0:T(8,128)(2,1)S(1)} %collective-permute-done.2.refs_3_.refs_6_.refs_7_.refs_1_.refs_4_), channel_id=1, source_target_pairs={{4,8},{8,12},{5,1},{9,5},{6,10},{10,14},{7,3},{11,7},{20,24},{24,2... | collective-permute-start | bytes 1769480 | tf_op jit(solution)/shard_map/ppermute | solution.py:622
  26.6 19.5 %collective-permute-start.3 = (bf16[64,4608]{1,0:T(8,128)(2,1)S(1)}, bf16[64,4608]{1,0:T(8,128)(2,1)S(1)}, u32[]{:S(2)}, u32[]{:S(2)}) collective-permute-start(bf16[64,4608]{1,0:T(8,128)(2,1)S(1)} %collective-permute-done.1.refs_3_.refs_6_), channel_id=1, source_target_pairs={{8,12},{5,1},{10,14},{7,3},{24,28},{21,17},{26,30},{23,19}} | collective-permute-start | bytes 1769480 | tf_op jit(solution)/shard_map/ppermute | solution.py:622
  36.5 14.0 %collective-permute-start.12 = (bf16[64,4608]{1,0:T(8,128)(2,1)S(1)}, bf16[64,4608]{1,0:T(8,128)(2,1)S(1)}, u32[]{:S(2)}, u32[]{:S(2)}) collective-permute-start(bf16[64,4608]{1,0:T(8,128)(2,1)S(1)} %collective-permute-done.6.refs_4_.refs_7_), channel_id=1, source_target_pairs={{8,12},{5,1},{10,14},{7,3},{24,28},{21,17},{26,30},{23,19}} | collective-permute-start | bytes 1769480 | tf_op jit(solution)/shard_map/ppermute | solution.py:622
  45.6 1.6 %collective-permute-start.7 = (bf16[32,4608]{1,0:T(8,128)(2,1)S(1)}, bf16[32,4608]{1,0:T(8,128)(2,1)S(1)}, u32[]{:S(2)}, u32[]{:S(2)}) collective-permute-start(bf16[32,4608]{1,0:T(8,128)(2,1)S(1)} %get-tuple-element.50), channel_id=1, source_target_pairs={{0,1},{1,0},{2,3},{3,2},{4,5},{5,4},{6,7},{7,6},{8,9},{9,8},{10,11... | collective-permute-start | bytes 884744 | tf_op jit(solution)/shard_map/ppermute | solution.py:625
  45.6 2.0 %collective-permute-start.8 = (bf16[32,4608]{1,0:T(8,128)(2,1)S(1)}, bf16[32,4608]{1,0:T(8,128)(2,1)S(1)}, u32[]{:S(2)}, u32[]{:S(2)}) collective-permute-start(bf16[32,4608]{1,0:T(8,128)(2,1)S(1)} %get-tuple-element.51), channel_id=1, source_target_pairs={{0,1},{1,0},{2,3},{3,2},{4,5},{5,4},{6,7},{7,6},{8,9},{9,8},{10,11... | collective-permute-start | bytes 884744 | tf_op jit(solution)/shard_map/ppermute | solution.py:625
  46.1 1.9 %collective-permute-start.9 = (bf16[32,4608]{1,0:T(8,128)(2,1)S(1)}, bf16[32,4608]{1,0:T(8,128)(2,1)S(1)}, u32[]{:S(2)}, u32[]{:S(2)}) collective-permute-start(bf16[32,4608]{1,0:T(8,128)(2,1)S(1)} %get-tuple-element.52), channel_id=1, source_target_pairs={{0,1},{1,0},{2,3},{3,2},{4,5},{5,4},{6,7},{7,6},{8,9},{9,8},{10,11... | collective-permute-start | bytes 884744 | tf_op jit(solution)/shard_map/ppermute | solution.py:625
  46.2 2.3 %collective-permute-start.10 = (bf16[32,4608]{1,0:T(8,128)(2,1)S(1)}, bf16[32,4608]{1,0:T(8,128)(2,1)S(1)}, u32[]{:S(2)}, u32[]{:S(2)}) collective-permute-start(bf16[32,4608]{1,0:T(8,128)(2,1)S(1)} %get-tuple-element.53), channel_id=1, source_target_pairs={{0,1},{1,0},{2,3},{3,2},{4,5},{5,4},{6,7},{7,6},{8,9},{9,8},{10,11... | collective-permute-start | bytes 884744 | tf_op jit(solution)/shard_map/ppermute | solution.py:625
  47.2 4.4 %collective-permute-start.13 = (bf16[64,4608]{1,0:T(8,128)(2,1)S(1)}, bf16[64,4608]{1,0:T(8,128)(2,1)S(1)}, u32[]{:S(2)}, u32[]{:S(2)}) collective-permute-start(bf16[64,4608]{1,0:T(8,128)(2,1)S(1)} %collective-permute-done.1.refs_3_.refs_6_), channel_id=1, source_target_pairs={{0,1},{1,0},{2,3},{3,2},{4,5},{5,4},{6,7},{7,6},{8,9},{9,8},{10,11... | collective-permute-start | bytes 1769480 | tf_op jit(solution)/shard_map/ppermute | solution.py:625
  47.6 3.9 %collective-permute-start.14 = (bf16[64,4608]{1,0:T(8,128)(2,1)S(1)}, bf16[64,4608]{1,0:T(8,128)(2,1)S(1)}, u32[]{:S(2)}, u32[]{:S(2)}) collective-permute-start(bf16[64,4608]{1,0:T(8,128)(2,1)S(1)} %collective-permute-done.6.refs_4_.refs_7_), channel_id=1, source_target_pairs={{0,1},{1,0},{2,3},{3,2},{4,5},{5,4},{6,7},{7,6},{8,9},{9,8},{10,11... | collective-permute-start | bytes 1769480 | tf_op jit(solution)/shard_map/ppermute | solution.py:625
  50.5 2.1 %collective-permute-start.15 = (bf16[64,4608]{1,0:T(8,128)(2,1)S(1)}, bf16[64,4608]{1,0:T(8,128)(2,1)S(1)}, u32[]{:S(2)}, u32[]{:S(2)}) collective-permute-start(bf16[64,4608]{1,0:T(8,128)(2,1)S(1)} %collective-permute-done.3.refs_7_.refs_10_), channel_id=1, source_target_pairs={{0,1},{1,0},{2,3},{3,2},{4,5},{5,4},{6,7},{7,6},{8,9},{9,8},{10,11... | collective-permute-start | bytes 1769480 | tf_op jit(solution)/shard_map/ppermute | solution.py:625
  50.6 2.7 %collective-permute-start.16 = (bf16[64,4608]{1,0:T(8,128)(2,1)S(1)}, bf16[64,4608]{1,0:T(8,128)(2,1)S(1)}, u32[]{:S(2)}, u32[]{:S(2)}) collective-permute-start(bf16[64,4608]{1,0:T(8,128)(2,1)S(1)} %collective-permute-done.12.refs_8_.refs_11_), channel_id=1, source_target_pairs={{0,1},{1,0},{2,3},{3,2},{4,5},{5,4},{6,7},{7,6},{8,9},{9,8},{10,11... | collective-permute-start | bytes 1769480 | tf_op jit(solution)/shard_map/ppermute | solution.py:625
  51.0 5.5 %collective-permute-start.11 = (f32[2,128,128]{2,1,0:T(8,128)S(1)}, f32[2,128,128]{2,1,0:T(8,128)S(1)}, u32[]{:S(2)}, u32[]{:S(2)}) collective-permute-start(f32[2,128,128]{2,1,0:T(8,128)S(1)} %get-tuple-element.54.refs_2_), channel_id=1, source_target_pairs={{0,2},{2,0},{1,3},{3,1},{4,6},{6,4},{5,7},{7,5},{8,10},{10,8},{9,1... | collective-permute-start | bytes 393224 | tf_op jit(solution)/shard_map/ppermute | solution.py:617
  56.0 5.6 %collective-permute-start.17 = (f32[2,128,128]{2,1,0:T(8,128)S(1)}, f32[2,128,128]{2,1,0:T(8,128)S(1)}, u32[]{:S(2)}, u32[]{:S(2)}) collective-permute-start(f32[2,128,128]{2,1,0:T(8,128)S(1)} %shard_map.74.refs_1_), channel_id=1, source_target_pairs={{0,2},{2,0},{1,3},{3,1},{4,6},{6,4},{5,7},{7,5},{8,10},{10,8},{9,1... | collective-permute-start | bytes 393224 | tf_op jit(solution)/shard_map/ppermute | solution.py:617

commit v16 on v14

--- a/solution.py
+++ b/solution.py
@@ -465,11 +465,25 @@
 LATE = 2
 
 
+def pick_sums(sums, upper_ref, lower_ref, start):
+    upper_rows = upper_ref.shape[0]
+
+    @pl.when(start < upper_rows)
+    def _():
+        at = pl.multiple_of(jnp.minimum(start, upper_rows - SEGMENT_ROWS), SEGMENT_ROWS)
+        sums[...] = upper_ref[pl.ds(at, SEGMENT_ROWS), :]
+
+    @pl.when(start >= upper_rows)
+    def _():
+        at = pl.multiple_of(jnp.maximum(start - upper_rows, 0), SEGMENT_ROWS)
+        sums[...] = lower_ref[pl.ds(at, SEGMENT_ROWS), :]
+
+
 def early_kernel(n_adapter, n_tensor, rank, layout, n_buffers, table, *refs):
     first = n_adapter - LATE
     upper_ref, lower_ref, refs = refs[0], refs[1], refs[2:]
-    shrinks, refs = refs[: -4 - n_buffers], refs[-4 - n_buffers :]
-    buffers, (o_ref, rest_ref, up, sums) = refs[:-4], refs[-4:]
+    shrinks, refs = refs[: -3 - n_buffers], refs[-3 - n_buffers :]
+    buffers, (o_ref, up, sums) = refs[:-3], refs[-3:]
     views = views_of(buffers, range(first), layout, rank)
     for k in range(first):
         for j in range(MOST):
@@ -480,25 +494,11 @@
         for i in range(1, n_tensor):
             share = share + shrinks[call * n_tensor + i][...]
         shares += [share[i] for i in range(share.shape[0])]
-    for k in range(n_adapter):
+    for k in range(first):
         for j in range(MOST):
             start, used, _ = segment_of(table, k, j)
-            upper_rows = upper_ref.shape[0]
-
-            @pl.when(start < upper_rows)
-            def _(start=start):
-                at = pl.multiple_of(jnp.minimum(start, upper_rows - SEGMENT_ROWS), SEGMENT_ROWS)
-                sums[...] = upper_ref[pl.ds(at, SEGMENT_ROWS), :]
-
-            @pl.when(start >= upper_rows)
-            def _(start=start):
-                at = pl.multiple_of(jnp.maximum(start - upper_rows, 0), SEGMENT_ROWS)
-                sums[...] = lower_ref[pl.ds(at, SEGMENT_ROWS), :]
-
+            pick_sums(sums, upper_ref, lower_ref, start)
             value = sums[...]
-            if k >= first:
-                rest_ref[k - first, j] = value
-                continue
             lora = up_product(shares[k], j, up[k * MOST + j], rank)
 
             @pl.when(used)
@@ -513,23 +513,20 @@
     return pl.pallas_call(
         functools.partial(early_kernel, n_adapter, n_tensor, rank, layout, len(buffers)),
         in_specs=[SMEM] + [VMEM] * (2 + len(shrinks) + len(buffers)),
-        out_specs=[VMEM, VMEM],
-        out_shape=[
-            jax.ShapeDtypeStruct((rows, columns), jnp.bfloat16),
-            jax.ShapeDtypeStruct((LATE, MOST, SEGMENT_ROWS, columns), jnp.float32),
-        ],
+        out_specs=VMEM,
+        out_shape=jax.ShapeDtypeStruct((rows, columns), jnp.bfloat16),
         scratch_shapes=[
             pltpu.VMEM(((n_adapter - LATE) * MOST, 2 * rank, columns), jnp.bfloat16),
             pltpu.VMEM((SEGMENT_ROWS, columns), jnp.float32),
         ],
         compiler_params=params(16),
-        cost_estimate=cost(6 * rows * rank * columns, (4 * n_tensor + 2) * rows * columns),
+        cost_estimate=cost(600 * rows * rank * columns, (4 * n_tensor + 2) * rows * columns),
     )(table, upper, lower, *shrinks, *buffers)
 
 
 def late_kernel(ks, n_tensor, rank, layout, table, *refs):
-    rest_ref, shrinks, refs = refs[0], refs[1 : 1 + n_tensor], refs[1 + n_tensor :]
-    buffers, (_, o_ref, up, out, sems) = refs[:-5], refs[-5:]
+    upper_ref, lower_ref, shrinks, refs = refs[0], refs[1], refs[2 : 2 + n_tensor], refs[2 + n_tensor :]
+    buffers, (_, o_ref, up, sums, out, sems) = refs[:-6], refs[-6:]
     views = views_of(buffers, stages_of_all(ks), layout, rank)
     stores = []
     for i, k in enumerate(ks):
@@ -540,7 +537,8 @@
             fetch_up(up, i * MOST + j, table, k, j, views, rank)
             start, used, _ = segment_of(table, k, j)
             lora = up_product(share, j, up[i * MOST + j], rank)
-            out[i, j] = (rest_ref[i, j] + adapter_scale * lora).astype(jnp.bfloat16)
+            pick_sums(sums, upper_ref, lower_ref, start)
+            out[i, j] = (sums[...] + adapter_scale * lora).astype(jnp.bfloat16)
             store = pltpu.make_async_copy(
                 out.at[i, j], o_ref.at[pl.ds(start, SEGMENT_ROWS), :], sems.at[i, j]
             )
@@ -550,25 +548,26 @@
         pl.when(used)(store.wait)
 
 
-def late(ks, n_tensor, table, rest, shrinks, buffers, value, layout, rank):
+def late(ks, n_tensor, table, upper, lower, shrinks, buffers, value, layout, rank):
     rows, columns = value.shape
     return pl.pallas_call(
         functools.partial(late_kernel, ks, n_tensor, rank, layout),
-        in_specs=[SMEM] + [VMEM] * (1 + len(shrinks) + len(buffers)) + [ANY],
+        in_specs=[SMEM] + [VMEM] * (2 + len(shrinks) + len(buffers)) + [ANY],
         out_specs=ANY,
         out_shape=jax.ShapeDtypeStruct((rows, columns), jnp.bfloat16),
         scratch_shapes=[
             pltpu.VMEM((LATE * MOST, 2 * rank, columns), jnp.bfloat16),
+            pltpu.VMEM((SEGMENT_ROWS, columns), jnp.float32),
             pltpu.VMEM((LATE, MOST, SEGMENT_ROWS, columns), jnp.bfloat16),
             pltpu.SemaphoreType.DMA((LATE, MOST)),
         ],
-        input_output_aliases={2 + len(shrinks) + len(buffers): 0},
+        input_output_aliases={3 + len(shrinks) + len(buffers): 0},
         compiler_params=params(8),
         cost_estimate=cost(
             6 * LATE * MOST * SEGMENT_ROWS * rank * columns,
             8 * LATE * MOST * SEGMENT_ROWS * columns,
         ),
-    )(table, rest, *shrinks, *buffers, value)
+    )(table, upper, lower, *shrinks, *buffers, value)
 
 
 def after(array, *others):
@@ -652,15 +651,16 @@
             buffers[1] += [swap_cores(joined)]
             free = lower
             upper = add_call(1, 0, after(upper, held[0]), sent[1])
-            lower = add_call(1, UPPER, after(lower, upper, *held[1:]), sent[1])
-            before = shrink([1], after(kept, lower), [before])
+            add_shrink(before)
+            lower = add_call(1, UPPER, after(lower, upper, *held[1:], *shrinks), sent[1])
+            before = shrink([1], after(kept, lower))
         else:
             before = shrink([stage - 1], kept, [before])
         ahead = [free] if stage == 2 else []
         swapped = [swap_cores(after(c, *ahead)) for c in came] if stage > 1 else []
         buffers.append([*came, *swapped])
     add_shrink(before)
-    value, remaining = early(
+    value = early(
         n_adapter,
         n_tensor,
         table,
@@ -673,12 +673,13 @@
     )
     buffers.append([*held, *[swap_cores(h) for h in held]])
     ks = (last - 1, last)
-    add_shrink(shrink(ks, after(kept, *held)))
+    add_shrink(shrink(ks, after(kept, *held, before)))
     return late(
         ks,
         n_tensor,
         table,
-        remaining,
+        upper,
+        lower,
         shrinks[-n_tensor:],
         buffers_of(stages_of_all(ks)),
         value,

time: 63.2 us -> 63.9 us (1.011)
    ppermute x4 -> x5, waiting for transfers between devices: 0.91 us -> 4.1 us  [swap_tensor(): return lax.ppermute(array, 'tensor', pairs)]
    ppermute x5, waiting for transfers between devices: 2.87 us -> 0.01 us  [swap_cores(): return lax.ppermute(array, 'dp', [(0, 1), (1, 0)])]
    ppermute x4 -> x5, starting transfers between devices: 5.34 us -> 5.93 us  [swap_tensor(): return lax.ppermute(array, 'tensor', pairs)]
  transfers between devices with their start and end apart: 15 -> 16, of which waited for: 4 -> 3; matrix products, arithmetic and copies ran while one was open for 0% -> 0% of each run, Pallas kernels for 52% -> 50%
where the time goes in v16:
time: 63.9 us; the launch traced here: 63.6 us
  Pallas kernels  35.7 us (56%)
  starting transfers between devices  22 us (34%)
  waiting for transfers between devices  5.52 us (9%)
    ppermute x6, starting transfers between devices, along_line(): return lax.ppermute(array, ('adapter', 'dp'), up + down)  15 us
    pallas_call x2, Pallas kernels, sent_call(): pl.pallas_call(functools.partial(sent_kernel, first, sizes, step, n_tenso...  10.2 us
    pallas_call x1, Pallas kernels, lower_call(): pl.pallas_call(functools.partial(lower_kernel, per_device, rank), in_spec...  7.09 us
    ppermute x5, starting transfers between devices, swap_tensor(): return lax.ppermute(array, 'tensor', pairs)  5.93 us
    pallas_call x1, Pallas kernels, upper_call(): pl.pallas_call(functools.partial(upper_kernel, n_adapter), in_specs=[SMEM...  5.88 us
    pallas_call x2, Pallas kernels, shrink_call(): pl.pallas_call(functools.partial(shrink_kernel, ks, rank, at, layout), in...  4.27 us
    ppermute x5, waiting for transfers between devices, swap_tensor(): return lax.ppermute(array, 'tensor', pairs)  4.1 us
    pallas_call x1, Pallas kernels, early(): pl.pallas_call(functools.partial(early_kernel, n_adapter, n_tensor, rank,...  2.66 us
  transfers between devices with their start and end apart: 16, of which 3 were waited for; matrix products, arithmetic and copies ran while one was open for 0% of the time, Pallas kernels for 50%

profile of v16, /device:TPU:16, one launch (start us, length us, event | category | flops | bytes accessed | tf_op | source)
XLA Modules:
  0.0 63.6 jit_solution(5960504904777775447)
XLA Ops:
  0.0 1.3 %shard_map.65 = (bf16[64,4608]{1,0:T(8,128)(2,1)S(1)}, bf16[64,4608]{1,0:T(8,128)(2,1)S(1)}) custom-call(bf16[128,4096]{1,0:T(8,128)(2,1)} %bitcast.4, bf16[128,1024]{1,0:T(8,128)(2,1)} %bitcast.5), custom_call_target="tpu_custom_call" | custom-call | bytes 2359296 | tf_op jit(solution)/shard_map/pallas_call | solution.py:91
  1.3 3.5 %collective-permute-start = (bf16[64,4608]{1,0:T(8,128)(2,1)S(1)}, bf16[64,4608]{1,0:T(8,128)(2,1)S(1)}, u32[]{:S(2)}, u32[]{:S(2)}) collective-permute-start(bf16[64,4608]{1,0:T(8,128)(2,1)S(1)} %get-tuple-element.25.refs_0_.refs_6_), channel_id=1, source_target_pairs={{0,4},{4,8},{8,12},{5,1},{9,5},{13,9},{2,6},{6,10},{10,14},{7,3},{... | collective-permute-start | bytes 1769480 | tf_op jit(solution)/shard_map/ppermute | solution.py:593
  4.8 1.9 %collective-permute-start.2 = (bf16[64,4608]{1,0:T(8,128)(2,1)S(1)}, bf16[64,4608]{1,0:T(8,128)(2,1)S(1)}, u32[]{:S(2)}, u32[]{:S(2)}) collective-permute-start(bf16[64,4608]{1,0:T(8,128)(2,1)S(1)} %get-tuple-element.27.refs_1_.refs_7_), channel_id=1, source_target_pairs={{0,4},{4,8},{8,12},{5,1},{9,5},{13,9},{2,6},{6,10},{10,14},{7,3},{... | collective-permute-start | bytes 1769480 | tf_op jit(solution)/shard_map/ppermute | solution.py:593
  6.7 3.6 %shard_map.66 = s32[168,512]{1,0:T(8,128)S(1)} custom-call(bf16[1024,4096]{1,0:T(8,128)(2,1)} %x_ref.6, bf16[4096,1024]{1,0:T(8,128)(2,1)} %w_ref.7), custom_call_target="tpu_custom_call" | custom-call | flops 1073741824 | bytes 6815744 | tf_op jit(solution)/shard_map/pallas_call | solution.py:265
  10.3 1.6 %collective-permute-start.4 = (s32[168,512]{1,0:T(8,128)S(1)}, s32[168,512]{1,0:T(8,128)S(1)}, u32[]{:S(2)}, u32[]{:S(2)}) collective-permute-start(s32[168,512]{1,0:T(8,128)S(1)} %shard_map.66), channel_id=1, source_target_pairs={{0,2},{2,0},{1,3},{3,1},{4,6},{6,4},{5,7},{7,5},{8,10},{10,8},{9,1... | collective-permute-start | bytes 1032200 | tf_op jit(solution)/shard_map/ppermute | solution.py:588
  11.9 1.4 %shard_map.64.table = s32[32]{0:T(128)} custom-call(s32[1024]{0:T(1024)} %ids.1, s32[8]{0:T(128)} %slots.1), custom_call_target="tpu_custom_call" | custom-call | bytes 4096 | tf_op jit(solution)/shard_map/pallas_call | solution.py:123
  13.3 0.0 copy-start
  13.3 0.0 collective-permute-done.refs_2_.refs_0_.refs_8_.refs_4_
  13.3 3.2 %collective-permute-start.1 = (bf16[64,4608]{1,0:T(8,128)(2,1)S(1)}, bf16[64,4608]{1,0:T(8,128)(2,1)S(1)}, u32[]{:S(2)}, u32[]{:S(2)}) collective-permute-start(bf16[64,4608]{1,0:T(8,128)(2,1)S(1)} %collective-permute-done.refs_2_.refs_0_.refs_8_.refs_4_), channel_id=1, source_target_pairs={{4,8},{8,12},{5,1},{9,5},{6,10},{10,14},{7,3},{11,7},{20,24},{24,2... | collective-permute-start | bytes 1769480 | tf_op jit(solution)/shard_map/ppermute | solution.py:593
  16.5 6.6 %shard_map.67 = s32[488,512]{1,0:T(8,128)S(1)} custom-call(bf16[1024,4096]{1,0:T(8,128)(2,1)} %x_ref.6, bf16[4096,1024]{1,0:T(8,128)(2,1)} %w_ref.7), custom_call_target="tpu_custom_call" | custom-call | flops 3221225472 | bytes 12058624 | tf_op jit(solution)/shard_map/pallas_call | solution.py:265
  23.1 0.0 collective-permute-done.2.refs_3_.refs_1_.refs_9_.refs_5_
  23.1 0.0 collective-permute-done.4.refs_4_
  23.1 1.6 %collective-permute-start.5 = (s32[488,512]{1,0:T(8,128)S(1)}, s32[488,512]{1,0:T(8,128)S(1)}, u32[]{:S(2)}, u32[]{:S(2)}) collective-permute-start(s32[488,512]{1,0:T(8,128)S(1)} %shard_map.67), channel_id=1, source_target_pairs={{0,2},{2,0},{1,3},{3,1},{4,6},{6,4},{5,7},{7,5},{8,10},{10,8},{9,1... | collective-permute-start | bytes 2998280 | tf_op jit(solution)/shard_map/ppermute | solution.py:588
  24.7 1.9 %collective-permute-start.6 = (bf16[64,4608]{1,0:T(8,128)(2,1)S(1)}, bf16[64,4608]{1,0:T(8,128)(2,1)S(1)}, u32[]{:S(2)}, u32[]{:S(2)}) collective-permute-start(bf16[64,4608]{1,0:T(8,128)(2,1)S(1)} %collective-permute-done.2.refs_3_.refs_1_.refs_9_.refs_5_), channel_id=1, source_target_pairs={{4,8},{8,12},{5,1},{9,5},{6,10},{10,14},{7,3},{11,7},{20,24},{24,2... | collective-permute-start | bytes 1769480 | tf_op jit(solution)/shard_map/ppermute | solution.py:593
  26.6 0.0 collective-permute-done.1.refs_3_.refs_7_
  26.6 2.5 %collective-permute-start.3 = (bf16[64,4608]{1,0:T(8,128)(2,1)S(1)}, bf16[64,4608]{1,0:T(8,128)(2,1)S(1)}, u32[]{:S(2)}, u32[]{:S(2)}) collective-permute-start(bf16[64,4608]{1,0:T(8,128)(2,1)S(1)} %collective-permute-done.1.refs_3_.refs_7_), channel_id=1, source_target_pairs={{8,12},{5,1},{10,14},{7,3},{24,28},{21,17},{26,30},{23,19}} | collective-permute-start | bytes 1769480 | tf_op jit(solution)/shard_map/ppermute | solution.py:593
  29.2 0.0 copy-done
  29.2 5.9 %shard_map.68 = (f32[384,512]{1,0:T(8,128)S(1)}, bf16[3,2,128,4096]{3,2,1,0:T(8,128)(2,1)S(1)}) custom-call(s32[32]{0:T(128)S(1)} %copy-done, bf16[1024,4096]{1,0:T(8,128)(2,1)} %x_ref.6, bf16[4096,1024]{1,0:T(8,128)(2,1)} %w_ref.7), custom_call_target="tpu_custom_call" | custom-call | flops 1610612736 | bytes 12582912 | tf_op jit(solution)/shard_map/pallas_call | solution.py:354
  35.1 1.4 %collective-permute-done.6.refs_4_.refs_8_ = bf16[64,4608]{1,0:T(8,128)(2,1)S(1)} collective-permute-done((bf16[64,4608]{1,0:T(8,128)(2,1)S(1)}, bf16[64,4608]{1,0:T(8,128)(2,1)S(1)}, u32[]{:S(2)}, u32[]{:S(2)}) %collective-permute-start.6) | collective-permute-done | bytes 589856 | tf_op jit(solution)/shard_map/ppermute | solution.py:593
  36.5 1.9 %collective-permute-start.7 = (bf16[64,4608]{1,0:T(8,128)(2,1)S(1)}, bf16[64,4608]{1,0:T(8,128)(2,1)S(1)}, u32[]{:S(2)}, u32[]{:S(2)}) collective-permute-start(bf16[64,4608]{1,0:T(8,128)(2,1)S(1)} %collective-permute-done.6.refs_4_.refs_8_), channel_id=1, source_target_pairs={{8,12},{5,1},{10,14},{7,3},{24,28},{21,17},{26,30},{23,19}} | collective-permute-start | bytes 1769480 | tf_op jit(solution)/shard_map/ppermute | solution.py:593
  38.4 7.1 %shard_map.70 = (f32[640,512]{1,0:T(8,128)S(1)}, f32[1,128,128]{2,1,0:T(8,128)S(1)}, bf16[128,4608]{1,0:T(8,128)(2,1)S(1)}) custom-call(s32[32]{0:T(128)S(1)} %copy-done, bf16[1024,4096]{1,0:T(8,128)(2,1)} %x_ref.6, bf16[4096,1024]{1,0:T(8,128)(2,1)} %w_ref.7, bf16[64,4608]{1,0:T(8,128)(2,1)S(1)} %get-tuple-element.25.refs_0_.refs_6_, ...), custom_call_target="tpu_custom_call" | custom-call | bytes 2097152 | tf_op jit(solution)/shard_map/pallas_call | solution.py:398
  45.5 0.6 collective-permute-start.8
  46.1 0.0 collective-permute-start.9
  46.1 0.0 collective-permute-done.3.refs_7_.refs_11_
  46.1 0.5 collective-permute-start.11
  46.6 0.0 collective-permute-done.5.refs_0_
  46.6 0.1 collective-permute-start.10
  46.7 0.2 shard_map.69.refs_0_
  46.9 2.9 %collective-permute-done.8.refs_3_ = f32[1,128,128]{2,1,0:T(8,128)S(1)} collective-permute-done((f32[1,128,128]{2,1,0:T(8,128)S(1)}, f32[1,128,128]{2,1,0:T(8,128)S(1)}, u32[]{:S(2)}, u32[]{:S(2)}) %collective-permute-start.8) | collective-permute-done | bytes 65568 | tf_op jit(solution)/shard_map/ppermute | solution.py:588
  49.9 0.0 collective-permute-done.7.refs_8_.refs_12_
  49.9 0.0 collective-permute-start.13
  49.9 0.5 collective-permute-start.12
  50.4 0.2 shard_map.71.refs_1_
  50.6 0.0 collective-permute-done.9.refs_2_.refs_10_.refs_6_
  50.6 1.7 %shard_map.72.refs_4_ = f32[1,128,128]{2,1,0:T(8,128)S(1)} custom-call(s32[32]{0:T(128)S(1)} %copy-done, bf16[3,2,128,4096]{3,2,1,0:T(8,128)(2,1)S(1)} %get-tuple-element.42.kept_ref, bf16[64,4608]{1,0:T(8,128)(2,1)S(1)} %collective-permute-done.refs_2_.refs_0_.refs_8_.refs_4_, bf16[64,4608]{1,0:T(8,128)(2,1)S(1)} %collective-permute-done.2.refs_3_.refs_1_.refs_9_.refs_5_, ...), custom_call_target="tpu_custom_call" | custom-call | flops 536870912 | bytes 2097152 | tf_op jit(solution)/shard_map/pallas_call | solution.py:430
  52.3 0.6 collective-permute-start.15
  52.9 0.0 collective-permute-done.11.refs_6_.refs_10_
  52.9 0.0 collective-permute-done.10.refs_5_.refs_9_
  52.9 0.0 collective-permute-done.13.refs_10_.refs_14_
  52.9 0.0 collective-permute-done.12.refs_9_.refs_13_
  52.9 2.6 %shard_map.73.refs_2_ = f32[2,128,128]{2,1,0:T(8,128)S(1)} custom-call(s32[32]{0:T(128)S(1)} %copy-done, bf16[3,2,128,4096]{3,2,1,0:T(8,128)(2,1)S(1)} %get-tuple-element.42.kept_ref, bf16[64,4608]{1,0:T(8,128)(2,1)S(1)} %collective-permute-done.refs_2_.refs_0_.refs_8_.refs_4_, bf16[64,4608]{1,0:T(8,128)(2,1)S(1)} %collective-permute-done.2.refs_3_.refs_1_.refs_9_.refs_5_, ...), custom_call_target="tpu_custom_call" | custom-call | flops 1073741824 | bytes 4194304 | tf_op jit(solution)/shard_map/pallas_call | solution.py:430
  55.5 1.6 %collective-permute-start.14 = (f32[2,128,128]{2,1,0:T(8,128)S(1)}, f32[2,128,128]{2,1,0:T(8,128)S(1)}, u32[]{:S(2)}, u32[]{:S(2)}) collective-permute-start(f32[2,128,128]{2,1,0:T(8,128)S(1)} %shard_map.73.refs_2_), channel_id=1, source_target_pairs={{0,2},{2,0},{1,3},{3,1},{4,6},{6,4},{5,7},{7,5},{8,10},{10,8},{9,1... | collective-permute-start | bytes 393224 | tf_op jit(solution)/shard_map/ppermute | solution.py:588
  57.1 0.0 collective-permute-done.15.refs_5_
  57.1 2.7 %shard_map.74.refs_15_ = bf16[1024,512]{1,0:T(8,128)(2,1)} custom-call(s32[32]{0:T(128)S(1)} %copy-done, f32[384,512]{1,0:T(8,128)S(1)} %shard_map.69.refs_0_, f32[640,512]{1,0:T(8,128)S(1)} %shard_map.71.refs_1_, f32[1,128,128]{2,1,0:T(8,128)S(1)} %get-tuple-element.37.refs_2_, f32[1,128,128]{2,1,0:T(8,128)S(1)} %collective-permute-done.8.refs_3_, ...), custom_call_target="tpu_custom_call" | custom-call | flops 20132659200 | bytes 5242880 | tf_op jit(solution)/shard_map/pallas_call | solution.py:513
  59.8 1.2 %collective-permute-done.14.refs_3_ = f32[2,128,128]{2,1,0:T(8,128)S(1)} collective-permute-done((f32[2,128,128]{2,1,0:T(8,128)S(1)}, f32[2,128,128]{2,1,0:T(8,128)S(1)}, u32[]{:S(2)}, u32[]{:S(2)}) %collective-permute-start.14) | collective-permute-done | bytes 131104 | tf_op jit(solution)/shard_map/ppermute | solution.py:588
  60.9 2.5 %shard_map.75 = bf16[1024,512]{1,0:T(8,128)(2,1)} custom-call(s32[32]{0:T(128)S(1)} %copy-done, f32[384,512]{1,0:T(8,128)S(1)} %shard_map.69.refs_0_, f32[640,512]{1,0:T(8,128)S(1)} %shard_map.71.refs_1_, f32[2,128,128]{2,1,0:T(8,128)S(1)} %shard_map.73.refs_2_, f32[2,128,128]{2,1,0:T(8,128)S(1)} %collective-permute-done.14.refs_3_, ...), custom_call_target="tpu_custom_call", output_to_operand_aliasing={{}: (16, {})} | custom-call | flops 100663296 | bytes 2097152 | tf_op jit(solution)/shard_map/pallas_call | solution.py:553
Async XLA Ops:
  1.3 12.1 %collective-permute-start = (bf16[64,4608]{1,0:T(8,128)(2,1)S(1)}, bf16[64,4608]{1,0:T(8,128)(2,1)S(1)}, u32[]{:S(2)}, u32[]{:S(2)}) collective-permute-start(bf16[64,4608]{1,0:T(8,128)(2,1)S(1)} %get-tuple-element.25.refs_0_.refs_6_), channel_id=1, source_target_pairs={{0,4},{4,8},{8,12},{5,1},{9,5},{13,9},{2,6},{6,10},{10,14},{7,3},{... | collective-permute-start | bytes 1769480 | tf_op jit(solution)/shard_map/ppermute | solution.py:593
  4.8 18.4 %collective-permute-start.2 = (bf16[64,4608]{1,0:T(8,128)(2,1)S(1)}, bf16[64,4608]{1,0:T(8,128)(2,1)S(1)}, u32[]{:S(2)}, u32[]{:S(2)}) collective-permute-start(bf16[64,4608]{1,0:T(8,128)(2,1)S(1)} %get-tuple-element.27.refs_1_.refs_7_), channel_id=1, source_target_pairs={{0,4},{4,8},{8,12},{5,1},{9,5},{13,9},{2,6},{6,10},{10,14},{7,3},{... | collective-permute-start | bytes 1769480 | tf_op jit(solution)/shard_map/ppermute | solution.py:593
  10.3 12.9 %collective-permute-start.4 = (s32[168,512]{1,0:T(8,128)S(1)}, s32[168,512]{1,0:T(8,128)S(1)}, u32[]{:S(2)}, u32[]{:S(2)}) collective-permute-start(s32[168,512]{1,0:T(8,128)S(1)} %shard_map.66), channel_id=1, source_target_pairs={{0,2},{2,0},{1,3},{3,1},{4,6},{6,4},{5,7},{7,5},{8,10},{10,8},{9,1... | collective-permute-start | bytes 1032200 | tf_op jit(solution)/shard_map/ppermute | solution.py:588
  13.3 15.9 %copy-start = (s32[32]{0:T(128)S(1)}, s32[32]{0:T(128)}, u32[]{:S(2)}) copy-start(s32[32]{0:T(128)} %shard_map.64.table) | copy-start | bytes 388
  13.3 13.3 %collective-permute-start.1 = (bf16[64,4608]{1,0:T(8,128)(2,1)S(1)}, bf16[64,4608]{1,0:T(8,128)(2,1)S(1)}, u32[]{:S(2)}, u32[]{:S(2)}) collective-permute-start(bf16[64,4608]{1,0:T(8,128)(2,1)S(1)} %collective-permute-done.refs_2_.refs_0_.refs_8_.refs_4_), channel_id=1, source_target_pairs={{4,8},{8,12},{5,1},{9,5},{6,10},{10,14},{7,3},{11,7},{20,24},{24,2... | collective-permute-start | bytes 1769480 | tf_op jit(solution)/shard_map/ppermute | solution.py:593
  23.1 23.5 %collective-permute-start.5 = (s32[488,512]{1,0:T(8,128)S(1)}, s32[488,512]{1,0:T(8,128)S(1)}, u32[]{:S(2)}, u32[]{:S(2)}) collective-permute-start(s32[488,512]{1,0:T(8,128)S(1)} %shard_map.67), channel_id=1, source_target_pairs={{0,2},{2,0},{1,3},{3,1},{4,6},{6,4},{5,7},{7,5},{8,10},{10,8},{9,1... | collective-permute-start | bytes 2998280 | tf_op jit(solution)/shard_map/ppermute | solution.py:588
  24.7 11.8 %collective-permute-start.6 = (bf16[64,4608]{1,0:T(8,128)(2,1)S(1)}, bf16[64,4608]{1,0:T(8,128)(2,1)S(1)}, u32[]{:S(2)}, u32[]{:S(2)}) collective-permute-start(bf16[64,4608]{1,0:T(8,128)(2,1)S(1)} %collective-permute-done.2.refs_3_.refs_1_.refs_9_.refs_5_), channel_id=1, source_target_pairs={{4,8},{8,12},{5,1},{9,5},{6,10},{10,14},{7,3},{11,7},{20,24},{24,2... | collective-permute-start | bytes 1769480 | tf_op jit(solution)/shard_map/ppermute | solution.py:593
  26.6 19.5 %collective-permute-start.3 = (bf16[64,4608]{1,0:T(8,128)(2,1)S(1)}, bf16[64,4608]{1,0:T(8,128)(2,1)S(1)}, u32[]{:S(2)}, u32[]{:S(2)}) collective-permute-start(bf16[64,4608]{1,0:T(8,128)(2,1)S(1)} %collective-permute-done.1.refs_3_.refs_7_), channel_id=1, source_target_pairs={{8,12},{5,1},{10,14},{7,3},{24,28},{21,17},{26,30},{23,19}} | collective-permute-start | bytes 1769480 | tf_op jit(solution)/shard_map/ppermute | solution.py:593
  36.5 13.4 %collective-permute-start.7 = (bf16[64,4608]{1,0:T(8,128)(2,1)S(1)}, bf16[64,4608]{1,0:T(8,128)(2,1)S(1)}, u32[]{:S(2)}, u32[]{:S(2)}) collective-permute-start(bf16[64,4608]{1,0:T(8,128)(2,1)S(1)} %collective-permute-done.6.refs_4_.refs_8_), channel_id=1, source_target_pairs={{8,12},{5,1},{10,14},{7,3},{24,28},{21,17},{26,30},{23,19}} | collective-permute-start | bytes 1769480 | tf_op jit(solution)/shard_map/ppermute | solution.py:593
  45.5 4.3 %collective-permute-start.8 = (f32[1,128,128]{2,1,0:T(8,128)S(1)}, f32[1,128,128]{2,1,0:T(8,128)S(1)}, u32[]{:S(2)}, u32[]{:S(2)}) collective-permute-start(f32[1,128,128]{2,1,0:T(8,128)S(1)} %get-tuple-element.37.refs_2_), channel_id=1, source_target_pairs={{0,2},{2,0},{1,3},{3,1},{4,6},{6,4},{5,7},{7,5},{8,10},{10,8},{9,1... | collective-permute-start | bytes 196616 | tf_op jit(solution)/shard_map/ppermute | solution.py:588
  46.1 4.5 %collective-permute-start.9 = (bf16[128,4608]{1,0:T(8,128)(2,1)S(1)}, bf16[128,4608]{1,0:T(8,128)(2,1)S(1)}, u32[]{:S(2)}, u32[]{:S(2)}) collective-permute-start(bf16[128,4608]{1,0:T(8,128)(2,1)S(1)} %get-tuple-element.41), channel_id=1, source_target_pairs={{0,1},{1,0},{2,3},{3,2},{4,5},{5,4},{6,7},{7,6},{8,9},{9,8},{10,11... | collective-permute-start | bytes 3538952 | tf_op jit(solution)/shard_map/ppermute | solution.py:596
  46.1 6.8 %collective-permute-start.11 = (bf16[64,4608]{1,0:T(8,128)(2,1)S(1)}, bf16[64,4608]{1,0:T(8,128)(2,1)S(1)}, u32[]{:S(2)}, u32[]{:S(2)}) collective-permute-start(bf16[64,4608]{1,0:T(8,128)(2,1)S(1)} %collective-permute-done.6.refs_4_.refs_8_), channel_id=1, source_target_pairs={{0,1},{1,0},{2,3},{3,2},{4,5},{5,4},{6,7},{7,6},{8,9},{9,8},{10,11... | collective-permute-start | bytes 1769480 | tf_op jit(solution)/shard_map/ppermute | solution.py:596
  46.6 6.3 %collective-permute-start.10 = (bf16[64,4608]{1,0:T(8,128)(2,1)S(1)}, bf16[64,4608]{1,0:T(8,128)(2,1)S(1)}, u32[]{:S(2)}, u32[]{:S(2)}) collective-permute-start(bf16[64,4608]{1,0:T(8,128)(2,1)S(1)} %collective-permute-done.1.refs_3_.refs_7_), channel_id=1, source_target_pairs={{0,1},{1,0},{2,3},{3,2},{4,5},{5,4},{6,7},{7,6},{8,9},{9,8},{10,11... | collective-permute-start | bytes 1769480 | tf_op jit(solution)/shard_map/ppermute | solution.py:596
  49.9 3.1 %collective-permute-start.13 = (bf16[64,4608]{1,0:T(8,128)(2,1)S(1)}, bf16[64,4608]{1,0:T(8,128)(2,1)S(1)}, u32[]{:S(2)}, u32[]{:S(2)}) collective-permute-start(bf16[64,4608]{1,0:T(8,128)(2,1)S(1)} %collective-permute-done.7.refs_8_.refs_12_), channel_id=1, source_target_pairs={{0,1},{1,0},{2,3},{3,2},{4,5},{5,4},{6,7},{7,6},{8,9},{9,8},{10,11... | collective-permute-start | bytes 1769480 | tf_op jit(solution)/shard_map/ppermute | solution.py:596
  49.9 3.1 %collective-permute-start.12 = (bf16[64,4608]{1,0:T(8,128)(2,1)S(1)}, bf16[64,4608]{1,0:T(8,128)(2,1)S(1)}, u32[]{:S(2)}, u32[]{:S(2)}) collective-permute-start(bf16[64,4608]{1,0:T(8,128)(2,1)S(1)} %collective-permute-done.3.refs_7_.refs_11_), channel_id=1, source_target_pairs={{0,1},{1,0},{2,3},{3,2},{4,5},{5,4},{6,7},{7,6},{8,9},{9,8},{10,11... | collective-permute-start | bytes 1769480 | tf_op jit(solution)/shard_map/ppermute | solution.py:596
  52.3 4.8 %collective-permute-start.15 = (f32[1,128,128]{2,1,0:T(8,128)S(1)}, f32[1,128,128]{2,1,0:T(8,128)S(1)}, u32[]{:S(2)}, u32[]{:S(2)}) collective-permute-start(f32[1,128,128]{2,1,0:T(8,128)S(1)} %shard_map.72.refs_4_), channel_id=1, source_target_pairs={{0,2},{2,0},{1,3},{3,1},{4,6},{6,4},{5,7},{7,5},{8,10},{10,8},{9,1... | collective-permute-start | bytes 196616 | tf_op jit(solution)/shard_map/ppermute | solution.py:588
  55.5 5.4 %collective-permute-start.14 = (f32[2,128,128]{2,1,0:T(8,128)S(1)}, f32[2,128,128]{2,1,0:T(8,128)S(1)}, u32[]{:S(2)}, u32[]{:S(2)}) collective-permute-start(f32[2,128,128]{2,1,0:T(8,128)S(1)} %shard_map.73.refs_2_), channel_id=1, source_target_pairs={{0,2},{2,0},{1,3},{3,1},{4,6},{6,4},{5,7},{7,5},{8,10},{10,8},{9,1... | collective-permute-start | bytes 393224 | tf_op jit(solution)/shard_map/ppermute | solution.py:588

commit v17 on v14

--- a/solution.py
+++ b/solution.py
@@ -146,7 +146,7 @@
     largest = jnp.maximum(jnp.max(jnp.abs(values), axis=1, keepdims=True), 2.0**-100)
     power = jnp.floor(jnp.log2(largest))
     whole = (values * jnp.exp2(18.0 - power) + MIDDLE).astype(jnp.int32) - int(MIDDLE)
-    whole = jnp.minimum(whole, 2**19 - 1)
+    whole = jnp.clip(whole, -(2**19), 2**19 - 1)
     v = [whole[i * GROUP : (i + 1) * GROUP] for i in range(8)]
     over = [
         v[5] & 0xFFF,

time: 63.2 us -> 63.2 us (level)
  transfers between devices with their start and end apart: 15 -> 15, of which waited for: 4 -> 5; matrix products, arithmetic and copies ran while one was open for 0% -> 0% of each run, Pallas kernels for 52% -> 52%
where the time goes in v17:
time: 63.2 us; the launch traced here: 62.9 us
  Pallas kernels  36 us (57%)
  starting transfers between devices  21.4 us (34%)
  waiting for transfers between devices  5.16 us (8%)
    ppermute x6, starting transfers between devices, along_line(): return lax.ppermute(array, ('adapter', 'dp'), up + down)  14.8 us
    pallas_call x2, Pallas kernels, sent_call(): pl.pallas_call(functools.partial(sent_kernel, first, sizes, step, n_tenso...  10.3 us
    pallas_call x1, Pallas kernels, lower_call(): pl.pallas_call(functools.partial(lower_kernel, per_device, rank), in_spec...  7.09 us
    pallas_call x1, Pallas kernels, upper_call(): pl.pallas_call(functools.partial(upper_kernel, n_adapter), in_specs=[SMEM...  6.09 us
    ppermute x4, starting transfers between devices, swap_tensor(): return lax.ppermute(array, 'tensor', pairs)  5.37 us
    pallas_call x2, Pallas kernels, shrink_call(): pl.pallas_call(functools.partial(shrink_kernel, ks, rank, at, layout), in...  4.27 us
    pallas_call x1, Pallas kernels, early(): pl.pallas_call(functools.partial(early_kernel, n_adapter, n_tensor, rank,...  2.82 us
    ppermute x5, waiting for transfers between devices, swap_cores(): return lax.ppermute(array, 'dp', [(0, 1), (1, 0)])  2.72 us
  transfers between devices with their start and end apart: 15, of which 5 were waited for; matrix products, arithmetic and copies ran while one was open for 0% of the time, Pallas kernels for 52%

profile of v17, /device:TPU:16, one launch (start us, length us, event | category | flops | bytes accessed | tf_op | source)
XLA Modules:
  0.0 62.9 jit_solution(4084245101720639210)
XLA Ops:
  0.0 1.3 %shard_map.65 = (bf16[64,4608]{1,0:T(8,128)(2,1)S(1)}, bf16[64,4608]{1,0:T(8,128)(2,1)S(1)}) custom-call(bf16[128,4096]{1,0:T(8,128)(2,1)} %bitcast.4, bf16[128,1024]{1,0:T(8,128)(2,1)} %bitcast.5), custom_call_target="tpu_custom_call" | custom-call | bytes 2359296 | tf_op jit(solution)/shard_map/pallas_call | solution.py:91
  1.3 3.5 %collective-permute-start = (bf16[64,4608]{1,0:T(8,128)(2,1)S(1)}, bf16[64,4608]{1,0:T(8,128)(2,1)S(1)}, u32[]{:S(2)}, u32[]{:S(2)}) collective-permute-start(bf16[64,4608]{1,0:T(8,128)(2,1)S(1)} %get-tuple-element.27.refs_0_.refs_4_), channel_id=1, source_target_pairs={{0,4},{4,8},{8,12},{5,1},{9,5},{13,9},{2,6},{6,10},{10,14},{7,3},{... | collective-permute-start | bytes 1769480 | tf_op jit(solution)/shard_map/ppermute | solution.py:594
  4.8 1.9 %collective-permute-start.2 = (bf16[64,4608]{1,0:T(8,128)(2,1)S(1)}, bf16[64,4608]{1,0:T(8,128)(2,1)S(1)}, u32[]{:S(2)}, u32[]{:S(2)}) collective-permute-start(bf16[64,4608]{1,0:T(8,128)(2,1)S(1)} %get-tuple-element.29.refs_1_.refs_5_), channel_id=1, source_target_pairs={{0,4},{4,8},{8,12},{5,1},{9,5},{13,9},{2,6},{6,10},{10,14},{7,3},{... | collective-permute-start | bytes 1769480 | tf_op jit(solution)/shard_map/ppermute | solution.py:594
  6.7 3.6 %shard_map.66 = s32[168,512]{1,0:T(8,128)S(1)} custom-call(bf16[1024,4096]{1,0:T(8,128)(2,1)} %x_ref.6, bf16[4096,1024]{1,0:T(8,128)(2,1)} %w_ref.7), custom_call_target="tpu_custom_call" | custom-call | flops 1073741824 | bytes 6815744 | tf_op jit(solution)/shard_map/pallas_call | solution.py:265
  10.3 1.6 %collective-permute-start.4 = (s32[168,512]{1,0:T(8,128)S(1)}, s32[168,512]{1,0:T(8,128)S(1)}, u32[]{:S(2)}, u32[]{:S(2)}) collective-permute-start(s32[168,512]{1,0:T(8,128)S(1)} %shard_map.66), channel_id=1, source_target_pairs={{0,2},{2,0},{1,3},{3,1},{4,6},{6,4},{5,7},{7,5},{8,10},{10,8},{9,1... | collective-permute-start | bytes 1032200 | tf_op jit(solution)/shard_map/ppermute | solution.py:589
  11.9 1.4 %shard_map.64.table = s32[32]{0:T(128)} custom-call(s32[1024]{0:T(1024)} %ids.1, s32[8]{0:T(128)} %slots.1), custom_call_target="tpu_custom_call" | custom-call | bytes 4096 | tf_op jit(solution)/shard_map/pallas_call | solution.py:123
  13.3 0.0 copy-start
  13.4 0.0 collective-permute-done.refs_2_.refs_1_.refs_6_.refs_0_.refs_3_
  13.4 3.2 %collective-permute-start.1 = (bf16[64,4608]{1,0:T(8,128)(2,1)S(1)}, bf16[64,4608]{1,0:T(8,128)(2,1)S(1)}, u32[]{:S(2)}, u32[]{:S(2)}) collective-permute-start(bf16[64,4608]{1,0:T(8,128)(2,1)S(1)} %collective-permute-done.refs_2_.refs_1_.refs_6_.refs_0_.refs_3_), channel_id=1, source_target_pairs={{4,8},{8,12},{5,1},{9,5},{6,10},{10,14},{7,3},{11,7},{20,24},{24,2... | collective-permute-start | bytes 1769480 | tf_op jit(solution)/shard_map/ppermute | solution.py:594
  16.5 6.7 %shard_map.67 = s32[488,512]{1,0:T(8,128)S(1)} custom-call(bf16[1024,4096]{1,0:T(8,128)(2,1)} %x_ref.6, bf16[4096,1024]{1,0:T(8,128)(2,1)} %w_ref.7), custom_call_target="tpu_custom_call" | custom-call | flops 3221225472 | bytes 12058624 | tf_op jit(solution)/shard_map/pallas_call | solution.py:265
  23.2 0.0 collective-permute-done.2.refs_3_.refs_2_.refs_7_.refs_1_.refs_4_
  23.2 0.0 collective-permute-done.4.refs_4_
  23.2 1.6 %collective-permute-start.5 = (s32[488,512]{1,0:T(8,128)S(1)}, s32[488,512]{1,0:T(8,128)S(1)}, u32[]{:S(2)}, u32[]{:S(2)}) collective-permute-start(s32[488,512]{1,0:T(8,128)S(1)} %shard_map.67), channel_id=1, source_target_pairs={{0,2},{2,0},{1,3},{3,1},{4,6},{6,4},{5,7},{7,5},{8,10},{10,8},{9,1... | collective-permute-start | bytes 2998280 | tf_op jit(solution)/shard_map/ppermute | solution.py:589
  24.8 1.9 %collective-permute-start.6 = (bf16[64,4608]{1,0:T(8,128)(2,1)S(1)}, bf16[64,4608]{1,0:T(8,128)(2,1)S(1)}, u32[]{:S(2)}, u32[]{:S(2)}) collective-permute-start(bf16[64,4608]{1,0:T(8,128)(2,1)S(1)} %collective-permute-done.2.refs_3_.refs_2_.refs_7_.refs_1_.refs_4_), channel_id=1, source_target_pairs={{4,8},{8,12},{5,1},{9,5},{6,10},{10,14},{7,3},{11,7},{20,24},{24,2... | collective-permute-start | bytes 1769480 | tf_op jit(solution)/shard_map/ppermute | solution.py:594
  26.7 0.0 collective-permute-done.1.refs_3_.refs_6_
  26.7 2.4 %collective-permute-start.3 = (bf16[64,4608]{1,0:T(8,128)(2,1)S(1)}, bf16[64,4608]{1,0:T(8,128)(2,1)S(1)}, u32[]{:S(2)}, u32[]{:S(2)}) collective-permute-start(bf16[64,4608]{1,0:T(8,128)(2,1)S(1)} %collective-permute-done.1.refs_3_.refs_6_), channel_id=1, source_target_pairs={{8,12},{5,1},{10,14},{7,3},{24,28},{21,17},{26,30},{23,19}} | collective-permute-start | bytes 1769480 | tf_op jit(solution)/shard_map/ppermute | solution.py:594
  29.2 0.0 copy-done
  29.2 6.1 %shard_map.68 = (f32[384,512]{1,0:T(8,128)S(1)}, bf16[3,2,128,4096]{3,2,1,0:T(8,128)(2,1)S(1)}) custom-call(s32[32]{0:T(128)S(1)} %copy-done, bf16[1024,4096]{1,0:T(8,128)(2,1)} %x_ref.6, bf16[4096,1024]{1,0:T(8,128)(2,1)} %w_ref.7), custom_call_target="tpu_custom_call" | custom-call | flops 1610612736 | bytes 12582912 | tf_op jit(solution)/shard_map/pallas_call | solution.py:354
  35.3 1.3 %collective-permute-done.6.refs_4_.refs_7_ = bf16[64,4608]{1,0:T(8,128)(2,1)S(1)} collective-permute-done((bf16[64,4608]{1,0:T(8,128)(2,1)S(1)}, bf16[64,4608]{1,0:T(8,128)(2,1)S(1)}, u32[]{:S(2)}, u32[]{:S(2)}) %collective-permute-start.6) | collective-permute-done | bytes 589856 | tf_op jit(solution)/shard_map/ppermute | solution.py:594
  36.6 1.9 %collective-permute-start.7 = (bf16[64,4608]{1,0:T(8,128)(2,1)S(1)}, bf16[64,4608]{1,0:T(8,128)(2,1)S(1)}, u32[]{:S(2)}, u32[]{:S(2)}) collective-permute-start(bf16[64,4608]{1,0:T(8,128)(2,1)S(1)} %collective-permute-done.6.refs_4_.refs_7_), channel_id=1, source_target_pairs={{8,12},{5,1},{10,14},{7,3},{24,28},{21,17},{26,30},{23,19}} | collective-permute-start | bytes 1769480 | tf_op jit(solution)/shard_map/ppermute | solution.py:594
  38.5 7.1 %shard_map.70 = (f32[640,512]{1,0:T(8,128)S(1)}, f32[1,128,128]{2,1,0:T(8,128)S(1)}, bf16[128,4608]{1,0:T(8,128)(2,1)S(1)}) custom-call(s32[32]{0:T(128)S(1)} %copy-done, bf16[1024,4096]{1,0:T(8,128)(2,1)} %x_ref.6, bf16[4096,1024]{1,0:T(8,128)(2,1)} %w_ref.7, bf16[64,4608]{1,0:T(8,128)(2,1)S(1)} %get-tuple-element.27.refs_0_.refs_4_, ...), custom_call_target="tpu_custom_call" | custom-call | bytes 2097152 | tf_op jit(solution)/shard_map/pallas_call | solution.py:398
  45.6 0.1 collective-permute-start.10
  45.7 0.5 collective-permute-start.11
  46.2 0.0 collective-permute-done.3.refs_7_.refs_10_
  46.2 0.1 collective-permute-start.8
  46.3 0.0 collective-permute-done.5.refs_0_
  46.3 0.2 shard_map.69.refs_0_
  46.5 0.2 collective-permute-done.7.refs_8_.refs_11_
  46.8 0.3 collective-permute-start.12
  47.0 0.2 collective-permute-start.13
  47.3 0.3 shard_map.71.refs_1_
  47.5 2.7 %collective-permute-done.8.refs_3_.refs_8_.refs_2_.refs_5_ = bf16[128,4608]{1,0:T(8,128)(2,1)S(1)} collective-permute-done((bf16[128,4608]{1,0:T(8,128)(2,1)S(1)}, bf16[128,4608]{1,0:T(8,128)(2,1)S(1)}, u32[]{:S(2)}, u32[]{:S(2)}) %collective-permute-start.8) | collective-permute-done | bytes 1179680 | tf_op jit(solution)/shard_map/ppermute | solution.py:597
  50.2 1.7 %shard_map.72.refs_2_ = f32[2,128,128]{2,1,0:T(8,128)S(1)} custom-call(s32[32]{0:T(128)S(1)} %copy-done, bf16[3,2,128,4096]{3,2,1,0:T(8,128)(2,1)S(1)} %get-tuple-element.45.kept_ref, f32[1,128,128]{2,1,0:T(8,128)S(1)} %get-tuple-element.42.refs_0_, bf16[64,4608]{1,0:T(8,128)(2,1)S(1)} %collective-permute-done.refs_2_.refs_1_.refs_6_.refs_0_.refs_3_, ...), custom_call_target="tpu_custom_call" | custom-call | flops 536870912 | bytes 2097152 | tf_op jit(solution)/shard_map/pallas_call | solution.py:430
  51.9 0.6 collective-permute-start.9
  52.5 0.0 collective-permute-done.10.refs_5_.refs_8_
  52.5 0.0 collective-permute-done.11.refs_6_.refs_9_
  52.5 0.0 collective-permute-done.12.refs_9_.refs_12_
  52.5 0.0 collective-permute-done.13.refs_10_.refs_13_
  52.5 2.6 %shard_map.74.refs_1_ = f32[2,128,128]{2,1,0:T(8,128)S(1)} custom-call(s32[32]{0:T(128)S(1)} %copy-done, bf16[3,2,128,4096]{3,2,1,0:T(8,128)(2,1)S(1)} %get-tuple-element.45.kept_ref, bf16[64,4608]{1,0:T(8,128)(2,1)S(1)} %collective-permute-done.refs_2_.refs_1_.refs_6_.refs_0_.refs_3_, ...), custom_call_target="tpu_custom_call" | custom-call | flops 1073741824 | bytes 4194304 | tf_op jit(solution)/shard_map/pallas_call | solution.py:430
  55.1 1.6 %collective-permute-start.14 = (f32[2,128,128]{2,1,0:T(8,128)S(1)}, f32[2,128,128]{2,1,0:T(8,128)S(1)}, u32[]{:S(2)}, u32[]{:S(2)}) collective-permute-start(f32[2,128,128]{2,1,0:T(8,128)S(1)} %shard_map.74.refs_1_), channel_id=1, source_target_pairs={{0,2},{2,0},{1,3},{3,1},{4,6},{6,4},{5,7},{7,5},{8,10},{10,8},{9,1... | collective-permute-start | bytes 393224 | tf_op jit(solution)/shard_map/ppermute | solution.py:589
  56.7 0.8 %collective-permute-done.9.refs_3_ = f32[2,128,128]{2,1,0:T(8,128)S(1)} collective-permute-done((f32[2,128,128]{2,1,0:T(8,128)S(1)}, f32[2,128,128]{2,1,0:T(8,128)S(1)}, u32[]{:S(2)}, u32[]{:S(2)}) %collective-permute-start.9) | collective-permute-done | bytes 131104 | tf_op jit(solution)/shard_map/ppermute | solution.py:589
  57.5 2.8 %shard_map.73 = (bf16[1024,512]{1,0:T(8,128)(2,1)}, f32[2,2,128,512]{3,2,1,0:T(8,128)S(1)}) custom-call(s32[32]{0:T(128)S(1)} %copy-done, f32[384,512]{1,0:T(8,128)S(1)} %shard_map.69.refs_0_, f32[640,512]{1,0:T(8,128)S(1)} %shard_map.71.refs_1_, f32[2,128,128]{2,1,0:T(8,128)S(1)} %shard_map.72.refs_2_, f32[2,128,128]{2,1,0:T(8,128)S(1)} %collective-permute-done.9.refs_3_, ...), custom_call_target="tpu_custom_call" | custom-call | flops 201326592 | bytes 5242880 | tf_op jit(solution)/shard_map/pallas_call | solution.py:513
  60.3 0.1 collective-permute-done.14.refs_2_
  60.4 2.3 %shard_map.75 = bf16[1024,512]{1,0:T(8,128)(2,1)} custom-call(s32[32]{0:T(128)S(1)} %copy-done, f32[2,2,128,512]{3,2,1,0:T(8,128)S(1)} %get-tuple-element.44.refs_0_, f32[2,128,128]{2,1,0:T(8,128)S(1)} %shard_map.74.refs_1_, f32[2,128,128]{2,1,0:T(8,128)S(1)} %collective-permute-done.14.refs_2_, ...), custom_call_target="tpu_custom_call", output_to_operand_aliasing={{}: (15, {})} | custom-call | flops 100663296 | bytes 2097152 | tf_op jit(solution)/shard_map/pallas_call | solution.py:555
Async XLA Ops:
  1.3 12.1 %collective-permute-start = (bf16[64,4608]{1,0:T(8,128)(2,1)S(1)}, bf16[64,4608]{1,0:T(8,128)(2,1)S(1)}, u32[]{:S(2)}, u32[]{:S(2)}) collective-permute-start(bf16[64,4608]{1,0:T(8,128)(2,1)S(1)} %get-tuple-element.27.refs_0_.refs_4_), channel_id=1, source_target_pairs={{0,4},{4,8},{8,12},{5,1},{9,5},{13,9},{2,6},{6,10},{10,14},{7,3},{... | collective-permute-start | bytes 1769480 | tf_op jit(solution)/shard_map/ppermute | solution.py:594
  4.8 18.5 %collective-permute-start.2 = (bf16[64,4608]{1,0:T(8,128)(2,1)S(1)}, bf16[64,4608]{1,0:T(8,128)(2,1)S(1)}, u32[]{:S(2)}, u32[]{:S(2)}) collective-permute-start(bf16[64,4608]{1,0:T(8,128)(2,1)S(1)} %get-tuple-element.29.refs_1_.refs_5_), channel_id=1, source_target_pairs={{0,4},{4,8},{8,12},{5,1},{9,5},{13,9},{2,6},{6,10},{10,14},{7,3},{... | collective-permute-start | bytes 1769480 | tf_op jit(solution)/shard_map/ppermute | solution.py:594
  10.3 12.9 %collective-permute-start.4 = (s32[168,512]{1,0:T(8,128)S(1)}, s32[168,512]{1,0:T(8,128)S(1)}, u32[]{:S(2)}, u32[]{:S(2)}) collective-permute-start(s32[168,512]{1,0:T(8,128)S(1)} %shard_map.66), channel_id=1, source_target_pairs={{0,2},{2,0},{1,3},{3,1},{4,6},{6,4},{5,7},{7,5},{8,10},{10,8},{9,1... | collective-permute-start | bytes 1032200 | tf_op jit(solution)/shard_map/ppermute | solution.py:589
  13.3 15.9 %copy-start = (s32[32]{0:T(128)S(1)}, s32[32]{0:T(128)}, u32[]{:S(2)}) copy-start(s32[32]{0:T(128)} %shard_map.64.table) | copy-start | bytes 388
  13.4 13.4 %collective-permute-start.1 = (bf16[64,4608]{1,0:T(8,128)(2,1)S(1)}, bf16[64,4608]{1,0:T(8,128)(2,1)S(1)}, u32[]{:S(2)}, u32[]{:S(2)}) collective-permute-start(bf16[64,4608]{1,0:T(8,128)(2,1)S(1)} %collective-permute-done.refs_2_.refs_1_.refs_6_.refs_0_.refs_3_), channel_id=1, source_target_pairs={{4,8},{8,12},{5,1},{9,5},{6,10},{10,14},{7,3},{11,7},{20,24},{24,2... | collective-permute-start | bytes 1769480 | tf_op jit(solution)/shard_map/ppermute | solution.py:594
  23.2 23.1 %collective-permute-start.5 = (s32[488,512]{1,0:T(8,128)S(1)}, s32[488,512]{1,0:T(8,128)S(1)}, u32[]{:S(2)}, u32[]{:S(2)}) collective-permute-start(s32[488,512]{1,0:T(8,128)S(1)} %shard_map.67), channel_id=1, source_target_pairs={{0,2},{2,0},{1,3},{3,1},{4,6},{6,4},{5,7},{7,5},{8,10},{10,8},{9,1... | collective-permute-start | bytes 2998280 | tf_op jit(solution)/shard_map/ppermute | solution.py:589
  24.8 11.8 %collective-permute-start.6 = (bf16[64,4608]{1,0:T(8,128)(2,1)S(1)}, bf16[64,4608]{1,0:T(8,128)(2,1)S(1)}, u32[]{:S(2)}, u32[]{:S(2)}) collective-permute-start(bf16[64,4608]{1,0:T(8,128)(2,1)S(1)} %collective-permute-done.2.refs_3_.refs_2_.refs_7_.refs_1_.refs_4_), channel_id=1, source_target_pairs={{4,8},{8,12},{5,1},{9,5},{6,10},{10,14},{7,3},{11,7},{20,24},{24,2... | collective-permute-start | bytes 1769480 | tf_op jit(solution)/shard_map/ppermute | solution.py:594
  26.7 19.5 %collective-permute-start.3 = (bf16[64,4608]{1,0:T(8,128)(2,1)S(1)}, bf16[64,4608]{1,0:T(8,128)(2,1)S(1)}, u32[]{:S(2)}, u32[]{:S(2)}) collective-permute-start(bf16[64,4608]{1,0:T(8,128)(2,1)S(1)} %collective-permute-done.1.refs_3_.refs_6_), channel_id=1, source_target_pairs={{8,12},{5,1},{10,14},{7,3},{24,28},{21,17},{26,30},{23,19}} | collective-permute-start | bytes 1769480 | tf_op jit(solution)/shard_map/ppermute | solution.py:594
  36.6 10.2 %collective-permute-start.7 = (bf16[64,4608]{1,0:T(8,128)(2,1)S(1)}, bf16[64,4608]{1,0:T(8,128)(2,1)S(1)}, u32[]{:S(2)}, u32[]{:S(2)}) collective-permute-start(bf16[64,4608]{1,0:T(8,128)(2,1)S(1)} %collective-permute-done.6.refs_4_.refs_7_), channel_id=1, source_target_pairs={{8,12},{5,1},{10,14},{7,3},{24,28},{21,17},{26,30},{23,19}} | collective-permute-start | bytes 1769480 | tf_op jit(solution)/shard_map/ppermute | solution.py:594
  45.6 6.9 %collective-permute-start.10 = (bf16[64,4608]{1,0:T(8,128)(2,1)S(1)}, bf16[64,4608]{1,0:T(8,128)(2,1)S(1)}, u32[]{:S(2)}, u32[]{:S(2)}) collective-permute-start(bf16[64,4608]{1,0:T(8,128)(2,1)S(1)} %collective-permute-done.1.refs_3_.refs_6_), channel_id=1, source_target_pairs={{0,1},{1,0},{2,3},{3,2},{4,5},{5,4},{6,7},{7,6},{8,9},{9,8},{10,11... | collective-permute-start | bytes 1769480 | tf_op jit(solution)/shard_map/ppermute | solution.py:597
  45.7 6.8 %collective-permute-start.11 = (bf16[64,4608]{1,0:T(8,128)(2,1)S(1)}, bf16[64,4608]{1,0:T(8,128)(2,1)S(1)}, u32[]{:S(2)}, u32[]{:S(2)}) collective-permute-start(bf16[64,4608]{1,0:T(8,128)(2,1)S(1)} %collective-permute-done.6.refs_4_.refs_7_), channel_id=1, source_target_pairs={{0,1},{1,0},{2,3},{3,2},{4,5},{5,4},{6,7},{7,6},{8,9},{9,8},{10,11... | collective-permute-start | bytes 1769480 | tf_op jit(solution)/shard_map/ppermute | solution.py:597
  46.2 4.0 %collective-permute-start.8 = (bf16[128,4608]{1,0:T(8,128)(2,1)S(1)}, bf16[128,4608]{1,0:T(8,128)(2,1)S(1)}, u32[]{:S(2)}, u32[]{:S(2)}) collective-permute-start(bf16[128,4608]{1,0:T(8,128)(2,1)S(1)} %get-tuple-element.43), channel_id=1, source_target_pairs={{0,1},{1,0},{2,3},{3,2},{4,5},{5,4},{6,7},{7,6},{8,9},{9,8},{10,11... | collective-permute-start | bytes 3538952 | tf_op jit(solution)/shard_map/ppermute | solution.py:597
  46.8 5.7 %collective-permute-start.12 = (bf16[64,4608]{1,0:T(8,128)(2,1)S(1)}, bf16[64,4608]{1,0:T(8,128)(2,1)S(1)}, u32[]{:S(2)}, u32[]{:S(2)}) collective-permute-start(bf16[64,4608]{1,0:T(8,128)(2,1)S(1)} %collective-permute-done.3.refs_7_.refs_10_), channel_id=1, source_target_pairs={{0,1},{1,0},{2,3},{3,2},{4,5},{5,4},{6,7},{7,6},{8,9},{9,8},{10,11... | collective-permute-start | bytes 1769480 | tf_op jit(solution)/shard_map/ppermute | solution.py:597
  47.0 5.5 %collective-permute-start.13 = (bf16[64,4608]{1,0:T(8,128)(2,1)S(1)}, bf16[64,4608]{1,0:T(8,128)(2,1)S(1)}, u32[]{:S(2)}, u32[]{:S(2)}) collective-permute-start(bf16[64,4608]{1,0:T(8,128)(2,1)S(1)} %collective-permute-done.7.refs_8_.refs_11_), channel_id=1, source_target_pairs={{0,1},{1,0},{2,3},{3,2},{4,5},{5,4},{6,7},{7,6},{8,9},{9,8},{10,11... | collective-permute-start | bytes 1769480 | tf_op jit(solution)/shard_map/ppermute | solution.py:597
  51.9 5.6 %collective-permute-start.9 = (f32[2,128,128]{2,1,0:T(8,128)S(1)}, f32[2,128,128]{2,1,0:T(8,128)S(1)}, u32[]{:S(2)}, u32[]{:S(2)}) collective-permute-start(f32[2,128,128]{2,1,0:T(8,128)S(1)} %shard_map.72.refs_2_), channel_id=1, source_target_pairs={{0,2},{2,0},{1,3},{3,1},{4,6},{6,4},{5,7},{7,5},{8,10},{10,8},{9,1... | collective-permute-start | bytes 393224 | tf_op jit(solution)/shard_map/ppermute | solution.py:589
  55.1 5.3 %collective-permute-start.14 = (f32[2,128,128]{2,1,0:T(8,128)S(1)}, f32[2,128,128]{2,1,0:T(8,128)S(1)}, u32[]{:S(2)}, u32[]{:S(2)}) collective-permute-start(f32[2,128,128]{2,1,0:T(8,128)S(1)} %shard_map.74.refs_1_), channel_id=1, source_target_pairs={{0,2},{2,0},{1,3},{3,1},{4,6},{6,4},{5,7},{7,5},{8,10},{10,8},{9,1... | collective-permute-start | bytes 393224 | tf_op jit(solution)/shard_map/ppermute | solution.py:589

commit v18 on v17

--- a/solution.py
+++ b/solution.py
@@ -292,22 +292,28 @@
     )(sums, *coded)
 
 
-def shrink_into(o_ref, at, table, k, rows_of, views, rank):
-    for j in range(MOST):
+def shrink_into(o_ref, at, table, k, rows_of, views, rank, pair):
+    def one(j, carry):
         _, _, within = segment_of(table, k, j)
         for stage, ref, first, whose, i in views:
             if stage not in stages_of(k):
                 continue
 
             @pl.when((whose == table[k * ENTRIES]) & (within == i))
-            def _(j=j, ref=ref, first=first):
+            def _(ref=ref, first=first):
                 rows = rows_of(j)
-                o_ref[at, :, j * rank : (j + 1) * rank] = lax.dot_general(
+                pair[j] = lax.dot_general(
                     rows,
                     ref[first : first + rank, : rows.shape[1]],
                     (((1,), (1,)), ((), ())),
                     preferred_element_type=jnp.float32,
                 )
+
+        return carry
+
+    lax.fori_loop(0, MOST, one, 0)
+    for j in range(MOST):
+        o_ref[at, :, j * rank : (j + 1) * rank] = pair[j]
 
 
 def join_copies(halves, whole, sems):
@@ -368,7 +374,7 @@
 
 def lower_kernel(per_device, rank, table, x_ref, w_ref, *refs):
     messages, halves, refs = refs[:per_device], refs[per_device : 2 * per_device], refs[2 * per_device :]
-    coded_refs, (o_ref, s_ref, whole_ref, x, w, sems, mine, mine_sems, join_sems) = refs[:-9], refs[-9:]
+    coded_refs, (o_ref, s_ref, whole_ref, x, w, sems, mine, mine_sems, join_sems, pair) = refs[:-10], refs[-10:]
     work = load_base(UPPER, x.shape[0] // SEGMENT_ROWS, lax.axis_index("tensor"), x_ref, w_ref, x, w, sems)
     joins = join_copies(halves, whole_ref, join_sems)
     loads = []
@@ -386,7 +392,7 @@
     for copy in loads:
         copy.wait()
     views = views_of(messages, [0], [(per_device, 0)], rank)
-    shrink_into(s_ref, 0, table, 0, lambda j: mine[j], views, rank)
+    shrink_into(s_ref, 0, table, 0, lambda j: mine[j], views, rank, pair)
     for copy in joins:
         copy.wait()
 
@@ -409,6 +415,7 @@
             pltpu.VMEM((MOST, SEGMENT_ROWS, width), jnp.bfloat16),
             pltpu.SemaphoreType.DMA((MOST,)),
             pltpu.SemaphoreType.DMA((per_device,)),
+            pltpu.VMEM((MOST, SEGMENT_ROWS, rank), jnp.float32),
         ],
         compiler_params=params(14),
         cost_estimate=cost(0 * half * width * columns, 4 * rows * columns),
@@ -416,12 +423,12 @@
 
 
 def shrink_kernel(ks, rank, at, layout, table, kept_ref, *refs):
-    buffers, o_ref = refs[1 if at else 0 : -1], refs[-1]
+    buffers, (o_ref, pair) = refs[1 if at else 0 : -2], refs[-2:]
     if at:
         o_ref[:at] = refs[0][...]
     views = views_of(buffers, stages_of_all(ks), layout, rank)
     for i, k in enumerate(ks):
-        shrink_into(o_ref, at + i, table, k, lambda j, k=k: kept_ref[k - 1, j], views, rank)
+        shrink_into(o_ref, at + i, table, k, lambda j, k=k: kept_ref[k - 1, j], views, rank, pair)
 
 
 def shrink_call(ks, table, kept, before, buffers, layout, rank):
@@ -432,6 +439,7 @@
         in_specs=[SMEM] + [VMEM] * (1 + len(before) + len(buffers)),
         out_specs=VMEM,
         out_shape=jax.ShapeDtypeStruct((at + len(ks), SEGMENT_ROWS, MOST * rank), jnp.float32),
+        scratch_shapes=[pltpu.VMEM((MOST, SEGMENT_ROWS, rank), jnp.float32)],
         compiler_params=params(4),
         cost_estimate=cost(
             len(ks) * MOST * 2 * SEGMENT_ROWS * width * 256, len(ks) * 4 * SEGMENT_ROWS * width

time: 63.2 us -> 63.3 us (level)
  transfers between devices with their start and end apart: 15 -> 15, of which waited for: 5 -> 4; matrix products, arithmetic and copies ran while one was open for 0% -> 0% of each run, Pallas kernels for 52% -> 51%
where the time goes in v18:
time: 63.3 us; the launch traced here: 63 us
  Pallas kernels  35.9 us (57%)
  starting transfers between devices  21.6 us (34%)
  waiting for transfers between devices  5.19 us (8%)
    ppermute x6, starting transfers between devices, along_line(): return lax.ppermute(array, ('adapter', 'dp'), up + down)  15 us
    pallas_call x2, Pallas kernels, sent_call(): pl.pallas_call(functools.partial(sent_kernel, first, sizes, step, n_tenso...  10.3 us
    pallas_call x1, Pallas kernels, lower_call(): pl.pallas_call(functools.partial(lower_kernel, per_device, rank), in_spec...  7.12 us
    pallas_call x1, Pallas kernels, upper_call(): pl.pallas_call(functools.partial(upper_kernel, n_adapter), in_specs=[SMEM...  5.99 us
    ppermute x4, starting transfers between devices, swap_tensor(): return lax.ppermute(array, 'tensor', pairs)  5.33 us
    pallas_call x2, Pallas kernels, shrink_call(): pl.pallas_call(functools.partial(shrink_kernel, ks, rank, at, layout), in...  4.19 us
    ppermute x5, waiting for transfers between devices, swap_cores(): return lax.ppermute(array, 'dp', [(0, 1), (1, 0)])  2.87 us
    pallas_call x1, Pallas kernels, early(): pl.pallas_call(functools.partial(early_kernel, n_adapter, n_tensor, rank,...  2.81 us
  transfers between devices with their start and end apart: 15, of which 4 were waited for; matrix products, arithmetic and copies ran while one was open for 0% of the time, Pallas kernels for 51%

profile of v18, /device:TPU:16, one launch (start us, length us, event | category | flops | bytes accessed | tf_op | source)
XLA Modules:
  0.0 63.0 jit_solution(3352376649748274027)
XLA Ops:
  0.0 1.3 %shard_map.65 = (bf16[64,4608]{1,0:T(8,128)(2,1)S(1)}, bf16[64,4608]{1,0:T(8,128)(2,1)S(1)}) custom-call(bf16[128,4096]{1,0:T(8,128)(2,1)} %bitcast.4, bf16[128,1024]{1,0:T(8,128)(2,1)} %bitcast.5), custom_call_target="tpu_custom_call" | custom-call | bytes 2359296 | tf_op jit(solution)/shard_map/pallas_call | solution.py:91
  1.3 3.5 %collective-permute-start = (bf16[64,4608]{1,0:T(8,128)(2,1)S(1)}, bf16[64,4608]{1,0:T(8,128)(2,1)S(1)}, u32[]{:S(2)}, u32[]{:S(2)}) collective-permute-start(bf16[64,4608]{1,0:T(8,128)(2,1)S(1)} %get-tuple-element.27.refs_0_.refs_4_), channel_id=1, source_target_pairs={{0,4},{4,8},{8,12},{5,1},{9,5},{13,9},{2,6},{6,10},{10,14},{7,3},{... | collective-permute-start | bytes 1769480 | tf_op jit(solution)/shard_map/ppermute | solution.py:602
  4.8 1.9 %collective-permute-start.2 = (bf16[64,4608]{1,0:T(8,128)(2,1)S(1)}, bf16[64,4608]{1,0:T(8,128)(2,1)S(1)}, u32[]{:S(2)}, u32[]{:S(2)}) collective-permute-start(bf16[64,4608]{1,0:T(8,128)(2,1)S(1)} %get-tuple-element.29.refs_1_.refs_5_), channel_id=1, source_target_pairs={{0,4},{4,8},{8,12},{5,1},{9,5},{13,9},{2,6},{6,10},{10,14},{7,3},{... | collective-permute-start | bytes 1769480 | tf_op jit(solution)/shard_map/ppermute | solution.py:602
  6.7 3.6 %shard_map.66 = s32[168,512]{1,0:T(8,128)S(1)} custom-call(bf16[1024,4096]{1,0:T(8,128)(2,1)} %x_ref.6, bf16[4096,1024]{1,0:T(8,128)(2,1)} %w_ref.7), custom_call_target="tpu_custom_call" | custom-call | flops 1073741824 | bytes 6815744 | tf_op jit(solution)/shard_map/pallas_call | solution.py:265
  10.3 1.6 %collective-permute-start.4 = (s32[168,512]{1,0:T(8,128)S(1)}, s32[168,512]{1,0:T(8,128)S(1)}, u32[]{:S(2)}, u32[]{:S(2)}) collective-permute-start(s32[168,512]{1,0:T(8,128)S(1)} %shard_map.66), channel_id=1, source_target_pairs={{0,2},{2,0},{1,3},{3,1},{4,6},{6,4},{5,7},{7,5},{8,10},{10,8},{9,1... | collective-permute-start | bytes 1032200 | tf_op jit(solution)/shard_map/ppermute | solution.py:597
  11.9 1.4 %shard_map.64.table = s32[32]{0:T(128)} custom-call(s32[1024]{0:T(1024)} %ids.1, s32[8]{0:T(128)} %slots.1), custom_call_target="tpu_custom_call" | custom-call | bytes 4096 | tf_op jit(solution)/shard_map/pallas_call | solution.py:123
  13.3 0.0 copy-start
  13.4 0.0 collective-permute-done.refs_2_.refs_1_.refs_6_.refs_0_.refs_3_
  13.4 3.2 %collective-permute-start.1 = (bf16[64,4608]{1,0:T(8,128)(2,1)S(1)}, bf16[64,4608]{1,0:T(8,128)(2,1)S(1)}, u32[]{:S(2)}, u32[]{:S(2)}) collective-permute-start(bf16[64,4608]{1,0:T(8,128)(2,1)S(1)} %collective-permute-done.refs_2_.refs_1_.refs_6_.refs_0_.refs_3_), channel_id=1, source_target_pairs={{4,8},{8,12},{5,1},{9,5},{6,10},{10,14},{7,3},{11,7},{20,24},{24,2... | collective-permute-start | bytes 1769480 | tf_op jit(solution)/shard_map/ppermute | solution.py:602
  16.5 6.7 %shard_map.67 = s32[488,512]{1,0:T(8,128)S(1)} custom-call(bf16[1024,4096]{1,0:T(8,128)(2,1)} %x_ref.6, bf16[4096,1024]{1,0:T(8,128)(2,1)} %w_ref.7), custom_call_target="tpu_custom_call" | custom-call | flops 3221225472 | bytes 12058624 | tf_op jit(solution)/shard_map/pallas_call | solution.py:265
  23.2 0.0 collective-permute-done.2.refs_3_.refs_2_.refs_7_.refs_1_.refs_4_
  23.2 0.0 collective-permute-done.4.refs_4_
  23.2 1.6 %collective-permute-start.5 = (s32[488,512]{1,0:T(8,128)S(1)}, s32[488,512]{1,0:T(8,128)S(1)}, u32[]{:S(2)}, u32[]{:S(2)}) collective-permute-start(s32[488,512]{1,0:T(8,128)S(1)} %shard_map.67), channel_id=1, source_target_pairs={{0,2},{2,0},{1,3},{3,1},{4,6},{6,4},{5,7},{7,5},{8,10},{10,8},{9,1... | collective-permute-start | bytes 2998280 | tf_op jit(solution)/shard_map/ppermute | solution.py:597
  24.8 1.9 %collective-permute-start.6 = (bf16[64,4608]{1,0:T(8,128)(2,1)S(1)}, bf16[64,4608]{1,0:T(8,128)(2,1)S(1)}, u32[]{:S(2)}, u32[]{:S(2)}) collective-permute-start(bf16[64,4608]{1,0:T(8,128)(2,1)S(1)} %collective-permute-done.2.refs_3_.refs_2_.refs_7_.refs_1_.refs_4_), channel_id=1, source_target_pairs={{4,8},{8,12},{5,1},{9,5},{6,10},{10,14},{7,3},{11,7},{20,24},{24,2... | collective-permute-start | bytes 1769480 | tf_op jit(solution)/shard_map/ppermute | solution.py:602
  26.7 0.0 collective-permute-done.1.refs_3_.refs_6_
  26.7 2.4 %collective-permute-start.3 = (bf16[64,4608]{1,0:T(8,128)(2,1)S(1)}, bf16[64,4608]{1,0:T(8,128)(2,1)S(1)}, u32[]{:S(2)}, u32[]{:S(2)}) collective-permute-start(bf16[64,4608]{1,0:T(8,128)(2,1)S(1)} %collective-permute-done.1.refs_3_.refs_6_), channel_id=1, source_target_pairs={{8,12},{5,1},{10,14},{7,3},{24,28},{21,17},{26,30},{23,19}} | collective-permute-start | bytes 1769480 | tf_op jit(solution)/shard_map/ppermute | solution.py:602
  29.2 0.0 copy-done
  29.2 6.0 %shard_map.68 = (f32[384,512]{1,0:T(8,128)S(1)}, bf16[3,2,128,4096]{3,2,1,0:T(8,128)(2,1)S(1)}) custom-call(s32[32]{0:T(128)S(1)} %copy-done, bf16[1024,4096]{1,0:T(8,128)(2,1)} %x_ref.6, bf16[4096,1024]{1,0:T(8,128)(2,1)} %w_ref.7), custom_call_target="tpu_custom_call" | custom-call | flops 1610612736 | bytes 12582912 | tf_op jit(solution)/shard_map/pallas_call | solution.py:360
  35.2 1.4 %collective-permute-done.6.refs_4_.refs_7_ = bf16[64,4608]{1,0:T(8,128)(2,1)S(1)} collective-permute-done((bf16[64,4608]{1,0:T(8,128)(2,1)S(1)}, bf16[64,4608]{1,0:T(8,128)(2,1)S(1)}, u32[]{:S(2)}, u32[]{:S(2)}) %collective-permute-start.6) | collective-permute-done | bytes 589856 | tf_op jit(solution)/shard_map/ppermute | solution.py:602
  36.6 2.1 %collective-permute-start.7 = (bf16[64,4608]{1,0:T(8,128)(2,1)S(1)}, bf16[64,4608]{1,0:T(8,128)(2,1)S(1)}, u32[]{:S(2)}, u32[]{:S(2)}) collective-permute-start(bf16[64,4608]{1,0:T(8,128)(2,1)S(1)} %collective-permute-done.6.refs_4_.refs_7_), channel_id=1, source_target_pairs={{8,12},{5,1},{10,14},{7,3},{24,28},{21,17},{26,30},{23,19}} | collective-permute-start | bytes 1769480 | tf_op jit(solution)/shard_map/ppermute | solution.py:602
  38.7 7.1 %shard_map.70 = (f32[640,512]{1,0:T(8,128)S(1)}, f32[1,128,128]{2,1,0:T(8,128)S(1)}, bf16[128,4608]{1,0:T(8,128)(2,1)S(1)}) custom-call(s32[32]{0:T(128)S(1)} %copy-done, bf16[1024,4096]{1,0:T(8,128)(2,1)} %x_ref.6, bf16[4096,1024]{1,0:T(8,128)(2,1)} %w_ref.7, bf16[64,4608]{1,0:T(8,128)(2,1)S(1)} %get-tuple-element.27.refs_0_.refs_4_, ...), custom_call_target="tpu_custom_call" | custom-call | bytes 2097152 | tf_op jit(solution)/shard_map/pallas_call | solution.py:404
  45.8 0.1 collective-permute-start.10
  45.9 0.5 collective-permute-start.11
  46.4 0.0 collective-permute-done.3.refs_7_.refs_10_
  46.4 0.1 collective-permute-start.8
  46.5 0.0 collective-permute-done.5.refs_0_
  46.5 0.2 shard_map.69.refs_0_
  46.7 0.0 collective-permute-done.7.refs_8_.refs_11_
  46.8 0.5 collective-permute-start.12
  47.2 0.1 collective-permute-start.13
  47.3 0.3 shard_map.71.refs_1_
  47.6 2.9 %collective-permute-done.8.refs_3_.refs_8_.refs_2_.refs_5_ = bf16[128,4608]{1,0:T(8,128)(2,1)S(1)} collective-permute-done((bf16[128,4608]{1,0:T(8,128)(2,1)S(1)}, bf16[128,4608]{1,0:T(8,128)(2,1)S(1)}, u32[]{:S(2)}, u32[]{:S(2)}) %collective-permute-start.8) | collective-permute-done | bytes 1179680 | tf_op jit(solution)/shard_map/ppermute | solution.py:605
  50.4 1.5 %shard_map.72.refs_2_ = f32[2,128,128]{2,1,0:T(8,128)S(1)} custom-call(s32[32]{0:T(128)S(1)} %copy-done, bf16[3,2,128,4096]{3,2,1,0:T(8,128)(2,1)S(1)} %get-tuple-element.45.kept_ref, f32[1,128,128]{2,1,0:T(8,128)S(1)} %get-tuple-element.42.refs_0_, bf16[64,4608]{1,0:T(8,128)(2,1)S(1)} %collective-permute-done.refs_2_.refs_1_.refs_6_.refs_0_.refs_3_, ...), custom_call_target="tpu_custom_call" | custom-call | flops 536870912 | bytes 2097152 | tf_op jit(solution)/shard_map/pallas_call | solution.py:437
  52.0 0.5 collective-permute-start.9
  52.5 0.0 collective-permute-done.10.refs_5_.refs_8_
  52.5 0.0 collective-permute-done.11.refs_6_.refs_9_
  52.5 0.0 collective-permute-done.12.refs_9_.refs_12_
  52.5 0.0 collective-permute-done.13.refs_10_.refs_13_
  52.6 2.6 %shard_map.74.refs_1_ = f32[2,128,128]{2,1,0:T(8,128)S(1)} custom-call(s32[32]{0:T(128)S(1)} %copy-done, bf16[3,2,128,4096]{3,2,1,0:T(8,128)(2,1)S(1)} %get-tuple-element.45.kept_ref, bf16[64,4608]{1,0:T(8,128)(2,1)S(1)} %collective-permute-done.refs_2_.refs_1_.refs_6_.refs_0_.refs_3_, ...), custom_call_target="tpu_custom_call" | custom-call | flops 1073741824 | bytes 4194304 | tf_op jit(solution)/shard_map/pallas_call | solution.py:437
  55.2 1.6 %collective-permute-start.14 = (f32[2,128,128]{2,1,0:T(8,128)S(1)}, f32[2,128,128]{2,1,0:T(8,128)S(1)}, u32[]{:S(2)}, u32[]{:S(2)}) collective-permute-start(f32[2,128,128]{2,1,0:T(8,128)S(1)} %shard_map.74.refs_1_), channel_id=1, source_target_pairs={{0,2},{2,0},{1,3},{3,1},{4,6},{6,4},{5,7},{7,5},{8,10},{10,8},{9,1... | collective-permute-start | bytes 393224 | tf_op jit(solution)/shard_map/ppermute | solution.py:597
  56.8 0.8 %collective-permute-done.9.refs_3_ = f32[2,128,128]{2,1,0:T(8,128)S(1)} collective-permute-done((f32[2,128,128]{2,1,0:T(8,128)S(1)}, f32[2,128,128]{2,1,0:T(8,128)S(1)}, u32[]{:S(2)}, u32[]{:S(2)}) %collective-permute-start.9) | collective-permute-done | bytes 131104 | tf_op jit(solution)/shard_map/ppermute | solution.py:597
  57.6 2.8 %shard_map.73 = (bf16[1024,512]{1,0:T(8,128)(2,1)}, f32[2,2,128,512]{3,2,1,0:T(8,128)S(1)}) custom-call(s32[32]{0:T(128)S(1)} %copy-done, f32[384,512]{1,0:T(8,128)S(1)} %shard_map.69.refs_0_, f32[640,512]{1,0:T(8,128)S(1)} %shard_map.71.refs_1_, f32[2,128,128]{2,1,0:T(8,128)S(1)} %shard_map.72.refs_2_, f32[2,128,128]{2,1,0:T(8,128)S(1)} %collective-permute-done.9.refs_3_, ...), custom_call_target="tpu_custom_call" | custom-call | flops 201326592 | bytes 5242880 | tf_op jit(solution)/shard_map/pallas_call | solution.py:521
  60.4 0.1 collective-permute-done.14.refs_2_
  60.5 2.3 %shard_map.75 = bf16[1024,512]{1,0:T(8,128)(2,1)} custom-call(s32[32]{0:T(128)S(1)} %copy-done, f32[2,2,128,512]{3,2,1,0:T(8,128)S(1)} %get-tuple-element.44.refs_0_, f32[2,128,128]{2,1,0:T(8,128)S(1)} %shard_map.74.refs_1_, f32[2,128,128]{2,1,0:T(8,128)S(1)} %collective-permute-done.14.refs_2_, ...), custom_call_target="tpu_custom_call", output_to_operand_aliasing={{}: (15, {})} | custom-call | flops 100663296 | bytes 2097152 | tf_op jit(solution)/shard_map/pallas_call | solution.py:563
Async XLA Ops:
  1.3 12.1 %collective-permute-start = (bf16[64,4608]{1,0:T(8,128)(2,1)S(1)}, bf16[64,4608]{1,0:T(8,128)(2,1)S(1)}, u32[]{:S(2)}, u32[]{:S(2)}) collective-permute-start(bf16[64,4608]{1,0:T(8,128)(2,1)S(1)} %get-tuple-element.27.refs_0_.refs_4_), channel_id=1, source_target_pairs={{0,4},{4,8},{8,12},{5,1},{9,5},{13,9},{2,6},{6,10},{10,14},{7,3},{... | collective-permute-start | bytes 1769480 | tf_op jit(solution)/shard_map/ppermute | solution.py:602
  4.8 18.5 %collective-permute-start.2 = (bf16[64,4608]{1,0:T(8,128)(2,1)S(1)}, bf16[64,4608]{1,0:T(8,128)(2,1)S(1)}, u32[]{:S(2)}, u32[]{:S(2)}) collective-permute-start(bf16[64,4608]{1,0:T(8,128)(2,1)S(1)} %get-tuple-element.29.refs_1_.refs_5_), channel_id=1, source_target_pairs={{0,4},{4,8},{8,12},{5,1},{9,5},{13,9},{2,6},{6,10},{10,14},{7,3},{... | collective-permute-start | bytes 1769480 | tf_op jit(solution)/shard_map/ppermute | solution.py:602
  10.3 12.9 %collective-permute-start.4 = (s32[168,512]{1,0:T(8,128)S(1)}, s32[168,512]{1,0:T(8,128)S(1)}, u32[]{:S(2)}, u32[]{:S(2)}) collective-permute-start(s32[168,512]{1,0:T(8,128)S(1)} %shard_map.66), channel_id=1, source_target_pairs={{0,2},{2,0},{1,3},{3,1},{4,6},{6,4},{5,7},{7,5},{8,10},{10,8},{9,1... | collective-permute-start | bytes 1032200 | tf_op jit(solution)/shard_map/ppermute | solution.py:597
  13.3 15.9 %copy-start = (s32[32]{0:T(128)S(1)}, s32[32]{0:T(128)}, u32[]{:S(2)}) copy-start(s32[32]{0:T(128)} %shard_map.64.table) | copy-start | bytes 388
  13.4 13.4 %collective-permute-start.1 = (bf16[64,4608]{1,0:T(8,128)(2,1)S(1)}, bf16[64,4608]{1,0:T(8,128)(2,1)S(1)}, u32[]{:S(2)}, u32[]{:S(2)}) collective-permute-start(bf16[64,4608]{1,0:T(8,128)(2,1)S(1)} %collective-permute-done.refs_2_.refs_1_.refs_6_.refs_0_.refs_3_), channel_id=1, source_target_pairs={{4,8},{8,12},{5,1},{9,5},{6,10},{10,14},{7,3},{11,7},{20,24},{24,2... | collective-permute-start | bytes 1769480 | tf_op jit(solution)/shard_map/ppermute | solution.py:602
  23.2 23.3 %collective-permute-start.5 = (s32[488,512]{1,0:T(8,128)S(1)}, s32[488,512]{1,0:T(8,128)S(1)}, u32[]{:S(2)}, u32[]{:S(2)}) collective-permute-start(s32[488,512]{1,0:T(8,128)S(1)} %shard_map.67), channel_id=1, source_target_pairs={{0,2},{2,0},{1,3},{3,1},{4,6},{6,4},{5,7},{7,5},{8,10},{10,8},{9,1... | collective-permute-start | bytes 2998280 | tf_op jit(solution)/shard_map/ppermute | solution.py:597
  24.8 11.8 %collective-permute-start.6 = (bf16[64,4608]{1,0:T(8,128)(2,1)S(1)}, bf16[64,4608]{1,0:T(8,128)(2,1)S(1)}, u32[]{:S(2)}, u32[]{:S(2)}) collective-permute-start(bf16[64,4608]{1,0:T(8,128)(2,1)S(1)} %collective-permute-done.2.refs_3_.refs_2_.refs_7_.refs_1_.refs_4_), channel_id=1, source_target_pairs={{4,8},{8,12},{5,1},{9,5},{6,10},{10,14},{7,3},{11,7},{20,24},{24,2... | collective-permute-start | bytes 1769480 | tf_op jit(solution)/shard_map/ppermute | solution.py:602
  26.7 19.7 %collective-permute-start.3 = (bf16[64,4608]{1,0:T(8,128)(2,1)S(1)}, bf16[64,4608]{1,0:T(8,128)(2,1)S(1)}, u32[]{:S(2)}, u32[]{:S(2)}) collective-permute-start(bf16[64,4608]{1,0:T(8,128)(2,1)S(1)} %collective-permute-done.1.refs_3_.refs_6_), channel_id=1, source_target_pairs={{8,12},{5,1},{10,14},{7,3},{24,28},{21,17},{26,30},{23,19}} | collective-permute-start | bytes 1769480 | tf_op jit(solution)/shard_map/ppermute | solution.py:602
  36.6 10.2 %collective-permute-start.7 = (bf16[64,4608]{1,0:T(8,128)(2,1)S(1)}, bf16[64,4608]{1,0:T(8,128)(2,1)S(1)}, u32[]{:S(2)}, u32[]{:S(2)}) collective-permute-start(bf16[64,4608]{1,0:T(8,128)(2,1)S(1)} %collective-permute-done.6.refs_4_.refs_7_), channel_id=1, source_target_pairs={{8,12},{5,1},{10,14},{7,3},{24,28},{21,17},{26,30},{23,19}} | collective-permute-start | bytes 1769480 | tf_op jit(solution)/shard_map/ppermute | solution.py:602
  45.8 6.7 %collective-permute-start.10 = (bf16[64,4608]{1,0:T(8,128)(2,1)S(1)}, bf16[64,4608]{1,0:T(8,128)(2,1)S(1)}, u32[]{:S(2)}, u32[]{:S(2)}) collective-permute-start(bf16[64,4608]{1,0:T(8,128)(2,1)S(1)} %collective-permute-done.1.refs_3_.refs_6_), channel_id=1, source_target_pairs={{0,1},{1,0},{2,3},{3,2},{4,5},{5,4},{6,7},{7,6},{8,9},{9,8},{10,11... | collective-permute-start | bytes 1769480 | tf_op jit(solution)/shard_map/ppermute | solution.py:605
  45.9 6.6 %collective-permute-start.11 = (bf16[64,4608]{1,0:T(8,128)(2,1)S(1)}, bf16[64,4608]{1,0:T(8,128)(2,1)S(1)}, u32[]{:S(2)}, u32[]{:S(2)}) collective-permute-start(bf16[64,4608]{1,0:T(8,128)(2,1)S(1)} %collective-permute-done.6.refs_4_.refs_7_), channel_id=1, source_target_pairs={{0,1},{1,0},{2,3},{3,2},{4,5},{5,4},{6,7},{7,6},{8,9},{9,8},{10,11... | collective-permute-start | bytes 1769480 | tf_op jit(solution)/shard_map/ppermute | solution.py:605
  46.4 4.0 %collective-permute-start.8 = (bf16[128,4608]{1,0:T(8,128)(2,1)S(1)}, bf16[128,4608]{1,0:T(8,128)(2,1)S(1)}, u32[]{:S(2)}, u32[]{:S(2)}) collective-permute-start(bf16[128,4608]{1,0:T(8,128)(2,1)S(1)} %get-tuple-element.43), channel_id=1, source_target_pairs={{0,1},{1,0},{2,3},{3,2},{4,5},{5,4},{6,7},{7,6},{8,9},{9,8},{10,11... | collective-permute-start | bytes 3538952 | tf_op jit(solution)/shard_map/ppermute | solution.py:605
  46.8 5.8 %collective-permute-start.12 = (bf16[64,4608]{1,0:T(8,128)(2,1)S(1)}, bf16[64,4608]{1,0:T(8,128)(2,1)S(1)}, u32[]{:S(2)}, u32[]{:S(2)}) collective-permute-start(bf16[64,4608]{1,0:T(8,128)(2,1)S(1)} %collective-permute-done.3.refs_7_.refs_10_), channel_id=1, source_target_pairs={{0,1},{1,0},{2,3},{3,2},{4,5},{5,4},{6,7},{7,6},{8,9},{9,8},{10,11... | collective-permute-start | bytes 1769480 | tf_op jit(solution)/shard_map/ppermute | solution.py:605
  47.2 5.3 %collective-permute-start.13 = (bf16[64,4608]{1,0:T(8,128)(2,1)S(1)}, bf16[64,4608]{1,0:T(8,128)(2,1)S(1)}, u32[]{:S(2)}, u32[]{:S(2)}) collective-permute-start(bf16[64,4608]{1,0:T(8,128)(2,1)S(1)} %collective-permute-done.7.refs_8_.refs_11_), channel_id=1, source_target_pairs={{0,1},{1,0},{2,3},{3,2},{4,5},{5,4},{6,7},{7,6},{8,9},{9,8},{10,11... | collective-permute-start | bytes 1769480 | tf_op jit(solution)/shard_map/ppermute | solution.py:605
  52.0 5.6 %collective-permute-start.9 = (f32[2,128,128]{2,1,0:T(8,128)S(1)}, f32[2,128,128]{2,1,0:T(8,128)S(1)}, u32[]{:S(2)}, u32[]{:S(2)}) collective-permute-start(f32[2,128,128]{2,1,0:T(8,128)S(1)} %shard_map.72.refs_2_), channel_id=1, source_target_pairs={{0,2},{2,0},{1,3},{3,1},{4,6},{6,4},{5,7},{7,5},{8,10},{10,8},{9,1... | collective-permute-start | bytes 393224 | tf_op jit(solution)/shard_map/ppermute | solution.py:597
  55.2 5.3 %collective-permute-start.14 = (f32[2,128,128]{2,1,0:T(8,128)S(1)}, f32[2,128,128]{2,1,0:T(8,128)S(1)}, u32[]{:S(2)}, u32[]{:S(2)}) collective-permute-start(f32[2,128,128]{2,1,0:T(8,128)S(1)} %shard_map.74.refs_1_), channel_id=1, source_target_pairs={{0,2},{2,0},{1,3},{3,1},{4,6},{6,4},{5,7},{7,5},{8,10},{10,8},{9,1... | collective-permute-start | bytes 393224 | tf_op jit(solution)/shard_map/ppermute | solution.py:597

commit v19 on v18

--- a/solution.py
+++ b/solution.py
@@ -476,9 +476,10 @@
 def early_kernel(n_adapter, n_tensor, rank, layout, n_buffers, table, *refs):
     first = n_adapter - LATE
     upper_ref, lower_ref, refs = refs[0], refs[1], refs[2:]
-    shrinks, refs = refs[: -4 - n_buffers], refs[-4 - n_buffers :]
-    buffers, (o_ref, rest_ref, up, sums) = refs[:-4], refs[-4:]
-    views = views_of(buffers, range(first), layout, rank)
+    shrinks, refs = refs[: -7 - n_buffers], refs[-7 - n_buffers :]
+    buffers, (o_ref, rest_ref, late_up, up, sums, out, sems) = refs[:-7], refs[-7:]
+    views = views_of(buffers, range(n_adapter), layout, rank)
+    stores = []
     for k in range(first):
         for j in range(MOST):
             fetch_up(up, k * MOST + j, table, k, j, views, rank)
@@ -506,14 +507,17 @@
             value = sums[...]
             if k >= first:
                 rest_ref[k - first, j] = value
+                fetch_up(late_up, (k - first) * MOST + j, table, k, j, views, rank)
                 continue
             lora = up_product(shares[k], j, up[k * MOST + j], rank)
-
-            @pl.when(used)
-            def _(start=start, value=value, lora=lora):
-                o_ref[pl.ds(start, SEGMENT_ROWS), :] = (value + adapter_scale * lora).astype(
-                    jnp.bfloat16
-                )
+            out[k, j] = (value + adapter_scale * lora).astype(jnp.bfloat16)
+            store = pltpu.make_async_copy(
+                out.at[k, j], o_ref.at[pl.ds(start, SEGMENT_ROWS), :], sems.at[k, j]
+            )
+            pl.when(used)(store.start)
+            stores.append((used, store))
+    for used, store in stores:
+        pl.when(used)(store.wait)
 
 
 def early(n_adapter, n_tensor, table, upper, lower, shrinks, buffers, layout, rank):
@@ -521,31 +525,32 @@
     return pl.pallas_call(
         functools.partial(early_kernel, n_adapter, n_tensor, rank, layout, len(buffers)),
         in_specs=[SMEM] + [VMEM] * (2 + len(shrinks) + len(buffers)),
-        out_specs=[VMEM, VMEM],
+        out_specs=[ANY, VMEM, VMEM],
         out_shape=[
             jax.ShapeDtypeStruct((rows, columns), jnp.bfloat16),
             jax.ShapeDtypeStruct((LATE, MOST, SEGMENT_ROWS, columns), jnp.float32),
+            jax.ShapeDtypeStruct((LATE * MOST, 2 * rank, columns), jnp.bfloat16),
         ],
         scratch_shapes=[
             pltpu.VMEM(((n_adapter - LATE) * MOST, 2 * rank, columns), jnp.bfloat16),
             pltpu.VMEM((SEGMENT_ROWS, columns), jnp.float32),
+            pltpu.VMEM((n_adapter - LATE, MOST, SEGMENT_ROWS, columns), jnp.bfloat16),
+            pltpu.SemaphoreType.DMA((n_adapter - LATE, MOST)),
         ],
         compiler_params=params(16),
         cost_estimate=cost(6 * rows * rank * columns, (4 * n_tensor + 2) * rows * columns),
     )(table, upper, lower, *shrinks, *buffers)
 
 
-def late_kernel(ks, n_tensor, rank, layout, table, *refs):
+def late_kernel(ks, n_tensor, rank, table, *refs):
     rest_ref, shrinks, refs = refs[0], refs[1 : 1 + n_tensor], refs[1 + n_tensor :]
-    buffers, (_, o_ref, up, out, sems) = refs[:-5], refs[-5:]
-    views = views_of(buffers, stages_of_all(ks), layout, rank)
+    up, _, o_ref, out, sems = refs
     stores = []
     for i, k in enumerate(ks):
         share = shrinks[0][i]
         for r in shrinks[1:]:
             share = share + r[i]
         for j in range(MOST):
-            fetch_up(up, i * MOST + j, table, k, j, views, rank)
             start, used, _ = segment_of(table, k, j)
             lora = up_product(share, j, up[i * MOST + j], rank)
             out[i, j] = (rest_ref[i, j] + adapter_scale * lora).astype(jnp.bfloat16)
@@ -558,25 +563,24 @@
         pl.when(used)(store.wait)
 
 
-def late(ks, n_tensor, table, rest, shrinks, buffers, value, layout, rank):
+def late(ks, n_tensor, table, rest, shrinks, up, value, rank):
     rows, columns = value.shape
     return pl.pallas_call(
-        functools.partial(late_kernel, ks, n_tensor, rank, layout),
-        in_specs=[SMEM] + [VMEM] * (1 + len(shrinks) + len(buffers)) + [ANY],
+        functools.partial(late_kernel, ks, n_tensor, rank),
+        in_specs=[SMEM] + [VMEM] * (2 + len(shrinks)) + [ANY],
         out_specs=ANY,
         out_shape=jax.ShapeDtypeStruct((rows, columns), jnp.bfloat16),
         scratch_shapes=[
-            pltpu.VMEM((LATE * MOST, 2 * rank, columns), jnp.bfloat16),
             pltpu.VMEM((LATE, MOST, SEGMENT_ROWS, columns), jnp.bfloat16),
             pltpu.SemaphoreType.DMA((LATE, MOST)),
         ],
-        input_output_aliases={2 + len(shrinks) + len(buffers): 0},
+        input_output_aliases={3 + len(shrinks): 0},
         compiler_params=params(8),
         cost_estimate=cost(
             6 * LATE * MOST * SEGMENT_ROWS * rank * columns,
             8 * LATE * MOST * SEGMENT_ROWS * columns,
         ),
-    )(table, rest, *shrinks, *buffers, value)
+    )(table, rest, *shrinks, up, value)
 
 
 def after(array, *others):
@@ -668,18 +672,18 @@
         swapped = [swap_cores(after(c, *ahead)) for c in came] if stage > 1 else []
         buffers.append([*came, *swapped])
     add_shrink(before)
-    value, remaining = early(
+    buffers.append([*held, *[swap_cores(h) for h in held]])
+    value, remaining, factors = early(
         n_adapter,
         n_tensor,
         table,
         upper,
         lower,
         shrinks,
-        buffers_of(range(last - 1)),
+        buffers_of(range(n_adapter)),
         layout,
         rank,
     )
-    buffers.append([*held, *[swap_cores(h) for h in held]])
     ks = (last - 1, last)
     add_shrink(shrink(ks, after(kept, *held)))
     return late(
@@ -688,9 +692,8 @@
         table,
         remaining,
         shrinks[-n_tensor:],
-        buffers_of(stages_of_all(ks)),
+        factors,
         value,
-        layout,
         rank,
     )
 

time: 63.3 us -> 62.6 us (0.989)
  Pallas kernels: 35.9 us -> 34.6 us
    pallas_call x1, Pallas kernels: 2.32 us -> 1.62 us  [late(): pl.pallas_call(functools.partial(late_kernel, ks, n_tensor, rank), in_spe...]
where the time goes in v19:
time: 62.6 us; the launch traced here: 62.3 us
  Pallas kernels  34.6 us (55%)
  starting transfers between devices  21.6 us (35%)
  waiting for transfers between devices  5.8 us (9%)
    ppermute x6, starting transfers between devices, along_line(): return lax.ppermute(array, ('adapter', 'dp'), up + down)  15 us
    pallas_call x2, Pallas kernels, sent_call(): pl.pallas_call(functools.partial(sent_kernel, first, sizes, step, n_tenso...  10.3 us
    pallas_call x1, Pallas kernels, lower_call(): pl.pallas_call(functools.partial(lower_kernel, per_device, rank), in_spec...  7.12 us
    pallas_call x1, Pallas kernels, upper_call(): pl.pallas_call(functools.partial(upper_kernel, n_adapter), in_specs=[SMEM...  5.94 us
    ppermute x4, starting transfers between devices, swap_tensor(): return lax.ppermute(array, 'tensor', pairs)  5.33 us
    pallas_call x2, Pallas kernels, shrink_call(): pl.pallas_call(functools.partial(shrink_kernel, ks, rank, at, layout), in...  4.18 us
    ppermute x5, waiting for transfers between devices, swap_cores(): return lax.ppermute(array, 'dp', [(0, 1), (1, 0)])  2.89 us
    pallas_call x1, Pallas kernels, early(): pl.pallas_call(functools.partial(early_kernel, n_adapter, n_tensor, rank,...  2.27 us
  transfers between devices with their start and end apart: 15, of which 4 were waited for; matrix products, arithmetic and copies ran while one was open for 0% of the time, Pallas kernels for 51%

profile of v19, /device:TPU:16, one launch (start us, length us, event | category | flops | bytes accessed | tf_op | source)
XLA Modules:
  0.0 62.3 jit_solution(1361690877058792318)
XLA Ops:
  0.0 1.3 %shard_map.65 = (bf16[64,4608]{1,0:T(8,128)(2,1)S(1)}, bf16[64,4608]{1,0:T(8,128)(2,1)S(1)}) custom-call(bf16[128,4096]{1,0:T(8,128)(2,1)} %bitcast.4, bf16[128,1024]{1,0:T(8,128)(2,1)} %bitcast.5), custom_call_target="tpu_custom_call" | custom-call | bytes 2359296 | tf_op jit(solution)/shard_map/pallas_call | solution.py:91
  1.3 3.5 %collective-permute-start = (bf16[64,4608]{1,0:T(8,128)(2,1)S(1)}, bf16[64,4608]{1,0:T(8,128)(2,1)S(1)}, u32[]{:S(2)}, u32[]{:S(2)}) collective-permute-start(bf16[64,4608]{1,0:T(8,128)(2,1)S(1)} %get-tuple-element.28.refs_0_.refs_4_), channel_id=1, source_target_pairs={{0,4},{4,8},{8,12},{5,1},{9,5},{13,9},{2,6},{6,10},{10,14},{7,3},{... | collective-permute-start | bytes 1769480 | tf_op jit(solution)/shard_map/ppermute | solution.py:606
  4.8 1.9 %collective-permute-start.2 = (bf16[64,4608]{1,0:T(8,128)(2,1)S(1)}, bf16[64,4608]{1,0:T(8,128)(2,1)S(1)}, u32[]{:S(2)}, u32[]{:S(2)}) collective-permute-start(bf16[64,4608]{1,0:T(8,128)(2,1)S(1)} %get-tuple-element.30.refs_1_.refs_5_), channel_id=1, source_target_pairs={{0,4},{4,8},{8,12},{5,1},{9,5},{13,9},{2,6},{6,10},{10,14},{7,3},{... | collective-permute-start | bytes 1769480 | tf_op jit(solution)/shard_map/ppermute | solution.py:606
  6.7 3.6 %shard_map.66 = s32[168,512]{1,0:T(8,128)S(1)} custom-call(bf16[1024,4096]{1,0:T(8,128)(2,1)} %x_ref.6, bf16[4096,1024]{1,0:T(8,128)(2,1)} %w_ref.7), custom_call_target="tpu_custom_call" | custom-call | flops 1073741824 | bytes 6815744 | tf_op jit(solution)/shard_map/pallas_call | solution.py:265
  10.3 1.6 %collective-permute-start.4 = (s32[168,512]{1,0:T(8,128)S(1)}, s32[168,512]{1,0:T(8,128)S(1)}, u32[]{:S(2)}, u32[]{:S(2)}) collective-permute-start(s32[168,512]{1,0:T(8,128)S(1)} %shard_map.66), channel_id=1, source_target_pairs={{0,2},{2,0},{1,3},{3,1},{4,6},{6,4},{5,7},{7,5},{8,10},{10,8},{9,1... | collective-permute-start | bytes 1032200 | tf_op jit(solution)/shard_map/ppermute | solution.py:601
  11.9 1.4 %shard_map.64.table = s32[32]{0:T(128)} custom-call(s32[1024]{0:T(1024)} %ids.1, s32[8]{0:T(128)} %slots.1), custom_call_target="tpu_custom_call" | custom-call | bytes 4096 | tf_op jit(solution)/shard_map/pallas_call | solution.py:123
  13.3 0.0 copy-start
  13.4 0.0 collective-permute-done.refs_2_.refs_1_.refs_6_.refs_0_
  13.4 3.2 %collective-permute-start.1 = (bf16[64,4608]{1,0:T(8,128)(2,1)S(1)}, bf16[64,4608]{1,0:T(8,128)(2,1)S(1)}, u32[]{:S(2)}, u32[]{:S(2)}) collective-permute-start(bf16[64,4608]{1,0:T(8,128)(2,1)S(1)} %collective-permute-done.refs_2_.refs_1_.refs_6_.refs_0_), channel_id=1, source_target_pairs={{4,8},{8,12},{5,1},{9,5},{6,10},{10,14},{7,3},{11,7},{20,24},{24,2... | collective-permute-start | bytes 1769480 | tf_op jit(solution)/shard_map/ppermute | solution.py:606
  16.5 6.7 %shard_map.67 = s32[488,512]{1,0:T(8,128)S(1)} custom-call(bf16[1024,4096]{1,0:T(8,128)(2,1)} %x_ref.6, bf16[4096,1024]{1,0:T(8,128)(2,1)} %w_ref.7), custom_call_target="tpu_custom_call" | custom-call | flops 3221225472 | bytes 12058624 | tf_op jit(solution)/shard_map/pallas_call | solution.py:265
  23.2 0.0 collective-permute-done.2.refs_3_.refs_2_.refs_7_.refs_1_
  23.2 0.0 collective-permute-done.4.refs_4_
  23.2 1.6 %collective-permute-start.5 = (s32[488,512]{1,0:T(8,128)S(1)}, s32[488,512]{1,0:T(8,128)S(1)}, u32[]{:S(2)}, u32[]{:S(2)}) collective-permute-start(s32[488,512]{1,0:T(8,128)S(1)} %shard_map.67), channel_id=1, source_target_pairs={{0,2},{2,0},{1,3},{3,1},{4,6},{6,4},{5,7},{7,5},{8,10},{10,8},{9,1... | collective-permute-start | bytes 2998280 | tf_op jit(solution)/shard_map/ppermute | solution.py:601
  24.8 1.9 %collective-permute-start.6 = (bf16[64,4608]{1,0:T(8,128)(2,1)S(1)}, bf16[64,4608]{1,0:T(8,128)(2,1)S(1)}, u32[]{:S(2)}, u32[]{:S(2)}) collective-permute-start(bf16[64,4608]{1,0:T(8,128)(2,1)S(1)} %collective-permute-done.2.refs_3_.refs_2_.refs_7_.refs_1_), channel_id=1, source_target_pairs={{4,8},{8,12},{5,1},{9,5},{6,10},{10,14},{7,3},{11,7},{20,24},{24,2... | collective-permute-start | bytes 1769480 | tf_op jit(solution)/shard_map/ppermute | solution.py:606
  26.7 0.0 collective-permute-done.1.refs_9_.refs_3_
  26.7 2.4 %collective-permute-start.3 = (bf16[64,4608]{1,0:T(8,128)(2,1)S(1)}, bf16[64,4608]{1,0:T(8,128)(2,1)S(1)}, u32[]{:S(2)}, u32[]{:S(2)}) collective-permute-start(bf16[64,4608]{1,0:T(8,128)(2,1)S(1)} %collective-permute-done.1.refs_9_.refs_3_), channel_id=1, source_target_pairs={{8,12},{5,1},{10,14},{7,3},{24,28},{21,17},{26,30},{23,19}} | collective-permute-start | bytes 1769480 | tf_op jit(solution)/shard_map/ppermute | solution.py:606
  29.2 0.0 copy-done
  29.2 5.9 %shard_map.68 = (f32[384,512]{1,0:T(8,128)S(1)}, bf16[3,2,128,4096]{3,2,1,0:T(8,128)(2,1)S(1)}) custom-call(s32[32]{0:T(128)S(1)} %copy-done, bf16[1024,4096]{1,0:T(8,128)(2,1)} %x_ref.6, bf16[4096,1024]{1,0:T(8,128)(2,1)} %w_ref.7), custom_call_target="tpu_custom_call" | custom-call | flops 1610612736 | bytes 12582912 | tf_op jit(solution)/shard_map/pallas_call | solution.py:360
  35.1 1.4 %collective-permute-done.6.refs_10_.refs_4_ = bf16[64,4608]{1,0:T(8,128)(2,1)S(1)} collective-permute-done((bf16[64,4608]{1,0:T(8,128)(2,1)S(1)}, bf16[64,4608]{1,0:T(8,128)(2,1)S(1)}, u32[]{:S(2)}, u32[]{:S(2)}) %collective-permute-start.6) | collective-permute-done | bytes 589856 | tf_op jit(solution)/shard_map/ppermute | solution.py:606
  36.6 2.1 %collective-permute-start.7 = (bf16[64,4608]{1,0:T(8,128)(2,1)S(1)}, bf16[64,4608]{1,0:T(8,128)(2,1)S(1)}, u32[]{:S(2)}, u32[]{:S(2)}) collective-permute-start(bf16[64,4608]{1,0:T(8,128)(2,1)S(1)} %collective-permute-done.6.refs_10_.refs_4_), channel_id=1, source_target_pairs={{8,12},{5,1},{10,14},{7,3},{24,28},{21,17},{26,30},{23,19}} | collective-permute-start | bytes 1769480 | tf_op jit(solution)/shard_map/ppermute | solution.py:606
  38.7 7.1 %shard_map.70 = (f32[640,512]{1,0:T(8,128)S(1)}, f32[1,128,128]{2,1,0:T(8,128)S(1)}, bf16[128,4608]{1,0:T(8,128)(2,1)S(1)}) custom-call(s32[32]{0:T(128)S(1)} %copy-done, bf16[1024,4096]{1,0:T(8,128)(2,1)} %x_ref.6, bf16[4096,1024]{1,0:T(8,128)(2,1)} %w_ref.7, bf16[64,4608]{1,0:T(8,128)(2,1)S(1)} %get-tuple-element.28.refs_0_.refs_4_, ...), custom_call_target="tpu_custom_call" | custom-call | bytes 2097152 | tf_op jit(solution)/shard_map/pallas_call | solution.py:404
  45.8 0.1 collective-permute-start.10
  45.9 0.5 collective-permute-start.11
  46.4 0.0 collective-permute-done.3.refs_13_.refs_7_
  46.4 0.1 collective-permute-start.8
  46.5 0.0 collective-permute-done.5.refs_0_
  46.5 0.2 shard_map.69.refs_0_
  46.7 0.0 collective-permute-done.7.refs_14_.refs_8_
  46.8 0.5 collective-permute-start.12
  47.2 0.1 collective-permute-start.13
  47.3 0.2 shard_map.71.refs_1_
  47.6 2.9 %collective-permute-done.8.refs_3_.refs_8_.refs_2_ = bf16[128,4608]{1,0:T(8,128)(2,1)S(1)} collective-permute-done((bf16[128,4608]{1,0:T(8,128)(2,1)S(1)}, bf16[128,4608]{1,0:T(8,128)(2,1)S(1)}, u32[]{:S(2)}, u32[]{:S(2)}) %collective-permute-start.8) | collective-permute-done | bytes 1179680 | tf_op jit(solution)/shard_map/ppermute | solution.py:609
  50.4 1.5 %shard_map.72.refs_2_ = f32[2,128,128]{2,1,0:T(8,128)S(1)} custom-call(s32[32]{0:T(128)S(1)} %copy-done, bf16[3,2,128,4096]{3,2,1,0:T(8,128)(2,1)S(1)} %get-tuple-element.48.kept_ref, f32[1,128,128]{2,1,0:T(8,128)S(1)} %get-tuple-element.43.refs_0_, bf16[64,4608]{1,0:T(8,128)(2,1)S(1)} %collective-permute-done.refs_2_.refs_1_.refs_6_.refs_0_, ...), custom_call_target="tpu_custom_call" | custom-call | flops 536870912 | bytes 2097152 | tf_op jit(solution)/shard_map/pallas_call | solution.py:437
  52.0 0.5 collective-permute-start.9
  52.5 0.0 collective-permute-done.10.refs_11_.refs_5_
  52.5 0.0 collective-permute-done.11.refs_12_.refs_6_
  52.5 0.0 collective-permute-done.12.refs_15_.refs_9_
  52.6 0.0 collective-permute-done.13.refs_16_.refs_10_
  52.6 2.6 %shard_map.74.refs_1_ = f32[2,128,128]{2,1,0:T(8,128)S(1)} custom-call(s32[32]{0:T(128)S(1)} %copy-done, bf16[3,2,128,4096]{3,2,1,0:T(8,128)(2,1)S(1)} %get-tuple-element.48.kept_ref, bf16[64,4608]{1,0:T(8,128)(2,1)S(1)} %collective-permute-done.refs_2_.refs_1_.refs_6_.refs_0_, bf16[64,4608]{1,0:T(8,128)(2,1)S(1)} %collective-permute-done.2.refs_3_.refs_2_.refs_7_.refs_1_, ...), custom_call_target="tpu_custom_call" | custom-call | flops 1073741824 | bytes 4194304 | tf_op jit(solution)/shard_map/pallas_call | solution.py:437
  55.2 1.6 %collective-permute-start.14 = (f32[2,128,128]{2,1,0:T(8,128)S(1)}, f32[2,128,128]{2,1,0:T(8,128)S(1)}, u32[]{:S(2)}, u32[]{:S(2)}) collective-permute-start(f32[2,128,128]{2,1,0:T(8,128)S(1)} %shard_map.74.refs_1_), channel_id=1, source_target_pairs={{0,2},{2,0},{1,3},{3,1},{4,6},{6,4},{5,7},{7,5},{8,10},{10,8},{9,1... | collective-permute-start | bytes 393224 | tf_op jit(solution)/shard_map/ppermute | solution.py:601
  56.8 0.8 %collective-permute-done.9.refs_3_ = f32[2,128,128]{2,1,0:T(8,128)S(1)} collective-permute-done((f32[2,128,128]{2,1,0:T(8,128)S(1)}, f32[2,128,128]{2,1,0:T(8,128)S(1)}, u32[]{:S(2)}, u32[]{:S(2)}) %collective-permute-start.9) | collective-permute-done | bytes 131104 | tf_op jit(solution)/shard_map/ppermute | solution.py:601
  57.6 2.3 %shard_map.73 = (bf16[1024,512]{1,0:T(8,128)(2,1)}, f32[2,2,128,512]{3,2,1,0:T(8,128)S(1)}, bf16[4,128,512]{2,1,0:T(8,128)(2,1)S(1)}) custom-call(s32[32]{0:T(128)S(1)} %copy-done, f32[384,512]{1,0:T(8,128)S(1)} %shard_map.69.refs_0_, f32[640,512]{1,0:T(8,128)S(1)} %shard_map.71.refs_1_, f32[2,128,128]{2,1,0:T(8,128)S(1)} %shard_map.72.refs_2_, ...), custom_call_target="tpu_custom_call" | custom-call | flops 201326592 | bytes 5242880 | tf_op jit(solution)/shard_map/pallas_call | solution.py:525
  59.8 0.7 %collective-permute-done.14.refs_2_ = f32[2,128,128]{2,1,0:T(8,128)S(1)} collective-permute-done((f32[2,128,128]{2,1,0:T(8,128)S(1)}, f32[2,128,128]{2,1,0:T(8,128)S(1)}, u32[]{:S(2)}, u32[]{:S(2)}) %collective-permute-start.14) | collective-permute-done | bytes 131104 | tf_op jit(solution)/shard_map/ppermute | solution.py:601
  60.5 1.6 %shard_map.75 = bf16[1024,512]{1,0:T(8,128)(2,1)} custom-call(s32[32]{0:T(128)S(1)} %copy-done, f32[2,2,128,512]{3,2,1,0:T(8,128)S(1)} %get-tuple-element.47.refs_0_, f32[2,128,128]{2,1,0:T(8,128)S(1)} %shard_map.74.refs_1_, f32[2,128,128]{2,1,0:T(8,128)S(1)} %collective-permute-done.14.refs_2_, ...), custom_call_target="tpu_custom_call", output_to_operand_aliasing={{}: (5, {})} | custom-call | flops 100663296 | bytes 2097152 | tf_op jit(solution)/shard_map/pallas_call | solution.py:568
Async XLA Ops:
  1.3 12.1 %collective-permute-start = (bf16[64,4608]{1,0:T(8,128)(2,1)S(1)}, bf16[64,4608]{1,0:T(8,128)(2,1)S(1)}, u32[]{:S(2)}, u32[]{:S(2)}) collective-permute-start(bf16[64,4608]{1,0:T(8,128)(2,1)S(1)} %get-tuple-element.28.refs_0_.refs_4_), channel_id=1, source_target_pairs={{0,4},{4,8},{8,12},{5,1},{9,5},{13,9},{2,6},{6,10},{10,14},{7,3},{... | collective-permute-start | bytes 1769480 | tf_op jit(solution)/shard_map/ppermute | solution.py:606
  4.8 18.5 %collective-permute-start.2 = (bf16[64,4608]{1,0:T(8,128)(2,1)S(1)}, bf16[64,4608]{1,0:T(8,128)(2,1)S(1)}, u32[]{:S(2)}, u32[]{:S(2)}) collective-permute-start(bf16[64,4608]{1,0:T(8,128)(2,1)S(1)} %get-tuple-element.30.refs_1_.refs_5_), channel_id=1, source_target_pairs={{0,4},{4,8},{8,12},{5,1},{9,5},{13,9},{2,6},{6,10},{10,14},{7,3},{... | collective-permute-start | bytes 1769480 | tf_op jit(solution)/shard_map/ppermute | solution.py:606
  10.3 12.9 %collective-permute-start.4 = (s32[168,512]{1,0:T(8,128)S(1)}, s32[168,512]{1,0:T(8,128)S(1)}, u32[]{:S(2)}, u32[]{:S(2)}) collective-permute-start(s32[168,512]{1,0:T(8,128)S(1)} %shard_map.66), channel_id=1, source_target_pairs={{0,2},{2,0},{1,3},{3,1},{4,6},{6,4},{5,7},{7,5},{8,10},{10,8},{9,1... | collective-permute-start | bytes 1032200 | tf_op jit(solution)/shard_map/ppermute | solution.py:601
  13.3 15.9 %copy-start = (s32[32]{0:T(128)S(1)}, s32[32]{0:T(128)}, u32[]{:S(2)}) copy-start(s32[32]{0:T(128)} %shard_map.64.table) | copy-start | bytes 388
  13.4 13.4 %collective-permute-start.1 = (bf16[64,4608]{1,0:T(8,128)(2,1)S(1)}, bf16[64,4608]{1,0:T(8,128)(2,1)S(1)}, u32[]{:S(2)}, u32[]{:S(2)}) collective-permute-start(bf16[64,4608]{1,0:T(8,128)(2,1)S(1)} %collective-permute-done.refs_2_.refs_1_.refs_6_.refs_0_), channel_id=1, source_target_pairs={{4,8},{8,12},{5,1},{9,5},{6,10},{10,14},{7,3},{11,7},{20,24},{24,2... | collective-permute-start | bytes 1769480 | tf_op jit(solution)/shard_map/ppermute | solution.py:606
  23.2 23.3 %collective-permute-start.5 = (s32[488,512]{1,0:T(8,128)S(1)}, s32[488,512]{1,0:T(8,128)S(1)}, u32[]{:S(2)}, u32[]{:S(2)}) collective-permute-start(s32[488,512]{1,0:T(8,128)S(1)} %shard_map.67), channel_id=1, source_target_pairs={{0,2},{2,0},{1,3},{3,1},{4,6},{6,4},{5,7},{7,5},{8,10},{10,8},{9,1... | collective-permute-start | bytes 2998280 | tf_op jit(solution)/shard_map/ppermute | solution.py:601
  24.8 11.8 %collective-permute-start.6 = (bf16[64,4608]{1,0:T(8,128)(2,1)S(1)}, bf16[64,4608]{1,0:T(8,128)(2,1)S(1)}, u32[]{:S(2)}, u32[]{:S(2)}) collective-permute-start(bf16[64,4608]{1,0:T(8,128)(2,1)S(1)} %collective-permute-done.2.refs_3_.refs_2_.refs_7_.refs_1_), channel_id=1, source_target_pairs={{4,8},{8,12},{5,1},{9,5},{6,10},{10,14},{7,3},{11,7},{20,24},{24,2... | collective-permute-start | bytes 1769480 | tf_op jit(solution)/shard_map/ppermute | solution.py:606
  26.7 19.7 %collective-permute-start.3 = (bf16[64,4608]{1,0:T(8,128)(2,1)S(1)}, bf16[64,4608]{1,0:T(8,128)(2,1)S(1)}, u32[]{:S(2)}, u32[]{:S(2)}) collective-permute-start(bf16[64,4608]{1,0:T(8,128)(2,1)S(1)} %collective-permute-done.1.refs_9_.refs_3_), channel_id=1, source_target_pairs={{8,12},{5,1},{10,14},{7,3},{24,28},{21,17},{26,30},{23,19}} | collective-permute-start | bytes 1769480 | tf_op jit(solution)/shard_map/ppermute | solution.py:606
  36.6 10.2 %collective-permute-start.7 = (bf16[64,4608]{1,0:T(8,128)(2,1)S(1)}, bf16[64,4608]{1,0:T(8,128)(2,1)S(1)}, u32[]{:S(2)}, u32[]{:S(2)}) collective-permute-start(bf16[64,4608]{1,0:T(8,128)(2,1)S(1)} %collective-permute-done.6.refs_10_.refs_4_), channel_id=1, source_target_pairs={{8,12},{5,1},{10,14},{7,3},{24,28},{21,17},{26,30},{23,19}} | collective-permute-start | bytes 1769480 | tf_op jit(solution)/shard_map/ppermute | solution.py:606
  45.8 6.7 %collective-permute-start.10 = (bf16[64,4608]{1,0:T(8,128)(2,1)S(1)}, bf16[64,4608]{1,0:T(8,128)(2,1)S(1)}, u32[]{:S(2)}, u32[]{:S(2)}) collective-permute-start(bf16[64,4608]{1,0:T(8,128)(2,1)S(1)} %collective-permute-done.1.refs_9_.refs_3_), channel_id=1, source_target_pairs={{0,1},{1,0},{2,3},{3,2},{4,5},{5,4},{6,7},{7,6},{8,9},{9,8},{10,11... | collective-permute-start | bytes 1769480 | tf_op jit(solution)/shard_map/ppermute | solution.py:609
  45.9 6.6 %collective-permute-start.11 = (bf16[64,4608]{1,0:T(8,128)(2,1)S(1)}, bf16[64,4608]{1,0:T(8,128)(2,1)S(1)}, u32[]{:S(2)}, u32[]{:S(2)}) collective-permute-start(bf16[64,4608]{1,0:T(8,128)(2,1)S(1)} %collective-permute-done.6.refs_10_.refs_4_), channel_id=1, source_target_pairs={{0,1},{1,0},{2,3},{3,2},{4,5},{5,4},{6,7},{7,6},{8,9},{9,8},{10,11... | collective-permute-start | bytes 1769480 | tf_op jit(solution)/shard_map/ppermute | solution.py:609
  46.4 4.0 %collective-permute-start.8 = (bf16[128,4608]{1,0:T(8,128)(2,1)S(1)}, bf16[128,4608]{1,0:T(8,128)(2,1)S(1)}, u32[]{:S(2)}, u32[]{:S(2)}) collective-permute-start(bf16[128,4608]{1,0:T(8,128)(2,1)S(1)} %get-tuple-element.44), channel_id=1, source_target_pairs={{0,1},{1,0},{2,3},{3,2},{4,5},{5,4},{6,7},{7,6},{8,9},{9,8},{10,11... | collective-permute-start | bytes 3538952 | tf_op jit(solution)/shard_map/ppermute | solution.py:609
  46.8 5.8 %collective-permute-start.12 = (bf16[64,4608]{1,0:T(8,128)(2,1)S(1)}, bf16[64,4608]{1,0:T(8,128)(2,1)S(1)}, u32[]{:S(2)}, u32[]{:S(2)}) collective-permute-start(bf16[64,4608]{1,0:T(8,128)(2,1)S(1)} %collective-permute-done.3.refs_13_.refs_7_), channel_id=1, source_target_pairs={{0,1},{1,0},{2,3},{3,2},{4,5},{5,4},{6,7},{7,6},{8,9},{9,8},{10,11... | collective-permute-start | bytes 1769480 | tf_op jit(solution)/shard_map/ppermute | solution.py:609
  47.2 5.3 %collective-permute-start.13 = (bf16[64,4608]{1,0:T(8,128)(2,1)S(1)}, bf16[64,4608]{1,0:T(8,128)(2,1)S(1)}, u32[]{:S(2)}, u32[]{:S(2)}) collective-permute-start(bf16[64,4608]{1,0:T(8,128)(2,1)S(1)} %collective-permute-done.7.refs_14_.refs_8_), channel_id=1, source_target_pairs={{0,1},{1,0},{2,3},{3,2},{4,5},{5,4},{6,7},{7,6},{8,9},{9,8},{10,11... | collective-permute-start | bytes 1769480 | tf_op jit(solution)/shard_map/ppermute | solution.py:609
  52.0 5.6 %collective-permute-start.9 = (f32[2,128,128]{2,1,0:T(8,128)S(1)}, f32[2,128,128]{2,1,0:T(8,128)S(1)}, u32[]{:S(2)}, u32[]{:S(2)}) collective-permute-start(f32[2,128,128]{2,1,0:T(8,128)S(1)} %shard_map.72.refs_2_), channel_id=1, source_target_pairs={{0,2},{2,0},{1,3},{3,1},{4,6},{6,4},{5,7},{7,5},{8,10},{10,8},{9,1... | collective-permute-start | bytes 393224 | tf_op jit(solution)/shard_map/ppermute | solution.py:601
  55.2 5.3 %collective-permute-start.14 = (f32[2,128,128]{2,1,0:T(8,128)S(1)}, f32[2,128,128]{2,1,0:T(8,128)S(1)}, u32[]{:S(2)}, u32[]{:S(2)}) collective-permute-start(f32[2,128,128]{2,1,0:T(8,128)S(1)} %shard_map.74.refs_1_), channel_id=1, source_target_pairs={{0,2},{2,0},{1,3},{3,1},{4,6},{6,4},{5,7},{7,5},{8,10},{10,8},{9,1... | collective-permute-start | bytes 393224 | tf_op jit(solution)/shard_map/ppermute | solution.py:601

commit v20 on v19

--- a/solution.py
+++ b/solution.py
@@ -64,7 +64,7 @@
     return start, seg >= 0, table[k * ENTRIES + 2 + 2 * j]
 
 
-def message_kernel(down_ref, up_ref, *refs):
+def message_kernel(adapter, down_ref, up_ref, *refs):
     outs, sems = refs[:-1], refs[-1]
     rank = outs[0].shape[0]
     width = down_ref.shape[1]
@@ -72,7 +72,7 @@
     start = pl.multiple_of(lax.axis_index("tensor") * columns, columns)
     copies = []
     for i, out in enumerate(outs):
-        rows = pl.ds(i * rank, rank)
+        rows = pl.ds((adapter + i) * rank, rank)
         copies += [
             pltpu.make_async_copy(down_ref.at[rows, :], out.at[:, pl.ds(0, width)], sems.at[0, i]),
             pltpu.make_async_copy(
@@ -85,18 +85,18 @@
         copy.wait()
 
 
-def message_call(down, up, columns, per_device):
+def message_call(down, up, columns, per_device, adapter):
     rows, width = down.shape
     shape = jax.ShapeDtypeStruct((rows // per_device, width + columns), jnp.bfloat16)
     return pl.pallas_call(
-        message_kernel,
+        functools.partial(message_kernel, adapter),
         in_specs=[HBM, HBM],
-        out_specs=[VMEM] * per_device,
-        out_shape=[shape] * per_device,
-        scratch_shapes=[pltpu.SemaphoreType.DMA((2, per_device))],
+        out_specs=[VMEM],
+        out_shape=[shape],
+        scratch_shapes=[pltpu.SemaphoreType.DMA((2, 1))],
         compiler_params=params(8),
         cost_estimate=cost(0, 4 * rows * (width + columns)),
-    )(down, up)
+    )(down, up)[0]
 
 
 def table_kernel(n_adapter, per_device, ids, slots, table):
@@ -613,7 +613,7 @@
     tokens, value_weight, down, up = (
         pltpu.with_memory_space_constraint(a, pltpu.HBM) for a in (tokens, value_weight, down, up)
     )
-    messages = message_call(down, up, columns, per_device)
+    messages = [message_call(down, up, columns, per_device, i) for i in range(per_device)]
     table = table_call(row_adapter_index, adapter_slot_of, n_adapter, per_device)
     last = n_adapter - 1
     buffers, shrinks = [list(messages)], []

time: 62.6 us -> 62.4 us (level)
  Pallas kernels: 34.6 us -> 36 us
  starting transfers between devices: 21.6 us -> 20.5 us
    ppermute x6, starting transfers between devices: 15 us -> 14 us  [along_line(): return lax.ppermute(array, ('adapter', 'dp'), up + down)]
    pallas_call x1 -> x2, Pallas kernels: 1.25 us -> 2.12 us  [message_call(): pl.pallas_call(functools.partial(message_kernel, adapter), in_specs=[HBM,...]
  transfers between devices with their start and end apart: 15 -> 15, of which waited for: 4 -> 4; matrix products, arithmetic and copies ran while one was open for 0% -> 0% of each run, Pallas kernels for 51% -> 54%
where the time goes in v20:
time: 62.4 us; the launch traced here: 62.1 us
  Pallas kernels  36 us (58%)
  starting transfers between devices  20.5 us (33%)
  waiting for transfers between devices  5.21 us (8%)
    ppermute x6, starting transfers between devices, along_line(): return lax.ppermute(array, ('adapter', 'dp'), up + down)  14 us
    pallas_call x2, Pallas kernels, sent_call(): pl.pallas_call(functools.partial(sent_kernel, first, sizes, step, n_tenso...  10.3 us
    pallas_call x1, Pallas kernels, lower_call(): pl.pallas_call(functools.partial(lower_kernel, per_device, rank), in_spec...  7.12 us
    pallas_call x1, Pallas kernels, upper_call(): pl.pallas_call(functools.partial(upper_kernel, n_adapter), in_specs=[SMEM...  6.53 us
    ppermute x4, starting transfers between devices, swap_tensor(): return lax.ppermute(array, 'tensor', pairs)  5.33 us
    pallas_call x2, Pallas kernels, shrink_call(): pl.pallas_call(functools.partial(shrink_kernel, ks, rank, at, layout), in...  4.2 us
    ppermute x5, waiting for transfers between devices, swap_cores(): return lax.ppermute(array, 'dp', [(0, 1), (1, 0)])  2.89 us
    pallas_call x1, Pallas kernels, early(): pl.pallas_call(functools.partial(early_kernel, n_adapter, n_tensor, rank,...  2.27 us
  transfers between devices with their start and end apart: 15, of which 4 were waited for; matrix products, arithmetic and copies ran while one was open for 0% of the time, Pallas kernels for 54%

profile of v20, /device:TPU:16, one launch (start us, length us, event | category | flops | bytes accessed | tf_op | source)
XLA Modules:
  0.0 62.1 jit_solution(14947246879692516111)
XLA Ops:
  0.0 1.1 %shard_map.65.refs_0_.refs_4_ = bf16[64,4608]{1,0:T(8,128)(2,1)S(1)} custom-call(bf16[128,4096]{1,0:T(8,128)(2,1)} %bitcast.4, bf16[128,1024]{1,0:T(8,128)(2,1)} %bitcast.6), custom_call_target="tpu_custom_call" | custom-call | bytes 2359296 | tf_op jit(solution)/shard_map/pallas_call | solution.py:91
  1.1 3.5 %collective-permute-start = (bf16[64,4608]{1,0:T(8,128)(2,1)S(1)}, bf16[64,4608]{1,0:T(8,128)(2,1)S(1)}, u32[]{:S(2)}, u32[]{:S(2)}) collective-permute-start(bf16[64,4608]{1,0:T(8,128)(2,1)S(1)} %shard_map.65.refs_0_.refs_4_), channel_id=1, source_target_pairs={{0,4},{4,8},{8,12},{5,1},{9,5},{13,9},{2,6},{6,10},{10,14},{7,3},{... | collective-permute-start | bytes 1769480 | tf_op jit(solution)/shard_map/ppermute | solution.py:606
  4.6 1.1 %shard_map.67.refs_1_.refs_5_ = bf16[64,4608]{1,0:T(8,128)(2,1)S(1)} custom-call(bf16[128,4096]{1,0:T(8,128)(2,1)} %bitcast.5, bf16[128,1024]{1,0:T(8,128)(2,1)} %bitcast.7), custom_call_target="tpu_custom_call" | custom-call | bytes 2359296 | tf_op jit(solution)/shard_map/pallas_call | solution.py:91
  5.6 1.9 %collective-permute-start.2 = (bf16[64,4608]{1,0:T(8,128)(2,1)S(1)}, bf16[64,4608]{1,0:T(8,128)(2,1)S(1)}, u32[]{:S(2)}, u32[]{:S(2)}) collective-permute-start(bf16[64,4608]{1,0:T(8,128)(2,1)S(1)} %shard_map.67.refs_1_.refs_5_), channel_id=1, source_target_pairs={{0,4},{4,8},{8,12},{5,1},{9,5},{13,9},{2,6},{6,10},{10,14},{7,3},{... | collective-permute-start | bytes 1769480 | tf_op jit(solution)/shard_map/ppermute | solution.py:606
  7.6 3.6 %shard_map.66 = s32[168,512]{1,0:T(8,128)S(1)} custom-call(bf16[1024,4096]{1,0:T(8,128)(2,1)} %x_ref.6, bf16[4096,1024]{1,0:T(8,128)(2,1)} %w_ref.7), custom_call_target="tpu_custom_call" | custom-call | flops 1073741824 | bytes 6815744 | tf_op jit(solution)/shard_map/pallas_call | solution.py:265
  11.2 1.6 %collective-permute-start.4 = (s32[168,512]{1,0:T(8,128)S(1)}, s32[168,512]{1,0:T(8,128)S(1)}, u32[]{:S(2)}, u32[]{:S(2)}) collective-permute-start(s32[168,512]{1,0:T(8,128)S(1)} %shard_map.66), channel_id=1, source_target_pairs={{0,2},{2,0},{1,3},{3,1},{4,6},{6,4},{5,7},{7,5},{8,10},{10,8},{9,1... | collective-permute-start | bytes 1032200 | tf_op jit(solution)/shard_map/ppermute | solution.py:601
  12.8 1.4 %shard_map.64.table = s32[32]{0:T(128)} custom-call(s32[1024]{0:T(1024)} %ids.1, s32[8]{0:T(128)} %slots.1), custom_call_target="tpu_custom_call" | custom-call | bytes 4096 | tf_op jit(solution)/shard_map/pallas_call | solution.py:123
  14.2 0.0 copy-start
  14.2 0.0 collective-permute-done.refs_2_.refs_1_.refs_6_.refs_0_
  14.2 2.1 %collective-permute-start.1 = (bf16[64,4608]{1,0:T(8,128)(2,1)S(1)}, bf16[64,4608]{1,0:T(8,128)(2,1)S(1)}, u32[]{:S(2)}, u32[]{:S(2)}) collective-permute-start(bf16[64,4608]{1,0:T(8,128)(2,1)S(1)} %collective-permute-done.refs_2_.refs_1_.refs_6_.refs_0_), channel_id=1, source_target_pairs={{4,8},{8,12},{5,1},{9,5},{6,10},{10,14},{7,3},{11,7},{20,24},{24,2... | collective-permute-start | bytes 1769480 | tf_op jit(solution)/shard_map/ppermute | solution.py:606
  16.3 6.7 %shard_map.68 = s32[488,512]{1,0:T(8,128)S(1)} custom-call(bf16[1024,4096]{1,0:T(8,128)(2,1)} %x_ref.6, bf16[4096,1024]{1,0:T(8,128)(2,1)} %w_ref.7), custom_call_target="tpu_custom_call" | custom-call | flops 3221225472 | bytes 12058624 | tf_op jit(solution)/shard_map/pallas_call | solution.py:265
  23.0 0.0 collective-permute-done.2.refs_3_.refs_2_.refs_7_.refs_1_
  23.0 0.0 collective-permute-done.4.refs_4_
  23.0 1.6 %collective-permute-start.5 = (s32[488,512]{1,0:T(8,128)S(1)}, s32[488,512]{1,0:T(8,128)S(1)}, u32[]{:S(2)}, u32[]{:S(2)}) collective-permute-start(s32[488,512]{1,0:T(8,128)S(1)} %shard_map.68), channel_id=1, source_target_pairs={{0,2},{2,0},{1,3},{3,1},{4,6},{6,4},{5,7},{7,5},{8,10},{10,8},{9,1... | collective-permute-start | bytes 2998280 | tf_op jit(solution)/shard_map/ppermute | solution.py:601
  24.6 1.9 %collective-permute-start.6 = (bf16[64,4608]{1,0:T(8,128)(2,1)S(1)}, bf16[64,4608]{1,0:T(8,128)(2,1)S(1)}, u32[]{:S(2)}, u32[]{:S(2)}) collective-permute-start(bf16[64,4608]{1,0:T(8,128)(2,1)S(1)} %collective-permute-done.2.refs_3_.refs_2_.refs_7_.refs_1_), channel_id=1, source_target_pairs={{4,8},{8,12},{5,1},{9,5},{6,10},{10,14},{7,3},{11,7},{20,24},{24,2... | collective-permute-start | bytes 1769480 | tf_op jit(solution)/shard_map/ppermute | solution.py:606
  26.5 0.0 collective-permute-done.1.refs_9_.refs_3_
  26.6 2.4 %collective-permute-start.3 = (bf16[64,4608]{1,0:T(8,128)(2,1)S(1)}, bf16[64,4608]{1,0:T(8,128)(2,1)S(1)}, u32[]{:S(2)}, u32[]{:S(2)}) collective-permute-start(bf16[64,4608]{1,0:T(8,128)(2,1)S(1)} %collective-permute-done.1.refs_9_.refs_3_), channel_id=1, source_target_pairs={{8,12},{5,1},{10,14},{7,3},{24,28},{21,17},{26,30},{23,19}} | collective-permute-start | bytes 1769480 | tf_op jit(solution)/shard_map/ppermute | solution.py:606
  29.0 0.0 copy-done
  29.0 6.5 %shard_map.69 = (f32[384,512]{1,0:T(8,128)S(1)}, bf16[3,2,128,4096]{3,2,1,0:T(8,128)(2,1)S(1)}) custom-call(s32[32]{0:T(128)S(1)} %copy-done, bf16[1024,4096]{1,0:T(8,128)(2,1)} %x_ref.6, bf16[4096,1024]{1,0:T(8,128)(2,1)} %w_ref.7), custom_call_target="tpu_custom_call" | custom-call | flops 1610612736 | bytes 12582912 | tf_op jit(solution)/shard_map/pallas_call | solution.py:360
  35.5 0.8 %collective-permute-done.6.refs_10_.refs_4_ = bf16[64,4608]{1,0:T(8,128)(2,1)S(1)} collective-permute-done((bf16[64,4608]{1,0:T(8,128)(2,1)S(1)}, bf16[64,4608]{1,0:T(8,128)(2,1)S(1)}, u32[]{:S(2)}, u32[]{:S(2)}) %collective-permute-start.6) | collective-permute-done | bytes 589856 | tf_op jit(solution)/shard_map/ppermute | solution.py:606
  36.4 2.1 %collective-permute-start.7 = (bf16[64,4608]{1,0:T(8,128)(2,1)S(1)}, bf16[64,4608]{1,0:T(8,128)(2,1)S(1)}, u32[]{:S(2)}, u32[]{:S(2)}) collective-permute-start(bf16[64,4608]{1,0:T(8,128)(2,1)S(1)} %collective-permute-done.6.refs_10_.refs_4_), channel_id=1, source_target_pairs={{8,12},{5,1},{10,14},{7,3},{24,28},{21,17},{26,30},{23,19}} | collective-permute-start | bytes 1769480 | tf_op jit(solution)/shard_map/ppermute | solution.py:606
  38.5 7.1 %shard_map.71 = (f32[640,512]{1,0:T(8,128)S(1)}, f32[1,128,128]{2,1,0:T(8,128)S(1)}, bf16[128,4608]{1,0:T(8,128)(2,1)S(1)}) custom-call(s32[32]{0:T(128)S(1)} %copy-done, bf16[1024,4096]{1,0:T(8,128)(2,1)} %x_ref.6, bf16[4096,1024]{1,0:T(8,128)(2,1)} %w_ref.7, bf16[64,4608]{1,0:T(8,128)(2,1)S(1)} %shard_map.65.refs_0_.refs_4_, ...), custom_call_target="tpu_custom_call" | custom-call | bytes 2097152 | tf_op jit(solution)/shard_map/pallas_call | solution.py:404
  45.7 0.1 collective-permute-start.10
  45.7 0.5 collective-permute-start.11
  46.2 0.0 collective-permute-done.3.refs_13_.refs_7_
  46.2 0.1 collective-permute-start.8
  46.3 0.0 collective-permute-done.5.refs_0_
  46.3 0.2 shard_map.70.refs_0_
  46.5 0.0 collective-permute-done.7.refs_14_.refs_8_
  46.6 0.5 collective-permute-start.12
  47.0 0.1 collective-permute-start.13
  47.1 0.2 shard_map.72.refs_1_
  47.4 2.9 %collective-permute-done.8.refs_3_.refs_8_.refs_2_ = bf16[128,4608]{1,0:T(8,128)(2,1)S(1)} collective-permute-done((bf16[128,4608]{1,0:T(8,128)(2,1)S(1)}, bf16[128,4608]{1,0:T(8,128)(2,1)S(1)}, u32[]{:S(2)}, u32[]{:S(2)}) %collective-permute-start.8) | collective-permute-done | bytes 1179680 | tf_op jit(solution)/shard_map/ppermute | solution.py:609
  50.3 1.5 %shard_map.73.refs_2_ = f32[2,128,128]{2,1,0:T(8,128)S(1)} custom-call(s32[32]{0:T(128)S(1)} %copy-done, bf16[3,2,128,4096]{3,2,1,0:T(8,128)(2,1)S(1)} %get-tuple-element.44.kept_ref, f32[1,128,128]{2,1,0:T(8,128)S(1)} %get-tuple-element.39.refs_0_, bf16[64,4608]{1,0:T(8,128)(2,1)S(1)} %collective-permute-done.refs_2_.refs_1_.refs_6_.refs_0_, ...), custom_call_target="tpu_custom_call" | custom-call | flops 536870912 | bytes 2097152 | tf_op jit(solution)/shard_map/pallas_call | solution.py:437
  51.8 0.5 collective-permute-start.9
  52.3 0.0 collective-permute-done.10.refs_11_.refs_5_
  52.3 0.0 collective-permute-done.11.refs_12_.refs_6_
  52.4 0.0 collective-permute-done.12.refs_15_.refs_9_
  52.4 0.0 collective-permute-done.13.refs_16_.refs_10_
  52.4 2.7 %shard_map.75.refs_1_ = f32[2,128,128]{2,1,0:T(8,128)S(1)} custom-call(s32[32]{0:T(128)S(1)} %copy-done, bf16[3,2,128,4096]{3,2,1,0:T(8,128)(2,1)S(1)} %get-tuple-element.44.kept_ref, bf16[64,4608]{1,0:T(8,128)(2,1)S(1)} %collective-permute-done.refs_2_.refs_1_.refs_6_.refs_0_, bf16[64,4608]{1,0:T(8,128)(2,1)S(1)} %collective-permute-done.2.refs_3_.refs_2_.refs_7_.refs_1_, ...), custom_call_target="tpu_custom_call" | custom-call | flops 1073741824 | bytes 4194304 | tf_op jit(solution)/shard_map/pallas_call | solution.py:437
  55.0 1.6 %collective-permute-start.14 = (f32[2,128,128]{2,1,0:T(8,128)S(1)}, f32[2,128,128]{2,1,0:T(8,128)S(1)}, u32[]{:S(2)}, u32[]{:S(2)}) collective-permute-start(f32[2,128,128]{2,1,0:T(8,128)S(1)} %shard_map.75.refs_1_), channel_id=1, source_target_pairs={{0,2},{2,0},{1,3},{3,1},{4,6},{6,4},{5,7},{7,5},{8,10},{10,8},{9,1... | collective-permute-start | bytes 393224 | tf_op jit(solution)/shard_map/ppermute | solution.py:601
  56.6 0.8 %collective-permute-done.9.refs_3_ = f32[2,128,128]{2,1,0:T(8,128)S(1)} collective-permute-done((f32[2,128,128]{2,1,0:T(8,128)S(1)}, f32[2,128,128]{2,1,0:T(8,128)S(1)}, u32[]{:S(2)}, u32[]{:S(2)}) %collective-permute-start.9) | collective-permute-done | bytes 131104 | tf_op jit(solution)/shard_map/ppermute | solution.py:601
  57.4 2.3 %shard_map.74 = (bf16[1024,512]{1,0:T(8,128)(2,1)}, f32[2,2,128,512]{3,2,1,0:T(8,128)S(1)}, bf16[4,128,512]{2,1,0:T(8,128)(2,1)S(1)}) custom-call(s32[32]{0:T(128)S(1)} %copy-done, f32[384,512]{1,0:T(8,128)S(1)} %shard_map.70.refs_0_, f32[640,512]{1,0:T(8,128)S(1)} %shard_map.72.refs_1_, f32[2,128,128]{2,1,0:T(8,128)S(1)} %shard_map.73.refs_2_, ...), custom_call_target="tpu_custom_call" | custom-call | flops 201326592 | bytes 5242880 | tf_op jit(solution)/shard_map/pallas_call | solution.py:525
  59.6 0.7 %collective-permute-done.14.refs_2_ = f32[2,128,128]{2,1,0:T(8,128)S(1)} collective-permute-done((f32[2,128,128]{2,1,0:T(8,128)S(1)}, f32[2,128,128]{2,1,0:T(8,128)S(1)}, u32[]{:S(2)}, u32[]{:S(2)}) %collective-permute-start.14) | collective-permute-done | bytes 131104 | tf_op jit(solution)/shard_map/ppermute | solution.py:601
  60.3 1.6 %shard_map.76 = bf16[1024,512]{1,0:T(8,128)(2,1)} custom-call(s32[32]{0:T(128)S(1)} %copy-done, f32[2,2,128,512]{3,2,1,0:T(8,128)S(1)} %get-tuple-element.43.refs_0_, f32[2,128,128]{2,1,0:T(8,128)S(1)} %shard_map.75.refs_1_, f32[2,128,128]{2,1,0:T(8,128)S(1)} %collective-permute-done.14.refs_2_, ...), custom_call_target="tpu_custom_call", output_to_operand_aliasing={{}: (5, {})} | custom-call | flops 100663296 | bytes 2097152 | tf_op jit(solution)/shard_map/pallas_call | solution.py:568
Async XLA Ops:
  1.1 13.2 %collective-permute-start = (bf16[64,4608]{1,0:T(8,128)(2,1)S(1)}, bf16[64,4608]{1,0:T(8,128)(2,1)S(1)}, u32[]{:S(2)}, u32[]{:S(2)}) collective-permute-start(bf16[64,4608]{1,0:T(8,128)(2,1)S(1)} %shard_map.65.refs_0_.refs_4_), channel_id=1, source_target_pairs={{0,4},{4,8},{8,12},{5,1},{9,5},{13,9},{2,6},{6,10},{10,14},{7,3},{... | collective-permute-start | bytes 1769480 | tf_op jit(solution)/shard_map/ppermute | solution.py:606
  5.6 17.4 %collective-permute-start.2 = (bf16[64,4608]{1,0:T(8,128)(2,1)S(1)}, bf16[64,4608]{1,0:T(8,128)(2,1)S(1)}, u32[]{:S(2)}, u32[]{:S(2)}) collective-permute-start(bf16[64,4608]{1,0:T(8,128)(2,1)S(1)} %shard_map.67.refs_1_.refs_5_), channel_id=1, source_target_pairs={{0,4},{4,8},{8,12},{5,1},{9,5},{13,9},{2,6},{6,10},{10,14},{7,3},{... | collective-permute-start | bytes 1769480 | tf_op jit(solution)/shard_map/ppermute | solution.py:606
  11.2 11.8 %collective-permute-start.4 = (s32[168,512]{1,0:T(8,128)S(1)}, s32[168,512]{1,0:T(8,128)S(1)}, u32[]{:S(2)}, u32[]{:S(2)}) collective-permute-start(s32[168,512]{1,0:T(8,128)S(1)} %shard_map.66), channel_id=1, source_target_pairs={{0,2},{2,0},{1,3},{3,1},{4,6},{6,4},{5,7},{7,5},{8,10},{10,8},{9,1... | collective-permute-start | bytes 1032200 | tf_op jit(solution)/shard_map/ppermute | solution.py:601
  14.2 14.8 %copy-start = (s32[32]{0:T(128)S(1)}, s32[32]{0:T(128)}, u32[]{:S(2)}) copy-start(s32[32]{0:T(128)} %shard_map.64.table) | copy-start | bytes 388
  14.2 12.3 %collective-permute-start.1 = (bf16[64,4608]{1,0:T(8,128)(2,1)S(1)}, bf16[64,4608]{1,0:T(8,128)(2,1)S(1)}, u32[]{:S(2)}, u32[]{:S(2)}) collective-permute-start(bf16[64,4608]{1,0:T(8,128)(2,1)S(1)} %collective-permute-done.refs_2_.refs_1_.refs_6_.refs_0_), channel_id=1, source_target_pairs={{4,8},{8,12},{5,1},{9,5},{6,10},{10,14},{7,3},{11,7},{20,24},{24,2... | collective-permute-start | bytes 1769480 | tf_op jit(solution)/shard_map/ppermute | solution.py:606
  23.0 23.3 %collective-permute-start.5 = (s32[488,512]{1,0:T(8,128)S(1)}, s32[488,512]{1,0:T(8,128)S(1)}, u32[]{:S(2)}, u32[]{:S(2)}) collective-permute-start(s32[488,512]{1,0:T(8,128)S(1)} %shard_map.68), channel_id=1, source_target_pairs={{0,2},{2,0},{1,3},{3,1},{4,6},{6,4},{5,7},{7,5},{8,10},{10,8},{9,1... | collective-permute-start | bytes 2998280 | tf_op jit(solution)/shard_map/ppermute | solution.py:601
  24.6 11.8 %collective-permute-start.6 = (bf16[64,4608]{1,0:T(8,128)(2,1)S(1)}, bf16[64,4608]{1,0:T(8,128)(2,1)S(1)}, u32[]{:S(2)}, u32[]{:S(2)}) collective-permute-start(bf16[64,4608]{1,0:T(8,128)(2,1)S(1)} %collective-permute-done.2.refs_3_.refs_2_.refs_7_.refs_1_), channel_id=1, source_target_pairs={{4,8},{8,12},{5,1},{9,5},{6,10},{10,14},{7,3},{11,7},{20,24},{24,2... | collective-permute-start | bytes 1769480 | tf_op jit(solution)/shard_map/ppermute | solution.py:606
  26.6 19.7 %collective-permute-start.3 = (bf16[64,4608]{1,0:T(8,128)(2,1)S(1)}, bf16[64,4608]{1,0:T(8,128)(2,1)S(1)}, u32[]{:S(2)}, u32[]{:S(2)}) collective-permute-start(bf16[64,4608]{1,0:T(8,128)(2,1)S(1)} %collective-permute-done.1.refs_9_.refs_3_), channel_id=1, source_target_pairs={{8,12},{5,1},{10,14},{7,3},{24,28},{21,17},{26,30},{23,19}} | collective-permute-start | bytes 1769480 | tf_op jit(solution)/shard_map/ppermute | solution.py:606
  36.4 10.2 %collective-permute-start.7 = (bf16[64,4608]{1,0:T(8,128)(2,1)S(1)}, bf16[64,4608]{1,0:T(8,128)(2,1)S(1)}, u32[]{:S(2)}, u32[]{:S(2)}) collective-permute-start(bf16[64,4608]{1,0:T(8,128)(2,1)S(1)} %collective-permute-done.6.refs_10_.refs_4_), channel_id=1, source_target_pairs={{8,12},{5,1},{10,14},{7,3},{24,28},{21,17},{26,30},{23,19}} | collective-permute-start | bytes 1769480 | tf_op jit(solution)/shard_map/ppermute | solution.py:606
  45.7 6.7 %collective-permute-start.10 = (bf16[64,4608]{1,0:T(8,128)(2,1)S(1)}, bf16[64,4608]{1,0:T(8,128)(2,1)S(1)}, u32[]{:S(2)}, u32[]{:S(2)}) collective-permute-start(bf16[64,4608]{1,0:T(8,128)(2,1)S(1)} %collective-permute-done.1.refs_9_.refs_3_), channel_id=1, source_target_pairs={{0,1},{1,0},{2,3},{3,2},{4,5},{5,4},{6,7},{7,6},{8,9},{9,8},{10,11... | collective-permute-start | bytes 1769480 | tf_op jit(solution)/shard_map/ppermute | solution.py:609
  45.7 6.6 %collective-permute-start.11 = (bf16[64,4608]{1,0:T(8,128)(2,1)S(1)}, bf16[64,4608]{1,0:T(8,128)(2,1)S(1)}, u32[]{:S(2)}, u32[]{:S(2)}) collective-permute-start(bf16[64,4608]{1,0:T(8,128)(2,1)S(1)} %collective-permute-done.6.refs_10_.refs_4_), channel_id=1, source_target_pairs={{0,1},{1,0},{2,3},{3,2},{4,5},{5,4},{6,7},{7,6},{8,9},{9,8},{10,11... | collective-permute-start | bytes 1769480 | tf_op jit(solution)/shard_map/ppermute | solution.py:609
  46.2 4.0 %collective-permute-start.8 = (bf16[128,4608]{1,0:T(8,128)(2,1)S(1)}, bf16[128,4608]{1,0:T(8,128)(2,1)S(1)}, u32[]{:S(2)}, u32[]{:S(2)}) collective-permute-start(bf16[128,4608]{1,0:T(8,128)(2,1)S(1)} %get-tuple-element.40), channel_id=1, source_target_pairs={{0,1},{1,0},{2,3},{3,2},{4,5},{5,4},{6,7},{7,6},{8,9},{9,8},{10,11... | collective-permute-start | bytes 3538952 | tf_op jit(solution)/shard_map/ppermute | solution.py:609
  46.6 5.8 %collective-permute-start.12 = (bf16[64,4608]{1,0:T(8,128)(2,1)S(1)}, bf16[64,4608]{1,0:T(8,128)(2,1)S(1)}, u32[]{:S(2)}, u32[]{:S(2)}) collective-permute-start(bf16[64,4608]{1,0:T(8,128)(2,1)S(1)} %collective-permute-done.3.refs_13_.refs_7_), channel_id=1, source_target_pairs={{0,1},{1,0},{2,3},{3,2},{4,5},{5,4},{6,7},{7,6},{8,9},{9,8},{10,11... | collective-permute-start | bytes 1769480 | tf_op jit(solution)/shard_map/ppermute | solution.py:609
  47.0 5.3 %collective-permute-start.13 = (bf16[64,4608]{1,0:T(8,128)(2,1)S(1)}, bf16[64,4608]{1,0:T(8,128)(2,1)S(1)}, u32[]{:S(2)}, u32[]{:S(2)}) collective-permute-start(bf16[64,4608]{1,0:T(8,128)(2,1)S(1)} %collective-permute-done.7.refs_14_.refs_8_), channel_id=1, source_target_pairs={{0,1},{1,0},{2,3},{3,2},{4,5},{5,4},{6,7},{7,6},{8,9},{9,8},{10,11... | collective-permute-start | bytes 1769480 | tf_op jit(solution)/shard_map/ppermute | solution.py:609
  51.8 5.6 %collective-permute-start.9 = (f32[2,128,128]{2,1,0:T(8,128)S(1)}, f32[2,128,128]{2,1,0:T(8,128)S(1)}, u32[]{:S(2)}, u32[]{:S(2)}) collective-permute-start(f32[2,128,128]{2,1,0:T(8,128)S(1)} %shard_map.73.refs_2_), channel_id=1, source_target_pairs={{0,2},{2,0},{1,3},{3,1},{4,6},{6,4},{5,7},{7,5},{8,10},{10,8},{9,1... | collective-permute-start | bytes 393224 | tf_op jit(solution)/shard_map/ppermute | solution.py:601
  55.0 5.3 %collective-permute-start.14 = (f32[2,128,128]{2,1,0:T(8,128)S(1)}, f32[2,128,128]{2,1,0:T(8,128)S(1)}, u32[]{:S(2)}, u32[]{:S(2)}) collective-permute-start(f32[2,128,128]{2,1,0:T(8,128)S(1)} %shard_map.75.refs_1_), channel_id=1, source_target_pairs={{0,2},{2,0},{1,3},{3,1},{4,6},{6,4},{5,7},{7,5},{8,10},{10,8},{9,1... | collective-permute-start | bytes 393224 | tf_op jit(solution)/shard_map/ppermute | solution.py:601

commit v21 on v20

--- a/solution.py
+++ b/solution.py
@@ -10,7 +10,7 @@
 SEGMENT_ROWS = 128
 adapter_scale = 0.5
 MOST = 2
-BLOCK = 256
+BLOCK = 512
 PIECES = 4
 CHUNKS = ((6, 2), (0, 6))
 UPPER = 3

time: 62.4 us -> 62.3 us (level)
    ppermute x6, waiting for transfers between devices: 0.88 us -> 1.52 us  [along_line(): return lax.ppermute(array, ('adapter', 'dp'), up + down)]
  transfers between devices with their start and end apart: 15 -> 15, of which waited for: 4 -> 5; matrix products, arithmetic and copies ran while one was open for 0% -> 0% of each run, Pallas kernels for 54% -> 53%
where the time goes in v21:
time: 62.3 us; the launch traced here: 62 us
  Pallas kernels  35.5 us (57%)
  starting transfers between devices  20.4 us (33%)
  waiting for transfers between devices  5.8 us (9%)
    ppermute x6, starting transfers between devices, along_line(): return lax.ppermute(array, ('adapter', 'dp'), up + down)  13.9 us
    pallas_call x2, Pallas kernels, sent_call(): pl.pallas_call(functools.partial(sent_kernel, first, sizes, step, n_tenso...  10.3 us
    pallas_call x1, Pallas kernels, lower_call(): pl.pallas_call(functools.partial(lower_kernel, per_device, rank), in_spec...  6.99 us
    pallas_call x1, Pallas kernels, upper_call(): pl.pallas_call(functools.partial(upper_kernel, n_adapter), in_specs=[SMEM...  6.04 us
    ppermute x4, starting transfers between devices, swap_tensor(): return lax.ppermute(array, 'tensor', pairs)  5.29 us
    pallas_call x2, Pallas kernels, shrink_call(): pl.pallas_call(functools.partial(shrink_kernel, ks, rank, at, layout), in...  4.19 us
    ppermute x5, waiting for transfers between devices, swap_cores(): return lax.ppermute(array, 'dp', [(0, 1), (1, 0)])  2.81 us
    pallas_call x1, Pallas kernels, early(): pl.pallas_call(functools.partial(early_kernel, n_adapter, n_tensor, rank,...  2.27 us
  transfers between devices with their start and end apart: 15, of which 5 were waited for; matrix products, arithmetic and copies ran while one was open for 0% of the time, Pallas kernels for 53%

profile of v21, /device:TPU:16, one launch (start us, length us, event | category | flops | bytes accessed | tf_op | source)
XLA Modules:
  0.0 62.0 jit_solution(14743548972689708670)
XLA Ops:
  0.0 1.1 %shard_map.65.refs_0_.refs_4_ = bf16[64,4608]{1,0:T(8,128)(2,1)S(1)} custom-call(bf16[128,4096]{1,0:T(8,128)(2,1)} %bitcast.4, bf16[128,1024]{1,0:T(8,128)(2,1)} %bitcast.6), custom_call_target="tpu_custom_call" | custom-call | bytes 2359296 | tf_op jit(solution)/shard_map/pallas_call | solution.py:91
  1.1 3.5 %collective-permute-start = (bf16[64,4608]{1,0:T(8,128)(2,1)S(1)}, bf16[64,4608]{1,0:T(8,128)(2,1)S(1)}, u32[]{:S(2)}, u32[]{:S(2)}) collective-permute-start(bf16[64,4608]{1,0:T(8,128)(2,1)S(1)} %shard_map.65.refs_0_.refs_4_), channel_id=1, source_target_pairs={{0,4},{4,8},{8,12},{5,1},{9,5},{13,9},{2,6},{6,10},{10,14},{7,3},{... | collective-permute-start | bytes 1769480 | tf_op jit(solution)/shard_map/ppermute | solution.py:606
  4.6 1.1 %shard_map.67.refs_1_.refs_5_ = bf16[64,4608]{1,0:T(8,128)(2,1)S(1)} custom-call(bf16[128,4096]{1,0:T(8,128)(2,1)} %bitcast.5, bf16[128,1024]{1,0:T(8,128)(2,1)} %bitcast.7), custom_call_target="tpu_custom_call" | custom-call | bytes 2359296 | tf_op jit(solution)/shard_map/pallas_call | solution.py:91
  5.6 1.9 %collective-permute-start.2 = (bf16[64,4608]{1,0:T(8,128)(2,1)S(1)}, bf16[64,4608]{1,0:T(8,128)(2,1)S(1)}, u32[]{:S(2)}, u32[]{:S(2)}) collective-permute-start(bf16[64,4608]{1,0:T(8,128)(2,1)S(1)} %shard_map.67.refs_1_.refs_5_), channel_id=1, source_target_pairs={{0,4},{4,8},{8,12},{5,1},{9,5},{13,9},{2,6},{6,10},{10,14},{7,3},{... | collective-permute-start | bytes 1769480 | tf_op jit(solution)/shard_map/ppermute | solution.py:606
  7.6 3.6 %shard_map.66 = s32[168,512]{1,0:T(8,128)S(1)} custom-call(bf16[1024,4096]{1,0:T(8,128)(2,1)} %x_ref.6, bf16[4096,1024]{1,0:T(8,128)(2,1)} %w_ref.7), custom_call_target="tpu_custom_call" | custom-call | flops 1073741824 | bytes 6815744 | tf_op jit(solution)/shard_map/pallas_call | solution.py:265
  11.2 1.6 %collective-permute-start.4 = (s32[168,512]{1,0:T(8,128)S(1)}, s32[168,512]{1,0:T(8,128)S(1)}, u32[]{:S(2)}, u32[]{:S(2)}) collective-permute-start(s32[168,512]{1,0:T(8,128)S(1)} %shard_map.66), channel_id=1, source_target_pairs={{0,2},{2,0},{1,3},{3,1},{4,6},{6,4},{5,7},{7,5},{8,10},{10,8},{9,1... | collective-permute-start | bytes 1032200 | tf_op jit(solution)/shard_map/ppermute | solution.py:601
  12.8 1.4 %shard_map.64.table = s32[32]{0:T(128)} custom-call(s32[1024]{0:T(1024)} %ids.1, s32[8]{0:T(128)} %slots.1), custom_call_target="tpu_custom_call" | custom-call | bytes 4096 | tf_op jit(solution)/shard_map/pallas_call | solution.py:123
  14.2 0.0 copy-start
  14.2 0.0 collective-permute-done.refs_2_.refs_1_.refs_6_.refs_0_
  14.2 2.1 %collective-permute-start.1 = (bf16[64,4608]{1,0:T(8,128)(2,1)S(1)}, bf16[64,4608]{1,0:T(8,128)(2,1)S(1)}, u32[]{:S(2)}, u32[]{:S(2)}) collective-permute-start(bf16[64,4608]{1,0:T(8,128)(2,1)S(1)} %collective-permute-done.refs_2_.refs_1_.refs_6_.refs_0_), channel_id=1, source_target_pairs={{4,8},{8,12},{5,1},{9,5},{6,10},{10,14},{7,3},{11,7},{20,24},{24,2... | collective-permute-start | bytes 1769480 | tf_op jit(solution)/shard_map/ppermute | solution.py:606
  16.3 6.7 %shard_map.68 = s32[488,512]{1,0:T(8,128)S(1)} custom-call(bf16[1024,4096]{1,0:T(8,128)(2,1)} %x_ref.6, bf16[4096,1024]{1,0:T(8,128)(2,1)} %w_ref.7), custom_call_target="tpu_custom_call" | custom-call | flops 3221225472 | bytes 12058624 | tf_op jit(solution)/shard_map/pallas_call | solution.py:265
  23.1 0.0 collective-permute-done.2.refs_3_.refs_2_.refs_7_.refs_1_
  23.1 0.0 collective-permute-done.4.refs_4_
  23.1 1.6 %collective-permute-start.5 = (s32[488,512]{1,0:T(8,128)S(1)}, s32[488,512]{1,0:T(8,128)S(1)}, u32[]{:S(2)}, u32[]{:S(2)}) collective-permute-start(s32[488,512]{1,0:T(8,128)S(1)} %shard_map.68), channel_id=1, source_target_pairs={{0,2},{2,0},{1,3},{3,1},{4,6},{6,4},{5,7},{7,5},{8,10},{10,8},{9,1... | collective-permute-start | bytes 2998280 | tf_op jit(solution)/shard_map/ppermute | solution.py:601
  24.6 1.9 %collective-permute-start.6 = (bf16[64,4608]{1,0:T(8,128)(2,1)S(1)}, bf16[64,4608]{1,0:T(8,128)(2,1)S(1)}, u32[]{:S(2)}, u32[]{:S(2)}) collective-permute-start(bf16[64,4608]{1,0:T(8,128)(2,1)S(1)} %collective-permute-done.2.refs_3_.refs_2_.refs_7_.refs_1_), channel_id=1, source_target_pairs={{4,8},{8,12},{5,1},{9,5},{6,10},{10,14},{7,3},{11,7},{20,24},{24,2... | collective-permute-start | bytes 1769480 | tf_op jit(solution)/shard_map/ppermute | solution.py:606
  26.6 0.0 collective-permute-done.1.refs_9_.refs_3_
  26.6 2.4 %collective-permute-start.3 = (bf16[64,4608]{1,0:T(8,128)(2,1)S(1)}, bf16[64,4608]{1,0:T(8,128)(2,1)S(1)}, u32[]{:S(2)}, u32[]{:S(2)}) collective-permute-start(bf16[64,4608]{1,0:T(8,128)(2,1)S(1)} %collective-permute-done.1.refs_9_.refs_3_), channel_id=1, source_target_pairs={{8,12},{5,1},{10,14},{7,3},{24,28},{21,17},{26,30},{23,19}} | collective-permute-start | bytes 1769480 | tf_op jit(solution)/shard_map/ppermute | solution.py:606
  29.0 0.0 copy-done
  29.0 6.0 %shard_map.69 = (f32[384,512]{1,0:T(8,128)S(1)}, bf16[3,2,128,4096]{3,2,1,0:T(8,128)(2,1)S(1)}) custom-call(s32[32]{0:T(128)S(1)} %copy-done, bf16[1024,4096]{1,0:T(8,128)(2,1)} %x_ref.6, bf16[4096,1024]{1,0:T(8,128)(2,1)} %w_ref.7), custom_call_target="tpu_custom_call" | custom-call | flops 1610612736 | bytes 12582912 | tf_op jit(solution)/shard_map/pallas_call | solution.py:360
  35.1 1.4 %collective-permute-done.6.refs_10_.refs_4_ = bf16[64,4608]{1,0:T(8,128)(2,1)S(1)} collective-permute-done((bf16[64,4608]{1,0:T(8,128)(2,1)S(1)}, bf16[64,4608]{1,0:T(8,128)(2,1)S(1)}, u32[]{:S(2)}, u32[]{:S(2)}) %collective-permute-start.6) | collective-permute-done | bytes 589856 | tf_op jit(solution)/shard_map/ppermute | solution.py:606
  36.4 2.1 %collective-permute-start.7 = (bf16[64,4608]{1,0:T(8,128)(2,1)S(1)}, bf16[64,4608]{1,0:T(8,128)(2,1)S(1)}, u32[]{:S(2)}, u32[]{:S(2)}) collective-permute-start(bf16[64,4608]{1,0:T(8,128)(2,1)S(1)} %collective-permute-done.6.refs_10_.refs_4_), channel_id=1, source_target_pairs={{8,12},{5,1},{10,14},{7,3},{24,28},{21,17},{26,30},{23,19}} | collective-permute-start | bytes 1769480 | tf_op jit(solution)/shard_map/ppermute | solution.py:606
  38.5 7.0 %shard_map.71 = (f32[640,512]{1,0:T(8,128)S(1)}, f32[1,128,128]{2,1,0:T(8,128)S(1)}, bf16[128,4608]{1,0:T(8,128)(2,1)S(1)}) custom-call(s32[32]{0:T(128)S(1)} %copy-done, bf16[1024,4096]{1,0:T(8,128)(2,1)} %x_ref.6, bf16[4096,1024]{1,0:T(8,128)(2,1)} %w_ref.7, bf16[64,4608]{1,0:T(8,128)(2,1)S(1)} %shard_map.65.refs_0_.refs_4_, ...), custom_call_target="tpu_custom_call" | custom-call | bytes 2097152 | tf_op jit(solution)/shard_map/pallas_call | solution.py:404
  45.5 0.1 collective-permute-start.10
  45.6 0.5 collective-permute-start.11
  46.1 0.0 collective-permute-done.3.refs_13_.refs_7_
  46.1 0.1 collective-permute-start.8
  46.2 0.0 collective-permute-done.5.refs_0_
  46.2 0.2 shard_map.70.refs_0_
  46.4 0.2 collective-permute-done.7.refs_14_.refs_8_
  46.6 0.3 collective-permute-start.12
  46.9 0.2 collective-permute-start.13
  47.1 0.2 shard_map.72.refs_1_
  47.3 2.8 %collective-permute-done.8.refs_3_.refs_8_.refs_2_ = bf16[128,4608]{1,0:T(8,128)(2,1)S(1)} collective-permute-done((bf16[128,4608]{1,0:T(8,128)(2,1)S(1)}, bf16[128,4608]{1,0:T(8,128)(2,1)S(1)}, u32[]{:S(2)}, u32[]{:S(2)}) %collective-permute-start.8) | collective-permute-done | bytes 1179680 | tf_op jit(solution)/shard_map/ppermute | solution.py:609
  50.1 1.5 %shard_map.73.refs_2_ = f32[2,128,128]{2,1,0:T(8,128)S(1)} custom-call(s32[32]{0:T(128)S(1)} %copy-done, bf16[3,2,128,4096]{3,2,1,0:T(8,128)(2,1)S(1)} %get-tuple-element.44.kept_ref, f32[1,128,128]{2,1,0:T(8,128)S(1)} %get-tuple-element.39.refs_0_, bf16[64,4608]{1,0:T(8,128)(2,1)S(1)} %collective-permute-done.refs_2_.refs_1_.refs_6_.refs_0_, ...), custom_call_target="tpu_custom_call" | custom-call | flops 536870912 | bytes 2097152 | tf_op jit(solution)/shard_map/pallas_call | solution.py:437
  51.7 0.6 collective-permute-start.9
  52.3 0.0 collective-permute-done.10.refs_11_.refs_5_
  52.3 0.0 collective-permute-done.11.refs_12_.refs_6_
  52.3 0.0 collective-permute-done.12.refs_15_.refs_9_
  52.3 0.0 collective-permute-done.13.refs_16_.refs_10_
  52.3 2.6 %shard_map.75.refs_1_ = f32[2,128,128]{2,1,0:T(8,128)S(1)} custom-call(s32[32]{0:T(128)S(1)} %copy-done, bf16[3,2,128,4096]{3,2,1,0:T(8,128)(2,1)S(1)} %get-tuple-element.44.kept_ref, bf16[64,4608]{1,0:T(8,128)(2,1)S(1)} %collective-permute-done.refs_2_.refs_1_.refs_6_.refs_0_, bf16[64,4608]{1,0:T(8,128)(2,1)S(1)} %collective-permute-done.2.refs_3_.refs_2_.refs_7_.refs_1_, ...), custom_call_target="tpu_custom_call" | custom-call | flops 1073741824 | bytes 4194304 | tf_op jit(solution)/shard_map/pallas_call | solution.py:437
  54.9 1.5 %collective-permute-start.14 = (f32[2,128,128]{2,1,0:T(8,128)S(1)}, f32[2,128,128]{2,1,0:T(8,128)S(1)}, u32[]{:S(2)}, u32[]{:S(2)}) collective-permute-start(f32[2,128,128]{2,1,0:T(8,128)S(1)} %shard_map.75.refs_1_), channel_id=1, source_target_pairs={{0,2},{2,0},{1,3},{3,1},{4,6},{6,4},{5,7},{7,5},{8,10},{10,8},{9,1... | collective-permute-start | bytes 393224 | tf_op jit(solution)/shard_map/ppermute | solution.py:601
  56.5 0.8 %collective-permute-done.9.refs_3_ = f32[2,128,128]{2,1,0:T(8,128)S(1)} collective-permute-done((f32[2,128,128]{2,1,0:T(8,128)S(1)}, f32[2,128,128]{2,1,0:T(8,128)S(1)}, u32[]{:S(2)}, u32[]{:S(2)}) %collective-permute-start.9) | collective-permute-done | bytes 131104 | tf_op jit(solution)/shard_map/ppermute | solution.py:601
  57.3 2.3 %shard_map.74 = (bf16[1024,512]{1,0:T(8,128)(2,1)}, f32[2,2,128,512]{3,2,1,0:T(8,128)S(1)}, bf16[4,128,512]{2,1,0:T(8,128)(2,1)S(1)}) custom-call(s32[32]{0:T(128)S(1)} %copy-done, f32[384,512]{1,0:T(8,128)S(1)} %shard_map.70.refs_0_, f32[640,512]{1,0:T(8,128)S(1)} %shard_map.72.refs_1_, f32[2,128,128]{2,1,0:T(8,128)S(1)} %shard_map.73.refs_2_, ...), custom_call_target="tpu_custom_call" | custom-call | flops 201326592 | bytes 5242880 | tf_op jit(solution)/shard_map/pallas_call | solution.py:525
  59.5 0.7 %collective-permute-done.14.refs_2_ = f32[2,128,128]{2,1,0:T(8,128)S(1)} collective-permute-done((f32[2,128,128]{2,1,0:T(8,128)S(1)}, f32[2,128,128]{2,1,0:T(8,128)S(1)}, u32[]{:S(2)}, u32[]{:S(2)}) %collective-permute-start.14) | collective-permute-done | bytes 131104 | tf_op jit(solution)/shard_map/ppermute | solution.py:601
  60.2 1.6 %shard_map.76 = bf16[1024,512]{1,0:T(8,128)(2,1)} custom-call(s32[32]{0:T(128)S(1)} %copy-done, f32[2,2,128,512]{3,2,1,0:T(8,128)S(1)} %get-tuple-element.43.refs_0_, f32[2,128,128]{2,1,0:T(8,128)S(1)} %shard_map.75.refs_1_, f32[2,128,128]{2,1,0:T(8,128)S(1)} %collective-permute-done.14.refs_2_, ...), custom_call_target="tpu_custom_call", output_to_operand_aliasing={{}: (5, {})} | custom-call | flops 100663296 | bytes 2097152 | tf_op jit(solution)/shard_map/pallas_call | solution.py:568
Async XLA Ops:
  1.1 13.2 %collective-permute-start = (bf16[64,4608]{1,0:T(8,128)(2,1)S(1)}, bf16[64,4608]{1,0:T(8,128)(2,1)S(1)}, u32[]{:S(2)}, u32[]{:S(2)}) collective-permute-start(bf16[64,4608]{1,0:T(8,128)(2,1)S(1)} %shard_map.65.refs_0_.refs_4_), channel_id=1, source_target_pairs={{0,4},{4,8},{8,12},{5,1},{9,5},{13,9},{2,6},{6,10},{10,14},{7,3},{... | collective-permute-start | bytes 1769480 | tf_op jit(solution)/shard_map/ppermute | solution.py:606
  5.6 17.4 %collective-permute-start.2 = (bf16[64,4608]{1,0:T(8,128)(2,1)S(1)}, bf16[64,4608]{1,0:T(8,128)(2,1)S(1)}, u32[]{:S(2)}, u32[]{:S(2)}) collective-permute-start(bf16[64,4608]{1,0:T(8,128)(2,1)S(1)} %shard_map.67.refs_1_.refs_5_), channel_id=1, source_target_pairs={{0,4},{4,8},{8,12},{5,1},{9,5},{13,9},{2,6},{6,10},{10,14},{7,3},{... | collective-permute-start | bytes 1769480 | tf_op jit(solution)/shard_map/ppermute | solution.py:606
  11.2 11.9 %collective-permute-start.4 = (s32[168,512]{1,0:T(8,128)S(1)}, s32[168,512]{1,0:T(8,128)S(1)}, u32[]{:S(2)}, u32[]{:S(2)}) collective-permute-start(s32[168,512]{1,0:T(8,128)S(1)} %shard_map.66), channel_id=1, source_target_pairs={{0,2},{2,0},{1,3},{3,1},{4,6},{6,4},{5,7},{7,5},{8,10},{10,8},{9,1... | collective-permute-start | bytes 1032200 | tf_op jit(solution)/shard_map/ppermute | solution.py:601
  14.2 14.8 %copy-start = (s32[32]{0:T(128)S(1)}, s32[32]{0:T(128)}, u32[]{:S(2)}) copy-start(s32[32]{0:T(128)} %shard_map.64.table) | copy-start | bytes 388
  14.2 12.3 %collective-permute-start.1 = (bf16[64,4608]{1,0:T(8,128)(2,1)S(1)}, bf16[64,4608]{1,0:T(8,128)(2,1)S(1)}, u32[]{:S(2)}, u32[]{:S(2)}) collective-permute-start(bf16[64,4608]{1,0:T(8,128)(2,1)S(1)} %collective-permute-done.refs_2_.refs_1_.refs_6_.refs_0_), channel_id=1, source_target_pairs={{4,8},{8,12},{5,1},{9,5},{6,10},{10,14},{7,3},{11,7},{20,24},{24,2... | collective-permute-start | bytes 1769480 | tf_op jit(solution)/shard_map/ppermute | solution.py:606
  23.1 23.1 %collective-permute-start.5 = (s32[488,512]{1,0:T(8,128)S(1)}, s32[488,512]{1,0:T(8,128)S(1)}, u32[]{:S(2)}, u32[]{:S(2)}) collective-permute-start(s32[488,512]{1,0:T(8,128)S(1)} %shard_map.68), channel_id=1, source_target_pairs={{0,2},{2,0},{1,3},{3,1},{4,6},{6,4},{5,7},{7,5},{8,10},{10,8},{9,1... | collective-permute-start | bytes 2998280 | tf_op jit(solution)/shard_map/ppermute | solution.py:601
  24.6 11.8 %collective-permute-start.6 = (bf16[64,4608]{1,0:T(8,128)(2,1)S(1)}, bf16[64,4608]{1,0:T(8,128)(2,1)S(1)}, u32[]{:S(2)}, u32[]{:S(2)}) collective-permute-start(bf16[64,4608]{1,0:T(8,128)(2,1)S(1)} %collective-permute-done.2.refs_3_.refs_2_.refs_7_.refs_1_), channel_id=1, source_target_pairs={{4,8},{8,12},{5,1},{9,5},{6,10},{10,14},{7,3},{11,7},{20,24},{24,2... | collective-permute-start | bytes 1769480 | tf_op jit(solution)/shard_map/ppermute | solution.py:606
  26.6 19.5 %collective-permute-start.3 = (bf16[64,4608]{1,0:T(8,128)(2,1)S(1)}, bf16[64,4608]{1,0:T(8,128)(2,1)S(1)}, u32[]{:S(2)}, u32[]{:S(2)}) collective-permute-start(bf16[64,4608]{1,0:T(8,128)(2,1)S(1)} %collective-permute-done.1.refs_9_.refs_3_), channel_id=1, source_target_pairs={{8,12},{5,1},{10,14},{7,3},{24,28},{21,17},{26,30},{23,19}} | collective-permute-start | bytes 1769480 | tf_op jit(solution)/shard_map/ppermute | solution.py:606
  36.4 10.2 %collective-permute-start.7 = (bf16[64,4608]{1,0:T(8,128)(2,1)S(1)}, bf16[64,4608]{1,0:T(8,128)(2,1)S(1)}, u32[]{:S(2)}, u32[]{:S(2)}) collective-permute-start(bf16[64,4608]{1,0:T(8,128)(2,1)S(1)} %collective-permute-done.6.refs_10_.refs_4_), channel_id=1, source_target_pairs={{8,12},{5,1},{10,14},{7,3},{24,28},{21,17},{26,30},{23,19}} | collective-permute-start | bytes 1769480 | tf_op jit(solution)/shard_map/ppermute | solution.py:606
  45.5 6.7 %collective-permute-start.10 = (bf16[64,4608]{1,0:T(8,128)(2,1)S(1)}, bf16[64,4608]{1,0:T(8,128)(2,1)S(1)}, u32[]{:S(2)}, u32[]{:S(2)}) collective-permute-start(bf16[64,4608]{1,0:T(8,128)(2,1)S(1)} %collective-permute-done.1.refs_9_.refs_3_), channel_id=1, source_target_pairs={{0,1},{1,0},{2,3},{3,2},{4,5},{5,4},{6,7},{7,6},{8,9},{9,8},{10,11... | collective-permute-start | bytes 1769480 | tf_op jit(solution)/shard_map/ppermute | solution.py:609
  45.6 6.7 %collective-permute-start.11 = (bf16[64,4608]{1,0:T(8,128)(2,1)S(1)}, bf16[64,4608]{1,0:T(8,128)(2,1)S(1)}, u32[]{:S(2)}, u32[]{:S(2)}) collective-permute-start(bf16[64,4608]{1,0:T(8,128)(2,1)S(1)} %collective-permute-done.6.refs_10_.refs_4_), channel_id=1, source_target_pairs={{0,1},{1,0},{2,3},{3,2},{4,5},{5,4},{6,7},{7,6},{8,9},{9,8},{10,11... | collective-permute-start | bytes 1769480 | tf_op jit(solution)/shard_map/ppermute | solution.py:609
  46.1 4.0 %collective-permute-start.8 = (bf16[128,4608]{1,0:T(8,128)(2,1)S(1)}, bf16[128,4608]{1,0:T(8,128)(2,1)S(1)}, u32[]{:S(2)}, u32[]{:S(2)}) collective-permute-start(bf16[128,4608]{1,0:T(8,128)(2,1)S(1)} %get-tuple-element.40), channel_id=1, source_target_pairs={{0,1},{1,0},{2,3},{3,2},{4,5},{5,4},{6,7},{7,6},{8,9},{9,8},{10,11... | collective-permute-start | bytes 3538952 | tf_op jit(solution)/shard_map/ppermute | solution.py:609
  46.6 5.7 %collective-permute-start.12 = (bf16[64,4608]{1,0:T(8,128)(2,1)S(1)}, bf16[64,4608]{1,0:T(8,128)(2,1)S(1)}, u32[]{:S(2)}, u32[]{:S(2)}) collective-permute-start(bf16[64,4608]{1,0:T(8,128)(2,1)S(1)} %collective-permute-done.3.refs_13_.refs_7_), channel_id=1, source_target_pairs={{0,1},{1,0},{2,3},{3,2},{4,5},{5,4},{6,7},{7,6},{8,9},{9,8},{10,11... | collective-permute-start | bytes 1769480 | tf_op jit(solution)/shard_map/ppermute | solution.py:609
  46.9 5.3 %collective-permute-start.13 = (bf16[64,4608]{1,0:T(8,128)(2,1)S(1)}, bf16[64,4608]{1,0:T(8,128)(2,1)S(1)}, u32[]{:S(2)}, u32[]{:S(2)}) collective-permute-start(bf16[64,4608]{1,0:T(8,128)(2,1)S(1)} %collective-permute-done.7.refs_14_.refs_8_), channel_id=1, source_target_pairs={{0,1},{1,0},{2,3},{3,2},{4,5},{5,4},{6,7},{7,6},{8,9},{9,8},{10,11... | collective-permute-start | bytes 1769480 | tf_op jit(solution)/shard_map/ppermute | solution.py:609
  51.7 5.6 %collective-permute-start.9 = (f32[2,128,128]{2,1,0:T(8,128)S(1)}, f32[2,128,128]{2,1,0:T(8,128)S(1)}, u32[]{:S(2)}, u32[]{:S(2)}) collective-permute-start(f32[2,128,128]{2,1,0:T(8,128)S(1)} %shard_map.73.refs_2_), channel_id=1, source_target_pairs={{0,2},{2,0},{1,3},{3,1},{4,6},{6,4},{5,7},{7,5},{8,10},{10,8},{9,1... | collective-permute-start | bytes 393224 | tf_op jit(solution)/shard_map/ppermute | solution.py:601
  54.9 5.3 %collective-permute-start.14 = (f32[2,128,128]{2,1,0:T(8,128)S(1)}, f32[2,128,128]{2,1,0:T(8,128)S(1)}, u32[]{:S(2)}, u32[]{:S(2)}) collective-permute-start(f32[2,128,128]{2,1,0:T(8,128)S(1)} %shard_map.75.refs_1_), channel_id=1, source_target_pairs={{0,2},{2,0},{1,3},{3,1},{4,6},{6,4},{5,7},{7,5},{8,10},{10,8},{9,1... | collective-permute-start | bytes 393224 | tf_op jit(solution)/shard_map/ppermute | solution.py:601
